TPU v7x, 32 devices: a whole 2x2x4 slice. The times are simulated.
32 devices in a mesh: gz: 8 (over z, x), gx: 4 (over y, core).
Axes of the slice: x: 2, y: 2, z: 4, core: 2. Of those that a mesh axis runs over, the one named last changes fastest.
Arguments:
- strength: float32 [3, 16384], P(None, ('gz', 'gx')), may hold values from -6 to 6
- offsets: float32 [3, 16384], P(None, ('gz', 'gx')), may hold values from -0.5 to 0.5
- cell_index: int32 [16384], P(('gz', 'gx')), may hold values from 0 to 131071
- migrate_count: int32 [8, 4, 2], P('gz', 'gx'), may hold values from 32 to 64, as said below
- ambient: float32 [3, 64, 256, 256], P(None, 'gz', 'gx'), may hold values from -2.5 to 2.5
Outputs:
- velocity: float32 [3, 64, 256, 256], P(None, 'gz', 'gx')
- vorticity: float32 [3, 64, 256, 256], P(None, 'gz', 'gx')
Inputs may be any that keep to these rules, and one draw needn't show every extreme that they name: `migrate_count`: some device has 64 in the first entry and some device has 64 in the second.
All inputs are finite; a program needn't handle non-finite values.
Results may differ from a plain program's by a relative error of at most 0.0003.
Values sent between devices are 32-bit elements; how exact they have to be, the bound alone decides.
No kernel may reach another device: no remote copies, remote signals or barrier semaphores. Data moves between devices by JAX's collectives and lax.ppermute only.
A program may use at most 128 MiB of HBM per device.

v0:
```python
import math

import jax
import jax.numpy as jnp
from jax import lax
from jax.sharding import PartitionSpec as P

NX = 256
NY = 256
PART = 512
MIG = 64


time_step = 0.25
highest = lax.Precision.HIGHEST


def padded_2(cells, sides, width):
    for axis, dim in sides:
        count = lax.axis_size(axis)
        head = lax.slice_in_dim(cells, 0, width, axis=dim)
        tail = lax.slice_in_dim(cells, cells.shape[dim] - width, cells.shape[dim], axis=dim)
        cells = jnp.concatenate(
            [
                lax.ppermute(tail, axis, [(i, (i + 1) % count) for i in range(count)]),
                cells,
                lax.ppermute(head, axis, [((i + 1) % count, i) for i in range(count)]),
            ],
            axis=dim,
        )
    return cells


def kernel_weight(distance):
    radius = jnp.abs(distance)
    near_part = 1.0 - 2.5 * radius * radius + 1.5 * radius * radius * radius
    far_part = 0.5 * (2.0 - radius) * (2.0 - radius) * (1.0 - radius)
    return jnp.where(radius < 1.0, near_part, jnp.where(radius < 2.0, far_part, 0.0))


def wave_of(position, extent):
    signed = jnp.where(position < extent // 2, position, position - extent)
    return 2.0 * jnp.pi * signed.astype(jnp.float32) / extent


def fourier_tables(extent):
    position = jnp.arange(extent, dtype=jnp.int32)
    phase = position[:, None] * position[None, :] % extent
    angle = 2.0 * jnp.pi * phase.astype(jnp.float32) / extent
    return (jnp.cos(angle), jnp.sin(angle))


def complex_table(extent, direction):
    cosine, sine = fourier_tables(extent)
    real_rows = jnp.stack([cosine, -direction * sine], axis=1)
    imag_rows = jnp.stack([direction * sine, cosine], axis=1)
    return jnp.stack([real_rows, imag_rows], axis=0)


def split_pairs(values):
    return values.reshape(values.shape[:-1] + (2, values.shape[-1] // 2))


def join_pairs(values):
    return values.reshape(values.shape[:-2] + (values.shape[-2] * values.shape[-1],))


def lateral_table(extent, pencil_count, mode_count):
    column = jnp.arange(2 * mode_count * pencil_count, dtype=jnp.int32)
    wave_number = column // (2 * mode_count) * mode_count + column % mode_count
    half_flag = column // mode_count % 2
    position = jnp.arange(extent, dtype=jnp.int32)
    phase = position[:, None] * wave_number[None, :] % extent
    angle = 2.0 * jnp.pi * phase.astype(jnp.float32) / extent
    return (jnp.where(half_flag[None, :] == 0, jnp.cos(angle), -jnp.sin(angle)), wave_number)


def halved_tables(extent, pencil_count):
    mode_count = extent // (2 * pencil_count)
    table, wave_number = lateral_table(extent, pencil_count, mode_count)
    column = jnp.arange(table.shape[1], dtype=jnp.int32)
    position = jnp.arange(extent, dtype=jnp.int32)
    alternating = (1 - 2 * (position % 2)).astype(jnp.float32)
    table = jnp.where(column[None, :] == mode_count, alternating[:, None], table)
    weights = jnp.where(wave_number == 0, 1.0, 2.0).astype(jnp.float32)
    return (table, table.T * weights[:, None] * (1.0 / extent))


def times_minus_i(values):
    half_width = values.shape[-1] // 2
    signs = jnp.where(jnp.arange(2 * half_width) < half_width, 1.0, -1.0).astype(jnp.float32)
    return jnp.roll(values, half_width, axis=values.ndim - 1) * signs


def mirrored(values, axis_number):
    return jnp.roll(jnp.flip(values, axis=axis_number), 1, axis=axis_number)


def reslot(values, pencil_index):
    mode_count = values.shape[3] // 2
    middle = values.shape[2] // 2
    real_part = values[..., 0]
    imag_part = values[..., mode_count]
    mirror_real = mirrored(real_part, 2)
    mirror_imag = mirrored(imag_part, 2)
    wave_index = jnp.arange(values.shape[2], dtype=jnp.int32)[None, None, :]
    self_paired = (wave_index == 0) | (wave_index == middle)
    new_real = jnp.where(
        wave_index <= middle, 0.5 * (real_part + mirror_real), 0.5 * (imag_part + mirror_imag)
    )
    new_imag = jnp.where(
        self_paired,
        imag_part,
        jnp.where(
            wave_index < middle, 0.5 * (imag_part - mirror_imag), 0.5 * (real_part - mirror_real)
        ),
    )
    first_pencil = pencil_index == 0
    values = values.at[..., 0].set(jnp.where(first_pencil, new_real, real_part))
    return values.at[..., mode_count].set(jnp.where(first_pencil, new_imag, imag_part))


def unslot(values, pencil_index):
    mode_count = values.shape[3] // 2
    middle = values.shape[2] // 2
    real_part = values[..., 0]
    imag_part = values[..., mode_count]
    mirror_real = mirrored(real_part, 2)
    mirror_imag = mirrored(imag_part, 2)
    wave_index = jnp.arange(values.shape[2], dtype=jnp.int32)[None, None, :]
    self_paired = (wave_index == 0) | (wave_index == middle)
    new_real = jnp.where(
        self_paired,
        real_part,
        jnp.where(wave_index < middle, real_part - mirror_imag, mirror_real + imag_part),
    )
    new_imag = jnp.where(
        self_paired,
        imag_part,
        jnp.where(wave_index < middle, imag_part + mirror_real, real_part - mirror_imag),
    )
    first_pencil = pencil_index == 0
    values = values.at[..., 0].set(jnp.where(first_pencil, new_real, real_part))
    return values.at[..., mode_count].set(jnp.where(first_pencil, new_imag, imag_part))


def curl_modes(spectral, wave_z, wave_x, wave_y, inverse_sq):
    stream = spectral * inverse_sq
    crossed = jnp.stack(
        [
            wave_x * stream[2] - wave_y * stream[1],
            wave_y * stream[0] - wave_z * stream[2],
            wave_z * stream[1] - wave_x * stream[0],
        ]
    )
    return -times_minus_i(crossed)


def packed_velocity(spectral, slab_index, pencil_index, block_width, wake_cells):
    column_pairs = spectral.shape[3]
    mode_count = column_pairs // 2
    z_index = jnp.arange(wake_cells, dtype=jnp.int32)[:, None, None]
    x_global = (slab_index * block_width + jnp.arange(block_width, dtype=jnp.int32))[None, :, None]
    column = jnp.arange(column_pairs, dtype=jnp.int32)[None, None, :]
    y_mode = pencil_index * mode_count + column % mode_count
    packed_column = (pencil_index == 0) & (column % mode_count == 0)
    nyquist = packed_column & (x_global > NX // 2)
    x_mode = jnp.where(nyquist, NX - x_global, x_global)
    wave_z = wave_of(z_index, wake_cells)
    wave_x = wave_of(x_mode, NX)
    wave_y = wave_of(y_mode, NY)
    wave_sq = (
        wave_z * wave_z + wave_x * wave_x + jnp.where(nyquist, jnp.pi * jnp.pi, wave_y * wave_y)
    )
    anchor = (z_index == 0) & (x_mode == 0) & (y_mode == 0) & jnp.logical_not(nyquist)
    inverse_sq = jnp.where(anchor, 0.0, 1.0 / jnp.where(anchor, 1.0, wave_sq))
    trim_z = jnp.where(z_index == wake_cells // 2, 0.0, wave_z)
    trim_x = jnp.where(x_mode == NX // 2, 0.0, wave_x)
    trim_y = jnp.where(nyquist, 0.0, wave_y)
    velocity_hat = curl_modes(spectral, trim_z, trim_x, trim_y, inverse_sq)
    real_part = spectral[..., 0]
    imag_part = spectral[..., mode_count]
    mirror_real = mirrored(real_part, 1)
    mirror_imag = mirrored(imag_part, 1)
    even_pack = jnp.stack(
        [0.5 * (real_part + mirror_real), 0.5 * (imag_part - mirror_imag)], axis=3
    )
    odd_pack = jnp.stack([0.5 * (imag_part + mirror_imag), 0.5 * (mirror_real - real_part)], axis=3)
    plane_z = z_index[:, :, 0]
    x_plane = x_global[:, :, 0]
    pair_wave_z = wave_of(plane_z, wake_cells)
    pair_wave_x = wave_of(x_plane, NX)
    base_sq = pair_wave_z * pair_wave_z + pair_wave_x * pair_wave_x
    pair_anchor = (plane_z == 0) & (x_plane == 0)
    even_inverse = jnp.where(pair_anchor, 0.0, 1.0 / jnp.where(pair_anchor, 1.0, base_sq))[
        ..., None
    ]
    odd_inverse = (1.0 / (base_sq + jnp.pi * jnp.pi))[..., None]
    pair_trim_z = jnp.where(plane_z == wake_cells // 2, 0.0, pair_wave_z)[..., None]
    nothing = jnp.zeros((1, 1, 1), jnp.float32)
    even_hat = curl_modes(even_pack, pair_trim_z, nothing, nothing, even_inverse)
    odd_hat = curl_modes(odd_pack, pair_trim_z, nothing, nothing, odd_inverse)
    joined_real = even_hat[..., 0] - odd_hat[..., 1]
    joined_imag = even_hat[..., 1] + odd_hat[..., 0]
    paired = (pencil_index == 0) & ((x_plane == 0) | (x_plane == NX // 2))
    velocity_hat = velocity_hat.at[..., 0].set(jnp.where(paired, joined_real, velocity_hat[..., 0]))
    return velocity_hat.at[..., mode_count].set(
        jnp.where(paired, joined_imag, velocity_hat[..., mode_count])
    )


def on_device(strength, offsets, cell_index, migrate_count, ambient):
    slab_planes = ambient.shape[1]
    pencil_cols = ambient.shape[2]
    slab_count = lax.axis_size("gz")
    pencil_count = lax.axis_size("gx")
    wake_cells = slab_planes * slab_count
    pencil_index = lax.axis_index("gx")
    up_count = migrate_count[0, 0, 0]
    down_count = migrate_count[0, 0, 1]
    slot_index = jnp.arange(PART, dtype=jnp.int32)
    packet = jnp.concatenate([strength, offsets, cell_index.astype(jnp.float32)[None, :]], axis=0)
    is_strength = (jnp.arange(7) < 3)[:, None]
    head_live = slot_index[:MIG] < up_count
    upward = jnp.where(is_strength & ~head_live[None, :], 0.0, packet[:, :MIG])
    downward = lax.dynamic_slice_in_dim(packet, up_count, MIG, axis=1)
    down_live = jnp.arange(MIG, dtype=jnp.int32) < down_count
    downward = jnp.where(is_strength & ~down_live[None, :], 0.0, downward)
    outgoing = jnp.concatenate([downward, upward], axis=1)
    extended = padded_2(outgoing, (("gz", 1),), MIG)
    arrived = jnp.concatenate([extended[:, :MIG], extended[:, 3 * MIG :]], axis=1)
    staying = slot_index >= up_count + down_count
    retained = jnp.where(is_strength & ~staying[None, :], 0.0, packet)
    particles = jnp.concatenate([retained, arrived], axis=1)
    particle_total = particles.shape[1]
    block_rows = math.gcd(particle_total, 256)
    row_blocks = particles.T.reshape(particle_total // block_rows, block_rows, 7)
    planes = jnp.arange(slab_planes + 4, dtype=jnp.int32) - 2
    columns = jnp.arange(pencil_cols + 4, dtype=jnp.int32) - 2
    lateral = jnp.arange(NY, dtype=jnp.int32)

    def deposit(deposited, row_group):
        cell_ids = row_group[:, 6].astype(jnp.int32)
        z_cell = cell_ids // (pencil_cols * NY)
        x_cell = cell_ids // NY % pencil_cols
        y_cell = cell_ids % NY
        weight_z = kernel_weight(
            (planes[None, :] - z_cell[:, None]).astype(jnp.float32) - row_group[:, 3:4]
        )
        weight_x = kernel_weight(
            (columns[None, :] - x_cell[:, None]).astype(jnp.float32) - row_group[:, 4:5]
        )
        y_offset = (lateral[None, :] - y_cell[:, None] + NY // 2) % NY - NY // 2
        weight_y = kernel_weight(y_offset.astype(jnp.float32) - row_group[:, 5:6])
        spread = (
            row_group[:, 0:3, None, None] * weight_z[:, None, :, None] * weight_x[:, None, None, :]
        )
        spread = spread.reshape(block_rows, -1)
        added = lax.dot_general(
            spread,
            weight_y,
            (((0,), (0,)), ((), ())),
            precision=highest,
            preferred_element_type=jnp.float32,
        )
        return (deposited + added, None)

    start_mesh = jnp.zeros((3 * (slab_planes + 4) * (pencil_cols + 4), NY), jnp.float32)
    deposited, _ = lax.scan(deposit, start_mesh, row_blocks)
    deposited = deposited.reshape(3, slab_planes + 4, pencil_cols + 4, NY)
    plane_rim = jnp.concatenate([deposited[:, :2], deposited[:, slab_planes + 2 :]], axis=1)
    plane_rim = padded_2(plane_rim, (("gz", 1),), 2)
    interior = deposited[:, 2 : slab_planes + 2]
    interior = (
        interior.at[:, :2].add(plane_rim[:, :2]).at[:, slab_planes - 2 :].add(plane_rim[:, 6:])
    )
    column_rim = jnp.concatenate([interior[:, :, :2], interior[:, :, pencil_cols + 2 :]], axis=2)
    column_rim = padded_2(column_rim, (("gx", 2),), 2)
    interior = interior[:, :, 2 : pencil_cols + 2]
    interior = (
        interior.at[:, :, :2]
        .add(column_rim[:, :, :2])
        .at[:, :, pencil_cols - 2 :]
        .add(column_rim[:, :, 6:])
    )
    vorticity_mesh = ambient + interior
    table_y, table_back = halved_tables(NY, pencil_count)
    spectral = jnp.einsum("bzxy,yc->bzxc", vorticity_mesh, table_y, precision=highest)
    ahead_x_table = complex_table(NX, -1.0)
    ahead_z_table = complex_table(wake_cells, -1.0)
    back_x_table = complex_table(NX, 1.0)
    back_z_table = complex_table(wake_cells, 1.0)
    result = join_pairs(
        jnp.einsum(
            "qkrx,bzxrm->bzkqm",
            ahead_x_table,
            split_pairs(lax.all_to_all(spectral, "gx", split_axis=3, concat_axis=2, tiled=True)),
            precision=highest,
        )
    )
    result = reslot(result, pencil_index)
    spectral = result
    block_width = NX // slab_count
    spectral = join_pairs(
        jnp.einsum(
            "qkrz,bzxrm->bkxqm",
            ahead_z_table,
            split_pairs(lax.all_to_all(spectral, "gz", split_axis=2, concat_axis=1, tiled=True)),
            precision=highest,
        )
    )
    velocity_hat = packed_velocity(
        spectral, lax.axis_index("gz"), pencil_index, block_width, wake_cells
    )
    physical = join_pairs(
        jnp.einsum("qkrz,bzxrm->bkxqm", back_z_table, split_pairs(velocity_hat), precision=highest)
    ) * (1.0 / wake_cells)
    pieces = lax.all_to_all(physical, "gz", split_axis=1, concat_axis=2, tiled=True)
    pieces = unslot(pieces, pencil_index)
    physical = join_pairs(
        jnp.einsum("qkrx,bzxrm->bzkqm", back_x_table, split_pairs(pieces), precision=highest)
    ) * (1.0 / NX)
    velocity = jnp.einsum(
        "bzxc,cy->bzxy",
        lax.all_to_all(physical, "gx", split_axis=2, concat_axis=3, tiled=True),
        table_back,
        precision=highest,
    )
    padded = padded_2(velocity, (("gz", 1), ("gx", 2)), 1)
    along_z = (padded[:, 2:, 1:-1] - padded[:, :-2, 1:-1]) * 0.5
    along_x = (padded[:, 1:-1, 2:] - padded[:, 1:-1, :-2]) * 0.5
    along_y = (jnp.roll(velocity, -1, axis=3) - jnp.roll(velocity, 1, axis=3)) * 0.5
    stretch = (
        vorticity_mesh[0] * along_z + vorticity_mesh[1] * along_x + vorticity_mesh[2] * along_y
    )
    return (velocity, vorticity_mesh + time_step * stretch)


def solution(mesh):
    placed = (
        P(None, ("gz", "gx")),
        P(None, ("gz", "gx")),
        P(("gz", "gx")),
        P("gz", "gx", None),
        P(None, "gz", "gx", None),
    )
    return jax.shard_map(
        on_device,
        mesh=mesh,
        in_specs=placed,
        out_specs=(P(None, "gz", "gx", None), P(None, "gz", "gx", None)),
        check_vma=False,
    )
```

profile of v0, /device:TPU:0, one launch (start us, length us, event | category | flops | bytes accessed | tf_op | source)
XLA Modules:
  0.0 505.6 jit_solution(12631410296446536182)
XLA Ops:
  8.1 2.9 collective-permute-start
  11.0 3.1 collective-permute-start.1
  15.7 28.0 %while.24 = (s32[]{:T(128)}, f32[2448,256]{1,0:T(8,128)}, f32[5,128,7]{1,2,0:T(8,128)S(1)}, s32[]{:T(128)}, s32[]{:T(128)}) while((s32[]{:T(128)}, f32[2448,256]{1,0:T(8,128)}, f32[5,128,7]{1,2,0:T(8,128)S(1)}, s32[]{:T(128)}, s32[]{:T(128)}) %tuple.143), condition=%wide.region_1.2_spmd.clone, body=%wide.region_0.1_spmd.clone.sunk | while | flops 965456192 | bytes 10168011 | solution.py:269
  16.2 3.8 convolution_add_fusion.2
  20.4 5.5 %convolution_add_fusion.2 = f32[2448,256]{1,0:T(8,128)} fusion(f32[128,2448]{0,1:T(8,128)S(1)} %mul.1479, f32[2448,256]{1,0:T(8,128)} %get-tuple-element.406, pred[]{:T(512)S(6)} %compare.123, f32[128]{0:T(128)S(1)} %get-tuple-element.398, s32[128]{0:T(128)S(1)} %get-tuple-element.399), kind=kOutput, calls=%fused_computation.3.clone.1 | convolution fusion | flops 964927488 | bytes 6267905 | tf_op jit(solution)/shard_map/while/body/eval_jaxpr/dot_general | solution.py:259
  26.4 5.5 %convolution_add_fusion.2 = f32[2448,256]{1,0:T(8,128)} fusion(f32[128,2448]{0,1:T(8,128)S(1)} %mul.1479, f32[2448,256]{1,0:T(8,128)} %get-tuple-element.406, pred[]{:T(512)S(6)} %compare.123, f32[128]{0:T(128)S(1)} %get-tuple-element.398, s32[128]{0:T(128)S(1)} %get-tuple-element.399), kind=kOutput, calls=%fused_computation.3.clone.1 | convolution fusion | flops 964927488 | bytes 6267905 | tf_op jit(solution)/shard_map/while/body/eval_jaxpr/dot_general | solution.py:259
  32.3 5.5 %convolution_add_fusion.2 = f32[2448,256]{1,0:T(8,128)} fusion(f32[128,2448]{0,1:T(8,128)S(1)} %mul.1479, f32[2448,256]{1,0:T(8,128)} %get-tuple-element.406, pred[]{:T(512)S(6)} %compare.123, f32[128]{0:T(128)S(1)} %get-tuple-element.398, s32[128]{0:T(128)S(1)} %get-tuple-element.399), kind=kOutput, calls=%fused_computation.3.clone.1 | convolution fusion | flops 964927488 | bytes 6267905 | tf_op jit(solution)/shard_map/while/body/eval_jaxpr/dot_general | solution.py:259
  38.2 5.5 %convolution_add_fusion.2 = f32[2448,256]{1,0:T(8,128)} fusion(f32[128,2448]{0,1:T(8,128)S(1)} %mul.1479, f32[2448,256]{1,0:T(8,128)} %get-tuple-element.406, pred[]{:T(512)S(6)} %compare.123, f32[128]{0:T(128)S(1)} %get-tuple-element.398, s32[128]{0:T(128)S(1)} %get-tuple-element.399), kind=kOutput, calls=%fused_computation.3.clone.1 | convolution fusion | flops 964927488 | bytes 6267905 | tf_op jit(solution)/shard_map/while/body/eval_jaxpr/dot_general | solution.py:259
  47.7 3.4 collective-permute-start.3
  51.2 13.9 %collective-permute-done.2 = f32[3,2,68,256]{3,2,1,0:T(8,128)S(1)} collective-permute-done((f32[3,2,68,256]{3,2,1,0:T(8,128)S(1)}, f32[3,2,68,256]{3,2,1,0:T(8,128)S(1)}, u32[]{:S(2)}, u32[]{:S(2)}) %collective-permute-start.2) | collective-permute-done | bytes 417824 | tf_op jit(solution)/shard_map/ppermute | solution.py:25
  72.8 3.6 fusion.107
  78.7 3.0 reshape.1395
  81.7 4.1 all-to-all-start
  89.3 16.6 %all-to-all-done = f32[4,1,98304]{2,1,0:T(1,128)S(1)} async-done(((f32[4,1,98304]{2,1,0:T(1,128)}), f32[4,1,98304]{2,1,0:T(1,128)S(1)}, u32[]{:S(2)}, u32[]{:S(2)}) %all-to-all-start) | async-done | bytes 1572896 | tf_op jit(solution)/shard_map/all_to_all | solution.py:297
  106.3 6.3 %reduce.20 = f32[4,98304]{1,0:T(4,128)} reduce(f32[4,1,98304]{2,1,0:T(1,128)S(1)} %all-to-all-done, f32[]{:T(128)} %broadcast.2003), dimensions={1}, to_apply=%all_to_all.48.reduce_sub_computation | reduce | bytes 3145732 | tf_op jit(solution)/shard_map/all_to_all | solution.py:297
  115.5 3.7 copy.149
  119.1 3.5 reshape.1381
  133.8 20.7 %scatter.20 = f32[3,8,256,64]{3,1,0,2:T(8,128)S(1)} dynamic-update-slice(f32[3,8,256,64]{3,1,0,2:T(8,128)S(1)} %copy.92, f32[3,8,256,1]{3,1,0,2:T(8,128)} %copy.93, s32[]{:T(128)} %constant.600.clone.1, s32[]{:T(128)} %constant.600.clone.1, s32[]{:T(128)} %constant.600.clone.1, s32[]{:T(128)} %constant.600.clone.1) | dynamic-update-slice | bytes 49156 | tf_op jit(solution)/shard_map/scatter | solution.py:119
  154.5 72.1 %scatter.21 = f32[3,8,256,64]{3,1,0,2:T(8,128)S(1)} dynamic-update-slice(f32[3,8,256,64]{3,1,0,2:T(8,128)S(1)} %scatter.20, f32[3,8,256,1]{3,1,0,2:T(8,128)} %copy.94, s32[]{:T(128)} %constant.600.clone.1, s32[]{:T(128)} %constant.600.clone.1, s32[]{:T(128)} %constant.600.clone.1, s32[]{:T(128)} %constant.602.clone.1) | dynamic-update-slice | bytes 49156 | tf_op jit(solution)/shard_map/scatter | solution.py:120
  226.7 3.0 reshape.1397
  229.6 5.5 %all-to-all-start.1 = ((f32[8,1,49152]{2,1,0:T(1,128)}), f32[8,1,49152]{2,1,0:T(1,128)S(1)}, u32[]{:S(2)}, u32[]{:S(2)}) async-start(f32[8,1,49152]{2,1,0:T(1,128)} %reshape.1397), calls=%async_computation.1 | async-start | bytes 3145728 | tf_op jit(solution)/shard_map/all_to_all | solution.py:308
  237.5 3.2 divide_select_fusion
  240.7 31.3 %all-to-all-done.1 = f32[8,1,49152]{2,1,0:T(1,128)S(1)} async-done(((f32[8,1,49152]{2,1,0:T(1,128)}), f32[8,1,49152]{2,1,0:T(1,128)S(1)}, u32[]{:S(2)}, u32[]{:S(2)}) %all-to-all-start.1) | async-done | bytes 1572896 | tf_op jit(solution)/shard_map/all_to_all | solution.py:308
  271.9 6.1 %reduce.21 = f32[8,49152]{1,0:T(8,128)} reduce(f32[8,1,49152]{2,1,0:T(1,128)S(1)} %all-to-all-done.1, f32[]{:T(128)} %broadcast.2003), dimensions={1}, to_apply=%all_to_all.51.reduce_sub_computation | reduce | bytes 3145732 | tf_op jit(solution)/shard_map/all_to_all | solution.py:308
  283.0 7.1 %reshape.1376 = f32[3,64,32,2,32]{4,3,2,1,0:T(2,128)} reshape(f32[3,8,8,32,64]{4,3,2,1,0:T(8,128)} %copy.96) | data formatting | bytes 3145728 | tf_op jit(solution)/shard_map/reshape | solution.py:61
  290.1 15.8 %fusion.70 = f32[3,32,32,2,64,1]{4,2,5,3,1,0:T(8,128)S(1)} fusion(f32[3,64,32,2,32,1]{4,3,2,1,0,5:T(2,128)} %bitcast.191, f32[1,64,2,64]{3,1,2,0:T(8,128)S(1)} %get-tuple-element.325, f32[1,64,2,64]{3,1,2,0:T(8,128)S(1)} %get-tuple-element.328), kind=kOutput, calls=%fused_computation.103 | convolution fusion | flops 603996160 | bytes 3211264 | tf_op jit(solution)/shard_map/qkrz,bzxrm->bkxqm/dot_general | solution.py:305
  305.8 4.1 copy.98
  312.7 3.8 broadcast_multiply_fusion.2
  319.5 3.6 fusion.69
  326.4 6.5 %copy.121 = f32[3,64,32,2,32,1]{1,4,3,5,2,0:T(8,128)} copy(f32[3,64,32,2,32,1]{2,1,0,4,3,5:T(8,128)} %bitcast.47) | data formatting | bytes 3145728 | tf_op jit(solution)/shard_map/reshape | solution.py:61
  332.8 4.5 bitcast_multiply_fusion
  340.0 3.8 reshape.1399
  343.9 40.7 %all_to_all.66 = f32[8,1,49152]{2,1,0:T(1,128)S(1)} all-to-all(f32[8,1,49152]{2,1,0:T(1,128)S(1)} %reshape.1399), channel_id=1, replica_groups=mesh['gz'=8,'gx'=4] {'gz'}, dimensions={0} | all-to-all | bytes 3145728 | tf_op jit(solution)/shard_map/all_to_all | solution.py:318
  384.6 4.3 reduce.22
  394.1 3.8 fusion.218
  405.5 9.3 %scatter.26 = f32[3,8,256,64]{3,2,1,0:T(8,128)S(1)} dynamic-update-slice(f32[3,8,256,64]{3,2,1,0:T(8,128)S(1)} %bitcast.193, f32[3,8,256,1]{3,2,1,0:T(8,128)} %copy.109, s32[]{:T(128)} %constant.600.clone.1, s32[]{:T(128)} %constant.600.clone.1, s32[]{:T(128)} %constant.600.clone.1, s32[]{:T(128)} %constant.600.clone.1) | dynamic-update-slice | bytes 49156 | tf_op jit(solution)/shard_map/scatter | solution.py:143
  417.0 11.2 %scatter.29 = f32[3,8,256,64]{3,2,1,0:T(8,128)S(1)} dynamic-update-slice(f32[3,8,256,64]{3,2,1,0:T(8,128)S(1)} %scatter.26, f32[3,8,256,1]{3,2,1,0:T(8,128)} %copy.110, s32[]{:T(128)} %constant.600.clone.1, s32[]{:T(128)} %constant.600.clone.1, s32[]{:T(128)} %constant.600.clone.1, s32[]{:T(128)} %constant.602.clone.1) | dynamic-update-slice | bytes 49156 | tf_op jit(solution)/shard_map/scatter | solution.py:144
  430.2 5.5 %bitcast_multiply_fusion.1 = f32[3,8,32,2,256]{4,2,3,1,0:T(8,128)} fusion(f32[3,8,256,2,32,1]{2,4,3,5,1,0:T(8,128)} %bitcast.208, f32[1,256,2,256]{3,1,2,0:T(8,128)} %get-tuple-element.309, f32[1,256,2,256]{3,1,2,0:T(8,128)} %get-tuple-element.304), kind=kOutput, calls=%fused_computation.131 | convolution fusion | flops 2416574464 | bytes 4194304 | tf_op jit(solution)/shard_map/qkrx,bzxrm->bzkqm/dot_general | solution.py:321
  438.2 3.0 reshape.1401
  441.1 3.7 all-to-all-start.3
  446.1 18.7 %all-to-all-done.3 = f32[4,1,98304]{2,1,0:T(1,128)S(1)} async-done(((f32[4,1,98304]{2,1,0:T(1,128)}), f32[4,1,98304]{2,1,0:T(1,128)S(1)}, u32[]{:S(2)}, u32[]{:S(2)}) %all-to-all-start.3) | async-done | bytes 1572896 | tf_op jit(solution)/shard_map/all_to_all | solution.py:325
  464.9 6.3 %reduce.23 = f32[4,98304]{1,0:T(4,128)} reduce(f32[4,1,98304]{2,1,0:T(1,128)S(1)} %all-to-all-done.3, f32[]{:T(128)} %broadcast.2003), dimensions={1}, to_apply=%all_to_all.58.reduce_sub_computation | reduce | bytes 3145732 | tf_op jit(solution)/shard_map/all_to_all | solution.py:325
  471.2 4.5 reshape.1402
  475.7 5.6 %copy.148 = f32[3,8,4,64,64]{4,2,3,1,0:T(4,128)} copy(f32[3,8,4,64,64]{4,1,0,3,2:T(8,128)} %bitcast.204) | data formatting | bytes 3145728 | tf_op jit(solution)/shard_map/all_to_all | solution.py:325
  481.3 3.5 all_to_all.61
  490.5 3.5 collective-permute-done.6
  494.0 4.8 collective-permute-done.7
  502.3 3.1 fusion.77
  (225 shorter events, 88.1 us)
Async XLA Ops:
  8.1 7.6 %collective-permute-start = (f32[7,64]{1,0:T(8,128)S(1)}, f32[7,64]{1,0:T(8,128)S(1)}, u32[]{:S(2)}, u32[]{:S(2)}) collective-permute-start(f32[7,64]{1,0:T(8,128)S(1)} %get-tuple-element.330), channel_id=1, source_target_pairs={{0,4},{4,8},{8,12},{12,16},{16,20},{20,24},{24,28},{28,0},{1,5},{5... | collective-permute-start | bytes 5384 | tf_op jit(solution)/shard_map/ppermute | solution.py:25
  11.0 4.6 collective-permute-start.1
  46.2 19.0 %collective-permute-start.2 = (f32[3,2,68,256]{3,2,1,0:T(8,128)S(1)}, f32[3,2,68,256]{3,2,1,0:T(8,128)S(1)}, u32[]{:S(2)}, u32[]{:S(2)}) collective-permute-start(f32[3,2,68,256]{3,2,1,0:T(8,128)S(1)} %get-tuple-element.288), channel_id=1, source_target_pairs={{0,4},{4,8},{8,12},{12,16},{16,20},{20,24},{24,28},{28,0},{1,5},{5... | collective-permute-start | bytes 1253384 | tf_op jit(solution)/shard_map/ppermute | solution.py:25
  47.7 19.7 %collective-permute-start.3 = (f32[3,2,68,256]{3,2,1,0:T(8,128)S(1)}, f32[3,2,68,256]{3,2,1,0:T(8,128)S(1)}, u32[]{:S(2)}, u32[]{:S(2)}) collective-permute-start(f32[3,2,68,256]{3,2,1,0:T(8,128)S(1)} %get-tuple-element.287), channel_id=1, source_target_pairs={{4,0},{8,4},{12,8},{16,12},{20,16},{24,20},{28,24},{0,28},{5,1},{9... | collective-permute-start | bytes 1253384 | tf_op jit(solution)/shard_map/ppermute | solution.py:27
  67.5 3.9 copy-start.10
  67.5 3.6 collective-permute-start.4
  67.6 4.1 copy-start.11
  67.8 3.5 collective-permute-start.5
  71.7 1.2 copy-start.1
  81.7 24.1 %all-to-all-start = ((f32[4,1,98304]{2,1,0:T(1,128)}), f32[4,1,98304]{2,1,0:T(1,128)S(1)}, u32[]{:S(2)}, u32[]{:S(2)}) async-start(f32[4,1,98304]{2,1,0:T(1,128)} %reshape.1395), calls=%async_computation | async-start | bytes 3145728 | tf_op jit(solution)/shard_map/all_to_all | solution.py:297
  85.8 43.4 %copy-start.13 = (pred[256]{0:T(512)(128)(4,1)}, pred[256]{0:T(512)(128)(4,1)S(1)}, u32[]{:S(2)}) copy-start(pred[256]{0:T(512)(128)(4,1)S(1)} %get-tuple-element.361) | copy-start | bytes 772
  85.9 43.4 %copy-start.15 = (pred[256]{0:T(512)(128)(4,1)}, pred[256]{0:T(512)(128)(4,1)S(1)}, u32[]{:S(2)}) copy-start(pred[256]{0:T(512)(128)(4,1)S(1)} %get-tuple-element.362) | copy-start | bytes 772
  119.1 3.5 copy-start.8
  119.1 3.5 copy-start.9
  125.4 1.1 copy-start.4
  229.6 42.3 %all-to-all-start.1 = ((f32[8,1,49152]{2,1,0:T(1,128)}), f32[8,1,49152]{2,1,0:T(1,128)S(1)}, u32[]{:S(2)}, u32[]{:S(2)}) async-start(f32[8,1,49152]{2,1,0:T(1,128)} %reshape.1397), calls=%async_computation.1 | async-start | bytes 3145728 | tf_op jit(solution)/shard_map/all_to_all | solution.py:308
  309.9 2.3 copy-start.17
  311.0 1.7 copy-start.3
  318.8 0.7 copy-start.18
  319.5 3.6 copy-start.19
  400.2 3.0 copy-start.14
  400.2 3.0 copy-start.16
  441.1 3.7 copy-start.2
  441.1 23.7 %all-to-all-start.3 = ((f32[4,1,98304]{2,1,0:T(1,128)}), f32[4,1,98304]{2,1,0:T(1,128)S(1)}, u32[]{:S(2)}, u32[]{:S(2)}) async-start(f32[4,1,98304]{2,1,0:T(1,128)} %reshape.1401), calls=%async_computation.3 | async-start | bytes 3145728 | tf_op jit(solution)/shard_map/all_to_all | solution.py:325
  481.3 3.5 copy-start.12
  487.4 14.8 %copy-start = (f32[3,8,64,256]{3,2,1,0:T(8,128)}, f32[3,8,64,256]{3,2,1,0:T(8,128)S(1)}, u32[]{:S(2)}) copy-start(f32[3,8,64,256]{3,2,1,0:T(8,128)S(1)} %fusion.105) | copy-start | bytes 4718596
  487.5 6.5 %collective-permute-start.6 = (f32[3,1,64,256]{3,2,1,0:T(8,128)S(1)}, f32[3,1,64,256]{3,2,1,0:T(8,128)S(1)}, u32[]{:S(2)}, u32[]{:S(2)}) collective-permute-start(f32[3,1,64,256]{3,2,1,0:T(8,128)S(1)} %get-tuple-element.301), channel_id=1, source_target_pairs={{4,0},{8,4},{12,8},{16,12},{20,16},{24,20},{28,24},{0,28},{5,1},{9... | collective-permute-start | bytes 589832 | tf_op jit(solution)/shard_map/ppermute | solution.py:27
  489.9 8.9 %collective-permute-start.7 = (f32[3,1,64,256]{3,2,1,0:T(8,128)S(1)}, f32[3,1,64,256]{3,2,1,0:T(8,128)S(1)}, u32[]{:S(2)}, u32[]{:S(2)}) collective-permute-start(f32[3,1,64,256]{3,2,1,0:T(8,128)S(1)} %get-tuple-element.300), channel_id=1, source_target_pairs={{0,4},{4,8},{8,12},{12,16},{16,20},{20,24},{24,28},{28,0},{1,5},{5... | collective-permute-start | bytes 589832 | tf_op jit(solution)/shard_map/ppermute | solution.py:25
  490.4 11.8 %copy-start.5 = (f32[8,64,256]{2,1,0:T(8,128)S(1)}, f32[8,64,256]{2,1,0:T(8,128)}, u32[]{:S(2)}) copy-start(f32[8,64,256]{2,1,0:T(8,128)} %get-tuple-element.293) | copy-start | bytes 1572868
  490.5 11.8 %copy-start.6 = (f32[8,64,256]{2,1,0:T(8,128)S(1)}, f32[8,64,256]{2,1,0:T(8,128)}, u32[]{:S(2)}) copy-start(f32[8,64,256]{2,1,0:T(8,128)} %get-tuple-element.294) | copy-start | bytes 1572868
  490.5 11.8 %copy-start.7 = (f32[8,64,256]{2,1,0:T(8,128)S(1)}, f32[8,64,256]{2,1,0:T(8,128)}, u32[]{:S(2)}) copy-start(f32[8,64,256]{2,1,0:T(8,128)} %get-tuple-element.295) | copy-start | bytes 1572868
  498.8 1.6 collective-permute-start.8
  498.9 3.4 collective-permute-start.9
where the time goes:
time: 513 us; the launch traced here: 506 us
  local copies, waits for them, and re-layouts  218 us (42%)
  waiting for transfers between devices  96.7 us (19%)
  matrix products  60.2 us (12%)
  other arithmetic  55.7 us (11%)
  blocking collectives  40.7 us (8%)
  starting transfers between devices  29 us (6%)
    scatter x1, local copies, waits for them, and re-layouts, reslot(): values.at[..., mode_count].set(jnp.where(first_pencil, new_imag, imag_part))  72.1 us
    all_to_all x1, blocking collectives, on_device(): lax.all_to_all(physical, 'gz', split_axis=1, concat_axis=2, tiled=True)  40.7 us
    unnamed x56, local copies, waits for them, and re-layouts  33.5 us
    all_to_all x1, waiting for transfers between devices, on_device(): lax.all_to_all(spectral, 'gz', split_axis=2, concat_axis=1, tiled=True)  31.3 us
    dot_general x5, matrix products, deposit(): lax.dot_general(spread, weight_y, (((0,), (0,)), ((), ())), precision=hig...  25.6 us
    ppermute x5, waiting for transfers between devices, padded_2(): lax.ppermute(tail, axis, [(i, (i + 1) % count) for i in range(count)])  23.6 us
    scatter x1, local copies, waits for them, and re-layouts, reslot(): values = values.at[..., 0].set(jnp.where(first_pencil, new_real, real_part))  20.7 us
    all_to_all x1, waiting for transfers between devices, on_device(): lax.all_to_all(physical, 'gx', split_axis=2, concat_axis=3, tiled=True)  18.7 us
  transfers between devices with their start and end apart: 13, of which 12 were waited for; matrix products, arithmetic and copies ran while one was open for 2% of the time, Pallas kernels for 0%

commit v1 on v0

v1 whole, which is shorter than its diff:
```python
import functools
import math

import jax
import jax.numpy as jnp
import ml_dtypes
import numpy as np
from jax import lax
from jax.experimental import pallas as pl
from jax.experimental.pallas import tpu as pltpu
from jax.sharding import PartitionSpec as P

MIG = 64
LANES = 128
RIM = 8
TIME_STEP = 0.25
VMEM = 48 * 1024 * 1024
F32 = jnp.float32
BF16 = jnp.bfloat16


def split_table(table):
    high = table.astype(np.float32).astype(ml_dtypes.bfloat16)
    low = (table - high.astype(np.float64)).astype(np.float32).astype(ml_dtypes.bfloat16)
    return high, low


def angles(rows, columns, extent):
    return 2.0 * np.pi * (np.multiply.outer(rows, columns) % extent) / extent


def y_tables(ny, pencils, scale):
    modes = ny // (2 * pencils)
    position = np.arange(ny)
    angle = angles(position, np.arange(ny // 2), ny)
    real, imag = np.cos(angle), -np.sin(angle)
    imag[:, 0] = 1.0 - 2.0 * (position % 2)
    weight = np.where(np.arange(ny // 2) == 0, 1.0, 2.0) * scale
    ahead = np.zeros((2, ny, pencils, 2, 2, modes))
    back = np.zeros((pencils, 2, 2, modes, 2, ny))
    for parity in range(2):
        for part, values in enumerate((real, imag)):
            ahead[parity, :, :, part, parity] = values.reshape(ny, pencils, modes)
            back[:, part, parity, :, parity] = (values * weight).T.reshape(pencils, modes, ny)
    return ahead.reshape(2 * ny, -1), back.reshape(-1, 2 * ny)


def wave_order(nx, slabs):
    half = nx // 2
    ahead = np.arange(half).reshape(slabs, 1, half // slabs)
    behind = np.where(ahead == 0, half, (nx - ahead) % nx)
    return np.concatenate([ahead, behind], axis=1).reshape(-1)


def x_tables(nx, cols, pencils, slabs):
    order = wave_order(nx, slabs)
    angle = angles(order, np.arange(nx), nx)
    ahead = np.concatenate([np.cos(angle), np.sin(angle)], axis=0)
    row = np.arange(cols + RIM)
    offset = np.where(row <= cols, row, -1)
    used = ((row <= cols) | (row == cols + RIM - 1)).astype(np.float64)
    place = (np.arange(pencils)[:, None] * cols + offset[None, :]) % nx
    angle = angles(place.reshape(-1), order, nx)
    mask = np.tile(used, pencils)[:, None]
    back = np.concatenate([np.cos(angle) * mask, np.sin(angle) * mask], axis=0)
    return ahead, back


def split(values):
    high = values.astype(BF16)
    return high, (values - high.astype(F32)).astype(BF16)


def dot(left, right):
    return jnp.dot(left, right, preferred_element_type=F32)


def table_left(high, low, values):
    v_high, v_low = split(values)
    return dot(high, v_high) + (dot(high, v_low) + dot(low, v_high))


def table_right(values, high, low):
    v_high, v_low = split(values)
    return dot(v_high, high) + (dot(v_low, high) + dot(v_high, low))


def lane_of():
    return lax.broadcasted_iota(jnp.int32, (1, LANES), 1)


def times_i(values):
    half = LANES // 2
    sign = jnp.where(lane_of() < half, -1.0, 1.0).astype(F32)
    return pltpu.roll(values, half, 1) * sign


def parity_swap(values):
    quarter = LANES // 4
    even = (lane_of() // quarter) % 2 == 0
    return jnp.where(
        even, pltpu.roll(values, LANES - quarter, 1), pltpu.roll(values, quarter, 1)
    )


def kernel_weight(distance):
    radius = jnp.abs(distance)
    near = 1.0 - 2.5 * radius * radius + 1.5 * radius * radius * radius
    far = 0.5 * (2.0 - radius) * (2.0 - radius) * (1.0 - radius)
    return jnp.where(radius < 1.0, near, jnp.where(radius < 2.0, far, 0.0))


def turned(values, wave, extent, sign):
    real = math.cos(2.0 * math.pi * wave / extent)
    imag = sign * math.sin(2.0 * math.pi * wave / extent)
    if wave == 0:
        return values
    if 4 * wave == extent:
        return times_i(values) * imag
    return values * real + times_i(values) * imag


def fft(values, sign):
    count = len(values)
    if count == 1:
        return values
    even, odd = fft(values[::2], sign), fft(values[1::2], sign)
    odd = [turned(v, k, count, sign) for k, v in enumerate(odd)]
    return [a + b for a, b in zip(even, odd)] + [a - b for a, b in zip(even, odd)]


def deposit_kernel(
    chunks, own, up1, down1, up2, down2, ambient, t_high, t_low, mesh, rim_high, rim_low, *rest
):
    parts, total = rest[: len(chunks)], rest[len(chunks)]
    _, planes, cols, ny = ambient.shape
    rows = cols + RIM
    movers = up2.shape[1]
    count = own.shape[1]

    def decode(ref, start, stop, shift):
        packet = ref[:, start:stop]
        cell = packet[6:7].astype(jnp.int32)
        move = packet[7:8].astype(jnp.int32)
        z_cell = lax.div(cell, cols * ny) + planes * (move + shift)
        x_cell = lax.rem(lax.div(cell, ny), cols)
        return packet[0:6], z_cell, x_cell, lax.rem(cell, ny)

    def joined(pieces):
        return [jnp.concatenate(p, axis=1) if len(p) > 1 else p[0] for p in zip(*pieces)]

    def add_block(pieces, first, used):
        values, z_cell, x_cell, y_cell = joined(pieces)
        width = values.shape[1]
        z_at = lax.broadcasted_iota(jnp.int32, (8, width), 0) + first
        w_z = kernel_weight((z_at - z_cell).astype(F32) - values[3:4])
        row = lax.broadcasted_iota(jnp.int32, (rows, width), 0)
        x_at = jnp.where(row < cols + 2, row, jnp.where(row >= rows - 2, row - rows, 4 * rows))
        w_x = kernel_weight((x_at - x_cell).astype(F32) - values[4:5])
        y_at = lax.broadcasted_iota(jnp.int32, (ny, width), 0)
        y_off = lax.rem(y_at - y_cell + (ny + ny // 2), ny) - ny // 2
        w_y = kernel_weight(y_off.astype(F32) - values[5:6])
        y_high, y_low = split(w_y)
        right = jnp.concatenate([y_high, y_high, y_low], axis=1)
        for c in range(3):
            s_z = values[c : c + 1] * w_z
            left = jnp.concatenate([s_z[k : k + 1] * w_x for k in range(used)], axis=0)
            l_high, l_low = split(left)
            left = jnp.concatenate([l_high, l_low, l_high], axis=1)
            added = lax.dot_general(
                left, right, (((1,), (1,)), ((), ())), preferred_element_type=F32
            )
            total[c, first : first + used] += added.reshape(used, rows, ny)

    total[:, :, 0:cols] = ambient[...]
    total[:, :, cols:rows] = jnp.zeros((3, planes, RIM, ny), F32)
    step = 256
    for at in range(0, count, step):
        add_block([decode(own, at, min(at + step, count), 0)], 0, planes)
    add_block([decode(up1, 0, movers, 1), decode(down1, 0, movers, -1)], 0, planes)
    for near, far, shift, first in ((up1, up2, 1, planes - 2), (down1, down2, -1, 0)):
        whole = [decode(near, movers, count, shift), decode(far, 0, movers, 2 * shift)]
        values, z_cell, x_cell, y_cell = joined(whole)
        for at in range(0, count, step):
            to = min(at + step, count)
            block = (values[:, at:to], z_cell[:, at:to], x_cell[:, at:to], y_cell[:, at:to])
            add_block([block], first, 2)

    for c in range(3):
        for z in range(planes):
            at = 2 * (c * planes + z)
            mesh[c, z] = total[c, z, 0:cols]
            rim_high[at : at + 2] = total[c, z, cols : cols + 2]
            rim_low[at : at + 2] = total[c, z, rows - 2 : rows]
    for pairs, part in zip(chunks, parts):
        groups = [(c, pair) for c in range(3) for pair in pairs]
        left = jnp.concatenate(
            [
                jnp.concatenate([total[c, 2 * p], total[c, 2 * p + 1]], axis=1)
                for c, p in groups
            ],
            axis=0,
        )
        wide = table_right(left, t_high[...], t_low[...])
        for n in range(len(groups)):
            for g in range(part.shape[0]):
                part[g, :, n * LANES : (n + 1) * LANES] = wide[
                    n * rows : (n + 1) * rows, g * LANES : (g + 1) * LANES
                ]


def x_ahead_kernel(part, t_high, t_low, out):
    pencils, rows, width = part.shape
    cols = rows - RIM
    row = lax.broadcasted_iota(jnp.int32, (RIM, width), 0)
    pieces = []
    for h in range(pencils):
        from_low = part[(h - 1) % pencils, cols:rows]
        from_high = part[(h + 1) % pencils, cols:rows]
        pieces.append(part[h, 0:RIM] + jnp.where(row < 2, from_low, 0.0))
        pieces.append(part[h, RIM : cols - RIM])
        pieces.append(part[h, cols - RIM : cols] + jnp.where(row >= RIM - 2, from_high, 0.0))
    both = table_left(t_high[...], t_low[...], jnp.concatenate(pieces, axis=0))
    half = both.shape[0] // 2
    for n in range(width // LANES):
        lanes = slice(n * LANES, (n + 1) * LANES)
        out[:, lanes] = both[:half, lanes] - times_i(both[half:, lanes])


def x_back_kernel(part, t_high, t_low, out):
    pencils, rows, width = out.shape
    both = table_left(t_high[...], t_low[...], part[...])
    half = both.shape[0] // 2
    for n in range(width // LANES):
        lanes = slice(n * LANES, (n + 1) * LANES)
        made = both[:half, lanes] + times_i(both[half:, lanes])
        out[:, :, lanes] = made.reshape(pencils, rows, LANES)


def wake_kernel(chunks, nx, ny, place, *refs):
    count = len(chunks)
    parts, outs = refs[:count], refs[count : 2 * count]
    spectrum, curled = refs[2 * count :]
    slabs, block, _ = parts[0].shape
    pairs = sum(len(c) for c in chunks)
    extent = 2 * pairs * slabs
    length = extent // 2
    reach = block // 2
    tile = min(8, reach)
    modes = LANES // 4
    lane = lane_of()
    odd = (lane // modes) % 2 == 1
    odd_float = odd.astype(F32)
    butterfly = 1.0 - 2.0 * odd_float
    slot = {p: (n, i) for n, chunk in enumerate(chunks) for i, p in enumerate(chunk)}

    def lanes_at(c, pair):
        n, i = slot[pair]
        return n, pl.ds(pl.multiple_of((c * len(chunks[n]) + i) * LANES, LANES), LANES)

    def odd_turned(values, k, sign):
        if k == 0:
            return values
        real = math.cos(2.0 * math.pi * k / extent)
        imag = sign * math.sin(2.0 * math.pi * k / extent)
        return values * (1.0 + odd_float * (real - 1.0)) + times_i(values) * (odd_float * imag)

    def ahead(c, carry):
        for side in range(2):
            for top in range(0, reach, tile):
                rows = slice(side * reach + top, side * reach + top + tile)
                values = []
                for s in range(slabs):
                    for pair in range(pairs):
                        n, lanes = lanes_at(c, pair)
                        values.append(parts[n][s, rows, lanes])
                for k, v in enumerate(fft(values, -1.0)):
                    v = odd_turned(v, k, -1.0)
                    spectrum[c, side, k, top : top + tile] = v * butterfly + parity_swap(v)
        return carry

    lax.fori_loop(0, 3, ahead, 0)

    slab_at, pencil_at = place[0], place[1]
    j = lax.broadcasted_iota(jnp.int32, (reach, LANES), 0)
    wave_number = slab_at * reach + j
    mode = jnp.broadcast_to(lane % modes, (reach, LANES)) + pencil_at * modes
    wave_y = mode.astype(F32) * (2.0 * math.pi / ny)
    packed = mode == 0
    alone = wave_number == 0
    conjugate = jnp.where(lane < LANES // 2, 1.0, -1.0).astype(F32)
    pi_sq = math.pi * math.pi

    def curl_at(k, with_mirror):
        z_wave = k - length * odd.astype(jnp.int32)
        z_base = jnp.broadcast_to(z_wave, (reach, LANES)).astype(F32) * (2.0 * math.pi / extent)
        z_trim = jnp.where(z_wave == -length, 0.0, z_base)
        opposite = lax.rem(length - k, length)
        for side in range(2):
            if side == 0:
                x_base = wave_number.astype(F32) * (2.0 * math.pi / nx)
                x_trim = x_base
            else:
                x_base = jnp.where(alone, math.pi, wave_number.astype(F32) * (-2.0 * math.pi / nx))
                x_trim = jnp.where(alone, 0.0, x_base)
            base = z_base * z_base + x_base * x_base
            full = base + wave_y * wave_y
            empty = full == 0.0
            inverse = jnp.where(empty, 0.0, 1.0 / jnp.where(empty, 1.0, full))
            if with_mirror:
                other = 1.0 / (base + pi_sq)
                mirror = jnp.where(packed, 0.5 * (inverse - other), 0.0) * conjugate
                inverse = jnp.where(packed, 0.5 * (inverse + other), inverse)
            stream = []
            for c in range(3):
                value = spectrum[c, side, k] * inverse
                if with_mirror:
                    across = jnp.where(
                        alone, spectrum[c, side, opposite], spectrum[c, 1 - side, opposite]
                    )
                    across = jnp.where(k == 0, across, parity_swap(across))
                    value = value + mirror * across
                stream.append(value)
            curled[0, side, k] = times_i(x_trim * stream[2] - wave_y * stream[1])
            curled[1, side, k] = times_i(wave_y * stream[0] - z_trim * stream[2])
            curled[2, side, k] = times_i(z_trim * stream[1] - x_trim * stream[0])

    def curl_all(with_mirror):
        def body(k, carry):
            curl_at(k, with_mirror)
            return carry

        lax.fori_loop(0, length, body, 0)

    @pl.when(pencil_at == 0)
    def _():
        curl_all(True)

    @pl.when(pencil_at != 0)
    def _():
        curl_all(False)

    def back(c, carry):
        for side in range(2):
            for top in range(0, reach, tile):
                rows = slice(side * reach + top, side * reach + top + tile)
                values = []
                for k in range(length):
                    v = curled[c, side, k, top : top + tile]
                    values.append(odd_turned(v * butterfly + parity_swap(v), k, 1.0))
                for z, v in enumerate(fft(values, 1.0)):
                    n, lanes = lanes_at(c, z % pairs)
                    outs[n][z // pairs, rows, lanes] = v
        return carry

    lax.fori_loop(0, 3, back, 0)


def planes_of(part, pairs, t_high, t_low):
    pencils, rows, _ = part.shape
    ny = t_high.shape[1] // 2
    groups = [(c, pair) for c in range(3) for pair in pairs]
    left = jnp.concatenate(
        [
            jnp.concatenate(
                [part[h, :, n * LANES : (n + 1) * LANES] for h in range(pencils)], axis=1
            )
            for n in range(len(groups))
        ],
        axis=0,
    )
    wide = table_right(left, t_high[...], t_low[...])
    made = {}
    for n, (c, pair) in enumerate(groups):
        for parity in range(2):
            made[c, 2 * pair + parity] = wide[
                n * rows : (n + 1) * rows, parity * ny : (parity + 1) * ny
            ]
    return made


def edge_kernel(pairs, part, t_high, t_low, out, first, last):
    listed = [2 * pair + parity for pair in pairs for parity in range(2)]
    cols = first.shape[1]
    made = planes_of(part, pairs, t_high, t_low)
    for c in range(3):
        for n, z in enumerate(listed):
            out[c, n] = made[c, z]
        first[c] = made[c, listed[0]][0:cols]
        last[c] = made[c, listed[-1]][0:cols]


def stretch_kernel(
    edge_pairs, pairs, edges, part, before, after, mesh, low_rim, high_rim, t_high, t_low,
    velocity, vorticity, held
):
    _, planes, cols, ny = velocity.shape
    rows = cols + RIM

    def hold(c, z, value):
        velocity[c, z] = value[0:cols]
        held[c, z, RIM : RIM + rows] = value
        held[c, z, 0:RIM] = value[cols:rows]

    listed = [2 * pair + parity for pair in edge_pairs for parity in range(2)]
    for c in range(3):
        for n, z in enumerate(listed):
            hold(c, z, edges[c, n])
    for (c, z), value in planes_of(part, pairs, t_high, t_low).items():
        hold(c, z, value)
    for z in range(planes):
        for c in range(3):
            at = 2 * (c * planes + z)
            vorticity[c, z] = mesh[c, z]
            vorticity[c, z, 0:2] += low_rim[at : at + 2]
            vorticity[c, z, cols - 2 : cols] += high_rim[at : at + 2]
        omega = [vorticity[c, z] for c in range(3)]
        for c in range(3):
            value = velocity[c, z]
            ahead = velocity[c, z + 1] if z + 1 < planes else after[c]
            behind = velocity[c, z - 1] if z > 0 else before[c]
            along_z = (ahead - behind) * 0.5
            along_x = (
                held[c, z, RIM + 1 : RIM + 1 + cols] - held[c, z, RIM - 1 : RIM - 1 + cols]
            ) * 0.5
            along_y = (pltpu.roll(value, ny - 1, 1) - pltpu.roll(value, 1, 1)) * 0.5
            stretch = omega[0] * along_z + omega[1] * along_x + omega[2] * along_y
            vorticity[c, z] = omega[c] + TIME_STEP * stretch


def call(kernel, outs, scratch=(), scalars=0, inputs=0):
    vmem = pl.BlockSpec(memory_space=pltpu.VMEM)
    smem = pl.BlockSpec(memory_space=pltpu.SMEM)
    return pl.pallas_call(
        kernel,
        out_shape=[jax.ShapeDtypeStruct(shape, F32) for shape in outs],
        in_specs=[smem] * scalars + [vmem] * inputs,
        out_specs=[vmem] * len(outs),
        scratch_shapes=[pltpu.VMEM(shape, F32) for shape in scratch],
        compiler_params=pltpu.CompilerParams(vmem_limit_bytes=VMEM),
    )


def ring(axis, step):
    count = lax.axis_size(axis)
    return [(i, (i + step) % count) for i in range(count)]


def exchange(values, axis):
    return lax.all_to_all(values, axis, split_axis=0, concat_axis=0, tiled=True)


def on_device(strength, offsets, cell_index, migrate_count, ambient):
    _, planes, cols, ny = ambient.shape
    slabs, pencils = lax.axis_size("gz"), lax.axis_size("gx")
    nx, nz, rows = cols * pencils, planes * slabs, cols + RIM
    pair_count = planes // 2
    edge = tuple(sorted({0, pair_count - 1}))
    chunks = (edge, tuple(range(1, pair_count - 1)))
    widths = [3 * len(c) * LANES for c in chunks]

    y_ahead, y_back = [
        split_table(t) for t in y_tables(ny, pencils, 1.0 / (float(nx) * ny * nz))
    ]
    x_ahead, x_back = [split_table(t) for t in x_tables(nx, cols, pencils, slabs)]

    slot = jnp.arange(strength.shape[1], dtype=jnp.int32)
    up_count = migrate_count[0, 0, 0]
    both_count = up_count + migrate_count[0, 0, 1]
    move = jnp.where(slot < up_count, 1.0, jnp.where(slot < both_count, -1.0, 0.0))
    packet = jnp.concatenate(
        [strength, offsets, cell_index.astype(F32)[None], move.astype(F32)[None]], axis=0
    )
    movers = packet[:, : 2 * MIG]
    up1 = lax.ppermute(packet, "gz", ring("gz", -1))
    down1 = lax.ppermute(packet, "gz", ring("gz", 1))
    up2 = lax.ppermute(movers, "gz", ring("gz", -2))
    down2 = lax.ppermute(movers, "gz", ring("gz", 2))

    rim = (6 * planes, ny)
    mesh, rim_high, rim_low, *parts = call(
        functools.partial(deposit_kernel, chunks),
        [ambient.shape, rim, rim] + [(pencils, rows, w) for w in widths],
        [(3, planes, rows, ny)],
        inputs=8,
    )(packet, up1, down1, up2, down2, ambient, *y_ahead)
    low_rim = lax.ppermute(rim_high, "gx", ring("gx", 1))
    high_rim = lax.ppermute(rim_low, "gx", ring("gx", -1))

    spectra = []
    for part, width in zip(parts, widths):
        part = exchange(part, "gx")
        (part,) = call(x_ahead_kernel, [(nx, width)], inputs=3)(part, *x_ahead)
        spectra.append(exchange(part.reshape(slabs, nx // slabs, width), "gz"))
    place = jnp.stack([lax.axis_index("gz"), lax.axis_index("gx")]).astype(jnp.int32)
    held = (3, 2, nz // 2, nx // (2 * slabs), LANES)
    spectra = call(
        functools.partial(wake_kernel, chunks, nx, ny),
        [s.shape for s in spectra],
        [held, held],
        scalars=1,
        inputs=len(spectra),
    )(place, *spectra)
    parts = []
    for part, width in zip(spectra, widths):
        part = exchange(part, "gz").reshape(nx, width)
        (part,) = call(x_back_kernel, [(pencils, rows, width)], inputs=3)(part, *x_back)
        parts.append(exchange(part, "gx"))
    plane = (3, cols, ny)
    edges, first, last = call(
        functools.partial(edge_kernel, chunks[0]),
        [(3, 2 * len(edge), rows, ny), plane, plane],
        inputs=3,
    )(parts[0], *y_back)
    after = lax.ppermute(first, "gz", ring("gz", -1))
    before = lax.ppermute(last, "gz", ring("gz", 1))
    return tuple(
        call(
            functools.partial(stretch_kernel, *chunks),
            [ambient.shape, ambient.shape],
            [(3, planes, cols + 2 * RIM, ny)],
            inputs=9,
        )(edges, parts[1], before, after, mesh, low_rim, high_rim, *y_back)
    )


def solution(mesh):
    placed = (
        P(None, ("gz", "gx")),
        P(None, ("gz", "gx")),
        P(("gz", "gx")),
        P("gz", "gx", None),
        P(None, "gz", "gx", None),
    )
    return jax.shard_map(
        on_device,
        mesh=mesh,
        in_specs=placed,
        out_specs=(P(None, "gz", "gx", None), P(None, "gz", "gx", None)),
        check_vma=False,
    )
```

time: 513 us -> 233 us (0.45); the launches traced: 506 us -> 232 us
  local copies, waits for them, and re-layouts: 218 us -> 9.46 us
  matrix products: 60.2 us -> 0 us
  Pallas kernels: 0 us -> 57.7 us
  other arithmetic: 55.7 us -> 2.14 us
  waiting for transfers between devices: 96.7 us -> 84.6 us
  starting transfers between devices: 29 us -> 39.3 us
    scatter x5 -> x0, local copies, waits for them, and re-layouts: 115 us -> none  [the longest x1 72.1 us: reslot(): values.at[..., mode_count].set(jnp.where(first_pencil, new_imag, imag_part))]
    dot_general x11 -> x0, matrix products: 60.2 us -> none  [the longest x5 25.6 us: deposit(): lax.dot_general(spread, weight_y, (((0,), (0,)), ((), ())), precision=hig...]
    pallas_call x0 -> x8, Pallas kernels: none -> 57.7 us  [the longest x1 36.1 us: on_device(): call(functools.partial(wake_kernel, chunks, nx, ny), [s.shape for s in sp...]
    reshape x6 -> x0, local copies, waits for them, and re-layouts: 25.9 us -> none  [the longest x3 17.1 us: split_pairs(): return values.reshape(values.shape[:-1] + (2, values.shape[-1] // 2))]
    unnamed x56 -> x26, local copies, waits for them, and re-layouts: 33.5 us -> 8.14 us
    all_to_all x4 -> x0, other arithmetic: 22.9 us -> none  [the longest x1 6.28 us: on_device(): lax.all_to_all(physical, 'gx', split_axis=2, concat_axis=3, tiled=True)]
    ppermute x10 -> x8, waiting for transfers between devices: 30.1 us -> 7.63 us  [the longest x1 4.32 us: on_device(): low_rim = lax.ppermute(rim_high, 'gx', ring('gx', 1))]
    all_to_all x6 -> x0, local copies, waits for them, and re-layouts: 17.8 us -> none  [the longest x2 9.11 us: on_device(): lax.all_to_all(physical, 'gx', split_axis=2, concat_axis=3, tiled=True)]
  transfers between devices with their start and end apart: 13 -> 14, of which waited for: 12 -> 8; matrix products, arithmetic and copies ran while one was open for 2% -> 0% of each run, Pallas kernels for 0% -> 4%
where the time goes in v1:
time: 233 us; the launch traced here: 232 us
  waiting for transfers between devices  84.6 us (36%)
  Pallas kernels  57.7 us (25%)
  starting transfers between devices  39.3 us (17%)
  blocking collectives  36.9 us (16%)
  local copies, waits for them, and re-layouts  9.46 us (4%)
    all_to_all x6, waiting for transfers between devices, exchange(): return lax.all_to_all(values, axis, split_axis=0, concat_axis=0, tiled=True)  77 us
    all_to_all x2, blocking collectives, exchange(): return lax.all_to_all(values, axis, split_axis=0, concat_axis=0, tiled=True)  36.9 us
    pallas_call x1, Pallas kernels, on_device(): call(functools.partial(wake_kernel, chunks, nx, ny), [s.shape for s in sp...  36.1 us
    all_to_all x6, starting transfers between devices, exchange(): return lax.all_to_all(values, axis, split_axis=0, concat_axis=0, tiled=True)  22.9 us
    pallas_call x1, Pallas kernels, on_device(): call(functools.partial(deposit_kernel, chunks), [ambient.shape, rim, rim]...  9.81 us
    unnamed x26, local copies, waits for them, and re-layouts  8.14 us
  transfers between devices with their start and end apart: 14, of which 8 were waited for; matrix products, arithmetic and copies ran while one was open for 0% of the time, Pallas kernels for 4%

profile of v1, /device:TPU:0, one launch (start us, length us, event | category | flops | bytes accessed | tf_op | source)
XLA Modules:
  0.0 232.1 jit_solution(6198110767432407232)
XLA Ops:
  0.6 1.3 fusion
  3.2 0.7 compare_select_fusion.1
  3.9 0.7 convert_element_type.3
  4.6 0.7 pad_maximum_fusion.own
  5.3 3.0 %collective-permute-start.1 = (f32[8,512]{1,0:T(8,128)S(1)}, f32[8,512]{1,0:T(8,128)S(1)}, u32[]{:S(2)}, u32[]{:S(2)}) collective-permute-start(f32[8,512]{1,0:T(8,128)S(1)} %pad_maximum_fusion.own), channel_id=1, source_target_pairs={{0,4},{4,8},{8,12},{12,16},{16,20},{20,24},{24,28},{28,0},{1,5},{5... | collective-permute-start | bytes 49160 | tf_op jit(solution)/shard_map/ppermute | solution.py:476
  8.3 3.1 %collective-permute-start = (f32[8,512]{1,0:T(8,128)S(1)}, f32[8,512]{1,0:T(8,128)S(1)}, u32[]{:S(2)}, u32[]{:S(2)}) collective-permute-start(f32[8,512]{1,0:T(8,128)S(1)} %pad_maximum_fusion.own), channel_id=1, source_target_pairs={{0,28},{4,0},{8,4},{12,8},{16,12},{20,16},{24,20},{28,24},{1,29},{... | collective-permute-start | bytes 49160 | tf_op jit(solution)/shard_map/ppermute | solution.py:475
  11.4 3.8 %collective-permute-start.2 = (f32[8,128]{1,0:T(8,128)S(1)}, f32[8,128]{1,0:T(8,128)S(1)}, u32[]{:S(2)}, u32[]{:S(2)}) collective-permute-start(f32[8,128]{1,0:T(8,128)S(1)} %slice.12), channel_id=1, source_target_pairs={{0,24},{4,28},{8,0},{12,4},{16,8},{20,12},{24,16},{28,20},{1,25},{... | collective-permute-start | bytes 12296 | tf_op jit(solution)/shard_map/ppermute | solution.py:477
  15.2 1.6 collective-permute-done.3.down2
  16.8 0.0 collective-permute-done.2.up2
  16.8 0.0 collective-permute-done.1.down1
  16.8 0.0 collective-permute-done.up1
  16.8 0.0 copy-start.2
  16.8 1.4 copy-done.2
  18.2 1.0 copy-done.11
  19.3 1.0 copy-done.12
  20.3 9.8 %shard_map.140 = (f32[3,8,64,256]{3,2,1,0:T(8,128)S(1)}, f32[48,256]{1,0:T(8,128)}, f32[48,256]{1,0:T(8,128)S(1)}, f32[4,72,768]{2,1,0:T(8,128)S(1)}, f32[4,72,768]{2,1,0:T(8,128)}) custom-call(f32[8,512]{1,0:T(8,128)S(1)} %pad_maximum_fusion.own, f32[8,512]{1,0:T(8,128)S(1)} %collective-permute-done.up1, f32[8,512]{1,0:T(8,128)S(1)} %collective-permute-done.1.down1, ...), custom_call_target="tpu_custom_call" | custom-call | tf_op jit(solution)/shard_map/pallas_call | solution.py:481
  30.1 1.1 copy-done.3
  31.3 15.5 %all_to_all.40.part = f32[4,72,768]{2,1,0:T(8,128)S(1)} all-to-all(f32[4,72,768]{2,1,0:T(8,128)S(1)} %get-tuple-element.12), channel_id=1, replica_groups=mesh['gz'=8,'gx'=4] {'gx'}, dimensions={0} | all-to-all | bytes 1769472 | tf_op jit(solution)/shard_map/all_to_all | solution.py:450
  46.8 3.5 %all-to-all-start.2 = ((f32[4,72,768]{2,1,0:T(8,128)}), f32[4,72,768]{2,1,0:T(8,128)S(1)}, u32[]{:S(2)}, u32[]{:S(2)}) async-start(f32[4,72,768]{2,1,0:T(8,128)} %get-tuple-element.13), calls=%async_computation.2 | async-start | bytes 1769472 | tf_op jit(solution)/shard_map/all_to_all | solution.py:450
  50.4 1.8 shard_map.141
  52.2 10.8 %all-to-all-done.2.part = f32[4,72,768]{2,1,0:T(8,128)S(1)} async-done(((f32[4,72,768]{2,1,0:T(8,128)}), f32[4,72,768]{2,1,0:T(8,128)S(1)}, u32[]{:S(2)}, u32[]{:S(2)}) %all-to-all-start.2) | async-done | bytes 884768 | tf_op jit(solution)/shard_map/all_to_all | solution.py:450
  63.0 5.1 %all-to-all-start.1 = ((f32[8,32,768]{2,1,0:T(8,128)}), f32[8,32,768]{2,1,0:T(8,128)S(1)}, u32[]{:S(2)}, u32[]{:S(2)}) async-start(f32[8,32,768]{2,1,0:T(8,128)} %bitcast.5), calls=%async_computation.1 | async-start | bytes 1572864 | tf_op jit(solution)/shard_map/all_to_all | solution.py:450
  68.1 1.8 shard_map.142
  69.9 18.2 %all-to-all-done.1.refs_0_ = f32[8,32,768]{2,1,0:T(8,128)S(1)} async-done(((f32[8,32,768]{2,1,0:T(8,128)}), f32[8,32,768]{2,1,0:T(8,128)S(1)}, u32[]{:S(2)}, u32[]{:S(2)}) %all-to-all-start.1) | async-done | bytes 786464 | tf_op jit(solution)/shard_map/all_to_all | solution.py:450
  88.2 3.5 %all-to-all-start.3 = ((f32[8,32,768]{2,1,0:T(8,128)}), f32[8,32,768]{2,1,0:T(8,128)S(1)}, u32[]{:S(2)}, u32[]{:S(2)}) async-start(f32[8,32,768]{2,1,0:T(8,128)} %bitcast.6), calls=%async_computation.3 | async-start | bytes 1572864 | tf_op jit(solution)/shard_map/all_to_all | solution.py:450
  91.7 0.1 pad_add_fusion.place
  91.8 20.2 %all-to-all-done.3.refs_1_ = f32[8,32,768]{2,1,0:T(8,128)S(1)} async-done(((f32[8,32,768]{2,1,0:T(8,128)}), f32[8,32,768]{2,1,0:T(8,128)S(1)}, u32[]{:S(2)}, u32[]{:S(2)}) %all-to-all-start.3) | async-done | bytes 786464 | tf_op jit(solution)/shard_map/all_to_all | solution.py:450
  112.0 36.1 %shard_map.143 = (f32[8,32,768]{2,1,0:T(8,128)S(1)}, f32[8,32,768]{2,1,0:T(8,128)}) custom-call(s32[2]{0:T(128)S(1)} %pad_add_fusion.place, f32[8,32,768]{2,1,0:T(8,128)S(1)} %all-to-all-done.1.refs_0_, f32[8,32,768]{2,1,0:T(8,128)S(1)} %all-to-all-done.3.refs_1_), custom_call_target="tpu_custom_call" | custom-call | tf_op jit(solution)/shard_map/pallas_call | solution.py:497
  148.1 21.3 %all_to_all.41 = f32[8,32,768]{2,1,0:T(8,128)S(1)} all-to-all(f32[8,32,768]{2,1,0:T(8,128)S(1)} %get-tuple-element.14), channel_id=1, replica_groups=mesh['gz'=8,'gx'=4] {'gz'}, dimensions={0} | all-to-all | bytes 1572864 | tf_op jit(solution)/shard_map/all_to_all | solution.py:450
  169.5 3.7 %all-to-all-start.6 = ((f32[8,32,768]{2,1,0:T(8,128)}), f32[8,32,768]{2,1,0:T(8,128)S(1)}, u32[]{:S(2)}, u32[]{:S(2)}) async-start(f32[8,32,768]{2,1,0:T(8,128)} %get-tuple-element.16), calls=%async_computation.6 | async-start | bytes 1572864 | tf_op jit(solution)/shard_map/all_to_all | solution.py:450
  173.2 1.9 shard_map.144
  175.1 17.0 %all-to-all-done.6 = f32[8,32,768]{2,1,0:T(8,128)S(1)} async-done(((f32[8,32,768]{2,1,0:T(8,128)}), f32[8,32,768]{2,1,0:T(8,128)S(1)}, u32[]{:S(2)}, u32[]{:S(2)}) %all-to-all-start.6) | async-done | bytes 786464 | tf_op jit(solution)/shard_map/all_to_all | solution.py:450
  192.1 3.5 %all-to-all-start.5 = ((f32[4,72,768]{2,1,0:T(8,128)}), f32[4,72,768]{2,1,0:T(8,128)S(1)}, u32[]{:S(2)}, u32[]{:S(2)}) async-start(f32[4,72,768]{2,1,0:T(8,128)} %shard_map.144), calls=%async_computation.5 | async-start | bytes 1769472 | tf_op jit(solution)/shard_map/all_to_all | solution.py:450
  195.6 0.0 copy-start
  195.7 0.0 copy-start.1
  195.7 1.9 shard_map.146
  197.6 10.7 %all-to-all-done.5.part = f32[4,72,768]{2,1,0:T(8,128)S(1)} async-done(((f32[4,72,768]{2,1,0:T(8,128)}), f32[4,72,768]{2,1,0:T(8,128)S(1)}, u32[]{:S(2)}, u32[]{:S(2)}) %all-to-all-start.5) | async-done | bytes 884768 | tf_op jit(solution)/shard_map/all_to_all | solution.py:450
  208.3 3.5 %all-to-all-start.7 = ((f32[4,72,768]{2,1,0:T(8,128)}), f32[4,72,768]{2,1,0:T(8,128)S(1)}, u32[]{:S(2)}, u32[]{:S(2)}) async-start(f32[4,72,768]{2,1,0:T(8,128)} %shard_map.146), calls=%async_computation.7 | async-start | bytes 1769472 | tf_op jit(solution)/shard_map/all_to_all | solution.py:450
  211.8 1.5 shard_map.145
  213.4 0.9 copy-done.9
  214.3 1.3 collective-permute-start.4
  215.6 3.4 %collective-permute-start.5 = (f32[3,64,256]{2,1,0:T(8,128)S(1)}, f32[3,64,256]{2,1,0:T(8,128)S(1)}, u32[]{:S(2)}, u32[]{:S(2)}) collective-permute-start(f32[3,64,256]{2,1,0:T(8,128)S(1)} %get-tuple-element.18), channel_id=1, source_target_pairs={{0,28},{4,0},{8,4},{12,8},{16,12},{20,16},{24,20},{28,24},{1,29},{... | collective-permute-start | bytes 589832 | tf_op jit(solution)/shard_map/ppermute | solution.py:515
  219.0 1.7 collective-permute-start.7
  220.7 4.3 %collective-permute-done.6.low_rim = f32[48,256]{1,0:T(8,128)S(1)} collective-permute-done((f32[48,256]{1,0:T(8,128)}, f32[48,256]{1,0:T(8,128)S(1)}, u32[]{:S(2)}, u32[]{:S(2)}) %collective-permute-start.6) | collective-permute-done | bytes 49184 | tf_op jit(solution)/shard_map/ppermute | solution.py:487
  225.1 1.7 collective-permute-done.5.after
  226.8 1.4 copy-done.4
  228.2 1.2 copy-done.10
  229.4 2.8 %shard_map.147 = (f32[3,8,64,256]{3,2,1,0:T(8,128)}, f32[3,8,64,256]{3,2,1,0:T(8,128)}) custom-call(f32[3,4,72,256]{3,2,1,0:T(8,128)S(1)} %copy-done.10, f32[4,72,768]{2,1,0:T(8,128)S(1)} %all-to-all-done.7.part, f32[3,64,256]{2,1,0:T(8,128)S(1)} %collective-permute-done.4.before, f32[3,64,256]{2,1,0:T(8,128)S(1)} %collective-permute-done.5.after, ...), custom_call_target="tpu_custom_call" | custom-call | tf_op jit(solution)/shard_map/pallas_call | solution.py:518
  (22 shorter events, 0.0 us)
Async XLA Ops:
  5.3 11.5 %collective-permute-start.1 = (f32[8,512]{1,0:T(8,128)S(1)}, f32[8,512]{1,0:T(8,128)S(1)}, u32[]{:S(2)}, u32[]{:S(2)}) collective-permute-start(f32[8,512]{1,0:T(8,128)S(1)} %pad_maximum_fusion.own), channel_id=1, source_target_pairs={{0,4},{4,8},{8,12},{12,16},{16,20},{20,24},{24,28},{28,0},{1,5},{5... | collective-permute-start | bytes 49160 | tf_op jit(solution)/shard_map/ppermute | solution.py:476
  8.3 8.5 %collective-permute-start = (f32[8,512]{1,0:T(8,128)S(1)}, f32[8,512]{1,0:T(8,128)S(1)}, u32[]{:S(2)}, u32[]{:S(2)}) collective-permute-start(f32[8,512]{1,0:T(8,128)S(1)} %pad_maximum_fusion.own), channel_id=1, source_target_pairs={{0,28},{4,0},{8,4},{12,8},{16,12},{20,16},{24,20},{28,24},{1,29},{... | collective-permute-start | bytes 49160 | tf_op jit(solution)/shard_map/ppermute | solution.py:475
  11.4 5.4 %collective-permute-start.3 = (f32[8,128]{1,0:T(8,128)S(1)}, f32[8,128]{1,0:T(8,128)S(1)}, u32[]{:S(2)}, u32[]{:S(2)}) collective-permute-start(f32[8,128]{1,0:T(8,128)S(1)} %slice.12), channel_id=1, source_target_pairs={{0,8},{4,12},{8,16},{12,20},{16,24},{20,28},{24,0},{28,4},{1,9},{5... | collective-permute-start | bytes 12296 | tf_op jit(solution)/shard_map/ppermute | solution.py:478
  11.4 5.4 %collective-permute-start.2 = (f32[8,128]{1,0:T(8,128)S(1)}, f32[8,128]{1,0:T(8,128)S(1)}, u32[]{:S(2)}, u32[]{:S(2)}) collective-permute-start(f32[8,128]{1,0:T(8,128)S(1)} %slice.12), channel_id=1, source_target_pairs={{0,24},{4,28},{8,0},{12,4},{16,8},{20,12},{24,16},{28,20},{1,25},{... | collective-permute-start | bytes 12296 | tf_op jit(solution)/shard_map/ppermute | solution.py:477
  16.8 1.4 copy-start.2
  18.2 1.0 copy-start.11
  19.3 1.0 copy-start.12
  30.1 1.1 copy-start.3
  31.3 19.1 %copy-start.7 = (bf16[512,256]{1,0:T(8,128)(2,1)S(1)}, bf16[512,256]{1,0:T(8,128)(2,1)}, u32[]{:S(2)}) copy-start(bf16[512,256]{1,0:T(8,128)(2,1)} %constant.34.clone.t_low) | copy-start | bytes 786436
  31.3 19.1 %copy-start.8 = (bf16[512,256]{1,0:T(8,128)(2,1)S(1)}, bf16[512,256]{1,0:T(8,128)(2,1)}, u32[]{:S(2)}) copy-start(bf16[512,256]{1,0:T(8,128)(2,1)} %constant.33.clone.t_high) | copy-start | bytes 786436
  46.8 16.2 %all-to-all-start.2 = ((f32[4,72,768]{2,1,0:T(8,128)}), f32[4,72,768]{2,1,0:T(8,128)S(1)}, u32[]{:S(2)}, u32[]{:S(2)}) async-start(f32[4,72,768]{2,1,0:T(8,128)} %get-tuple-element.13), calls=%async_computation.2 | async-start | bytes 1769472 | tf_op jit(solution)/shard_map/all_to_all | solution.py:450
  63.0 25.1 %all-to-all-start.1 = ((f32[8,32,768]{2,1,0:T(8,128)}), f32[8,32,768]{2,1,0:T(8,128)S(1)}, u32[]{:S(2)}, u32[]{:S(2)}) async-start(f32[8,32,768]{2,1,0:T(8,128)} %bitcast.5), calls=%async_computation.1 | async-start | bytes 1572864 | tf_op jit(solution)/shard_map/all_to_all | solution.py:450
  88.2 23.9 %all-to-all-start.3 = ((f32[8,32,768]{2,1,0:T(8,128)}), f32[8,32,768]{2,1,0:T(8,128)S(1)}, u32[]{:S(2)}, u32[]{:S(2)}) async-start(f32[8,32,768]{2,1,0:T(8,128)} %bitcast.6), calls=%async_computation.3 | async-start | bytes 1572864 | tf_op jit(solution)/shard_map/all_to_all | solution.py:450
  148.1 25.1 %copy-start.5 = (bf16[576,256]{1,0:T(8,128)(2,1)S(1)}, bf16[576,256]{1,0:T(8,128)(2,1)}, u32[]{:S(2)}) copy-start(bf16[576,256]{1,0:T(8,128)(2,1)} %constant.36.clone.t_low) | copy-start | bytes 884740
  148.1 25.1 %copy-start.6 = (bf16[576,256]{1,0:T(8,128)(2,1)S(1)}, bf16[576,256]{1,0:T(8,128)(2,1)}, u32[]{:S(2)}) copy-start(bf16[576,256]{1,0:T(8,128)(2,1)} %constant.35.clone.t_high) | copy-start | bytes 884740
  169.5 22.7 %all-to-all-start.6 = ((f32[8,32,768]{2,1,0:T(8,128)}), f32[8,32,768]{2,1,0:T(8,128)S(1)}, u32[]{:S(2)}, u32[]{:S(2)}) async-start(f32[8,32,768]{2,1,0:T(8,128)} %get-tuple-element.16), calls=%async_computation.6 | async-start | bytes 1572864 | tf_op jit(solution)/shard_map/all_to_all | solution.py:450
  192.1 16.2 %all-to-all-start.5 = ((f32[4,72,768]{2,1,0:T(8,128)}), f32[4,72,768]{2,1,0:T(8,128)S(1)}, u32[]{:S(2)}, u32[]{:S(2)}) async-start(f32[4,72,768]{2,1,0:T(8,128)} %shard_map.144), calls=%async_computation.5 | async-start | bytes 1769472 | tf_op jit(solution)/shard_map/all_to_all | solution.py:450
  195.6 16.2 %copy-start = (bf16[512,512]{1,0:T(8,128)(2,1)S(1)}, bf16[512,512]{1,0:T(8,128)(2,1)}, u32[]{:S(2)}) copy-start(bf16[512,512]{1,0:T(8,128)(2,1)} %constant.38.clone.t_low) | copy-start | bytes 1572868
  195.7 16.2 %copy-start.1 = (bf16[512,512]{1,0:T(8,128)(2,1)S(1)}, bf16[512,512]{1,0:T(8,128)(2,1)}, u32[]{:S(2)}) copy-start(bf16[512,512]{1,0:T(8,128)(2,1)} %constant.37.clone.t_high) | copy-start | bytes 1572868
  208.3 16.8 %all-to-all-start.7 = ((f32[4,72,768]{2,1,0:T(8,128)}), f32[4,72,768]{2,1,0:T(8,128)S(1)}, u32[]{:S(2)}, u32[]{:S(2)}) async-start(f32[4,72,768]{2,1,0:T(8,128)} %shard_map.146), calls=%async_computation.7 | async-start | bytes 1769472 | tf_op jit(solution)/shard_map/all_to_all | solution.py:450
  213.4 0.9 copy-start.9
  214.3 10.8 %collective-permute-start.4 = (f32[3,64,256]{2,1,0:T(8,128)}, f32[3,64,256]{2,1,0:T(8,128)S(1)}, u32[]{:S(2)}, u32[]{:S(2)}) collective-permute-start(f32[3,64,256]{2,1,0:T(8,128)} %get-tuple-element.17), channel_id=1, source_target_pairs={{0,4},{4,8},{8,12},{12,16},{16,20},{20,24},{24,28},{28,0},{1,5},{5... | collective-permute-start | bytes 589832 | tf_op jit(solution)/shard_map/ppermute | solution.py:516
  215.6 11.2 %collective-permute-start.5 = (f32[3,64,256]{2,1,0:T(8,128)S(1)}, f32[3,64,256]{2,1,0:T(8,128)S(1)}, u32[]{:S(2)}, u32[]{:S(2)}) collective-permute-start(f32[3,64,256]{2,1,0:T(8,128)S(1)} %get-tuple-element.18), channel_id=1, source_target_pairs={{0,28},{4,0},{8,4},{12,8},{16,12},{20,16},{24,20},{28,24},{1,29},{... | collective-permute-start | bytes 589832 | tf_op jit(solution)/shard_map/ppermute | solution.py:515
  219.0 6.1 %collective-permute-start.6 = (f32[48,256]{1,0:T(8,128)}, f32[48,256]{1,0:T(8,128)S(1)}, u32[]{:S(2)}, u32[]{:S(2)}) collective-permute-start(f32[48,256]{1,0:T(8,128)} %get-tuple-element.20), channel_id=1, source_target_pairs={{0,1},{1,2},{2,3},{3,0},{4,5},{5,6},{6,7},{7,4},{8,9},{9,10},{10,1... | collective-permute-start | bytes 147464 | tf_op jit(solution)/shard_map/ppermute | solution.py:487
  219.0 6.1 %collective-permute-start.7 = (f32[48,256]{1,0:T(8,128)S(1)}, f32[48,256]{1,0:T(8,128)S(1)}, u32[]{:S(2)}, u32[]{:S(2)}) collective-permute-start(f32[48,256]{1,0:T(8,128)S(1)} %get-tuple-element.21), channel_id=1, source_target_pairs={{0,3},{1,0},{2,1},{3,2},{4,7},{5,4},{6,5},{7,6},{8,11},{9,8},{10,9... | collective-permute-start | bytes 147464 | tf_op jit(solution)/shard_map/ppermute | solution.py:488
  226.8 1.4 copy-start.4
  228.2 1.2 copy-start.10

commit v2 on v1

v2 whole, which is shorter than its diff:
```python
import functools
import math

import jax
import jax.numpy as jnp
import ml_dtypes
import numpy as np
from jax import lax
from jax.experimental import pallas as pl
from jax.experimental.pallas import tpu as pltpu
from jax.sharding import PartitionSpec as P

MIG = 64
LANES = 128
RIM = 8
TIME_STEP = 0.25
VMEM = 48 * 1024 * 1024
F32 = jnp.float32
BF16 = jnp.bfloat16


def split_table(table):
    high = table.astype(np.float32).astype(ml_dtypes.bfloat16)
    low = (table - high.astype(np.float64)).astype(np.float32).astype(ml_dtypes.bfloat16)
    return high, low


def angles(rows, columns, extent):
    return 2.0 * np.pi * (np.multiply.outer(rows, columns) % extent) / extent


def y_tables(ny, pencils, scale):
    modes = ny // (2 * pencils)
    position = np.arange(ny)
    angle = angles(position, np.arange(ny // 2), ny)
    real, imag = np.cos(angle), -np.sin(angle)
    imag[:, 0] = 1.0 - 2.0 * (position % 2)
    weight = np.where(np.arange(ny // 2) == 0, 1.0, 2.0) * scale
    ahead = np.zeros((2, ny, pencils, 2, 2, modes))
    back = np.zeros((pencils, 2, 2, modes, 2, ny))
    for parity in range(2):
        for part, values in enumerate((real, imag)):
            ahead[parity, :, :, part, parity] = values.reshape(ny, pencils, modes)
            back[:, part, parity, :, parity] = (values * weight).T.reshape(pencils, modes, ny)
    return ahead.reshape(2 * ny, -1), back.reshape(-1, 2 * ny)


def wave_order(nx, slabs):
    half = nx // 2
    ahead = np.arange(half).reshape(slabs, 1, half // slabs)
    behind = np.where(ahead == 0, half, (nx - ahead) % nx)
    return np.concatenate([ahead, behind], axis=1).reshape(-1)


def x_tables(nx, cols, pencils, slabs):
    order = wave_order(nx, slabs)
    angle = angles(order, np.arange(nx), nx)
    ahead = np.concatenate([np.cos(angle), np.sin(angle)], axis=0)
    row = np.arange(cols + RIM)
    offset = np.where(row <= cols, row, -1)
    used = ((row <= cols) | (row == cols + RIM - 1)).astype(np.float64)
    place = (np.arange(pencils)[:, None] * cols + offset[None, :]) % nx
    angle = angles(place.reshape(-1), order, nx)
    mask = np.tile(used, pencils)[:, None]
    back = np.concatenate([np.cos(angle) * mask, np.sin(angle) * mask], axis=0)
    return ahead, back


def split(values):
    high = values.astype(BF16)
    return high, (values - high.astype(F32)).astype(BF16)


def dot(left, right):
    return jnp.dot(left, right, preferred_element_type=F32)


def table_left(high, low, values):
    v_high, v_low = split(values)
    return dot(high, v_high) + (dot(high, v_low) + dot(low, v_high))


def table_right(values, high, low):
    v_high, v_low = split(values)
    return dot(v_high, high) + (dot(v_low, high) + dot(v_high, low))


def lane_of():
    return lax.broadcasted_iota(jnp.int32, (1, LANES), 1)


def times_i(values):
    half = LANES // 2
    sign = jnp.where(lane_of() < half, -1.0, 1.0).astype(F32)
    return pltpu.roll(values, half, 1) * sign


def kernel_weight(distance):
    radius = jnp.abs(distance)
    near = 1.0 - 2.5 * radius * radius + 1.5 * radius * radius * radius
    far = 0.5 * (2.0 - radius) * (2.0 - radius) * (1.0 - radius)
    return jnp.where(radius < 1.0, near, jnp.where(radius < 2.0, far, 0.0))


def turned(value, wave, extent, sign):
    wave = wave % extent
    real, imag = value
    if wave == 0:
        return value
    if 2 * wave == extent:
        return -real, -imag
    if 4 * wave == extent:
        return (-imag, real) if sign > 0 else (imag, -real)
    if 4 * wave == 3 * extent:
        return (imag, -real) if sign > 0 else (-imag, real)
    a = math.cos(2.0 * math.pi * wave / extent)
    b = sign * math.sin(2.0 * math.pi * wave / extent)
    return real * a - imag * b, real * b + imag * a


def fft(values, sign):
    count = len(values)
    if count == 1:
        return values
    even, odd = fft(values[::2], sign), fft(values[1::2], sign)
    odd = [turned(v, k, count, sign) for k, v in enumerate(odd)]
    plus = [(a[0] + b[0], a[1] + b[1]) for a, b in zip(even, odd)]
    minus = [(a[0] - b[0], a[1] - b[1]) for a, b in zip(even, odd)]
    return plus + minus


def blocks_of(refs, at):
    if len(refs) == 1:
        return [(d, refs[0].at[d]) for d in range(refs[0].shape[0])]
    return [(at ^ k, ref) for k, ref in enumerate(refs)]


def gather_blocks(refs, held, at):
    for d, ref in blocks_of(refs, at):
        held[d] = ref[...]


def packet_kernel(counts, strength, offsets, cells, packet, movers):
    slot = lax.broadcasted_iota(jnp.int32, (1, strength.shape[1]), 1)
    up, both = counts[0], counts[0] + counts[1]
    packet[0:3] = strength[...]
    packet[3:6] = offsets[...]
    packet[6:7] = cells[...].astype(F32)
    packet[7:8] = jnp.where(slot < up, 1.0, jnp.where(slot < both, -1.0, 0.0))
    movers[...] = packet[:, : movers.shape[1]]


def deposit_kernel(
    pairs, place, own, up1, down1, up2, down2, ambient, table_high, table_low, *refs
):
    mesh, rim_high, rim_low = refs[:3]
    total, t_high, t_low, made, sems = refs[-5:]
    outs = refs[3:-5]
    _, planes, cols, ny = ambient.shape
    rows = cols + RIM
    movers = up2.shape[1]
    count = own.shape[1]
    listed = [2 * pair + parity for pair in pairs for parity in range(2)]
    fetches = [
        pltpu.make_async_copy(
            ambient.at[:, z], total.at[:, n, pl.ds(0, cols)], sems.at[n]
        )
        for n, z in enumerate(listed)
    ]
    tables = [
        pltpu.make_async_copy(table_high, t_high, sems.at[len(listed)]),
        pltpu.make_async_copy(table_low, t_low, sems.at[len(listed) + 1]),
    ]
    for fetch in fetches + tables:
        fetch.start()

    def decode(ref, start, stop, shift):
        packet = ref[:, start:stop]
        cell = packet[6:7].astype(jnp.int32)
        move = packet[7:8].astype(jnp.int32)
        z_cell = lax.div(cell, cols * ny) + planes * (move + shift)
        x_cell = lax.rem(lax.div(cell, ny), cols)
        return packet[0:6], z_cell, x_cell, lax.rem(cell, ny)

    def joined(pieces):
        return [jnp.concatenate(p, axis=1) if len(p) > 1 else p[0] for p in zip(*pieces)]

    def add_block(pieces, wanted, waits=()):
        values, z_cell, x_cell, y_cell = joined(pieces)
        width = values.shape[1]
        z_at = lax.broadcasted_iota(jnp.int32, (planes, width), 0)
        w_z = kernel_weight((z_at - z_cell).astype(F32) - values[3:4])
        row = lax.broadcasted_iota(jnp.int32, (rows, width), 0)
        x_at = jnp.where(row < cols + 2, row, jnp.where(row >= rows - 2, row - rows, 4 * rows))
        w_x = kernel_weight((x_at - x_cell).astype(F32) - values[4:5])
        y_at = lax.broadcasted_iota(jnp.int32, (ny, width), 0)
        y_off = lax.rem(y_at - y_cell + (ny + ny // 2), ny) - ny // 2
        w_y = kernel_weight(y_off.astype(F32) - values[5:6])
        y_high, y_low = split(w_y)
        right = jnp.concatenate([y_high, y_high, y_low], axis=1)
        for wait in waits:
            wait.wait()
        at = [listed.index(z) for z in wanted]
        for c in range(3):
            s_z = values[c : c + 1] * w_z
            left = jnp.concatenate([s_z[z : z + 1] * w_x for z in wanted], axis=0)
            l_high, l_low = split(left)
            left = jnp.concatenate([l_high, l_low, l_high], axis=1)
            added = lax.dot_general(
                left, right, (((1,), (1,)), ((), ())), preferred_element_type=F32
            )
            total[c, at[0] : at[-1] + 1] += added.reshape(len(wanted), rows, ny)

    total[:, :, cols:rows] = jnp.zeros((3, len(listed), RIM, ny), F32)
    step = 256
    for at in range(0, count, step):
        waits = fetches if at == 0 else ()
        add_block([decode(own, at, min(at + step, count), 0)], listed, waits)
    add_block([decode(up1, 0, movers, 1), decode(down1, 0, movers, -1)], listed)
    sides = ((up1, up2, 1, (planes - 2, planes - 1)), (down1, down2, -1, (0, 1)))
    for near, far, shift, wanted in sides:
        if not set(wanted) <= set(listed):
            continue
        whole = [decode(near, movers, count, shift), decode(far, 0, movers, 2 * shift)]
        values, z_cell, x_cell, y_cell = joined(whole)
        for at in range(0, count, step):
            to = min(at + step, count)
            block = (values[:, at:to], z_cell[:, at:to], x_cell[:, at:to], y_cell[:, at:to])
            add_block([block], wanted)

    keep = pltpu.make_async_copy(total.at[:, :, pl.ds(0, cols)], mesh, sems.at[0])
    keep.start()
    for n in range(3 * len(listed)):
        c, i = n // len(listed), n % len(listed)
        rim_high[2 * n : 2 * n + 2] = total[c, i, cols : cols + 2]
        rim_low[2 * n : 2 * n + 2] = total[c, i, rows - 2 : rows]
    groups = [(c, 2 * n) for c in range(3) for n in range(len(pairs))]
    left = jnp.concatenate(
        [jnp.concatenate([total[c, n], total[c, n + 1]], axis=1) for c, n in groups], axis=0
    )
    for table in tables:
        table.wait()
    wide = table_right(left, t_high[...], t_low[...])
    for n in range(len(groups)):
        for g in range(made.shape[0]):
            made[g, :, n * LANES : (n + 1) * LANES] = wide[
                n * rows : (n + 1) * rows, g * LANES : (g + 1) * LANES
            ]
    for d, out in blocks_of(outs, place[1]):
        out[...] = made[d]
    keep.wait()


def x_ahead_kernel(sends, place, t_high, t_low, *refs):
    held, made = refs[-2:]
    outs, parts = refs[-2 - sends : -2], refs[: -2 - sends]
    gather_blocks(parts, held, place[1])
    pencils, rows, width = held.shape
    cols = rows - RIM
    row = lax.broadcasted_iota(jnp.int32, (RIM, width), 0)
    pieces = []
    for h in range(pencils):
        from_low = held[(h - 1) % pencils, cols:rows]
        from_high = held[(h + 1) % pencils, cols:rows]
        pieces.append(held[h, 0:RIM] + jnp.where(row < 2, from_low, 0.0))
        pieces.append(held[h, RIM : cols - RIM])
        pieces.append(held[h, cols - RIM : cols] + jnp.where(row >= RIM - 2, from_high, 0.0))
    both = table_left(t_high[...], t_low[...], jnp.concatenate(pieces, axis=0))
    half = both.shape[0] // 2
    for n in range(width // LANES):
        lanes = slice(n * LANES, (n + 1) * LANES)
        value = both[:half, lanes] - times_i(both[half:, lanes])
        made[:, :, lanes] = value.reshape(made.shape[0], made.shape[1], LANES)
    for d, out in blocks_of(outs, place[0]):
        out[...] = made[d]


def x_back_kernel(sends, place, t_high, t_low, *refs):
    held, made = refs[-2:]
    outs, parts = refs[-2 - sends : -2], refs[: -2 - sends]
    gather_blocks(parts, held, place[0])
    pencils, rows, width = made.shape
    both = table_left(t_high[...], t_low[...], held[...].reshape(-1, width))
    half = both.shape[0] // 2
    for n in range(width // LANES):
        lanes = slice(n * LANES, (n + 1) * LANES)
        value = both[:half, lanes] + times_i(both[half:, lanes])
        made[:, :, lanes] = value.reshape(pencils, rows, LANES)
    for d, out in blocks_of(outs, place[1]):
        out[...] = made[d]


def wake_kernel(chunks, nx, ny, place, *refs):
    data, spectrum = refs[-2:]
    each = (len(refs) - 2) // (2 * len(chunks))
    parts = [refs[n * each : (n + 1) * each] for n in range(len(chunks))]
    outs = [refs[(n + len(chunks)) * each :][:each] for n in range(len(chunks))]
    _, _, planes, slabs, tile, _ = data.shape
    nz = planes * slabs
    lane = lane_of()
    modes = LANES // 4
    low_half = lane < LANES // 2
    first = (lane // modes) % 2 == 0
    half, quarter = LANES // 2, LANES // 4
    slab_at, pencil_at = place[0], place[1]

    def roll(values, shift):
        return pltpu.roll(values, shift, 1)

    def cross_half(a, b):
        return jnp.where(low_half, a, roll(b, half)), jnp.where(low_half, roll(a, half), b)

    def cross_quarter(a, b):
        return (
            jnp.where(first, a, roll(b, quarter)),
            jnp.where(first, roll(a, LANES - quarter), b),
        )

    def lanes_at(c, chunk, i):
        return pl.ds(pl.multiple_of((c * len(chunk) + i) * LANES, LANES), LANES)

    def enter(c, carry):
        for chunk, refs_in in zip(chunks, parts):
            for i, pair in enumerate(chunk):
                lanes = lanes_at(c, chunk, i)
                for s, ref in blocks_of(refs_in, slab_at):
                    quad = [ref[q * tile : (q + 1) * tile, lanes] for q in range(4)]
                    real0, imag0 = cross_half(quad[0], quad[2])
                    real1, imag1 = cross_half(quad[1], quad[3])
                    for part, (a, b) in enumerate(((real0, real1), (imag0, imag1))):
                        even, odd = cross_quarter(a, b)
                        data[c, part, 2 * pair, s] = even
                        data[c, part, 2 * pair + 1, s] = odd
        return carry

    def leave(c, carry):
        for chunk, refs_out in zip(chunks, outs):
            for i, pair in enumerate(chunk):
                lanes = lanes_at(c, chunk, i)
                for s, ref in blocks_of(refs_out, slab_at):
                    real0, real1 = cross_quarter(data[c, 0, 2 * pair, s], data[c, 0, 2 * pair + 1, s])
                    imag0, imag1 = cross_quarter(data[c, 1, 2 * pair, s], data[c, 1, 2 * pair + 1, s])
                    quad = [None] * 4
                    quad[0], quad[2] = cross_half(real0, imag0)
                    quad[1], quad[3] = cross_half(real1, imag1)
                    for q in range(4):
                        ref[q * tile : (q + 1) * tile, lanes] = quad[q]
        return carry

    def across_slabs(c, carry):
        for l in range(planes):
            line = [(data[c, 0, l, s], data[c, 1, l, s]) for s in range(slabs)]
            for k, v in enumerate(fft(line, -1.0)):
                v = turned(v, l * k, nz, -1.0)
                data[c, 0, l, k], data[c, 1, l, k] = v
        return carry

    def back_across_slabs(c, carry):
        for l in range(planes):
            line = [
                turned((data[c, 0, l, k], data[c, 1, l, k]), l * k, nz, 1.0) for k in range(slabs)
            ]
            for s, v in enumerate(fft(line, 1.0)):
                data[c, 0, l, s], data[c, 1, l, s] = v
        return carry

    def across_planes(k, carry):
        for c in range(3):
            line = [(data[c, 0, l, k], data[c, 1, l, k]) for l in range(planes)]
            for n, v in enumerate(fft(line, -1.0)):
                spectrum[c, 0, k + slabs * n], spectrum[c, 1, k + slabs * n] = v
        return carry

    reach = 2 * tile
    row = lax.broadcasted_iota(jnp.int32, (tile, LANES), 0)
    lane_all = lax.broadcasted_iota(jnp.int32, (tile, LANES), 1)
    number = slab_at * reach + (lane_all // modes) % 2 * tile + row
    ahead = lane_all < half
    mode = lane_all % modes + pencil_at * modes
    alone = number == 0
    number = number.astype(F32) * (2.0 * math.pi / nx)
    x_base = jnp.where(ahead, number, jnp.where(alone, math.pi, -number))
    x_trim = jnp.where(ahead, number, jnp.where(alone, 0.0, -number))
    wave_y = mode.astype(F32) * (2.0 * math.pi / ny)
    packed = mode == 0
    x_sq = x_base * x_base
    lateral = x_sq + wave_y * wave_y

    def curl_at(k, with_mirror):
        z_wave = jnp.where(k < nz // 2, k, k - nz).astype(F32) * (2.0 * math.pi / nz)
        z_trim = jnp.where(k == nz // 2, 0.0, z_wave)
        full = lateral + z_wave * z_wave
        empty = full == 0.0
        inverse = jnp.where(empty, 0.0, 1.0 / jnp.where(empty, 1.0, full))
        if with_mirror:
            other = 1.0 / (x_sq + (z_wave * z_wave + math.pi * math.pi))
            mirror = jnp.where(packed, 0.5 * (inverse - other), 0.0)
            inverse = jnp.where(packed, 0.5 * (inverse + other), inverse)
            opposite = lax.rem(nz - k, nz)
        stream = []
        for c in range(3):
            value = [spectrum[c, part, k] * inverse for part in range(2)]
            if with_mirror:
                for part, sign in enumerate((1.0, -1.0)):
                    there = spectrum[c, part, opposite]
                    there = jnp.where(alone, there, roll(there, half))
                    value[part] = value[part] + (mirror * sign) * there
            stream.append(value)
        made = []
        for part in range(2):
            s = [value[part] for value in stream]
            made.append(
                (
                    x_trim * s[2] - wave_y * s[1],
                    wave_y * s[0] - z_trim * s[2],
                    z_trim * s[1] - x_trim * s[0],
                )
            )
        return [(-made[1][c], made[0][c]) for c in range(3)]

    def curl_all(with_mirror):
        def body(k, carry):
            made = [curl_at(k + slabs * n, with_mirror) for n in range(planes)]
            for c in range(3):
                for l, v in enumerate(fft([m[c] for m in made], 1.0)):
                    data[c, 0, l, k], data[c, 1, l, k] = v
            return carry

        lax.fori_loop(0, slabs, body, 0)

    lax.fori_loop(0, 3, enter, 0)
    lax.fori_loop(0, 3, across_slabs, 0)
    lax.fori_loop(0, slabs, across_planes, 0)

    @pl.when(pencil_at == 0)
    def _():
        curl_all(True)

    @pl.when(pencil_at != 0)
    def _():
        curl_all(False)

    lax.fori_loop(0, 3, back_across_slabs, 0)
    lax.fori_loop(0, 3, leave, 0)


def planes_of(held, pairs, t_high, t_low):
    pencils, rows, _ = held.shape
    ny = t_high.shape[1] // 2
    groups = [(c, pair) for c in range(3) for pair in pairs]
    left = jnp.concatenate(
        [
            jnp.concatenate(
                [held[h, :, n * LANES : (n + 1) * LANES] for h in range(pencils)], axis=1
            )
            for n in range(len(groups))
        ],
        axis=0,
    )
    wide = table_right(left, t_high[...], t_low[...])
    made = {}
    for n, (c, pair) in enumerate(groups):
        for parity in range(2):
            made[c, 2 * pair + parity] = wide[
                n * rows : (n + 1) * rows, parity * ny : (parity + 1) * ny
            ]
    return made


def edge_kernel(pairs, place, t_high, t_low, *refs):
    out, first, last, held, made, sem = refs[-6:]
    gather_blocks(refs[:-6], held, place[1])
    listed = [2 * pair + parity for pair in pairs for parity in range(2)]
    cols = first.shape[1]
    values = planes_of(held, pairs, t_high, t_low)
    for c in range(3):
        for n, z in enumerate(listed):
            made[c, n] = values[c, z]
    keep = pltpu.make_async_copy(made, out, sem.at[0])
    keep.start()
    for c in range(3):
        first[c] = values[c, listed[0]][0:cols]
        last[c] = values[c, listed[-1]][0:cols]
    keep.wait()


def stretch_kernel(chunks, place, t_high, t_low, edges, before, after, *refs):
    meshes, rims, refs = refs[:2], refs[2:6], refs[6:]
    velocity, vorticity, held, tall, omega, sems = refs[-6:]
    parts = refs[:-6]
    _, planes, cols, ny = velocity.shape
    rows = cols + RIM
    lists = [[2 * pair + parity for pair in chunk for parity in range(2)] for chunk in chunks]
    copies, used = [], 0
    for chunk, mesh in zip(lists, meshes):
        for n, z in enumerate(chunk):
            copies.append(pltpu.make_async_copy(mesh.at[:, n], omega.at[:, z], sems.at[used]))
            used += 1
    for n, z in enumerate(lists[0]):
        copies.append(
            pltpu.make_async_copy(
                edges.at[:, n], tall.at[:, z, pl.ds(RIM, rows)], sems.at[used]
            )
        )
        copies.append(
            pltpu.make_async_copy(
                edges.at[:, n, pl.ds(cols, RIM)], tall.at[:, z, pl.ds(0, RIM)], sems.at[used + 1]
            )
        )
        used += 2
    for copy in copies:
        copy.start()
    gather_blocks(parts, held, place[1])
    for (c, z), value in planes_of(held, chunks[1], t_high, t_low).items():
        tall[c, z, RIM : RIM + rows] = value
        tall[c, z, 0:RIM] = value[cols:rows]
    for copy in copies:
        copy.wait()
    sent = []
    for z in range(planes):
        sent.append(
            pltpu.make_async_copy(tall.at[:, z, pl.ds(RIM, cols)], velocity.at[:, z], sems.at[z])
        )
        sent[-1].start()
    for z in range(planes):
        which = 0 if z in lists[0] else 1
        n, size = lists[which].index(z), len(lists[which])
        low_rim, high_rim = rims[2 * which], rims[2 * which + 1]
        for c in range(3):
            at = 2 * (c * size + n)
            omega[c, z, 0:2] += low_rim[at : at + 2]
            omega[c, z, cols - 2 : cols] += high_rim[at : at + 2]
        mesh = [omega[c, z] for c in range(3)]
        for c in range(3):
            value = tall[c, z, RIM : RIM + cols]
            above = tall[c, z + 1, RIM : RIM + cols] if z + 1 < planes else after[c]
            below = tall[c, z - 1, RIM : RIM + cols] if z > 0 else before[c]
            along_z = (above - below) * 0.5
            along_x = (
                tall[c, z, RIM + 1 : RIM + 1 + cols] - tall[c, z, RIM - 1 : RIM - 1 + cols]
            ) * 0.5
            along_y = (pltpu.roll(value, ny - 1, 1) - pltpu.roll(value, 1, 1)) * 0.5
            stretch = mesh[0] * along_z + mesh[1] * along_x + mesh[2] * along_y
            omega[c, z] = mesh[c] + TIME_STEP * stretch
        sent.append(
            pltpu.make_async_copy(omega.at[:, z], vorticity.at[:, z], sems.at[planes + z])
        )
        sent[-1].start()
    for copy in sent:
        copy.wait()


VM = pl.BlockSpec(memory_space=pltpu.VMEM)
SM = pl.BlockSpec(memory_space=pltpu.SMEM)
HB = pl.BlockSpec(memory_space=pltpu.HBM)


def call(kernel, ins, outs, scratch=(), sems=0, micros=2.0):
    extra = [pltpu.SemaphoreType.DMA((sems,))] if sems else []
    return pl.pallas_call(
        kernel,
        out_shape=[jax.ShapeDtypeStruct(shape, F32) for _, shape in outs],
        in_specs=[spec for spec, _ in ins],
        out_specs=[spec for spec, _ in outs],
        scratch_shapes=[pltpu.VMEM(shape, kind) for shape, kind in scratch] + extra,
        compiler_params=pltpu.CompilerParams(vmem_limit_bytes=VMEM),
        cost_estimate=pl.CostEstimate(
            flops=int(micros * 1.0e9), bytes_accessed=int(micros * 3.0e6), transcendentals=0
        ),
    )(*[value for _, value in ins])


def ring(axis, step):
    count = lax.axis_size(axis)
    return [(i, (i + step) % count) for i in range(count)]


def spread(axis):
    count = lax.axis_size(axis)
    return count <= 8 and count & (count - 1) == 0


def sent_shapes(axis, rows, width):
    count = lax.axis_size(axis)
    return [(rows, width)] * count if spread(axis) else [(count, rows, width)]


def exchange(blocks, axis):
    if not spread(axis):
        return [lax.all_to_all(blocks[0], axis, split_axis=0, concat_axis=0, tiled=True)]
    count = lax.axis_size(axis)
    moved = [blocks[0]] + [None] * (count - 1)
    for k in range(count - 1, 0, -1):
        moved[k] = lax.ppermute(blocks[k], axis, [(i, i ^ k) for i in range(count)])
    return moved


def on_device(strength, offsets, cell_index, migrate_count, ambient):
    _, planes, cols, ny = ambient.shape
    slabs, pencils = lax.axis_size("gz"), lax.axis_size("gx")
    nx, nz, rows = cols * pencils, planes * slabs, cols + RIM
    count = strength.shape[1]
    pair_count = planes // 2
    chunks = ((0, pair_count - 1), tuple(range(1, pair_count - 1)))
    widths = [3 * len(c) * LANES for c in chunks]
    block = nx // slabs

    y_ahead, y_back = [split_table(t) for t in y_tables(ny, pencils, 1.0 / (float(nx) * ny * nz))]
    x_ahead, x_back = [split_table(t) for t in x_tables(nx, cols, pencils, slabs)]
    place = jnp.stack([lax.axis_index("gz"), lax.axis_index("gx")]).astype(jnp.int32)
    here = (SM, place)

    packet, movers = call(
        packet_kernel,
        [
            (SM, migrate_count.reshape(2)),
            (VM, strength),
            (VM, offsets),
            (VM, cell_index.reshape(1, count)),
        ],
        [(VM, (8, count)), (VM, (8, 2 * MIG))],
    )
    up1 = lax.ppermute(packet, "gz", ring("gz", -1))
    down1 = lax.ppermute(packet, "gz", ring("gz", 1))
    up2 = lax.ppermute(movers, "gz", ring("gz", -2))
    down2 = lax.ppermute(movers, "gz", ring("gz", 2))

    meshes, rims, parts = [], [], []
    for chunk, width in zip(chunks, widths):
        size = 2 * len(chunk)
        mesh, rim_high, rim_low, *part = call(
            functools.partial(deposit_kernel, chunk),
            [here]
            + [(VM, value) for value in (packet, up1, down1, up2, down2)]
            + [(HB, ambient), (HB, y_ahead[0]), (HB, y_ahead[1])],
            [(HB, (3, size, cols, ny)), (VM, (6 * size, ny)), (VM, (6 * size, ny))]
            + [(VM, shape) for shape in sent_shapes("gx", rows, width)],
            [
                ((3, size, rows, ny), F32),
                (y_ahead[0].shape, BF16),
                (y_ahead[0].shape, BF16),
                ((pencils, rows, width), F32),
            ],
            sems=size + 2,
            micros=6.0,
        )
        meshes.append(mesh)
        rims.append(lax.ppermute(rim_high, "gx", ring("gx", 1)))
        rims.append(lax.ppermute(rim_low, "gx", ring("gx", -1)))
        parts.append(exchange(part, "gx"))

    spectra = []
    for part, width in zip(parts, widths):
        shapes = sent_shapes("gz", block, width)
        part = call(
            functools.partial(x_ahead_kernel, len(shapes)),
            [here, (VM, x_ahead[0]), (VM, x_ahead[1])] + [(VM, p) for p in part],
            [(VM, shape) for shape in shapes],
            [((pencils, rows, width), F32), ((slabs, block, width), F32)],
        )
        spectra += exchange(part, "gz")
    tile = max(1, block // 4)
    spectra = call(
        functools.partial(wake_kernel, chunks, nx, ny),
        [here] + [(VM, s) for s in spectra],
        [(VM, s.shape) for s in spectra],
        [((3, 2, planes, slabs, tile, LANES), F32), ((3, 2, nz, tile, LANES), F32)],
        micros=6.0,
    )
    each = len(spectra) // len(chunks)
    parts = []
    for n, width in enumerate(widths):
        part = exchange(spectra[n * each : (n + 1) * each], "gz")
        shapes = sent_shapes("gx", rows, width)
        part = call(
            functools.partial(x_back_kernel, len(shapes)),
            [here, (VM, x_back[0]), (VM, x_back[1])] + [(VM, p) for p in part],
            [(VM, shape) for shape in shapes],
            [((slabs, block, width), F32), ((pencils, rows, width), F32)],
        )
        parts.append(exchange(part, "gx"))
    plane = (3, cols, ny)
    tables = [(VM, y_back[0]), (VM, y_back[1])]
    size = 2 * len(chunks[0])
    edges, first, last = call(
        functools.partial(edge_kernel, chunks[0]),
        [here] + tables + [(VM, p) for p in parts[0]],
        [(HB, (3, size, rows, ny)), (VM, plane), (VM, plane)],
        [((pencils, rows, widths[0]), F32), ((3, size, rows, ny), F32)],
        sems=1,
    )
    after = lax.ppermute(first, "gz", ring("gz", -1))
    before = lax.ppermute(last, "gz", ring("gz", 1))
    return tuple(
        call(
            functools.partial(stretch_kernel, chunks),
            [here]
            + tables
            + [(HB, edges), (VM, before), (VM, after)]
            + [(HB, mesh) for mesh in meshes]
            + [(VM, rim) for rim in rims]
            + [(VM, p) for p in parts[1]],
            [(HB, ambient.shape), (HB, ambient.shape)],
            [
                ((pencils, rows, widths[1]), F32),
                ((3, planes, cols + 2 * RIM, ny), F32),
                ((3, planes, cols, ny), F32),
            ],
            sems=4 * planes,
            micros=4.0,
        )
    )


def solution(mesh):
    placed = (
        P(None, ("gz", "gx")),
        P(None, ("gz", "gx")),
        P(("gz", "gx")),
        P("gz", "gx", None),
        P(None, "gz", "gx", None),
    )
    return jax.shard_map(
        on_device,
        mesh=mesh,
        in_specs=placed,
        out_specs=(P(None, "gz", "gx", None), P(None, "gz", "gx", None)),
        check_vma=False,
    )
```

time: 233 us -> 155 us (0.67)
  waiting for transfers between devices: 84.6 us -> 37.8 us
  starting transfers between devices: 39.3 us -> 76.3 us
  blocking collectives: 36.9 us -> 0 us
  Pallas kernels: 57.7 us -> 37 us
  local copies, waits for them, and re-layouts: 9.46 us -> 2.76 us
    all_to_all x6 -> x0, waiting for transfers between devices: 77 us -> none  [exchange(): return lax.all_to_all(values, axis, split_axis=0, concat_axis=0, tiled=True)]
    ppermute x2 -> x44, starting transfers between devices: 1.75 us -> 61.6 us  [the longest x40 58.1 us: exchange(): moved[k] = lax.ppermute(blocks[k], axis, [(i, i ^ k) for i in range(count)])]
    all_to_all x2 -> x0, blocking collectives: 36.9 us -> none  [exchange(): return lax.all_to_all(values, axis, split_axis=0, concat_axis=0, tiled=True)]
    ppermute x2 -> x44, waiting for transfers between devices: 4.32 us -> 32.8 us  [the longest x40 28 us: exchange(): moved[k] = lax.ppermute(blocks[k], axis, [(i, i ^ k) for i in range(count)])]
    all_to_all x6 -> x0, starting transfers between devices: 22.9 us -> none  [exchange(): return lax.all_to_all(values, axis, split_axis=0, concat_axis=0, tiled=True)]
    pallas_call x8 -> x10, Pallas kernels: 57.7 us -> 37 us  [call(): pl.pallas_call(kernel, out_shape=[jax.ShapeDtypeStruct(shape, F32) for _,...]
    unnamed x26, local copies, waits for them, and re-layouts: 8.14 us -> 2.76 us
    ppermute x1, starting transfers between devices: 0.01 us -> 3.08 us  [on_device(): down2 = lax.ppermute(movers, 'gz', ring('gz', 2))]
  transfers between devices with their start and end apart: 14 -> 50, of which waited for: 8 -> 14; matrix products, arithmetic and copies ran while one was open for 0% -> 0% of each run, Pallas kernels for 4% -> 10%
where the time goes in v2:
time: 155 us
  starting transfers between devices  76.3 us (49%)
  waiting for transfers between devices  37.8 us (24%)
  Pallas kernels  37 us (24%)
  local copies, waits for them, and re-layouts  2.76 us (2%)
    ppermute x40, starting transfers between devices, exchange(): moved[k] = lax.ppermute(blocks[k], axis, [(i, i ^ k) for i in range(count)])  58.1 us
    pallas_call x10, Pallas kernels, call(): pl.pallas_call(kernel, out_shape=[jax.ShapeDtypeStruct(shape, F32) for _,...  37 us
    ppermute x40, waiting for transfers between devices, exchange(): moved[k] = lax.ppermute(blocks[k], axis, [(i, i ^ k) for i in range(count)])  28 us
    ppermute x2, waiting for transfers between devices, on_device(): rims.append(lax.ppermute(rim_high, 'gx', ring('gx', 1)))  4.83 us
    ppermute x1, starting transfers between devices, on_device(): after = lax.ppermute(first, 'gz', ring('gz', -1))  3.95 us
  transfers between devices with their start and end apart: 50, of which 14 were waited for; matrix products, arithmetic and copies ran while one was open for 0% of the time, Pallas kernels for 10%

profile of v2, /device:TPU:0, one launch (start us, length us, event | category | flops | bytes accessed | tf_op | source)
XLA Modules:
  0.0 155.0 jit_solution(17253825655353242781)
XLA Ops:
  3.9 3.1 %collective-permute-start.3 = (f32[8,128]{1,0:T(8,128)S(1)}, f32[8,128]{1,0:T(8,128)S(1)}, u32[]{:S(2)}, u32[]{:S(2)}) collective-permute-start(f32[8,128]{1,0:T(8,128)S(1)} %get-tuple-element.62), channel_id=1, source_target_pairs={{0,8},{4,12},{8,16},{12,20},{16,24},{20,28},{24,0},{28,4},{1,9},{5... | collective-permute-start | bytes 12296 | tf_op jit(solution)/shard_map/ppermute | solution.py:626
  7.0 2.1 %collective-permute-start.2 = (f32[8,128]{1,0:T(8,128)S(1)}, f32[8,128]{1,0:T(8,128)S(1)}, u32[]{:S(2)}, u32[]{:S(2)}) collective-permute-start(f32[8,128]{1,0:T(8,128)S(1)} %get-tuple-element.62), channel_id=1, source_target_pairs={{0,24},{4,28},{8,0},{12,4},{16,8},{20,12},{24,16},{28,20},{1,25},{... | collective-permute-start | bytes 12296 | tf_op jit(solution)/shard_map/ppermute | solution.py:625
  9.1 1.6 %collective-permute-start.1 = (f32[8,512]{1,0:T(8,128)S(1)}, f32[8,512]{1,0:T(8,128)S(1)}, u32[]{:S(2)}, u32[]{:S(2)}) collective-permute-start(f32[8,512]{1,0:T(8,128)S(1)} %get-tuple-element.61.own), channel_id=1, source_target_pairs={{0,4},{4,8},{8,12},{12,16},{16,20},{20,24},{24,28},{28,0},{1,5},{5... | collective-permute-start | bytes 49160 | tf_op jit(solution)/shard_map/ppermute | solution.py:624
  10.7 3.1 %collective-permute-start = (f32[8,512]{1,0:T(8,128)S(1)}, f32[8,512]{1,0:T(8,128)S(1)}, u32[]{:S(2)}, u32[]{:S(2)}) collective-permute-start(f32[8,512]{1,0:T(8,128)S(1)} %get-tuple-element.61.own), channel_id=1, source_target_pairs={{0,28},{4,0},{8,4},{12,8},{16,12},{20,16},{24,20},{28,24},{1,29},{... | collective-permute-start | bytes 49160 | tf_op jit(solution)/shard_map/ppermute | solution.py:623
  13.9 1.6 %collective-permute-done.1.down1 = f32[8,512]{1,0:T(8,128)S(1)} collective-permute-done((f32[8,512]{1,0:T(8,128)S(1)}, f32[8,512]{1,0:T(8,128)S(1)}, u32[]{:S(2)}, u32[]{:S(2)}) %collective-permute-start.1) | collective-permute-done | bytes 16416 | tf_op jit(solution)/shard_map/ppermute | solution.py:624
  15.6 4.8 %shard_map.143 = (f32[3,4,64,256]{3,2,1,0:T(8,128)S(1)}, f32[24,256]{1,0:T(8,128)S(1)}, f32[24,256]{1,0:T(8,128)S(1)}, f32[72,768]{1,0:T(8,128)S(1)}, f32[72,768...) custom-call(s32[2]{0:T(128)S(1)} %pad_add_fusion.place, f32[8,512]{1,0:T(8,128)S(1)} %get-tuple-element.61.own, ...), custom_call_target="tpu_custom_call" | custom-call | flops 6000000000 | bytes 18000000 | tf_op jit(solution)/shard_map/pallas_call | solution.py:560
  20.4 1.7 %collective-permute-start.15 = (f32[72,768]{1,0:T(8,128)S(1)}, f32[72,768]{1,0:T(8,128)S(1)}, u32[]{:S(2)}, u32[]{:S(2)}) collective-permute-start(f32[72,768]{1,0:T(8,128)S(1)} %get-tuple-element.77), channel_id=1, source_target_pairs={{0,2},{1,3},{2,0},{3,1},{4,6},{5,7},{6,4},{7,5},{8,10},{9,11},{10,... | collective-permute-start | bytes 663560 | tf_op jit(solution)/shard_map/ppermute | solution.py:594
  22.3 7.7 %shard_map.141 = (f32[3,4,64,256]{3,2,1,0:T(8,128)S(1)}, f32[24,256]{1,0:T(8,128)S(1)}, f32[24,256]{1,0:T(8,128)S(1)}, f32[72,768]{1,0:T(8,128)S(1)}, f32[72,768...) custom-call(s32[2]{0:T(128)S(1)} %pad_add_fusion.place, f32[8,512]{1,0:T(8,128)S(1)} %get-tuple-element.61.own, ...), custom_call_target="tpu_custom_call" | custom-call | flops 6000000000 | bytes 18000000 | tf_op jit(solution)/shard_map/pallas_call | solution.py:560
  30.4 1.7 %collective-permute-start.5 = (f32[72,768]{1,0:T(8,128)S(1)}, f32[72,768]{1,0:T(8,128)S(1)}, u32[]{:S(2)}, u32[]{:S(2)}) collective-permute-start(f32[72,768]{1,0:T(8,128)S(1)} %get-tuple-element.65), channel_id=1, source_target_pairs={{0,2},{1,3},{2,0},{3,1},{4,6},{5,7},{6,4},{7,5},{8,10},{9,11},{10,... | collective-permute-start | bytes 663560 | tf_op jit(solution)/shard_map/ppermute | solution.py:594
  32.6 1.6 %shard_map.144 = (f32[32,768]{1,0:T(8,128)S(1)}, f32[32,768]{1,0:T(8,128)S(1)}, f32[32,768]{1,0:T(8,128)S(1)}, f32[32,768]{1,0:T(8,128)S(1)}, f32[32,768]{1,0:T(...) custom-call(s32[2]{0:T(128)S(1)} %pad_add_fusion.place, ...), custom_call_target="tpu_custom_call" | custom-call | flops 2000000000 | bytes 6000000 | tf_op jit(solution)/shard_map/pallas_call | solution.py:560
  35.4 2.3 %collective-permute-start.19 = (f32[32,768]{1,0:T(8,128)S(1)}, f32[32,768]{1,0:T(8,128)S(1)}, u32[]{:S(2)}, u32[]{:S(2)}) collective-permute-start(f32[32,768]{1,0:T(8,128)S(1)} %get-tuple-element.82), channel_id=1, source_target_pairs={{0,12},{4,8},{8,4},{12,0},{16,28},{20,24},{24,20},{28,16},{1,13},{... | collective-permute-start | bytes 294920 | tf_op jit(solution)/shard_map/ppermute | solution.py:594
  38.7 1.5 collective-permute-start.20
  40.2 1.7 %collective-permute-done.6.refs_3_ = f32[72,768]{1,0:T(8,128)S(1)} collective-permute-done((f32[72,768]{1,0:T(8,128)S(1)}, f32[72,768]{1,0:T(8,128)S(1)}, u32[]{:S(2)}, u32[]{:S(2)}) %collective-permute-start.6) | collective-permute-done | bytes 221216 | tf_op jit(solution)/shard_map/ppermute | solution.py:594
  41.9 1.6 %collective-permute-start.21 = (f32[32,768]{1,0:T(8,128)S(1)}, f32[32,768]{1,0:T(8,128)S(1)}, u32[]{:S(2)}, u32[]{:S(2)}) collective-permute-start(f32[32,768]{1,0:T(8,128)S(1)} %get-tuple-element.84), channel_id=1, source_target_pairs={{0,20},{4,16},{8,28},{12,24},{16,4},{20,0},{24,12},{28,8},{1,21},{... | collective-permute-start | bytes 294920 | tf_op jit(solution)/shard_map/ppermute | solution.py:594
  43.5 1.6 %shard_map.142 = (f32[32,768]{1,0:T(8,128)S(1)}, f32[32,768]{1,0:T(8,128)S(1)}, f32[32,768]{1,0:T(8,128)S(1)}, f32[32,768]{1,0:T(8,128)S(1)}, f32[32,768]{1,0:T(...) custom-call(s32[2]{0:T(128)S(1)} %pad_add_fusion.place, ...), custom_call_target="tpu_custom_call" | custom-call | flops 2000000000 | bytes 6000000 | tf_op jit(solution)/shard_map/pallas_call | solution.py:560
  45.1 2.9 %collective-permute-start.22 = (f32[32,768]{1,0:T(8,128)S(1)}, f32[32,768]{1,0:T(8,128)S(1)}, u32[]{:S(2)}, u32[]{:S(2)}) collective-permute-start(f32[32,768]{1,0:T(8,128)S(1)} %get-tuple-element.85), channel_id=1, source_target_pairs={{0,24},{4,28},{8,16},{12,20},{16,8},{20,12},{24,0},{28,4},{1,25},{... | collective-permute-start | bytes 294920 | tf_op jit(solution)/shard_map/ppermute | solution.py:594
  48.3 2.1 %collective-permute-start.7 = (f32[32,768]{1,0:T(8,128)S(1)}, f32[32,768]{1,0:T(8,128)S(1)}, u32[]{:S(2)}, u32[]{:S(2)}) collective-permute-start(f32[32,768]{1,0:T(8,128)S(1)} %get-tuple-element.68), channel_id=1, source_target_pairs={{0,4},{4,0},{8,12},{12,8},{16,20},{20,16},{24,28},{28,24},{1,5},{5... | collective-permute-start | bytes 294920 | tf_op jit(solution)/shard_map/ppermute | solution.py:594
  50.4 1.9 %collective-permute-start.8 = (f32[32,768]{1,0:T(8,128)S(1)}, f32[32,768]{1,0:T(8,128)S(1)}, u32[]{:S(2)}, u32[]{:S(2)}) collective-permute-start(f32[32,768]{1,0:T(8,128)S(1)} %get-tuple-element.69), channel_id=1, source_target_pairs={{0,8},{4,12},{8,0},{12,4},{16,24},{20,28},{24,16},{28,20},{1,9},{5... | collective-permute-start | bytes 294920 | tf_op jit(solution)/shard_map/ppermute | solution.py:594
  52.3 3.0 %collective-permute-done.21.refs_13_ = f32[32,768]{1,0:T(8,128)S(1)} collective-permute-done((f32[32,768]{1,0:T(8,128)S(1)}, f32[32,768]{1,0:T(8,128)S(1)}, u32[]{:S(2)}, u32[]{:S(2)}) %collective-permute-start.21) | collective-permute-done | bytes 98336 | tf_op jit(solution)/shard_map/ppermute | solution.py:594
  55.4 3.5 %collective-permute-start.10 = (f32[32,768]{1,0:T(8,128)S(1)}, f32[32,768]{1,0:T(8,128)S(1)}, u32[]{:S(2)}, u32[]{:S(2)}) collective-permute-start(f32[32,768]{1,0:T(8,128)S(1)} %get-tuple-element.71), channel_id=1, source_target_pairs={{0,16},{4,20},{8,24},{12,28},{16,0},{20,4},{24,8},{28,12},{1,17},{... | collective-permute-start | bytes 294920 | tf_op jit(solution)/shard_map/ppermute | solution.py:594
  58.9 4.0 %collective-permute-start.11 = (f32[32,768]{1,0:T(8,128)S(1)}, f32[32,768]{1,0:T(8,128)S(1)}, u32[]{:S(2)}, u32[]{:S(2)}) collective-permute-start(f32[32,768]{1,0:T(8,128)S(1)} %get-tuple-element.72), channel_id=1, source_target_pairs={{0,20},{4,16},{8,28},{12,24},{16,4},{20,0},{24,12},{28,8},{1,21},{... | collective-permute-start | bytes 294920 | tf_op jit(solution)/shard_map/ppermute | solution.py:594
  62.9 2.2 %collective-permute-start.12 = (f32[32,768]{1,0:T(8,128)S(1)}, f32[32,768]{1,0:T(8,128)S(1)}, u32[]{:S(2)}, u32[]{:S(2)}) collective-permute-start(f32[32,768]{1,0:T(8,128)S(1)} %get-tuple-element.73), channel_id=1, source_target_pairs={{0,24},{4,28},{8,16},{12,20},{16,8},{20,12},{24,0},{28,4},{1,25},{... | collective-permute-start | bytes 294920 | tf_op jit(solution)/shard_map/ppermute | solution.py:594
  65.1 2.1 %collective-permute-start.13 = (f32[32,768]{1,0:T(8,128)S(1)}, f32[32,768]{1,0:T(8,128)S(1)}, u32[]{:S(2)}, u32[]{:S(2)}) collective-permute-start(f32[32,768]{1,0:T(8,128)S(1)} %get-tuple-element.74), channel_id=1, source_target_pairs={{0,28},{4,24},{8,20},{12,16},{16,12},{20,8},{24,4},{28,0},{1,29},{... | collective-permute-start | bytes 294920 | tf_op jit(solution)/shard_map/ppermute | solution.py:594
  67.2 6.9 %collective-permute-done.11.refs_5_ = f32[32,768]{1,0:T(8,128)S(1)} collective-permute-done((f32[32,768]{1,0:T(8,128)S(1)}, f32[32,768]{1,0:T(8,128)S(1)}, u32[]{:S(2)}, u32[]{:S(2)}) %collective-permute-start.11) | collective-permute-done | bytes 98336 | tf_op jit(solution)/shard_map/ppermute | solution.py:594
  74.1 11.1 %shard_map.145 = (f32[32,768]{1,0:T(8,128)S(1)}, f32[32,768]{1,0:T(8,128)S(1)}, f32[32,768]{1,0:T(8,128)S(1)}, f32[32,768]{1,0:T(8,128)S(1)}, f32[32,768]{1,0:T(...) custom-call(s32[2]{0:T(128)S(1)} %pad_add_fusion.place, ...), custom_call_target="tpu_custom_call" | custom-call | flops 6000000000 | bytes 18000000 | tf_op jit(solution)/shard_map/pallas_call | solution.py:560
  85.8 4.5 %collective-permute-start.25 = (f32[32,768]{1,0:T(8,128)S(1)}, f32[32,768]{1,0:T(8,128)S(1)}, u32[]{:S(2)}, u32[]{:S(2)}) collective-permute-start(f32[32,768]{1,0:T(8,128)S(1)} %get-tuple-element.89), channel_id=1, source_target_pairs={{0,8},{4,12},{8,0},{12,4},{16,24},{20,28},{24,16},{28,20},{1,9},{5... | collective-permute-start | bytes 294920 | tf_op jit(solution)/shard_map/ppermute | solution.py:594
  90.8 1.8 %collective-permute-start.27 = (f32[32,768]{1,0:T(8,128)S(1)}, f32[32,768]{1,0:T(8,128)S(1)}, u32[]{:S(2)}, u32[]{:S(2)}) collective-permute-start(f32[32,768]{1,0:T(8,128)S(1)} %get-tuple-element.91), channel_id=1, source_target_pairs={{0,16},{4,20},{8,24},{12,28},{16,0},{20,4},{24,8},{28,12},{1,17},{... | collective-permute-start | bytes 294920 | tf_op jit(solution)/shard_map/ppermute | solution.py:594
  94.1 1.8 %collective-permute-start.29 = (f32[32,768]{1,0:T(8,128)S(1)}, f32[32,768]{1,0:T(8,128)S(1)}, u32[]{:S(2)}, u32[]{:S(2)}) collective-permute-start(f32[32,768]{1,0:T(8,128)S(1)} %get-tuple-element.93), channel_id=1, source_target_pairs={{0,24},{4,28},{8,16},{12,20},{16,8},{20,12},{24,0},{28,4},{1,25},{... | collective-permute-start | bytes 294920 | tf_op jit(solution)/shard_map/ppermute | solution.py:594
  95.9 2.6 %collective-permute-start.30 = (f32[32,768]{1,0:T(8,128)S(1)}, f32[32,768]{1,0:T(8,128)S(1)}, u32[]{:S(2)}, u32[]{:S(2)}) collective-permute-start(f32[32,768]{1,0:T(8,128)S(1)} %get-tuple-element.94), channel_id=1, source_target_pairs={{0,28},{4,24},{8,20},{12,16},{16,12},{20,8},{24,4},{28,0},{1,29},{... | collective-permute-start | bytes 294920 | tf_op jit(solution)/shard_map/ppermute | solution.py:594
  99.4 4.6 %collective-permute-done.27.refs_4_ = f32[32,768]{1,0:T(8,128)S(1)} collective-permute-done((f32[32,768]{1,0:T(8,128)S(1)}, f32[32,768]{1,0:T(8,128)S(1)}, u32[]{:S(2)}, u32[]{:S(2)}) %collective-permute-start.27) | collective-permute-done | bytes 98336 | tf_op jit(solution)/shard_map/ppermute | solution.py:594
  104.0 3.7 %collective-permute-done.28.refs_5_ = f32[32,768]{1,0:T(8,128)S(1)} collective-permute-done((f32[32,768]{1,0:T(8,128)S(1)}, f32[32,768]{1,0:T(8,128)S(1)}, u32[]{:S(2)}, u32[]{:S(2)}) %collective-permute-start.28) | collective-permute-done | bytes 98336 | tf_op jit(solution)/shard_map/ppermute | solution.py:594
  107.7 2.5 %collective-permute-start.43 = (f32[32,768]{1,0:T(8,128)S(1)}, f32[32,768]{1,0:T(8,128)S(1)}, u32[]{:S(2)}, u32[]{:S(2)}) collective-permute-start(f32[32,768]{1,0:T(8,128)S(1)} %get-tuple-element.112), channel_id=1, source_target_pairs={{0,16},{4,20},{8,24},{12,28},{16,0},{20,4},{24,8},{28,12},{1,17},{... | collective-permute-start | bytes 294920 | tf_op jit(solution)/shard_map/ppermute | solution.py:594
  110.2 3.4 %collective-permute-start.44 = (f32[32,768]{1,0:T(8,128)S(1)}, f32[32,768]{1,0:T(8,128)S(1)}, u32[]{:S(2)}, u32[]{:S(2)}) collective-permute-start(f32[32,768]{1,0:T(8,128)S(1)} %get-tuple-element.113), channel_id=1, source_target_pairs={{0,20},{4,16},{8,28},{12,24},{16,4},{20,0},{24,12},{28,8},{1,21},{... | collective-permute-start | bytes 294920 | tf_op jit(solution)/shard_map/ppermute | solution.py:594
  113.6 1.9 %collective-permute-start.45 = (f32[32,768]{1,0:T(8,128)S(1)}, f32[32,768]{1,0:T(8,128)S(1)}, u32[]{:S(2)}, u32[]{:S(2)}) collective-permute-start(f32[32,768]{1,0:T(8,128)S(1)} %get-tuple-element.114), channel_id=1, source_target_pairs={{0,24},{4,28},{8,16},{12,20},{16,8},{20,12},{24,0},{28,4},{1,25},{... | collective-permute-start | bytes 294920 | tf_op jit(solution)/shard_map/ppermute | solution.py:594
  115.5 2.8 %collective-permute-start.46 = (f32[32,768]{1,0:T(8,128)S(1)}, f32[32,768]{1,0:T(8,128)S(1)}, u32[]{:S(2)}, u32[]{:S(2)}) collective-permute-start(f32[32,768]{1,0:T(8,128)S(1)} %get-tuple-element.115), channel_id=1, source_target_pairs={{0,28},{4,24},{8,20},{12,16},{16,12},{20,8},{24,4},{28,0},{1,29},{... | collective-permute-start | bytes 294920 | tf_op jit(solution)/shard_map/ppermute | solution.py:594
  118.3 1.7 %shard_map.146 = (f32[72,768]{1,0:T(8,128)S(1)}, f32[72,768]{1,0:T(8,128)S(1)}, f32[72,768]{1,0:T(8,128)S(1)}, f32[72,768]{1,0:T(8,128)S(1)}) custom-call(s32[2]{0:T(128)S(1)} %pad_add_fusion.place, bf16[576,256]{1,0:T(8,128)(2,1)S(1)} %copy-done.10, bf16[576,256]{1,0:T(8,128)(2,1)S(1)} %copy-done.9, f32[32,768]{1,0:T(8,128)S(1)} %get-tuple-element.87.refs_0_, ...), custom_call_target="tpu_custom_call" | custom-call | flops 2000000000 | bytes 6000000 | tf_op jit(solution)/shard_map/pallas_call | solution.py:560
  120.7 1.5 collective-permute-start.32
  122.3 2.3 %collective-permute-done.44.refs_5_ = f32[32,768]{1,0:T(8,128)S(1)} collective-permute-done((f32[32,768]{1,0:T(8,128)S(1)}, f32[32,768]{1,0:T(8,128)S(1)}, u32[]{:S(2)}, u32[]{:S(2)}) %collective-permute-start.44) | collective-permute-done | bytes 98336 | tf_op jit(solution)/shard_map/ppermute | solution.py:594
  124.6 1.6 %collective-permute-start.38 = (f32[24,256]{1,0:T(8,128)S(1)}, f32[24,256]{1,0:T(8,128)S(1)}, u32[]{:S(2)}, u32[]{:S(2)}) collective-permute-start(f32[24,256]{1,0:T(8,128)S(1)} %get-tuple-element.106), channel_id=1, source_target_pairs={{0,1},{1,2},{2,3},{3,0},{4,5},{5,6},{6,7},{7,4},{8,9},{9,10},{10,1... | collective-permute-start | bytes 73736 | tf_op jit(solution)/shard_map/ppermute | solution.py:648
  126.4 1.7 %shard_map.148 = (f32[72,768]{1,0:T(8,128)S(1)}, f32[72,768]{1,0:T(8,128)S(1)}, f32[72,768]{1,0:T(8,128)S(1)}, f32[72,768]{1,0:T(8,128)S(1)}) custom-call(s32[2]{0:T(128)S(1)} %pad_add_fusion.place, bf16[576,256]{1,0:T(8,128)(2,1)S(1)} %copy-done.10, bf16[576,256]{1,0:T(8,128)(2,1)S(1)} %copy-done.9, f32[32,768]{1,0:T(8,128)S(1)} %get-tuple-element.108.refs_0_, ...), custom_call_target="tpu_custom_call" | custom-call | flops 2000000000 | bytes 6000000 | tf_op jit(solution)/shard_map/pallas_call | solution.py:560
  128.1 4.8 %collective-permute-done.38.refs_4_ = f32[24,256]{1,0:T(8,128)S(1)} collective-permute-done((f32[24,256]{1,0:T(8,128)S(1)}, f32[24,256]{1,0:T(8,128)S(1)}, u32[]{:S(2)}, u32[]{:S(2)}) %collective-permute-start.38) | collective-permute-done | bytes 24608 | tf_op jit(solution)/shard_map/ppermute | solution.py:648
  132.9 1.7 %collective-permute-start.37 = (f32[24,256]{1,0:T(8,128)S(1)}, f32[24,256]{1,0:T(8,128)S(1)}, u32[]{:S(2)}, u32[]{:S(2)}) collective-permute-start(f32[24,256]{1,0:T(8,128)S(1)} %get-tuple-element.105), channel_id=1, source_target_pairs={{0,3},{1,0},{2,1},{3,2},{4,7},{5,4},{6,5},{7,6},{8,11},{9,8},{10,9... | collective-permute-start | bytes 73736 | tf_op jit(solution)/shard_map/ppermute | solution.py:649
  136.5 1.7 %shard_map.147 = (f32[3,4,72,256]{3,2,1,0:T(8,128)S(1)}, f32[3,64,256]{2,1,0:T(8,128)S(1)}, f32[3,64,256]{2,1,0:T(8,128)S(1)}) custom-call(s32[2]{0:T(128)S(1)} %pad_add_fusion.place, bf16[512,512]{1,0:T(8,128)(2,1)S(1)} %copy-done.6, bf16[512,512]{1,0:T(8,128)(2,1)S(1)} %copy-done.5, f32[72,768]{1,0:T(8,128)S(1)} %get-tuple-element.95.refs_0_, ...), custom_call_target="tpu_custom_call" | custom-call | flops 2000000000 | bytes 6000000 | tf_op jit(solution)/shard_map/pallas_call | solution.py:560
  139.1 4.0 %collective-permute-start.35 = (f32[3,64,256]{2,1,0:T(8,128)S(1)}, f32[3,64,256]{2,1,0:T(8,128)S(1)}, u32[]{:S(2)}, u32[]{:S(2)}) collective-permute-start(f32[3,64,256]{2,1,0:T(8,128)S(1)} %get-tuple-element.101), channel_id=1, source_target_pairs={{0,28},{4,0},{8,4},{12,8},{16,12},{20,16},{24,20},{28,24},{1,29},{... | collective-permute-start | bytes 589832 | tf_op jit(solution)/shard_map/ppermute | solution.py:692
  143.0 3.8 %collective-permute-done.49.refs_9_ = f32[72,768]{1,0:T(8,128)S(1)} collective-permute-done((f32[72,768]{1,0:T(8,128)S(1)}, f32[72,768]{1,0:T(8,128)S(1)}, u32[]{:S(2)}, u32[]{:S(2)}) %collective-permute-start.49) | collective-permute-done | bytes 221216 | tf_op jit(solution)/shard_map/ppermute | solution.py:594
  146.8 1.5 collective-permute-done.34.before
  148.2 1.9 %collective-permute-done.35.after = f32[3,64,256]{2,1,0:T(8,128)S(1)} collective-permute-done((f32[3,64,256]{2,1,0:T(8,128)S(1)}, f32[3,64,256]{2,1,0:T(8,128)S(1)}, u32[]{:S(2)}, u32[]{:S(2)}) %collective-permute-start.35) | collective-permute-done | bytes 196640 | tf_op jit(solution)/shard_map/ppermute | solution.py:692
  150.1 4.7 %shard_map.149 = (f32[3,8,64,256]{3,2,1,0:T(8,128)}, f32[3,8,64,256]{3,2,1,0:T(8,128)}) custom-call(s32[2]{0:T(128)S(1)} %pad_add_fusion.place, bf16[512,512]{1,0:T(8,128)(2,1)S(1)} %copy-done.6, bf16[512,512]{1,0:T(8,128)(2,1)S(1)} %copy-done.5, f32[3,4,72,256]{3,2,1,0:T(8,128)S(1)} %get-tuple-element.99.edges, ...), custom_call_target="tpu_custom_call" | custom-call | flops 4000000000 | bytes 12000000 | tf_op jit(solution)/shard_map/pallas_call | solution.py:560
  (89 shorter events, 14.4 us)
Async XLA Ops:
  3.9 10.0 %collective-permute-start.3 = (f32[8,128]{1,0:T(8,128)S(1)}, f32[8,128]{1,0:T(8,128)S(1)}, u32[]{:S(2)}, u32[]{:S(2)}) collective-permute-start(f32[8,128]{1,0:T(8,128)S(1)} %get-tuple-element.62), channel_id=1, source_target_pairs={{0,8},{4,12},{8,16},{12,20},{16,24},{20,28},{24,0},{28,4},{1,9},{5... | collective-permute-start | bytes 12296 | tf_op jit(solution)/shard_map/ppermute | solution.py:626
  7.0 6.9 %collective-permute-start.2 = (f32[8,128]{1,0:T(8,128)S(1)}, f32[8,128]{1,0:T(8,128)S(1)}, u32[]{:S(2)}, u32[]{:S(2)}) collective-permute-start(f32[8,128]{1,0:T(8,128)S(1)} %get-tuple-element.62), channel_id=1, source_target_pairs={{0,24},{4,28},{8,0},{12,4},{16,8},{20,12},{24,16},{28,20},{1,25},{... | collective-permute-start | bytes 12296 | tf_op jit(solution)/shard_map/ppermute | solution.py:625
  9.1 6.4 %collective-permute-start.1 = (f32[8,512]{1,0:T(8,128)S(1)}, f32[8,512]{1,0:T(8,128)S(1)}, u32[]{:S(2)}, u32[]{:S(2)}) collective-permute-start(f32[8,512]{1,0:T(8,128)S(1)} %get-tuple-element.61.own), channel_id=1, source_target_pairs={{0,4},{4,8},{8,12},{12,16},{16,20},{20,24},{24,28},{28,0},{1,5},{5... | collective-permute-start | bytes 49160 | tf_op jit(solution)/shard_map/ppermute | solution.py:624
  20.4 11.7 %collective-permute-start.14 = (f32[72,768]{1,0:T(8,128)S(1)}, f32[72,768]{1,0:T(8,128)S(1)}, u32[]{:S(2)}, u32[]{:S(2)}) collective-permute-start(f32[72,768]{1,0:T(8,128)S(1)} %get-tuple-element.76), channel_id=1, source_target_pairs={{0,1},{1,0},{2,3},{3,2},{4,5},{5,4},{6,7},{7,6},{8,9},{9,8},{10,11... | collective-permute-start | bytes 663560 | tf_op jit(solution)/shard_map/ppermute | solution.py:594
  20.4 11.7 %collective-permute-start.15 = (f32[72,768]{1,0:T(8,128)S(1)}, f32[72,768]{1,0:T(8,128)S(1)}, u32[]{:S(2)}, u32[]{:S(2)}) collective-permute-start(f32[72,768]{1,0:T(8,128)S(1)} %get-tuple-element.77), channel_id=1, source_target_pairs={{0,2},{1,3},{2,0},{3,1},{4,6},{5,7},{6,4},{7,5},{8,10},{9,11},{10,... | collective-permute-start | bytes 663560 | tf_op jit(solution)/shard_map/ppermute | solution.py:594
  22.2 10.4 %collective-permute-start.16 = (f32[72,768]{1,0:T(8,128)S(1)}, f32[72,768]{1,0:T(8,128)S(1)}, u32[]{:S(2)}, u32[]{:S(2)}) collective-permute-start(f32[72,768]{1,0:T(8,128)S(1)} %get-tuple-element.78), channel_id=1, source_target_pairs={{0,3},{1,2},{2,1},{3,0},{4,7},{5,6},{6,5},{7,4},{8,11},{9,10},{10,... | collective-permute-start | bytes 663560 | tf_op jit(solution)/shard_map/ppermute | solution.py:594
  30.0 5.4 %collective-permute-start.4 = (f32[72,768]{1,0:T(8,128)S(1)}, f32[72,768]{1,0:T(8,128)S(1)}, u32[]{:S(2)}, u32[]{:S(2)}) collective-permute-start(f32[72,768]{1,0:T(8,128)S(1)} %get-tuple-element.64), channel_id=1, source_target_pairs={{0,1},{1,0},{2,3},{3,2},{4,5},{5,4},{6,7},{7,6},{8,9},{9,8},{10,11... | collective-permute-start | bytes 663560 | tf_op jit(solution)/shard_map/ppermute | solution.py:594
  30.4 8.3 %collective-permute-start.5 = (f32[72,768]{1,0:T(8,128)S(1)}, f32[72,768]{1,0:T(8,128)S(1)}, u32[]{:S(2)}, u32[]{:S(2)}) collective-permute-start(f32[72,768]{1,0:T(8,128)S(1)} %get-tuple-element.65), channel_id=1, source_target_pairs={{0,2},{1,3},{2,0},{3,1},{4,6},{5,7},{6,4},{7,5},{8,10},{9,11},{10,... | collective-permute-start | bytes 663560 | tf_op jit(solution)/shard_map/ppermute | solution.py:594
  32.1 9.8 %collective-permute-start.6 = (f32[72,768]{1,0:T(8,128)S(1)}, f32[72,768]{1,0:T(8,128)S(1)}, u32[]{:S(2)}, u32[]{:S(2)}) collective-permute-start(f32[72,768]{1,0:T(8,128)S(1)} %get-tuple-element.66), channel_id=1, source_target_pairs={{0,3},{1,2},{2,1},{3,0},{4,7},{5,6},{6,5},{7,4},{8,11},{9,10},{10,... | collective-permute-start | bytes 663560 | tf_op jit(solution)/shard_map/ppermute | solution.py:594
  34.2 10.9 %collective-permute-start.17 = (f32[32,768]{1,0:T(8,128)S(1)}, f32[32,768]{1,0:T(8,128)S(1)}, u32[]{:S(2)}, u32[]{:S(2)}) collective-permute-start(f32[32,768]{1,0:T(8,128)S(1)} %get-tuple-element.80), channel_id=1, source_target_pairs={{0,4},{4,0},{8,12},{12,8},{16,20},{20,16},{24,28},{28,24},{1,5},{5... | collective-permute-start | bytes 294920 | tf_op jit(solution)/shard_map/ppermute | solution.py:594
  34.3 13.7 %collective-permute-start.18 = (f32[32,768]{1,0:T(8,128)S(1)}, f32[32,768]{1,0:T(8,128)S(1)}, u32[]{:S(2)}, u32[]{:S(2)}) collective-permute-start(f32[32,768]{1,0:T(8,128)S(1)} %get-tuple-element.81), channel_id=1, source_target_pairs={{0,8},{4,12},{8,0},{12,4},{16,24},{20,28},{24,16},{28,20},{1,9},{5... | collective-permute-start | bytes 294920 | tf_op jit(solution)/shard_map/ppermute | solution.py:594
  35.4 12.9 %collective-permute-start.19 = (f32[32,768]{1,0:T(8,128)S(1)}, f32[32,768]{1,0:T(8,128)S(1)}, u32[]{:S(2)}, u32[]{:S(2)}) collective-permute-start(f32[32,768]{1,0:T(8,128)S(1)} %get-tuple-element.82), channel_id=1, source_target_pairs={{0,12},{4,8},{8,4},{12,0},{16,28},{20,24},{24,20},{28,16},{1,13},{... | collective-permute-start | bytes 294920 | tf_op jit(solution)/shard_map/ppermute | solution.py:594
  38.7 11.8 %collective-permute-start.20 = (f32[32,768]{1,0:T(8,128)S(1)}, f32[32,768]{1,0:T(8,128)S(1)}, u32[]{:S(2)}, u32[]{:S(2)}) collective-permute-start(f32[32,768]{1,0:T(8,128)S(1)} %get-tuple-element.83), channel_id=1, source_target_pairs={{0,16},{4,20},{8,24},{12,28},{16,0},{20,4},{24,8},{28,12},{1,17},{... | collective-permute-start | bytes 294920 | tf_op jit(solution)/shard_map/ppermute | solution.py:594
  41.9 13.4 %collective-permute-start.21 = (f32[32,768]{1,0:T(8,128)S(1)}, f32[32,768]{1,0:T(8,128)S(1)}, u32[]{:S(2)}, u32[]{:S(2)}) collective-permute-start(f32[32,768]{1,0:T(8,128)S(1)} %get-tuple-element.84), channel_id=1, source_target_pairs={{0,20},{4,16},{8,28},{12,24},{16,4},{20,0},{24,12},{28,8},{1,21},{... | collective-permute-start | bytes 294920 | tf_op jit(solution)/shard_map/ppermute | solution.py:594
  45.1 10.4 %collective-permute-start.22 = (f32[32,768]{1,0:T(8,128)S(1)}, f32[32,768]{1,0:T(8,128)S(1)}, u32[]{:S(2)}, u32[]{:S(2)}) collective-permute-start(f32[32,768]{1,0:T(8,128)S(1)} %get-tuple-element.85), channel_id=1, source_target_pairs={{0,24},{4,28},{8,16},{12,20},{16,8},{20,12},{24,0},{28,4},{1,25},{... | collective-permute-start | bytes 294920 | tf_op jit(solution)/shard_map/ppermute | solution.py:594
  48.0 10.9 %collective-permute-start.23 = (f32[32,768]{1,0:T(8,128)S(1)}, f32[32,768]{1,0:T(8,128)S(1)}, u32[]{:S(2)}, u32[]{:S(2)}) collective-permute-start(f32[32,768]{1,0:T(8,128)S(1)} %get-tuple-element.86), channel_id=1, source_target_pairs={{0,28},{4,24},{8,20},{12,16},{16,12},{20,8},{24,4},{28,0},{1,29},{... | collective-permute-start | bytes 294920 | tf_op jit(solution)/shard_map/ppermute | solution.py:594
  48.3 14.6 %collective-permute-start.7 = (f32[32,768]{1,0:T(8,128)S(1)}, f32[32,768]{1,0:T(8,128)S(1)}, u32[]{:S(2)}, u32[]{:S(2)}) collective-permute-start(f32[32,768]{1,0:T(8,128)S(1)} %get-tuple-element.68), channel_id=1, source_target_pairs={{0,4},{4,0},{8,12},{12,8},{16,20},{20,16},{24,28},{28,24},{1,5},{5... | collective-permute-start | bytes 294920 | tf_op jit(solution)/shard_map/ppermute | solution.py:594
  50.4 14.7 %collective-permute-start.8 = (f32[32,768]{1,0:T(8,128)S(1)}, f32[32,768]{1,0:T(8,128)S(1)}, u32[]{:S(2)}, u32[]{:S(2)}) collective-permute-start(f32[32,768]{1,0:T(8,128)S(1)} %get-tuple-element.69), channel_id=1, source_target_pairs={{0,8},{4,12},{8,0},{12,4},{16,24},{20,28},{24,16},{28,20},{1,9},{5... | collective-permute-start | bytes 294920 | tf_op jit(solution)/shard_map/ppermute | solution.py:594
  55.3 11.9 %collective-permute-start.9 = (f32[32,768]{1,0:T(8,128)S(1)}, f32[32,768]{1,0:T(8,128)S(1)}, u32[]{:S(2)}, u32[]{:S(2)}) collective-permute-start(f32[32,768]{1,0:T(8,128)S(1)} %get-tuple-element.70), channel_id=1, source_target_pairs={{0,12},{4,8},{8,4},{12,0},{16,28},{20,24},{24,20},{28,16},{1,13},{... | collective-permute-start | bytes 294920 | tf_op jit(solution)/shard_map/ppermute | solution.py:594
  55.4 11.8 %collective-permute-start.10 = (f32[32,768]{1,0:T(8,128)S(1)}, f32[32,768]{1,0:T(8,128)S(1)}, u32[]{:S(2)}, u32[]{:S(2)}) collective-permute-start(f32[32,768]{1,0:T(8,128)S(1)} %get-tuple-element.71), channel_id=1, source_target_pairs={{0,16},{4,20},{8,24},{12,28},{16,0},{20,4},{24,8},{28,12},{1,17},{... | collective-permute-start | bytes 294920 | tf_op jit(solution)/shard_map/ppermute | solution.py:594
  58.9 15.2 %collective-permute-start.11 = (f32[32,768]{1,0:T(8,128)S(1)}, f32[32,768]{1,0:T(8,128)S(1)}, u32[]{:S(2)}, u32[]{:S(2)}) collective-permute-start(f32[32,768]{1,0:T(8,128)S(1)} %get-tuple-element.72), channel_id=1, source_target_pairs={{0,20},{4,16},{8,28},{12,24},{16,4},{20,0},{24,12},{28,8},{1,21},{... | collective-permute-start | bytes 294920 | tf_op jit(solution)/shard_map/ppermute | solution.py:594
  62.9 11.2 %collective-permute-start.12 = (f32[32,768]{1,0:T(8,128)S(1)}, f32[32,768]{1,0:T(8,128)S(1)}, u32[]{:S(2)}, u32[]{:S(2)}) collective-permute-start(f32[32,768]{1,0:T(8,128)S(1)} %get-tuple-element.73), channel_id=1, source_target_pairs={{0,24},{4,28},{8,16},{12,20},{16,8},{20,12},{24,0},{28,4},{1,25},{... | collective-permute-start | bytes 294920 | tf_op jit(solution)/shard_map/ppermute | solution.py:594
  65.1 8.9 %collective-permute-start.13 = (f32[32,768]{1,0:T(8,128)S(1)}, f32[32,768]{1,0:T(8,128)S(1)}, u32[]{:S(2)}, u32[]{:S(2)}) collective-permute-start(f32[32,768]{1,0:T(8,128)S(1)} %get-tuple-element.74), channel_id=1, source_target_pairs={{0,28},{4,24},{8,20},{12,16},{16,12},{20,8},{24,4},{28,0},{1,29},{... | collective-permute-start | bytes 294920 | tf_op jit(solution)/shard_map/ppermute | solution.py:594
  85.2 8.9 %collective-permute-start.24 = (f32[32,768]{1,0:T(8,128)S(1)}, f32[32,768]{1,0:T(8,128)S(1)}, u32[]{:S(2)}, u32[]{:S(2)}) collective-permute-start(f32[32,768]{1,0:T(8,128)S(1)} %get-tuple-element.88), channel_id=1, source_target_pairs={{0,4},{4,0},{8,12},{12,8},{16,20},{20,16},{24,28},{28,24},{1,5},{5... | collective-permute-start | bytes 294920 | tf_op jit(solution)/shard_map/ppermute | solution.py:594
  85.8 10.1 %collective-permute-start.25 = (f32[32,768]{1,0:T(8,128)S(1)}, f32[32,768]{1,0:T(8,128)S(1)}, u32[]{:S(2)}, u32[]{:S(2)}) collective-permute-start(f32[32,768]{1,0:T(8,128)S(1)} %get-tuple-element.89), channel_id=1, source_target_pairs={{0,8},{4,12},{8,0},{12,4},{16,24},{20,28},{24,16},{28,20},{1,9},{5... | collective-permute-start | bytes 294920 | tf_op jit(solution)/shard_map/ppermute | solution.py:594
  90.3 8.2 %collective-permute-start.26 = (f32[32,768]{1,0:T(8,128)S(1)}, f32[32,768]{1,0:T(8,128)S(1)}, u32[]{:S(2)}, u32[]{:S(2)}) collective-permute-start(f32[32,768]{1,0:T(8,128)S(1)} %get-tuple-element.90), channel_id=1, source_target_pairs={{0,12},{4,8},{8,4},{12,0},{16,28},{20,24},{24,20},{28,16},{1,13},{... | collective-permute-start | bytes 294920 | tf_op jit(solution)/shard_map/ppermute | solution.py:594
  90.8 13.2 %collective-permute-start.27 = (f32[32,768]{1,0:T(8,128)S(1)}, f32[32,768]{1,0:T(8,128)S(1)}, u32[]{:S(2)}, u32[]{:S(2)}) collective-permute-start(f32[32,768]{1,0:T(8,128)S(1)} %get-tuple-element.91), channel_id=1, source_target_pairs={{0,16},{4,20},{8,24},{12,28},{16,0},{20,4},{24,8},{28,12},{1,17},{... | collective-permute-start | bytes 294920 | tf_op jit(solution)/shard_map/ppermute | solution.py:594
  92.7 15.0 %collective-permute-start.28 = (f32[32,768]{1,0:T(8,128)S(1)}, f32[32,768]{1,0:T(8,128)S(1)}, u32[]{:S(2)}, u32[]{:S(2)}) collective-permute-start(f32[32,768]{1,0:T(8,128)S(1)} %get-tuple-element.92), channel_id=1, source_target_pairs={{0,20},{4,16},{8,28},{12,24},{16,4},{20,0},{24,12},{28,8},{1,21},{... | collective-permute-start | bytes 294920 | tf_op jit(solution)/shard_map/ppermute | solution.py:594
  94.1 13.6 %collective-permute-start.29 = (f32[32,768]{1,0:T(8,128)S(1)}, f32[32,768]{1,0:T(8,128)S(1)}, u32[]{:S(2)}, u32[]{:S(2)}) collective-permute-start(f32[32,768]{1,0:T(8,128)S(1)} %get-tuple-element.93), channel_id=1, source_target_pairs={{0,24},{4,28},{8,16},{12,20},{16,8},{20,12},{24,0},{28,4},{1,25},{... | collective-permute-start | bytes 294920 | tf_op jit(solution)/shard_map/ppermute | solution.py:594
  95.9 14.3 %collective-permute-start.30 = (f32[32,768]{1,0:T(8,128)S(1)}, f32[32,768]{1,0:T(8,128)S(1)}, u32[]{:S(2)}, u32[]{:S(2)}) collective-permute-start(f32[32,768]{1,0:T(8,128)S(1)} %get-tuple-element.94), channel_id=1, source_target_pairs={{0,28},{4,24},{8,20},{12,16},{16,12},{20,8},{24,4},{28,0},{1,29},{... | collective-permute-start | bytes 294920 | tf_op jit(solution)/shard_map/ppermute | solution.py:594
  98.5 15.1 %collective-permute-start.40 = (f32[32,768]{1,0:T(8,128)S(1)}, f32[32,768]{1,0:T(8,128)S(1)}, u32[]{:S(2)}, u32[]{:S(2)}) collective-permute-start(f32[32,768]{1,0:T(8,128)S(1)} %get-tuple-element.109), channel_id=1, source_target_pairs={{0,4},{4,0},{8,12},{12,8},{16,20},{20,16},{24,28},{28,24},{1,5},{5... | collective-permute-start | bytes 294920 | tf_op jit(solution)/shard_map/ppermute | solution.py:594
  104.0 11.5 %collective-permute-start.41 = (f32[32,768]{1,0:T(8,128)S(1)}, f32[32,768]{1,0:T(8,128)S(1)}, u32[]{:S(2)}, u32[]{:S(2)}) collective-permute-start(f32[32,768]{1,0:T(8,128)S(1)} %get-tuple-element.110), channel_id=1, source_target_pairs={{0,8},{4,12},{8,0},{12,4},{16,24},{20,28},{24,16},{28,20},{1,9},{5... | collective-permute-start | bytes 294920 | tf_op jit(solution)/shard_map/ppermute | solution.py:594
  107.7 12.3 %collective-permute-start.42 = (f32[32,768]{1,0:T(8,128)S(1)}, f32[32,768]{1,0:T(8,128)S(1)}, u32[]{:S(2)}, u32[]{:S(2)}) collective-permute-start(f32[32,768]{1,0:T(8,128)S(1)} %get-tuple-element.111), channel_id=1, source_target_pairs={{0,12},{4,8},{8,4},{12,0},{16,28},{20,24},{24,20},{28,16},{1,13},{... | collective-permute-start | bytes 294920 | tf_op jit(solution)/shard_map/ppermute | solution.py:594
  107.7 13.0 %collective-permute-start.43 = (f32[32,768]{1,0:T(8,128)S(1)}, f32[32,768]{1,0:T(8,128)S(1)}, u32[]{:S(2)}, u32[]{:S(2)}) collective-permute-start(f32[32,768]{1,0:T(8,128)S(1)} %get-tuple-element.112), channel_id=1, source_target_pairs={{0,16},{4,20},{8,24},{12,28},{16,0},{20,4},{24,8},{28,12},{1,17},{... | collective-permute-start | bytes 294920 | tf_op jit(solution)/shard_map/ppermute | solution.py:594
  110.2 14.4 %collective-permute-start.44 = (f32[32,768]{1,0:T(8,128)S(1)}, f32[32,768]{1,0:T(8,128)S(1)}, u32[]{:S(2)}, u32[]{:S(2)}) collective-permute-start(f32[32,768]{1,0:T(8,128)S(1)} %get-tuple-element.113), channel_id=1, source_target_pairs={{0,20},{4,16},{8,28},{12,24},{16,4},{20,0},{24,12},{28,8},{1,21},{... | collective-permute-start | bytes 294920 | tf_op jit(solution)/shard_map/ppermute | solution.py:594
  113.6 11.0 %collective-permute-start.45 = (f32[32,768]{1,0:T(8,128)S(1)}, f32[32,768]{1,0:T(8,128)S(1)}, u32[]{:S(2)}, u32[]{:S(2)}) collective-permute-start(f32[32,768]{1,0:T(8,128)S(1)} %get-tuple-element.114), channel_id=1, source_target_pairs={{0,24},{4,28},{8,16},{12,20},{16,8},{20,12},{24,0},{28,4},{1,25},{... | collective-permute-start | bytes 294920 | tf_op jit(solution)/shard_map/ppermute | solution.py:594
  115.5 10.6 %collective-permute-start.46 = (f32[32,768]{1,0:T(8,128)S(1)}, f32[32,768]{1,0:T(8,128)S(1)}, u32[]{:S(2)}, u32[]{:S(2)}) collective-permute-start(f32[32,768]{1,0:T(8,128)S(1)} %get-tuple-element.115), channel_id=1, source_target_pairs={{0,28},{4,24},{8,20},{12,16},{16,12},{20,8},{24,4},{28,0},{1,29},{... | collective-permute-start | bytes 294920 | tf_op jit(solution)/shard_map/ppermute | solution.py:594
  120.0 14.6 %collective-permute-start.31 = (f32[72,768]{1,0:T(8,128)S(1)}, f32[72,768]{1,0:T(8,128)S(1)}, u32[]{:S(2)}, u32[]{:S(2)}) collective-permute-start(f32[72,768]{1,0:T(8,128)S(1)} %get-tuple-element.96), channel_id=1, source_target_pairs={{0,1},{1,0},{2,3},{3,2},{4,5},{5,4},{6,7},{7,6},{8,9},{9,8},{10,11... | collective-permute-start | bytes 663560 | tf_op jit(solution)/shard_map/ppermute | solution.py:594
  120.7 13.9 %collective-permute-start.32 = (f32[72,768]{1,0:T(8,128)S(1)}, f32[72,768]{1,0:T(8,128)S(1)}, u32[]{:S(2)}, u32[]{:S(2)}) collective-permute-start(f32[72,768]{1,0:T(8,128)S(1)} %get-tuple-element.97), channel_id=1, source_target_pairs={{0,2},{1,3},{2,0},{3,1},{4,6},{5,7},{6,4},{7,5},{8,10},{9,11},{10,... | collective-permute-start | bytes 663560 | tf_op jit(solution)/shard_map/ppermute | solution.py:594
  124.6 10.9 %collective-permute-start.33 = (f32[72,768]{1,0:T(8,128)S(1)}, f32[72,768]{1,0:T(8,128)S(1)}, u32[]{:S(2)}, u32[]{:S(2)}) collective-permute-start(f32[72,768]{1,0:T(8,128)S(1)} %get-tuple-element.98), channel_id=1, source_target_pairs={{0,3},{1,2},{2,1},{3,0},{4,7},{5,6},{6,5},{7,4},{8,11},{9,10},{10,... | collective-permute-start | bytes 663560 | tf_op jit(solution)/shard_map/ppermute | solution.py:594
  124.6 8.3 %collective-permute-start.38 = (f32[24,256]{1,0:T(8,128)S(1)}, f32[24,256]{1,0:T(8,128)S(1)}, u32[]{:S(2)}, u32[]{:S(2)}) collective-permute-start(f32[24,256]{1,0:T(8,128)S(1)} %get-tuple-element.106), channel_id=1, source_target_pairs={{0,1},{1,2},{2,3},{3,0},{4,5},{5,6},{6,7},{7,4},{8,9},{9,10},{10,1... | collective-permute-start | bytes 73736 | tf_op jit(solution)/shard_map/ppermute | solution.py:648
  126.2 6.8 %collective-permute-start.39 = (f32[24,256]{1,0:T(8,128)S(1)}, f32[24,256]{1,0:T(8,128)S(1)}, u32[]{:S(2)}, u32[]{:S(2)}) collective-permute-start(f32[24,256]{1,0:T(8,128)S(1)} %get-tuple-element.107), channel_id=1, source_target_pairs={{0,3},{1,0},{2,1},{3,2},{4,7},{5,4},{6,5},{7,6},{8,11},{9,8},{10,9... | collective-permute-start | bytes 73736 | tf_op jit(solution)/shard_map/ppermute | solution.py:649
  132.9 6.1 %collective-permute-start.37 = (f32[24,256]{1,0:T(8,128)S(1)}, f32[24,256]{1,0:T(8,128)S(1)}, u32[]{:S(2)}, u32[]{:S(2)}) collective-permute-start(f32[24,256]{1,0:T(8,128)S(1)} %get-tuple-element.105), channel_id=1, source_target_pairs={{0,3},{1,0},{2,1},{3,2},{4,7},{5,4},{6,5},{7,6},{8,11},{9,8},{10,9... | collective-permute-start | bytes 73736 | tf_op jit(solution)/shard_map/ppermute | solution.py:649
  134.7 8.4 %collective-permute-start.47 = (f32[72,768]{1,0:T(8,128)S(1)}, f32[72,768]{1,0:T(8,128)S(1)}, u32[]{:S(2)}, u32[]{:S(2)}) collective-permute-start(f32[72,768]{1,0:T(8,128)S(1)} %get-tuple-element.117), channel_id=1, source_target_pairs={{0,1},{1,0},{2,3},{3,2},{4,5},{5,4},{6,7},{7,6},{8,9},{9,8},{10,11... | collective-permute-start | bytes 663560 | tf_op jit(solution)/shard_map/ppermute | solution.py:594
  134.7 8.3 %collective-permute-start.48 = (f32[72,768]{1,0:T(8,128)S(1)}, f32[72,768]{1,0:T(8,128)S(1)}, u32[]{:S(2)}, u32[]{:S(2)}) collective-permute-start(f32[72,768]{1,0:T(8,128)S(1)} %get-tuple-element.118), channel_id=1, source_target_pairs={{0,2},{1,3},{2,0},{3,1},{4,6},{5,7},{6,4},{7,5},{8,10},{9,11},{10,... | collective-permute-start | bytes 663560 | tf_op jit(solution)/shard_map/ppermute | solution.py:594
  135.5 11.2 %collective-permute-start.49 = (f32[72,768]{1,0:T(8,128)S(1)}, f32[72,768]{1,0:T(8,128)S(1)}, u32[]{:S(2)}, u32[]{:S(2)}) collective-permute-start(f32[72,768]{1,0:T(8,128)S(1)} %get-tuple-element.119), channel_id=1, source_target_pairs={{0,3},{1,2},{2,1},{3,0},{4,7},{5,6},{6,5},{7,4},{8,11},{9,10},{10,... | collective-permute-start | bytes 663560 | tf_op jit(solution)/shard_map/ppermute | solution.py:594
  138.2 10.0 %collective-permute-start.34 = (f32[3,64,256]{2,1,0:T(8,128)S(1)}, f32[3,64,256]{2,1,0:T(8,128)S(1)}, u32[]{:S(2)}, u32[]{:S(2)}) collective-permute-start(f32[3,64,256]{2,1,0:T(8,128)S(1)} %get-tuple-element.100), channel_id=1, source_target_pairs={{0,4},{4,8},{8,12},{12,16},{16,20},{20,24},{24,28},{28,0},{1,5},{5... | collective-permute-start | bytes 589832 | tf_op jit(solution)/shard_map/ppermute | solution.py:693
  139.1 11.1 %collective-permute-start.35 = (f32[3,64,256]{2,1,0:T(8,128)S(1)}, f32[3,64,256]{2,1,0:T(8,128)S(1)}, u32[]{:S(2)}, u32[]{:S(2)}) collective-permute-start(f32[3,64,256]{2,1,0:T(8,128)S(1)} %get-tuple-element.101), channel_id=1, source_target_pairs={{0,28},{4,0},{8,4},{12,8},{16,12},{20,16},{24,20},{28,24},{1,29},{... | collective-permute-start | bytes 589832 | tf_op jit(solution)/shard_map/ppermute | solution.py:692
  (15 other events, 178.9 us)

commit v3 on v2

v3 whole, which is shorter than its diff:
```python
import functools
import math

import jax
import jax.numpy as jnp
import ml_dtypes
import numpy as np
from jax import lax
from jax.experimental import pallas as pl
from jax.experimental.pallas import tpu as pltpu
from jax.sharding import PartitionSpec as P

MIG = 64
LANES = 128
RIM = 8
TIME_STEP = 0.25
VMEM = 24 * 1024 * 1024
F32 = jnp.float32
BF16 = jnp.bfloat16


def split_table(table):
    high = table.astype(np.float32).astype(ml_dtypes.bfloat16)
    low = (table - high.astype(np.float64)).astype(np.float32).astype(ml_dtypes.bfloat16)
    return high, low


def angles(rows, columns, extent):
    return 2.0 * np.pi * (np.multiply.outer(rows, columns) % extent) / extent


def y_tables(ny, pencils, scale):
    modes = ny // (2 * pencils)
    position = np.arange(ny)
    angle = angles(position, np.arange(ny // 2), ny)
    real, imag = np.cos(angle), -np.sin(angle)
    imag[:, 0] = 1.0 - 2.0 * (position % 2)
    weight = np.where(np.arange(ny // 2) == 0, 1.0, 2.0) * scale
    ahead = np.zeros((2, ny, pencils, 2, 2, modes))
    back = np.zeros((pencils, 2, 2, modes, 2, ny))
    for parity in range(2):
        for part, values in enumerate((real, imag)):
            ahead[parity, :, :, part, parity] = values.reshape(ny, pencils, modes)
            back[:, part, parity, :, parity] = (values * weight).T.reshape(pencils, modes, ny)
    return ahead.reshape(2 * ny, -1), back.reshape(-1, 2 * ny)


def wave_order(nx, slabs):
    half = nx // 2
    ahead = np.arange(half).reshape(slabs, 1, half // slabs)
    behind = np.where(ahead == 0, half, (nx - ahead) % nx)
    return np.concatenate([ahead, behind], axis=1).reshape(-1)


def x_tables(nx, cols, pencils, slabs):
    order = wave_order(nx, slabs)
    angle = angles(order, np.arange(nx), nx)
    ahead = np.concatenate([np.cos(angle), np.sin(angle)], axis=0)
    row = np.arange(cols + RIM)
    offset = np.where(row <= cols, row, -1)
    used = ((row <= cols) | (row == cols + RIM - 1)).astype(np.float64)
    place = (np.arange(pencils)[:, None] * cols + offset[None, :]) % nx
    angle = angles(place.reshape(-1), order, nx)
    mask = np.tile(used, pencils)[:, None]
    back = np.concatenate([np.cos(angle) * mask, np.sin(angle) * mask], axis=0)
    return ahead, back


def split(values):
    high = values.astype(BF16)
    return high, (values - high.astype(F32)).astype(BF16)


def dot(left, right):
    return jnp.dot(left, right, preferred_element_type=F32)


def table_left(high, low, values):
    v_high, v_low = split(values)
    return dot(high, v_high) + (dot(high, v_low) + dot(low, v_high))


def table_right(values, high, low):
    v_high, v_low = split(values)
    return dot(v_high, high) + (dot(v_low, high) + dot(v_high, low))


def lane_of():
    return lax.broadcasted_iota(jnp.int32, (1, LANES), 1)


def times_i(values):
    half = LANES // 2
    sign = jnp.where(lane_of() < half, -1.0, 1.0).astype(F32)
    return pltpu.roll(values, half, 1) * sign


def kernel_weight(distance):
    radius = jnp.abs(distance)
    near = 1.0 - 2.5 * radius * radius + 1.5 * radius * radius * radius
    far = 0.5 * (2.0 - radius) * (2.0 - radius) * (1.0 - radius)
    return jnp.where(radius < 1.0, near, jnp.where(radius < 2.0, far, 0.0))


def turned(value, wave, extent, sign):
    wave = wave % extent
    real, imag = value
    if wave == 0:
        return value
    if 2 * wave == extent:
        return -real, -imag
    if 4 * wave == extent:
        return (-imag, real) if sign > 0 else (imag, -real)
    if 4 * wave == 3 * extent:
        return (imag, -real) if sign > 0 else (-imag, real)
    a = math.cos(2.0 * math.pi * wave / extent)
    b = sign * math.sin(2.0 * math.pi * wave / extent)
    return real * a - imag * b, real * b + imag * a


def fft(values, sign):
    count = len(values)
    if count == 1:
        return values
    even, odd = fft(values[::2], sign), fft(values[1::2], sign)
    odd = [turned(v, k, count, sign) for k, v in enumerate(odd)]
    plus = [(a[0] + b[0], a[1] + b[1]) for a, b in zip(even, odd)]
    minus = [(a[0] - b[0], a[1] - b[1]) for a, b in zip(even, odd)]
    return plus + minus


def offset_order(count):
    if count < 4:
        return list(range(count))
    far, near = list(range(count // 2, count)), list(range(1, count // 2))
    order = [0, far.pop(0)]
    while far or near:
        order += far[:1] + near[:1]
        far, near = far[1:], near[1:]
    return order


def blocks_of(refs, at):
    if len(refs) == 1:
        return [(d, refs[0].at[d]) for d in range(refs[0].shape[0])]
    return [(at ^ k, ref) for k, ref in zip(offset_order(len(refs)), refs)]


def gather_blocks(refs, held, at):
    for d, ref in blocks_of(refs, at):
        held[d] = ref[...]


def packet_kernel(
    counts, strength, offsets, cells, packet, movers, near_counts, near_cells, sems
):
    copies = [
        pltpu.make_async_copy(counts, near_counts, sems.at[0]),
        pltpu.make_async_copy(cells, near_cells, sems.at[1]),
        pltpu.make_async_copy(strength, packet.at[pl.ds(0, 3)], sems.at[2]),
        pltpu.make_async_copy(offsets, packet.at[pl.ds(3, 3)], sems.at[3]),
    ]
    for copy in copies:
        copy.start()
    for copy in copies:
        copy.wait()
    slot = lax.broadcasted_iota(jnp.int32, (1, packet.shape[1]), 1)
    up = near_counts[0:1, 0:1]
    both = up + near_counts[0:1, 1:2]
    packet[6:7] = near_cells[...].astype(F32)
    packet[7:8] = jnp.where(slot < up, 1.0, jnp.where(slot < both, -1.0, 0.0))
    movers[...] = packet[:, : movers.shape[1]]


def deposit_kernel(
    pairs, rims_before, place, own, up1, down1, up2, down2, ambient, t_high, t_low, *refs
):
    rims, refs = refs[:rims_before], refs[rims_before:]
    mesh, rim_high, rim_low = refs[:3]
    total, made = refs[-2:]
    outs = refs[3:-2]
    _, planes, cols, ny = ambient.shape
    rows = cols + RIM
    movers = up2.shape[1]
    count = own.shape[1]
    listed = [2 * pair + parity for pair in pairs for parity in range(2)]

    def decode(ref, start, stop, shift):
        packet = ref[:, start:stop]
        cell = packet[6:7].astype(jnp.int32)
        move = packet[7:8].astype(jnp.int32)
        z_cell = lax.div(cell, cols * ny) + planes * (move + shift)
        x_cell = lax.rem(lax.div(cell, ny), cols)
        return packet[0:6], z_cell, x_cell, lax.rem(cell, ny)

    def joined(pieces):
        return [jnp.concatenate(p, axis=1) if len(p) > 1 else p[0] for p in zip(*pieces)]

    def add_block(pieces, wanted):
        values, z_cell, x_cell, y_cell = joined(pieces)
        width = values.shape[1]
        z_at = lax.broadcasted_iota(jnp.int32, (planes, width), 0)
        w_z = kernel_weight((z_at - z_cell).astype(F32) - values[3:4])
        row = lax.broadcasted_iota(jnp.int32, (rows, width), 0)
        x_at = jnp.where(row < cols + 2, row, jnp.where(row >= rows - 2, row - rows, 4 * rows))
        w_x = kernel_weight((x_at - x_cell).astype(F32) - values[4:5])
        y_at = lax.broadcasted_iota(jnp.int32, (ny, width), 0)
        y_off = lax.rem(y_at - y_cell + (ny + ny // 2), ny) - ny // 2
        w_y = kernel_weight(y_off.astype(F32) - values[5:6])
        y_high, y_low = split(w_y)
        right = jnp.concatenate([y_high, y_high, y_low], axis=1)
        at = [listed.index(z) for z in wanted]
        for c in range(3):
            s_z = values[c : c + 1] * w_z
            left = jnp.concatenate([s_z[z : z + 1] * w_x for z in wanted], axis=0)
            l_high, l_low = split(left)
            left = jnp.concatenate([l_high, l_low, l_high], axis=1)
            added = lax.dot_general(
                left, right, (((1,), (1,)), ((), ())), preferred_element_type=F32
            )
            total[c, at[0] : at[-1] + 1] += added.reshape(len(wanted), rows, ny)

    for n, z in enumerate(listed):
        total[:, n, 0:cols] = ambient[:, z]
    total[:, :, cols:rows] = jnp.zeros((3, len(listed), RIM, ny), F32)
    step = 256
    for at in range(0, count, step):
        add_block([decode(own, at, min(at + step, count), 0)], listed)
    add_block([decode(up1, 0, movers, 1), decode(down1, 0, movers, -1)], listed)
    sides = ((up1, up2, 1, (planes - 2, planes - 1)), (down1, down2, -1, (0, 1)))
    for near, far, shift, wanted in sides:
        if not set(wanted) <= set(listed):
            continue
        whole = [decode(near, movers, count, shift), decode(far, 0, movers, 2 * shift)]
        values, z_cell, x_cell, y_cell = joined(whole)
        for at in range(0, count, step):
            to = min(at + step, count)
            block = (values[:, at:to], z_cell[:, at:to], x_cell[:, at:to], y_cell[:, at:to])
            add_block([block], wanted)

    mesh[...] = total[:, :, 0:cols]
    at = 0
    if rims:
        at = rims[0].shape[0]
        rim_high[0:at] = rims[0][...]
        rim_low[0:at] = rims[1][...]
    for n in range(3 * len(listed)):
        c, i = n // len(listed), n % len(listed)
        rim_high[at + 2 * n : at + 2 * n + 2] = total[c, i, cols : cols + 2]
        rim_low[at + 2 * n : at + 2 * n + 2] = total[c, i, rows - 2 : rows]
    groups = [(c, 2 * n) for c in range(3) for n in range(len(pairs))]
    left = jnp.concatenate(
        [jnp.concatenate([total[c, n], total[c, n + 1]], axis=1) for c, n in groups], axis=0
    )
    wide = table_right(left, t_high[...], t_low[...])
    for n in range(len(groups)):
        for g in range(made.shape[0]):
            made[g, :, n * LANES : (n + 1) * LANES] = wide[
                n * rows : (n + 1) * rows, g * LANES : (g + 1) * LANES
            ]
    for d, out in blocks_of(outs, place[1]):
        out[...] = made[d]


def x_ahead_kernel(sends, place, t_high, t_low, *refs):
    held, made = refs[-2:]
    outs, parts = refs[-2 - sends : -2], refs[: -2 - sends]
    gather_blocks(parts, held, place[1])
    pencils, rows, width = held.shape
    cols = rows - RIM
    row = lax.broadcasted_iota(jnp.int32, (RIM, width), 0)
    pieces = []
    for h in range(pencils):
        from_low = held[(h - 1) % pencils, cols:rows]
        from_high = held[(h + 1) % pencils, cols:rows]
        pieces.append(held[h, 0:RIM] + jnp.where(row < 2, from_low, 0.0))
        pieces.append(held[h, RIM : cols - RIM])
        pieces.append(held[h, cols - RIM : cols] + jnp.where(row >= RIM - 2, from_high, 0.0))
    both = table_left(t_high[...], t_low[...], jnp.concatenate(pieces, axis=0))
    half = both.shape[0] // 2
    for n in range(width // LANES):
        lanes = slice(n * LANES, (n + 1) * LANES)
        value = both[:half, lanes] - times_i(both[half:, lanes])
        made[:, :, lanes] = value.reshape(made.shape[0], made.shape[1], LANES)
    for d, out in blocks_of(outs, place[0]):
        out[...] = made[d]


def x_back_kernel(sends, place, t_high, t_low, *refs):
    held, made = refs[-2:]
    outs, parts = refs[-2 - sends : -2], refs[: -2 - sends]
    gather_blocks(parts, held, place[0])
    pencils, rows, width = made.shape
    both = table_left(t_high[...], t_low[...], held[...].reshape(-1, width))
    half = both.shape[0] // 2
    for n in range(width // LANES):
        lanes = slice(n * LANES, (n + 1) * LANES)
        value = both[:half, lanes] + times_i(both[half:, lanes])
        made[:, :, lanes] = value.reshape(pencils, rows, LANES)
    for d, out in blocks_of(outs, place[1]):
        out[...] = made[d]


def wave_lanes():
    lane = lane_of()
    return lane < LANES // 2, (lane // (LANES // 4)) % 2 == 0


def roll(values, shift):
    return pltpu.roll(values, shift, 1)


def cross_half(a, b):
    low, _ = wave_lanes()
    half = LANES // 2
    return jnp.where(low, a, roll(b, half)), jnp.where(low, roll(a, half), b)


def cross_quarter(a, b):
    _, first = wave_lanes()
    quarter = LANES // 4
    return (
        jnp.where(first, a, roll(b, quarter)),
        jnp.where(first, roll(a, LANES - quarter), b),
    )


def lanes_at(c, count, i):
    return pl.ds(pl.multiple_of((c * count + i) * LANES, LANES), LANES)


def enter_kernel(pairs, nz, place, *refs):
    parts, data = refs[:-1], refs[-1]
    _, _, _, slabs, tile, _ = data.shape

    def body(c, carry):
        for i, pair in enumerate(pairs):
            lanes = lanes_at(c, len(pairs), i)
            for s, ref in blocks_of(parts, place[0]):
                quad = [ref[q * tile : (q + 1) * tile, lanes] for q in range(4)]
                real0, imag0 = cross_half(quad[0], quad[2])
                real1, imag1 = cross_half(quad[1], quad[3])
                for part, (a, b) in enumerate(((real0, real1), (imag0, imag1))):
                    even, odd = cross_quarter(a, b)
                    data[c, part, 2 * i, s] = even
                    data[c, part, 2 * i + 1, s] = odd
            for parity in range(2):
                at = 2 * i + parity
                line = [(data[c, 0, at, s], data[c, 1, at, s]) for s in range(slabs)]
                for k, v in enumerate(fft(line, -1.0)):
                    v = turned(v, (2 * pair + parity) * k, nz, -1.0)
                    data[c, 0, at, k], data[c, 1, at, k] = v
        return carry

    lax.fori_loop(0, 3, body, 0)


def leave_kernel(pairs, nz, place, source, *refs):
    outs, data = refs[:-1], refs[-1]
    _, _, _, slabs, tile, _ = source.shape

    def body(c, carry):
        for i, pair in enumerate(pairs):
            lanes = lanes_at(c, len(pairs), i)
            for parity in range(2):
                at = 2 * i + parity
                line = [
                    turned(
                        (source[c, 0, at, k], source[c, 1, at, k]),
                        (2 * pair + parity) * k,
                        nz,
                        1.0,
                    )
                    for k in range(slabs)
                ]
                for s, v in enumerate(fft(line, 1.0)):
                    data[c, 0, at, s], data[c, 1, at, s] = v
            for s, ref in blocks_of(outs, place[0]):
                real0, real1 = cross_quarter(data[c, 0, 2 * i, s], data[c, 0, 2 * i + 1, s])
                imag0, imag1 = cross_quarter(data[c, 1, 2 * i, s], data[c, 1, 2 * i + 1, s])
                quad = [None] * 4
                quad[0], quad[2] = cross_half(real0, imag0)
                quad[1], quad[3] = cross_half(real1, imag1)
                for q in range(4):
                    ref[q * tile : (q + 1) * tile, lanes] = quad[q]
        return carry

    lax.fori_loop(0, 3, body, 0)


def curl_kernel(chunks, nx, ny, place, low_rim, high_rim, *refs):
    sources, outs = refs[: len(chunks)], refs[len(chunks) : 2 * len(chunks)]
    spectrum = refs[-1]
    _, _, nz, tile, _ = spectrum.shape
    slabs = sources[0].shape[3]
    planes = nz // slabs
    modes, half = LANES // 4, LANES // 2
    slab_at, pencil_at = place[0], place[1]
    spot = {}
    for n, chunk in enumerate(chunks):
        for i, pair in enumerate(chunk):
            spot[2 * pair], spot[2 * pair + 1] = (n, 2 * i), (n, 2 * i + 1)

    def across_planes(k, carry):
        for c in range(3):
            line = []
            for l in range(planes):
                n, i = spot[l]
                line.append((sources[n][c, 0, i, k], sources[n][c, 1, i, k]))
            for n, v in enumerate(fft(line, -1.0)):
                spectrum[c, 0, k + slabs * n], spectrum[c, 1, k + slabs * n] = v
        return carry

    reach = 2 * tile
    row = lax.broadcasted_iota(jnp.int32, (tile, LANES), 0)
    lane = lax.broadcasted_iota(jnp.int32, (tile, LANES), 1)
    number = slab_at * reach + (lane // modes) % 2 * tile + row
    ahead = lane < half
    mode = lane % modes + pencil_at * modes
    alone = number == 0
    number = number.astype(F32) * (2.0 * math.pi / nx)
    x_base = jnp.where(ahead, number, jnp.where(alone, math.pi, -number))
    x_trim = jnp.where(ahead, number, jnp.where(alone, 0.0, -number))
    wave_y = mode.astype(F32) * (2.0 * math.pi / ny)
    packed = mode == 0
    x_sq = x_base * x_base
    lateral = x_sq + wave_y * wave_y

    def curl_at(k, with_mirror):
        z_wave = jnp.where(k < nz // 2, k, k - nz).astype(F32) * (2.0 * math.pi / nz)
        z_trim = jnp.where(k == nz // 2, 0.0, z_wave)
        full = lateral + z_wave * z_wave
        empty = full == 0.0
        inverse = jnp.where(empty, 0.0, 1.0 / jnp.where(empty, 1.0, full))
        if with_mirror:
            other = 1.0 / (x_sq + (z_wave * z_wave + math.pi * math.pi))
            mirror = jnp.where(packed, 0.5 * (inverse - other), 0.0)
            inverse = jnp.where(packed, 0.5 * (inverse + other), inverse)
            opposite = lax.rem(nz - k, nz)
        stream = []
        for c in range(3):
            value = [spectrum[c, part, k] * inverse for part in range(2)]
            if with_mirror:
                for part, sign in enumerate((1.0, -1.0)):
                    there = spectrum[c, part, opposite]
                    there = jnp.where(alone, there, roll(there, half))
                    value[part] = value[part] + (mirror * sign) * there
            stream.append(value)
        made = []
        for part in range(2):
            s = [value[part] for value in stream]
            made.append(
                (
                    x_trim * s[2] - wave_y * s[1],
                    wave_y * s[0] - z_trim * s[2],
                    z_trim * s[1] - x_trim * s[0],
                )
            )
        return [(-made[1][c], made[0][c]) for c in range(3)]

    def curl_all(with_mirror):
        def body(k, carry):
            made = [curl_at(k + slabs * n, with_mirror) for n in range(planes)]
            for c in range(3):
                for l, v in enumerate(fft([m[c] for m in made], 1.0)):
                    n, i = spot[l]
                    outs[n][c, 0, i, k], outs[n][c, 1, i, k] = v
            return carry

        lax.fori_loop(0, slabs, body, 0)

    lax.fori_loop(0, slabs, across_planes, 0)

    @pl.when(pencil_at == 0)
    def _():
        curl_all(True)

    @pl.when(pencil_at != 0)
    def _():
        curl_all(False)


def planes_of(held, pairs, t_high, t_low):
    pencils, rows, _ = held.shape
    ny = t_high.shape[1] // 2
    groups = [(c, pair) for c in range(3) for pair in pairs]
    left = jnp.concatenate(
        [
            jnp.concatenate(
                [held[h, :, n * LANES : (n + 1) * LANES] for h in range(pencils)], axis=1
            )
            for n in range(len(groups))
        ],
        axis=0,
    )
    wide = table_right(left, t_high[...], t_low[...])
    made = {}
    for n, (c, pair) in enumerate(groups):
        for parity in range(2):
            made[c, 2 * pair + parity] = wide[
                n * rows : (n + 1) * rows, parity * ny : (parity + 1) * ny
            ]
    return made


def hold(tall, c, n, value):
    rows = value.shape[0]
    tall[c, n, RIM : RIM + rows] = value
    tall[c, n, 0:RIM] = value[rows - RIM : rows]


def edge_kernel(pairs, place, t_high, t_low, *refs):
    tall, first, last, held = refs[-4:]
    gather_blocks(refs[:-4], held, place[1])
    listed = [2 * pair + parity for pair in pairs for parity in range(2)]
    cols = first.shape[1]
    values = planes_of(held, pairs, t_high, t_low)
    for c in range(3):
        for n, z in enumerate(listed):
            hold(tall, c, n, values[c, z])
        first[c] = values[c, listed[0]][0:cols]
        last[c] = values[c, listed[-1]][0:cols]


def stretch_kernel(
    chunks, place, t_high, t_low, edges, before, after, low_rim, high_rim, *refs
):
    meshes, refs = refs[:2], refs[2:]
    velocity, vorticity, held, inner, omega, sems = refs[-6:]
    _, planes, cols, ny = velocity.shape
    spot = {}
    for n, chunk in enumerate(chunks):
        for i, pair in enumerate(chunk):
            spot[2 * pair], spot[2 * pair + 1] = (n, 2 * i), (n, 2 * i + 1)
    talls = (edges, inner)
    sent = []

    def send(source, target):
        sent.append(pltpu.make_async_copy(source, target, sems.at[len(sent)]))
        sent[-1].start()

    def send_velocity(z):
        n, i = spot[z]
        send(talls[n].at[:, i, pl.ds(RIM, cols)], velocity.at[:, z])

    def rows_of(c, z, start=RIM):
        n, i = spot[z]
        return talls[n][c, i, start : start + cols]

    for z in range(planes):
        if spot[z][0] == 0:
            send_velocity(z)
    gather_blocks(refs[:-6], held, place[1])
    for (c, z), value in planes_of(held, chunks[1], t_high, t_low).items():
        hold(inner, c, spot[z][1], value)
    for z in range(planes):
        if spot[z][0] == 1:
            send_velocity(z)
    rim_at = 0
    for which, mesh in enumerate(meshes):
        size = mesh.shape[1]
        for z in range(planes):
            n, i = spot[z]
            if n != which:
                continue
            for c in range(3):
                at = rim_at + 2 * (c * size + i)
                omega[c, z] = mesh[c, i]
                omega[c, z, 0:2] += low_rim[at : at + 2]
                omega[c, z, cols - 2 : cols] += high_rim[at : at + 2]
            omega_z = [omega[c, z] for c in range(3)]
            for c in range(3):
                value = rows_of(c, z)
                above = rows_of(c, z + 1) if z + 1 < planes else after[c]
                below = rows_of(c, z - 1) if z > 0 else before[c]
                along_z = (above - below) * 0.5
                along_x = (rows_of(c, z, RIM + 1) - rows_of(c, z, RIM - 1)) * 0.5
                along_y = (pltpu.roll(value, ny - 1, 1) - pltpu.roll(value, 1, 1)) * 0.5
                stretch = omega_z[0] * along_z + omega_z[1] * along_x + omega_z[2] * along_y
                omega[c, z] = omega_z[c] + TIME_STEP * stretch
            send(omega.at[:, z], vorticity.at[:, z])
        rim_at += 6 * size
    for copy in sent:
        copy.wait()


VM = pl.BlockSpec(memory_space=pltpu.VMEM)
SM = pl.BlockSpec(memory_space=pltpu.SMEM)
AN = pl.BlockSpec(memory_space=pl.ANY)


def call(kernel, ins, outs, scratch=(), sems=0, micros=2.0, vmem=VMEM):
    extra = [pltpu.SemaphoreType.DMA((sems,))] if sems else []
    return pl.pallas_call(
        kernel,
        out_shape=[jax.ShapeDtypeStruct(shape, F32) for _, shape in outs],
        in_specs=[spec for spec, _ in ins],
        out_specs=[spec for spec, _ in outs],
        scratch_shapes=[pltpu.VMEM(shape, kind) for shape, kind in scratch] + extra,
        compiler_params=pltpu.CompilerParams(vmem_limit_bytes=vmem),
        cost_estimate=pl.CostEstimate(
            flops=int(micros * 1.0e9), bytes_accessed=int(micros * 3.0e6), transcendentals=0
        ),
    )(*[value for _, value in ins])


def ring(axis, step):
    count = lax.axis_size(axis)
    return [(i, (i + step) % count) for i in range(count)]


def spread(axis):
    count = lax.axis_size(axis)
    return count <= 8 and count & (count - 1) == 0


def sent_shapes(axis, rows, width, whole=False):
    count = lax.axis_size(axis)
    return [(count, rows, width)] if whole or not spread(axis) else [(rows, width)] * count


def exchange(blocks, axis):
    if len(blocks) == 1:
        return [lax.all_to_all(blocks[0], axis, split_axis=0, concat_axis=0, tiled=True)]
    count = lax.axis_size(axis)
    order = offset_order(count)
    return [blocks[0]] + [
        lax.ppermute(block, axis, [(i, i ^ k) for i in range(count)])
        for k, block in zip(order[1:], blocks[1:])
    ]


def on_device(strength, offsets, cell_index, migrate_count, ambient):
    _, planes, cols, ny = ambient.shape
    slabs, pencils = lax.axis_size("gz"), lax.axis_size("gx")
    nx, nz, rows = cols * pencils, planes * slabs, cols + RIM
    count = strength.shape[1]
    pair_count = planes // 2
    chunks = ((0, pair_count - 1), tuple(range(1, pair_count - 1)))
    widths = [3 * len(c) * LANES for c in chunks]
    block = nx // slabs

    y_ahead, y_back = [split_table(t) for t in y_tables(ny, pencils, 1.0 / (float(nx) * ny * nz))]
    x_ahead, x_back = [split_table(t) for t in x_tables(nx, cols, pencils, slabs)]
    place = jnp.stack([lax.axis_index("gz"), lax.axis_index("gx")]).astype(jnp.int32)
    here = (SM, place)

    packet, movers = call(
        packet_kernel,
        [
            (AN, migrate_count.reshape(1, 2)),
            (AN, strength),
            (AN, offsets),
            (AN, cell_index.reshape(1, count)),
        ],
        [(VM, (8, count)), (VM, (8, 2 * MIG))],
        [((1, 2), jnp.int32), ((1, count), jnp.int32)],
        sems=4,
        micros=1.0,
        vmem=63 * 1024 * 1024,
    )
    up1 = lax.ppermute(packet, "gz", ring("gz", -1))
    down1 = lax.ppermute(packet, "gz", ring("gz", 1))
    up2 = lax.ppermute(movers, "gz", ring("gz", -2))
    down2 = lax.ppermute(movers, "gz", ring("gz", 2))

    meshes, rims, parts = [], [], []
    for chunk, width in zip(chunks, widths):
        size = 2 * len(chunk)
        rim = (6 * size + (rims[0].shape[0] if rims else 0), ny)
        mesh, rim_high, rim_low, *part = call(
            functools.partial(deposit_kernel, chunk, len(rims)),
            [here]
            + [(VM, value) for value in (packet, up1, down1, up2, down2)]
            + [(VM, ambient), (VM, y_ahead[0]), (VM, y_ahead[1])]
            + [(VM, value) for value in rims],
            [(VM, (3, size, cols, ny)), (VM, rim), (VM, rim)]
            + [(VM, shape) for shape in sent_shapes("gx", rows, width)],
            [((3, size, rows, ny), F32), ((pencils, rows, width), F32)],
            micros=5.0,
        )
        meshes.append(mesh)
        rims = [rim_high, rim_low]
        parts.append(exchange(part, "gx"))
    low_rim = lax.ppermute(rims[0], "gx", ring("gx", 1))
    high_rim = lax.ppermute(rims[1], "gx", ring("gx", -1))

    tile = max(1, block // 4)
    data = []
    for chunk, part, width in zip(chunks, parts, widths):
        shapes = sent_shapes("gz", block, width)
        part = call(
            functools.partial(x_ahead_kernel, len(shapes)),
            [here, (VM, x_ahead[0]), (VM, x_ahead[1])] + [(VM, p) for p in part],
            [(VM, shape) for shape in shapes],
            [((pencils, rows, width), F32), ((slabs, block, width), F32)],
        )
        (entered,) = call(
            functools.partial(enter_kernel, chunk, nz),
            [here] + [(VM, p) for p in exchange(part, "gz")],
            [(VM, (3, 2, 2 * len(chunk), slabs, tile, LANES))],
        )
        data.append(entered)
    data = call(
        functools.partial(curl_kernel, chunks, nx, ny),
        [here, (VM, low_rim), (VM, high_rim)] + [(VM, d) for d in data],
        [(VM, d.shape) for d in data],
        [((3, 2, nz, tile, LANES), F32)],
        micros=5.0,
    )
    parts = []
    for chunk, source, width in zip(chunks, data, widths):
        part = call(
            functools.partial(leave_kernel, chunk, nz),
            [here, (VM, source)],
            [(VM, shape) for shape in sent_shapes("gz", block, width)],
            [(source.shape, F32)],
        )
        part = exchange(part, "gz")
        shapes = sent_shapes("gx", rows, width, whole=not parts)
        part = call(
            functools.partial(x_back_kernel, len(shapes)),
            [here, (VM, x_back[0]), (VM, x_back[1])] + [(VM, p) for p in part],
            [(VM, shape) for shape in shapes],
            [((slabs, block, width), F32), ((pencils, rows, width), F32)],
        )
        parts.append(exchange(part, "gx"))
    plane = (3, cols, ny)
    tables = [(VM, y_back[0]), (VM, y_back[1])]
    tall = [(3, 2 * len(chunk), cols + 2 * RIM, ny) for chunk in chunks]
    edges, first, last = call(
        functools.partial(edge_kernel, chunks[0]),
        [here] + tables + [(VM, p) for p in parts[0]],
        [(VM, tall[0]), (VM, plane), (VM, plane)],
        [((pencils, rows, widths[0]), F32)],
    )
    after = lax.ppermute(first, "gz", ring("gz", -1))
    before = lax.ppermute(last, "gz", ring("gz", 1))
    return tuple(
        call(
            functools.partial(stretch_kernel, chunks),
            [here]
            + tables
            + [(VM, v) for v in (edges, before, after, low_rim, high_rim, *meshes)]
            + [(VM, p) for p in parts[1]],
            [(AN, ambient.shape), (AN, ambient.shape)],
            [
                ((pencils, rows, widths[1]), F32),
                (tall[1], F32),
                ((3, planes, cols, ny), F32),
            ],
            sems=2 * planes,
            micros=4.0,
        )
    )


def solution(mesh):
    placed = (
        P(None, ("gz", "gx")),
        P(None, ("gz", "gx")),
        P(("gz", "gx")),
        P("gz", "gx", None),
        P(None, "gz", "gx", None),
    )
    return jax.shard_map(
        on_device,
        mesh=mesh,
        in_specs=placed,
        out_specs=(P(None, "gz", "gx", None), P(None, "gz", "gx", None)),
        check_vma=False,
    )
```

time: 155 us -> 154 us (level)
  waiting for transfers between devices: 37.8 us -> 53.7 us
  starting transfers between devices: 76.3 us -> 61.4 us
  Pallas kernels: 37 us -> 31.9 us
  local copies, waits for them, and re-layouts: 2.76 us -> 5.71 us
    ppermute x44 -> x39, starting transfers between devices: 61.6 us -> 43.1 us  [the longest x37 41.3 us: exchange(): lax.ppermute(block, axis, [(i, i ^ k) for i in range(count)])]
    ppermute x44 -> x39, waiting for transfers between devices: 32.8 us -> 46.7 us  [the longest x37 46.7 us: exchange(): lax.ppermute(block, axis, [(i, i ^ k) for i in range(count)])]
    pallas_call x10 -> x14, Pallas kernels: 37 us -> 31.9 us  [call(): pl.pallas_call(kernel, out_shape=[jax.ShapeDtypeStruct(shape, F32) for _,...]
    all_to_all x0 -> x1, starting transfers between devices: none -> 3.63 us  [exchange(): lax.all_to_all(blocks[0], axis, split_axis=0, concat_axis=0, tiled=True)]
    unnamed x26 -> x38, local copies, waits for them, and re-layouts: 2.76 us -> 5.71 us
    ppermute x1, waiting for transfers between devices: 1.46 us -> 3.22 us  [on_device(): before = lax.ppermute(last, 'gz', ring('gz', 1))]
  transfers between devices with their start and end apart: 50 -> 46, of which waited for: 14 -> 21; matrix products, arithmetic and copies ran while one was open for 0% -> 0% of each run, Pallas kernels for 10% -> 9%
where the time goes in v3:
time: 154 us
  starting transfers between devices  61.4 us (40%)
  waiting for transfers between devices  53.7 us (35%)
  Pallas kernels  31.9 us (21%)
  local copies, waits for them, and re-layouts  5.71 us (4%)
    ppermute x37, waiting for transfers between devices, exchange(): lax.ppermute(block, axis, [(i, i ^ k) for i in range(count)])  46.7 us
    ppermute x37, starting transfers between devices, exchange(): lax.ppermute(block, axis, [(i, i ^ k) for i in range(count)])  41.3 us
    pallas_call x14, Pallas kernels, call(): pl.pallas_call(kernel, out_shape=[jax.ShapeDtypeStruct(shape, F32) for _,...  31.9 us
    unnamed x38, local copies, waits for them, and re-layouts  5.71 us
    ppermute x1, starting transfers between devices, on_device(): after = lax.ppermute(first, 'gz', ring('gz', -1))  3.87 us
    all_to_all x1, starting transfers between devices, exchange(): lax.all_to_all(blocks[0], axis, split_axis=0, concat_axis=0, tiled=True)  3.63 us
    ppermute x1, waiting for transfers between devices, on_device(): before = lax.ppermute(last, 'gz', ring('gz', 1))  3.22 us
  transfers between devices with their start and end apart: 46, of which 21 were waited for; matrix products, arithmetic and copies ran while one was open for 0% of the time, Pallas kernels for 9%

profile of v3, /device:TPU:0, one launch (start us, length us, event | category | flops | bytes accessed | tf_op | source)
XLA Modules:
  0.0 153.9 jit_solution(8013641304897863031)
XLA Ops:
  0.6 1.6 %shard_map.140 = (f32[8,512]{1,0:T(8,128)}, f32[8,128]{1,0:T(8,128)}) custom-call(s32[1,2]{1,0:T(1,128)} %bitcast.5, f32[3,512]{1,0:T(4,128)} %strength.1, f32[3,512]{1,0:T(4,128)} %offsets.1, s32[1,512]{1,0:T(1,128)} %bitcast.4), custom_call_target="tpu_custom_call" | custom-call | flops 1000000000 | bytes 3000000 | tf_op jit(solution)/shard_map/pallas_call | solution.py:594
  2.2 3.1 %collective-permute-start.3 = (f32[8,128]{1,0:T(8,128)}, f32[8,128]{1,0:T(8,128)S(1)}, u32[]{:S(2)}, u32[]{:S(2)}) collective-permute-start(f32[8,128]{1,0:T(8,128)} %get-tuple-element.60), channel_id=1, source_target_pairs={{0,8},{4,12},{8,16},{12,20},{16,24},{20,28},{24,0},{28,4},{1,9},{5... | collective-permute-start | bytes 12296 | tf_op jit(solution)/shard_map/ppermute | solution.py:665
  5.3 2.1 %collective-permute-start.2 = (f32[8,128]{1,0:T(8,128)}, f32[8,128]{1,0:T(8,128)S(1)}, u32[]{:S(2)}, u32[]{:S(2)}) collective-permute-start(f32[8,128]{1,0:T(8,128)} %get-tuple-element.60), channel_id=1, source_target_pairs={{0,24},{4,28},{8,0},{12,4},{16,8},{20,12},{24,16},{28,20},{1,25},{... | collective-permute-start | bytes 12296 | tf_op jit(solution)/shard_map/ppermute | solution.py:664
  7.4 1.6 %collective-permute-start.1 = (f32[8,512]{1,0:T(8,128)}, f32[8,512]{1,0:T(8,128)S(1)}, u32[]{:S(2)}, u32[]{:S(2)}) collective-permute-start(f32[8,512]{1,0:T(8,128)} %get-tuple-element.59.own), channel_id=1, source_target_pairs={{0,4},{4,8},{8,12},{12,16},{16,20},{20,24},{24,28},{28,0},{1,5},{5... | collective-permute-start | bytes 49160 | tf_op jit(solution)/shard_map/ppermute | solution.py:663
  9.1 3.1 %collective-permute-start = (f32[8,512]{1,0:T(8,128)}, f32[8,512]{1,0:T(8,128)S(1)}, u32[]{:S(2)}, u32[]{:S(2)}) collective-permute-start(f32[8,512]{1,0:T(8,128)} %get-tuple-element.59.own), channel_id=1, source_target_pairs={{0,28},{4,0},{8,4},{12,8},{16,12},{20,16},{24,20},{28,24},{1,29},{... | collective-permute-start | bytes 49160 | tf_op jit(solution)/shard_map/ppermute | solution.py:662
  12.2 1.8 %collective-permute-done.1.down1 = f32[8,512]{1,0:T(8,128)S(1)} collective-permute-done((f32[8,512]{1,0:T(8,128)}, f32[8,512]{1,0:T(8,128)S(1)}, u32[]{:S(2)}, u32[]{:S(2)}) %collective-permute-start.1) | collective-permute-done | bytes 16416 | tf_op jit(solution)/shard_map/ppermute | solution.py:663
  14.1 1.4 copy-done
  17.2 6.6 %shard_map.141 = (f32[3,4,64,256]{3,2,1,0:T(8,128)S(1)}, f32[24,256]{1,0:T(8,128)S(1)}, f32[24,256]{1,0:T(8,128)S(1)}, f32[72,768]{1,0:T(8,128)S(1)}, f32[72,768...) custom-call(s32[2]{0:T(128)S(1)} %pad_add_fusion.place, f32[8,512]{1,0:T(8,128)S(1)} %copy-done.1, ...), custom_call_target="tpu_custom_call" | custom-call | flops 5000000000 | bytes 15000000 | tf_op jit(solution)/shard_map/pallas_call | solution.py:594
  24.7 1.7 %collective-permute-start.6 = (f32[72,768]{1,0:T(8,128)S(1)}, f32[72,768]{1,0:T(8,128)S(1)}, u32[]{:S(2)}, u32[]{:S(2)}) collective-permute-start(f32[72,768]{1,0:T(8,128)S(1)} %get-tuple-element.66), channel_id=1, source_target_pairs={{0,2},{1,3},{2,0},{3,1},{4,6},{5,7},{6,4},{7,5},{8,10},{9,11},{10,... | collective-permute-start | bytes 663560 | tf_op jit(solution)/shard_map/ppermute | solution.py:628
  26.9 3.9 %shard_map.142 = (f32[3,4,64,256]{3,2,1,0:T(8,128)S(1)}, f32[48,256]{1,0:T(8,128)S(1)}, f32[48,256]{1,0:T(8,128)S(1)}, f32[72,768]{1,0:T(8,128)S(1)}, f32[72,768...) custom-call(s32[2]{0:T(128)S(1)} %pad_add_fusion.place, f32[8,512]{1,0:T(8,128)S(1)} %copy-done.1, ...), custom_call_target="tpu_custom_call" | custom-call | flops 5000000000 | bytes 15000000 | tf_op jit(solution)/shard_map/pallas_call | solution.py:594
  31.7 1.7 %collective-permute-start.16 = (f32[72,768]{1,0:T(8,128)S(1)}, f32[72,768]{1,0:T(8,128)S(1)}, u32[]{:S(2)}, u32[]{:S(2)}) collective-permute-start(f32[72,768]{1,0:T(8,128)S(1)} %get-tuple-element.78), channel_id=1, source_target_pairs={{0,2},{1,3},{2,0},{3,1},{4,6},{5,7},{6,4},{7,5},{8,10},{9,11},{10,... | collective-permute-start | bytes 663560 | tf_op jit(solution)/shard_map/ppermute | solution.py:628
  35.1 1.6 %shard_map.143 = (f32[32,768]{1,0:T(8,128)S(1)}, f32[32,768]{1,0:T(8,128)S(1)}, f32[32,768]{1,0:T(8,128)S(1)}, f32[32,768]{1,0:T(8,128)S(1)}, f32[32,768]{1,0:T(...) custom-call(s32[2]{0:T(128)S(1)} %pad_add_fusion.place, ...), custom_call_target="tpu_custom_call" | custom-call | flops 2000000000 | bytes 6000000 | tf_op jit(solution)/shard_map/pallas_call | solution.py:594
  36.8 2.4 %collective-permute-start.10 = (f32[32,768]{1,0:T(8,128)S(1)}, f32[32,768]{1,0:T(8,128)S(1)}, u32[]{:S(2)}, u32[]{:S(2)}) collective-permute-start(f32[32,768]{1,0:T(8,128)S(1)} %get-tuple-element.71), channel_id=1, source_target_pairs={{0,20},{4,16},{8,28},{12,24},{16,4},{20,0},{24,12},{28,8},{1,21},{... | collective-permute-start | bytes 294920 | tf_op jit(solution)/shard_map/ppermute | solution.py:628
  39.2 1.9 %collective-permute-done.16.refs_1_ = f32[72,768]{1,0:T(8,128)S(1)} collective-permute-done((f32[72,768]{1,0:T(8,128)S(1)}, f32[72,768]{1,0:T(8,128)S(1)}, u32[]{:S(2)}, u32[]{:S(2)}) %collective-permute-start.16) | collective-permute-done | bytes 221216 | tf_op jit(solution)/shard_map/ppermute | solution.py:628
  41.2 2.8 %collective-permute-done.17.refs_2_ = f32[72,768]{1,0:T(8,128)S(1)} collective-permute-done((f32[72,768]{1,0:T(8,128)S(1)}, f32[72,768]{1,0:T(8,128)S(1)}, u32[]{:S(2)}, u32[]{:S(2)}) %collective-permute-start.17) | collective-permute-done | bytes 221216 | tf_op jit(solution)/shard_map/ppermute | solution.py:628
  43.9 2.4 %collective-permute-start.12 = (f32[32,768]{1,0:T(8,128)S(1)}, f32[32,768]{1,0:T(8,128)S(1)}, u32[]{:S(2)}, u32[]{:S(2)}) collective-permute-start(f32[32,768]{1,0:T(8,128)S(1)} %get-tuple-element.73), channel_id=1, source_target_pairs={{0,24},{4,28},{8,16},{12,20},{16,8},{20,12},{24,0},{28,4},{1,25},{... | collective-permute-start | bytes 294920 | tf_op jit(solution)/shard_map/ppermute | solution.py:628
  46.4 1.6 %shard_map.145 = (f32[32,768]{1,0:T(8,128)S(1)}, f32[32,768]{1,0:T(8,128)S(1)}, f32[32,768]{1,0:T(8,128)S(1)}, f32[32,768]{1,0:T(8,128)S(1)}, f32[32,768]{1,0:T(...) custom-call(s32[2]{0:T(128)S(1)} %pad_add_fusion.place, ...), custom_call_target="tpu_custom_call" | custom-call | flops 2000000000 | bytes 6000000 | tf_op jit(solution)/shard_map/pallas_call | solution.py:594
  48.0 2.4 %collective-permute-start.14 = (f32[32,768]{1,0:T(8,128)S(1)}, f32[32,768]{1,0:T(8,128)S(1)}, u32[]{:S(2)}, u32[]{:S(2)}) collective-permute-start(f32[32,768]{1,0:T(8,128)S(1)} %get-tuple-element.75), channel_id=1, source_target_pairs={{0,28},{4,24},{8,20},{12,16},{16,12},{20,8},{24,4},{28,0},{1,29},{... | collective-permute-start | bytes 294920 | tf_op jit(solution)/shard_map/ppermute | solution.py:628
  50.4 2.1 %collective-permute-start.15 = (f32[32,768]{1,0:T(8,128)S(1)}, f32[32,768]{1,0:T(8,128)S(1)}, u32[]{:S(2)}, u32[]{:S(2)}) collective-permute-start(f32[32,768]{1,0:T(8,128)S(1)} %get-tuple-element.76), channel_id=1, source_target_pairs={{0,12},{4,8},{8,4},{12,0},{16,28},{20,24},{24,20},{28,16},{1,13},{... | collective-permute-start | bytes 294920 | tf_op jit(solution)/shard_map/ppermute | solution.py:628
  52.5 1.4 collective-permute-start.19
  53.9 1.8 %collective-permute-start.20 = (f32[32,768]{1,0:T(8,128)S(1)}, f32[32,768]{1,0:T(8,128)S(1)}, u32[]{:S(2)}, u32[]{:S(2)}) collective-permute-start(f32[32,768]{1,0:T(8,128)S(1)} %get-tuple-element.83), channel_id=1, source_target_pairs={{0,20},{4,16},{8,28},{12,24},{16,4},{20,0},{24,12},{28,8},{1,21},{... | collective-permute-start | bytes 294920 | tf_op jit(solution)/shard_map/ppermute | solution.py:628
  56.9 3.5 %collective-permute-start.22 = (f32[32,768]{1,0:T(8,128)S(1)}, f32[32,768]{1,0:T(8,128)S(1)}, u32[]{:S(2)}, u32[]{:S(2)}) collective-permute-start(f32[32,768]{1,0:T(8,128)S(1)} %get-tuple-element.85), channel_id=1, source_target_pairs={{0,24},{4,28},{8,16},{12,20},{16,8},{20,12},{24,0},{28,4},{1,25},{... | collective-permute-start | bytes 294920 | tf_op jit(solution)/shard_map/ppermute | solution.py:628
  60.8 7.2 %collective-permute-done.19.refs_1_ = f32[32,768]{1,0:T(8,128)S(1)} collective-permute-done((f32[32,768]{1,0:T(8,128)S(1)}, f32[32,768]{1,0:T(8,128)S(1)}, u32[]{:S(2)}, u32[]{:S(2)}) %collective-permute-start.19) | collective-permute-done | bytes 98336 | tf_op jit(solution)/shard_map/ppermute | solution.py:628
  70.7 1.7 %collective-permute-start.5 = (f32[48,256]{1,0:T(8,128)S(1)}, f32[48,256]{1,0:T(8,128)S(1)}, u32[]{:S(2)}, u32[]{:S(2)}) collective-permute-start(f32[48,256]{1,0:T(8,128)S(1)} %get-tuple-element.64), channel_id=1, source_target_pairs={{0,3},{1,0},{2,1},{3,2},{4,7},{5,4},{6,5},{7,6},{8,11},{9,8},{10,9... | collective-permute-start | bytes 147464 | tf_op jit(solution)/shard_map/ppermute | solution.py:686
  72.4 3.4 %collective-permute-done.24.refs_6_ = f32[32,768]{1,0:T(8,128)S(1)} collective-permute-done((f32[32,768]{1,0:T(8,128)S(1)}, f32[32,768]{1,0:T(8,128)S(1)}, u32[]{:S(2)}, u32[]{:S(2)}) %collective-permute-start.24) | collective-permute-done | bytes 98336 | tf_op jit(solution)/shard_map/ppermute | solution.py:628
  78.1 2.4 %shard_map.147 = (f32[3,2,4,8,8,128]{5,4,3,2,1,0:T(8,128)S(1)}, f32[3,2,4,8,8,128]{5,4,3,2,1,0:T(8,128)S(1)}) custom-call(s32[2]{0:T(128)S(1)} %pad_add_fusion.place, f32[48,256]{1,0:T(8,128)S(1)} %collective-permute-done.4.low_rim, f32[48,256]{1,0:T(8,128)S(1)} %collective-permute-done.5.high_rim, f32[3,2,4,8,8,128]{5,4,3,2,1,0:T(8,128)S(1)} %shard_map.144.refs_0_, ...), custom_call_target="tpu_custom_call" | custom-call | flops 5000000000 | bytes 15000000 | tf_op jit(solution)/shard_map/pallas_call | solution.py:594
  81.9 1.7 %collective-permute-start.26 = (f32[32,768]{1,0:T(8,128)S(1)}, f32[32,768]{1,0:T(8,128)S(1)}, u32[]{:S(2)}, u32[]{:S(2)}) collective-permute-start(f32[32,768]{1,0:T(8,128)S(1)} %get-tuple-element.91), channel_id=1, source_target_pairs={{0,16},{4,20},{8,24},{12,28},{16,0},{20,4},{24,8},{28,12},{1,17},{... | collective-permute-start | bytes 294920 | tf_op jit(solution)/shard_map/ppermute | solution.py:628
  83.7 2.1 %collective-permute-start.27 = (f32[32,768]{1,0:T(8,128)S(1)}, f32[32,768]{1,0:T(8,128)S(1)}, u32[]{:S(2)}, u32[]{:S(2)}) collective-permute-start(f32[32,768]{1,0:T(8,128)S(1)} %get-tuple-element.92), channel_id=1, source_target_pairs={{0,20},{4,16},{8,28},{12,24},{16,4},{20,0},{24,12},{28,8},{1,21},{... | collective-permute-start | bytes 294920 | tf_op jit(solution)/shard_map/ppermute | solution.py:628
  88.6 6.3 %collective-permute-done.26.refs_1_ = f32[32,768]{1,0:T(8,128)S(1)} collective-permute-done((f32[32,768]{1,0:T(8,128)S(1)}, f32[32,768]{1,0:T(8,128)S(1)}, u32[]{:S(2)}, u32[]{:S(2)}) %collective-permute-start.26) | collective-permute-done | bytes 98336 | tf_op jit(solution)/shard_map/ppermute | solution.py:628
  94.9 1.4 collective-permute-start.31
  96.3 1.5 collective-permute-done.27.refs_2_
  98.6 3.7 %collective-permute-done.31.refs_6_ = f32[32,768]{1,0:T(8,128)S(1)} collective-permute-done((f32[32,768]{1,0:T(8,128)S(1)}, f32[32,768]{1,0:T(8,128)S(1)}, u32[]{:S(2)}, u32[]{:S(2)}) %collective-permute-start.31) | collective-permute-done | bytes 98336 | tf_op jit(solution)/shard_map/ppermute | solution.py:628
  103.6 2.5 %shard_map.149 = f32[4,72,768]{2,1,0:T(8,128)} custom-call(s32[2]{0:T(128)S(1)} %pad_add_fusion.place, bf16[576,256]{1,0:T(8,128)(2,1)S(1)} %copy-done.7, bf16[576,256]{1,0:T(8,128)(2,1)S(1)} %copy-done.6, f32[32,768]{1,0:T(8,128)S(1)} %get-tuple-element.90.refs_0_, f32[32,768]{1,0:T(8,128)S(1)} %collective-permute-done.26.refs_1_, ...), custom_call_target="tpu_custom_call" | custom-call | flops 2000000000 | bytes 6000000 | tf_op jit(solution)/shard_map/pallas_call | solution.py:594
  106.1 3.6 %all-to-all-start = ((f32[4,72,768]{2,1,0:T(8,128)}), f32[4,72,768]{2,1,0:T(8,128)S(1)}, u32[]{:S(2)}, u32[]{:S(2)}) async-start(f32[4,72,768]{2,1,0:T(8,128)} %shard_map.149), calls=%async_computation | async-start | bytes 1769472 | tf_op jit(solution)/shard_map/all_to_all | solution.py:624
  112.0 1.9 %collective-permute-start.36 = (f32[32,768]{1,0:T(8,128)S(1)}, f32[32,768]{1,0:T(8,128)S(1)}, u32[]{:S(2)}, u32[]{:S(2)}) collective-permute-start(f32[32,768]{1,0:T(8,128)S(1)} %get-tuple-element.106), channel_id=1, source_target_pairs={{0,20},{4,16},{8,28},{12,24},{16,4},{20,0},{24,12},{28,8},{1,21},{... | collective-permute-start | bytes 294920 | tf_op jit(solution)/shard_map/ppermute | solution.py:628
  114.0 1.6 %collective-permute-start.37 = (f32[32,768]{1,0:T(8,128)S(1)}, f32[32,768]{1,0:T(8,128)S(1)}, u32[]{:S(2)}, u32[]{:S(2)}) collective-permute-start(f32[32,768]{1,0:T(8,128)S(1)} %get-tuple-element.107), channel_id=1, source_target_pairs={{0,4},{4,0},{8,12},{12,8},{16,20},{20,16},{24,28},{28,24},{1,5},{5... | collective-permute-start | bytes 294920 | tf_op jit(solution)/shard_map/ppermute | solution.py:628
  115.6 1.8 %collective-permute-start.38 = (f32[32,768]{1,0:T(8,128)S(1)}, f32[32,768]{1,0:T(8,128)S(1)}, u32[]{:S(2)}, u32[]{:S(2)}) collective-permute-start(f32[32,768]{1,0:T(8,128)S(1)} %get-tuple-element.108), channel_id=1, source_target_pairs={{0,24},{4,28},{8,16},{12,20},{16,8},{20,12},{24,0},{28,4},{1,25},{... | collective-permute-start | bytes 294920 | tf_op jit(solution)/shard_map/ppermute | solution.py:628
  117.4 6.5 %collective-permute-done.35.refs_1_ = f32[32,768]{1,0:T(8,128)S(1)} collective-permute-done((f32[32,768]{1,0:T(8,128)S(1)}, f32[32,768]{1,0:T(8,128)S(1)}, u32[]{:S(2)}, u32[]{:S(2)}) %collective-permute-start.35) | collective-permute-done | bytes 98336 | tf_op jit(solution)/shard_map/ppermute | solution.py:628
  123.9 1.6 %collective-permute-start.40 = (f32[32,768]{1,0:T(8,128)S(1)}, f32[32,768]{1,0:T(8,128)S(1)}, u32[]{:S(2)}, u32[]{:S(2)}) collective-permute-start(f32[32,768]{1,0:T(8,128)S(1)} %get-tuple-element.110), channel_id=1, source_target_pairs={{0,28},{4,24},{8,20},{12,16},{16,12},{20,8},{24,4},{28,0},{1,29},{... | collective-permute-start | bytes 294920 | tf_op jit(solution)/shard_map/ppermute | solution.py:628
  126.0 1.5 collective-permute-done.39.refs_5_
  127.5 4.6 %collective-permute-done.40.refs_6_ = f32[32,768]{1,0:T(8,128)S(1)} collective-permute-done((f32[32,768]{1,0:T(8,128)S(1)}, f32[32,768]{1,0:T(8,128)S(1)}, u32[]{:S(2)}, u32[]{:S(2)}) %collective-permute-start.40) | collective-permute-done | bytes 98336 | tf_op jit(solution)/shard_map/ppermute | solution.py:628
  132.9 1.7 %shard_map.152 = (f32[72,768]{1,0:T(8,128)S(1)}, f32[72,768]{1,0:T(8,128)S(1)}, f32[72,768]{1,0:T(8,128)S(1)}, f32[72,768]{1,0:T(8,128)S(1)}) custom-call(s32[2]{0:T(128)S(1)} %pad_add_fusion.place, bf16[576,256]{1,0:T(8,128)(2,1)S(1)} %copy-done.8, bf16[576,256]{1,0:T(8,128)(2,1)S(1)} %copy-done.6, f32[32,768]{1,0:T(8,128)S(1)} %get-tuple-element.104.refs_0_, ...), custom_call_target="tpu_custom_call" | custom-call | flops 2000000000 | bytes 6000000 | tf_op jit(solution)/shard_map/pallas_call | solution.py:594
  135.3 1.5 %collective-permute-start.42 = (f32[72,768]{1,0:T(8,128)S(1)}, f32[72,768]{1,0:T(8,128)S(1)}, u32[]{:S(2)}, u32[]{:S(2)}) collective-permute-start(f32[72,768]{1,0:T(8,128)S(1)} %get-tuple-element.113), channel_id=1, source_target_pairs={{0,2},{1,3},{2,0},{3,1},{4,6},{5,7},{6,4},{7,5},{8,10},{9,11},{10,... | collective-permute-start | bytes 663560 | tf_op jit(solution)/shard_map/ppermute | solution.py:628
  139.8 3.9 %collective-permute-start.34 = (f32[3,64,256]{2,1,0:T(8,128)S(1)}, f32[3,64,256]{2,1,0:T(8,128)S(1)}, u32[]{:S(2)}, u32[]{:S(2)}) collective-permute-start(f32[3,64,256]{2,1,0:T(8,128)S(1)} %get-tuple-element.100), channel_id=1, source_target_pairs={{0,28},{4,0},{8,4},{12,8},{16,12},{20,16},{24,20},{28,24},{1,29},{... | collective-permute-start | bytes 589832 | tf_op jit(solution)/shard_map/ppermute | solution.py:737
  143.7 1.7 %collective-permute-done.43.refs_4_ = f32[72,768]{1,0:T(8,128)S(1)} collective-permute-done((f32[72,768]{1,0:T(8,128)S(1)}, f32[72,768]{1,0:T(8,128)S(1)}, u32[]{:S(2)}, u32[]{:S(2)}) %collective-permute-start.43) | collective-permute-done | bytes 221216 | tf_op jit(solution)/shard_map/ppermute | solution.py:628
  145.4 3.2 %collective-permute-done.33.before = f32[3,64,256]{2,1,0:T(8,128)S(1)} collective-permute-done((f32[3,64,256]{2,1,0:T(8,128)S(1)}, f32[3,64,256]{2,1,0:T(8,128)S(1)}, u32[]{:S(2)}, u32[]{:S(2)}) %collective-permute-start.33) | collective-permute-done | bytes 196640 | tf_op jit(solution)/shard_map/ppermute | solution.py:738
  148.6 2.0 %collective-permute-done.34.after = f32[3,64,256]{2,1,0:T(8,128)S(1)} collective-permute-done((f32[3,64,256]{2,1,0:T(8,128)S(1)}, f32[3,64,256]{2,1,0:T(8,128)S(1)}, u32[]{:S(2)}, u32[]{:S(2)}) %collective-permute-start.34) | collective-permute-done | bytes 196640 | tf_op jit(solution)/shard_map/ppermute | solution.py:737
  150.6 3.1 %shard_map.153 = (f32[3,8,64,256]{3,2,1,0:T(8,128)}, f32[3,8,64,256]{3,2,1,0:T(8,128)}) custom-call(s32[2]{0:T(128)S(1)} %pad_add_fusion.place, bf16[512,512]{1,0:T(8,128)(2,1)S(1)} %copy-done.3, bf16[512,512]{1,0:T(8,128)(2,1)S(1)} %copy-done.2, f32[3,4,80,256]{3,2,1,0:T(8,128)S(1)} %get-tuple-element.98.edges, ...), custom_call_target="tpu_custom_call" | custom-call | flops 4000000000 | bytes 12000000 | tf_op jit(solution)/shard_map/pallas_call | solution.py:594
  (97 shorter events, 26.1 us)
Async XLA Ops:
  2.2 10.0 %collective-permute-start.3 = (f32[8,128]{1,0:T(8,128)}, f32[8,128]{1,0:T(8,128)S(1)}, u32[]{:S(2)}, u32[]{:S(2)}) collective-permute-start(f32[8,128]{1,0:T(8,128)} %get-tuple-element.60), channel_id=1, source_target_pairs={{0,8},{4,12},{8,16},{12,20},{16,24},{20,28},{24,0},{28,4},{1,9},{5... | collective-permute-start | bytes 12296 | tf_op jit(solution)/shard_map/ppermute | solution.py:665
  5.3 6.9 %collective-permute-start.2 = (f32[8,128]{1,0:T(8,128)}, f32[8,128]{1,0:T(8,128)S(1)}, u32[]{:S(2)}, u32[]{:S(2)}) collective-permute-start(f32[8,128]{1,0:T(8,128)} %get-tuple-element.60), channel_id=1, source_target_pairs={{0,24},{4,28},{8,0},{12,4},{16,8},{20,12},{24,16},{28,20},{1,25},{... | collective-permute-start | bytes 12296 | tf_op jit(solution)/shard_map/ppermute | solution.py:664
  7.4 6.6 %collective-permute-start.1 = (f32[8,512]{1,0:T(8,128)}, f32[8,512]{1,0:T(8,128)S(1)}, u32[]{:S(2)}, u32[]{:S(2)}) collective-permute-start(f32[8,512]{1,0:T(8,128)} %get-tuple-element.59.own), channel_id=1, source_target_pairs={{0,4},{4,8},{8,12},{12,16},{16,20},{20,24},{24,28},{28,0},{1,5},{5... | collective-permute-start | bytes 49160 | tf_op jit(solution)/shard_map/ppermute | solution.py:663
  9.1 5.0 %collective-permute-start = (f32[8,512]{1,0:T(8,128)}, f32[8,512]{1,0:T(8,128)S(1)}, u32[]{:S(2)}, u32[]{:S(2)}) collective-permute-start(f32[8,512]{1,0:T(8,128)} %get-tuple-element.59.own), channel_id=1, source_target_pairs={{0,28},{4,0},{8,4},{12,8},{16,12},{20,16},{24,20},{28,24},{1,29},{... | collective-permute-start | bytes 49160 | tf_op jit(solution)/shard_map/ppermute | solution.py:662
  24.7 8.7 %collective-permute-start.6 = (f32[72,768]{1,0:T(8,128)S(1)}, f32[72,768]{1,0:T(8,128)S(1)}, u32[]{:S(2)}, u32[]{:S(2)}) collective-permute-start(f32[72,768]{1,0:T(8,128)S(1)} %get-tuple-element.66), channel_id=1, source_target_pairs={{0,2},{1,3},{2,0},{3,1},{4,6},{5,7},{6,4},{7,5},{8,10},{9,11},{10,... | collective-permute-start | bytes 663560 | tf_op jit(solution)/shard_map/ppermute | solution.py:628
  26.4 8.7 %collective-permute-start.7 = (f32[72,768]{1,0:T(8,128)S(1)}, f32[72,768]{1,0:T(8,128)S(1)}, u32[]{:S(2)}, u32[]{:S(2)}) collective-permute-start(f32[72,768]{1,0:T(8,128)S(1)} %get-tuple-element.67), channel_id=1, source_target_pairs={{0,3},{1,2},{2,1},{3,0},{4,7},{5,6},{6,5},{7,4},{8,11},{9,10},{10,... | collective-permute-start | bytes 663560 | tf_op jit(solution)/shard_map/ppermute | solution.py:628
  26.4 8.7 %collective-permute-start.8 = (f32[72,768]{1,0:T(8,128)S(1)}, f32[72,768]{1,0:T(8,128)S(1)}, u32[]{:S(2)}, u32[]{:S(2)}) collective-permute-start(f32[72,768]{1,0:T(8,128)S(1)} %get-tuple-element.68), channel_id=1, source_target_pairs={{0,1},{1,0},{2,3},{3,2},{4,5},{5,4},{6,7},{7,6},{8,9},{9,8},{10,11... | collective-permute-start | bytes 663560 | tf_op jit(solution)/shard_map/ppermute | solution.py:628
  31.7 9.3 %collective-permute-start.16 = (f32[72,768]{1,0:T(8,128)S(1)}, f32[72,768]{1,0:T(8,128)S(1)}, u32[]{:S(2)}, u32[]{:S(2)}) collective-permute-start(f32[72,768]{1,0:T(8,128)S(1)} %get-tuple-element.78), channel_id=1, source_target_pairs={{0,2},{1,3},{2,0},{3,1},{4,6},{5,7},{6,4},{7,5},{8,10},{9,11},{10,... | collective-permute-start | bytes 663560 | tf_op jit(solution)/shard_map/ppermute | solution.py:628
  33.4 10.5 %collective-permute-start.17 = (f32[72,768]{1,0:T(8,128)S(1)}, f32[72,768]{1,0:T(8,128)S(1)}, u32[]{:S(2)}, u32[]{:S(2)}) collective-permute-start(f32[72,768]{1,0:T(8,128)S(1)} %get-tuple-element.79), channel_id=1, source_target_pairs={{0,3},{1,2},{2,1},{3,0},{4,7},{5,6},{6,5},{7,4},{8,11},{9,10},{10,... | collective-permute-start | bytes 663560 | tf_op jit(solution)/shard_map/ppermute | solution.py:628
  33.4 12.9 %collective-permute-start.18 = (f32[72,768]{1,0:T(8,128)S(1)}, f32[72,768]{1,0:T(8,128)S(1)}, u32[]{:S(2)}, u32[]{:S(2)}) collective-permute-start(f32[72,768]{1,0:T(8,128)S(1)} %get-tuple-element.80), channel_id=1, source_target_pairs={{0,1},{1,0},{2,3},{3,2},{4,5},{5,4},{6,7},{7,6},{8,9},{9,8},{10,11... | collective-permute-start | bytes 663560 | tf_op jit(solution)/shard_map/ppermute | solution.py:628
  36.7 11.2 %collective-permute-start.9 = (f32[32,768]{1,0:T(8,128)S(1)}, f32[32,768]{1,0:T(8,128)S(1)}, u32[]{:S(2)}, u32[]{:S(2)}) collective-permute-start(f32[32,768]{1,0:T(8,128)S(1)} %get-tuple-element.70), channel_id=1, source_target_pairs={{0,16},{4,20},{8,24},{12,28},{16,0},{20,4},{24,8},{28,12},{1,17},{... | collective-permute-start | bytes 294920 | tf_op jit(solution)/shard_map/ppermute | solution.py:628
  36.8 13.6 %collective-permute-start.10 = (f32[32,768]{1,0:T(8,128)S(1)}, f32[32,768]{1,0:T(8,128)S(1)}, u32[]{:S(2)}, u32[]{:S(2)}) collective-permute-start(f32[32,768]{1,0:T(8,128)S(1)} %get-tuple-element.71), channel_id=1, source_target_pairs={{0,20},{4,16},{8,28},{12,24},{16,4},{20,0},{24,12},{28,8},{1,21},{... | collective-permute-start | bytes 294920 | tf_op jit(solution)/shard_map/ppermute | solution.py:628
  41.0 11.4 %collective-permute-start.11 = (f32[32,768]{1,0:T(8,128)S(1)}, f32[32,768]{1,0:T(8,128)S(1)}, u32[]{:S(2)}, u32[]{:S(2)}) collective-permute-start(f32[32,768]{1,0:T(8,128)S(1)} %get-tuple-element.72), channel_id=1, source_target_pairs={{0,4},{4,0},{8,12},{12,8},{16,20},{20,16},{24,28},{28,24},{1,5},{5... | collective-permute-start | bytes 294920 | tf_op jit(solution)/shard_map/ppermute | solution.py:628
  43.9 10.0 %collective-permute-start.12 = (f32[32,768]{1,0:T(8,128)S(1)}, f32[32,768]{1,0:T(8,128)S(1)}, u32[]{:S(2)}, u32[]{:S(2)}) collective-permute-start(f32[32,768]{1,0:T(8,128)S(1)} %get-tuple-element.73), channel_id=1, source_target_pairs={{0,24},{4,28},{8,16},{12,20},{16,8},{20,12},{24,0},{28,4},{1,25},{... | collective-permute-start | bytes 294920 | tf_op jit(solution)/shard_map/ppermute | solution.py:628
  46.3 9.4 %collective-permute-start.13 = (f32[32,768]{1,0:T(8,128)S(1)}, f32[32,768]{1,0:T(8,128)S(1)}, u32[]{:S(2)}, u32[]{:S(2)}) collective-permute-start(f32[32,768]{1,0:T(8,128)S(1)} %get-tuple-element.74), channel_id=1, source_target_pairs={{0,8},{4,12},{8,0},{12,4},{16,24},{20,28},{24,16},{28,20},{1,9},{5... | collective-permute-start | bytes 294920 | tf_op jit(solution)/shard_map/ppermute | solution.py:628
  48.0 8.9 %collective-permute-start.14 = (f32[32,768]{1,0:T(8,128)S(1)}, f32[32,768]{1,0:T(8,128)S(1)}, u32[]{:S(2)}, u32[]{:S(2)}) collective-permute-start(f32[32,768]{1,0:T(8,128)S(1)} %get-tuple-element.75), channel_id=1, source_target_pairs={{0,28},{4,24},{8,20},{12,16},{16,12},{20,8},{24,4},{28,0},{1,29},{... | collective-permute-start | bytes 294920 | tf_op jit(solution)/shard_map/ppermute | solution.py:628
  50.4 10.1 %collective-permute-start.15 = (f32[32,768]{1,0:T(8,128)S(1)}, f32[32,768]{1,0:T(8,128)S(1)}, u32[]{:S(2)}, u32[]{:S(2)}) collective-permute-start(f32[32,768]{1,0:T(8,128)S(1)} %get-tuple-element.76), channel_id=1, source_target_pairs={{0,12},{4,8},{8,4},{12,0},{16,28},{20,24},{24,20},{28,16},{1,13},{... | collective-permute-start | bytes 294920 | tf_op jit(solution)/shard_map/ppermute | solution.py:628
  52.5 15.6 %collective-permute-start.19 = (f32[32,768]{1,0:T(8,128)S(1)}, f32[32,768]{1,0:T(8,128)S(1)}, u32[]{:S(2)}, u32[]{:S(2)}) collective-permute-start(f32[32,768]{1,0:T(8,128)S(1)} %get-tuple-element.82), channel_id=1, source_target_pairs={{0,16},{4,20},{8,24},{12,28},{16,0},{20,4},{24,8},{28,12},{1,17},{... | collective-permute-start | bytes 294920 | tf_op jit(solution)/shard_map/ppermute | solution.py:628
  53.9 15.4 %collective-permute-start.20 = (f32[32,768]{1,0:T(8,128)S(1)}, f32[32,768]{1,0:T(8,128)S(1)}, u32[]{:S(2)}, u32[]{:S(2)}) collective-permute-start(f32[32,768]{1,0:T(8,128)S(1)} %get-tuple-element.83), channel_id=1, source_target_pairs={{0,20},{4,16},{8,28},{12,24},{16,4},{20,0},{24,12},{28,8},{1,21},{... | collective-permute-start | bytes 294920 | tf_op jit(solution)/shard_map/ppermute | solution.py:628
  55.7 14.9 %collective-permute-start.21 = (f32[32,768]{1,0:T(8,128)S(1)}, f32[32,768]{1,0:T(8,128)S(1)}, u32[]{:S(2)}, u32[]{:S(2)}) collective-permute-start(f32[32,768]{1,0:T(8,128)S(1)} %get-tuple-element.84), channel_id=1, source_target_pairs={{0,4},{4,0},{8,12},{12,8},{16,20},{20,16},{24,28},{28,24},{1,5},{5... | collective-permute-start | bytes 294920 | tf_op jit(solution)/shard_map/ppermute | solution.py:628
  56.9 13.8 %collective-permute-start.22 = (f32[32,768]{1,0:T(8,128)S(1)}, f32[32,768]{1,0:T(8,128)S(1)}, u32[]{:S(2)}, u32[]{:S(2)}) collective-permute-start(f32[32,768]{1,0:T(8,128)S(1)} %get-tuple-element.85), channel_id=1, source_target_pairs={{0,24},{4,28},{8,16},{12,20},{16,8},{20,12},{24,0},{28,4},{1,25},{... | collective-permute-start | bytes 294920 | tf_op jit(solution)/shard_map/ppermute | solution.py:628
  60.5 12.0 %collective-permute-start.23 = (f32[32,768]{1,0:T(8,128)S(1)}, f32[32,768]{1,0:T(8,128)S(1)}, u32[]{:S(2)}, u32[]{:S(2)}) collective-permute-start(f32[32,768]{1,0:T(8,128)S(1)} %get-tuple-element.86), channel_id=1, source_target_pairs={{0,8},{4,12},{8,0},{12,4},{16,24},{20,28},{24,16},{28,20},{1,9},{5... | collective-permute-start | bytes 294920 | tf_op jit(solution)/shard_map/ppermute | solution.py:628
  68.0 7.8 %collective-permute-start.24 = (f32[32,768]{1,0:T(8,128)S(1)}, f32[32,768]{1,0:T(8,128)S(1)}, u32[]{:S(2)}, u32[]{:S(2)}) collective-permute-start(f32[32,768]{1,0:T(8,128)S(1)} %get-tuple-element.87), channel_id=1, source_target_pairs={{0,28},{4,24},{8,20},{12,16},{16,12},{20,8},{24,4},{28,0},{1,29},{... | collective-permute-start | bytes 294920 | tf_op jit(solution)/shard_map/ppermute | solution.py:628
  69.3 7.5 %collective-permute-start.25 = (f32[32,768]{1,0:T(8,128)S(1)}, f32[32,768]{1,0:T(8,128)S(1)}, u32[]{:S(2)}, u32[]{:S(2)}) collective-permute-start(f32[32,768]{1,0:T(8,128)S(1)} %get-tuple-element.88), channel_id=1, source_target_pairs={{0,12},{4,8},{8,4},{12,0},{16,28},{20,24},{24,20},{28,16},{1,13},{... | collective-permute-start | bytes 294920 | tf_op jit(solution)/shard_map/ppermute | solution.py:628
  70.6 7.5 %collective-permute-start.4 = (f32[48,256]{1,0:T(8,128)S(1)}, f32[48,256]{1,0:T(8,128)S(1)}, u32[]{:S(2)}, u32[]{:S(2)}) collective-permute-start(f32[48,256]{1,0:T(8,128)S(1)} %get-tuple-element.63), channel_id=1, source_target_pairs={{0,1},{1,2},{2,3},{3,0},{4,5},{5,6},{6,7},{7,4},{8,9},{9,10},{10,1... | collective-permute-start | bytes 147464 | tf_op jit(solution)/shard_map/ppermute | solution.py:685
  70.7 7.4 %collective-permute-start.5 = (f32[48,256]{1,0:T(8,128)S(1)}, f32[48,256]{1,0:T(8,128)S(1)}, u32[]{:S(2)}, u32[]{:S(2)}) collective-permute-start(f32[48,256]{1,0:T(8,128)S(1)} %get-tuple-element.64), channel_id=1, source_target_pairs={{0,3},{1,0},{2,1},{3,2},{4,7},{5,4},{6,5},{7,6},{8,11},{9,8},{10,9... | collective-permute-start | bytes 147464 | tf_op jit(solution)/shard_map/ppermute | solution.py:686
  80.5 23.0 %copy-start.6 = (bf16[576,256]{1,0:T(8,128)(2,1)S(1)}, bf16[576,256]{1,0:T(8,128)(2,1)}, u32[]{:S(2)}) copy-start(bf16[576,256]{1,0:T(8,128)(2,1)} %constant.30.clone.t_low) | copy-start | bytes 884740
  81.9 13.0 %collective-permute-start.26 = (f32[32,768]{1,0:T(8,128)S(1)}, f32[32,768]{1,0:T(8,128)S(1)}, u32[]{:S(2)}, u32[]{:S(2)}) collective-permute-start(f32[32,768]{1,0:T(8,128)S(1)} %get-tuple-element.91), channel_id=1, source_target_pairs={{0,16},{4,20},{8,24},{12,28},{16,0},{20,4},{24,8},{28,12},{1,17},{... | collective-permute-start | bytes 294920 | tf_op jit(solution)/shard_map/ppermute | solution.py:628
  83.7 14.2 %collective-permute-start.27 = (f32[32,768]{1,0:T(8,128)S(1)}, f32[32,768]{1,0:T(8,128)S(1)}, u32[]{:S(2)}, u32[]{:S(2)}) collective-permute-start(f32[32,768]{1,0:T(8,128)S(1)} %get-tuple-element.92), channel_id=1, source_target_pairs={{0,20},{4,16},{8,28},{12,24},{16,4},{20,0},{24,12},{28,8},{1,21},{... | collective-permute-start | bytes 294920 | tf_op jit(solution)/shard_map/ppermute | solution.py:628
  85.7 12.1 %collective-permute-start.28 = (f32[32,768]{1,0:T(8,128)S(1)}, f32[32,768]{1,0:T(8,128)S(1)}, u32[]{:S(2)}, u32[]{:S(2)}) collective-permute-start(f32[32,768]{1,0:T(8,128)S(1)} %get-tuple-element.93), channel_id=1, source_target_pairs={{0,4},{4,0},{8,12},{12,8},{16,20},{20,16},{24,28},{28,24},{1,5},{5... | collective-permute-start | bytes 294920 | tf_op jit(solution)/shard_map/ppermute | solution.py:628
  86.4 11.4 %collective-permute-start.29 = (f32[32,768]{1,0:T(8,128)S(1)}, f32[32,768]{1,0:T(8,128)S(1)}, u32[]{:S(2)}, u32[]{:S(2)}) collective-permute-start(f32[32,768]{1,0:T(8,128)S(1)} %get-tuple-element.94), channel_id=1, source_target_pairs={{0,24},{4,28},{8,16},{12,20},{16,8},{20,12},{24,0},{28,4},{1,25},{... | collective-permute-start | bytes 294920 | tf_op jit(solution)/shard_map/ppermute | solution.py:628
  87.3 11.3 %collective-permute-start.30 = (f32[32,768]{1,0:T(8,128)S(1)}, f32[32,768]{1,0:T(8,128)S(1)}, u32[]{:S(2)}, u32[]{:S(2)}) collective-permute-start(f32[32,768]{1,0:T(8,128)S(1)} %get-tuple-element.95), channel_id=1, source_target_pairs={{0,8},{4,12},{8,0},{12,4},{16,24},{20,28},{24,16},{28,20},{1,9},{5... | collective-permute-start | bytes 294920 | tf_op jit(solution)/shard_map/ppermute | solution.py:628
  94.9 7.4 %collective-permute-start.31 = (f32[32,768]{1,0:T(8,128)S(1)}, f32[32,768]{1,0:T(8,128)S(1)}, u32[]{:S(2)}, u32[]{:S(2)}) collective-permute-start(f32[32,768]{1,0:T(8,128)S(1)} %get-tuple-element.96), channel_id=1, source_target_pairs={{0,28},{4,24},{8,20},{12,16},{16,12},{20,8},{24,4},{28,0},{1,29},{... | collective-permute-start | bytes 294920 | tf_op jit(solution)/shard_map/ppermute | solution.py:628
  97.8 5.7 %collective-permute-start.32 = (f32[32,768]{1,0:T(8,128)S(1)}, f32[32,768]{1,0:T(8,128)S(1)}, u32[]{:S(2)}, u32[]{:S(2)}) collective-permute-start(f32[32,768]{1,0:T(8,128)S(1)} %get-tuple-element.97), channel_id=1, source_target_pairs={{0,12},{4,8},{8,4},{12,0},{16,28},{20,24},{24,20},{28,16},{1,13},{... | collective-permute-start | bytes 294920 | tf_op jit(solution)/shard_map/ppermute | solution.py:628
  106.1 31.4 %all-to-all-start = ((f32[4,72,768]{2,1,0:T(8,128)}), f32[4,72,768]{2,1,0:T(8,128)S(1)}, u32[]{:S(2)}, u32[]{:S(2)}) async-start(f32[4,72,768]{2,1,0:T(8,128)} %shard_map.149), calls=%async_computation | async-start | bytes 1769472 | tf_op jit(solution)/shard_map/all_to_all | solution.py:624
  109.7 23.2 %copy-start.8 = (bf16[576,256]{1,0:T(8,128)(2,1)S(1)}, bf16[576,256]{1,0:T(8,128)(2,1)}, u32[]{:S(2)}) copy-start(bf16[576,256]{1,0:T(8,128)(2,1)} %constant.29.clone.t_high) | copy-start | bytes 884740
  111.1 12.7 %collective-permute-start.35 = (f32[32,768]{1,0:T(8,128)S(1)}, f32[32,768]{1,0:T(8,128)S(1)}, u32[]{:S(2)}, u32[]{:S(2)}) collective-permute-start(f32[32,768]{1,0:T(8,128)S(1)} %get-tuple-element.105), channel_id=1, source_target_pairs={{0,16},{4,20},{8,24},{12,28},{16,0},{20,4},{24,8},{28,12},{1,17},{... | collective-permute-start | bytes 294920 | tf_op jit(solution)/shard_map/ppermute | solution.py:628
  112.0 14.0 %collective-permute-start.36 = (f32[32,768]{1,0:T(8,128)S(1)}, f32[32,768]{1,0:T(8,128)S(1)}, u32[]{:S(2)}, u32[]{:S(2)}) collective-permute-start(f32[32,768]{1,0:T(8,128)S(1)} %get-tuple-element.106), channel_id=1, source_target_pairs={{0,20},{4,16},{8,28},{12,24},{16,4},{20,0},{24,12},{28,8},{1,21},{... | collective-permute-start | bytes 294920 | tf_op jit(solution)/shard_map/ppermute | solution.py:628
  114.0 12.1 %collective-permute-start.37 = (f32[32,768]{1,0:T(8,128)S(1)}, f32[32,768]{1,0:T(8,128)S(1)}, u32[]{:S(2)}, u32[]{:S(2)}) collective-permute-start(f32[32,768]{1,0:T(8,128)S(1)} %get-tuple-element.107), channel_id=1, source_target_pairs={{0,4},{4,0},{8,12},{12,8},{16,20},{20,16},{24,28},{28,24},{1,5},{5... | collective-permute-start | bytes 294920 | tf_op jit(solution)/shard_map/ppermute | solution.py:628
  115.6 10.4 %collective-permute-start.38 = (f32[32,768]{1,0:T(8,128)S(1)}, f32[32,768]{1,0:T(8,128)S(1)}, u32[]{:S(2)}, u32[]{:S(2)}) collective-permute-start(f32[32,768]{1,0:T(8,128)S(1)} %get-tuple-element.108), channel_id=1, source_target_pairs={{0,24},{4,28},{8,16},{12,20},{16,8},{20,12},{24,0},{28,4},{1,25},{... | collective-permute-start | bytes 294920 | tf_op jit(solution)/shard_map/ppermute | solution.py:628
  117.4 10.1 %collective-permute-start.39 = (f32[32,768]{1,0:T(8,128)S(1)}, f32[32,768]{1,0:T(8,128)S(1)}, u32[]{:S(2)}, u32[]{:S(2)}) collective-permute-start(f32[32,768]{1,0:T(8,128)S(1)} %get-tuple-element.109), channel_id=1, source_target_pairs={{0,8},{4,12},{8,0},{12,4},{16,24},{20,28},{24,16},{28,20},{1,9},{5... | collective-permute-start | bytes 294920 | tf_op jit(solution)/shard_map/ppermute | solution.py:628
  123.9 8.2 %collective-permute-start.40 = (f32[32,768]{1,0:T(8,128)S(1)}, f32[32,768]{1,0:T(8,128)S(1)}, u32[]{:S(2)}, u32[]{:S(2)}) collective-permute-start(f32[32,768]{1,0:T(8,128)S(1)} %get-tuple-element.110), channel_id=1, source_target_pairs={{0,28},{4,24},{8,20},{12,16},{16,12},{20,8},{24,4},{28,0},{1,29},{... | collective-permute-start | bytes 294920 | tf_op jit(solution)/shard_map/ppermute | solution.py:628
  126.0 6.9 %collective-permute-start.41 = (f32[32,768]{1,0:T(8,128)S(1)}, f32[32,768]{1,0:T(8,128)S(1)}, u32[]{:S(2)}, u32[]{:S(2)}) collective-permute-start(f32[32,768]{1,0:T(8,128)S(1)} %get-tuple-element.111), channel_id=1, source_target_pairs={{0,12},{4,8},{8,4},{12,0},{16,28},{20,24},{24,20},{28,16},{1,13},{... | collective-permute-start | bytes 294920 | tf_op jit(solution)/shard_map/ppermute | solution.py:628
  135.3 8.4 %collective-permute-start.42 = (f32[72,768]{1,0:T(8,128)S(1)}, f32[72,768]{1,0:T(8,128)S(1)}, u32[]{:S(2)}, u32[]{:S(2)}) collective-permute-start(f32[72,768]{1,0:T(8,128)S(1)} %get-tuple-element.113), channel_id=1, source_target_pairs={{0,2},{1,3},{2,0},{3,1},{4,6},{5,7},{6,4},{7,5},{8,10},{9,11},{10,... | collective-permute-start | bytes 663560 | tf_op jit(solution)/shard_map/ppermute | solution.py:628
  136.9 8.5 %collective-permute-start.43 = (f32[72,768]{1,0:T(8,128)S(1)}, f32[72,768]{1,0:T(8,128)S(1)}, u32[]{:S(2)}, u32[]{:S(2)}) collective-permute-start(f32[72,768]{1,0:T(8,128)S(1)} %get-tuple-element.114), channel_id=1, source_target_pairs={{0,3},{1,2},{2,1},{3,0},{4,7},{5,6},{6,5},{7,4},{8,11},{9,10},{10,... | collective-permute-start | bytes 663560 | tf_op jit(solution)/shard_map/ppermute | solution.py:628
  136.9 8.5 %collective-permute-start.44 = (f32[72,768]{1,0:T(8,128)S(1)}, f32[72,768]{1,0:T(8,128)S(1)}, u32[]{:S(2)}, u32[]{:S(2)}) collective-permute-start(f32[72,768]{1,0:T(8,128)S(1)} %get-tuple-element.115), channel_id=1, source_target_pairs={{0,1},{1,0},{2,3},{3,2},{4,5},{5,4},{6,7},{7,6},{8,9},{9,8},{10,11... | collective-permute-start | bytes 663560 | tf_op jit(solution)/shard_map/ppermute | solution.py:628
  138.9 9.7 %collective-permute-start.33 = (f32[3,64,256]{2,1,0:T(8,128)S(1)}, f32[3,64,256]{2,1,0:T(8,128)S(1)}, u32[]{:S(2)}, u32[]{:S(2)}) collective-permute-start(f32[3,64,256]{2,1,0:T(8,128)S(1)} %get-tuple-element.99), channel_id=1, source_target_pairs={{0,4},{4,8},{8,12},{12,16},{16,20},{20,24},{24,28},{28,0},{1,5},{5... | collective-permute-start | bytes 589832 | tf_op jit(solution)/shard_map/ppermute | solution.py:738
  139.8 10.8 %collective-permute-start.34 = (f32[3,64,256]{2,1,0:T(8,128)S(1)}, f32[3,64,256]{2,1,0:T(8,128)S(1)}, u32[]{:S(2)}, u32[]{:S(2)}) collective-permute-start(f32[3,64,256]{2,1,0:T(8,128)S(1)} %get-tuple-element.100), channel_id=1, source_target_pairs={{0,28},{4,0},{8,4},{12,8},{16,12},{20,16},{24,20},{28,24},{1,29},{... | collective-permute-start | bytes 589832 | tf_op jit(solution)/shard_map/ppermute | solution.py:737
  (17 other events, 112.1 us)

commit v4 on v3

--- a/solution.py
+++ b/solution.py
@@ -286,7 +286,7 @@
         out[...] = made[d]
 
 
-def x_back_kernel(sends, place, t_high, t_low, *refs):
+def x_back_kernel(sends, place, last_left, t_high, t_low, *refs):
     held, made = refs[-2:]
     outs, parts = refs[-2 - sends : -2], refs[: -2 - sends]
     gather_blocks(parts, held, place[0])
@@ -589,7 +589,7 @@
 AN = pl.BlockSpec(memory_space=pl.ANY)
 
 
-def call(kernel, ins, outs, scratch=(), sems=0, micros=2.0, vmem=VMEM):
+def call(kernel, ins, outs, scratch=(), sems=0, micros=2.0, moved=None):
     extra = [pltpu.SemaphoreType.DMA((sems,))] if sems else []
     return pl.pallas_call(
         kernel,
@@ -597,9 +597,11 @@
         in_specs=[spec for spec, _ in ins],
         out_specs=[spec for spec, _ in outs],
         scratch_shapes=[pltpu.VMEM(shape, kind) for shape, kind in scratch] + extra,
-        compiler_params=pltpu.CompilerParams(vmem_limit_bytes=vmem),
+        compiler_params=pltpu.CompilerParams(vmem_limit_bytes=VMEM),
         cost_estimate=pl.CostEstimate(
-            flops=int(micros * 1.0e9), bytes_accessed=int(micros * 3.0e6), transcendentals=0
+            flops=int(micros * 1.0e9),
+            bytes_accessed=int(micros * 3.0e6) if moved is None else moved,
+            transcendentals=0,
         ),
     )(*[value for _, value in ins])
 
@@ -657,7 +659,7 @@
         [((1, 2), jnp.int32), ((1, count), jnp.int32)],
         sems=4,
         micros=1.0,
-        vmem=63 * 1024 * 1024,
+        moved=1000,
     )
     up1 = lax.ppermute(packet, "gz", ring("gz", -1))
     down1 = lax.ppermute(packet, "gz", ring("gz", 1))
@@ -708,19 +710,22 @@
         [((3, 2, nz, tile, LANES), F32)],
         micros=5.0,
     )
-    parts = []
-    for chunk, source, width in zip(chunks, data, widths):
-        part = call(
+    left = [
+        call(
             functools.partial(leave_kernel, chunk, nz),
             [here, (VM, source)],
             [(VM, shape) for shape in sent_shapes("gz", block, width)],
             [(source.shape, F32)],
         )
+        for chunk, source, width in zip(chunks, data, widths)
+    ]
+    parts = []
+    for part, width in zip(left, widths):
         part = exchange(part, "gz")
         shapes = sent_shapes("gx", rows, width, whole=not parts)
         part = call(
             functools.partial(x_back_kernel, len(shapes)),
-            [here, (VM, x_back[0]), (VM, x_back[1])] + [(VM, p) for p in part],
+            [here, (AN, left[-1][0]), (VM, x_back[0]), (VM, x_back[1])] + [(VM, p) for p in part],
             [(VM, shape) for shape in shapes],
             [((slabs, block, width), F32), ((pencils, rows, width), F32)],
         )

time: 154 us -> 152 us (0.987)
  waiting for transfers between devices: 53.7 us -> 51.2 us
    unnamed x38 -> x42, local copies, waits for them, and re-layouts: 5.71 us -> 7.2 us
  transfers between devices with their start and end apart: 46 -> 46, of which waited for: 21 -> 20; matrix products, arithmetic and copies ran while one was open for 0% -> 0% of each run, Pallas kernels for 9% -> 9%
where the time goes in v4:
time: 152 us
  starting transfers between devices  61.8 us (41%)
  waiting for transfers between devices  51.2 us (34%)
  Pallas kernels  30.5 us (20%)
  local copies, waits for them, and re-layouts  7.2 us (5%)
    ppermute x37, waiting for transfers between devices, exchange(): lax.ppermute(block, axis, [(i, i ^ k) for i in range(count)])  45.3 us
    ppermute x37, starting transfers between devices, exchange(): lax.ppermute(block, axis, [(i, i ^ k) for i in range(count)])  41.8 us
    pallas_call x14, Pallas kernels, call(): pl.pallas_call(kernel, out_shape=[jax.ShapeDtypeStruct(shape, F32) for _,...  30.5 us
    unnamed x42, local copies, waits for them, and re-layouts  7.2 us
    ppermute x1, starting transfers between devices, on_device(): after = lax.ppermute(first, 'gz', ring('gz', -1))  4.1 us
    all_to_all x1, starting transfers between devices, exchange(): lax.all_to_all(blocks[0], axis, split_axis=0, concat_axis=0, tiled=True)  3.5 us
    ppermute x1, starting transfers between devices, on_device(): down2 = lax.ppermute(movers, 'gz', ring('gz', 2))  3.08 us
    ppermute x1, starting transfers between devices, on_device(): up1 = lax.ppermute(packet, 'gz', ring('gz', -1))  3.08 us
  transfers between devices with their start and end apart: 46, of which 20 were waited for; matrix products, arithmetic and copies ran while one was open for 0% of the time, Pallas kernels for 9%

profile of v4, /device:TPU:0, one launch (start us, length us, event | category | flops | bytes accessed | tf_op | source)
XLA Modules:
  0.0 151.9 jit_solution(3556462669018555085)
XLA Ops:
  3.6 3.1 %collective-permute-start.3 = (f32[8,128]{1,0:T(8,128)S(1)}, f32[8,128]{1,0:T(8,128)S(1)}, u32[]{:S(2)}, u32[]{:S(2)}) collective-permute-start(f32[8,128]{1,0:T(8,128)S(1)} %get-tuple-element.60), channel_id=1, source_target_pairs={{0,8},{4,12},{8,16},{12,20},{16,24},{20,28},{24,0},{28,4},{1,9},{5... | collective-permute-start | bytes 12296 | tf_op jit(solution)/shard_map/ppermute | solution.py:667
  6.7 2.1 %collective-permute-start.2 = (f32[8,128]{1,0:T(8,128)S(1)}, f32[8,128]{1,0:T(8,128)S(1)}, u32[]{:S(2)}, u32[]{:S(2)}) collective-permute-start(f32[8,128]{1,0:T(8,128)S(1)} %get-tuple-element.60), channel_id=1, source_target_pairs={{0,24},{4,28},{8,0},{12,4},{16,8},{20,12},{24,16},{28,20},{1,25},{... | collective-permute-start | bytes 12296 | tf_op jit(solution)/shard_map/ppermute | solution.py:666
  8.7 1.6 %collective-permute-start.1 = (f32[8,512]{1,0:T(8,128)S(1)}, f32[8,512]{1,0:T(8,128)S(1)}, u32[]{:S(2)}, u32[]{:S(2)}) collective-permute-start(f32[8,512]{1,0:T(8,128)S(1)} %get-tuple-element.59.own), channel_id=1, source_target_pairs={{0,4},{4,8},{8,12},{12,16},{16,20},{20,24},{24,28},{28,0},{1,5},{5... | collective-permute-start | bytes 49160 | tf_op jit(solution)/shard_map/ppermute | solution.py:665
  10.4 3.1 %collective-permute-start = (f32[8,512]{1,0:T(8,128)S(1)}, f32[8,512]{1,0:T(8,128)S(1)}, u32[]{:S(2)}, u32[]{:S(2)}) collective-permute-start(f32[8,512]{1,0:T(8,128)S(1)} %get-tuple-element.59.own), channel_id=1, source_target_pairs={{0,28},{4,0},{8,4},{12,8},{16,12},{20,16},{24,20},{28,24},{1,29},{... | collective-permute-start | bytes 49160 | tf_op jit(solution)/shard_map/ppermute | solution.py:664
  13.6 1.6 %collective-permute-done.1.down1 = f32[8,512]{1,0:T(8,128)S(1)} collective-permute-done((f32[8,512]{1,0:T(8,128)S(1)}, f32[8,512]{1,0:T(8,128)S(1)}, u32[]{:S(2)}, u32[]{:S(2)}) %collective-permute-start.1) | collective-permute-done | bytes 16416 | tf_op jit(solution)/shard_map/ppermute | solution.py:665
  15.2 6.6 %shard_map.141 = (f32[3,4,64,256]{3,2,1,0:T(8,128)S(1)}, f32[24,256]{1,0:T(8,128)S(1)}, f32[24,256]{1,0:T(8,128)S(1)}, f32[72,768]{1,0:T(8,128)S(1)}, f32[72,768...) custom-call(s32[2]{0:T(128)S(1)} %pad_add_fusion.place, f32[8,512]{1,0:T(8,128)S(1)} %get-tuple-element.59.own, ...), custom_call_target="tpu_custom_call" | custom-call | flops 5000000000 | bytes 15000000 | tf_op jit(solution)/shard_map/pallas_call | solution.py:594
  22.7 1.7 %collective-permute-start.6 = (f32[72,768]{1,0:T(8,128)S(1)}, f32[72,768]{1,0:T(8,128)S(1)}, u32[]{:S(2)}, u32[]{:S(2)}) collective-permute-start(f32[72,768]{1,0:T(8,128)S(1)} %get-tuple-element.66), channel_id=1, source_target_pairs={{0,2},{1,3},{2,0},{3,1},{4,6},{5,7},{6,4},{7,5},{8,10},{9,11},{10,... | collective-permute-start | bytes 663560 | tf_op jit(solution)/shard_map/ppermute | solution.py:630
  24.8 3.9 %shard_map.142 = (f32[3,4,64,256]{3,2,1,0:T(8,128)S(1)}, f32[48,256]{1,0:T(8,128)S(1)}, f32[48,256]{1,0:T(8,128)S(1)}, f32[72,768]{1,0:T(8,128)S(1)}, f32[72,768...) custom-call(s32[2]{0:T(128)S(1)} %pad_add_fusion.place, f32[8,512]{1,0:T(8,128)S(1)} %get-tuple-element.59.own, ...), custom_call_target="tpu_custom_call" | custom-call | flops 5000000000 | bytes 15000000 | tf_op jit(solution)/shard_map/pallas_call | solution.py:594
  29.7 1.7 %collective-permute-start.16 = (f32[72,768]{1,0:T(8,128)S(1)}, f32[72,768]{1,0:T(8,128)S(1)}, u32[]{:S(2)}, u32[]{:S(2)}) collective-permute-start(f32[72,768]{1,0:T(8,128)S(1)} %get-tuple-element.78), channel_id=1, source_target_pairs={{0,2},{1,3},{2,0},{3,1},{4,6},{5,7},{6,4},{7,5},{8,10},{9,11},{10,... | collective-permute-start | bytes 663560 | tf_op jit(solution)/shard_map/ppermute | solution.py:630
  33.1 1.6 %shard_map.143 = (f32[32,768]{1,0:T(8,128)S(1)}, f32[32,768]{1,0:T(8,128)S(1)}, f32[32,768]{1,0:T(8,128)S(1)}, f32[32,768]{1,0:T(8,128)S(1)}, f32[32,768]{1,0:T(...) custom-call(s32[2]{0:T(128)S(1)} %pad_add_fusion.place, ...), custom_call_target="tpu_custom_call" | custom-call | flops 2000000000 | bytes 6000000 | tf_op jit(solution)/shard_map/pallas_call | solution.py:594
  34.8 2.3 %collective-permute-start.10 = (f32[32,768]{1,0:T(8,128)S(1)}, f32[32,768]{1,0:T(8,128)S(1)}, u32[]{:S(2)}, u32[]{:S(2)}) collective-permute-start(f32[32,768]{1,0:T(8,128)S(1)} %get-tuple-element.71), channel_id=1, source_target_pairs={{0,20},{4,16},{8,28},{12,24},{16,4},{20,0},{24,12},{28,8},{1,21},{... | collective-permute-start | bytes 294920 | tf_op jit(solution)/shard_map/ppermute | solution.py:630
  37.1 1.9 %collective-permute-done.16.refs_1_ = f32[72,768]{1,0:T(8,128)S(1)} collective-permute-done((f32[72,768]{1,0:T(8,128)S(1)}, f32[72,768]{1,0:T(8,128)S(1)}, u32[]{:S(2)}, u32[]{:S(2)}) %collective-permute-start.16) | collective-permute-done | bytes 221216 | tf_op jit(solution)/shard_map/ppermute | solution.py:630
  39.1 2.8 %collective-permute-done.17.refs_2_ = f32[72,768]{1,0:T(8,128)S(1)} collective-permute-done((f32[72,768]{1,0:T(8,128)S(1)}, f32[72,768]{1,0:T(8,128)S(1)}, u32[]{:S(2)}, u32[]{:S(2)}) %collective-permute-start.17) | collective-permute-done | bytes 221216 | tf_op jit(solution)/shard_map/ppermute | solution.py:630
  41.9 2.4 %collective-permute-start.12 = (f32[32,768]{1,0:T(8,128)S(1)}, f32[32,768]{1,0:T(8,128)S(1)}, u32[]{:S(2)}, u32[]{:S(2)}) collective-permute-start(f32[32,768]{1,0:T(8,128)S(1)} %get-tuple-element.73), channel_id=1, source_target_pairs={{0,24},{4,28},{8,16},{12,20},{16,8},{20,12},{24,0},{28,4},{1,25},{... | collective-permute-start | bytes 294920 | tf_op jit(solution)/shard_map/ppermute | solution.py:630
  44.3 1.6 %shard_map.145 = (f32[32,768]{1,0:T(8,128)S(1)}, f32[32,768]{1,0:T(8,128)S(1)}, f32[32,768]{1,0:T(8,128)S(1)}, f32[32,768]{1,0:T(8,128)S(1)}, f32[32,768]{1,0:T(...) custom-call(s32[2]{0:T(128)S(1)} %pad_add_fusion.place, ...), custom_call_target="tpu_custom_call" | custom-call | flops 2000000000 | bytes 6000000 | tf_op jit(solution)/shard_map/pallas_call | solution.py:594
  45.9 2.4 %collective-permute-start.14 = (f32[32,768]{1,0:T(8,128)S(1)}, f32[32,768]{1,0:T(8,128)S(1)}, u32[]{:S(2)}, u32[]{:S(2)}) collective-permute-start(f32[32,768]{1,0:T(8,128)S(1)} %get-tuple-element.75), channel_id=1, source_target_pairs={{0,28},{4,24},{8,20},{12,16},{16,12},{20,8},{24,4},{28,0},{1,29},{... | collective-permute-start | bytes 294920 | tf_op jit(solution)/shard_map/ppermute | solution.py:630
  48.3 2.1 %collective-permute-start.15 = (f32[32,768]{1,0:T(8,128)S(1)}, f32[32,768]{1,0:T(8,128)S(1)}, u32[]{:S(2)}, u32[]{:S(2)}) collective-permute-start(f32[32,768]{1,0:T(8,128)S(1)} %get-tuple-element.76), channel_id=1, source_target_pairs={{0,12},{4,8},{8,4},{12,0},{16,28},{20,24},{24,20},{28,16},{1,13},{... | collective-permute-start | bytes 294920 | tf_op jit(solution)/shard_map/ppermute | solution.py:630
  50.4 1.4 collective-permute-start.19
  51.9 1.8 %collective-permute-start.20 = (f32[32,768]{1,0:T(8,128)S(1)}, f32[32,768]{1,0:T(8,128)S(1)}, u32[]{:S(2)}, u32[]{:S(2)}) collective-permute-start(f32[32,768]{1,0:T(8,128)S(1)} %get-tuple-element.83), channel_id=1, source_target_pairs={{0,20},{4,16},{8,28},{12,24},{16,4},{20,0},{24,12},{28,8},{1,21},{... | collective-permute-start | bytes 294920 | tf_op jit(solution)/shard_map/ppermute | solution.py:630
  54.8 3.5 %collective-permute-start.22 = (f32[32,768]{1,0:T(8,128)S(1)}, f32[32,768]{1,0:T(8,128)S(1)}, u32[]{:S(2)}, u32[]{:S(2)}) collective-permute-start(f32[32,768]{1,0:T(8,128)S(1)} %get-tuple-element.85), channel_id=1, source_target_pairs={{0,24},{4,28},{8,16},{12,20},{16,8},{20,12},{24,0},{28,4},{1,25},{... | collective-permute-start | bytes 294920 | tf_op jit(solution)/shard_map/ppermute | solution.py:630
  58.7 7.2 %collective-permute-done.19.refs_1_ = f32[32,768]{1,0:T(8,128)S(1)} collective-permute-done((f32[32,768]{1,0:T(8,128)S(1)}, f32[32,768]{1,0:T(8,128)S(1)}, u32[]{:S(2)}, u32[]{:S(2)}) %collective-permute-start.19) | collective-permute-done | bytes 98336 | tf_op jit(solution)/shard_map/ppermute | solution.py:630
  68.7 1.7 %collective-permute-start.5 = (f32[48,256]{1,0:T(8,128)S(1)}, f32[48,256]{1,0:T(8,128)S(1)}, u32[]{:S(2)}, u32[]{:S(2)}) collective-permute-start(f32[48,256]{1,0:T(8,128)S(1)} %get-tuple-element.64), channel_id=1, source_target_pairs={{0,3},{1,0},{2,1},{3,2},{4,7},{5,4},{6,5},{7,6},{8,11},{9,8},{10,9... | collective-permute-start | bytes 147464 | tf_op jit(solution)/shard_map/ppermute | solution.py:688
  70.4 3.4 %collective-permute-done.24.refs_6_ = f32[32,768]{1,0:T(8,128)S(1)} collective-permute-done((f32[32,768]{1,0:T(8,128)S(1)}, f32[32,768]{1,0:T(8,128)S(1)}, u32[]{:S(2)}, u32[]{:S(2)}) %collective-permute-start.24) | collective-permute-done | bytes 98336 | tf_op jit(solution)/shard_map/ppermute | solution.py:630
  76.1 2.4 %shard_map.147 = (f32[3,2,4,8,8,128]{5,4,3,2,1,0:T(8,128)S(1)}, f32[3,2,4,8,8,128]{5,4,3,2,1,0:T(8,128)S(1)}) custom-call(s32[2]{0:T(128)S(1)} %pad_add_fusion.place, f32[48,256]{1,0:T(8,128)S(1)} %collective-permute-done.4.low_rim, f32[48,256]{1,0:T(8,128)S(1)} %collective-permute-done.5.high_rim, f32[3,2,4,8,8,128]{5,4,3,2,1,0:T(8,128)S(1)} %shard_map.144.refs_0_, ...), custom_call_target="tpu_custom_call" | custom-call | flops 5000000000 | bytes 15000000 | tf_op jit(solution)/shard_map/pallas_call | solution.py:594
  78.5 1.4 shard_map.149
  79.9 1.7 %collective-permute-start.26 = (f32[32,768]{1,0:T(8,128)S(1)}, f32[32,768]{1,0:T(8,128)S(1)}, u32[]{:S(2)}, u32[]{:S(2)}) collective-permute-start(f32[32,768]{1,0:T(8,128)S(1)} %get-tuple-element.93), channel_id=1, source_target_pairs={{0,16},{4,20},{8,24},{12,28},{16,0},{20,4},{24,8},{28,12},{1,17},{... | collective-permute-start | bytes 294920 | tf_op jit(solution)/shard_map/ppermute | solution.py:630
  81.5 2.1 %collective-permute-start.27 = (f32[32,768]{1,0:T(8,128)S(1)}, f32[32,768]{1,0:T(8,128)S(1)}, u32[]{:S(2)}, u32[]{:S(2)}) collective-permute-start(f32[32,768]{1,0:T(8,128)S(1)} %get-tuple-element.94), channel_id=1, source_target_pairs={{0,20},{4,16},{8,28},{12,24},{16,4},{20,0},{24,12},{28,8},{1,21},{... | collective-permute-start | bytes 294920 | tf_op jit(solution)/shard_map/ppermute | solution.py:630
  86.5 6.3 %collective-permute-done.26.refs_1_ = f32[32,768]{1,0:T(8,128)S(1)} collective-permute-done((f32[32,768]{1,0:T(8,128)S(1)}, f32[32,768]{1,0:T(8,128)S(1)}, u32[]{:S(2)}, u32[]{:S(2)}) %collective-permute-start.26) | collective-permute-done | bytes 98336 | tf_op jit(solution)/shard_map/ppermute | solution.py:630
  92.8 1.4 collective-permute-start.31
  94.3 1.5 collective-permute-done.27.refs_2_
  95.7 1.4 shard_map.148
  97.2 3.0 %collective-permute-done.31.refs_6_ = f32[32,768]{1,0:T(8,128)S(1)} collective-permute-done((f32[32,768]{1,0:T(8,128)S(1)}, f32[32,768]{1,0:T(8,128)S(1)}, u32[]{:S(2)}, u32[]{:S(2)}) %collective-permute-start.31) | collective-permute-done | bytes 98336 | tf_op jit(solution)/shard_map/ppermute | solution.py:630
  101.3 2.5 %shard_map.150 = f32[4,72,768]{2,1,0:T(8,128)} custom-call(s32[2]{0:T(128)S(1)} %pad_add_fusion.place, f32[32,768]{1,0:T(8,128)S(1)} %get-tuple-element.90.last_left.refs_0_, bf16[576,256]{1,0:T(8,128)(2,1)S(1)} %copy-done.11, bf16[576,256]{1,0:T(8,128)(2,1)S(1)} %copy-done.9, f32[32,768]{1,0:T(8,128)S(1)} %get-tuple-element.92.refs_0_, ...), custom_call_target="tpu_custom_call" | custom-call | flops 2000000000 | bytes 6000000 | tf_op jit(solution)/shard_map/pallas_call | solution.py:594
  103.8 3.5 %all-to-all-start = ((f32[4,72,768]{2,1,0:T(8,128)}), f32[4,72,768]{2,1,0:T(8,128)S(1)}, u32[]{:S(2)}, u32[]{:S(2)}) async-start(f32[4,72,768]{2,1,0:T(8,128)} %shard_map.150), calls=%async_computation | async-start | bytes 1769472 | tf_op jit(solution)/shard_map/all_to_all | solution.py:626
  108.4 1.9 %collective-permute-start.36 = (f32[32,768]{1,0:T(8,128)S(1)}, f32[32,768]{1,0:T(8,128)S(1)}, u32[]{:S(2)}, u32[]{:S(2)}) collective-permute-start(f32[32,768]{1,0:T(8,128)S(1)} %get-tuple-element.106), channel_id=1, source_target_pairs={{0,20},{4,16},{8,28},{12,24},{16,4},{20,0},{24,12},{28,8},{1,21},{... | collective-permute-start | bytes 294920 | tf_op jit(solution)/shard_map/ppermute | solution.py:630
  110.3 1.5 collective-permute-start.37
  111.8 1.9 %collective-permute-start.38 = (f32[32,768]{1,0:T(8,128)S(1)}, f32[32,768]{1,0:T(8,128)S(1)}, u32[]{:S(2)}, u32[]{:S(2)}) collective-permute-start(f32[32,768]{1,0:T(8,128)S(1)} %get-tuple-element.108), channel_id=1, source_target_pairs={{0,24},{4,28},{8,16},{12,20},{16,8},{20,12},{24,0},{28,4},{1,25},{... | collective-permute-start | bytes 294920 | tf_op jit(solution)/shard_map/ppermute | solution.py:630
  113.7 6.4 %collective-permute-done.35.refs_1_ = f32[32,768]{1,0:T(8,128)S(1)} collective-permute-done((f32[32,768]{1,0:T(8,128)S(1)}, f32[32,768]{1,0:T(8,128)S(1)}, u32[]{:S(2)}, u32[]{:S(2)}) %collective-permute-start.35) | collective-permute-done | bytes 98336 | tf_op jit(solution)/shard_map/ppermute | solution.py:630
  120.1 2.0 %collective-permute-start.40 = (f32[32,768]{1,0:T(8,128)S(1)}, f32[32,768]{1,0:T(8,128)S(1)}, u32[]{:S(2)}, u32[]{:S(2)}) collective-permute-start(f32[32,768]{1,0:T(8,128)S(1)} %get-tuple-element.110), channel_id=1, source_target_pairs={{0,28},{4,24},{8,20},{12,16},{16,12},{20,8},{24,4},{28,0},{1,29},{... | collective-permute-start | bytes 294920 | tf_op jit(solution)/shard_map/ppermute | solution.py:630
  123.7 4.4 %collective-permute-done.40.refs_6_ = f32[32,768]{1,0:T(8,128)S(1)} collective-permute-done((f32[32,768]{1,0:T(8,128)S(1)}, f32[32,768]{1,0:T(8,128)S(1)}, u32[]{:S(2)}, u32[]{:S(2)}) %collective-permute-start.40) | collective-permute-done | bytes 98336 | tf_op jit(solution)/shard_map/ppermute | solution.py:630
  131.2 1.7 %shard_map.152 = (f32[72,768]{1,0:T(8,128)S(1)}, f32[72,768]{1,0:T(8,128)S(1)}, f32[72,768]{1,0:T(8,128)S(1)}, f32[72,768]{1,0:T(8,128)S(1)}) custom-call(s32[2]{0:T(128)S(1)} %pad_add_fusion.place, f32[32,768]{1,0:T(8,128)S(1)} %get-tuple-element.90.last_left.refs_0_, bf16[576,256]{1,0:T(8,128)(2,1)S(1)} %copy-done.12, bf16[576,256]{1,0:T(8,128)(2,1)S(1)} %copy-done.10, ...), custom_call_target="tpu_custom_call" | custom-call | flops 2000000000 | bytes 6000000 | tf_op jit(solution)/shard_map/pallas_call | solution.py:594
  133.6 1.6 %collective-permute-start.42 = (f32[72,768]{1,0:T(8,128)S(1)}, f32[72,768]{1,0:T(8,128)S(1)}, u32[]{:S(2)}, u32[]{:S(2)}) collective-permute-start(f32[72,768]{1,0:T(8,128)S(1)} %get-tuple-element.113), channel_id=1, source_target_pairs={{0,2},{1,3},{2,0},{3,1},{4,6},{5,7},{6,4},{7,5},{8,10},{9,11},{10,... | collective-permute-start | bytes 663560 | tf_op jit(solution)/shard_map/ppermute | solution.py:630
  135.7 1.4 shard_map.151
  137.8 4.1 %collective-permute-start.34 = (f32[3,64,256]{2,1,0:T(8,128)S(1)}, f32[3,64,256]{2,1,0:T(8,128)S(1)}, u32[]{:S(2)}, u32[]{:S(2)}) collective-permute-start(f32[3,64,256]{2,1,0:T(8,128)S(1)} %get-tuple-element.102), channel_id=1, source_target_pairs={{0,28},{4,0},{8,4},{12,8},{16,12},{20,16},{24,20},{28,24},{1,29},{... | collective-permute-start | bytes 589832 | tf_op jit(solution)/shard_map/ppermute | solution.py:742
  141.9 2.3 %collective-permute-done.43.refs_4_ = f32[72,768]{1,0:T(8,128)S(1)} collective-permute-done((f32[72,768]{1,0:T(8,128)S(1)}, f32[72,768]{1,0:T(8,128)S(1)}, u32[]{:S(2)}, u32[]{:S(2)}) %collective-permute-start.43) | collective-permute-done | bytes 221216 | tf_op jit(solution)/shard_map/ppermute | solution.py:630
  144.2 2.6 %collective-permute-done.33.before = f32[3,64,256]{2,1,0:T(8,128)S(1)} collective-permute-done((f32[3,64,256]{2,1,0:T(8,128)S(1)}, f32[3,64,256]{2,1,0:T(8,128)S(1)}, u32[]{:S(2)}, u32[]{:S(2)}) %collective-permute-start.33) | collective-permute-done | bytes 196640 | tf_op jit(solution)/shard_map/ppermute | solution.py:743
  146.8 1.7 %collective-permute-done.34.after = f32[3,64,256]{2,1,0:T(8,128)S(1)} collective-permute-done((f32[3,64,256]{2,1,0:T(8,128)S(1)}, f32[3,64,256]{2,1,0:T(8,128)S(1)}, u32[]{:S(2)}, u32[]{:S(2)}) %collective-permute-start.34) | collective-permute-done | bytes 196640 | tf_op jit(solution)/shard_map/ppermute | solution.py:742
  148.6 3.1 %shard_map.153 = (f32[3,8,64,256]{3,2,1,0:T(8,128)}, f32[3,8,64,256]{3,2,1,0:T(8,128)}) custom-call(s32[2]{0:T(128)S(1)} %pad_add_fusion.place, bf16[512,512]{1,0:T(8,128)(2,1)S(1)} %copy-done.6, bf16[512,512]{1,0:T(8,128)(2,1)S(1)} %copy-done.5, f32[3,4,80,256]{3,2,1,0:T(8,128)S(1)} %get-tuple-element.100.edges, ...), custom_call_target="tpu_custom_call" | custom-call | flops 4000000000 | bytes 12000000 | tf_op jit(solution)/shard_map/pallas_call | solution.py:594
  (101 shorter events, 25.2 us)
Async XLA Ops:
  3.6 10.0 %collective-permute-start.3 = (f32[8,128]{1,0:T(8,128)S(1)}, f32[8,128]{1,0:T(8,128)S(1)}, u32[]{:S(2)}, u32[]{:S(2)}) collective-permute-start(f32[8,128]{1,0:T(8,128)S(1)} %get-tuple-element.60), channel_id=1, source_target_pairs={{0,8},{4,12},{8,16},{12,20},{16,24},{20,28},{24,0},{28,4},{1,9},{5... | collective-permute-start | bytes 12296 | tf_op jit(solution)/shard_map/ppermute | solution.py:667
  6.7 6.9 %collective-permute-start.2 = (f32[8,128]{1,0:T(8,128)S(1)}, f32[8,128]{1,0:T(8,128)S(1)}, u32[]{:S(2)}, u32[]{:S(2)}) collective-permute-start(f32[8,128]{1,0:T(8,128)S(1)} %get-tuple-element.60), channel_id=1, source_target_pairs={{0,24},{4,28},{8,0},{12,4},{16,8},{20,12},{24,16},{28,20},{1,25},{... | collective-permute-start | bytes 12296 | tf_op jit(solution)/shard_map/ppermute | solution.py:666
  8.7 6.4 %collective-permute-start.1 = (f32[8,512]{1,0:T(8,128)S(1)}, f32[8,512]{1,0:T(8,128)S(1)}, u32[]{:S(2)}, u32[]{:S(2)}) collective-permute-start(f32[8,512]{1,0:T(8,128)S(1)} %get-tuple-element.59.own), channel_id=1, source_target_pairs={{0,4},{4,8},{8,12},{12,16},{16,20},{20,24},{24,28},{28,0},{1,5},{5... | collective-permute-start | bytes 49160 | tf_op jit(solution)/shard_map/ppermute | solution.py:665
  10.4 4.8 %collective-permute-start = (f32[8,512]{1,0:T(8,128)S(1)}, f32[8,512]{1,0:T(8,128)S(1)}, u32[]{:S(2)}, u32[]{:S(2)}) collective-permute-start(f32[8,512]{1,0:T(8,128)S(1)} %get-tuple-element.59.own), channel_id=1, source_target_pairs={{0,28},{4,0},{8,4},{12,8},{16,12},{20,16},{24,20},{28,24},{1,29},{... | collective-permute-start | bytes 49160 | tf_op jit(solution)/shard_map/ppermute | solution.py:664
  22.7 8.7 %collective-permute-start.6 = (f32[72,768]{1,0:T(8,128)S(1)}, f32[72,768]{1,0:T(8,128)S(1)}, u32[]{:S(2)}, u32[]{:S(2)}) collective-permute-start(f32[72,768]{1,0:T(8,128)S(1)} %get-tuple-element.66), channel_id=1, source_target_pairs={{0,2},{1,3},{2,0},{3,1},{4,6},{5,7},{6,4},{7,5},{8,10},{9,11},{10,... | collective-permute-start | bytes 663560 | tf_op jit(solution)/shard_map/ppermute | solution.py:630
  24.4 8.7 %collective-permute-start.7 = (f32[72,768]{1,0:T(8,128)S(1)}, f32[72,768]{1,0:T(8,128)S(1)}, u32[]{:S(2)}, u32[]{:S(2)}) collective-permute-start(f32[72,768]{1,0:T(8,128)S(1)} %get-tuple-element.67), channel_id=1, source_target_pairs={{0,3},{1,2},{2,1},{3,0},{4,7},{5,6},{6,5},{7,4},{8,11},{9,10},{10,... | collective-permute-start | bytes 663560 | tf_op jit(solution)/shard_map/ppermute | solution.py:630
  24.4 8.7 %collective-permute-start.8 = (f32[72,768]{1,0:T(8,128)S(1)}, f32[72,768]{1,0:T(8,128)S(1)}, u32[]{:S(2)}, u32[]{:S(2)}) collective-permute-start(f32[72,768]{1,0:T(8,128)S(1)} %get-tuple-element.68), channel_id=1, source_target_pairs={{0,1},{1,0},{2,3},{3,2},{4,5},{5,4},{6,7},{7,6},{8,9},{9,8},{10,11... | collective-permute-start | bytes 663560 | tf_op jit(solution)/shard_map/ppermute | solution.py:630
  29.7 9.3 %collective-permute-start.16 = (f32[72,768]{1,0:T(8,128)S(1)}, f32[72,768]{1,0:T(8,128)S(1)}, u32[]{:S(2)}, u32[]{:S(2)}) collective-permute-start(f32[72,768]{1,0:T(8,128)S(1)} %get-tuple-element.78), channel_id=1, source_target_pairs={{0,2},{1,3},{2,0},{3,1},{4,6},{5,7},{6,4},{7,5},{8,10},{9,11},{10,... | collective-permute-start | bytes 663560 | tf_op jit(solution)/shard_map/ppermute | solution.py:630
  31.4 10.5 %collective-permute-start.17 = (f32[72,768]{1,0:T(8,128)S(1)}, f32[72,768]{1,0:T(8,128)S(1)}, u32[]{:S(2)}, u32[]{:S(2)}) collective-permute-start(f32[72,768]{1,0:T(8,128)S(1)} %get-tuple-element.79), channel_id=1, source_target_pairs={{0,3},{1,2},{2,1},{3,0},{4,7},{5,6},{6,5},{7,4},{8,11},{9,10},{10,... | collective-permute-start | bytes 663560 | tf_op jit(solution)/shard_map/ppermute | solution.py:630
  31.4 12.9 %collective-permute-start.18 = (f32[72,768]{1,0:T(8,128)S(1)}, f32[72,768]{1,0:T(8,128)S(1)}, u32[]{:S(2)}, u32[]{:S(2)}) collective-permute-start(f32[72,768]{1,0:T(8,128)S(1)} %get-tuple-element.80), channel_id=1, source_target_pairs={{0,1},{1,0},{2,3},{3,2},{4,5},{5,4},{6,7},{7,6},{8,9},{9,8},{10,11... | collective-permute-start | bytes 663560 | tf_op jit(solution)/shard_map/ppermute | solution.py:630
  34.7 11.2 %collective-permute-start.9 = (f32[32,768]{1,0:T(8,128)S(1)}, f32[32,768]{1,0:T(8,128)S(1)}, u32[]{:S(2)}, u32[]{:S(2)}) collective-permute-start(f32[32,768]{1,0:T(8,128)S(1)} %get-tuple-element.70), channel_id=1, source_target_pairs={{0,16},{4,20},{8,24},{12,28},{16,0},{20,4},{24,8},{28,12},{1,17},{... | collective-permute-start | bytes 294920 | tf_op jit(solution)/shard_map/ppermute | solution.py:630
  34.8 13.5 %collective-permute-start.10 = (f32[32,768]{1,0:T(8,128)S(1)}, f32[32,768]{1,0:T(8,128)S(1)}, u32[]{:S(2)}, u32[]{:S(2)}) collective-permute-start(f32[32,768]{1,0:T(8,128)S(1)} %get-tuple-element.71), channel_id=1, source_target_pairs={{0,20},{4,16},{8,28},{12,24},{16,4},{20,0},{24,12},{28,8},{1,21},{... | collective-permute-start | bytes 294920 | tf_op jit(solution)/shard_map/ppermute | solution.py:630
  39.0 11.4 %collective-permute-start.11 = (f32[32,768]{1,0:T(8,128)S(1)}, f32[32,768]{1,0:T(8,128)S(1)}, u32[]{:S(2)}, u32[]{:S(2)}) collective-permute-start(f32[32,768]{1,0:T(8,128)S(1)} %get-tuple-element.72), channel_id=1, source_target_pairs={{0,4},{4,0},{8,12},{12,8},{16,20},{20,16},{24,28},{28,24},{1,5},{5... | collective-permute-start | bytes 294920 | tf_op jit(solution)/shard_map/ppermute | solution.py:630
  41.9 10.0 %collective-permute-start.12 = (f32[32,768]{1,0:T(8,128)S(1)}, f32[32,768]{1,0:T(8,128)S(1)}, u32[]{:S(2)}, u32[]{:S(2)}) collective-permute-start(f32[32,768]{1,0:T(8,128)S(1)} %get-tuple-element.73), channel_id=1, source_target_pairs={{0,24},{4,28},{8,16},{12,20},{16,8},{20,12},{24,0},{28,4},{1,25},{... | collective-permute-start | bytes 294920 | tf_op jit(solution)/shard_map/ppermute | solution.py:630
  44.3 9.4 %collective-permute-start.13 = (f32[32,768]{1,0:T(8,128)S(1)}, f32[32,768]{1,0:T(8,128)S(1)}, u32[]{:S(2)}, u32[]{:S(2)}) collective-permute-start(f32[32,768]{1,0:T(8,128)S(1)} %get-tuple-element.74), channel_id=1, source_target_pairs={{0,8},{4,12},{8,0},{12,4},{16,24},{20,28},{24,16},{28,20},{1,9},{5... | collective-permute-start | bytes 294920 | tf_op jit(solution)/shard_map/ppermute | solution.py:630
  45.9 8.9 %collective-permute-start.14 = (f32[32,768]{1,0:T(8,128)S(1)}, f32[32,768]{1,0:T(8,128)S(1)}, u32[]{:S(2)}, u32[]{:S(2)}) collective-permute-start(f32[32,768]{1,0:T(8,128)S(1)} %get-tuple-element.75), channel_id=1, source_target_pairs={{0,28},{4,24},{8,20},{12,16},{16,12},{20,8},{24,4},{28,0},{1,29},{... | collective-permute-start | bytes 294920 | tf_op jit(solution)/shard_map/ppermute | solution.py:630
  48.3 10.1 %collective-permute-start.15 = (f32[32,768]{1,0:T(8,128)S(1)}, f32[32,768]{1,0:T(8,128)S(1)}, u32[]{:S(2)}, u32[]{:S(2)}) collective-permute-start(f32[32,768]{1,0:T(8,128)S(1)} %get-tuple-element.76), channel_id=1, source_target_pairs={{0,12},{4,8},{8,4},{12,0},{16,28},{20,24},{24,20},{28,16},{1,13},{... | collective-permute-start | bytes 294920 | tf_op jit(solution)/shard_map/ppermute | solution.py:630
  50.4 15.6 %collective-permute-start.19 = (f32[32,768]{1,0:T(8,128)S(1)}, f32[32,768]{1,0:T(8,128)S(1)}, u32[]{:S(2)}, u32[]{:S(2)}) collective-permute-start(f32[32,768]{1,0:T(8,128)S(1)} %get-tuple-element.82), channel_id=1, source_target_pairs={{0,16},{4,20},{8,24},{12,28},{16,0},{20,4},{24,8},{28,12},{1,17},{... | collective-permute-start | bytes 294920 | tf_op jit(solution)/shard_map/ppermute | solution.py:630
  51.9 15.4 %collective-permute-start.20 = (f32[32,768]{1,0:T(8,128)S(1)}, f32[32,768]{1,0:T(8,128)S(1)}, u32[]{:S(2)}, u32[]{:S(2)}) collective-permute-start(f32[32,768]{1,0:T(8,128)S(1)} %get-tuple-element.83), channel_id=1, source_target_pairs={{0,20},{4,16},{8,28},{12,24},{16,4},{20,0},{24,12},{28,8},{1,21},{... | collective-permute-start | bytes 294920 | tf_op jit(solution)/shard_map/ppermute | solution.py:630
  53.7 14.9 %collective-permute-start.21 = (f32[32,768]{1,0:T(8,128)S(1)}, f32[32,768]{1,0:T(8,128)S(1)}, u32[]{:S(2)}, u32[]{:S(2)}) collective-permute-start(f32[32,768]{1,0:T(8,128)S(1)} %get-tuple-element.84), channel_id=1, source_target_pairs={{0,4},{4,0},{8,12},{12,8},{16,20},{20,16},{24,28},{28,24},{1,5},{5... | collective-permute-start | bytes 294920 | tf_op jit(solution)/shard_map/ppermute | solution.py:630
  54.8 13.8 %collective-permute-start.22 = (f32[32,768]{1,0:T(8,128)S(1)}, f32[32,768]{1,0:T(8,128)S(1)}, u32[]{:S(2)}, u32[]{:S(2)}) collective-permute-start(f32[32,768]{1,0:T(8,128)S(1)} %get-tuple-element.85), channel_id=1, source_target_pairs={{0,24},{4,28},{8,16},{12,20},{16,8},{20,12},{24,0},{28,4},{1,25},{... | collective-permute-start | bytes 294920 | tf_op jit(solution)/shard_map/ppermute | solution.py:630
  58.4 12.0 %collective-permute-start.23 = (f32[32,768]{1,0:T(8,128)S(1)}, f32[32,768]{1,0:T(8,128)S(1)}, u32[]{:S(2)}, u32[]{:S(2)}) collective-permute-start(f32[32,768]{1,0:T(8,128)S(1)} %get-tuple-element.86), channel_id=1, source_target_pairs={{0,8},{4,12},{8,0},{12,4},{16,24},{20,28},{24,16},{28,20},{1,9},{5... | collective-permute-start | bytes 294920 | tf_op jit(solution)/shard_map/ppermute | solution.py:630
  66.0 7.8 %collective-permute-start.24 = (f32[32,768]{1,0:T(8,128)S(1)}, f32[32,768]{1,0:T(8,128)S(1)}, u32[]{:S(2)}, u32[]{:S(2)}) collective-permute-start(f32[32,768]{1,0:T(8,128)S(1)} %get-tuple-element.87), channel_id=1, source_target_pairs={{0,28},{4,24},{8,20},{12,16},{16,12},{20,8},{24,4},{28,0},{1,29},{... | collective-permute-start | bytes 294920 | tf_op jit(solution)/shard_map/ppermute | solution.py:630
  67.2 7.5 %collective-permute-start.25 = (f32[32,768]{1,0:T(8,128)S(1)}, f32[32,768]{1,0:T(8,128)S(1)}, u32[]{:S(2)}, u32[]{:S(2)}) collective-permute-start(f32[32,768]{1,0:T(8,128)S(1)} %get-tuple-element.88), channel_id=1, source_target_pairs={{0,12},{4,8},{8,4},{12,0},{16,28},{20,24},{24,20},{28,16},{1,13},{... | collective-permute-start | bytes 294920 | tf_op jit(solution)/shard_map/ppermute | solution.py:630
  68.6 7.5 %collective-permute-start.4 = (f32[48,256]{1,0:T(8,128)S(1)}, f32[48,256]{1,0:T(8,128)S(1)}, u32[]{:S(2)}, u32[]{:S(2)}) collective-permute-start(f32[48,256]{1,0:T(8,128)S(1)} %get-tuple-element.63), channel_id=1, source_target_pairs={{0,1},{1,2},{2,3},{3,0},{4,5},{5,6},{6,7},{7,4},{8,9},{9,10},{10,1... | collective-permute-start | bytes 147464 | tf_op jit(solution)/shard_map/ppermute | solution.py:687
  68.7 7.4 %collective-permute-start.5 = (f32[48,256]{1,0:T(8,128)S(1)}, f32[48,256]{1,0:T(8,128)S(1)}, u32[]{:S(2)}, u32[]{:S(2)}) collective-permute-start(f32[48,256]{1,0:T(8,128)S(1)} %get-tuple-element.64), channel_id=1, source_target_pairs={{0,3},{1,0},{2,1},{3,2},{4,7},{5,4},{6,5},{7,6},{8,11},{9,8},{10,9... | collective-permute-start | bytes 147464 | tf_op jit(solution)/shard_map/ppermute | solution.py:688
  79.9 13.0 %collective-permute-start.26 = (f32[32,768]{1,0:T(8,128)S(1)}, f32[32,768]{1,0:T(8,128)S(1)}, u32[]{:S(2)}, u32[]{:S(2)}) collective-permute-start(f32[32,768]{1,0:T(8,128)S(1)} %get-tuple-element.93), channel_id=1, source_target_pairs={{0,16},{4,20},{8,24},{12,28},{16,0},{20,4},{24,8},{28,12},{1,17},{... | collective-permute-start | bytes 294920 | tf_op jit(solution)/shard_map/ppermute | solution.py:630
  81.5 14.2 %collective-permute-start.27 = (f32[32,768]{1,0:T(8,128)S(1)}, f32[32,768]{1,0:T(8,128)S(1)}, u32[]{:S(2)}, u32[]{:S(2)}) collective-permute-start(f32[32,768]{1,0:T(8,128)S(1)} %get-tuple-element.94), channel_id=1, source_target_pairs={{0,20},{4,16},{8,28},{12,24},{16,4},{20,0},{24,12},{28,8},{1,21},{... | collective-permute-start | bytes 294920 | tf_op jit(solution)/shard_map/ppermute | solution.py:630
  83.7 13.5 %collective-permute-start.28 = (f32[32,768]{1,0:T(8,128)S(1)}, f32[32,768]{1,0:T(8,128)S(1)}, u32[]{:S(2)}, u32[]{:S(2)}) collective-permute-start(f32[32,768]{1,0:T(8,128)S(1)} %get-tuple-element.95), channel_id=1, source_target_pairs={{0,4},{4,0},{8,12},{12,8},{16,20},{20,16},{24,28},{28,24},{1,5},{5... | collective-permute-start | bytes 294920 | tf_op jit(solution)/shard_map/ppermute | solution.py:630
  84.3 12.9 %collective-permute-start.29 = (f32[32,768]{1,0:T(8,128)S(1)}, f32[32,768]{1,0:T(8,128)S(1)}, u32[]{:S(2)}, u32[]{:S(2)}) collective-permute-start(f32[32,768]{1,0:T(8,128)S(1)} %get-tuple-element.96), channel_id=1, source_target_pairs={{0,24},{4,28},{8,16},{12,20},{16,8},{20,12},{24,0},{28,4},{1,25},{... | collective-permute-start | bytes 294920 | tf_op jit(solution)/shard_map/ppermute | solution.py:630
  85.2 12.0 %collective-permute-start.30 = (f32[32,768]{1,0:T(8,128)S(1)}, f32[32,768]{1,0:T(8,128)S(1)}, u32[]{:S(2)}, u32[]{:S(2)}) collective-permute-start(f32[32,768]{1,0:T(8,128)S(1)} %get-tuple-element.97), channel_id=1, source_target_pairs={{0,8},{4,12},{8,0},{12,4},{16,24},{20,28},{24,16},{28,20},{1,9},{5... | collective-permute-start | bytes 294920 | tf_op jit(solution)/shard_map/ppermute | solution.py:630
  92.8 7.4 %collective-permute-start.31 = (f32[32,768]{1,0:T(8,128)S(1)}, f32[32,768]{1,0:T(8,128)S(1)}, u32[]{:S(2)}, u32[]{:S(2)}) collective-permute-start(f32[32,768]{1,0:T(8,128)S(1)} %get-tuple-element.98), channel_id=1, source_target_pairs={{0,28},{4,24},{8,20},{12,16},{16,12},{20,8},{24,4},{28,0},{1,29},{... | collective-permute-start | bytes 294920 | tf_op jit(solution)/shard_map/ppermute | solution.py:630
  95.7 5.6 %collective-permute-start.32 = (f32[32,768]{1,0:T(8,128)S(1)}, f32[32,768]{1,0:T(8,128)S(1)}, u32[]{:S(2)}, u32[]{:S(2)}) collective-permute-start(f32[32,768]{1,0:T(8,128)S(1)} %get-tuple-element.99), channel_id=1, source_target_pairs={{0,12},{4,8},{8,4},{12,0},{16,28},{20,24},{24,20},{28,16},{1,13},{... | collective-permute-start | bytes 294920 | tf_op jit(solution)/shard_map/ppermute | solution.py:630
  103.8 31.9 %all-to-all-start = ((f32[4,72,768]{2,1,0:T(8,128)}), f32[4,72,768]{2,1,0:T(8,128)S(1)}, u32[]{:S(2)}, u32[]{:S(2)}) async-start(f32[4,72,768]{2,1,0:T(8,128)} %shard_map.150), calls=%async_computation | async-start | bytes 1769472 | tf_op jit(solution)/shard_map/all_to_all | solution.py:626
  107.3 12.8 %collective-permute-start.35 = (f32[32,768]{1,0:T(8,128)S(1)}, f32[32,768]{1,0:T(8,128)S(1)}, u32[]{:S(2)}, u32[]{:S(2)}) collective-permute-start(f32[32,768]{1,0:T(8,128)S(1)} %get-tuple-element.105), channel_id=1, source_target_pairs={{0,16},{4,20},{8,24},{12,28},{16,0},{20,4},{24,8},{28,12},{1,17},{... | collective-permute-start | bytes 294920 | tf_op jit(solution)/shard_map/ppermute | solution.py:630
  108.4 14.0 %collective-permute-start.36 = (f32[32,768]{1,0:T(8,128)S(1)}, f32[32,768]{1,0:T(8,128)S(1)}, u32[]{:S(2)}, u32[]{:S(2)}) collective-permute-start(f32[32,768]{1,0:T(8,128)S(1)} %get-tuple-element.106), channel_id=1, source_target_pairs={{0,20},{4,16},{8,28},{12,24},{16,4},{20,0},{24,12},{28,8},{1,21},{... | collective-permute-start | bytes 294920 | tf_op jit(solution)/shard_map/ppermute | solution.py:630
  110.3 12.0 %collective-permute-start.37 = (f32[32,768]{1,0:T(8,128)S(1)}, f32[32,768]{1,0:T(8,128)S(1)}, u32[]{:S(2)}, u32[]{:S(2)}) collective-permute-start(f32[32,768]{1,0:T(8,128)S(1)} %get-tuple-element.107), channel_id=1, source_target_pairs={{0,4},{4,0},{8,12},{12,8},{16,20},{20,16},{24,28},{28,24},{1,5},{5... | collective-permute-start | bytes 294920 | tf_op jit(solution)/shard_map/ppermute | solution.py:630
  111.8 10.6 %collective-permute-start.38 = (f32[32,768]{1,0:T(8,128)S(1)}, f32[32,768]{1,0:T(8,128)S(1)}, u32[]{:S(2)}, u32[]{:S(2)}) collective-permute-start(f32[32,768]{1,0:T(8,128)S(1)} %get-tuple-element.108), channel_id=1, source_target_pairs={{0,24},{4,28},{8,16},{12,20},{16,8},{20,12},{24,0},{28,4},{1,25},{... | collective-permute-start | bytes 294920 | tf_op jit(solution)/shard_map/ppermute | solution.py:630
  113.7 10.0 %collective-permute-start.39 = (f32[32,768]{1,0:T(8,128)S(1)}, f32[32,768]{1,0:T(8,128)S(1)}, u32[]{:S(2)}, u32[]{:S(2)}) collective-permute-start(f32[32,768]{1,0:T(8,128)S(1)} %get-tuple-element.109), channel_id=1, source_target_pairs={{0,8},{4,12},{8,0},{12,4},{16,24},{20,28},{24,16},{28,20},{1,9},{5... | collective-permute-start | bytes 294920 | tf_op jit(solution)/shard_map/ppermute | solution.py:630
  120.1 8.0 %collective-permute-start.40 = (f32[32,768]{1,0:T(8,128)S(1)}, f32[32,768]{1,0:T(8,128)S(1)}, u32[]{:S(2)}, u32[]{:S(2)}) collective-permute-start(f32[32,768]{1,0:T(8,128)S(1)} %get-tuple-element.110), channel_id=1, source_target_pairs={{0,28},{4,24},{8,20},{12,16},{16,12},{20,8},{24,4},{28,0},{1,29},{... | collective-permute-start | bytes 294920 | tf_op jit(solution)/shard_map/ppermute | solution.py:630
  122.4 13.3 %copy-start.5 = (bf16[512,512]{1,0:T(8,128)(2,1)S(1)}, bf16[512,512]{1,0:T(8,128)(2,1)}, u32[]{:S(2)}) copy-start(bf16[512,512]{1,0:T(8,128)(2,1)} %constant.32.clone.t_low) | copy-start | bytes 1572868
  122.4 13.3 %copy-start.6 = (bf16[512,512]{1,0:T(8,128)(2,1)S(1)}, bf16[512,512]{1,0:T(8,128)(2,1)}, u32[]{:S(2)}) copy-start(bf16[512,512]{1,0:T(8,128)(2,1)} %constant.31.clone.t_high) | copy-start | bytes 1572868
  122.4 6.9 %collective-permute-start.41 = (f32[32,768]{1,0:T(8,128)S(1)}, f32[32,768]{1,0:T(8,128)S(1)}, u32[]{:S(2)}, u32[]{:S(2)}) collective-permute-start(f32[32,768]{1,0:T(8,128)S(1)} %get-tuple-element.111), channel_id=1, source_target_pairs={{0,12},{4,8},{8,4},{12,0},{16,28},{20,24},{24,20},{28,16},{1,13},{... | collective-permute-start | bytes 294920 | tf_op jit(solution)/shard_map/ppermute | solution.py:630
  133.6 8.4 %collective-permute-start.42 = (f32[72,768]{1,0:T(8,128)S(1)}, f32[72,768]{1,0:T(8,128)S(1)}, u32[]{:S(2)}, u32[]{:S(2)}) collective-permute-start(f32[72,768]{1,0:T(8,128)S(1)} %get-tuple-element.113), channel_id=1, source_target_pairs={{0,2},{1,3},{2,0},{3,1},{4,6},{5,7},{6,4},{7,5},{8,10},{9,11},{10,... | collective-permute-start | bytes 663560 | tf_op jit(solution)/shard_map/ppermute | solution.py:630
  135.2 9.0 %collective-permute-start.43 = (f32[72,768]{1,0:T(8,128)S(1)}, f32[72,768]{1,0:T(8,128)S(1)}, u32[]{:S(2)}, u32[]{:S(2)}) collective-permute-start(f32[72,768]{1,0:T(8,128)S(1)} %get-tuple-element.114), channel_id=1, source_target_pairs={{0,3},{1,2},{2,1},{3,0},{4,7},{5,6},{6,5},{7,4},{8,11},{9,10},{10,... | collective-permute-start | bytes 663560 | tf_op jit(solution)/shard_map/ppermute | solution.py:630
  135.2 9.0 %collective-permute-start.44 = (f32[72,768]{1,0:T(8,128)S(1)}, f32[72,768]{1,0:T(8,128)S(1)}, u32[]{:S(2)}, u32[]{:S(2)}) collective-permute-start(f32[72,768]{1,0:T(8,128)S(1)} %get-tuple-element.115), channel_id=1, source_target_pairs={{0,1},{1,0},{2,3},{3,2},{4,5},{5,4},{6,7},{7,6},{8,9},{9,8},{10,11... | collective-permute-start | bytes 663560 | tf_op jit(solution)/shard_map/ppermute | solution.py:630
  137.1 9.7 %collective-permute-start.33 = (f32[3,64,256]{2,1,0:T(8,128)S(1)}, f32[3,64,256]{2,1,0:T(8,128)S(1)}, u32[]{:S(2)}, u32[]{:S(2)}) collective-permute-start(f32[3,64,256]{2,1,0:T(8,128)S(1)} %get-tuple-element.101), channel_id=1, source_target_pairs={{0,4},{4,8},{8,12},{12,16},{16,20},{20,24},{24,28},{28,0},{1,5},{5... | collective-permute-start | bytes 589832 | tf_op jit(solution)/shard_map/ppermute | solution.py:743
  137.8 10.8 %collective-permute-start.34 = (f32[3,64,256]{2,1,0:T(8,128)S(1)}, f32[3,64,256]{2,1,0:T(8,128)S(1)}, u32[]{:S(2)}, u32[]{:S(2)}) collective-permute-start(f32[3,64,256]{2,1,0:T(8,128)S(1)} %get-tuple-element.102), channel_id=1, source_target_pairs={{0,28},{4,0},{8,4},{12,8},{16,12},{20,16},{24,20},{28,24},{1,29},{... | collective-permute-start | bytes 589832 | tf_op jit(solution)/shard_map/ppermute | solution.py:742
  (19 other events, 108.8 us)

commit v5 on v4

--- a/solution.py
+++ b/solution.py
@@ -177,8 +177,8 @@
 ):
     rims, refs = refs[:rims_before], refs[rims_before:]
     mesh, rim_high, rim_low = refs[:3]
-    total, made = refs[-2:]
-    outs = refs[3:-2]
+    total, made, sems = refs[-3:]
+    outs = refs[3:-3]
     _, planes, cols, ny = ambient.shape
     rows = cols + RIM
     movers = up2.shape[1]
@@ -238,7 +238,8 @@
             block = (values[:, at:to], z_cell[:, at:to], x_cell[:, at:to], y_cell[:, at:to])
             add_block([block], wanted)
 
-    mesh[...] = total[:, :, 0:cols]
+    keep = pltpu.make_async_copy(total.at[:, :, pl.ds(0, cols)], mesh, sems.at[0])
+    keep.start()
     at = 0
     if rims:
         at = rims[0].shape[0]
@@ -260,6 +261,7 @@
             ]
     for d, out in blocks_of(outs, place[1]):
         out[...] = made[d]
+    keep.wait()
 
 
 def x_ahead_kernel(sends, place, t_high, t_low, *refs):
@@ -286,12 +288,12 @@
         out[...] = made[d]
 
 
-def x_back_kernel(sends, place, last_left, t_high, t_low, *refs):
+def x_back_kernel(sends, tables, place, last_left, *refs):
     held, made = refs[-2:]
     outs, parts = refs[-2 - sends : -2], refs[: -2 - sends]
     gather_blocks(parts, held, place[0])
     pencils, rows, width = made.shape
-    both = table_left(t_high[...], t_low[...], held[...].reshape(-1, width))
+    both = table_left(*tables(), held[...].reshape(-1, width))
     half = both.shape[0] // 2
     for n in range(width // LANES):
         lanes = slice(n * LANES, (n + 1) * LANES)
@@ -480,9 +482,8 @@
         curl_all(False)
 
 
-def planes_of(held, pairs, t_high, t_low):
+def planes_of(held, pairs, tables):
     pencils, rows, _ = held.shape
-    ny = t_high.shape[1] // 2
     groups = [(c, pair) for c in range(3) for pair in pairs]
     left = jnp.concatenate(
         [
@@ -493,7 +494,9 @@
         ],
         axis=0,
     )
-    wide = table_right(left, t_high[...], t_low[...])
+    t_high, t_low = tables()
+    ny = t_high.shape[1] // 2
+    wide = table_right(left, t_high, t_low)
     made = {}
     for n, (c, pair) in enumerate(groups):
         for parity in range(2):
@@ -509,12 +512,12 @@
     tall[c, n, 0:RIM] = value[rows - RIM : rows]
 
 
-def edge_kernel(pairs, place, t_high, t_low, *refs):
+def edge_kernel(pairs, tables, place, *refs):
     tall, first, last, held = refs[-4:]
     gather_blocks(refs[:-4], held, place[1])
     listed = [2 * pair + parity for pair in pairs for parity in range(2)]
     cols = first.shape[1]
-    values = planes_of(held, pairs, t_high, t_low)
+    values = planes_of(held, pairs, tables)
     for c in range(3):
         for n, z in enumerate(listed):
             hold(tall, c, n, values[c, z])
@@ -523,10 +526,10 @@
 
 
 def stretch_kernel(
-    chunks, place, t_high, t_low, edges, before, after, low_rim, high_rim, *refs
+    chunks, place, table_high, table_low, edges, before, after, low_rim, high_rim, *refs
 ):
     meshes, refs = refs[:2], refs[2:]
-    velocity, vorticity, held, inner, omega, sems = refs[-6:]
+    velocity, vorticity, held, inner, omega, t_high, t_low, sems = refs[-8:]
     _, planes, cols, ny = velocity.shape
     spot = {}
     for n, chunk in enumerate(chunks):
@@ -534,6 +537,25 @@
             spot[2 * pair], spot[2 * pair + 1] = (n, 2 * i), (n, 2 * i + 1)
     talls = (edges, inner)
     sent = []
+    fetched = {}
+    table_copies = [
+        pltpu.make_async_copy(table_high, t_high, sems.at[3 * planes]),
+        pltpu.make_async_copy(table_low, t_low, sems.at[3 * planes + 1]),
+    ]
+    for copy in table_copies:
+        copy.start()
+
+    def tables():
+        for copy in table_copies:
+            copy.wait()
+        return t_high[...], t_low[...]
+
+    for z in range(planes):
+        n, i = spot[z]
+        fetched[z] = pltpu.make_async_copy(
+            meshes[n].at[:, i], omega.at[:, z], sems.at[2 * planes + z]
+        )
+        fetched[z].start()
 
     def send(source, target):
         sent.append(pltpu.make_async_copy(source, target, sems.at[len(sent)]))
@@ -550,22 +572,22 @@
     for z in range(planes):
         if spot[z][0] == 0:
             send_velocity(z)
-    gather_blocks(refs[:-6], held, place[1])
-    for (c, z), value in planes_of(held, chunks[1], t_high, t_low).items():
+    gather_blocks(refs[:-8], held, place[1])
+    for (c, z), value in planes_of(held, chunks[1], tables).items():
         hold(inner, c, spot[z][1], value)
     for z in range(planes):
         if spot[z][0] == 1:
             send_velocity(z)
     rim_at = 0
-    for which, mesh in enumerate(meshes):
-        size = mesh.shape[1]
+    for which in (1, 0):
+        size = meshes[which].shape[1]
         for z in range(planes):
             n, i = spot[z]
             if n != which:
                 continue
+            fetched[z].wait()
             for c in range(3):
                 at = rim_at + 2 * (c * size + i)
-                omega[c, z] = mesh[c, i]
                 omega[c, z, 0:2] += low_rim[at : at + 2]
                 omega[c, z, cols - 2 : cols] += high_rim[at : at + 2]
             omega_z = [omega[c, z] for c in range(3)]
@@ -587,13 +609,42 @@
 VM = pl.BlockSpec(memory_space=pltpu.VMEM)
 SM = pl.BlockSpec(memory_space=pltpu.SMEM)
 AN = pl.BlockSpec(memory_space=pl.ANY)
+HB = pl.BlockSpec(memory_space=pltpu.HBM)
+
+
+def kept(values):
+    return pltpu.with_memory_space_constraint(values, pltpu.HBM)
+
+
+def copied(kernel, count):
+    def run(place, *refs):
+        tables, refs = refs[:count], refs[count:]
+        scratch, sems = refs[-count - 1 : -1], refs[-1]
+        copies = [
+            pltpu.make_async_copy(source, target, sems.at[n])
+            for n, (source, target) in enumerate(zip(tables, scratch))
+        ]
+        for copy in copies:
+            copy.start()
+
+        def ready():
+            for copy in copies:
+                copy.wait()
+            return [target[...] for target in scratch]
+
+        kernel(ready, place, *refs[: -count - 1])
+
+    return run
 
 
 def call(kernel, ins, outs, scratch=(), sems=0, micros=2.0, moved=None):
     extra = [pltpu.SemaphoreType.DMA((sems,))] if sems else []
     return pl.pallas_call(
         kernel,
-        out_shape=[jax.ShapeDtypeStruct(shape, F32) for _, shape in outs],
+        out_shape=[
+            pltpu.HBM(shape, F32) if spec is HB else jax.ShapeDtypeStruct(shape, F32)
+            for spec, shape in outs
+        ],
         in_specs=[spec for spec, _ in ins],
         out_specs=[spec for spec, _ in outs],
         scratch_shapes=[pltpu.VMEM(shape, kind) for shape, kind in scratch] + extra,
@@ -650,10 +701,10 @@
     packet, movers = call(
         packet_kernel,
         [
-            (AN, migrate_count.reshape(1, 2)),
-            (AN, strength),
-            (AN, offsets),
-            (AN, cell_index.reshape(1, count)),
+            (HB, kept(migrate_count.reshape(1, 2))),
+            (HB, kept(strength)),
+            (HB, kept(offsets)),
+            (HB, kept(cell_index.reshape(1, count))),
         ],
         [(VM, (8, count)), (VM, (8, 2 * MIG))],
         [((1, 2), jnp.int32), ((1, count), jnp.int32)],
@@ -666,8 +717,9 @@
     up2 = lax.ppermute(movers, "gz", ring("gz", -2))
     down2 = lax.ppermute(movers, "gz", ring("gz", 2))
 
-    meshes, rims, parts = [], [], []
-    for chunk, width in zip(chunks, widths):
+    meshes, rims, parts = [None, None], [], [None, None]
+    for n in (1, 0):
+        chunk, width = chunks[n], widths[n]
         size = 2 * len(chunk)
         rim = (6 * size + (rims[0].shape[0] if rims else 0), ny)
         mesh, rim_high, rim_low, *part = call(
@@ -676,20 +728,22 @@
             + [(VM, value) for value in (packet, up1, down1, up2, down2)]
             + [(VM, ambient), (VM, y_ahead[0]), (VM, y_ahead[1])]
             + [(VM, value) for value in rims],
-            [(VM, (3, size, cols, ny)), (VM, rim), (VM, rim)]
+            [(HB, (3, size, cols, ny)), (VM, rim), (VM, rim)]
             + [(VM, shape) for shape in sent_shapes("gx", rows, width)],
             [((3, size, rows, ny), F32), ((pencils, rows, width), F32)],
+            sems=1,
             micros=5.0,
         )
-        meshes.append(mesh)
+        meshes[n] = mesh
         rims = [rim_high, rim_low]
-        parts.append(exchange(part, "gx"))
+        parts[n] = exchange(part, "gx")
     low_rim = lax.ppermute(rims[0], "gx", ring("gx", 1))
     high_rim = lax.ppermute(rims[1], "gx", ring("gx", -1))
 
     tile = max(1, block // 4)
-    data = []
-    for chunk, part, width in zip(chunks, parts, widths):
+    data = [None, None]
+    for n in (1, 0):
+        chunk, part, width = chunks[n], parts[n], widths[n]
         shapes = sent_shapes("gz", block, width)
         part = call(
             functools.partial(x_ahead_kernel, len(shapes)),
@@ -702,7 +756,7 @@
             [here] + [(VM, p) for p in exchange(part, "gz")],
             [(VM, (3, 2, 2 * len(chunk), slabs, tile, LANES))],
         )
-        data.append(entered)
+        data[n] = entered
     data = call(
         functools.partial(curl_kernel, chunks, nx, ny),
         [here, (VM, low_rim), (VM, high_rim)] + [(VM, d) for d in data],
@@ -714,30 +768,37 @@
         call(
             functools.partial(leave_kernel, chunk, nz),
             [here, (VM, source)],
-            [(VM, shape) for shape in sent_shapes("gz", block, width)],
+            [(VM, shape) for shape in sent_shapes("gz", block, width, whole)],
             [(source.shape, F32)],
         )
-        for chunk, source, width in zip(chunks, data, widths)
+        for chunk, source, width, whole in zip(chunks, data, widths, (False, True))
     ]
     parts = []
     for part, width in zip(left, widths):
         part = exchange(part, "gz")
-        shapes = sent_shapes("gx", rows, width, whole=not parts)
+        shapes = sent_shapes("gx", rows, width)
         part = call(
-            functools.partial(x_back_kernel, len(shapes)),
-            [here, (AN, left[-1][0]), (VM, x_back[0]), (VM, x_back[1])] + [(VM, p) for p in part],
+            copied(functools.partial(x_back_kernel, len(shapes)), 2),
+            [here]
+            + [(HB, kept(t)) for t in x_back]
+            + [(AN, left[-1][0])]
+            + [(VM, p) for p in part],
             [(VM, shape) for shape in shapes],
-            [((slabs, block, width), F32), ((pencils, rows, width), F32)],
+            [((slabs, block, width), F32), ((pencils, rows, width), F32)]
+            + [(t.shape, BF16) for t in x_back],
+            sems=2,
         )
         parts.append(exchange(part, "gx"))
     plane = (3, cols, ny)
-    tables = [(VM, y_back[0]), (VM, y_back[1])]
+    tables = [(HB, kept(t)) for t in y_back]
+    near = [(t.shape, BF16) for t in y_back]
     tall = [(3, 2 * len(chunk), cols + 2 * RIM, ny) for chunk in chunks]
     edges, first, last = call(
-        functools.partial(edge_kernel, chunks[0]),
+        copied(functools.partial(edge_kernel, chunks[0]), 2),
         [here] + tables + [(VM, p) for p in parts[0]],
         [(VM, tall[0]), (VM, plane), (VM, plane)],
-        [((pencils, rows, widths[0]), F32)],
+        [((pencils, rows, widths[0]), F32)] + near,
+        sems=2,
     )
     after = lax.ppermute(first, "gz", ring("gz", -1))
     before = lax.ppermute(last, "gz", ring("gz", 1))
@@ -746,15 +807,17 @@
             functools.partial(stretch_kernel, chunks),
             [here]
             + tables
-            + [(VM, v) for v in (edges, before, after, low_rim, high_rim, *meshes)]
+            + [(VM, v) for v in (edges, before, after, low_rim, high_rim)]
+            + [(HB, mesh) for mesh in meshes]
             + [(VM, p) for p in parts[1]],
             [(AN, ambient.shape), (AN, ambient.shape)],
             [
                 ((pencils, rows, widths[1]), F32),
                 (tall[1], F32),
                 ((3, planes, cols, ny), F32),
-            ],
-            sems=2 * planes,
+            ]
+            + near,
+            sems=3 * planes + 2,
             micros=4.0,
         )
     )

time: 152 us -> 155 us (1.020)
  waiting for transfers between devices: 51.2 us -> 59.6 us
  local copies, waits for them, and re-layouts: 7.2 us -> 0.03 us
  Pallas kernels: 30.5 us -> 37.3 us
  starting transfers between devices: 61.8 us -> 56.4 us
    unnamed x42 -> x14, local copies, waits for them, and re-layouts: 7.2 us -> 0.03 us
    pallas_call x14, Pallas kernels: 30.5 us -> 37.3 us  [call(): pl.pallas_call(kernel, out_shape=[pltpu.HBM(shape, F32) if spec is HB els...]
    ppermute x37 -> x33, starting transfers between devices: 41.8 us -> 35.3 us  [exchange(): lax.ppermute(block, axis, [(i, i ^ k) for i in range(count)])]
    ppermute x37 -> x33, waiting for transfers between devices: 45.3 us -> 49.5 us  [exchange(): lax.ppermute(block, axis, [(i, i ^ k) for i in range(count)])]
    ppermute x1, waiting for transfers between devices: 2.57 us -> 6.07 us  [on_device(): before = lax.ppermute(last, 'gz', ring('gz', 1))]
  transfers between devices with their start and end apart: 46 -> 42, of which waited for: 20 -> 16; matrix products, arithmetic and copies ran while one was open for 0% -> 0% of each run, Pallas kernels for 9% -> 14%
where the time goes in v5:
time: 155 us; the launch traced here: 154 us
  waiting for transfers between devices  59.6 us (38%)
  starting transfers between devices  56.4 us (36%)
  Pallas kernels  37.3 us (24%)
    ppermute x33, waiting for transfers between devices, exchange(): lax.ppermute(block, axis, [(i, i ^ k) for i in range(count)])  49.5 us
    pallas_call x14, Pallas kernels, call(): pl.pallas_call(kernel, out_shape=[pltpu.HBM(shape, F32) if spec is HB els...  37.3 us
    ppermute x33, starting transfers between devices, exchange(): lax.ppermute(block, axis, [(i, i ^ k) for i in range(count)])  35.3 us
    ppermute x1, waiting for transfers between devices, on_device(): before = lax.ppermute(last, 'gz', ring('gz', 1))  6.07 us
    all_to_all x1, starting transfers between devices, exchange(): lax.all_to_all(blocks[0], axis, split_axis=0, concat_axis=0, tiled=True)  4.7 us
    ppermute x1, starting transfers between devices, on_device(): after = lax.ppermute(first, 'gz', ring('gz', -1))  3.38 us
  transfers between devices with their start and end apart: 42, of which 16 were waited for; matrix products, arithmetic and copies ran while one was open for 0% of the time, Pallas kernels for 14%

profile of v5, /device:TPU:0, one launch (start us, length us, event | category | flops | bytes accessed | tf_op | source)
XLA Modules:
  0.0 154.5 jit_solution(4422107063652299978)
XLA Ops:
  1.8 3.1 %collective-permute-start.3 = (f32[8,128]{1,0:T(8,128)S(1)}, f32[8,128]{1,0:T(8,128)S(1)}, u32[]{:S(2)}, u32[]{:S(2)}) collective-permute-start(f32[8,128]{1,0:T(8,128)S(1)} %get-tuple-element.56), channel_id=1, source_target_pairs={{0,8},{4,12},{8,16},{12,20},{16,24},{20,28},{24,0},{28,4},{1,9},{5... | collective-permute-start | bytes 12296 | tf_op jit(solution)/shard_map/ppermute | solution.py:718
  4.8 2.1 %collective-permute-start.2 = (f32[8,128]{1,0:T(8,128)S(1)}, f32[8,128]{1,0:T(8,128)S(1)}, u32[]{:S(2)}, u32[]{:S(2)}) collective-permute-start(f32[8,128]{1,0:T(8,128)S(1)} %get-tuple-element.56), channel_id=1, source_target_pairs={{0,24},{4,28},{8,0},{12,4},{16,8},{20,12},{24,16},{28,20},{1,25},{... | collective-permute-start | bytes 12296 | tf_op jit(solution)/shard_map/ppermute | solution.py:717
  6.9 1.6 %collective-permute-start.1 = (f32[8,512]{1,0:T(8,128)S(1)}, f32[8,512]{1,0:T(8,128)S(1)}, u32[]{:S(2)}, u32[]{:S(2)}) collective-permute-start(f32[8,512]{1,0:T(8,128)S(1)} %get-tuple-element.55.own), channel_id=1, source_target_pairs={{0,4},{4,8},{8,12},{12,16},{16,20},{20,24},{24,28},{28,0},{1,5},{5... | collective-permute-start | bytes 49160 | tf_op jit(solution)/shard_map/ppermute | solution.py:716
  8.6 3.1 %collective-permute-start = (f32[8,512]{1,0:T(8,128)S(1)}, f32[8,512]{1,0:T(8,128)S(1)}, u32[]{:S(2)}, u32[]{:S(2)}) collective-permute-start(f32[8,512]{1,0:T(8,128)S(1)} %get-tuple-element.55.own), channel_id=1, source_target_pairs={{0,28},{4,0},{8,4},{12,8},{16,12},{20,16},{24,20},{28,24},{1,29},{... | collective-permute-start | bytes 49160 | tf_op jit(solution)/shard_map/ppermute | solution.py:715
  11.7 1.6 %collective-permute-done.1.down1 = f32[8,512]{1,0:T(8,128)S(1)} collective-permute-done((f32[8,512]{1,0:T(8,128)S(1)}, f32[8,512]{1,0:T(8,128)S(1)}, u32[]{:S(2)}, u32[]{:S(2)}) %collective-permute-start.1) | collective-permute-done | bytes 16416 | tf_op jit(solution)/shard_map/ppermute | solution.py:716
  13.4 4.5 %shard_map.141 = (f32[3,4,64,256]{3,2,1,0:T(8,128)}, f32[24,256]{1,0:T(8,128)S(1)}, f32[24,256]{1,0:T(8,128)S(1)}, f32[72,768]{1,0:T(8,128)S(1)}, f32[72,768]{1,...) custom-call(s32[2]{0:T(128)S(1)} %pad_add_fusion.place, f32[8,512]{1,0:T(8,128)S(1)} %get-tuple-element.55.own, ...), custom_call_target="tpu_custom_call" | custom-call | flops 5000000000 | bytes 15000000 | tf_op jit(solution)/shard_map/pallas_call | solution.py:642
  17.8 1.7 %collective-permute-start.16 = (f32[72,768]{1,0:T(8,128)S(1)}, f32[72,768]{1,0:T(8,128)S(1)}, u32[]{:S(2)}, u32[]{:S(2)}) collective-permute-start(f32[72,768]{1,0:T(8,128)S(1)} %get-tuple-element.74), channel_id=1, source_target_pairs={{0,2},{1,3},{2,0},{3,1},{4,6},{5,7},{6,4},{7,5},{8,10},{9,11},{10,... | collective-permute-start | bytes 663560 | tf_op jit(solution)/shard_map/ppermute | solution.py:681
  20.1 6.9 %shard_map.142 = (f32[3,4,64,256]{3,2,1,0:T(8,128)}, f32[48,256]{1,0:T(8,128)S(1)}, f32[48,256]{1,0:T(8,128)S(1)}, f32[72,768]{1,0:T(8,128)S(1)}, f32[72,768]{1,...) custom-call(s32[2]{0:T(128)S(1)} %pad_add_fusion.place, f32[8,512]{1,0:T(8,128)S(1)} %get-tuple-element.55.own, ...), custom_call_target="tpu_custom_call" | custom-call | flops 5000000000 | bytes 15000000 | tf_op jit(solution)/shard_map/pallas_call | solution.py:642
  26.9 1.7 %collective-permute-start.6 = (f32[72,768]{1,0:T(8,128)S(1)}, f32[72,768]{1,0:T(8,128)S(1)}, u32[]{:S(2)}, u32[]{:S(2)}) collective-permute-start(f32[72,768]{1,0:T(8,128)S(1)} %get-tuple-element.62), channel_id=1, source_target_pairs={{0,2},{1,3},{2,0},{3,1},{4,6},{5,7},{6,4},{7,5},{8,10},{9,11},{10,... | collective-permute-start | bytes 663560 | tf_op jit(solution)/shard_map/ppermute | solution.py:681
  29.1 1.6 %shard_map.145 = (f32[32,768]{1,0:T(8,128)S(1)}, f32[32,768]{1,0:T(8,128)S(1)}, f32[32,768]{1,0:T(8,128)S(1)}, f32[32,768]{1,0:T(8,128)S(1)}, f32[32,768]{1,0:T(...) custom-call(s32[2]{0:T(128)S(1)} %pad_add_fusion.place, ...), custom_call_target="tpu_custom_call" | custom-call | flops 2000000000 | bytes 6000000 | tf_op jit(solution)/shard_map/pallas_call | solution.py:642
  30.8 2.2 %collective-permute-start.20 = (f32[32,768]{1,0:T(8,128)S(1)}, f32[32,768]{1,0:T(8,128)S(1)}, u32[]{:S(2)}, u32[]{:S(2)}) collective-permute-start(f32[32,768]{1,0:T(8,128)S(1)} %get-tuple-element.79), channel_id=1, source_target_pairs={{0,20},{4,16},{8,28},{12,24},{16,4},{20,0},{24,12},{28,8},{1,21},{... | collective-permute-start | bytes 294920 | tf_op jit(solution)/shard_map/ppermute | solution.py:681
  33.0 2.2 %collective-permute-done.6.refs_1_ = f32[72,768]{1,0:T(8,128)S(1)} collective-permute-done((f32[72,768]{1,0:T(8,128)S(1)}, f32[72,768]{1,0:T(8,128)S(1)}, u32[]{:S(2)}, u32[]{:S(2)}) %collective-permute-start.6) | collective-permute-done | bytes 221216 | tf_op jit(solution)/shard_map/ppermute | solution.py:681
  35.3 3.0 %collective-permute-done.7.refs_2_ = f32[72,768]{1,0:T(8,128)S(1)} collective-permute-done((f32[72,768]{1,0:T(8,128)S(1)}, f32[72,768]{1,0:T(8,128)S(1)}, u32[]{:S(2)}, u32[]{:S(2)}) %collective-permute-start.7) | collective-permute-done | bytes 221216 | tf_op jit(solution)/shard_map/ppermute | solution.py:681
  38.3 2.3 %collective-permute-start.22 = (f32[32,768]{1,0:T(8,128)S(1)}, f32[32,768]{1,0:T(8,128)S(1)}, u32[]{:S(2)}, u32[]{:S(2)}) collective-permute-start(f32[32,768]{1,0:T(8,128)S(1)} %get-tuple-element.81), channel_id=1, source_target_pairs={{0,24},{4,28},{8,16},{12,20},{16,8},{20,12},{24,0},{28,4},{1,25},{... | collective-permute-start | bytes 294920 | tf_op jit(solution)/shard_map/ppermute | solution.py:681
  40.6 1.6 %shard_map.143 = (f32[32,768]{1,0:T(8,128)S(1)}, f32[32,768]{1,0:T(8,128)S(1)}, f32[32,768]{1,0:T(8,128)S(1)}, f32[32,768]{1,0:T(8,128)S(1)}, f32[32,768]{1,0:T(...) custom-call(s32[2]{0:T(128)S(1)} %pad_add_fusion.place, ...), custom_call_target="tpu_custom_call" | custom-call | flops 2000000000 | bytes 6000000 | tf_op jit(solution)/shard_map/pallas_call | solution.py:642
  42.2 2.5 %collective-permute-start.24 = (f32[32,768]{1,0:T(8,128)S(1)}, f32[32,768]{1,0:T(8,128)S(1)}, u32[]{:S(2)}, u32[]{:S(2)}) collective-permute-start(f32[32,768]{1,0:T(8,128)S(1)} %get-tuple-element.83), channel_id=1, source_target_pairs={{0,28},{4,24},{8,20},{12,16},{16,12},{20,8},{24,4},{28,0},{1,29},{... | collective-permute-start | bytes 294920 | tf_op jit(solution)/shard_map/ppermute | solution.py:681
  44.7 2.1 %collective-permute-start.25 = (f32[32,768]{1,0:T(8,128)S(1)}, f32[32,768]{1,0:T(8,128)S(1)}, u32[]{:S(2)}, u32[]{:S(2)}) collective-permute-start(f32[32,768]{1,0:T(8,128)S(1)} %get-tuple-element.84), channel_id=1, source_target_pairs={{0,12},{4,8},{8,4},{12,0},{16,28},{20,24},{24,20},{28,16},{1,13},{... | collective-permute-start | bytes 294920 | tf_op jit(solution)/shard_map/ppermute | solution.py:681
  46.8 1.4 collective-permute-start.9
  48.2 1.8 %collective-permute-start.10 = (f32[32,768]{1,0:T(8,128)S(1)}, f32[32,768]{1,0:T(8,128)S(1)}, u32[]{:S(2)}, u32[]{:S(2)}) collective-permute-start(f32[32,768]{1,0:T(8,128)S(1)} %get-tuple-element.67), channel_id=1, source_target_pairs={{0,20},{4,16},{8,28},{12,24},{16,4},{20,0},{24,12},{28,8},{1,21},{... | collective-permute-start | bytes 294920 | tf_op jit(solution)/shard_map/ppermute | solution.py:681
  51.2 3.6 %collective-permute-start.12 = (f32[32,768]{1,0:T(8,128)S(1)}, f32[32,768]{1,0:T(8,128)S(1)}, u32[]{:S(2)}, u32[]{:S(2)}) collective-permute-start(f32[32,768]{1,0:T(8,128)S(1)} %get-tuple-element.69), channel_id=1, source_target_pairs={{0,24},{4,28},{8,16},{12,20},{16,8},{20,12},{24,0},{28,4},{1,25},{... | collective-permute-start | bytes 294920 | tf_op jit(solution)/shard_map/ppermute | solution.py:681
  55.1 7.2 %collective-permute-done.9.refs_1_ = f32[32,768]{1,0:T(8,128)S(1)} collective-permute-done((f32[32,768]{1,0:T(8,128)S(1)}, f32[32,768]{1,0:T(8,128)S(1)}, u32[]{:S(2)}, u32[]{:S(2)}) %collective-permute-start.9) | collective-permute-done | bytes 98336 | tf_op jit(solution)/shard_map/ppermute | solution.py:681
  62.3 1.1 collective-permute-start.14
  63.5 1.4 shard_map.146.refs_1_
  64.9 1.7 %collective-permute-start.5 = (f32[48,256]{1,0:T(8,128)S(1)}, f32[48,256]{1,0:T(8,128)S(1)}, u32[]{:S(2)}, u32[]{:S(2)}) collective-permute-start(f32[48,256]{1,0:T(8,128)S(1)} %get-tuple-element.60), channel_id=1, source_target_pairs={{0,3},{1,0},{2,1},{3,2},{4,7},{5,4},{6,5},{7,6},{8,11},{9,8},{10,9... | collective-permute-start | bytes 147464 | tf_op jit(solution)/shard_map/ppermute | solution.py:741
  67.3 2.8 %collective-permute-done.14.refs_6_ = f32[32,768]{1,0:T(8,128)S(1)} collective-permute-done((f32[32,768]{1,0:T(8,128)S(1)}, f32[32,768]{1,0:T(8,128)S(1)}, u32[]{:S(2)}, u32[]{:S(2)}) %collective-permute-start.14) | collective-permute-done | bytes 98336 | tf_op jit(solution)/shard_map/ppermute | solution.py:681
  70.1 1.3 shard_map.144.refs_0_
  71.4 2.3 %shard_map.147 = (f32[3,2,4,8,8,128]{5,4,3,2,1,0:T(8,128)S(1)}, f32[3,2,4,8,8,128]{5,4,3,2,1,0:T(8,128)S(1)}) custom-call(s32[2]{0:T(128)S(1)} %pad_add_fusion.place, f32[48,256]{1,0:T(8,128)S(1)} %collective-permute-done.4.low_rim, f32[48,256]{1,0:T(8,128)S(1)} %collective-permute-done.5.high_rim, f32[3,2,4,8,8,128]{5,4,3,2,1,0:T(8,128)S(1)} %shard_map.144.refs_0_, ...), custom_call_target="tpu_custom_call" | custom-call | flops 5000000000 | bytes 15000000 | tf_op jit(solution)/shard_map/pallas_call | solution.py:642
  73.7 2.3 %shard_map.148.refs_2_ = f32[8,32,768]{2,1,0:T(8,128)} custom-call(s32[2]{0:T(128)S(1)} %pad_add_fusion.place, f32[3,2,4,8,8,128]{5,4,3,2,1,0:T(8,128)S(1)} %get-tuple-element.85.source), custom_call_target="tpu_custom_call" | custom-call | flops 2000000000 | bytes 6000000 | tf_op jit(solution)/shard_map/pallas_call | solution.py:642
  76.0 4.7 %all-to-all-start = ((f32[8,32,768]{2,1,0:T(8,128)}), f32[8,32,768]{2,1,0:T(8,128)S(1)}, u32[]{:S(2)}, u32[]{:S(2)}) async-start(f32[8,32,768]{2,1,0:T(8,128)} %shard_map.148.refs_2_), calls=%async_computation | async-start | bytes 1572864 | tf_op jit(solution)/shard_map/all_to_all | solution.py:677
  80.7 1.4 shard_map.149
  82.1 3.0 %collective-permute-start.26 = (f32[32,768]{1,0:T(8,128)S(1)}, f32[32,768]{1,0:T(8,128)S(1)}, u32[]{:S(2)}, u32[]{:S(2)}) collective-permute-start(f32[32,768]{1,0:T(8,128)S(1)} %get-tuple-element.88), channel_id=1, source_target_pairs={{0,16},{4,20},{8,24},{12,28},{16,0},{20,4},{24,8},{28,12},{1,17},{... | collective-permute-start | bytes 294920 | tf_op jit(solution)/shard_map/ppermute | solution.py:681
  85.1 1.7 %collective-permute-start.27 = (f32[32,768]{1,0:T(8,128)S(1)}, f32[32,768]{1,0:T(8,128)S(1)}, u32[]{:S(2)}, u32[]{:S(2)}) collective-permute-start(f32[32,768]{1,0:T(8,128)S(1)} %get-tuple-element.89), channel_id=1, source_target_pairs={{0,20},{4,16},{8,28},{12,24},{16,4},{20,0},{24,12},{28,8},{1,21},{... | collective-permute-start | bytes 294920 | tf_op jit(solution)/shard_map/ppermute | solution.py:681
  86.8 3.6 %collective-permute-start.29 = (f32[32,768]{1,0:T(8,128)S(1)}, f32[32,768]{1,0:T(8,128)S(1)}, u32[]{:S(2)}, u32[]{:S(2)}) collective-permute-start(f32[32,768]{1,0:T(8,128)S(1)} %get-tuple-element.91), channel_id=1, source_target_pairs={{0,24},{4,28},{8,16},{12,20},{16,8},{20,12},{24,0},{28,4},{1,25},{... | collective-permute-start | bytes 294920 | tf_op jit(solution)/shard_map/ppermute | solution.py:681
  90.4 20.3 %collective-permute-done.26.refs_4_ = f32[32,768]{1,0:T(8,128)S(1)} collective-permute-done((f32[32,768]{1,0:T(8,128)S(1)}, f32[32,768]{1,0:T(8,128)S(1)}, u32[]{:S(2)}, u32[]{:S(2)}) %collective-permute-start.26) | collective-permute-done | bytes 98336 | tf_op jit(solution)/shard_map/ppermute | solution.py:681
  111.4 2.7 %collective-permute-done.27.refs_5_ = f32[32,768]{1,0:T(8,128)S(1)} collective-permute-done((f32[32,768]{1,0:T(8,128)S(1)}, f32[32,768]{1,0:T(8,128)S(1)}, u32[]{:S(2)}, u32[]{:S(2)}) %collective-permute-start.27) | collective-permute-done | bytes 98336 | tf_op jit(solution)/shard_map/ppermute | solution.py:681
  114.1 4.1 %collective-permute-done.31.refs_9_ = f32[32,768]{1,0:T(8,128)S(1)} collective-permute-done((f32[32,768]{1,0:T(8,128)S(1)}, f32[32,768]{1,0:T(8,128)S(1)}, u32[]{:S(2)}, u32[]{:S(2)}) %collective-permute-start.31) | collective-permute-done | bytes 98336 | tf_op jit(solution)/shard_map/ppermute | solution.py:681
  118.2 1.4 collective-permute-done.32.refs_10_
  119.6 2.7 %shard_map.150 = (f32[72,768]{1,0:T(8,128)S(1)}, f32[72,768]{1,0:T(8,128)S(1)}, f32[72,768]{1,0:T(8,128)S(1)}, f32[72,768]{1,0:T(8,128)S(1)}) custom-call(s32[2]{0:T(128)S(1)} %pad_add_fusion.place, bf16[576,256]{1,0:T(8,128)(2,1)} %constant.29.clone.refs_0_, bf16[576,256]{1,0:T(8,128)(2,1)} %constant.30.clone.refs_1_, f32[8,32,768]{2,1,0:T(8,128)} %shard_map.148.refs_2_, ...), custom_call_target="tpu_custom_call" | custom-call | flops 2000000000 | bytes 6000000 | tf_op jit(solution)/shard_map/pallas_call | solution.py:642
  122.8 1.7 %collective-permute-start.35 = (f32[72,768]{1,0:T(8,128)S(1)}, f32[72,768]{1,0:T(8,128)S(1)}, u32[]{:S(2)}, u32[]{:S(2)}) collective-permute-start(f32[72,768]{1,0:T(8,128)S(1)} %get-tuple-element.98), channel_id=1, source_target_pairs={{0,1},{1,0},{2,3},{3,2},{4,5},{5,4},{6,7},{7,6},{8,9},{9,8},{10,11... | collective-permute-start | bytes 663560 | tf_op jit(solution)/shard_map/ppermute | solution.py:681
  124.5 2.7 %shard_map.152 = (f32[72,768]{1,0:T(8,128)S(1)}, f32[72,768]{1,0:T(8,128)S(1)}, f32[72,768]{1,0:T(8,128)S(1)}, f32[72,768]{1,0:T(8,128)S(1)}) custom-call(s32[2]{0:T(128)S(1)} %pad_add_fusion.place, bf16[576,256]{1,0:T(8,128)(2,1)} %constant.29.clone.refs_0_, bf16[576,256]{1,0:T(8,128)(2,1)} %constant.30.clone.refs_1_, f32[8,32,768]{2,1,0:T(8,128)} %shard_map.148.refs_2_, ...), custom_call_target="tpu_custom_call" | custom-call | flops 2000000000 | bytes 6000000 | tf_op jit(solution)/shard_map/pallas_call | solution.py:642
  128.6 2.0 %collective-permute-done.33.refs_3_ = f32[72,768]{1,0:T(8,128)S(1)} collective-permute-done((f32[72,768]{1,0:T(8,128)S(1)}, f32[72,768]{1,0:T(8,128)S(1)}, u32[]{:S(2)}, u32[]{:S(2)}) %collective-permute-start.33) | collective-permute-done | bytes 221216 | tf_op jit(solution)/shard_map/ppermute | solution.py:681
  130.6 2.8 %collective-permute-done.34.refs_4_ = f32[72,768]{1,0:T(8,128)S(1)} collective-permute-done((f32[72,768]{1,0:T(8,128)S(1)}, f32[72,768]{1,0:T(8,128)S(1)}, u32[]{:S(2)}, u32[]{:S(2)}) %collective-permute-start.34) | collective-permute-done | bytes 221216 | tf_op jit(solution)/shard_map/ppermute | solution.py:681
  133.4 2.6 %shard_map.151 = (f32[3,4,80,256]{3,2,1,0:T(8,128)S(1)}, f32[3,64,256]{2,1,0:T(8,128)S(1)}, f32[3,64,256]{2,1,0:T(8,128)S(1)}) custom-call(s32[2]{0:T(128)S(1)} %pad_add_fusion.place, bf16[512,512]{1,0:T(8,128)(2,1)} %constant.31.clone.refs_0_.table_high, bf16[512,512]{1,0:T(8,128)(2,1)} %constant.32.clone.refs_1_.table_low, ...), custom_call_target="tpu_custom_call" | custom-call | flops 2000000000 | bytes 6000000 | tf_op jit(solution)/shard_map/pallas_call | solution.py:642
  136.0 1.4 collective-permute-start.36
  137.4 3.4 %collective-permute-start.37 = (f32[3,64,256]{2,1,0:T(8,128)S(1)}, f32[3,64,256]{2,1,0:T(8,128)S(1)}, u32[]{:S(2)}, u32[]{:S(2)}) collective-permute-start(f32[3,64,256]{2,1,0:T(8,128)S(1)} %get-tuple-element.101), channel_id=1, source_target_pairs={{0,28},{4,0},{8,4},{12,8},{16,12},{20,16},{24,20},{28,24},{1,29},{... | collective-permute-start | bytes 589832 | tf_op jit(solution)/shard_map/ppermute | solution.py:803
  140.8 6.1 %collective-permute-done.36.before = f32[3,64,256]{2,1,0:T(8,128)S(1)} collective-permute-done((f32[3,64,256]{2,1,0:T(8,128)S(1)}, f32[3,64,256]{2,1,0:T(8,128)S(1)}, u32[]{:S(2)}, u32[]{:S(2)}) %collective-permute-start.36) | collective-permute-done | bytes 196640 | tf_op jit(solution)/shard_map/ppermute | solution.py:804
  146.9 2.4 %collective-permute-done.37.after = f32[3,64,256]{2,1,0:T(8,128)S(1)} collective-permute-done((f32[3,64,256]{2,1,0:T(8,128)S(1)}, f32[3,64,256]{2,1,0:T(8,128)S(1)}, u32[]{:S(2)}, u32[]{:S(2)}) %collective-permute-start.37) | collective-permute-done | bytes 196640 | tf_op jit(solution)/shard_map/ppermute | solution.py:803
  149.3 5.1 %shard_map.153 = (f32[3,8,64,256]{3,2,1,0:T(8,128)}, f32[3,8,64,256]{3,2,1,0:T(8,128)}) custom-call(s32[2]{0:T(128)S(1)} %pad_add_fusion.place, bf16[512,512]{1,0:T(8,128)(2,1)} %constant.31.clone.refs_0_.table_high, bf16[512,512]{1,0:T(8,128)(2,1)} %constant.32.clone.refs_1_.table_low, f32[3,4,80,256]{3,2,1,0:T(8,128)S(1)} %get-tuple-element.99.edges, ...), custom_call_target="tpu_custom_call" | custom-call | flops 4000000000 | bytes 12000000 | tf_op jit(solution)/shard_map/pallas_call | solution.py:642
  (65 shorter events, 7.0 us)
Async XLA Ops:
  0.6 12.7 %copy-start = (f32[3,8,64,256]{3,2,1,0:T(8,128)S(1)}, f32[3,8,64,256]{3,2,1,0:T(8,128)}, u32[]{:S(2)}) copy-start(f32[3,8,64,256]{3,2,1,0:T(8,128)} %ambient.3) | copy-start | bytes 4718596
  0.6 12.7 %copy-start.1 = (bf16[512,512]{1,0:T(8,128)(2,1)S(1)}, bf16[512,512]{1,0:T(8,128)(2,1)}, u32[]{:S(2)}) copy-start(bf16[512,512]{1,0:T(8,128)(2,1)} %constant.26.clone.t_low) | copy-start | bytes 1572868
  0.7 12.7 %copy-start.2 = (bf16[512,512]{1,0:T(8,128)(2,1)S(1)}, bf16[512,512]{1,0:T(8,128)(2,1)}, u32[]{:S(2)}) copy-start(bf16[512,512]{1,0:T(8,128)(2,1)} %constant.25.clone.t_high) | copy-start | bytes 1572868
  1.8 10.0 %collective-permute-start.3 = (f32[8,128]{1,0:T(8,128)S(1)}, f32[8,128]{1,0:T(8,128)S(1)}, u32[]{:S(2)}, u32[]{:S(2)}) collective-permute-start(f32[8,128]{1,0:T(8,128)S(1)} %get-tuple-element.56), channel_id=1, source_target_pairs={{0,8},{4,12},{8,16},{12,20},{16,24},{20,28},{24,0},{28,4},{1,9},{5... | collective-permute-start | bytes 12296 | tf_op jit(solution)/shard_map/ppermute | solution.py:718
  4.8 6.9 %collective-permute-start.2 = (f32[8,128]{1,0:T(8,128)S(1)}, f32[8,128]{1,0:T(8,128)S(1)}, u32[]{:S(2)}, u32[]{:S(2)}) collective-permute-start(f32[8,128]{1,0:T(8,128)S(1)} %get-tuple-element.56), channel_id=1, source_target_pairs={{0,24},{4,28},{8,0},{12,4},{16,8},{20,12},{24,16},{28,20},{1,25},{... | collective-permute-start | bytes 12296 | tf_op jit(solution)/shard_map/ppermute | solution.py:717
  6.9 6.4 %collective-permute-start.1 = (f32[8,512]{1,0:T(8,128)S(1)}, f32[8,512]{1,0:T(8,128)S(1)}, u32[]{:S(2)}, u32[]{:S(2)}) collective-permute-start(f32[8,512]{1,0:T(8,128)S(1)} %get-tuple-element.55.own), channel_id=1, source_target_pairs={{0,4},{4,8},{8,12},{12,16},{16,20},{20,24},{24,28},{28,0},{1,5},{5... | collective-permute-start | bytes 49160 | tf_op jit(solution)/shard_map/ppermute | solution.py:716
  8.6 4.8 %collective-permute-start = (f32[8,512]{1,0:T(8,128)S(1)}, f32[8,512]{1,0:T(8,128)S(1)}, u32[]{:S(2)}, u32[]{:S(2)}) collective-permute-start(f32[8,512]{1,0:T(8,128)S(1)} %get-tuple-element.55.own), channel_id=1, source_target_pairs={{0,28},{4,0},{8,4},{12,8},{16,12},{20,16},{24,20},{28,24},{1,29},{... | collective-permute-start | bytes 49160 | tf_op jit(solution)/shard_map/ppermute | solution.py:715
  17.8 10.8 %collective-permute-start.16 = (f32[72,768]{1,0:T(8,128)S(1)}, f32[72,768]{1,0:T(8,128)S(1)}, u32[]{:S(2)}, u32[]{:S(2)}) collective-permute-start(f32[72,768]{1,0:T(8,128)S(1)} %get-tuple-element.74), channel_id=1, source_target_pairs={{0,2},{1,3},{2,0},{3,1},{4,6},{5,7},{6,4},{7,5},{8,10},{9,11},{10,... | collective-permute-start | bytes 663560 | tf_op jit(solution)/shard_map/ppermute | solution.py:681
  19.6 9.5 %collective-permute-start.17 = (f32[72,768]{1,0:T(8,128)S(1)}, f32[72,768]{1,0:T(8,128)S(1)}, u32[]{:S(2)}, u32[]{:S(2)}) collective-permute-start(f32[72,768]{1,0:T(8,128)S(1)} %get-tuple-element.75), channel_id=1, source_target_pairs={{0,3},{1,2},{2,1},{3,0},{4,7},{5,6},{6,5},{7,4},{8,11},{9,10},{10,... | collective-permute-start | bytes 663560 | tf_op jit(solution)/shard_map/ppermute | solution.py:681
  19.6 9.5 %collective-permute-start.18 = (f32[72,768]{1,0:T(8,128)S(1)}, f32[72,768]{1,0:T(8,128)S(1)}, u32[]{:S(2)}, u32[]{:S(2)}) collective-permute-start(f32[72,768]{1,0:T(8,128)S(1)} %get-tuple-element.76), channel_id=1, source_target_pairs={{0,1},{1,0},{2,3},{3,2},{4,5},{5,4},{6,7},{7,6},{8,9},{9,8},{10,11... | collective-permute-start | bytes 663560 | tf_op jit(solution)/shard_map/ppermute | solution.py:681
  20.1 9.1 %copy-start.4 = (bf16[512,256]{1,0:T(8,128)(2,1)S(1)}, bf16[512,256]{1,0:T(8,128)(2,1)}, u32[]{:S(2)}) copy-start(bf16[512,256]{1,0:T(8,128)(2,1)} %constant.27.clone.t_high) | copy-start | bytes 786436
  26.9 8.3 %collective-permute-start.6 = (f32[72,768]{1,0:T(8,128)S(1)}, f32[72,768]{1,0:T(8,128)S(1)}, u32[]{:S(2)}, u32[]{:S(2)}) collective-permute-start(f32[72,768]{1,0:T(8,128)S(1)} %get-tuple-element.62), channel_id=1, source_target_pairs={{0,2},{1,3},{2,0},{3,1},{4,6},{5,7},{6,4},{7,5},{8,10},{9,11},{10,... | collective-permute-start | bytes 663560 | tf_op jit(solution)/shard_map/ppermute | solution.py:681
  28.7 9.6 %collective-permute-start.7 = (f32[72,768]{1,0:T(8,128)S(1)}, f32[72,768]{1,0:T(8,128)S(1)}, u32[]{:S(2)}, u32[]{:S(2)}) collective-permute-start(f32[72,768]{1,0:T(8,128)S(1)} %get-tuple-element.63), channel_id=1, source_target_pairs={{0,3},{1,2},{2,1},{3,0},{4,7},{5,6},{6,5},{7,4},{8,11},{9,10},{10,... | collective-permute-start | bytes 663560 | tf_op jit(solution)/shard_map/ppermute | solution.py:681
  28.7 11.9 %collective-permute-start.8 = (f32[72,768]{1,0:T(8,128)S(1)}, f32[72,768]{1,0:T(8,128)S(1)}, u32[]{:S(2)}, u32[]{:S(2)}) collective-permute-start(f32[72,768]{1,0:T(8,128)S(1)} %get-tuple-element.64), channel_id=1, source_target_pairs={{0,1},{1,0},{2,3},{3,2},{4,5},{5,4},{6,7},{7,6},{8,9},{9,8},{10,11... | collective-permute-start | bytes 663560 | tf_op jit(solution)/shard_map/ppermute | solution.py:681
  30.8 11.4 %collective-permute-start.19 = (f32[32,768]{1,0:T(8,128)S(1)}, f32[32,768]{1,0:T(8,128)S(1)}, u32[]{:S(2)}, u32[]{:S(2)}) collective-permute-start(f32[32,768]{1,0:T(8,128)S(1)} %get-tuple-element.78), channel_id=1, source_target_pairs={{0,16},{4,20},{8,24},{12,28},{16,0},{20,4},{24,8},{28,12},{1,17},{... | collective-permute-start | bytes 294920 | tf_op jit(solution)/shard_map/ppermute | solution.py:681
  30.8 13.8 %collective-permute-start.20 = (f32[32,768]{1,0:T(8,128)S(1)}, f32[32,768]{1,0:T(8,128)S(1)}, u32[]{:S(2)}, u32[]{:S(2)}) collective-permute-start(f32[32,768]{1,0:T(8,128)S(1)} %get-tuple-element.79), channel_id=1, source_target_pairs={{0,20},{4,16},{8,28},{12,24},{16,4},{20,0},{24,12},{28,8},{1,21},{... | collective-permute-start | bytes 294920 | tf_op jit(solution)/shard_map/ppermute | solution.py:681
  35.3 11.5 %collective-permute-start.21 = (f32[32,768]{1,0:T(8,128)S(1)}, f32[32,768]{1,0:T(8,128)S(1)}, u32[]{:S(2)}, u32[]{:S(2)}) collective-permute-start(f32[32,768]{1,0:T(8,128)S(1)} %get-tuple-element.80), channel_id=1, source_target_pairs={{0,4},{4,0},{8,12},{12,8},{16,20},{20,16},{24,28},{28,24},{1,5},{5... | collective-permute-start | bytes 294920 | tf_op jit(solution)/shard_map/ppermute | solution.py:681
  38.3 10.0 %collective-permute-start.22 = (f32[32,768]{1,0:T(8,128)S(1)}, f32[32,768]{1,0:T(8,128)S(1)}, u32[]{:S(2)}, u32[]{:S(2)}) collective-permute-start(f32[32,768]{1,0:T(8,128)S(1)} %get-tuple-element.81), channel_id=1, source_target_pairs={{0,24},{4,28},{8,16},{12,20},{16,8},{20,12},{24,0},{28,4},{1,25},{... | collective-permute-start | bytes 294920 | tf_op jit(solution)/shard_map/ppermute | solution.py:681
  40.6 9.5 %collective-permute-start.23 = (f32[32,768]{1,0:T(8,128)S(1)}, f32[32,768]{1,0:T(8,128)S(1)}, u32[]{:S(2)}, u32[]{:S(2)}) collective-permute-start(f32[32,768]{1,0:T(8,128)S(1)} %get-tuple-element.82), channel_id=1, source_target_pairs={{0,8},{4,12},{8,0},{12,4},{16,24},{20,28},{24,16},{28,20},{1,9},{5... | collective-permute-start | bytes 294920 | tf_op jit(solution)/shard_map/ppermute | solution.py:681
  42.2 9.0 %collective-permute-start.24 = (f32[32,768]{1,0:T(8,128)S(1)}, f32[32,768]{1,0:T(8,128)S(1)}, u32[]{:S(2)}, u32[]{:S(2)}) collective-permute-start(f32[32,768]{1,0:T(8,128)S(1)} %get-tuple-element.83), channel_id=1, source_target_pairs={{0,28},{4,24},{8,20},{12,16},{16,12},{20,8},{24,4},{28,0},{1,29},{... | collective-permute-start | bytes 294920 | tf_op jit(solution)/shard_map/ppermute | solution.py:681
  44.7 10.4 %collective-permute-start.25 = (f32[32,768]{1,0:T(8,128)S(1)}, f32[32,768]{1,0:T(8,128)S(1)}, u32[]{:S(2)}, u32[]{:S(2)}) collective-permute-start(f32[32,768]{1,0:T(8,128)S(1)} %get-tuple-element.84), channel_id=1, source_target_pairs={{0,12},{4,8},{8,4},{12,0},{16,28},{20,24},{24,20},{28,16},{1,13},{... | collective-permute-start | bytes 294920 | tf_op jit(solution)/shard_map/ppermute | solution.py:681
  46.8 15.6 %collective-permute-start.9 = (f32[32,768]{1,0:T(8,128)S(1)}, f32[32,768]{1,0:T(8,128)S(1)}, u32[]{:S(2)}, u32[]{:S(2)}) collective-permute-start(f32[32,768]{1,0:T(8,128)S(1)} %get-tuple-element.66), channel_id=1, source_target_pairs={{0,16},{4,20},{8,24},{12,28},{16,0},{20,4},{24,8},{28,12},{1,17},{... | collective-permute-start | bytes 294920 | tf_op jit(solution)/shard_map/ppermute | solution.py:681
  48.2 15.3 %collective-permute-start.10 = (f32[32,768]{1,0:T(8,128)S(1)}, f32[32,768]{1,0:T(8,128)S(1)}, u32[]{:S(2)}, u32[]{:S(2)}) collective-permute-start(f32[32,768]{1,0:T(8,128)S(1)} %get-tuple-element.67), channel_id=1, source_target_pairs={{0,20},{4,16},{8,28},{12,24},{16,4},{20,0},{24,12},{28,8},{1,21},{... | collective-permute-start | bytes 294920 | tf_op jit(solution)/shard_map/ppermute | solution.py:681
  50.0 14.8 %collective-permute-start.11 = (f32[32,768]{1,0:T(8,128)S(1)}, f32[32,768]{1,0:T(8,128)S(1)}, u32[]{:S(2)}, u32[]{:S(2)}) collective-permute-start(f32[32,768]{1,0:T(8,128)S(1)} %get-tuple-element.68), channel_id=1, source_target_pairs={{0,4},{4,0},{8,12},{12,8},{16,20},{20,16},{24,28},{28,24},{1,5},{5... | collective-permute-start | bytes 294920 | tf_op jit(solution)/shard_map/ppermute | solution.py:681
  51.2 13.8 %collective-permute-start.12 = (f32[32,768]{1,0:T(8,128)S(1)}, f32[32,768]{1,0:T(8,128)S(1)}, u32[]{:S(2)}, u32[]{:S(2)}) collective-permute-start(f32[32,768]{1,0:T(8,128)S(1)} %get-tuple-element.69), channel_id=1, source_target_pairs={{0,24},{4,28},{8,16},{12,20},{16,8},{20,12},{24,0},{28,4},{1,25},{... | collective-permute-start | bytes 294920 | tf_op jit(solution)/shard_map/ppermute | solution.py:681
  55.1 12.1 %collective-permute-start.13 = (f32[32,768]{1,0:T(8,128)S(1)}, f32[32,768]{1,0:T(8,128)S(1)}, u32[]{:S(2)}, u32[]{:S(2)}) collective-permute-start(f32[32,768]{1,0:T(8,128)S(1)} %get-tuple-element.70), channel_id=1, source_target_pairs={{0,8},{4,12},{8,0},{12,4},{16,24},{20,28},{24,16},{28,20},{1,9},{5... | collective-permute-start | bytes 294920 | tf_op jit(solution)/shard_map/ppermute | solution.py:681
  62.3 7.7 %collective-permute-start.14 = (f32[32,768]{1,0:T(8,128)S(1)}, f32[32,768]{1,0:T(8,128)S(1)}, u32[]{:S(2)}, u32[]{:S(2)}) collective-permute-start(f32[32,768]{1,0:T(8,128)S(1)} %get-tuple-element.71), channel_id=1, source_target_pairs={{0,28},{4,24},{8,20},{12,16},{16,12},{20,8},{24,4},{28,0},{1,29},{... | collective-permute-start | bytes 294920 | tf_op jit(solution)/shard_map/ppermute | solution.py:681
  63.5 6.6 %collective-permute-start.15 = (f32[32,768]{1,0:T(8,128)S(1)}, f32[32,768]{1,0:T(8,128)S(1)}, u32[]{:S(2)}, u32[]{:S(2)}) collective-permute-start(f32[32,768]{1,0:T(8,128)S(1)} %get-tuple-element.72), channel_id=1, source_target_pairs={{0,12},{4,8},{8,4},{12,0},{16,28},{20,24},{24,20},{28,16},{1,13},{... | collective-permute-start | bytes 294920 | tf_op jit(solution)/shard_map/ppermute | solution.py:681
  64.9 6.6 %collective-permute-start.4 = (f32[48,256]{1,0:T(8,128)S(1)}, f32[48,256]{1,0:T(8,128)S(1)}, u32[]{:S(2)}, u32[]{:S(2)}) collective-permute-start(f32[48,256]{1,0:T(8,128)S(1)} %get-tuple-element.59), channel_id=1, source_target_pairs={{0,1},{1,2},{2,3},{3,0},{4,5},{5,6},{6,7},{7,4},{8,9},{9,10},{10,1... | collective-permute-start | bytes 147464 | tf_op jit(solution)/shard_map/ppermute | solution.py:740
  64.9 6.5 %collective-permute-start.5 = (f32[48,256]{1,0:T(8,128)S(1)}, f32[48,256]{1,0:T(8,128)S(1)}, u32[]{:S(2)}, u32[]{:S(2)}) collective-permute-start(f32[48,256]{1,0:T(8,128)S(1)} %get-tuple-element.60), channel_id=1, source_target_pairs={{0,3},{1,0},{2,1},{3,2},{4,7},{5,4},{6,5},{7,6},{8,11},{9,8},{10,9... | collective-permute-start | bytes 147464 | tf_op jit(solution)/shard_map/ppermute | solution.py:741
  76.0 48.4 %all-to-all-start = ((f32[8,32,768]{2,1,0:T(8,128)}), f32[8,32,768]{2,1,0:T(8,128)S(1)}, u32[]{:S(2)}, u32[]{:S(2)}) async-start(f32[8,32,768]{2,1,0:T(8,128)} %shard_map.148.refs_2_), calls=%async_computation | async-start | bytes 1572864 | tf_op jit(solution)/shard_map/all_to_all | solution.py:677
  82.1 28.6 %collective-permute-start.26 = (f32[32,768]{1,0:T(8,128)S(1)}, f32[32,768]{1,0:T(8,128)S(1)}, u32[]{:S(2)}, u32[]{:S(2)}) collective-permute-start(f32[32,768]{1,0:T(8,128)S(1)} %get-tuple-element.88), channel_id=1, source_target_pairs={{0,16},{4,20},{8,24},{12,28},{16,0},{20,4},{24,8},{28,12},{1,17},{... | collective-permute-start | bytes 294920 | tf_op jit(solution)/shard_map/ppermute | solution.py:681
  85.1 28.9 %collective-permute-start.27 = (f32[32,768]{1,0:T(8,128)S(1)}, f32[32,768]{1,0:T(8,128)S(1)}, u32[]{:S(2)}, u32[]{:S(2)}) collective-permute-start(f32[32,768]{1,0:T(8,128)S(1)} %get-tuple-element.89), channel_id=1, source_target_pairs={{0,20},{4,16},{8,28},{12,24},{16,4},{20,0},{24,12},{28,8},{1,21},{... | collective-permute-start | bytes 294920 | tf_op jit(solution)/shard_map/ppermute | solution.py:681
  86.8 27.2 %collective-permute-start.28 = (f32[32,768]{1,0:T(8,128)S(1)}, f32[32,768]{1,0:T(8,128)S(1)}, u32[]{:S(2)}, u32[]{:S(2)}) collective-permute-start(f32[32,768]{1,0:T(8,128)S(1)} %get-tuple-element.90), channel_id=1, source_target_pairs={{0,4},{4,0},{8,12},{12,8},{16,20},{20,16},{24,28},{28,24},{1,5},{5... | collective-permute-start | bytes 294920 | tf_op jit(solution)/shard_map/ppermute | solution.py:681
  86.8 27.2 %collective-permute-start.29 = (f32[32,768]{1,0:T(8,128)S(1)}, f32[32,768]{1,0:T(8,128)S(1)}, u32[]{:S(2)}, u32[]{:S(2)}) collective-permute-start(f32[32,768]{1,0:T(8,128)S(1)} %get-tuple-element.91), channel_id=1, source_target_pairs={{0,24},{4,28},{8,16},{12,20},{16,8},{20,12},{24,0},{28,4},{1,25},{... | collective-permute-start | bytes 294920 | tf_op jit(solution)/shard_map/ppermute | solution.py:681
  90.4 23.6 %collective-permute-start.30 = (f32[32,768]{1,0:T(8,128)S(1)}, f32[32,768]{1,0:T(8,128)S(1)}, u32[]{:S(2)}, u32[]{:S(2)}) collective-permute-start(f32[32,768]{1,0:T(8,128)S(1)} %get-tuple-element.92), channel_id=1, source_target_pairs={{0,8},{4,12},{8,0},{12,4},{16,24},{20,28},{24,16},{28,20},{1,9},{5... | collective-permute-start | bytes 294920 | tf_op jit(solution)/shard_map/ppermute | solution.py:681
  110.8 7.4 %collective-permute-start.31 = (f32[32,768]{1,0:T(8,128)S(1)}, f32[32,768]{1,0:T(8,128)S(1)}, u32[]{:S(2)}, u32[]{:S(2)}) collective-permute-start(f32[32,768]{1,0:T(8,128)S(1)} %get-tuple-element.93), channel_id=1, source_target_pairs={{0,28},{4,24},{8,20},{12,16},{16,12},{20,8},{24,4},{28,0},{1,29},{... | collective-permute-start | bytes 294920 | tf_op jit(solution)/shard_map/ppermute | solution.py:681
  114.0 5.5 %collective-permute-start.32 = (f32[32,768]{1,0:T(8,128)S(1)}, f32[32,768]{1,0:T(8,128)S(1)}, u32[]{:S(2)}, u32[]{:S(2)}) collective-permute-start(f32[32,768]{1,0:T(8,128)S(1)} %get-tuple-element.94), channel_id=1, source_target_pairs={{0,12},{4,8},{8,4},{12,0},{16,28},{20,24},{24,20},{28,16},{1,13},{... | collective-permute-start | bytes 294920 | tf_op jit(solution)/shard_map/ppermute | solution.py:681
  122.2 8.4 %collective-permute-start.33 = (f32[72,768]{1,0:T(8,128)S(1)}, f32[72,768]{1,0:T(8,128)S(1)}, u32[]{:S(2)}, u32[]{:S(2)}) collective-permute-start(f32[72,768]{1,0:T(8,128)S(1)} %get-tuple-element.96), channel_id=1, source_target_pairs={{0,2},{1,3},{2,0},{3,1},{4,6},{5,7},{6,4},{7,5},{8,10},{9,11},{10,... | collective-permute-start | bytes 663560 | tf_op jit(solution)/shard_map/ppermute | solution.py:681
  122.8 10.6 %collective-permute-start.34 = (f32[72,768]{1,0:T(8,128)S(1)}, f32[72,768]{1,0:T(8,128)S(1)}, u32[]{:S(2)}, u32[]{:S(2)}) collective-permute-start(f32[72,768]{1,0:T(8,128)S(1)} %get-tuple-element.97), channel_id=1, source_target_pairs={{0,3},{1,2},{2,1},{3,0},{4,7},{5,6},{6,5},{7,4},{8,11},{9,10},{10,... | collective-permute-start | bytes 663560 | tf_op jit(solution)/shard_map/ppermute | solution.py:681
  122.8 10.6 %collective-permute-start.35 = (f32[72,768]{1,0:T(8,128)S(1)}, f32[72,768]{1,0:T(8,128)S(1)}, u32[]{:S(2)}, u32[]{:S(2)}) collective-permute-start(f32[72,768]{1,0:T(8,128)S(1)} %get-tuple-element.98), channel_id=1, source_target_pairs={{0,1},{1,0},{2,3},{3,2},{4,5},{5,4},{6,7},{7,6},{8,9},{9,8},{10,11... | collective-permute-start | bytes 663560 | tf_op jit(solution)/shard_map/ppermute | solution.py:681
  127.1 22.1 %collective-permute-start.38 = (f32[72,768]{1,0:T(8,128)S(1)}, f32[72,768]{1,0:T(8,128)S(1)}, u32[]{:S(2)}, u32[]{:S(2)}) collective-permute-start(f32[72,768]{1,0:T(8,128)S(1)} %get-tuple-element.105), channel_id=1, source_target_pairs={{0,2},{1,3},{2,0},{3,1},{4,6},{5,7},{6,4},{7,5},{8,10},{9,11},{10,... | collective-permute-start | bytes 663560 | tf_op jit(solution)/shard_map/ppermute | solution.py:681
  127.7 21.6 %collective-permute-start.39 = (f32[72,768]{1,0:T(8,128)S(1)}, f32[72,768]{1,0:T(8,128)S(1)}, u32[]{:S(2)}, u32[]{:S(2)}) collective-permute-start(f32[72,768]{1,0:T(8,128)S(1)} %get-tuple-element.106), channel_id=1, source_target_pairs={{0,3},{1,2},{2,1},{3,0},{4,7},{5,6},{6,5},{7,4},{8,11},{9,10},{10,... | collective-permute-start | bytes 663560 | tf_op jit(solution)/shard_map/ppermute | solution.py:681
  130.6 18.6 %collective-permute-start.40 = (f32[72,768]{1,0:T(8,128)S(1)}, f32[72,768]{1,0:T(8,128)S(1)}, u32[]{:S(2)}, u32[]{:S(2)}) collective-permute-start(f32[72,768]{1,0:T(8,128)S(1)} %get-tuple-element.107), channel_id=1, source_target_pairs={{0,1},{1,0},{2,3},{3,2},{4,5},{5,4},{6,7},{7,6},{8,9},{9,8},{10,11... | collective-permute-start | bytes 663560 | tf_op jit(solution)/shard_map/ppermute | solution.py:681
  133.4 15.9 %copy-start.5 = (f32[3,4,64,256]{3,2,1,0:T(8,128)S(1)}, f32[3,4,64,256]{3,2,1,0:T(8,128)}, u32[]{:S(2)}) copy-start(f32[3,4,64,256]{3,2,1,0:T(8,128)} %get-tuple-element.103.refs_1_) | copy-start | bytes 2359300
  133.4 15.9 %copy-start.6 = (f32[3,4,64,256]{3,2,1,0:T(8,128)S(1)}, f32[3,4,64,256]{3,2,1,0:T(8,128)}, u32[]{:S(2)}) copy-start(f32[3,4,64,256]{3,2,1,0:T(8,128)} %get-tuple-element.102.refs_0_) | copy-start | bytes 2359300
  136.0 10.8 %collective-permute-start.36 = (f32[3,64,256]{2,1,0:T(8,128)S(1)}, f32[3,64,256]{2,1,0:T(8,128)S(1)}, u32[]{:S(2)}, u32[]{:S(2)}) collective-permute-start(f32[3,64,256]{2,1,0:T(8,128)S(1)} %get-tuple-element.100), channel_id=1, source_target_pairs={{0,4},{4,8},{8,12},{12,16},{16,20},{20,24},{24,28},{28,0},{1,5},{5... | collective-permute-start | bytes 589832 | tf_op jit(solution)/shard_map/ppermute | solution.py:804
  137.4 11.8 %collective-permute-start.37 = (f32[3,64,256]{2,1,0:T(8,128)S(1)}, f32[3,64,256]{2,1,0:T(8,128)S(1)}, u32[]{:S(2)}, u32[]{:S(2)}) collective-permute-start(f32[3,64,256]{2,1,0:T(8,128)S(1)} %get-tuple-element.101), channel_id=1, source_target_pairs={{0,28},{4,0},{8,4},{12,8},{16,12},{20,16},{24,20},{28,24},{1,29},{... | collective-permute-start | bytes 589832 | tf_op jit(solution)/shard_map/ppermute | solution.py:803
  (1 other events, 9.1 us)

commit v6 on v4

--- a/solution.py
+++ b/solution.py
@@ -13,6 +13,7 @@
 MIG = 64
 LANES = 128
 RIM = 8
+LATE = 3
 TIME_STEP = 0.25
 VMEM = 24 * 1024 * 1024
 F32 = jnp.float32
@@ -133,7 +134,7 @@
     if count < 4:
         return list(range(count))
     far, near = list(range(count // 2, count)), list(range(1, count // 2))
-    order = [0, far.pop(0)]
+    order = [0]
     while far or near:
         order += far[:1] + near[:1]
         far, near = far[1:], near[1:]
@@ -286,12 +287,12 @@
         out[...] = made[d]
 
 
-def x_back_kernel(sends, place, last_left, t_high, t_low, *refs):
+def x_back_kernel(sends, tables, place, *refs):
     held, made = refs[-2:]
     outs, parts = refs[-2 - sends : -2], refs[: -2 - sends]
     gather_blocks(parts, held, place[0])
     pencils, rows, width = made.shape
-    both = table_left(t_high[...], t_low[...], held[...].reshape(-1, width))
+    both = table_left(tables[0][...], tables[1][...], held[...].reshape(-1, width))
     half = both.shape[0] // 2
     for n in range(width // LANES):
         lanes = slice(n * LANES, (n + 1) * LANES)
@@ -353,6 +354,11 @@
         return carry
 
     lax.fori_loop(0, 3, body, 0)
+
+
+def pass_kernel(before, *refs):
+    for source, target in zip(refs[: len(refs) // 2], refs[len(refs) // 2 :]):
+        target[...] = source[...]
 
 
 def leave_kernel(pairs, nz, place, source, *refs):
@@ -480,9 +486,8 @@
         curl_all(False)
 
 
-def planes_of(held, pairs, t_high, t_low):
+def planes_of(held, pairs, tables):
     pencils, rows, _ = held.shape
-    ny = t_high.shape[1] // 2
     groups = [(c, pair) for c in range(3) for pair in pairs]
     left = jnp.concatenate(
         [
@@ -493,7 +498,8 @@
         ],
         axis=0,
     )
-    wide = table_right(left, t_high[...], t_low[...])
+    ny = tables[0].shape[1] // 2
+    wide = table_right(left, tables[0][...], tables[1][...])
     made = {}
     for n, (c, pair) in enumerate(groups):
         for parity in range(2):
@@ -509,12 +515,12 @@
     tall[c, n, 0:RIM] = value[rows - RIM : rows]
 
 
-def edge_kernel(pairs, place, t_high, t_low, *refs):
+def edge_kernel(pairs, tables, place, *refs):
     tall, first, last, held = refs[-4:]
     gather_blocks(refs[:-4], held, place[1])
     listed = [2 * pair + parity for pair in pairs for parity in range(2)]
     cols = first.shape[1]
-    values = planes_of(held, pairs, t_high, t_low)
+    values = planes_of(held, pairs, tables)
     for c in range(3):
         for n, z in enumerate(listed):
             hold(tall, c, n, values[c, z])
@@ -523,7 +529,7 @@
 
 
 def stretch_kernel(
-    chunks, place, t_high, t_low, edges, before, after, low_rim, high_rim, *refs
+    chunks, tables, place, edges, before, after, low_rim, high_rim, *refs
 ):
     meshes, refs = refs[:2], refs[2:]
     velocity, vorticity, held, inner, omega, sems = refs[-6:]
@@ -551,21 +557,21 @@
         if spot[z][0] == 0:
             send_velocity(z)
     gather_blocks(refs[:-6], held, place[1])
-    for (c, z), value in planes_of(held, chunks[1], t_high, t_low).items():
+    for (c, z), value in planes_of(held, chunks[1], tables).items():
         hold(inner, c, spot[z][1], value)
     for z in range(planes):
         if spot[z][0] == 1:
             send_velocity(z)
     rim_at = 0
-    for which, mesh in enumerate(meshes):
-        size = mesh.shape[1]
+    for which in (1, 0):
+        size = meshes[which].shape[1]
         for z in range(planes):
             n, i = spot[z]
             if n != which:
                 continue
             for c in range(3):
                 at = rim_at + 2 * (c * size + i)
-                omega[c, z] = mesh[c, i]
+                omega[c, z] = meshes[which][c, i]
                 omega[c, z, 0:2] += low_rim[at : at + 2]
                 omega[c, z, cols - 2 : cols] += high_rim[at : at + 2]
             omega_z = [omega[c, z] for c in range(3)]
@@ -587,6 +593,18 @@
 VM = pl.BlockSpec(memory_space=pltpu.VMEM)
 SM = pl.BlockSpec(memory_space=pltpu.SMEM)
 AN = pl.BlockSpec(memory_space=pl.ANY)
+HB = pl.BlockSpec(memory_space=pltpu.HBM)
+
+
+def kept(values):
+    return pltpu.with_memory_space_constraint(values, pltpu.HBM)
+
+
+def loaded(kernel):
+    def run(place, t_high, t_low, *refs):
+        kernel((t_high, t_low), place, *refs)
+
+    return run
 
 
 def call(kernel, ins, outs, scratch=(), sems=0, micros=2.0, moved=None):
@@ -621,14 +639,13 @@
     return [(count, rows, width)] if whole or not spread(axis) else [(rows, width)] * count
 
 
-def exchange(blocks, axis):
-    if len(blocks) == 1:
+def exchange(blocks, axis, start=0):
+    if not spread(axis):
         return [lax.all_to_all(blocks[0], axis, split_axis=0, concat_axis=0, tiled=True)]
     count = lax.axis_size(axis)
-    order = offset_order(count)
-    return [blocks[0]] + [
-        lax.ppermute(block, axis, [(i, i ^ k) for i in range(count)])
-        for k, block in zip(order[1:], blocks[1:])
+    return [
+        lax.ppermute(block, axis, [(i, i ^ k) for i in range(count)]) if k else block
+        for k, block in zip(offset_order(count)[start:], blocks)
     ]
 
 
@@ -650,10 +667,10 @@
     packet, movers = call(
         packet_kernel,
         [
-            (AN, migrate_count.reshape(1, 2)),
-            (AN, strength),
-            (AN, offsets),
-            (AN, cell_index.reshape(1, count)),
+            (HB, kept(migrate_count.reshape(1, 2))),
+            (HB, kept(strength)),
+            (HB, kept(offsets)),
+            (HB, kept(cell_index.reshape(1, count))),
         ],
         [(VM, (8, count)), (VM, (8, 2 * MIG))],
         [((1, 2), jnp.int32), ((1, count), jnp.int32)],
@@ -666,8 +683,9 @@
     up2 = lax.ppermute(movers, "gz", ring("gz", -2))
     down2 = lax.ppermute(movers, "gz", ring("gz", 2))
 
-    meshes, rims, parts = [], [], []
-    for chunk, width in zip(chunks, widths):
+    meshes, rims, parts = [None, None], [], [None, None]
+    for n in (1, 0):
+        chunk, width = chunks[n], widths[n]
         size = 2 * len(chunk)
         rim = (6 * size + (rims[0].shape[0] if rims else 0), ny)
         mesh, rim_high, rim_low, *part = call(
@@ -681,15 +699,16 @@
             [((3, size, rows, ny), F32), ((pencils, rows, width), F32)],
             micros=5.0,
         )
-        meshes.append(mesh)
+        meshes[n] = mesh
         rims = [rim_high, rim_low]
-        parts.append(exchange(part, "gx"))
+        parts[n] = exchange(part, "gx")
     low_rim = lax.ppermute(rims[0], "gx", ring("gx", 1))
     high_rim = lax.ppermute(rims[1], "gx", ring("gx", -1))
 
     tile = max(1, block // 4)
-    data = []
-    for chunk, part, width in zip(chunks, parts, widths):
+    data = [None, None]
+    for n in (1, 0):
+        chunk, part, width = chunks[n], parts[n], widths[n]
         shapes = sent_shapes("gz", block, width)
         part = call(
             functools.partial(x_ahead_kernel, len(shapes)),
@@ -702,7 +721,7 @@
             [here] + [(VM, p) for p in exchange(part, "gz")],
             [(VM, (3, 2, 2 * len(chunk), slabs, tile, LANES))],
         )
-        data.append(entered)
+        data[n] = entered
     data = call(
         functools.partial(curl_kernel, chunks, nx, ny),
         [here, (VM, low_rim), (VM, high_rim)] + [(VM, d) for d in data],
@@ -710,6 +729,9 @@
         [((3, 2, nz, tile, LANES), F32)],
         micros=5.0,
     )
+    plane = (3, cols, ny)
+    tables = [(VM, t) for t in y_back]
+    tall = [(3, 2 * len(chunk), cols + 2 * RIM, ny) for chunk in chunks]
     left = [
         call(
             functools.partial(leave_kernel, chunk, nz),
@@ -719,31 +741,40 @@
         )
         for chunk, source, width in zip(chunks, data, widths)
     ]
-    parts = []
-    for part, width in zip(left, widths):
-        part = exchange(part, "gz")
-        shapes = sent_shapes("gx", rows, width, whole=not parts)
+
+    def back(part, width):
+        shapes = sent_shapes("gx", rows, width)
         part = call(
-            functools.partial(x_back_kernel, len(shapes)),
-            [here, (AN, left[-1][0]), (VM, x_back[0]), (VM, x_back[1])] + [(VM, p) for p in part],
+            loaded(functools.partial(x_back_kernel, len(shapes))),
+            [here] + [(VM, t) for t in x_back] + [(VM, p) for p in part],
             [(VM, shape) for shape in shapes],
             [((slabs, block, width), F32), ((pencils, rows, width), F32)],
         )
-        parts.append(exchange(part, "gx"))
-    plane = (3, cols, ny)
-    tables = [(VM, y_back[0]), (VM, y_back[1])]
-    tall = [(3, 2 * len(chunk), cols + 2 * RIM, ny) for chunk in chunks]
+        return exchange(part, "gx")
+
+    early = max(1, len(left[1]) - LATE)
+    second = exchange(left[1][:early], "gz")
+    parts = [back(exchange(left[0], "gz"), widths[0])]
     edges, first, last = call(
-        functools.partial(edge_kernel, chunks[0]),
+        loaded(functools.partial(edge_kernel, chunks[0])),
         [here] + tables + [(VM, p) for p in parts[0]],
         [(VM, tall[0]), (VM, plane), (VM, plane)],
         [((pencils, rows, widths[0]), F32)],
     )
+    if early < len(left[1]):
+        late = call(
+            pass_kernel,
+            [(AN, parts[0][0])] + [(VM, p) for p in left[1][early:]],
+            [(VM, p.shape) for p in left[1][early:]],
+            micros=0.3,
+        )
+        second += exchange(late, "gz", early)
+    parts.append(back(second, widths[1]))
     after = lax.ppermute(first, "gz", ring("gz", -1))
     before = lax.ppermute(last, "gz", ring("gz", 1))
     return tuple(
         call(
-            functools.partial(stretch_kernel, chunks),
+            loaded(functools.partial(stretch_kernel, chunks)),
             [here]
             + tables
             + [(VM, v) for v in (edges, before, after, low_rim, high_rim, *meshes)]

time: 152 us -> 134 us (0.88)
  waiting for transfers between devices: 51.2 us -> 31.8 us
  starting transfers between devices: 61.8 us -> 69.7 us
  local copies, waits for them, and re-layouts: 7.2 us -> 0.04 us
    ppermute x37 -> x40, waiting for transfers between devices: 45.3 us -> 22.7 us  [exchange(): lax.ppermute(block, axis, [(i, i ^ k) for i in range(count)])]
    ppermute x37 -> x40, starting transfers between devices: 41.8 us -> 53.3 us  [exchange(): lax.ppermute(block, axis, [(i, i ^ k) for i in range(count)])]
    unnamed x42 -> x18, local copies, waits for them, and re-layouts: 7.2 us -> 0.04 us
    ppermute x1, starting transfers between devices: 0.67 us -> 4.48 us  [on_device(): before = lax.ppermute(last, 'gz', ring('gz', 1))]
    ppermute x1, starting transfers between devices: 4.1 us -> 0.29 us  [on_device(): after = lax.ppermute(first, 'gz', ring('gz', -1))]
    all_to_all x1 -> x0, starting transfers between devices: 3.5 us -> none  [exchange(): lax.all_to_all(blocks[0], axis, split_axis=0, concat_axis=0, tiled=True)]
    ppermute x1, waiting for transfers between devices: 2.57 us -> 5.82 us  [on_device(): before = lax.ppermute(last, 'gz', ring('gz', 1))]
    pallas_call x14 -> x15, Pallas kernels: 30.5 us -> 30.7 us  [call(): pl.pallas_call(kernel, out_shape=[jax.ShapeDtypeStruct(shape, F32) for _,...]
  transfers between devices with their start and end apart: 46 -> 48, of which waited for: 20 -> 15; matrix products, arithmetic and copies ran while one was open for 0% -> 0% of each run, Pallas kernels for 9% -> 14%
where the time goes in v6:
time: 134 us; the launch traced here: 133 us
  starting transfers between devices  69.7 us (52%)
  waiting for transfers between devices  31.8 us (24%)
  Pallas kernels  30.7 us (23%)
    ppermute x40, starting transfers between devices, exchange(): lax.ppermute(block, axis, [(i, i ^ k) for i in range(count)])  53.3 us
    pallas_call x15, Pallas kernels, call(): pl.pallas_call(kernel, out_shape=[jax.ShapeDtypeStruct(shape, F32) for _,...  30.7 us
    ppermute x40, waiting for transfers between devices, exchange(): lax.ppermute(block, axis, [(i, i ^ k) for i in range(count)])  22.7 us
    ppermute x1, waiting for transfers between devices, on_device(): before = lax.ppermute(last, 'gz', ring('gz', 1))  5.82 us
    ppermute x1, starting transfers between devices, on_device(): before = lax.ppermute(last, 'gz', ring('gz', 1))  4.48 us
    ppermute x1, starting transfers between devices, on_device(): down2 = lax.ppermute(movers, 'gz', ring('gz', 2))  3.08 us
    ppermute x1, starting transfers between devices, on_device(): up1 = lax.ppermute(packet, 'gz', ring('gz', -1))  3.08 us
  transfers between devices with their start and end apart: 48, of which 15 were waited for; matrix products, arithmetic and copies ran while one was open for 0% of the time, Pallas kernels for 14%

profile of v6, /device:TPU:0, one launch (start us, length us, event | category | flops | bytes accessed | tf_op | source)
XLA Modules:
  0.0 133.4 jit_solution(16296838553984140199)
XLA Ops:
  1.8 3.1 %collective-permute-start.3 = (f32[8,128]{1,0:T(8,128)S(1)}, f32[8,128]{1,0:T(8,128)S(1)}, u32[]{:S(2)}, u32[]{:S(2)}) collective-permute-start(f32[8,128]{1,0:T(8,128)S(1)} %get-tuple-element.67), channel_id=1, source_target_pairs={{0,8},{4,12},{8,16},{12,20},{16,24},{20,28},{24,0},{28,4},{1,9},{5... | collective-permute-start | bytes 12296 | tf_op jit(solution)/shard_map/ppermute | solution.py:684
  4.8 2.1 %collective-permute-start.2 = (f32[8,128]{1,0:T(8,128)S(1)}, f32[8,128]{1,0:T(8,128)S(1)}, u32[]{:S(2)}, u32[]{:S(2)}) collective-permute-start(f32[8,128]{1,0:T(8,128)S(1)} %get-tuple-element.67), channel_id=1, source_target_pairs={{0,24},{4,28},{8,0},{12,4},{16,8},{20,12},{24,16},{28,20},{1,25},{... | collective-permute-start | bytes 12296 | tf_op jit(solution)/shard_map/ppermute | solution.py:683
  6.9 1.6 %collective-permute-start.1 = (f32[8,512]{1,0:T(8,128)S(1)}, f32[8,512]{1,0:T(8,128)S(1)}, u32[]{:S(2)}, u32[]{:S(2)}) collective-permute-start(f32[8,512]{1,0:T(8,128)S(1)} %get-tuple-element.66.own), channel_id=1, source_target_pairs={{0,4},{4,8},{8,12},{12,16},{16,20},{20,24},{24,28},{28,0},{1,5},{5... | collective-permute-start | bytes 49160 | tf_op jit(solution)/shard_map/ppermute | solution.py:682
  8.6 3.1 %collective-permute-start = (f32[8,512]{1,0:T(8,128)S(1)}, f32[8,512]{1,0:T(8,128)S(1)}, u32[]{:S(2)}, u32[]{:S(2)}) collective-permute-start(f32[8,512]{1,0:T(8,128)S(1)} %get-tuple-element.66.own), channel_id=1, source_target_pairs={{0,28},{4,0},{8,4},{12,8},{16,12},{20,16},{24,20},{28,24},{1,29},{... | collective-permute-start | bytes 49160 | tf_op jit(solution)/shard_map/ppermute | solution.py:681
  11.7 1.6 %collective-permute-done.1.down1 = f32[8,512]{1,0:T(8,128)S(1)} collective-permute-done((f32[8,512]{1,0:T(8,128)S(1)}, f32[8,512]{1,0:T(8,128)S(1)}, u32[]{:S(2)}, u32[]{:S(2)}) %collective-permute-start.1) | collective-permute-done | bytes 16416 | tf_op jit(solution)/shard_map/ppermute | solution.py:682
  13.4 3.9 %shard_map.141 = (f32[3,4,64,256]{3,2,1,0:T(8,128)S(1)}, f32[24,256]{1,0:T(8,128)S(1)}, f32[24,256]{1,0:T(8,128)S(1)}, f32[72,768]{1,0:T(8,128)S(1)}, f32[72,768...) custom-call(s32[2]{0:T(128)S(1)} %pad_add_fusion.place, f32[8,512]{1,0:T(8,128)S(1)} %get-tuple-element.66.own, ...), custom_call_target="tpu_custom_call" | custom-call | flops 5000000000 | bytes 15000000 | tf_op jit(solution)/shard_map/pallas_call | solution.py:612
  17.3 1.7 %collective-permute-start.16 = (f32[72,768]{1,0:T(8,128)S(1)}, f32[72,768]{1,0:T(8,128)S(1)}, u32[]{:S(2)}, u32[]{:S(2)}) collective-permute-start(f32[72,768]{1,0:T(8,128)S(1)} %get-tuple-element.85), channel_id=1, source_target_pairs={{0,2},{1,3},{2,0},{3,1},{4,6},{5,7},{6,4},{7,5},{8,10},{9,11},{10,... | collective-permute-start | bytes 663560 | tf_op jit(solution)/shard_map/ppermute | solution.py:647
  19.5 6.6 %shard_map.142 = (f32[3,4,64,256]{3,2,1,0:T(8,128)S(1)}, f32[48,256]{1,0:T(8,128)S(1)}, f32[48,256]{1,0:T(8,128)S(1)}, f32[72,768]{1,0:T(8,128)S(1)}, f32[72,768...) custom-call(s32[2]{0:T(128)S(1)} %pad_add_fusion.place, f32[8,512]{1,0:T(8,128)S(1)} %get-tuple-element.66.own, ...), custom_call_target="tpu_custom_call" | custom-call | flops 5000000000 | bytes 15000000 | tf_op jit(solution)/shard_map/pallas_call | solution.py:612
  26.1 1.7 %collective-permute-start.6 = (f32[72,768]{1,0:T(8,128)S(1)}, f32[72,768]{1,0:T(8,128)S(1)}, u32[]{:S(2)}, u32[]{:S(2)}) collective-permute-start(f32[72,768]{1,0:T(8,128)S(1)} %get-tuple-element.73), channel_id=1, source_target_pairs={{0,2},{1,3},{2,0},{3,1},{4,6},{5,7},{6,4},{7,5},{8,10},{9,11},{10,... | collective-permute-start | bytes 663560 | tf_op jit(solution)/shard_map/ppermute | solution.py:647
  28.4 1.6 %shard_map.145 = (f32[32,768]{1,0:T(8,128)S(1)}, f32[32,768]{1,0:T(8,128)S(1)}, f32[32,768]{1,0:T(8,128)S(1)}, f32[32,768]{1,0:T(8,128)S(1)}, f32[32,768]{1,0:T(...) custom-call(s32[2]{0:T(128)S(1)} %pad_add_fusion.place, ...), custom_call_target="tpu_custom_call" | custom-call | flops 2000000000 | bytes 6000000 | tf_op jit(solution)/shard_map/pallas_call | solution.py:612
  30.1 2.2 %collective-permute-start.20 = (f32[32,768]{1,0:T(8,128)S(1)}, f32[32,768]{1,0:T(8,128)S(1)}, u32[]{:S(2)}, u32[]{:S(2)}) collective-permute-start(f32[32,768]{1,0:T(8,128)S(1)} %get-tuple-element.90), channel_id=1, source_target_pairs={{0,4},{4,0},{8,12},{12,8},{16,20},{20,16},{24,28},{28,24},{1,5},{5... | collective-permute-start | bytes 294920 | tf_op jit(solution)/shard_map/ppermute | solution.py:647
  32.2 2.3 %collective-permute-done.6.refs_1_ = f32[72,768]{1,0:T(8,128)S(1)} collective-permute-done((f32[72,768]{1,0:T(8,128)S(1)}, f32[72,768]{1,0:T(8,128)S(1)}, u32[]{:S(2)}, u32[]{:S(2)}) %collective-permute-start.6) | collective-permute-done | bytes 221216 | tf_op jit(solution)/shard_map/ppermute | solution.py:647
  34.5 1.6 %collective-permute-start.21 = (f32[32,768]{1,0:T(8,128)S(1)}, f32[32,768]{1,0:T(8,128)S(1)}, u32[]{:S(2)}, u32[]{:S(2)}) collective-permute-start(f32[32,768]{1,0:T(8,128)S(1)} %get-tuple-element.91), channel_id=1, source_target_pairs={{0,20},{4,16},{8,28},{12,24},{16,4},{20,0},{24,12},{28,8},{1,21},{... | collective-permute-start | bytes 294920 | tf_op jit(solution)/shard_map/ppermute | solution.py:647
  36.1 3.7 %collective-permute-start.22 = (f32[32,768]{1,0:T(8,128)S(1)}, f32[32,768]{1,0:T(8,128)S(1)}, u32[]{:S(2)}, u32[]{:S(2)}) collective-permute-start(f32[32,768]{1,0:T(8,128)S(1)} %get-tuple-element.92), channel_id=1, source_target_pairs={{0,8},{4,12},{8,0},{12,4},{16,24},{20,28},{24,16},{28,20},{1,9},{5... | collective-permute-start | bytes 294920 | tf_op jit(solution)/shard_map/ppermute | solution.py:647
  39.8 1.6 %shard_map.143 = (f32[32,768]{1,0:T(8,128)S(1)}, f32[32,768]{1,0:T(8,128)S(1)}, f32[32,768]{1,0:T(8,128)S(1)}, f32[32,768]{1,0:T(8,128)S(1)}, f32[32,768]{1,0:T(...) custom-call(s32[2]{0:T(128)S(1)} %pad_add_fusion.place, ...), custom_call_target="tpu_custom_call" | custom-call | flops 2000000000 | bytes 6000000 | tf_op jit(solution)/shard_map/pallas_call | solution.py:612
  42.0 3.3 %collective-permute-start.25 = (f32[32,768]{1,0:T(8,128)S(1)}, f32[32,768]{1,0:T(8,128)S(1)}, u32[]{:S(2)}, u32[]{:S(2)}) collective-permute-start(f32[32,768]{1,0:T(8,128)S(1)} %get-tuple-element.95), channel_id=1, source_target_pairs={{0,28},{4,24},{8,20},{12,16},{16,12},{20,8},{24,4},{28,0},{1,29},{... | collective-permute-start | bytes 294920 | tf_op jit(solution)/shard_map/ppermute | solution.py:647
  45.9 3.0 %collective-permute-start.10 = (f32[32,768]{1,0:T(8,128)S(1)}, f32[32,768]{1,0:T(8,128)S(1)}, u32[]{:S(2)}, u32[]{:S(2)}) collective-permute-start(f32[32,768]{1,0:T(8,128)S(1)} %get-tuple-element.78), channel_id=1, source_target_pairs={{0,4},{4,0},{8,12},{12,8},{16,20},{20,16},{24,28},{28,24},{1,5},{5... | collective-permute-start | bytes 294920 | tf_op jit(solution)/shard_map/ppermute | solution.py:647
  49.8 2.0 %collective-permute-start.12 = (f32[32,768]{1,0:T(8,128)S(1)}, f32[32,768]{1,0:T(8,128)S(1)}, u32[]{:S(2)}, u32[]{:S(2)}) collective-permute-start(f32[32,768]{1,0:T(8,128)S(1)} %get-tuple-element.80), channel_id=1, source_target_pairs={{0,8},{4,12},{8,0},{12,4},{16,24},{20,28},{24,16},{28,20},{1,9},{5... | collective-permute-start | bytes 294920 | tf_op jit(solution)/shard_map/ppermute | solution.py:647
  51.7 2.2 %collective-permute-start.13 = (f32[32,768]{1,0:T(8,128)S(1)}, f32[32,768]{1,0:T(8,128)S(1)}, u32[]{:S(2)}, u32[]{:S(2)}) collective-permute-start(f32[32,768]{1,0:T(8,128)S(1)} %get-tuple-element.81), channel_id=1, source_target_pairs={{0,24},{4,28},{8,16},{12,20},{16,8},{20,12},{24,0},{28,4},{1,25},{... | collective-permute-start | bytes 294920 | tf_op jit(solution)/shard_map/ppermute | solution.py:647
  54.0 6.1 %collective-permute-done.9.refs_1_ = f32[32,768]{1,0:T(8,128)S(1)} collective-permute-done((f32[32,768]{1,0:T(8,128)S(1)}, f32[32,768]{1,0:T(8,128)S(1)}, u32[]{:S(2)}, u32[]{:S(2)}) %collective-permute-start.9) | collective-permute-done | bytes 98336 | tf_op jit(solution)/shard_map/ppermute | solution.py:647
  60.0 2.5 %collective-permute-start.15 = (f32[32,768]{1,0:T(8,128)S(1)}, f32[32,768]{1,0:T(8,128)S(1)}, u32[]{:S(2)}, u32[]{:S(2)}) collective-permute-start(f32[32,768]{1,0:T(8,128)S(1)} %get-tuple-element.83), channel_id=1, source_target_pairs={{0,28},{4,24},{8,20},{12,16},{16,12},{20,8},{24,4},{28,0},{1,29},{... | collective-permute-start | bytes 294920 | tf_op jit(solution)/shard_map/ppermute | solution.py:647
  64.0 1.7 %collective-permute-start.5 = (f32[48,256]{1,0:T(8,128)S(1)}, f32[48,256]{1,0:T(8,128)S(1)}, u32[]{:S(2)}, u32[]{:S(2)}) collective-permute-start(f32[48,256]{1,0:T(8,128)S(1)} %get-tuple-element.71), channel_id=1, source_target_pairs={{0,3},{1,0},{2,1},{3,2},{4,7},{5,4},{6,5},{7,6},{8,11},{9,8},{10,9... | collective-permute-start | bytes 147464 | tf_op jit(solution)/shard_map/ppermute | solution.py:706
  65.7 1.9 %collective-permute-done.14.refs_6_ = f32[32,768]{1,0:T(8,128)S(1)} collective-permute-done((f32[32,768]{1,0:T(8,128)S(1)}, f32[32,768]{1,0:T(8,128)S(1)}, u32[]{:S(2)}, u32[]{:S(2)}) %collective-permute-start.14) | collective-permute-done | bytes 98336 | tf_op jit(solution)/shard_map/ppermute | solution.py:647
  69.0 2.3 %shard_map.147 = (f32[3,2,4,8,8,128]{5,4,3,2,1,0:T(8,128)S(1)}, f32[3,2,4,8,8,128]{5,4,3,2,1,0:T(8,128)S(1)}) custom-call(s32[2]{0:T(128)S(1)} %pad_add_fusion.place, f32[48,256]{1,0:T(8,128)S(1)} %collective-permute-done.4.low_rim.refs_3_, f32[48,256]{1,0:T(8,128)S(1)} %collective-permute-done.5.high_rim.refs_4_, ...), custom_call_target="tpu_custom_call" | custom-call | flops 5000000000 | bytes 15000000 | tf_op jit(solution)/shard_map/pallas_call | solution.py:612
  71.3 1.4 %shard_map.148 = (f32[32,768]{1,0:T(8,128)S(1)}, f32[32,768]{1,0:T(8,128)S(1)}, f32[32,768]{1,0:T(8,128)S(1)}, f32[32,768]{1,0:T(8,128)S(1)}, f32[32,768]{1,0:T(...) custom-call(s32[2]{0:T(128)S(1)} %pad_add_fusion.place, ...), custom_call_target="tpu_custom_call" | custom-call | flops 2000000000 | bytes 6000000 | tf_op jit(solution)/shard_map/pallas_call | solution.py:612
  72.7 2.2 %collective-permute-start.26 = (f32[32,768]{1,0:T(8,128)S(1)}, f32[32,768]{1,0:T(8,128)S(1)}, u32[]{:S(2)}, u32[]{:S(2)}) collective-permute-start(f32[32,768]{1,0:T(8,128)S(1)} %get-tuple-element.98), channel_id=1, source_target_pairs={{0,16},{4,20},{8,24},{12,28},{16,0},{20,4},{24,8},{28,12},{1,17},{... | collective-permute-start | bytes 294920 | tf_op jit(solution)/shard_map/ppermute | solution.py:647
  77.2 2.0 %collective-permute-start.29 = (f32[32,768]{1,0:T(8,128)S(1)}, f32[32,768]{1,0:T(8,128)S(1)}, u32[]{:S(2)}, u32[]{:S(2)}) collective-permute-start(f32[32,768]{1,0:T(8,128)S(1)} %get-tuple-element.101), channel_id=1, source_target_pairs={{0,8},{4,12},{8,0},{12,4},{16,24},{20,28},{24,16},{28,20},{1,9},{5... | collective-permute-start | bytes 294920 | tf_op jit(solution)/shard_map/ppermute | solution.py:647
  79.1 1.6 %collective-permute-start.30 = (f32[32,768]{1,0:T(8,128)S(1)}, f32[32,768]{1,0:T(8,128)S(1)}, u32[]{:S(2)}, u32[]{:S(2)}) collective-permute-start(f32[32,768]{1,0:T(8,128)S(1)} %get-tuple-element.102), channel_id=1, source_target_pairs={{0,24},{4,28},{8,16},{12,20},{16,8},{20,12},{24,0},{28,4},{1,25},{... | collective-permute-start | bytes 294920 | tf_op jit(solution)/shard_map/ppermute | solution.py:647
  80.7 1.4 %collective-permute-done.26.refs_1_ = f32[32,768]{1,0:T(8,128)S(1)} collective-permute-done((f32[32,768]{1,0:T(8,128)S(1)}, f32[32,768]{1,0:T(8,128)S(1)}, u32[]{:S(2)}, u32[]{:S(2)}) %collective-permute-start.26) | collective-permute-done | bytes 98336 | tf_op jit(solution)/shard_map/ppermute | solution.py:647
  82.2 3.8 %collective-permute-start.32 = (f32[32,768]{1,0:T(8,128)S(1)}, f32[32,768]{1,0:T(8,128)S(1)}, u32[]{:S(2)}, u32[]{:S(2)}) collective-permute-start(f32[32,768]{1,0:T(8,128)S(1)} %get-tuple-element.104), channel_id=1, source_target_pairs={{0,28},{4,24},{8,20},{12,16},{16,12},{20,8},{24,4},{28,0},{1,29},{... | collective-permute-start | bytes 294920 | tf_op jit(solution)/shard_map/ppermute | solution.py:647
  85.9 1.4 %shard_map.151 = (f32[32,768]{1,0:T(8,128)S(1)}, f32[32,768]{1,0:T(8,128)S(1)}, f32[32,768]{1,0:T(8,128)S(1)}, f32[32,768]{1,0:T(8,128)S(1)}, f32[32,768]{1,0:T(...) custom-call(s32[2]{0:T(128)S(1)} %pad_add_fusion.place, ...), custom_call_target="tpu_custom_call" | custom-call | flops 2000000000 | bytes 6000000 | tf_op jit(solution)/shard_map/pallas_call | solution.py:612
  87.4 1.8 %collective-permute-done.28.refs_3_ = f32[32,768]{1,0:T(8,128)S(1)} collective-permute-done((f32[32,768]{1,0:T(8,128)S(1)}, f32[32,768]{1,0:T(8,128)S(1)}, u32[]{:S(2)}, u32[]{:S(2)}) %collective-permute-start.28) | collective-permute-done | bytes 98336 | tf_op jit(solution)/shard_map/ppermute | solution.py:647
  89.1 2.1 %collective-permute-start.39 = (f32[32,768]{1,0:T(8,128)S(1)}, f32[32,768]{1,0:T(8,128)S(1)}, u32[]{:S(2)}, u32[]{:S(2)}) collective-permute-start(f32[32,768]{1,0:T(8,128)S(1)} %get-tuple-element.117), channel_id=1, source_target_pairs={{0,4},{4,0},{8,12},{12,8},{16,20},{20,16},{24,28},{28,24},{1,5},{5... | collective-permute-start | bytes 294920 | tf_op jit(solution)/shard_map/ppermute | solution.py:647
  91.2 2.6 %collective-permute-start.40 = (f32[32,768]{1,0:T(8,128)S(1)}, f32[32,768]{1,0:T(8,128)S(1)}, u32[]{:S(2)}, u32[]{:S(2)}) collective-permute-start(f32[32,768]{1,0:T(8,128)S(1)} %get-tuple-element.118), channel_id=1, source_target_pairs={{0,20},{4,16},{8,28},{12,24},{16,4},{20,0},{24,12},{28,8},{1,21},{... | collective-permute-start | bytes 294920 | tf_op jit(solution)/shard_map/ppermute | solution.py:647
  93.8 1.7 %shard_map.149 = (f32[72,768]{1,0:T(8,128)S(1)}, f32[72,768]{1,0:T(8,128)S(1)}, f32[72,768]{1,0:T(8,128)S(1)}, f32[72,768]{1,0:T(8,128)S(1)}) custom-call(s32[2]{0:T(128)S(1)} %pad_add_fusion.place, bf16[576,256]{1,0:T(8,128)(2,1)S(1)} %copy-done.6, bf16[576,256]{1,0:T(8,128)(2,1)S(1)} %copy-done.5, f32[32,768]{1,0:T(8,128)S(1)} %get-tuple-element.97.refs_0_, ...), custom_call_target="tpu_custom_call" | custom-call | flops 2000000000 | bytes 6000000 | tf_op jit(solution)/shard_map/pallas_call | solution.py:612
  95.5 2.3 %collective-permute-start.42 = (f32[32,768]{1,0:T(8,128)S(1)}, f32[32,768]{1,0:T(8,128)S(1)}, u32[]{:S(2)}, u32[]{:S(2)}) collective-permute-start(f32[32,768]{1,0:T(8,128)S(1)} %get-tuple-element.123), channel_id=1, source_target_pairs={{0,24},{4,28},{8,16},{12,20},{16,8},{20,12},{24,0},{28,4},{1,25},{... | collective-permute-start | bytes 294920 | tf_op jit(solution)/shard_map/ppermute | solution.py:647
  97.9 2.6 %collective-permute-done.38.refs_1_ = f32[32,768]{1,0:T(8,128)S(1)} collective-permute-done((f32[32,768]{1,0:T(8,128)S(1)}, f32[32,768]{1,0:T(8,128)S(1)}, u32[]{:S(2)}, u32[]{:S(2)}) %collective-permute-start.38) | collective-permute-done | bytes 98336 | tf_op jit(solution)/shard_map/ppermute | solution.py:647
  101.0 2.6 %collective-permute-start.44 = (f32[32,768]{1,0:T(8,128)S(1)}, f32[32,768]{1,0:T(8,128)S(1)}, u32[]{:S(2)}, u32[]{:S(2)}) collective-permute-start(f32[32,768]{1,0:T(8,128)S(1)} %get-tuple-element.125), channel_id=1, source_target_pairs={{0,28},{4,24},{8,20},{12,16},{16,12},{20,8},{24,4},{28,0},{1,29},{... | collective-permute-start | bytes 294920 | tf_op jit(solution)/shard_map/ppermute | solution.py:647
  104.8 2.1 %collective-permute-start.35 = (f32[72,768]{1,0:T(8,128)S(1)}, f32[72,768]{1,0:T(8,128)S(1)}, u32[]{:S(2)}, u32[]{:S(2)}) collective-permute-start(f32[72,768]{1,0:T(8,128)S(1)} %get-tuple-element.108), channel_id=1, source_target_pairs={{0,3},{1,2},{2,1},{3,0},{4,7},{5,6},{6,5},{7,4},{8,11},{9,10},{10,... | collective-permute-start | bytes 663560 | tf_op jit(solution)/shard_map/ppermute | solution.py:647
  106.9 1.5 %collective-permute-done.43.refs_6_ = f32[32,768]{1,0:T(8,128)S(1)} collective-permute-done((f32[32,768]{1,0:T(8,128)S(1)}, f32[32,768]{1,0:T(8,128)S(1)}, u32[]{:S(2)}, u32[]{:S(2)}) %collective-permute-start.43) | collective-permute-done | bytes 98336 | tf_op jit(solution)/shard_map/ppermute | solution.py:647
  108.4 1.7 %shard_map.153 = (f32[72,768]{1,0:T(8,128)S(1)}, f32[72,768]{1,0:T(8,128)S(1)}, f32[72,768]{1,0:T(8,128)S(1)}, f32[72,768]{1,0:T(8,128)S(1)}) custom-call(s32[2]{0:T(128)S(1)} %pad_add_fusion.place, bf16[576,256]{1,0:T(8,128)(2,1)S(1)} %copy-done.6, bf16[576,256]{1,0:T(8,128)(2,1)S(1)} %copy-done.5, f32[32,768]{1,0:T(8,128)S(1)} %get-tuple-element.115.refs_0_, ...), custom_call_target="tpu_custom_call" | custom-call | flops 2000000000 | bytes 6000000 | tf_op jit(solution)/shard_map/pallas_call | solution.py:612
  110.1 2.3 %collective-permute-start.45 = (f32[72,768]{1,0:T(8,128)S(1)}, f32[72,768]{1,0:T(8,128)S(1)}, u32[]{:S(2)}, u32[]{:S(2)}) collective-permute-start(f32[72,768]{1,0:T(8,128)S(1)} %get-tuple-element.127), channel_id=1, source_target_pairs={{0,2},{1,3},{2,0},{3,1},{4,6},{5,7},{6,4},{7,5},{8,10},{9,11},{10,... | collective-permute-start | bytes 663560 | tf_op jit(solution)/shard_map/ppermute | solution.py:647
  113.8 1.5 %shard_map.150 = (f32[3,4,80,256]{3,2,1,0:T(8,128)S(1)}, f32[3,64,256]{2,1,0:T(8,128)S(1)}, f32[3,64,256]{2,1,0:T(8,128)S(1)}) custom-call(s32[2]{0:T(128)S(1)} %pad_add_fusion.place, bf16[512,512]{1,0:T(8,128)(2,1)S(1)} %copy-done.2, bf16[512,512]{1,0:T(8,128)(2,1)S(1)} %copy-done.1, f32[72,768]{1,0:T(8,128)S(1)} %get-tuple-element.105.refs_0_.before, ...), custom_call_target="tpu_custom_call" | custom-call | flops 2000000000 | bytes 6000000 | tf_op jit(solution)/shard_map/pallas_call | solution.py:612
  115.2 4.5 %collective-permute-start.36 = (f32[3,64,256]{2,1,0:T(8,128)S(1)}, f32[3,64,256]{2,1,0:T(8,128)S(1)}, u32[]{:S(2)}, u32[]{:S(2)}) collective-permute-start(f32[3,64,256]{2,1,0:T(8,128)S(1)} %get-tuple-element.110), channel_id=1, source_target_pairs={{0,4},{4,8},{8,12},{12,16},{16,20},{20,24},{24,28},{28,0},{1,5},{5... | collective-permute-start | bytes 589832 | tf_op jit(solution)/shard_map/ppermute | solution.py:774
  120.0 2.4 %collective-permute-done.45.refs_8_ = f32[72,768]{1,0:T(8,128)S(1)} collective-permute-done((f32[72,768]{1,0:T(8,128)S(1)}, f32[72,768]{1,0:T(8,128)S(1)}, u32[]{:S(2)}, u32[]{:S(2)}) %collective-permute-start.45) | collective-permute-done | bytes 221216 | tf_op jit(solution)/shard_map/ppermute | solution.py:647
  122.5 5.8 %collective-permute-done.36.refs_1_ = f32[3,64,256]{2,1,0:T(8,128)S(1)} collective-permute-done((f32[3,64,256]{2,1,0:T(8,128)S(1)}, f32[3,64,256]{2,1,0:T(8,128)S(1)}, u32[]{:S(2)}, u32[]{:S(2)}) %collective-permute-start.36) | collective-permute-done | bytes 196640 | tf_op jit(solution)/shard_map/ppermute | solution.py:774
  128.3 1.7 %collective-permute-done.37.refs_2_ = f32[3,64,256]{2,1,0:T(8,128)S(1)} collective-permute-done((f32[3,64,256]{2,1,0:T(8,128)S(1)}, f32[3,64,256]{2,1,0:T(8,128)S(1)}, u32[]{:S(2)}, u32[]{:S(2)}) %collective-permute-start.37) | collective-permute-done | bytes 196640 | tf_op jit(solution)/shard_map/ppermute | solution.py:773
  130.0 3.3 %shard_map.154 = (f32[3,8,64,256]{3,2,1,0:T(8,128)}, f32[3,8,64,256]{3,2,1,0:T(8,128)}) custom-call(s32[2]{0:T(128)S(1)} %pad_add_fusion.place, bf16[512,512]{1,0:T(8,128)(2,1)S(1)} %copy-done.2, bf16[512,512]{1,0:T(8,128)(2,1)S(1)} %copy-done.1, f32[3,4,80,256]{3,2,1,0:T(8,128)S(1)} %get-tuple-element.109.refs_0_, ...), custom_call_target="tpu_custom_call" | custom-call | flops 4000000000 | bytes 12000000 | tf_op jit(solution)/shard_map/pallas_call | solution.py:612
  (82 shorter events, 12.8 us)
Async XLA Ops:
  1.8 10.0 %collective-permute-start.3 = (f32[8,128]{1,0:T(8,128)S(1)}, f32[8,128]{1,0:T(8,128)S(1)}, u32[]{:S(2)}, u32[]{:S(2)}) collective-permute-start(f32[8,128]{1,0:T(8,128)S(1)} %get-tuple-element.67), channel_id=1, source_target_pairs={{0,8},{4,12},{8,16},{12,20},{16,24},{20,28},{24,0},{28,4},{1,9},{5... | collective-permute-start | bytes 12296 | tf_op jit(solution)/shard_map/ppermute | solution.py:684
  4.8 6.9 %collective-permute-start.2 = (f32[8,128]{1,0:T(8,128)S(1)}, f32[8,128]{1,0:T(8,128)S(1)}, u32[]{:S(2)}, u32[]{:S(2)}) collective-permute-start(f32[8,128]{1,0:T(8,128)S(1)} %get-tuple-element.67), channel_id=1, source_target_pairs={{0,24},{4,28},{8,0},{12,4},{16,8},{20,12},{24,16},{28,20},{1,25},{... | collective-permute-start | bytes 12296 | tf_op jit(solution)/shard_map/ppermute | solution.py:683
  6.9 6.4 %collective-permute-start.1 = (f32[8,512]{1,0:T(8,128)S(1)}, f32[8,512]{1,0:T(8,128)S(1)}, u32[]{:S(2)}, u32[]{:S(2)}) collective-permute-start(f32[8,512]{1,0:T(8,128)S(1)} %get-tuple-element.66.own), channel_id=1, source_target_pairs={{0,4},{4,8},{8,12},{12,16},{16,20},{20,24},{24,28},{28,0},{1,5},{5... | collective-permute-start | bytes 49160 | tf_op jit(solution)/shard_map/ppermute | solution.py:682
  8.6 4.8 %collective-permute-start = (f32[8,512]{1,0:T(8,128)S(1)}, f32[8,512]{1,0:T(8,128)S(1)}, u32[]{:S(2)}, u32[]{:S(2)}) collective-permute-start(f32[8,512]{1,0:T(8,128)S(1)} %get-tuple-element.66.own), channel_id=1, source_target_pairs={{0,28},{4,0},{8,4},{12,8},{16,12},{20,16},{24,20},{28,24},{1,29},{... | collective-permute-start | bytes 49160 | tf_op jit(solution)/shard_map/ppermute | solution.py:681
  17.3 10.6 %collective-permute-start.16 = (f32[72,768]{1,0:T(8,128)S(1)}, f32[72,768]{1,0:T(8,128)S(1)}, u32[]{:S(2)}, u32[]{:S(2)}) collective-permute-start(f32[72,768]{1,0:T(8,128)S(1)} %get-tuple-element.85), channel_id=1, source_target_pairs={{0,2},{1,3},{2,0},{3,1},{4,6},{5,7},{6,4},{7,5},{8,10},{9,11},{10,... | collective-permute-start | bytes 663560 | tf_op jit(solution)/shard_map/ppermute | solution.py:647
  19.1 9.3 %collective-permute-start.17 = (f32[72,768]{1,0:T(8,128)S(1)}, f32[72,768]{1,0:T(8,128)S(1)}, u32[]{:S(2)}, u32[]{:S(2)}) collective-permute-start(f32[72,768]{1,0:T(8,128)S(1)} %get-tuple-element.86), channel_id=1, source_target_pairs={{0,1},{1,0},{2,3},{3,2},{4,5},{5,4},{6,7},{7,6},{8,9},{9,8},{10,11... | collective-permute-start | bytes 663560 | tf_op jit(solution)/shard_map/ppermute | solution.py:647
  19.1 9.3 %collective-permute-start.18 = (f32[72,768]{1,0:T(8,128)S(1)}, f32[72,768]{1,0:T(8,128)S(1)}, u32[]{:S(2)}, u32[]{:S(2)}) collective-permute-start(f32[72,768]{1,0:T(8,128)S(1)} %get-tuple-element.87), channel_id=1, source_target_pairs={{0,3},{1,2},{2,1},{3,0},{4,7},{5,6},{6,5},{7,4},{8,11},{9,10},{10,... | collective-permute-start | bytes 663560 | tf_op jit(solution)/shard_map/ppermute | solution.py:647
  26.1 8.4 %collective-permute-start.6 = (f32[72,768]{1,0:T(8,128)S(1)}, f32[72,768]{1,0:T(8,128)S(1)}, u32[]{:S(2)}, u32[]{:S(2)}) collective-permute-start(f32[72,768]{1,0:T(8,128)S(1)} %get-tuple-element.73), channel_id=1, source_target_pairs={{0,2},{1,3},{2,0},{3,1},{4,6},{5,7},{6,4},{7,5},{8,10},{9,11},{10,... | collective-permute-start | bytes 663560 | tf_op jit(solution)/shard_map/ppermute | solution.py:647
  27.9 8.2 %collective-permute-start.7 = (f32[72,768]{1,0:T(8,128)S(1)}, f32[72,768]{1,0:T(8,128)S(1)}, u32[]{:S(2)}, u32[]{:S(2)}) collective-permute-start(f32[72,768]{1,0:T(8,128)S(1)} %get-tuple-element.74), channel_id=1, source_target_pairs={{0,1},{1,0},{2,3},{3,2},{4,5},{5,4},{6,7},{7,6},{8,9},{9,8},{10,11... | collective-permute-start | bytes 663560 | tf_op jit(solution)/shard_map/ppermute | solution.py:647
  27.9 11.9 %collective-permute-start.8 = (f32[72,768]{1,0:T(8,128)S(1)}, f32[72,768]{1,0:T(8,128)S(1)}, u32[]{:S(2)}, u32[]{:S(2)}) collective-permute-start(f32[72,768]{1,0:T(8,128)S(1)} %get-tuple-element.75), channel_id=1, source_target_pairs={{0,3},{1,2},{2,1},{3,0},{4,7},{5,6},{6,5},{7,4},{8,11},{9,10},{10,... | collective-permute-start | bytes 663560 | tf_op jit(solution)/shard_map/ppermute | solution.py:647
  30.0 11.4 %collective-permute-start.19 = (f32[32,768]{1,0:T(8,128)S(1)}, f32[32,768]{1,0:T(8,128)S(1)}, u32[]{:S(2)}, u32[]{:S(2)}) collective-permute-start(f32[32,768]{1,0:T(8,128)S(1)} %get-tuple-element.89), channel_id=1, source_target_pairs={{0,16},{4,20},{8,24},{12,28},{16,0},{20,4},{24,8},{28,12},{1,17},{... | collective-permute-start | bytes 294920 | tf_op jit(solution)/shard_map/ppermute | solution.py:647
  30.1 12.0 %collective-permute-start.20 = (f32[32,768]{1,0:T(8,128)S(1)}, f32[32,768]{1,0:T(8,128)S(1)}, u32[]{:S(2)}, u32[]{:S(2)}) collective-permute-start(f32[32,768]{1,0:T(8,128)S(1)} %get-tuple-element.90), channel_id=1, source_target_pairs={{0,4},{4,0},{8,12},{12,8},{16,20},{20,16},{24,28},{28,24},{1,5},{5... | collective-permute-start | bytes 294920 | tf_op jit(solution)/shard_map/ppermute | solution.py:647
  34.5 10.9 %collective-permute-start.21 = (f32[32,768]{1,0:T(8,128)S(1)}, f32[32,768]{1,0:T(8,128)S(1)}, u32[]{:S(2)}, u32[]{:S(2)}) collective-permute-start(f32[32,768]{1,0:T(8,128)S(1)} %get-tuple-element.91), channel_id=1, source_target_pairs={{0,20},{4,16},{8,28},{12,24},{16,4},{20,0},{24,12},{28,8},{1,21},{... | collective-permute-start | bytes 294920 | tf_op jit(solution)/shard_map/ppermute | solution.py:647
  36.1 9.7 %collective-permute-start.22 = (f32[32,768]{1,0:T(8,128)S(1)}, f32[32,768]{1,0:T(8,128)S(1)}, u32[]{:S(2)}, u32[]{:S(2)}) collective-permute-start(f32[32,768]{1,0:T(8,128)S(1)} %get-tuple-element.92), channel_id=1, source_target_pairs={{0,8},{4,12},{8,0},{12,4},{16,24},{20,28},{24,16},{28,20},{1,9},{5... | collective-permute-start | bytes 294920 | tf_op jit(solution)/shard_map/ppermute | solution.py:647
  39.8 9.1 %collective-permute-start.23 = (f32[32,768]{1,0:T(8,128)S(1)}, f32[32,768]{1,0:T(8,128)S(1)}, u32[]{:S(2)}, u32[]{:S(2)}) collective-permute-start(f32[32,768]{1,0:T(8,128)S(1)} %get-tuple-element.93), channel_id=1, source_target_pairs={{0,24},{4,28},{8,16},{12,20},{16,8},{20,12},{24,0},{28,4},{1,25},{... | collective-permute-start | bytes 294920 | tf_op jit(solution)/shard_map/ppermute | solution.py:647
  41.4 8.4 %collective-permute-start.24 = (f32[32,768]{1,0:T(8,128)S(1)}, f32[32,768]{1,0:T(8,128)S(1)}, u32[]{:S(2)}, u32[]{:S(2)}) collective-permute-start(f32[32,768]{1,0:T(8,128)S(1)} %get-tuple-element.94), channel_id=1, source_target_pairs={{0,12},{4,8},{8,4},{12,0},{16,28},{20,24},{24,20},{28,16},{1,13},{... | collective-permute-start | bytes 294920 | tf_op jit(solution)/shard_map/ppermute | solution.py:647
  42.0 9.7 %collective-permute-start.25 = (f32[32,768]{1,0:T(8,128)S(1)}, f32[32,768]{1,0:T(8,128)S(1)}, u32[]{:S(2)}, u32[]{:S(2)}) collective-permute-start(f32[32,768]{1,0:T(8,128)S(1)} %get-tuple-element.95), channel_id=1, source_target_pairs={{0,28},{4,24},{8,20},{12,16},{16,12},{20,8},{24,4},{28,0},{1,29},{... | collective-permute-start | bytes 294920 | tf_op jit(solution)/shard_map/ppermute | solution.py:647
  45.4 14.7 %collective-permute-start.9 = (f32[32,768]{1,0:T(8,128)S(1)}, f32[32,768]{1,0:T(8,128)S(1)}, u32[]{:S(2)}, u32[]{:S(2)}) collective-permute-start(f32[32,768]{1,0:T(8,128)S(1)} %get-tuple-element.77), channel_id=1, source_target_pairs={{0,16},{4,20},{8,24},{12,28},{16,0},{20,4},{24,8},{28,12},{1,17},{... | collective-permute-start | bytes 294920 | tf_op jit(solution)/shard_map/ppermute | solution.py:647
  45.9 14.2 %collective-permute-start.10 = (f32[32,768]{1,0:T(8,128)S(1)}, f32[32,768]{1,0:T(8,128)S(1)}, u32[]{:S(2)}, u32[]{:S(2)}) collective-permute-start(f32[32,768]{1,0:T(8,128)S(1)} %get-tuple-element.78), channel_id=1, source_target_pairs={{0,4},{4,0},{8,12},{12,8},{16,20},{20,16},{24,28},{28,24},{1,5},{5... | collective-permute-start | bytes 294920 | tf_op jit(solution)/shard_map/ppermute | solution.py:647
  48.9 15.1 %collective-permute-start.11 = (f32[32,768]{1,0:T(8,128)S(1)}, f32[32,768]{1,0:T(8,128)S(1)}, u32[]{:S(2)}, u32[]{:S(2)}) collective-permute-start(f32[32,768]{1,0:T(8,128)S(1)} %get-tuple-element.79), channel_id=1, source_target_pairs={{0,20},{4,16},{8,28},{12,24},{16,4},{20,0},{24,12},{28,8},{1,21},{... | collective-permute-start | bytes 294920 | tf_op jit(solution)/shard_map/ppermute | solution.py:647
  49.8 14.2 %collective-permute-start.12 = (f32[32,768]{1,0:T(8,128)S(1)}, f32[32,768]{1,0:T(8,128)S(1)}, u32[]{:S(2)}, u32[]{:S(2)}) collective-permute-start(f32[32,768]{1,0:T(8,128)S(1)} %get-tuple-element.80), channel_id=1, source_target_pairs={{0,8},{4,12},{8,0},{12,4},{16,24},{20,28},{24,16},{28,20},{1,9},{5... | collective-permute-start | bytes 294920 | tf_op jit(solution)/shard_map/ppermute | solution.py:647
  51.7 14.0 %collective-permute-start.13 = (f32[32,768]{1,0:T(8,128)S(1)}, f32[32,768]{1,0:T(8,128)S(1)}, u32[]{:S(2)}, u32[]{:S(2)}) collective-permute-start(f32[32,768]{1,0:T(8,128)S(1)} %get-tuple-element.81), channel_id=1, source_target_pairs={{0,24},{4,28},{8,16},{12,20},{16,8},{20,12},{24,0},{28,4},{1,25},{... | collective-permute-start | bytes 294920 | tf_op jit(solution)/shard_map/ppermute | solution.py:647
  60.0 7.6 %collective-permute-start.14 = (f32[32,768]{1,0:T(8,128)S(1)}, f32[32,768]{1,0:T(8,128)S(1)}, u32[]{:S(2)}, u32[]{:S(2)}) collective-permute-start(f32[32,768]{1,0:T(8,128)S(1)} %get-tuple-element.82), channel_id=1, source_target_pairs={{0,12},{4,8},{8,4},{12,0},{16,28},{20,24},{24,20},{28,16},{1,13},{... | collective-permute-start | bytes 294920 | tf_op jit(solution)/shard_map/ppermute | solution.py:647
  60.0 7.6 %collective-permute-start.15 = (f32[32,768]{1,0:T(8,128)S(1)}, f32[32,768]{1,0:T(8,128)S(1)}, u32[]{:S(2)}, u32[]{:S(2)}) collective-permute-start(f32[32,768]{1,0:T(8,128)S(1)} %get-tuple-element.83), channel_id=1, source_target_pairs={{0,28},{4,24},{8,20},{12,16},{16,12},{20,8},{24,4},{28,0},{1,29},{... | collective-permute-start | bytes 294920 | tf_op jit(solution)/shard_map/ppermute | solution.py:647
  64.0 5.1 %collective-permute-start.4 = (f32[48,256]{1,0:T(8,128)S(1)}, f32[48,256]{1,0:T(8,128)S(1)}, u32[]{:S(2)}, u32[]{:S(2)}) collective-permute-start(f32[48,256]{1,0:T(8,128)S(1)} %get-tuple-element.70), channel_id=1, source_target_pairs={{0,1},{1,2},{2,3},{3,0},{4,5},{5,6},{6,7},{7,4},{8,9},{9,10},{10,1... | collective-permute-start | bytes 147464 | tf_op jit(solution)/shard_map/ppermute | solution.py:705
  64.0 5.0 %collective-permute-start.5 = (f32[48,256]{1,0:T(8,128)S(1)}, f32[48,256]{1,0:T(8,128)S(1)}, u32[]{:S(2)}, u32[]{:S(2)}) collective-permute-start(f32[48,256]{1,0:T(8,128)S(1)} %get-tuple-element.71), channel_id=1, source_target_pairs={{0,3},{1,0},{2,1},{3,2},{4,7},{5,4},{6,5},{7,6},{8,11},{9,8},{10,9... | collective-permute-start | bytes 147464 | tf_op jit(solution)/shard_map/ppermute | solution.py:706
  72.7 9.5 %collective-permute-start.26 = (f32[32,768]{1,0:T(8,128)S(1)}, f32[32,768]{1,0:T(8,128)S(1)}, u32[]{:S(2)}, u32[]{:S(2)}) collective-permute-start(f32[32,768]{1,0:T(8,128)S(1)} %get-tuple-element.98), channel_id=1, source_target_pairs={{0,16},{4,20},{8,24},{12,28},{16,0},{20,4},{24,8},{28,12},{1,17},{... | collective-permute-start | bytes 294920 | tf_op jit(solution)/shard_map/ppermute | solution.py:647
  74.9 7.3 %collective-permute-start.27 = (f32[32,768]{1,0:T(8,128)S(1)}, f32[32,768]{1,0:T(8,128)S(1)}, u32[]{:S(2)}, u32[]{:S(2)}) collective-permute-start(f32[32,768]{1,0:T(8,128)S(1)} %get-tuple-element.99), channel_id=1, source_target_pairs={{0,4},{4,0},{8,12},{12,8},{16,20},{20,16},{24,28},{28,24},{1,5},{5... | collective-permute-start | bytes 294920 | tf_op jit(solution)/shard_map/ppermute | solution.py:647
  76.0 13.1 %collective-permute-start.28 = (f32[32,768]{1,0:T(8,128)S(1)}, f32[32,768]{1,0:T(8,128)S(1)}, u32[]{:S(2)}, u32[]{:S(2)}) collective-permute-start(f32[32,768]{1,0:T(8,128)S(1)} %get-tuple-element.100), channel_id=1, source_target_pairs={{0,20},{4,16},{8,28},{12,24},{16,4},{20,0},{24,12},{28,8},{1,21},{... | collective-permute-start | bytes 294920 | tf_op jit(solution)/shard_map/ppermute | solution.py:647
  77.2 12.0 %collective-permute-start.29 = (f32[32,768]{1,0:T(8,128)S(1)}, f32[32,768]{1,0:T(8,128)S(1)}, u32[]{:S(2)}, u32[]{:S(2)}) collective-permute-start(f32[32,768]{1,0:T(8,128)S(1)} %get-tuple-element.101), channel_id=1, source_target_pairs={{0,8},{4,12},{8,0},{12,4},{16,24},{20,28},{24,16},{28,20},{1,9},{5... | collective-permute-start | bytes 294920 | tf_op jit(solution)/shard_map/ppermute | solution.py:647
  79.1 12.1 %collective-permute-start.30 = (f32[32,768]{1,0:T(8,128)S(1)}, f32[32,768]{1,0:T(8,128)S(1)}, u32[]{:S(2)}, u32[]{:S(2)}) collective-permute-start(f32[32,768]{1,0:T(8,128)S(1)} %get-tuple-element.102), channel_id=1, source_target_pairs={{0,24},{4,28},{8,16},{12,20},{16,8},{20,12},{24,0},{28,4},{1,25},{... | collective-permute-start | bytes 294920 | tf_op jit(solution)/shard_map/ppermute | solution.py:647
  82.2 11.6 %collective-permute-start.31 = (f32[32,768]{1,0:T(8,128)S(1)}, f32[32,768]{1,0:T(8,128)S(1)}, u32[]{:S(2)}, u32[]{:S(2)}) collective-permute-start(f32[32,768]{1,0:T(8,128)S(1)} %get-tuple-element.103), channel_id=1, source_target_pairs={{0,12},{4,8},{8,4},{12,0},{16,28},{20,24},{24,20},{28,16},{1,13},{... | collective-permute-start | bytes 294920 | tf_op jit(solution)/shard_map/ppermute | solution.py:647
  82.2 11.6 %collective-permute-start.32 = (f32[32,768]{1,0:T(8,128)S(1)}, f32[32,768]{1,0:T(8,128)S(1)}, u32[]{:S(2)}, u32[]{:S(2)}) collective-permute-start(f32[32,768]{1,0:T(8,128)S(1)} %get-tuple-element.104), channel_id=1, source_target_pairs={{0,28},{4,24},{8,20},{12,16},{16,12},{20,8},{24,4},{28,0},{1,29},{... | collective-permute-start | bytes 294920 | tf_op jit(solution)/shard_map/ppermute | solution.py:647
  89.1 11.4 %collective-permute-start.38 = (f32[32,768]{1,0:T(8,128)S(1)}, f32[32,768]{1,0:T(8,128)S(1)}, u32[]{:S(2)}, u32[]{:S(2)}) collective-permute-start(f32[32,768]{1,0:T(8,128)S(1)} %get-tuple-element.116), channel_id=1, source_target_pairs={{0,16},{4,20},{8,24},{12,28},{16,0},{20,4},{24,8},{28,12},{1,17},{... | collective-permute-start | bytes 294920 | tf_op jit(solution)/shard_map/ppermute | solution.py:647
  89.1 11.8 %collective-permute-start.39 = (f32[32,768]{1,0:T(8,128)S(1)}, f32[32,768]{1,0:T(8,128)S(1)}, u32[]{:S(2)}, u32[]{:S(2)}) collective-permute-start(f32[32,768]{1,0:T(8,128)S(1)} %get-tuple-element.117), channel_id=1, source_target_pairs={{0,4},{4,0},{8,12},{12,8},{16,20},{20,16},{24,28},{28,24},{1,5},{5... | collective-permute-start | bytes 294920 | tf_op jit(solution)/shard_map/ppermute | solution.py:647
  91.2 13.5 %collective-permute-start.40 = (f32[32,768]{1,0:T(8,128)S(1)}, f32[32,768]{1,0:T(8,128)S(1)}, u32[]{:S(2)}, u32[]{:S(2)}) collective-permute-start(f32[32,768]{1,0:T(8,128)S(1)} %get-tuple-element.118), channel_id=1, source_target_pairs={{0,20},{4,16},{8,28},{12,24},{16,4},{20,0},{24,12},{28,8},{1,21},{... | collective-permute-start | bytes 294920 | tf_op jit(solution)/shard_map/ppermute | solution.py:647
  93.8 11.0 %collective-permute-start.41 = (f32[32,768]{1,0:T(8,128)S(1)}, f32[32,768]{1,0:T(8,128)S(1)}, u32[]{:S(2)}, u32[]{:S(2)}) collective-permute-start(f32[32,768]{1,0:T(8,128)S(1)} %get-tuple-element.119), channel_id=1, source_target_pairs={{0,8},{4,12},{8,0},{12,4},{16,24},{20,28},{24,16},{28,20},{1,9},{5... | collective-permute-start | bytes 294920 | tf_op jit(solution)/shard_map/ppermute | solution.py:647
  95.5 9.3 %collective-permute-start.42 = (f32[32,768]{1,0:T(8,128)S(1)}, f32[32,768]{1,0:T(8,128)S(1)}, u32[]{:S(2)}, u32[]{:S(2)}) collective-permute-start(f32[32,768]{1,0:T(8,128)S(1)} %get-tuple-element.123), channel_id=1, source_target_pairs={{0,24},{4,28},{8,16},{12,20},{16,8},{20,12},{24,0},{28,4},{1,25},{... | collective-permute-start | bytes 294920 | tf_op jit(solution)/shard_map/ppermute | solution.py:647
  100.5 7.9 %collective-permute-start.43 = (f32[32,768]{1,0:T(8,128)S(1)}, f32[32,768]{1,0:T(8,128)S(1)}, u32[]{:S(2)}, u32[]{:S(2)}) collective-permute-start(f32[32,768]{1,0:T(8,128)S(1)} %get-tuple-element.124), channel_id=1, source_target_pairs={{0,12},{4,8},{8,4},{12,0},{16,28},{20,24},{24,20},{28,16},{1,13},{... | collective-permute-start | bytes 294920 | tf_op jit(solution)/shard_map/ppermute | solution.py:647
  101.0 7.5 %collective-permute-start.44 = (f32[32,768]{1,0:T(8,128)S(1)}, f32[32,768]{1,0:T(8,128)S(1)}, u32[]{:S(2)}, u32[]{:S(2)}) collective-permute-start(f32[32,768]{1,0:T(8,128)S(1)} %get-tuple-element.125), channel_id=1, source_target_pairs={{0,28},{4,24},{8,20},{12,16},{16,12},{20,8},{24,4},{28,0},{1,29},{... | collective-permute-start | bytes 294920 | tf_op jit(solution)/shard_map/ppermute | solution.py:647
  104.8 8.3 %collective-permute-start.33 = (f32[72,768]{1,0:T(8,128)S(1)}, f32[72,768]{1,0:T(8,128)S(1)}, u32[]{:S(2)}, u32[]{:S(2)}) collective-permute-start(f32[72,768]{1,0:T(8,128)S(1)} %get-tuple-element.106), channel_id=1, source_target_pairs={{0,2},{1,3},{2,0},{3,1},{4,6},{5,7},{6,4},{7,5},{8,10},{9,11},{10,... | collective-permute-start | bytes 663560 | tf_op jit(solution)/shard_map/ppermute | solution.py:647
  104.8 8.3 %collective-permute-start.34 = (f32[72,768]{1,0:T(8,128)S(1)}, f32[72,768]{1,0:T(8,128)S(1)}, u32[]{:S(2)}, u32[]{:S(2)}) collective-permute-start(f32[72,768]{1,0:T(8,128)S(1)} %get-tuple-element.107), channel_id=1, source_target_pairs={{0,1},{1,0},{2,3},{3,2},{4,5},{5,4},{6,7},{7,6},{8,9},{9,8},{10,11... | collective-permute-start | bytes 663560 | tf_op jit(solution)/shard_map/ppermute | solution.py:647
  104.8 8.9 %collective-permute-start.35 = (f32[72,768]{1,0:T(8,128)S(1)}, f32[72,768]{1,0:T(8,128)S(1)}, u32[]{:S(2)}, u32[]{:S(2)}) collective-permute-start(f32[72,768]{1,0:T(8,128)S(1)} %get-tuple-element.108), channel_id=1, source_target_pairs={{0,3},{1,2},{2,1},{3,0},{4,7},{5,6},{6,5},{7,4},{8,11},{9,10},{10,... | collective-permute-start | bytes 663560 | tf_op jit(solution)/shard_map/ppermute | solution.py:647
  110.1 12.3 %collective-permute-start.45 = (f32[72,768]{1,0:T(8,128)S(1)}, f32[72,768]{1,0:T(8,128)S(1)}, u32[]{:S(2)}, u32[]{:S(2)}) collective-permute-start(f32[72,768]{1,0:T(8,128)S(1)} %get-tuple-element.127), channel_id=1, source_target_pairs={{0,2},{1,3},{2,0},{3,1},{4,6},{5,7},{6,4},{7,5},{8,10},{9,11},{10,... | collective-permute-start | bytes 663560 | tf_op jit(solution)/shard_map/ppermute | solution.py:647
  112.4 10.0 %collective-permute-start.46 = (f32[72,768]{1,0:T(8,128)S(1)}, f32[72,768]{1,0:T(8,128)S(1)}, u32[]{:S(2)}, u32[]{:S(2)}) collective-permute-start(f32[72,768]{1,0:T(8,128)S(1)} %get-tuple-element.128), channel_id=1, source_target_pairs={{0,1},{1,0},{2,3},{3,2},{4,5},{5,4},{6,7},{7,6},{8,9},{9,8},{10,11... | collective-permute-start | bytes 663560 | tf_op jit(solution)/shard_map/ppermute | solution.py:647
  113.1 9.4 %collective-permute-start.47 = (f32[72,768]{1,0:T(8,128)S(1)}, f32[72,768]{1,0:T(8,128)S(1)}, u32[]{:S(2)}, u32[]{:S(2)}) collective-permute-start(f32[72,768]{1,0:T(8,128)S(1)} %get-tuple-element.129), channel_id=1, source_target_pairs={{0,3},{1,2},{2,1},{3,0},{4,7},{5,6},{6,5},{7,4},{8,11},{9,10},{10,... | collective-permute-start | bytes 663560 | tf_op jit(solution)/shard_map/ppermute | solution.py:647
  115.2 13.1 %collective-permute-start.36 = (f32[3,64,256]{2,1,0:T(8,128)S(1)}, f32[3,64,256]{2,1,0:T(8,128)S(1)}, u32[]{:S(2)}, u32[]{:S(2)}) collective-permute-start(f32[3,64,256]{2,1,0:T(8,128)S(1)} %get-tuple-element.110), channel_id=1, source_target_pairs={{0,4},{4,8},{8,12},{12,16},{16,20},{20,24},{24,28},{28,0},{1,5},{5... | collective-permute-start | bytes 589832 | tf_op jit(solution)/shard_map/ppermute | solution.py:774
  119.7 10.3 %collective-permute-start.37 = (f32[3,64,256]{2,1,0:T(8,128)S(1)}, f32[3,64,256]{2,1,0:T(8,128)S(1)}, u32[]{:S(2)}, u32[]{:S(2)}) collective-permute-start(f32[3,64,256]{2,1,0:T(8,128)S(1)} %get-tuple-element.111), channel_id=1, source_target_pairs={{0,28},{4,0},{8,4},{12,8},{16,12},{20,16},{24,20},{28,24},{1,29},{... | collective-permute-start | bytes 589832 | tf_op jit(solution)/shard_map/ppermute | solution.py:773
  (9 other events, 82.2 us)

commit v7 on v6

--- a/solution.py
+++ b/solution.py
@@ -136,8 +136,8 @@
     far, near = list(range(count // 2, count)), list(range(1, count // 2))
     order = [0]
     while far or near:
-        order += far[:1] + near[:1]
-        far, near = far[1:], near[1:]
+        order += far[:2] + near[:2]
+        far, near = far[2:], near[2:]
     return order
 
 
@@ -287,9 +287,9 @@
         out[...] = made[d]
 
 
-def x_back_kernel(sends, tables, place, *refs):
+def x_back_kernel(sends, passed, tables, place, *refs):
     held, made = refs[-2:]
-    outs, parts = refs[-2 - sends : -2], refs[: -2 - sends]
+    outs, parts = refs[-2 - sends : -2], refs[passed : -2 - sends]
     gather_blocks(parts, held, place[0])
     pencils, rows, width = made.shape
     both = table_left(tables[0][...], tables[1][...], held[...].reshape(-1, width))
@@ -357,7 +357,8 @@
 
 
 def pass_kernel(before, *refs):
-    for source, target in zip(refs[: len(refs) // 2], refs[len(refs) // 2 :]):
+    half = LATE
+    for source, target in zip(refs[-2 * half : -half], refs[-half:]):
         target[...] = source[...]
 
 
@@ -528,16 +529,61 @@
         last[c] = values[c, listed[-1]][0:cols]
 
 
-def stretch_kernel(
-    chunks, tables, place, edges, before, after, low_rim, high_rim, *refs
-):
-    meshes, refs = refs[:2], refs[2:]
-    velocity, vorticity, held, inner, omega, sems = refs[-6:]
-    _, planes, cols, ny = velocity.shape
+def where_planes(chunks):
     spot = {}
     for n, chunk in enumerate(chunks):
         for i, pair in enumerate(chunk):
             spot[2 * pair], spot[2 * pair + 1] = (n, 2 * i), (n, 2 * i + 1)
+    return spot
+
+
+def rim_start(meshes, which, c, i):
+    before = 6 * meshes[1].shape[1] if which == 0 else 0
+    return before + 2 * (c * meshes[which].shape[1] + i)
+
+
+def stretch_plane(out, mesh, rims, at, rows_of, above, below):
+    cols, ny = out[0].shape
+    low_rim, high_rim = rims
+    for c in range(3):
+        out[c][...] = mesh[c][...]
+        out[c][0:2] += low_rim[at[c] : at[c] + 2]
+        out[c][cols - 2 : cols] += high_rim[at[c] : at[c] + 2]
+    omega = [ref[...] for ref in out]
+    for c in range(3):
+        value = rows_of(c, RIM)
+        along_z = (above(c) - below(c)) * 0.5
+        along_x = (rows_of(c, RIM + 1) - rows_of(c, RIM - 1)) * 0.5
+        along_y = (pltpu.roll(value, ny - 1, 1) - pltpu.roll(value, 1, 1)) * 0.5
+        stretch = omega[0] * along_z + omega[1] * along_x + omega[2] * along_y
+        out[c][...] = omega[c] + TIME_STEP * stretch
+
+
+def ends_kernel(chunks, edges, before, after, low_rim, high_rim, *refs):
+    meshes, out = refs[:-1], refs[-1]
+    cols = before.shape[1]
+    size = edges.shape[1]
+
+    def rows_of(i):
+        return lambda c, start=RIM: edges[c, i, start : start + cols]
+
+    for n, i in enumerate((0, size - 1)):
+        stretch_plane(
+            [out.at[c, n] for c in range(3)],
+            [meshes[0].at[c, i] for c in range(3)],
+            (low_rim, high_rim),
+            [rim_start(meshes, 0, c, i) for c in range(3)],
+            rows_of(i),
+            (lambda c: after[c]) if i else rows_of(1),
+            rows_of(size - 2) if i else (lambda c: before[c]),
+        )
+
+
+def stretch_kernel(chunks, tables, place, edges, ends, low_rim, high_rim, *refs):
+    meshes, refs = refs[:2], refs[2:]
+    velocity, vorticity, held, inner, omega, sems = refs[-6:]
+    _, planes, cols, ny = velocity.shape
+    spot = where_planes(chunks)
     talls = (edges, inner)
     sent = []
 
@@ -545,47 +591,35 @@
         sent.append(pltpu.make_async_copy(source, target, sems.at[len(sent)]))
         sent[-1].start()
 
-    def send_velocity(z):
+    def rows_of(z):
         n, i = spot[z]
-        send(talls[n].at[:, i, pl.ds(RIM, cols)], velocity.at[:, z])
-
-    def rows_of(c, z, start=RIM):
-        n, i = spot[z]
-        return talls[n][c, i, start : start + cols]
-
-    for z in range(planes):
-        if spot[z][0] == 0:
-            send_velocity(z)
+        return lambda c, start=RIM: talls[n][c, i, start : start + cols]
+
+    def send_velocity(which):
+        for z in range(planes):
+            n, i = spot[z]
+            if n == which:
+                send(talls[n].at[:, i, pl.ds(RIM, cols)], velocity.at[:, z])
+
+    send_velocity(0)
+    send(ends.at[:, 0], vorticity.at[:, 0])
+    send(ends.at[:, 1], vorticity.at[:, planes - 1])
     gather_blocks(refs[:-6], held, place[1])
     for (c, z), value in planes_of(held, chunks[1], tables).items():
         hold(inner, c, spot[z][1], value)
-    for z in range(planes):
-        if spot[z][0] == 1:
-            send_velocity(z)
-    rim_at = 0
-    for which in (1, 0):
-        size = meshes[which].shape[1]
-        for z in range(planes):
-            n, i = spot[z]
-            if n != which:
-                continue
-            for c in range(3):
-                at = rim_at + 2 * (c * size + i)
-                omega[c, z] = meshes[which][c, i]
-                omega[c, z, 0:2] += low_rim[at : at + 2]
-                omega[c, z, cols - 2 : cols] += high_rim[at : at + 2]
-            omega_z = [omega[c, z] for c in range(3)]
-            for c in range(3):
-                value = rows_of(c, z)
-                above = rows_of(c, z + 1) if z + 1 < planes else after[c]
-                below = rows_of(c, z - 1) if z > 0 else before[c]
-                along_z = (above - below) * 0.5
-                along_x = (rows_of(c, z, RIM + 1) - rows_of(c, z, RIM - 1)) * 0.5
-                along_y = (pltpu.roll(value, ny - 1, 1) - pltpu.roll(value, 1, 1)) * 0.5
-                stretch = omega_z[0] * along_z + omega_z[1] * along_x + omega_z[2] * along_y
-                omega[c, z] = omega_z[c] + TIME_STEP * stretch
-            send(omega.at[:, z], vorticity.at[:, z])
-        rim_at += 6 * size
+    send_velocity(1)
+    for z in range(1, planes - 1):
+        which, i = spot[z]
+        stretch_plane(
+            [omega.at[c, z] for c in range(3)],
+            [meshes[which].at[c, i] for c in range(3)],
+            (low_rim, high_rim),
+            [rim_start(meshes, which, c, i) for c in range(3)],
+            rows_of(z),
+            rows_of(z + 1),
+            rows_of(z - 1),
+        )
+        send(omega.at[:, z], vorticity.at[:, z])
     for copy in sent:
         copy.wait()
 
@@ -742,11 +776,14 @@
         for chunk, source, width in zip(chunks, data, widths)
     ]
 
-    def back(part, width):
+    def back(part, width, before=()):
         shapes = sent_shapes("gx", rows, width)
         part = call(
-            loaded(functools.partial(x_back_kernel, len(shapes))),
-            [here] + [(VM, t) for t in x_back] + [(VM, p) for p in part],
+            loaded(functools.partial(x_back_kernel, len(shapes), len(before))),
+            [here]
+            + [(VM, t) for t in x_back]
+            + [(AN, b) for b in before]
+            + [(VM, p) for p in part],
             [(VM, shape) for shape in shapes],
             [((slabs, block, width), F32), ((pencils, rows, width), F32)],
         )
@@ -764,20 +801,25 @@
     if early < len(left[1]):
         late = call(
             pass_kernel,
-            [(AN, parts[0][0])] + [(VM, p) for p in left[1][early:]],
+            [(AN, parts[0][0])] + [(AN, p) for p in second[1:]] + [(VM, p) for p in left[1][early:]],
             [(VM, p.shape) for p in left[1][early:]],
             micros=0.3,
         )
         second += exchange(late, "gz", early)
-    parts.append(back(second, widths[1]))
+    parts.append(back(second, widths[1], [first]))
     after = lax.ppermute(first, "gz", ring("gz", -1))
     before = lax.ppermute(last, "gz", ring("gz", 1))
+    (ends,) = call(
+        functools.partial(ends_kernel, chunks),
+        [(VM, v) for v in (edges, before, after, low_rim, high_rim, *meshes)],
+        [(VM, (3, 2, cols, ny))],
+    )
     return tuple(
         call(
             loaded(functools.partial(stretch_kernel, chunks)),
             [here]
             + tables
-            + [(VM, v) for v in (edges, before, after, low_rim, high_rim, *meshes)]
+            + [(VM, v) for v in (edges, ends, low_rim, high_rim, *meshes)]
             + [(VM, p) for p in parts[1]],
             [(AN, ambient.shape), (AN, ambient.shape)],
             [

time: 134 us -> 138 us (1.030)
  waiting for transfers between devices: 31.8 us -> 33.4 us
    ppermute x40, waiting for transfers between devices: 22.7 us -> 31.7 us  [exchange(): lax.ppermute(block, axis, [(i, i ^ k) for i in range(count)])]
    ppermute x1, waiting for transfers between devices: 5.82 us -> 0.01 us  [on_device(): before = lax.ppermute(last, 'gz', ring('gz', 1))]
    ppermute x1, starting transfers between devices: 0.29 us -> 3.74 us  [on_device(): after = lax.ppermute(first, 'gz', ring('gz', -1))]
    ppermute x1, starting transfers between devices: 4.48 us -> 1.04 us  [on_device(): before = lax.ppermute(last, 'gz', ring('gz', 1))]
    ppermute x1, waiting for transfers between devices: 1.68 us -> 0.01 us  [on_device(): after = lax.ppermute(first, 'gz', ring('gz', -1))]
    pallas_call x15 -> x16, Pallas kernels: 30.7 us -> 30.8 us  [call(): pl.pallas_call(kernel, out_shape=[jax.ShapeDtypeStruct(shape, F32) for _,...]
  transfers between devices with their start and end apart: 48 -> 48, of which waited for: 15 -> 17; matrix products, arithmetic and copies ran while one was open for 0% -> 0% of each run, Pallas kernels for 14% -> 14%
where the time goes in v7:
time: 138 us; the launch traced here: 136 us
  starting transfers between devices  70.8 us (51%)
  waiting for transfers between devices  33.4 us (24%)
  Pallas kernels  30.8 us (22%)
    ppermute x40, starting transfers between devices, exchange(): lax.ppermute(block, axis, [(i, i ^ k) for i in range(count)])  54.4 us
    ppermute x40, waiting for transfers between devices, exchange(): lax.ppermute(block, axis, [(i, i ^ k) for i in range(count)])  31.7 us
    pallas_call x16, Pallas kernels, call(): pl.pallas_call(kernel, out_shape=[jax.ShapeDtypeStruct(shape, F32) for _,...  30.8 us
    ppermute x1, starting transfers between devices, on_device(): after = lax.ppermute(first, 'gz', ring('gz', -1))  3.74 us
    ppermute x1, starting transfers between devices, on_device(): down2 = lax.ppermute(movers, 'gz', ring('gz', 2))  3.08 us
    ppermute x1, starting transfers between devices, on_device(): up1 = lax.ppermute(packet, 'gz', ring('gz', -1))  3.08 us
  transfers between devices with their start and end apart: 48, of which 17 were waited for; matrix products, arithmetic and copies ran while one was open for 0% of the time, Pallas kernels for 14%

profile of v7, /device:TPU:0, one launch (start us, length us, event | category | flops | bytes accessed | tf_op | source)
XLA Modules:
  0.0 136.2 jit_solution(5059443816507943918)
XLA Ops:
  1.8 3.1 %collective-permute-start.3 = (f32[8,128]{1,0:T(8,128)S(1)}, f32[8,128]{1,0:T(8,128)S(1)}, u32[]{:S(2)}, u32[]{:S(2)}) collective-permute-start(f32[8,128]{1,0:T(8,128)S(1)} %get-tuple-element.67), channel_id=1, source_target_pairs={{0,8},{4,12},{8,16},{12,20},{16,24},{20,28},{24,0},{28,4},{1,9},{5... | collective-permute-start | bytes 12296 | tf_op jit(solution)/shard_map/ppermute | solution.py:718
  4.8 2.1 %collective-permute-start.2 = (f32[8,128]{1,0:T(8,128)S(1)}, f32[8,128]{1,0:T(8,128)S(1)}, u32[]{:S(2)}, u32[]{:S(2)}) collective-permute-start(f32[8,128]{1,0:T(8,128)S(1)} %get-tuple-element.67), channel_id=1, source_target_pairs={{0,24},{4,28},{8,0},{12,4},{16,8},{20,12},{24,16},{28,20},{1,25},{... | collective-permute-start | bytes 12296 | tf_op jit(solution)/shard_map/ppermute | solution.py:717
  6.9 1.6 %collective-permute-start.1 = (f32[8,512]{1,0:T(8,128)S(1)}, f32[8,512]{1,0:T(8,128)S(1)}, u32[]{:S(2)}, u32[]{:S(2)}) collective-permute-start(f32[8,512]{1,0:T(8,128)S(1)} %get-tuple-element.66.own), channel_id=1, source_target_pairs={{0,4},{4,8},{8,12},{12,16},{16,20},{20,24},{24,28},{28,0},{1,5},{5... | collective-permute-start | bytes 49160 | tf_op jit(solution)/shard_map/ppermute | solution.py:716
  8.6 3.1 %collective-permute-start = (f32[8,512]{1,0:T(8,128)S(1)}, f32[8,512]{1,0:T(8,128)S(1)}, u32[]{:S(2)}, u32[]{:S(2)}) collective-permute-start(f32[8,512]{1,0:T(8,128)S(1)} %get-tuple-element.66.own), channel_id=1, source_target_pairs={{0,28},{4,0},{8,4},{12,8},{16,12},{20,16},{24,20},{28,24},{1,29},{... | collective-permute-start | bytes 49160 | tf_op jit(solution)/shard_map/ppermute | solution.py:715
  11.7 1.6 %collective-permute-done.1.down1 = f32[8,512]{1,0:T(8,128)S(1)} collective-permute-done((f32[8,512]{1,0:T(8,128)S(1)}, f32[8,512]{1,0:T(8,128)S(1)}, u32[]{:S(2)}, u32[]{:S(2)}) %collective-permute-start.1) | collective-permute-done | bytes 16416 | tf_op jit(solution)/shard_map/ppermute | solution.py:716
  13.4 3.9 %shard_map.141 = (f32[3,4,64,256]{3,2,1,0:T(8,128)S(1)}, f32[24,256]{1,0:T(8,128)S(1)}, f32[24,256]{1,0:T(8,128)S(1)}, f32[72,768]{1,0:T(8,128)S(1)}, f32[72,768...) custom-call(s32[2]{0:T(128)S(1)} %pad_add_fusion.place, f32[8,512]{1,0:T(8,128)S(1)} %get-tuple-element.66.own, ...), custom_call_target="tpu_custom_call" | custom-call | flops 5000000000 | bytes 15000000 | tf_op jit(solution)/shard_map/pallas_call | solution.py:646
  17.3 1.7 %collective-permute-start.16 = (f32[72,768]{1,0:T(8,128)S(1)}, f32[72,768]{1,0:T(8,128)S(1)}, u32[]{:S(2)}, u32[]{:S(2)}) collective-permute-start(f32[72,768]{1,0:T(8,128)S(1)} %get-tuple-element.85), channel_id=1, source_target_pairs={{0,2},{1,3},{2,0},{3,1},{4,6},{5,7},{6,4},{7,5},{8,10},{9,11},{10,... | collective-permute-start | bytes 663560 | tf_op jit(solution)/shard_map/ppermute | solution.py:681
  19.5 6.6 %shard_map.142 = (f32[3,4,64,256]{3,2,1,0:T(8,128)S(1)}, f32[48,256]{1,0:T(8,128)S(1)}, f32[48,256]{1,0:T(8,128)S(1)}, f32[72,768]{1,0:T(8,128)S(1)}, f32[72,768...) custom-call(s32[2]{0:T(128)S(1)} %pad_add_fusion.place, f32[8,512]{1,0:T(8,128)S(1)} %get-tuple-element.66.own, ...), custom_call_target="tpu_custom_call" | custom-call | flops 5000000000 | bytes 15000000 | tf_op jit(solution)/shard_map/pallas_call | solution.py:646
  26.1 1.7 %collective-permute-start.6 = (f32[72,768]{1,0:T(8,128)S(1)}, f32[72,768]{1,0:T(8,128)S(1)}, u32[]{:S(2)}, u32[]{:S(2)}) collective-permute-start(f32[72,768]{1,0:T(8,128)S(1)} %get-tuple-element.73), channel_id=1, source_target_pairs={{0,2},{1,3},{2,0},{3,1},{4,6},{5,7},{6,4},{7,5},{8,10},{9,11},{10,... | collective-permute-start | bytes 663560 | tf_op jit(solution)/shard_map/ppermute | solution.py:681
  28.4 1.6 %shard_map.145 = (f32[32,768]{1,0:T(8,128)S(1)}, f32[32,768]{1,0:T(8,128)S(1)}, f32[32,768]{1,0:T(8,128)S(1)}, f32[32,768]{1,0:T(8,128)S(1)}, f32[32,768]{1,0:T(...) custom-call(s32[2]{0:T(128)S(1)} %pad_add_fusion.place, ...), custom_call_target="tpu_custom_call" | custom-call | flops 2000000000 | bytes 6000000 | tf_op jit(solution)/shard_map/pallas_call | solution.py:646
  30.1 2.2 %collective-permute-start.20 = (f32[32,768]{1,0:T(8,128)S(1)}, f32[32,768]{1,0:T(8,128)S(1)}, u32[]{:S(2)}, u32[]{:S(2)}) collective-permute-start(f32[32,768]{1,0:T(8,128)S(1)} %get-tuple-element.90), channel_id=1, source_target_pairs={{0,20},{4,16},{8,28},{12,24},{16,4},{20,0},{24,12},{28,8},{1,21},{... | collective-permute-start | bytes 294920 | tf_op jit(solution)/shard_map/ppermute | solution.py:681
  32.2 2.3 %collective-permute-done.6.refs_1_ = f32[72,768]{1,0:T(8,128)S(1)} collective-permute-done((f32[72,768]{1,0:T(8,128)S(1)}, f32[72,768]{1,0:T(8,128)S(1)}, u32[]{:S(2)}, u32[]{:S(2)}) %collective-permute-start.6) | collective-permute-done | bytes 221216 | tf_op jit(solution)/shard_map/ppermute | solution.py:681
  34.5 3.0 %collective-permute-done.7.refs_2_ = f32[72,768]{1,0:T(8,128)S(1)} collective-permute-done((f32[72,768]{1,0:T(8,128)S(1)}, f32[72,768]{1,0:T(8,128)S(1)}, u32[]{:S(2)}, u32[]{:S(2)}) %collective-permute-start.7) | collective-permute-done | bytes 221216 | tf_op jit(solution)/shard_map/ppermute | solution.py:681
  37.5 2.4 %collective-permute-start.23 = (f32[32,768]{1,0:T(8,128)S(1)}, f32[32,768]{1,0:T(8,128)S(1)}, u32[]{:S(2)}, u32[]{:S(2)}) collective-permute-start(f32[32,768]{1,0:T(8,128)S(1)} %get-tuple-element.93), channel_id=1, source_target_pairs={{0,24},{4,28},{8,16},{12,20},{16,8},{20,12},{24,0},{28,4},{1,25},{... | collective-permute-start | bytes 294920 | tf_op jit(solution)/shard_map/ppermute | solution.py:681
  39.9 1.6 %shard_map.143 = (f32[32,768]{1,0:T(8,128)S(1)}, f32[32,768]{1,0:T(8,128)S(1)}, f32[32,768]{1,0:T(8,128)S(1)}, f32[32,768]{1,0:T(8,128)S(1)}, f32[32,768]{1,0:T(...) custom-call(s32[2]{0:T(128)S(1)} %pad_add_fusion.place, ...), custom_call_target="tpu_custom_call" | custom-call | flops 2000000000 | bytes 6000000 | tf_op jit(solution)/shard_map/pallas_call | solution.py:646
  41.5 2.4 %collective-permute-start.24 = (f32[32,768]{1,0:T(8,128)S(1)}, f32[32,768]{1,0:T(8,128)S(1)}, u32[]{:S(2)}, u32[]{:S(2)}) collective-permute-start(f32[32,768]{1,0:T(8,128)S(1)} %get-tuple-element.94), channel_id=1, source_target_pairs={{0,28},{4,24},{8,20},{12,16},{16,12},{20,8},{24,4},{28,0},{1,29},{... | collective-permute-start | bytes 294920 | tf_op jit(solution)/shard_map/ppermute | solution.py:681
  45.1 1.7 %collective-permute-start.9 = (f32[32,768]{1,0:T(8,128)S(1)}, f32[32,768]{1,0:T(8,128)S(1)}, u32[]{:S(2)}, u32[]{:S(2)}) collective-permute-start(f32[32,768]{1,0:T(8,128)S(1)} %get-tuple-element.77), channel_id=1, source_target_pairs={{0,16},{4,20},{8,24},{12,28},{16,0},{20,4},{24,8},{28,12},{1,17},{... | collective-permute-start | bytes 294920 | tf_op jit(solution)/shard_map/ppermute | solution.py:681
  46.8 2.4 %collective-permute-start.10 = (f32[32,768]{1,0:T(8,128)S(1)}, f32[32,768]{1,0:T(8,128)S(1)}, u32[]{:S(2)}, u32[]{:S(2)}) collective-permute-start(f32[32,768]{1,0:T(8,128)S(1)} %get-tuple-element.78), channel_id=1, source_target_pairs={{0,20},{4,16},{8,28},{12,24},{16,4},{20,0},{24,12},{28,8},{1,21},{... | collective-permute-start | bytes 294920 | tf_op jit(solution)/shard_map/ppermute | solution.py:681
  50.1 7.6 %collective-permute-start.12 = (f32[32,768]{1,0:T(8,128)S(1)}, f32[32,768]{1,0:T(8,128)S(1)}, u32[]{:S(2)}, u32[]{:S(2)}) collective-permute-start(f32[32,768]{1,0:T(8,128)S(1)} %get-tuple-element.80), channel_id=1, source_target_pairs={{0,8},{4,12},{8,0},{12,4},{16,24},{20,28},{24,16},{28,20},{1,9},{5... | collective-permute-start | bytes 294920 | tf_op jit(solution)/shard_map/ppermute | solution.py:681
  57.7 2.7 %collective-permute-start.13 = (f32[32,768]{1,0:T(8,128)S(1)}, f32[32,768]{1,0:T(8,128)S(1)}, u32[]{:S(2)}, u32[]{:S(2)}) collective-permute-start(f32[32,768]{1,0:T(8,128)S(1)} %get-tuple-element.81), channel_id=1, source_target_pairs={{0,24},{4,28},{8,16},{12,20},{16,8},{20,12},{24,0},{28,4},{1,25},{... | collective-permute-start | bytes 294920 | tf_op jit(solution)/shard_map/ppermute | solution.py:681
  60.5 1.6 %collective-permute-start.14 = (f32[32,768]{1,0:T(8,128)S(1)}, f32[32,768]{1,0:T(8,128)S(1)}, u32[]{:S(2)}, u32[]{:S(2)}) collective-permute-start(f32[32,768]{1,0:T(8,128)S(1)} %get-tuple-element.82), channel_id=1, source_target_pairs={{0,28},{4,24},{8,20},{12,16},{16,12},{20,8},{24,4},{28,0},{1,29},{... | collective-permute-start | bytes 294920 | tf_op jit(solution)/shard_map/ppermute | solution.py:681
  64.9 1.7 %collective-permute-start.5 = (f32[48,256]{1,0:T(8,128)S(1)}, f32[48,256]{1,0:T(8,128)S(1)}, u32[]{:S(2)}, u32[]{:S(2)}) collective-permute-start(f32[48,256]{1,0:T(8,128)S(1)} %get-tuple-element.71), channel_id=1, source_target_pairs={{0,3},{1,0},{2,1},{3,2},{4,7},{5,4},{6,5},{7,6},{8,11},{9,8},{10,9... | collective-permute-start | bytes 147464 | tf_op jit(solution)/shard_map/ppermute | solution.py:740
  66.6 1.4 %collective-permute-done.14.refs_6_ = f32[32,768]{1,0:T(8,128)S(1)} collective-permute-done((f32[32,768]{1,0:T(8,128)S(1)}, f32[32,768]{1,0:T(8,128)S(1)}, u32[]{:S(2)}, u32[]{:S(2)}) %collective-permute-start.14) | collective-permute-done | bytes 98336 | tf_op jit(solution)/shard_map/ppermute | solution.py:681
  68.1 1.7 %collective-permute-done.15.refs_7_ = f32[32,768]{1,0:T(8,128)S(1)} collective-permute-done((f32[32,768]{1,0:T(8,128)S(1)}, f32[32,768]{1,0:T(8,128)S(1)}, u32[]{:S(2)}, u32[]{:S(2)}) %collective-permute-start.15) | collective-permute-done | bytes 98336 | tf_op jit(solution)/shard_map/ppermute | solution.py:681
  71.1 2.3 %shard_map.147 = (f32[3,2,4,8,8,128]{5,4,3,2,1,0:T(8,128)S(1)}, f32[3,2,4,8,8,128]{5,4,3,2,1,0:T(8,128)S(1)}) custom-call(s32[2]{0:T(128)S(1)} %pad_add_fusion.place, f32[48,256]{1,0:T(8,128)S(1)} %collective-permute-done.4.low_rim.refs_2_, f32[48,256]{1,0:T(8,128)S(1)} %collective-permute-done.5.high_rim.refs_3_, ...), custom_call_target="tpu_custom_call" | custom-call | flops 5000000000 | bytes 15000000 | tf_op jit(solution)/shard_map/pallas_call | solution.py:646
  73.4 1.4 %shard_map.148 = (f32[32,768]{1,0:T(8,128)S(1)}, f32[32,768]{1,0:T(8,128)S(1)}, f32[32,768]{1,0:T(8,128)S(1)}, f32[32,768]{1,0:T(8,128)S(1)}, f32[32,768]{1,0:T(...) custom-call(s32[2]{0:T(128)S(1)} %pad_add_fusion.place, ...), custom_call_target="tpu_custom_call" | custom-call | flops 2000000000 | bytes 6000000 | tf_op jit(solution)/shard_map/pallas_call | solution.py:646
  74.8 2.0 %collective-permute-start.26 = (f32[32,768]{1,0:T(8,128)S(1)}, f32[32,768]{1,0:T(8,128)S(1)}, u32[]{:S(2)}, u32[]{:S(2)}) collective-permute-start(f32[32,768]{1,0:T(8,128)S(1)} %get-tuple-element.98), channel_id=1, source_target_pairs={{0,16},{4,20},{8,24},{12,28},{16,0},{20,4},{24,8},{28,12},{1,17},{... | collective-permute-start | bytes 294920 | tf_op jit(solution)/shard_map/ppermute | solution.py:681
  76.8 1.4 %collective-permute-start.27 = (f32[32,768]{1,0:T(8,128)S(1)}, f32[32,768]{1,0:T(8,128)S(1)}, u32[]{:S(2)}, u32[]{:S(2)}) collective-permute-start(f32[32,768]{1,0:T(8,128)S(1)} %get-tuple-element.99), channel_id=1, source_target_pairs={{0,20},{4,16},{8,28},{12,24},{16,4},{20,0},{24,12},{28,8},{1,21},{... | collective-permute-start | bytes 294920 | tf_op jit(solution)/shard_map/ppermute | solution.py:681
  80.1 2.6 %collective-permute-start.30 = (f32[32,768]{1,0:T(8,128)S(1)}, f32[32,768]{1,0:T(8,128)S(1)}, u32[]{:S(2)}, u32[]{:S(2)}) collective-permute-start(f32[32,768]{1,0:T(8,128)S(1)} %get-tuple-element.102), channel_id=1, source_target_pairs={{0,24},{4,28},{8,16},{12,20},{16,8},{20,12},{24,0},{28,4},{1,25},{... | collective-permute-start | bytes 294920 | tf_op jit(solution)/shard_map/ppermute | solution.py:681
  82.7 3.2 %collective-permute-done.26.refs_1_ = f32[32,768]{1,0:T(8,128)S(1)} collective-permute-done((f32[32,768]{1,0:T(8,128)S(1)}, f32[32,768]{1,0:T(8,128)S(1)}, u32[]{:S(2)}, u32[]{:S(2)}) %collective-permute-start.26) | collective-permute-done | bytes 98336 | tf_op jit(solution)/shard_map/ppermute | solution.py:681
  85.8 2.1 %collective-permute-start.31 = (f32[32,768]{1,0:T(8,128)S(1)}, f32[32,768]{1,0:T(8,128)S(1)}, u32[]{:S(2)}, u32[]{:S(2)}) collective-permute-start(f32[32,768]{1,0:T(8,128)S(1)} %get-tuple-element.103), channel_id=1, source_target_pairs={{0,28},{4,24},{8,20},{12,16},{16,12},{20,8},{24,4},{28,0},{1,29},{... | collective-permute-start | bytes 294920 | tf_op jit(solution)/shard_map/ppermute | solution.py:681
  87.9 2.5 %collective-permute-done.27.refs_2_ = f32[32,768]{1,0:T(8,128)S(1)} collective-permute-done((f32[32,768]{1,0:T(8,128)S(1)}, f32[32,768]{1,0:T(8,128)S(1)}, u32[]{:S(2)}, u32[]{:S(2)}) %collective-permute-start.27) | collective-permute-done | bytes 98336 | tf_op jit(solution)/shard_map/ppermute | solution.py:681
  90.4 1.4 %shard_map.152 = (f32[32,768]{1,0:T(8,128)S(1)}, f32[32,768]{1,0:T(8,128)S(1)}, f32[32,768]{1,0:T(8,128)S(1)}, f32[32,768]{1,0:T(8,128)S(1)}, f32[32,768]{1,0:T(...) custom-call(s32[2]{0:T(128)S(1)} %pad_add_fusion.place, ...), custom_call_target="tpu_custom_call" | custom-call | flops 2000000000 | bytes 6000000 | tf_op jit(solution)/shard_map/pallas_call | solution.py:646
  91.8 3.3 %collective-permute-start.38 = (f32[32,768]{1,0:T(8,128)S(1)}, f32[32,768]{1,0:T(8,128)S(1)}, u32[]{:S(2)}, u32[]{:S(2)}) collective-permute-start(f32[32,768]{1,0:T(8,128)S(1)} %get-tuple-element.116), channel_id=1, source_target_pairs={{0,16},{4,20},{8,24},{12,28},{16,0},{20,4},{24,8},{28,12},{1,17},{... | collective-permute-start | bytes 294920 | tf_op jit(solution)/shard_map/ppermute | solution.py:681
  96.3 1.7 %shard_map.149 = (f32[72,768]{1,0:T(8,128)S(1)}, f32[72,768]{1,0:T(8,128)S(1)}, f32[72,768]{1,0:T(8,128)S(1)}, f32[72,768]{1,0:T(8,128)S(1)}) custom-call(s32[2]{0:T(128)S(1)} %pad_add_fusion.place, bf16[576,256]{1,0:T(8,128)(2,1)S(1)} %copy-done.6, bf16[576,256]{1,0:T(8,128)(2,1)S(1)} %copy-done.5, f32[32,768]{1,0:T(8,128)S(1)} %get-tuple-element.97.refs_0_, ...), custom_call_target="tpu_custom_call" | custom-call | flops 2000000000 | bytes 6000000 | tf_op jit(solution)/shard_map/pallas_call | solution.py:646
  98.0 1.9 %collective-permute-start.33 = (f32[72,768]{1,0:T(8,128)S(1)}, f32[72,768]{1,0:T(8,128)S(1)}, u32[]{:S(2)}, u32[]{:S(2)}) collective-permute-start(f32[72,768]{1,0:T(8,128)S(1)} %get-tuple-element.106), channel_id=1, source_target_pairs={{0,2},{1,3},{2,0},{3,1},{4,6},{5,7},{6,4},{7,5},{8,10},{9,11},{10,... | collective-permute-start | bytes 663560 | tf_op jit(solution)/shard_map/ppermute | solution.py:681
  100.2 1.6 %collective-permute-done.38.refs_0_.refs_2_ = f32[32,768]{1,0:T(8,128)S(1)} collective-permute-done((f32[32,768]{1,0:T(8,128)S(1)}, f32[32,768]{1,0:T(8,128)S(1)}, u32[]{:S(2)}, u32[]{:S(2)}) %collective-permute-start.38) | collective-permute-done | bytes 98336 | tf_op jit(solution)/shard_map/ppermute | solution.py:681
  103.3 3.1 %collective-permute-done.40.refs_2_.refs_4_ = f32[32,768]{1,0:T(8,128)S(1)} collective-permute-done((f32[32,768]{1,0:T(8,128)S(1)}, f32[32,768]{1,0:T(8,128)S(1)}, u32[]{:S(2)}, u32[]{:S(2)}) %collective-permute-start.40) | collective-permute-done | bytes 98336 | tf_op jit(solution)/shard_map/ppermute | solution.py:681
  106.4 1.5 %collective-permute-done.41.refs_3_.refs_5_ = f32[32,768]{1,0:T(8,128)S(1)} collective-permute-done((f32[32,768]{1,0:T(8,128)S(1)}, f32[32,768]{1,0:T(8,128)S(1)}, u32[]{:S(2)}, u32[]{:S(2)}) %collective-permute-start.41) | collective-permute-done | bytes 98336 | tf_op jit(solution)/shard_map/ppermute | solution.py:681
  107.9 2.6 %collective-permute-start.42 = (f32[32,768]{1,0:T(8,128)S(1)}, f32[32,768]{1,0:T(8,128)S(1)}, u32[]{:S(2)}, u32[]{:S(2)}) collective-permute-start(f32[32,768]{1,0:T(8,128)S(1)} %get-tuple-element.123), channel_id=1, source_target_pairs={{0,24},{4,28},{8,16},{12,20},{16,8},{20,12},{24,0},{28,4},{1,25},{... | collective-permute-start | bytes 294920 | tf_op jit(solution)/shard_map/ppermute | solution.py:681
  110.5 1.8 %collective-permute-start.43 = (f32[32,768]{1,0:T(8,128)S(1)}, f32[32,768]{1,0:T(8,128)S(1)}, u32[]{:S(2)}, u32[]{:S(2)}) collective-permute-start(f32[32,768]{1,0:T(8,128)S(1)} %get-tuple-element.124), channel_id=1, source_target_pairs={{0,28},{4,24},{8,20},{12,16},{16,12},{20,8},{24,4},{28,0},{1,29},{... | collective-permute-start | bytes 294920 | tf_op jit(solution)/shard_map/ppermute | solution.py:681
  112.3 1.5 %shard_map.150 = (f32[3,4,80,256]{3,2,1,0:T(8,128)S(1)}, f32[3,64,256]{2,1,0:T(8,128)S(1)}, f32[3,64,256]{2,1,0:T(8,128)S(1)}) custom-call(s32[2]{0:T(128)S(1)} %pad_add_fusion.place, bf16[512,512]{1,0:T(8,128)(2,1)S(1)} %copy-done.2, bf16[512,512]{1,0:T(8,128)(2,1)S(1)} %copy-done.1, f32[72,768]{1,0:T(8,128)S(1)} %get-tuple-element.105.refs_0_.before, ...), custom_call_target="tpu_custom_call" | custom-call | flops 2000000000 | bytes 6000000 | tf_op jit(solution)/shard_map/pallas_call | solution.py:646
  114.8 3.7 %collective-permute-start.37 = (f32[3,64,256]{2,1,0:T(8,128)S(1)}, f32[3,64,256]{2,1,0:T(8,128)S(1)}, u32[]{:S(2)}, u32[]{:S(2)}) collective-permute-start(f32[3,64,256]{2,1,0:T(8,128)S(1)} %get-tuple-element.111.refs_0_), channel_id=1, source_target_pairs={{0,28},{4,0},{8,4},{12,8},{16,12},{20,16},{24,20},{28,24},{1,29},{... | collective-permute-start | bytes 589832 | tf_op jit(solution)/shard_map/ppermute | solution.py:810
  119.2 3.9 %collective-permute-done.44.refs_8_ = f32[32,768]{1,0:T(8,128)S(1)} collective-permute-done((f32[32,768]{1,0:T(8,128)S(1)}, f32[32,768]{1,0:T(8,128)S(1)}, u32[]{:S(2)}, u32[]{:S(2)}) %collective-permute-start.44) | collective-permute-done | bytes 98336 | tf_op jit(solution)/shard_map/ppermute | solution.py:681
  123.1 1.7 %shard_map.154 = (f32[72,768]{1,0:T(8,128)S(1)}, f32[72,768]{1,0:T(8,128)S(1)}, f32[72,768]{1,0:T(8,128)S(1)}, f32[72,768]{1,0:T(8,128)S(1)}) custom-call(s32[2]{0:T(128)S(1)} %pad_add_fusion.place, bf16[576,256]{1,0:T(8,128)(2,1)S(1)} %copy-done.6, bf16[576,256]{1,0:T(8,128)(2,1)S(1)} %copy-done.5, f32[3,64,256]{2,1,0:T(8,128)S(1)} %get-tuple-element.111.refs_0_, ...), custom_call_target="tpu_custom_call" | custom-call | flops 2000000000 | bytes 6000000 | tf_op jit(solution)/shard_map/pallas_call | solution.py:646
  124.9 2.0 %collective-permute-start.47 = (f32[72,768]{1,0:T(8,128)S(1)}, f32[72,768]{1,0:T(8,128)S(1)}, u32[]{:S(2)}, u32[]{:S(2)}) collective-permute-start(f32[72,768]{1,0:T(8,128)S(1)} %get-tuple-element.129), channel_id=1, source_target_pairs={{0,1},{1,0},{2,3},{3,2},{4,5},{5,4},{6,7},{7,6},{8,9},{9,8},{10,11... | collective-permute-start | bytes 663560 | tf_op jit(solution)/shard_map/ppermute | solution.py:681
  127.4 5.3 %collective-permute-done.45.refs_7_ = f32[72,768]{1,0:T(8,128)S(1)} collective-permute-done((f32[72,768]{1,0:T(8,128)S(1)}, f32[72,768]{1,0:T(8,128)S(1)}, u32[]{:S(2)}, u32[]{:S(2)}) %collective-permute-start.45) | collective-permute-done | bytes 221216 | tf_op jit(solution)/shard_map/ppermute | solution.py:681
  133.1 3.0 %shard_map.155 = (f32[3,8,64,256]{3,2,1,0:T(8,128)}, f32[3,8,64,256]{3,2,1,0:T(8,128)}) custom-call(s32[2]{0:T(128)S(1)} %pad_add_fusion.place, bf16[512,512]{1,0:T(8,128)(2,1)S(1)} %copy-done.2, bf16[512,512]{1,0:T(8,128)(2,1)S(1)} %copy-done.1, f32[3,4,80,256]{3,2,1,0:T(8,128)S(1)} %get-tuple-element.109.edges.refs_0_, ...), custom_call_target="tpu_custom_call" | custom-call | flops 4000000000 | bytes 12000000 | tf_op jit(solution)/shard_map/pallas_call | solution.py:646
  (83 shorter events, 15.8 us)
Async XLA Ops:
  1.8 10.0 %collective-permute-start.3 = (f32[8,128]{1,0:T(8,128)S(1)}, f32[8,128]{1,0:T(8,128)S(1)}, u32[]{:S(2)}, u32[]{:S(2)}) collective-permute-start(f32[8,128]{1,0:T(8,128)S(1)} %get-tuple-element.67), channel_id=1, source_target_pairs={{0,8},{4,12},{8,16},{12,20},{16,24},{20,28},{24,0},{28,4},{1,9},{5... | collective-permute-start | bytes 12296 | tf_op jit(solution)/shard_map/ppermute | solution.py:718
  4.8 6.9 %collective-permute-start.2 = (f32[8,128]{1,0:T(8,128)S(1)}, f32[8,128]{1,0:T(8,128)S(1)}, u32[]{:S(2)}, u32[]{:S(2)}) collective-permute-start(f32[8,128]{1,0:T(8,128)S(1)} %get-tuple-element.67), channel_id=1, source_target_pairs={{0,24},{4,28},{8,0},{12,4},{16,8},{20,12},{24,16},{28,20},{1,25},{... | collective-permute-start | bytes 12296 | tf_op jit(solution)/shard_map/ppermute | solution.py:717
  6.9 6.4 %collective-permute-start.1 = (f32[8,512]{1,0:T(8,128)S(1)}, f32[8,512]{1,0:T(8,128)S(1)}, u32[]{:S(2)}, u32[]{:S(2)}) collective-permute-start(f32[8,512]{1,0:T(8,128)S(1)} %get-tuple-element.66.own), channel_id=1, source_target_pairs={{0,4},{4,8},{8,12},{12,16},{16,20},{20,24},{24,28},{28,0},{1,5},{5... | collective-permute-start | bytes 49160 | tf_op jit(solution)/shard_map/ppermute | solution.py:716
  8.6 4.8 %collective-permute-start = (f32[8,512]{1,0:T(8,128)S(1)}, f32[8,512]{1,0:T(8,128)S(1)}, u32[]{:S(2)}, u32[]{:S(2)}) collective-permute-start(f32[8,512]{1,0:T(8,128)S(1)} %get-tuple-element.66.own), channel_id=1, source_target_pairs={{0,28},{4,0},{8,4},{12,8},{16,12},{20,16},{24,20},{28,24},{1,29},{... | collective-permute-start | bytes 49160 | tf_op jit(solution)/shard_map/ppermute | solution.py:715
  17.3 10.6 %collective-permute-start.16 = (f32[72,768]{1,0:T(8,128)S(1)}, f32[72,768]{1,0:T(8,128)S(1)}, u32[]{:S(2)}, u32[]{:S(2)}) collective-permute-start(f32[72,768]{1,0:T(8,128)S(1)} %get-tuple-element.85), channel_id=1, source_target_pairs={{0,2},{1,3},{2,0},{3,1},{4,6},{5,7},{6,4},{7,5},{8,10},{9,11},{10,... | collective-permute-start | bytes 663560 | tf_op jit(solution)/shard_map/ppermute | solution.py:681
  19.1 9.3 %collective-permute-start.17 = (f32[72,768]{1,0:T(8,128)S(1)}, f32[72,768]{1,0:T(8,128)S(1)}, u32[]{:S(2)}, u32[]{:S(2)}) collective-permute-start(f32[72,768]{1,0:T(8,128)S(1)} %get-tuple-element.86), channel_id=1, source_target_pairs={{0,3},{1,2},{2,1},{3,0},{4,7},{5,6},{6,5},{7,4},{8,11},{9,10},{10,... | collective-permute-start | bytes 663560 | tf_op jit(solution)/shard_map/ppermute | solution.py:681
  19.1 9.3 %collective-permute-start.18 = (f32[72,768]{1,0:T(8,128)S(1)}, f32[72,768]{1,0:T(8,128)S(1)}, u32[]{:S(2)}, u32[]{:S(2)}) collective-permute-start(f32[72,768]{1,0:T(8,128)S(1)} %get-tuple-element.87), channel_id=1, source_target_pairs={{0,1},{1,0},{2,3},{3,2},{4,5},{5,4},{6,7},{7,6},{8,9},{9,8},{10,11... | collective-permute-start | bytes 663560 | tf_op jit(solution)/shard_map/ppermute | solution.py:681
  26.1 8.4 %collective-permute-start.6 = (f32[72,768]{1,0:T(8,128)S(1)}, f32[72,768]{1,0:T(8,128)S(1)}, u32[]{:S(2)}, u32[]{:S(2)}) collective-permute-start(f32[72,768]{1,0:T(8,128)S(1)} %get-tuple-element.73), channel_id=1, source_target_pairs={{0,2},{1,3},{2,0},{3,1},{4,6},{5,7},{6,4},{7,5},{8,10},{9,11},{10,... | collective-permute-start | bytes 663560 | tf_op jit(solution)/shard_map/ppermute | solution.py:681
  27.9 9.6 %collective-permute-start.7 = (f32[72,768]{1,0:T(8,128)S(1)}, f32[72,768]{1,0:T(8,128)S(1)}, u32[]{:S(2)}, u32[]{:S(2)}) collective-permute-start(f32[72,768]{1,0:T(8,128)S(1)} %get-tuple-element.74), channel_id=1, source_target_pairs={{0,3},{1,2},{2,1},{3,0},{4,7},{5,6},{6,5},{7,4},{8,11},{9,10},{10,... | collective-permute-start | bytes 663560 | tf_op jit(solution)/shard_map/ppermute | solution.py:681
  27.9 9.6 %collective-permute-start.8 = (f32[72,768]{1,0:T(8,128)S(1)}, f32[72,768]{1,0:T(8,128)S(1)}, u32[]{:S(2)}, u32[]{:S(2)}) collective-permute-start(f32[72,768]{1,0:T(8,128)S(1)} %get-tuple-element.75), channel_id=1, source_target_pairs={{0,1},{1,0},{2,3},{3,2},{4,5},{5,4},{6,7},{7,6},{8,9},{9,8},{10,11... | collective-permute-start | bytes 663560 | tf_op jit(solution)/shard_map/ppermute | solution.py:681
  30.0 11.5 %collective-permute-start.19 = (f32[32,768]{1,0:T(8,128)S(1)}, f32[32,768]{1,0:T(8,128)S(1)}, u32[]{:S(2)}, u32[]{:S(2)}) collective-permute-start(f32[32,768]{1,0:T(8,128)S(1)} %get-tuple-element.89), channel_id=1, source_target_pairs={{0,16},{4,20},{8,24},{12,28},{16,0},{20,4},{24,8},{28,12},{1,17},{... | collective-permute-start | bytes 294920 | tf_op jit(solution)/shard_map/ppermute | solution.py:681
  30.1 13.8 %collective-permute-start.20 = (f32[32,768]{1,0:T(8,128)S(1)}, f32[32,768]{1,0:T(8,128)S(1)}, u32[]{:S(2)}, u32[]{:S(2)}) collective-permute-start(f32[32,768]{1,0:T(8,128)S(1)} %get-tuple-element.90), channel_id=1, source_target_pairs={{0,20},{4,16},{8,28},{12,24},{16,4},{20,0},{24,12},{28,8},{1,21},{... | collective-permute-start | bytes 294920 | tf_op jit(solution)/shard_map/ppermute | solution.py:681
  34.5 10.6 %collective-permute-start.21 = (f32[32,768]{1,0:T(8,128)S(1)}, f32[32,768]{1,0:T(8,128)S(1)}, u32[]{:S(2)}, u32[]{:S(2)}) collective-permute-start(f32[32,768]{1,0:T(8,128)S(1)} %get-tuple-element.91), channel_id=1, source_target_pairs={{0,4},{4,0},{8,12},{12,8},{16,20},{20,16},{24,28},{28,24},{1,5},{5... | collective-permute-start | bytes 294920 | tf_op jit(solution)/shard_map/ppermute | solution.py:681
  37.5 9.3 %collective-permute-start.22 = (f32[32,768]{1,0:T(8,128)S(1)}, f32[32,768]{1,0:T(8,128)S(1)}, u32[]{:S(2)}, u32[]{:S(2)}) collective-permute-start(f32[32,768]{1,0:T(8,128)S(1)} %get-tuple-element.92), channel_id=1, source_target_pairs={{0,8},{4,12},{8,0},{12,4},{16,24},{20,28},{24,16},{28,20},{1,9},{5... | collective-permute-start | bytes 294920 | tf_op jit(solution)/shard_map/ppermute | solution.py:681
  37.5 11.8 %collective-permute-start.23 = (f32[32,768]{1,0:T(8,128)S(1)}, f32[32,768]{1,0:T(8,128)S(1)}, u32[]{:S(2)}, u32[]{:S(2)}) collective-permute-start(f32[32,768]{1,0:T(8,128)S(1)} %get-tuple-element.93), channel_id=1, source_target_pairs={{0,24},{4,28},{8,16},{12,20},{16,8},{20,12},{24,0},{28,4},{1,25},{... | collective-permute-start | bytes 294920 | tf_op jit(solution)/shard_map/ppermute | solution.py:681
  41.5 8.6 %collective-permute-start.24 = (f32[32,768]{1,0:T(8,128)S(1)}, f32[32,768]{1,0:T(8,128)S(1)}, u32[]{:S(2)}, u32[]{:S(2)}) collective-permute-start(f32[32,768]{1,0:T(8,128)S(1)} %get-tuple-element.94), channel_id=1, source_target_pairs={{0,28},{4,24},{8,20},{12,16},{16,12},{20,8},{24,4},{28,0},{1,29},{... | collective-permute-start | bytes 294920 | tf_op jit(solution)/shard_map/ppermute | solution.py:681
  43.9 13.9 %collective-permute-start.25 = (f32[32,768]{1,0:T(8,128)S(1)}, f32[32,768]{1,0:T(8,128)S(1)}, u32[]{:S(2)}, u32[]{:S(2)}) collective-permute-start(f32[32,768]{1,0:T(8,128)S(1)} %get-tuple-element.95), channel_id=1, source_target_pairs={{0,12},{4,8},{8,4},{12,0},{16,28},{20,24},{24,20},{28,16},{1,13},{... | collective-permute-start | bytes 294920 | tf_op jit(solution)/shard_map/ppermute | solution.py:681
  45.1 15.4 %collective-permute-start.9 = (f32[32,768]{1,0:T(8,128)S(1)}, f32[32,768]{1,0:T(8,128)S(1)}, u32[]{:S(2)}, u32[]{:S(2)}) collective-permute-start(f32[32,768]{1,0:T(8,128)S(1)} %get-tuple-element.77), channel_id=1, source_target_pairs={{0,16},{4,20},{8,24},{12,28},{16,0},{20,4},{24,8},{28,12},{1,17},{... | collective-permute-start | bytes 294920 | tf_op jit(solution)/shard_map/ppermute | solution.py:681
  46.8 15.7 %collective-permute-start.10 = (f32[32,768]{1,0:T(8,128)S(1)}, f32[32,768]{1,0:T(8,128)S(1)}, u32[]{:S(2)}, u32[]{:S(2)}) collective-permute-start(f32[32,768]{1,0:T(8,128)S(1)} %get-tuple-element.78), channel_id=1, source_target_pairs={{0,20},{4,16},{8,28},{12,24},{16,4},{20,0},{24,12},{28,8},{1,21},{... | collective-permute-start | bytes 294920 | tf_op jit(solution)/shard_map/ppermute | solution.py:681
  49.2 15.6 %collective-permute-start.11 = (f32[32,768]{1,0:T(8,128)S(1)}, f32[32,768]{1,0:T(8,128)S(1)}, u32[]{:S(2)}, u32[]{:S(2)}) collective-permute-start(f32[32,768]{1,0:T(8,128)S(1)} %get-tuple-element.79), channel_id=1, source_target_pairs={{0,4},{4,0},{8,12},{12,8},{16,20},{20,16},{24,28},{28,24},{1,5},{5... | collective-permute-start | bytes 294920 | tf_op jit(solution)/shard_map/ppermute | solution.py:681
  50.1 14.8 %collective-permute-start.12 = (f32[32,768]{1,0:T(8,128)S(1)}, f32[32,768]{1,0:T(8,128)S(1)}, u32[]{:S(2)}, u32[]{:S(2)}) collective-permute-start(f32[32,768]{1,0:T(8,128)S(1)} %get-tuple-element.80), channel_id=1, source_target_pairs={{0,8},{4,12},{8,0},{12,4},{16,24},{20,28},{24,16},{28,20},{1,9},{5... | collective-permute-start | bytes 294920 | tf_op jit(solution)/shard_map/ppermute | solution.py:681
  57.7 8.9 %collective-permute-start.13 = (f32[32,768]{1,0:T(8,128)S(1)}, f32[32,768]{1,0:T(8,128)S(1)}, u32[]{:S(2)}, u32[]{:S(2)}) collective-permute-start(f32[32,768]{1,0:T(8,128)S(1)} %get-tuple-element.81), channel_id=1, source_target_pairs={{0,24},{4,28},{8,16},{12,20},{16,8},{20,12},{24,0},{28,4},{1,25},{... | collective-permute-start | bytes 294920 | tf_op jit(solution)/shard_map/ppermute | solution.py:681
  60.5 7.6 %collective-permute-start.14 = (f32[32,768]{1,0:T(8,128)S(1)}, f32[32,768]{1,0:T(8,128)S(1)}, u32[]{:S(2)}, u32[]{:S(2)}) collective-permute-start(f32[32,768]{1,0:T(8,128)S(1)} %get-tuple-element.82), channel_id=1, source_target_pairs={{0,28},{4,24},{8,20},{12,16},{16,12},{20,8},{24,4},{28,0},{1,29},{... | collective-permute-start | bytes 294920 | tf_op jit(solution)/shard_map/ppermute | solution.py:681
  62.5 7.3 %collective-permute-start.15 = (f32[32,768]{1,0:T(8,128)S(1)}, f32[32,768]{1,0:T(8,128)S(1)}, u32[]{:S(2)}, u32[]{:S(2)}) collective-permute-start(f32[32,768]{1,0:T(8,128)S(1)} %get-tuple-element.83), channel_id=1, source_target_pairs={{0,12},{4,8},{8,4},{12,0},{16,28},{20,24},{24,20},{28,16},{1,13},{... | collective-permute-start | bytes 294920 | tf_op jit(solution)/shard_map/ppermute | solution.py:681
  64.8 6.3 %collective-permute-start.4 = (f32[48,256]{1,0:T(8,128)S(1)}, f32[48,256]{1,0:T(8,128)S(1)}, u32[]{:S(2)}, u32[]{:S(2)}) collective-permute-start(f32[48,256]{1,0:T(8,128)S(1)} %get-tuple-element.70), channel_id=1, source_target_pairs={{0,1},{1,2},{2,3},{3,0},{4,5},{5,6},{6,7},{7,4},{8,9},{9,10},{10,1... | collective-permute-start | bytes 147464 | tf_op jit(solution)/shard_map/ppermute | solution.py:739
  64.9 6.2 %collective-permute-start.5 = (f32[48,256]{1,0:T(8,128)S(1)}, f32[48,256]{1,0:T(8,128)S(1)}, u32[]{:S(2)}, u32[]{:S(2)}) collective-permute-start(f32[48,256]{1,0:T(8,128)S(1)} %get-tuple-element.71), channel_id=1, source_target_pairs={{0,3},{1,0},{2,1},{3,2},{4,7},{5,4},{6,5},{7,6},{8,11},{9,8},{10,9... | collective-permute-start | bytes 147464 | tf_op jit(solution)/shard_map/ppermute | solution.py:740
  74.8 11.0 %collective-permute-start.26 = (f32[32,768]{1,0:T(8,128)S(1)}, f32[32,768]{1,0:T(8,128)S(1)}, u32[]{:S(2)}, u32[]{:S(2)}) collective-permute-start(f32[32,768]{1,0:T(8,128)S(1)} %get-tuple-element.98), channel_id=1, source_target_pairs={{0,16},{4,20},{8,24},{12,28},{16,0},{20,4},{24,8},{28,12},{1,17},{... | collective-permute-start | bytes 294920 | tf_op jit(solution)/shard_map/ppermute | solution.py:681
  76.8 13.6 %collective-permute-start.27 = (f32[32,768]{1,0:T(8,128)S(1)}, f32[32,768]{1,0:T(8,128)S(1)}, u32[]{:S(2)}, u32[]{:S(2)}) collective-permute-start(f32[32,768]{1,0:T(8,128)S(1)} %get-tuple-element.99), channel_id=1, source_target_pairs={{0,20},{4,16},{8,28},{12,24},{16,4},{20,0},{24,12},{28,8},{1,21},{... | collective-permute-start | bytes 294920 | tf_op jit(solution)/shard_map/ppermute | solution.py:681
  78.2 13.6 %collective-permute-start.28 = (f32[32,768]{1,0:T(8,128)S(1)}, f32[32,768]{1,0:T(8,128)S(1)}, u32[]{:S(2)}, u32[]{:S(2)}) collective-permute-start(f32[32,768]{1,0:T(8,128)S(1)} %get-tuple-element.100), channel_id=1, source_target_pairs={{0,4},{4,0},{8,12},{12,8},{16,20},{20,16},{24,28},{28,24},{1,5},{5... | collective-permute-start | bytes 294920 | tf_op jit(solution)/shard_map/ppermute | solution.py:681
  79.3 15.8 %collective-permute-start.29 = (f32[32,768]{1,0:T(8,128)S(1)}, f32[32,768]{1,0:T(8,128)S(1)}, u32[]{:S(2)}, u32[]{:S(2)}) collective-permute-start(f32[32,768]{1,0:T(8,128)S(1)} %get-tuple-element.101), channel_id=1, source_target_pairs={{0,8},{4,12},{8,0},{12,4},{16,24},{20,28},{24,16},{28,20},{1,9},{5... | collective-permute-start | bytes 294920 | tf_op jit(solution)/shard_map/ppermute | solution.py:681
  80.1 16.2 %collective-permute-start.30 = (f32[32,768]{1,0:T(8,128)S(1)}, f32[32,768]{1,0:T(8,128)S(1)}, u32[]{:S(2)}, u32[]{:S(2)}) collective-permute-start(f32[32,768]{1,0:T(8,128)S(1)} %get-tuple-element.102), channel_id=1, source_target_pairs={{0,24},{4,28},{8,16},{12,20},{16,8},{20,12},{24,0},{28,4},{1,25},{... | collective-permute-start | bytes 294920 | tf_op jit(solution)/shard_map/ppermute | solution.py:681
  85.8 10.4 %collective-permute-start.31 = (f32[32,768]{1,0:T(8,128)S(1)}, f32[32,768]{1,0:T(8,128)S(1)}, u32[]{:S(2)}, u32[]{:S(2)}) collective-permute-start(f32[32,768]{1,0:T(8,128)S(1)} %get-tuple-element.103), channel_id=1, source_target_pairs={{0,28},{4,24},{8,20},{12,16},{16,12},{20,8},{24,4},{28,0},{1,29},{... | collective-permute-start | bytes 294920 | tf_op jit(solution)/shard_map/ppermute | solution.py:681
  90.4 5.9 %collective-permute-start.32 = (f32[32,768]{1,0:T(8,128)S(1)}, f32[32,768]{1,0:T(8,128)S(1)}, u32[]{:S(2)}, u32[]{:S(2)}) collective-permute-start(f32[32,768]{1,0:T(8,128)S(1)} %get-tuple-element.104), channel_id=1, source_target_pairs={{0,12},{4,8},{8,4},{12,0},{16,28},{20,24},{24,20},{28,16},{1,13},{... | collective-permute-start | bytes 294920 | tf_op jit(solution)/shard_map/ppermute | solution.py:681
  91.8 10.0 %collective-permute-start.38 = (f32[32,768]{1,0:T(8,128)S(1)}, f32[32,768]{1,0:T(8,128)S(1)}, u32[]{:S(2)}, u32[]{:S(2)}) collective-permute-start(f32[32,768]{1,0:T(8,128)S(1)} %get-tuple-element.116), channel_id=1, source_target_pairs={{0,16},{4,20},{8,24},{12,28},{16,0},{20,4},{24,8},{28,12},{1,17},{... | collective-permute-start | bytes 294920 | tf_op jit(solution)/shard_map/ppermute | solution.py:681
  95.1 8.2 %collective-permute-start.39 = (f32[32,768]{1,0:T(8,128)S(1)}, f32[32,768]{1,0:T(8,128)S(1)}, u32[]{:S(2)}, u32[]{:S(2)}) collective-permute-start(f32[32,768]{1,0:T(8,128)S(1)} %get-tuple-element.117), channel_id=1, source_target_pairs={{0,20},{4,16},{8,28},{12,24},{16,4},{20,0},{24,12},{28,8},{1,21},{... | collective-permute-start | bytes 294920 | tf_op jit(solution)/shard_map/ppermute | solution.py:681
  98.0 14.3 %collective-permute-start.33 = (f32[72,768]{1,0:T(8,128)S(1)}, f32[72,768]{1,0:T(8,128)S(1)}, u32[]{:S(2)}, u32[]{:S(2)}) collective-permute-start(f32[72,768]{1,0:T(8,128)S(1)} %get-tuple-element.106), channel_id=1, source_target_pairs={{0,2},{1,3},{2,0},{3,1},{4,6},{5,7},{6,4},{7,5},{8,10},{9,11},{10,... | collective-permute-start | bytes 663560 | tf_op jit(solution)/shard_map/ppermute | solution.py:681
  99.9 12.4 %collective-permute-start.34 = (f32[72,768]{1,0:T(8,128)S(1)}, f32[72,768]{1,0:T(8,128)S(1)}, u32[]{:S(2)}, u32[]{:S(2)}) collective-permute-start(f32[72,768]{1,0:T(8,128)S(1)} %get-tuple-element.107), channel_id=1, source_target_pairs={{0,3},{1,2},{2,1},{3,0},{4,7},{5,6},{6,5},{7,4},{8,11},{9,10},{10,... | collective-permute-start | bytes 663560 | tf_op jit(solution)/shard_map/ppermute | solution.py:681
  99.9 12.4 %collective-permute-start.35 = (f32[72,768]{1,0:T(8,128)S(1)}, f32[72,768]{1,0:T(8,128)S(1)}, u32[]{:S(2)}, u32[]{:S(2)}) collective-permute-start(f32[72,768]{1,0:T(8,128)S(1)} %get-tuple-element.108), channel_id=1, source_target_pairs={{0,1},{1,0},{2,3},{3,2},{4,5},{5,4},{6,7},{7,6},{8,9},{9,8},{10,11... | collective-permute-start | bytes 663560 | tf_op jit(solution)/shard_map/ppermute | solution.py:681
  101.8 4.6 %collective-permute-start.40 = (f32[32,768]{1,0:T(8,128)S(1)}, f32[32,768]{1,0:T(8,128)S(1)}, u32[]{:S(2)}, u32[]{:S(2)}) collective-permute-start(f32[32,768]{1,0:T(8,128)S(1)} %get-tuple-element.118), channel_id=1, source_target_pairs={{0,4},{4,0},{8,12},{12,8},{16,20},{20,16},{24,28},{28,24},{1,5},{5... | collective-permute-start | bytes 294920 | tf_op jit(solution)/shard_map/ppermute | solution.py:681
  103.3 4.6 %collective-permute-start.41 = (f32[32,768]{1,0:T(8,128)S(1)}, f32[32,768]{1,0:T(8,128)S(1)}, u32[]{:S(2)}, u32[]{:S(2)}) collective-permute-start(f32[32,768]{1,0:T(8,128)S(1)} %get-tuple-element.119), channel_id=1, source_target_pairs={{0,8},{4,12},{8,0},{12,4},{16,24},{20,28},{24,16},{28,20},{1,9},{5... | collective-permute-start | bytes 294920 | tf_op jit(solution)/shard_map/ppermute | solution.py:681
  107.9 10.7 %collective-permute-start.42 = (f32[32,768]{1,0:T(8,128)S(1)}, f32[32,768]{1,0:T(8,128)S(1)}, u32[]{:S(2)}, u32[]{:S(2)}) collective-permute-start(f32[32,768]{1,0:T(8,128)S(1)} %get-tuple-element.123), channel_id=1, source_target_pairs={{0,24},{4,28},{8,16},{12,20},{16,8},{20,12},{24,0},{28,4},{1,25},{... | collective-permute-start | bytes 294920 | tf_op jit(solution)/shard_map/ppermute | solution.py:681
  110.5 8.7 %collective-permute-start.43 = (f32[32,768]{1,0:T(8,128)S(1)}, f32[32,768]{1,0:T(8,128)S(1)}, u32[]{:S(2)}, u32[]{:S(2)}) collective-permute-start(f32[32,768]{1,0:T(8,128)S(1)} %get-tuple-element.124), channel_id=1, source_target_pairs={{0,28},{4,24},{8,20},{12,16},{16,12},{20,8},{24,4},{28,0},{1,29},{... | collective-permute-start | bytes 294920 | tf_op jit(solution)/shard_map/ppermute | solution.py:681
  112.3 10.8 %collective-permute-start.44 = (f32[32,768]{1,0:T(8,128)S(1)}, f32[32,768]{1,0:T(8,128)S(1)}, u32[]{:S(2)}, u32[]{:S(2)}) collective-permute-start(f32[32,768]{1,0:T(8,128)S(1)} %get-tuple-element.125), channel_id=1, source_target_pairs={{0,12},{4,8},{8,4},{12,0},{16,28},{20,24},{24,20},{28,16},{1,13},{... | collective-permute-start | bytes 294920 | tf_op jit(solution)/shard_map/ppermute | solution.py:681
  113.8 13.2 %collective-permute-start.36 = (f32[3,64,256]{2,1,0:T(8,128)S(1)}, f32[3,64,256]{2,1,0:T(8,128)S(1)}, u32[]{:S(2)}, u32[]{:S(2)}) collective-permute-start(f32[3,64,256]{2,1,0:T(8,128)S(1)} %get-tuple-element.110), channel_id=1, source_target_pairs={{0,4},{4,8},{8,12},{12,16},{16,20},{20,24},{24,28},{28,0},{1,5},{5... | collective-permute-start | bytes 589832 | tf_op jit(solution)/shard_map/ppermute | solution.py:811
  114.8 12.2 %collective-permute-start.37 = (f32[3,64,256]{2,1,0:T(8,128)S(1)}, f32[3,64,256]{2,1,0:T(8,128)S(1)}, u32[]{:S(2)}, u32[]{:S(2)}) collective-permute-start(f32[3,64,256]{2,1,0:T(8,128)S(1)} %get-tuple-element.111.refs_0_), channel_id=1, source_target_pairs={{0,28},{4,0},{8,4},{12,8},{16,12},{20,16},{24,20},{28,24},{1,29},{... | collective-permute-start | bytes 589832 | tf_op jit(solution)/shard_map/ppermute | solution.py:810
  124.8 7.9 %collective-permute-start.45 = (f32[72,768]{1,0:T(8,128)S(1)}, f32[72,768]{1,0:T(8,128)S(1)}, u32[]{:S(2)}, u32[]{:S(2)}) collective-permute-start(f32[72,768]{1,0:T(8,128)S(1)} %get-tuple-element.127), channel_id=1, source_target_pairs={{0,2},{1,3},{2,0},{3,1},{4,6},{5,7},{6,4},{7,5},{8,10},{9,11},{10,... | collective-permute-start | bytes 663560 | tf_op jit(solution)/shard_map/ppermute | solution.py:681
  124.9 8.2 %collective-permute-start.46 = (f32[72,768]{1,0:T(8,128)S(1)}, f32[72,768]{1,0:T(8,128)S(1)}, u32[]{:S(2)}, u32[]{:S(2)}) collective-permute-start(f32[72,768]{1,0:T(8,128)S(1)} %get-tuple-element.128), channel_id=1, source_target_pairs={{0,3},{1,2},{2,1},{3,0},{4,7},{5,6},{6,5},{7,4},{8,11},{9,10},{10,... | collective-permute-start | bytes 663560 | tf_op jit(solution)/shard_map/ppermute | solution.py:681
  124.9 8.1 %collective-permute-start.47 = (f32[72,768]{1,0:T(8,128)S(1)}, f32[72,768]{1,0:T(8,128)S(1)}, u32[]{:S(2)}, u32[]{:S(2)}) collective-permute-start(f32[72,768]{1,0:T(8,128)S(1)} %get-tuple-element.129), channel_id=1, source_target_pairs={{0,1},{1,0},{2,3},{3,2},{4,5},{5,4},{6,7},{7,6},{8,9},{9,8},{10,11... | collective-permute-start | bytes 663560 | tf_op jit(solution)/shard_map/ppermute | solution.py:681
  (9 other events, 99.6 us)

commit v8 on v7

--- a/solution.py
+++ b/solution.py
@@ -136,8 +136,8 @@
     far, near = list(range(count // 2, count)), list(range(1, count // 2))
     order = [0]
     while far or near:
-        order += far[:2] + near[:2]
-        far, near = far[2:], near[2:]
+        order += far[:1] + near[:1]
+        far, near = far[1:], near[1:]
     return order
 
 
@@ -287,9 +287,9 @@
         out[...] = made[d]
 
 
-def x_back_kernel(sends, passed, tables, place, *refs):
+def x_back_kernel(sends, tables, place, *refs):
     held, made = refs[-2:]
-    outs, parts = refs[-2 - sends : -2], refs[passed : -2 - sends]
+    outs, parts = refs[-2 - sends : -2], refs[: -2 - sends]
     gather_blocks(parts, held, place[0])
     pencils, rows, width = made.shape
     both = table_left(tables[0][...], tables[1][...], held[...].reshape(-1, width))
@@ -357,8 +357,7 @@
 
 
 def pass_kernel(before, *refs):
-    half = LATE
-    for source, target in zip(refs[-2 * half : -half], refs[-half:]):
+    for source, target in zip(refs[: len(refs) // 2], refs[len(refs) // 2 :]):
         target[...] = source[...]
 
 
@@ -559,10 +558,11 @@
         out[c][...] = omega[c] + TIME_STEP * stretch
 
 
-def ends_kernel(chunks, edges, before, after, low_rim, high_rim, *refs):
-    meshes, out = refs[:-1], refs[-1]
+def ends_kernel(_, edges, before, after, low_rim, high_rim, *refs):
+    meshes, vorticity, out, sems = refs[:-3], refs[-3], refs[-2], refs[-1]
     cols = before.shape[1]
     size = edges.shape[1]
+    copies = []
 
     def rows_of(i):
         return lambda c, start=RIM: edges[c, i, start : start + cols]
@@ -577,9 +577,17 @@
             (lambda c: after[c]) if i else rows_of(1),
             rows_of(size - 2) if i else (lambda c: before[c]),
         )
-
-
-def stretch_kernel(chunks, tables, place, edges, ends, low_rim, high_rim, *refs):
+        copies.append(
+            pltpu.make_async_copy(
+                out.at[:, n], vorticity.at[:, n * (vorticity.shape[1] - 1)], sems.at[n]
+            )
+        )
+        copies[-1].start()
+    for copy in copies:
+        copy.wait()
+
+
+def stretch_kernel(chunks, tables, place, edges, low_rim, high_rim, *refs):
     meshes, refs = refs[:2], refs[2:]
     velocity, vorticity, held, inner, omega, sems = refs[-6:]
     _, planes, cols, ny = velocity.shape
@@ -602,8 +610,6 @@
                 send(talls[n].at[:, i, pl.ds(RIM, cols)], velocity.at[:, z])
 
     send_velocity(0)
-    send(ends.at[:, 0], vorticity.at[:, 0])
-    send(ends.at[:, 1], vorticity.at[:, planes - 1])
     gather_blocks(refs[:-6], held, place[1])
     for (c, z), value in planes_of(held, chunks[1], tables).items():
         hold(inner, c, spot[z][1], value)
@@ -641,7 +647,7 @@
     return run
 
 
-def call(kernel, ins, outs, scratch=(), sems=0, micros=2.0, moved=None):
+def call(kernel, ins, outs, scratch=(), sems=0, micros=2.0, moved=None, aliases=None):
     extra = [pltpu.SemaphoreType.DMA((sems,))] if sems else []
     return pl.pallas_call(
         kernel,
@@ -650,6 +656,7 @@
         out_specs=[spec for spec, _ in outs],
         scratch_shapes=[pltpu.VMEM(shape, kind) for shape, kind in scratch] + extra,
         compiler_params=pltpu.CompilerParams(vmem_limit_bytes=VMEM),
+        input_output_aliases=aliases or {},
         cost_estimate=pl.CostEstimate(
             flops=int(micros * 1.0e9),
             bytes_accessed=int(micros * 3.0e6) if moved is None else moved,
@@ -776,13 +783,12 @@
         for chunk, source, width in zip(chunks, data, widths)
     ]
 
-    def back(part, width, before=()):
+    def back(part, width):
         shapes = sent_shapes("gx", rows, width)
         part = call(
-            loaded(functools.partial(x_back_kernel, len(shapes), len(before))),
+            loaded(functools.partial(x_back_kernel, len(shapes))),
             [here]
             + [(VM, t) for t in x_back]
-            + [(AN, b) for b in before]
             + [(VM, p) for p in part],
             [(VM, shape) for shape in shapes],
             [((slabs, block, width), F32), ((pencils, rows, width), F32)],
@@ -801,36 +807,40 @@
     if early < len(left[1]):
         late = call(
             pass_kernel,
-            [(AN, parts[0][0])] + [(AN, p) for p in second[1:]] + [(VM, p) for p in left[1][early:]],
+            [(AN, parts[0][0])] + [(VM, p) for p in left[1][early:]],
             [(VM, p.shape) for p in left[1][early:]],
             micros=0.3,
         )
         second += exchange(late, "gz", early)
-    parts.append(back(second, widths[1], [first]))
+    parts.append(back(second, widths[1]))
     after = lax.ppermute(first, "gz", ring("gz", -1))
     before = lax.ppermute(last, "gz", ring("gz", 1))
-    (ends,) = call(
-        functools.partial(ends_kernel, chunks),
-        [(VM, v) for v in (edges, before, after, low_rim, high_rim, *meshes)],
-        [(VM, (3, 2, cols, ny))],
-    )
-    return tuple(
-        call(
-            loaded(functools.partial(stretch_kernel, chunks)),
-            [here]
-            + tables
-            + [(VM, v) for v in (edges, ends, low_rim, high_rim, *meshes)]
-            + [(VM, p) for p in parts[1]],
-            [(AN, ambient.shape), (AN, ambient.shape)],
-            [
-                ((pencils, rows, widths[1]), F32),
-                (tall[1], F32),
-                ((3, planes, cols, ny), F32),
-            ],
-            sems=2 * planes,
-            micros=4.0,
-        )
-    )
+    velocity, vorticity = call(
+        loaded(functools.partial(stretch_kernel, chunks)),
+        [here]
+        + tables
+        + [(VM, v) for v in (edges, low_rim, high_rim, *meshes)]
+        + [(VM, p) for p in parts[1]],
+        [(AN, ambient.shape), (AN, ambient.shape)],
+        [
+            ((pencils, rows, widths[1]), F32),
+            (tall[1], F32),
+            ((3, planes, cols, ny), F32),
+        ],
+        sems=2 * planes,
+        micros=4.0,
+    )
+    (vorticity,) = call(
+        ends_kernel,
+        [(AN, vorticity)]
+        + [(VM, v) for v in (edges, before, after, low_rim, high_rim, *meshes)],
+        [(AN, ambient.shape)],
+        [((3, 2, cols, ny), F32)],
+        sems=2,
+        micros=1.0,
+        aliases={0: 0},
+    )
+    return velocity, vorticity
 
 
 def solution(mesh):

time: 138 us -> 139 us (level)
  waiting for transfers between devices: 33.4 us -> 38.7 us
  starting transfers between devices: 70.8 us -> 65.5 us
    ppermute x40, starting transfers between devices: 54.4 us -> 50.9 us  [exchange(): lax.ppermute(block, axis, [(i, i ^ k) for i in range(count)])]
    ppermute x1, starting transfers between devices: 3.08 us -> 6.03 us  [on_device(): up1 = lax.ppermute(packet, 'gz', ring('gz', -1))]
    ppermute x1, waiting for transfers between devices: 0.01 us -> 2.89 us  [on_device(): down2 = lax.ppermute(movers, 'gz', ring('gz', 2))]
    ppermute x40, waiting for transfers between devices: 31.7 us -> 34.3 us  [exchange(): lax.ppermute(block, axis, [(i, i ^ k) for i in range(count)])]
    ppermute x1, starting transfers between devices: 3.08 us -> 0.93 us  [on_device(): down2 = lax.ppermute(movers, 'gz', ring('gz', 2))]
    ppermute x1, starting transfers between devices: 1.65 us -> 0.01 us  [on_device(): down1 = lax.ppermute(packet, 'gz', ring('gz', 1))]
    ppermute x1, waiting for transfers between devices: 1.63 us -> 0.01 us  [on_device(): down1 = lax.ppermute(packet, 'gz', ring('gz', 1))]
    ppermute x1, waiting for transfers between devices: 0.01 us -> 1.51 us  [on_device(): up2 = lax.ppermute(movers, 'gz', ring('gz', -2))]
  transfers between devices with their start and end apart: 48 -> 48, of which waited for: 17 -> 16; matrix products, arithmetic and copies ran while one was open for 0% -> 0% of each run, Pallas kernels for 14% -> 11%
where the time goes in v8:
time: 139 us; the launch traced here: 137 us
  starting transfers between devices  65.5 us (47%)
  waiting for transfers between devices  38.7 us (28%)
  Pallas kernels  31.5 us (23%)
    ppermute x40, starting transfers between devices, exchange(): lax.ppermute(block, axis, [(i, i ^ k) for i in range(count)])  50.9 us
    ppermute x40, waiting for transfers between devices, exchange(): lax.ppermute(block, axis, [(i, i ^ k) for i in range(count)])  34.3 us
    pallas_call x16, Pallas kernels, call(): pl.pallas_call(kernel, out_shape=[jax.ShapeDtypeStruct(shape, F32) for _,...  31.5 us
    ppermute x1, starting transfers between devices, on_device(): up1 = lax.ppermute(packet, 'gz', ring('gz', -1))  6.03 us
    ppermute x1, starting transfers between devices, on_device(): after = lax.ppermute(first, 'gz', ring('gz', -1))  3.98 us
    ppermute x1, waiting for transfers between devices, on_device(): down2 = lax.ppermute(movers, 'gz', ring('gz', 2))  2.89 us
  transfers between devices with their start and end apart: 48, of which 16 were waited for; matrix products, arithmetic and copies ran while one was open for 0% of the time, Pallas kernels for 11%

profile of v8, /device:TPU:0, one launch (start us, length us, event | category | flops | bytes accessed | tf_op | source)
XLA Modules:
  0.0 136.9 jit_solution(13314892685500538386)
XLA Ops:
  1.8 6.0 %collective-permute-start = (f32[8,512]{1,0:T(8,128)S(1)}, f32[8,512]{1,0:T(8,128)S(1)}, u32[]{:S(2)}, u32[]{:S(2)}) collective-permute-start(f32[8,512]{1,0:T(8,128)S(1)} %get-tuple-element.68.own), channel_id=1, source_target_pairs={{0,28},{4,0},{8,4},{12,8},{16,12},{20,16},{24,20},{28,24},{1,29},{... | collective-permute-start | bytes 49160 | tf_op jit(solution)/shard_map/ppermute | solution.py:722
  9.9 1.5 %collective-permute-done.2.up2 = f32[8,128]{1,0:T(8,128)S(1)} collective-permute-done((f32[8,128]{1,0:T(8,128)S(1)}, f32[8,128]{1,0:T(8,128)S(1)}, u32[]{:S(2)}, u32[]{:S(2)}) %collective-permute-start.2) | collective-permute-done | bytes 4128 | tf_op jit(solution)/shard_map/ppermute | solution.py:724
  11.4 2.9 %collective-permute-done.3.down2 = f32[8,128]{1,0:T(8,128)S(1)} collective-permute-done((f32[8,128]{1,0:T(8,128)S(1)}, f32[8,128]{1,0:T(8,128)S(1)}, u32[]{:S(2)}, u32[]{:S(2)}) %collective-permute-start.3) | collective-permute-done | bytes 4128 | tf_op jit(solution)/shard_map/ppermute | solution.py:725
  14.3 4.0 %shard_map.141 = (f32[3,4,64,256]{3,2,1,0:T(8,128)S(1)}, f32[24,256]{1,0:T(8,128)S(1)}, f32[24,256]{1,0:T(8,128)S(1)}, f32[72,768]{1,0:T(8,128)S(1)}, f32[72,768...) custom-call(s32[2]{0:T(128)S(1)} %pad_add_fusion.place, f32[8,512]{1,0:T(8,128)S(1)} %get-tuple-element.68.own, ...), custom_call_target="tpu_custom_call" | custom-call | flops 5000000000 | bytes 15000000 | tf_op jit(solution)/shard_map/pallas_call | solution.py:652
  18.3 6.6 %shard_map.142 = (f32[3,4,64,256]{3,2,1,0:T(8,128)S(1)}, f32[48,256]{1,0:T(8,128)S(1)}, f32[48,256]{1,0:T(8,128)S(1)}, f32[72,768]{1,0:T(8,128)S(1)}, f32[72,768...) custom-call(s32[2]{0:T(128)S(1)} %pad_add_fusion.place, f32[8,512]{1,0:T(8,128)S(1)} %get-tuple-element.68.own, ...), custom_call_target="tpu_custom_call" | custom-call | flops 5000000000 | bytes 15000000 | tf_op jit(solution)/shard_map/pallas_call | solution.py:652
  24.9 1.6 %collective-permute-start.6 = (f32[72,768]{1,0:T(8,128)S(1)}, f32[72,768]{1,0:T(8,128)S(1)}, u32[]{:S(2)}, u32[]{:S(2)}) collective-permute-start(f32[72,768]{1,0:T(8,128)S(1)} %get-tuple-element.75), channel_id=1, source_target_pairs={{0,2},{1,3},{2,0},{3,1},{4,6},{5,7},{6,4},{7,5},{8,10},{9,11},{10,... | collective-permute-start | bytes 663560 | tf_op jit(solution)/shard_map/ppermute | solution.py:688
  27.1 1.5 %collective-permute-start.16 = (f32[72,768]{1,0:T(8,128)S(1)}, f32[72,768]{1,0:T(8,128)S(1)}, u32[]{:S(2)}, u32[]{:S(2)}) collective-permute-start(f32[72,768]{1,0:T(8,128)S(1)} %get-tuple-element.87), channel_id=1, source_target_pairs={{0,2},{1,3},{2,0},{3,1},{4,6},{5,7},{6,4},{7,5},{8,10},{9,11},{10,... | collective-permute-start | bytes 663560 | tf_op jit(solution)/shard_map/ppermute | solution.py:688
  28.6 3.7 %collective-permute-done.6.refs_1_ = f32[72,768]{1,0:T(8,128)S(1)} collective-permute-done((f32[72,768]{1,0:T(8,128)S(1)}, f32[72,768]{1,0:T(8,128)S(1)}, u32[]{:S(2)}, u32[]{:S(2)}) %collective-permute-start.6) | collective-permute-done | bytes 221216 | tf_op jit(solution)/shard_map/ppermute | solution.py:688
  32.3 4.7 %collective-permute-done.8.refs_3_ = f32[72,768]{1,0:T(8,128)S(1)} collective-permute-done((f32[72,768]{1,0:T(8,128)S(1)}, f32[72,768]{1,0:T(8,128)S(1)}, u32[]{:S(2)}, u32[]{:S(2)}) %collective-permute-start.8) | collective-permute-done | bytes 221216 | tf_op jit(solution)/shard_map/ppermute | solution.py:688
  37.1 1.6 %shard_map.143 = (f32[32,768]{1,0:T(8,128)S(1)}, f32[32,768]{1,0:T(8,128)S(1)}, f32[32,768]{1,0:T(8,128)S(1)}, f32[32,768]{1,0:T(8,128)S(1)}, f32[32,768]{1,0:T(...) custom-call(s32[2]{0:T(128)S(1)} %pad_add_fusion.place, ...), custom_call_target="tpu_custom_call" | custom-call | flops 2000000000 | bytes 6000000 | tf_op jit(solution)/shard_map/pallas_call | solution.py:652
  38.7 4.3 %collective-permute-start.10 = (f32[32,768]{1,0:T(8,128)S(1)}, f32[32,768]{1,0:T(8,128)S(1)}, u32[]{:S(2)}, u32[]{:S(2)}) collective-permute-start(f32[32,768]{1,0:T(8,128)S(1)} %get-tuple-element.80), channel_id=1, source_target_pairs={{0,4},{4,0},{8,12},{12,8},{16,20},{20,16},{24,28},{28,24},{1,5},{5... | collective-permute-start | bytes 294920 | tf_op jit(solution)/shard_map/ppermute | solution.py:688
  43.0 2.3 %collective-permute-start.11 = (f32[32,768]{1,0:T(8,128)S(1)}, f32[32,768]{1,0:T(8,128)S(1)}, u32[]{:S(2)}, u32[]{:S(2)}) collective-permute-start(f32[32,768]{1,0:T(8,128)S(1)} %get-tuple-element.81), channel_id=1, source_target_pairs={{0,20},{4,16},{8,28},{12,24},{16,4},{20,0},{24,12},{28,8},{1,21},{... | collective-permute-start | bytes 294920 | tf_op jit(solution)/shard_map/ppermute | solution.py:688
  46.0 3.8 %collective-permute-start.13 = (f32[32,768]{1,0:T(8,128)S(1)}, f32[32,768]{1,0:T(8,128)S(1)}, u32[]{:S(2)}, u32[]{:S(2)}) collective-permute-start(f32[32,768]{1,0:T(8,128)S(1)} %get-tuple-element.83), channel_id=1, source_target_pairs={{0,24},{4,28},{8,16},{12,20},{16,8},{20,12},{24,0},{28,4},{1,25},{... | collective-permute-start | bytes 294920 | tf_op jit(solution)/shard_map/ppermute | solution.py:688
  49.8 1.6 %shard_map.145 = (f32[32,768]{1,0:T(8,128)S(1)}, f32[32,768]{1,0:T(8,128)S(1)}, f32[32,768]{1,0:T(8,128)S(1)}, f32[32,768]{1,0:T(8,128)S(1)}, f32[32,768]{1,0:T(...) custom-call(s32[2]{0:T(128)S(1)} %pad_add_fusion.place, ...), custom_call_target="tpu_custom_call" | custom-call | flops 2000000000 | bytes 6000000 | tf_op jit(solution)/shard_map/pallas_call | solution.py:652
  51.5 1.8 %collective-permute-start.15 = (f32[32,768]{1,0:T(8,128)S(1)}, f32[32,768]{1,0:T(8,128)S(1)}, u32[]{:S(2)}, u32[]{:S(2)}) collective-permute-start(f32[32,768]{1,0:T(8,128)S(1)} %get-tuple-element.85), channel_id=1, source_target_pairs={{0,28},{4,24},{8,20},{12,16},{16,12},{20,8},{24,4},{28,0},{1,29},{... | collective-permute-start | bytes 294920 | tf_op jit(solution)/shard_map/ppermute | solution.py:688
  53.3 2.6 %collective-permute-start.19 = (f32[32,768]{1,0:T(8,128)S(1)}, f32[32,768]{1,0:T(8,128)S(1)}, u32[]{:S(2)}, u32[]{:S(2)}) collective-permute-start(f32[32,768]{1,0:T(8,128)S(1)} %get-tuple-element.91), channel_id=1, source_target_pairs={{0,16},{4,20},{8,24},{12,28},{16,0},{20,4},{24,8},{28,12},{1,17},{... | collective-permute-start | bytes 294920 | tf_op jit(solution)/shard_map/ppermute | solution.py:688
  56.6 1.8 %collective-permute-start.21 = (f32[32,768]{1,0:T(8,128)S(1)}, f32[32,768]{1,0:T(8,128)S(1)}, u32[]{:S(2)}, u32[]{:S(2)}) collective-permute-start(f32[32,768]{1,0:T(8,128)S(1)} %get-tuple-element.93), channel_id=1, source_target_pairs={{0,20},{4,16},{8,28},{12,24},{16,4},{20,0},{24,12},{28,8},{1,21},{... | collective-permute-start | bytes 294920 | tf_op jit(solution)/shard_map/ppermute | solution.py:688
  58.7 1.4 %collective-permute-done.15.refs_7_ = f32[32,768]{1,0:T(8,128)S(1)} collective-permute-done((f32[32,768]{1,0:T(8,128)S(1)}, f32[32,768]{1,0:T(8,128)S(1)}, u32[]{:S(2)}, u32[]{:S(2)}) %collective-permute-start.15) | collective-permute-done | bytes 98336 | tf_op jit(solution)/shard_map/ppermute | solution.py:688
  60.1 1.9 %collective-permute-start.23 = (f32[32,768]{1,0:T(8,128)S(1)}, f32[32,768]{1,0:T(8,128)S(1)}, u32[]{:S(2)}, u32[]{:S(2)}) collective-permute-start(f32[32,768]{1,0:T(8,128)S(1)} %get-tuple-element.95), channel_id=1, source_target_pairs={{0,24},{4,28},{8,16},{12,20},{16,8},{20,12},{24,0},{28,4},{1,25},{... | collective-permute-start | bytes 294920 | tf_op jit(solution)/shard_map/ppermute | solution.py:688
  62.1 6.7 %collective-permute-done.19.refs_1_ = f32[32,768]{1,0:T(8,128)S(1)} collective-permute-done((f32[32,768]{1,0:T(8,128)S(1)}, f32[32,768]{1,0:T(8,128)S(1)}, u32[]{:S(2)}, u32[]{:S(2)}) %collective-permute-start.19) | collective-permute-done | bytes 98336 | tf_op jit(solution)/shard_map/ppermute | solution.py:688
  68.8 2.5 %collective-permute-start.25 = (f32[32,768]{1,0:T(8,128)S(1)}, f32[32,768]{1,0:T(8,128)S(1)}, u32[]{:S(2)}, u32[]{:S(2)}) collective-permute-start(f32[32,768]{1,0:T(8,128)S(1)} %get-tuple-element.97), channel_id=1, source_target_pairs={{0,28},{4,24},{8,20},{12,16},{16,12},{20,8},{24,4},{28,0},{1,29},{... | collective-permute-start | bytes 294920 | tf_op jit(solution)/shard_map/ppermute | solution.py:688
  71.2 1.3 shard_map.144.refs_0_
  72.7 1.7 %collective-permute-start.5 = (f32[48,256]{1,0:T(8,128)S(1)}, f32[48,256]{1,0:T(8,128)S(1)}, u32[]{:S(2)}, u32[]{:S(2)}) collective-permute-start(f32[48,256]{1,0:T(8,128)S(1)} %get-tuple-element.73), channel_id=1, source_target_pairs={{0,3},{1,0},{2,1},{3,2},{4,7},{5,4},{6,5},{7,6},{8,11},{9,8},{10,9... | collective-permute-start | bytes 147464 | tf_op jit(solution)/shard_map/ppermute | solution.py:747
  74.4 2.0 %collective-permute-done.24.refs_6_ = f32[32,768]{1,0:T(8,128)S(1)} collective-permute-done((f32[32,768]{1,0:T(8,128)S(1)}, f32[32,768]{1,0:T(8,128)S(1)}, u32[]{:S(2)}, u32[]{:S(2)}) %collective-permute-start.24) | collective-permute-done | bytes 98336 | tf_op jit(solution)/shard_map/ppermute | solution.py:688
  76.4 1.3 shard_map.146.refs_1_
  77.8 2.3 %shard_map.147 = (f32[3,2,4,8,8,128]{5,4,3,2,1,0:T(8,128)S(1)}, f32[3,2,4,8,8,128]{5,4,3,2,1,0:T(8,128)S(1)}) custom-call(s32[2]{0:T(128)S(1)} %pad_add_fusion.place, f32[48,256]{1,0:T(8,128)S(1)} %collective-permute-done.4.low_rim.refs_1_, f32[48,256]{1,0:T(8,128)S(1)} %collective-permute-done.5.high_rim.refs_2_, ...), custom_call_target="tpu_custom_call" | custom-call | flops 5000000000 | bytes 15000000 | tf_op jit(solution)/shard_map/pallas_call | solution.py:652
  80.1 1.4 %shard_map.148 = (f32[32,768]{1,0:T(8,128)S(1)}, f32[32,768]{1,0:T(8,128)S(1)}, f32[32,768]{1,0:T(8,128)S(1)}, f32[32,768]{1,0:T(8,128)S(1)}, f32[32,768]{1,0:T(...) custom-call(s32[2]{0:T(128)S(1)} %pad_add_fusion.place, ...), custom_call_target="tpu_custom_call" | custom-call | flops 2000000000 | bytes 6000000 | tf_op jit(solution)/shard_map/pallas_call | solution.py:652
  81.5 2.3 %collective-permute-start.26 = (f32[32,768]{1,0:T(8,128)S(1)}, f32[32,768]{1,0:T(8,128)S(1)}, u32[]{:S(2)}, u32[]{:S(2)}) collective-permute-start(f32[32,768]{1,0:T(8,128)S(1)} %get-tuple-element.100), channel_id=1, source_target_pairs={{0,16},{4,20},{8,24},{12,28},{16,0},{20,4},{24,8},{28,12},{1,17},{... | collective-permute-start | bytes 294920 | tf_op jit(solution)/shard_map/ppermute | solution.py:688
  84.4 1.5 %collective-permute-start.28 = (f32[32,768]{1,0:T(8,128)S(1)}, f32[32,768]{1,0:T(8,128)S(1)}, u32[]{:S(2)}, u32[]{:S(2)}) collective-permute-start(f32[32,768]{1,0:T(8,128)S(1)} %get-tuple-element.102), channel_id=1, source_target_pairs={{0,20},{4,16},{8,28},{12,24},{16,4},{20,0},{24,12},{28,8},{1,21},{... | collective-permute-start | bytes 294920 | tf_op jit(solution)/shard_map/ppermute | solution.py:688
  85.9 1.4 %collective-permute-start.29 = (f32[32,768]{1,0:T(8,128)S(1)}, f32[32,768]{1,0:T(8,128)S(1)}, u32[]{:S(2)}, u32[]{:S(2)}) collective-permute-start(f32[32,768]{1,0:T(8,128)S(1)} %get-tuple-element.103), channel_id=1, source_target_pairs={{0,8},{4,12},{8,0},{12,4},{16,24},{20,28},{24,16},{28,20},{1,9},{5... | collective-permute-start | bytes 294920 | tf_op jit(solution)/shard_map/ppermute | solution.py:688
  87.4 2.2 %collective-permute-start.30 = (f32[32,768]{1,0:T(8,128)S(1)}, f32[32,768]{1,0:T(8,128)S(1)}, u32[]{:S(2)}, u32[]{:S(2)}) collective-permute-start(f32[32,768]{1,0:T(8,128)S(1)} %get-tuple-element.104), channel_id=1, source_target_pairs={{0,24},{4,28},{8,16},{12,20},{16,8},{20,12},{24,0},{28,4},{1,25},{... | collective-permute-start | bytes 294920 | tf_op jit(solution)/shard_map/ppermute | solution.py:688
  89.6 3.6 %collective-permute-done.26.refs_1_ = f32[32,768]{1,0:T(8,128)S(1)} collective-permute-done((f32[32,768]{1,0:T(8,128)S(1)}, f32[32,768]{1,0:T(8,128)S(1)}, u32[]{:S(2)}, u32[]{:S(2)}) %collective-permute-start.26) | collective-permute-done | bytes 98336 | tf_op jit(solution)/shard_map/ppermute | solution.py:688
  93.2 1.6 %collective-permute-start.32 = (f32[32,768]{1,0:T(8,128)S(1)}, f32[32,768]{1,0:T(8,128)S(1)}, u32[]{:S(2)}, u32[]{:S(2)}) collective-permute-start(f32[32,768]{1,0:T(8,128)S(1)} %get-tuple-element.106), channel_id=1, source_target_pairs={{0,28},{4,24},{8,20},{12,16},{16,12},{20,8},{24,4},{28,0},{1,29},{... | collective-permute-start | bytes 294920 | tf_op jit(solution)/shard_map/ppermute | solution.py:688
  94.8 1.4 %shard_map.151 = (f32[32,768]{1,0:T(8,128)S(1)}, f32[32,768]{1,0:T(8,128)S(1)}, f32[32,768]{1,0:T(8,128)S(1)}, f32[32,768]{1,0:T(8,128)S(1)}, f32[32,768]{1,0:T(...) custom-call(s32[2]{0:T(128)S(1)} %pad_add_fusion.place, ...), custom_call_target="tpu_custom_call" | custom-call | flops 2000000000 | bytes 6000000 | tf_op jit(solution)/shard_map/pallas_call | solution.py:652
  96.3 2.2 %collective-permute-done.28.refs_3_ = f32[32,768]{1,0:T(8,128)S(1)} collective-permute-done((f32[32,768]{1,0:T(8,128)S(1)}, f32[32,768]{1,0:T(8,128)S(1)}, u32[]{:S(2)}, u32[]{:S(2)}) %collective-permute-start.28) | collective-permute-done | bytes 98336 | tf_op jit(solution)/shard_map/ppermute | solution.py:688
  99.1 1.3 collective-permute-start.37
  100.5 2.4 %collective-permute-start.38 = (f32[32,768]{1,0:T(8,128)S(1)}, f32[32,768]{1,0:T(8,128)S(1)}, u32[]{:S(2)}, u32[]{:S(2)}) collective-permute-start(f32[32,768]{1,0:T(8,128)S(1)} %get-tuple-element.118), channel_id=1, source_target_pairs={{0,20},{4,16},{8,28},{12,24},{16,4},{20,0},{24,12},{28,8},{1,21},{... | collective-permute-start | bytes 294920 | tf_op jit(solution)/shard_map/ppermute | solution.py:688
  103.2 1.7 %shard_map.149 = (f32[72,768]{1,0:T(8,128)S(1)}, f32[72,768]{1,0:T(8,128)S(1)}, f32[72,768]{1,0:T(8,128)S(1)}, f32[72,768]{1,0:T(8,128)S(1)}) custom-call(s32[2]{0:T(128)S(1)} %pad_add_fusion.place, bf16[576,256]{1,0:T(8,128)(2,1)S(1)} %copy-done.5, bf16[576,256]{1,0:T(8,128)(2,1)S(1)} %copy-done.6, f32[32,768]{1,0:T(8,128)S(1)} %get-tuple-element.99.refs_0_, ...), custom_call_target="tpu_custom_call" | custom-call | flops 2000000000 | bytes 6000000 | tf_op jit(solution)/shard_map/pallas_call | solution.py:652
  105.0 3.2 %collective-permute-start.40 = (f32[32,768]{1,0:T(8,128)S(1)}, f32[32,768]{1,0:T(8,128)S(1)}, u32[]{:S(2)}, u32[]{:S(2)}) collective-permute-start(f32[32,768]{1,0:T(8,128)S(1)} %get-tuple-element.123), channel_id=1, source_target_pairs={{0,24},{4,28},{8,16},{12,20},{16,8},{20,12},{24,0},{28,4},{1,25},{... | collective-permute-start | bytes 294920 | tf_op jit(solution)/shard_map/ppermute | solution.py:688
  108.2 1.9 %collective-permute-done.36.refs_1_ = f32[32,768]{1,0:T(8,128)S(1)} collective-permute-done((f32[32,768]{1,0:T(8,128)S(1)}, f32[32,768]{1,0:T(8,128)S(1)}, u32[]{:S(2)}, u32[]{:S(2)}) %collective-permute-start.36) | collective-permute-done | bytes 98336 | tf_op jit(solution)/shard_map/ppermute | solution.py:688
  110.1 3.7 %collective-permute-start.42 = (f32[32,768]{1,0:T(8,128)S(1)}, f32[32,768]{1,0:T(8,128)S(1)}, u32[]{:S(2)}, u32[]{:S(2)}) collective-permute-start(f32[32,768]{1,0:T(8,128)S(1)} %get-tuple-element.125), channel_id=1, source_target_pairs={{0,28},{4,24},{8,20},{12,16},{16,12},{20,8},{24,4},{28,0},{1,29},{... | collective-permute-start | bytes 294920 | tf_op jit(solution)/shard_map/ppermute | solution.py:688
  115.0 2.1 %collective-permute-start.35 = (f32[72,768]{1,0:T(8,128)S(1)}, f32[72,768]{1,0:T(8,128)S(1)}, u32[]{:S(2)}, u32[]{:S(2)}) collective-permute-start(f32[72,768]{1,0:T(8,128)S(1)} %get-tuple-element.110), channel_id=1, source_target_pairs={{0,3},{1,2},{2,1},{3,0},{4,7},{5,6},{6,5},{7,4},{8,11},{9,10},{10,... | collective-permute-start | bytes 663560 | tf_op jit(solution)/shard_map/ppermute | solution.py:688
  117.6 1.7 %shard_map.153 = (f32[72,768]{1,0:T(8,128)S(1)}, f32[72,768]{1,0:T(8,128)S(1)}, f32[72,768]{1,0:T(8,128)S(1)}, f32[72,768]{1,0:T(8,128)S(1)}) custom-call(s32[2]{0:T(128)S(1)} %pad_add_fusion.place, bf16[576,256]{1,0:T(8,128)(2,1)S(1)} %copy-done.5, bf16[576,256]{1,0:T(8,128)(2,1)S(1)} %copy-done.6, f32[32,768]{1,0:T(8,128)S(1)} %get-tuple-element.115.refs_0_, ...), custom_call_target="tpu_custom_call" | custom-call | flops 2000000000 | bytes 6000000 | tf_op jit(solution)/shard_map/pallas_call | solution.py:652
  120.0 3.3 %collective-permute-done.33.refs_1_ = f32[72,768]{1,0:T(8,128)S(1)} collective-permute-done((f32[72,768]{1,0:T(8,128)S(1)}, f32[72,768]{1,0:T(8,128)S(1)}, u32[]{:S(2)}, u32[]{:S(2)}) %collective-permute-start.33) | collective-permute-done | bytes 221216 | tf_op jit(solution)/shard_map/ppermute | solution.py:688
  124.0 1.5 %shard_map.150 = (f32[3,4,80,256]{3,2,1,0:T(8,128)S(1)}, f32[3,64,256]{2,1,0:T(8,128)S(1)}, f32[3,64,256]{2,1,0:T(8,128)S(1)}) custom-call(s32[2]{0:T(128)S(1)} %pad_add_fusion.place, bf16[512,512]{1,0:T(8,128)(2,1)S(1)} %copy-done.1, bf16[512,512]{1,0:T(8,128)(2,1)S(1)} %copy-done.2, f32[72,768]{1,0:T(8,128)S(1)} %get-tuple-element.107.refs_0_.before, ...), custom_call_target="tpu_custom_call" | custom-call | flops 2000000000 | bytes 6000000 | tf_op jit(solution)/shard_map/pallas_call | solution.py:652
  126.2 4.0 %collective-permute-start.47 = (f32[3,64,256]{2,1,0:T(8,128)S(1)}, f32[3,64,256]{2,1,0:T(8,128)S(1)}, u32[]{:S(2)}, u32[]{:S(2)}) collective-permute-start(f32[3,64,256]{2,1,0:T(8,128)S(1)} %get-tuple-element.133), channel_id=1, source_target_pairs={{0,28},{4,0},{8,4},{12,8},{16,12},{20,16},{24,20},{28,24},{1,29},{... | collective-permute-start | bytes 589832 | tf_op jit(solution)/shard_map/ppermute | solution.py:816
  130.2 2.4 %collective-permute-done.43.refs_6_ = f32[72,768]{1,0:T(8,128)S(1)} collective-permute-done((f32[72,768]{1,0:T(8,128)S(1)}, f32[72,768]{1,0:T(8,128)S(1)}, u32[]{:S(2)}, u32[]{:S(2)}) %collective-permute-start.43) | collective-permute-done | bytes 221216 | tf_op jit(solution)/shard_map/ppermute | solution.py:688
  132.7 3.0 %shard_map.154 = (f32[3,8,64,256]{3,2,1,0:T(8,128)}, f32[3,8,64,256]{3,2,1,0:T(8,128)}) custom-call(s32[2]{0:T(128)S(1)} %pad_add_fusion.place, bf16[512,512]{1,0:T(8,128)(2,1)S(1)} %copy-done.1, bf16[512,512]{1,0:T(8,128)(2,1)S(1)} %copy-done.2, f32[3,4,80,256]{3,2,1,0:T(8,128)S(1)} %get-tuple-element.111.refs_0_.edges, ...), custom_call_target="tpu_custom_call" | custom-call | flops 4000000000 | bytes 12000000 | tf_op jit(solution)/shard_map/pallas_call | solution.py:652
  (83 shorter events, 12.6 us)
Async XLA Ops:
  1.8 12.5 %collective-permute-start = (f32[8,512]{1,0:T(8,128)S(1)}, f32[8,512]{1,0:T(8,128)S(1)}, u32[]{:S(2)}, u32[]{:S(2)}) collective-permute-start(f32[8,512]{1,0:T(8,128)S(1)} %get-tuple-element.68.own), channel_id=1, source_target_pairs={{0,28},{4,0},{8,4},{12,8},{16,12},{20,16},{24,20},{28,24},{1,29},{... | collective-permute-start | bytes 49160 | tf_op jit(solution)/shard_map/ppermute | solution.py:722
  7.8 6.5 %collective-permute-start.1 = (f32[8,512]{1,0:T(8,128)S(1)}, f32[8,512]{1,0:T(8,128)S(1)}, u32[]{:S(2)}, u32[]{:S(2)}) collective-permute-start(f32[8,512]{1,0:T(8,128)S(1)} %get-tuple-element.68.own), channel_id=1, source_target_pairs={{0,4},{4,8},{8,12},{12,16},{16,20},{20,24},{24,28},{28,0},{1,5},{5... | collective-permute-start | bytes 49160 | tf_op jit(solution)/shard_map/ppermute | solution.py:723
  7.8 3.6 %collective-permute-start.2 = (f32[8,128]{1,0:T(8,128)S(1)}, f32[8,128]{1,0:T(8,128)S(1)}, u32[]{:S(2)}, u32[]{:S(2)}) collective-permute-start(f32[8,128]{1,0:T(8,128)S(1)} %get-tuple-element.69), channel_id=1, source_target_pairs={{0,24},{4,28},{8,0},{12,4},{16,8},{20,12},{24,16},{28,20},{1,25},{... | collective-permute-start | bytes 12296 | tf_op jit(solution)/shard_map/ppermute | solution.py:724
  8.9 5.4 %collective-permute-start.3 = (f32[8,128]{1,0:T(8,128)S(1)}, f32[8,128]{1,0:T(8,128)S(1)}, u32[]{:S(2)}, u32[]{:S(2)}) collective-permute-start(f32[8,128]{1,0:T(8,128)S(1)} %get-tuple-element.69), channel_id=1, source_target_pairs={{0,8},{4,12},{8,16},{12,20},{16,24},{20,28},{24,0},{28,4},{1,9},{5... | collective-permute-start | bytes 12296 | tf_op jit(solution)/shard_map/ppermute | solution.py:725
  24.9 7.4 %collective-permute-start.6 = (f32[72,768]{1,0:T(8,128)S(1)}, f32[72,768]{1,0:T(8,128)S(1)}, u32[]{:S(2)}, u32[]{:S(2)}) collective-permute-start(f32[72,768]{1,0:T(8,128)S(1)} %get-tuple-element.75), channel_id=1, source_target_pairs={{0,2},{1,3},{2,0},{3,1},{4,6},{5,7},{6,4},{7,5},{8,10},{9,11},{10,... | collective-permute-start | bytes 663560 | tf_op jit(solution)/shard_map/ppermute | solution.py:688
  26.5 5.9 %collective-permute-start.7 = (f32[72,768]{1,0:T(8,128)S(1)}, f32[72,768]{1,0:T(8,128)S(1)}, u32[]{:S(2)}, u32[]{:S(2)}) collective-permute-start(f32[72,768]{1,0:T(8,128)S(1)} %get-tuple-element.76), channel_id=1, source_target_pairs={{0,1},{1,0},{2,3},{3,2},{4,5},{5,4},{6,7},{7,6},{8,9},{9,8},{10,11... | collective-permute-start | bytes 663560 | tf_op jit(solution)/shard_map/ppermute | solution.py:688
  26.5 10.6 %collective-permute-start.8 = (f32[72,768]{1,0:T(8,128)S(1)}, f32[72,768]{1,0:T(8,128)S(1)}, u32[]{:S(2)}, u32[]{:S(2)}) collective-permute-start(f32[72,768]{1,0:T(8,128)S(1)} %get-tuple-element.77), channel_id=1, source_target_pairs={{0,3},{1,2},{2,1},{3,0},{4,7},{5,6},{6,5},{7,4},{8,11},{9,10},{10,... | collective-permute-start | bytes 663560 | tf_op jit(solution)/shard_map/ppermute | solution.py:688
  27.1 15.9 %collective-permute-start.16 = (f32[72,768]{1,0:T(8,128)S(1)}, f32[72,768]{1,0:T(8,128)S(1)}, u32[]{:S(2)}, u32[]{:S(2)}) collective-permute-start(f32[72,768]{1,0:T(8,128)S(1)} %get-tuple-element.87), channel_id=1, source_target_pairs={{0,2},{1,3},{2,0},{3,1},{4,6},{5,7},{6,4},{7,5},{8,10},{9,11},{10,... | collective-permute-start | bytes 663560 | tf_op jit(solution)/shard_map/ppermute | solution.py:688
  28.6 16.7 %collective-permute-start.17 = (f32[72,768]{1,0:T(8,128)S(1)}, f32[72,768]{1,0:T(8,128)S(1)}, u32[]{:S(2)}, u32[]{:S(2)}) collective-permute-start(f32[72,768]{1,0:T(8,128)S(1)} %get-tuple-element.88), channel_id=1, source_target_pairs={{0,1},{1,0},{2,3},{3,2},{4,5},{5,4},{6,7},{7,6},{8,9},{9,8},{10,11... | collective-permute-start | bytes 663560 | tf_op jit(solution)/shard_map/ppermute | solution.py:688
  32.3 13.7 %collective-permute-start.18 = (f32[72,768]{1,0:T(8,128)S(1)}, f32[72,768]{1,0:T(8,128)S(1)}, u32[]{:S(2)}, u32[]{:S(2)}) collective-permute-start(f32[72,768]{1,0:T(8,128)S(1)} %get-tuple-element.89), channel_id=1, source_target_pairs={{0,3},{1,2},{2,1},{3,0},{4,7},{5,6},{6,5},{7,4},{8,11},{9,10},{10,... | collective-permute-start | bytes 663560 | tf_op jit(solution)/shard_map/ppermute | solution.py:688
  38.7 12.8 %collective-permute-start.9 = (f32[32,768]{1,0:T(8,128)S(1)}, f32[32,768]{1,0:T(8,128)S(1)}, u32[]{:S(2)}, u32[]{:S(2)}) collective-permute-start(f32[32,768]{1,0:T(8,128)S(1)} %get-tuple-element.79), channel_id=1, source_target_pairs={{0,16},{4,20},{8,24},{12,28},{16,0},{20,4},{24,8},{28,12},{1,17},{... | collective-permute-start | bytes 294920 | tf_op jit(solution)/shard_map/ppermute | solution.py:688
  38.7 12.8 %collective-permute-start.10 = (f32[32,768]{1,0:T(8,128)S(1)}, f32[32,768]{1,0:T(8,128)S(1)}, u32[]{:S(2)}, u32[]{:S(2)}) collective-permute-start(f32[32,768]{1,0:T(8,128)S(1)} %get-tuple-element.80), channel_id=1, source_target_pairs={{0,4},{4,0},{8,12},{12,8},{16,20},{20,16},{24,28},{28,24},{1,5},{5... | collective-permute-start | bytes 294920 | tf_op jit(solution)/shard_map/ppermute | solution.py:688
  43.0 10.3 %collective-permute-start.11 = (f32[32,768]{1,0:T(8,128)S(1)}, f32[32,768]{1,0:T(8,128)S(1)}, u32[]{:S(2)}, u32[]{:S(2)}) collective-permute-start(f32[32,768]{1,0:T(8,128)S(1)} %get-tuple-element.81), channel_id=1, source_target_pairs={{0,20},{4,16},{8,28},{12,24},{16,4},{20,0},{24,12},{28,8},{1,21},{... | collective-permute-start | bytes 294920 | tf_op jit(solution)/shard_map/ppermute | solution.py:688
  45.3 10.6 %collective-permute-start.12 = (f32[32,768]{1,0:T(8,128)S(1)}, f32[32,768]{1,0:T(8,128)S(1)}, u32[]{:S(2)}, u32[]{:S(2)}) collective-permute-start(f32[32,768]{1,0:T(8,128)S(1)} %get-tuple-element.82), channel_id=1, source_target_pairs={{0,8},{4,12},{8,0},{12,4},{16,24},{20,28},{24,16},{28,20},{1,9},{5... | collective-permute-start | bytes 294920 | tf_op jit(solution)/shard_map/ppermute | solution.py:688
  46.0 10.6 %collective-permute-start.13 = (f32[32,768]{1,0:T(8,128)S(1)}, f32[32,768]{1,0:T(8,128)S(1)}, u32[]{:S(2)}, u32[]{:S(2)}) collective-permute-start(f32[32,768]{1,0:T(8,128)S(1)} %get-tuple-element.83), channel_id=1, source_target_pairs={{0,24},{4,28},{8,16},{12,20},{16,8},{20,12},{24,0},{28,4},{1,25},{... | collective-permute-start | bytes 294920 | tf_op jit(solution)/shard_map/ppermute | solution.py:688
  51.4 6.9 %collective-permute-start.14 = (f32[32,768]{1,0:T(8,128)S(1)}, f32[32,768]{1,0:T(8,128)S(1)}, u32[]{:S(2)}, u32[]{:S(2)}) collective-permute-start(f32[32,768]{1,0:T(8,128)S(1)} %get-tuple-element.84), channel_id=1, source_target_pairs={{0,12},{4,8},{8,4},{12,0},{16,28},{20,24},{24,20},{28,16},{1,13},{... | collective-permute-start | bytes 294920 | tf_op jit(solution)/shard_map/ppermute | solution.py:688
  51.5 8.6 %collective-permute-start.15 = (f32[32,768]{1,0:T(8,128)S(1)}, f32[32,768]{1,0:T(8,128)S(1)}, u32[]{:S(2)}, u32[]{:S(2)}) collective-permute-start(f32[32,768]{1,0:T(8,128)S(1)} %get-tuple-element.85), channel_id=1, source_target_pairs={{0,28},{4,24},{8,20},{12,16},{16,12},{20,8},{24,4},{28,0},{1,29},{... | collective-permute-start | bytes 294920 | tf_op jit(solution)/shard_map/ppermute | solution.py:688
  53.3 15.5 %collective-permute-start.19 = (f32[32,768]{1,0:T(8,128)S(1)}, f32[32,768]{1,0:T(8,128)S(1)}, u32[]{:S(2)}, u32[]{:S(2)}) collective-permute-start(f32[32,768]{1,0:T(8,128)S(1)} %get-tuple-element.91), channel_id=1, source_target_pairs={{0,16},{4,20},{8,24},{12,28},{16,0},{20,4},{24,8},{28,12},{1,17},{... | collective-permute-start | bytes 294920 | tf_op jit(solution)/shard_map/ppermute | solution.py:688
  55.9 12.9 %collective-permute-start.20 = (f32[32,768]{1,0:T(8,128)S(1)}, f32[32,768]{1,0:T(8,128)S(1)}, u32[]{:S(2)}, u32[]{:S(2)}) collective-permute-start(f32[32,768]{1,0:T(8,128)S(1)} %get-tuple-element.92), channel_id=1, source_target_pairs={{0,4},{4,0},{8,12},{12,8},{16,20},{20,16},{24,28},{28,24},{1,5},{5... | collective-permute-start | bytes 294920 | tf_op jit(solution)/shard_map/ppermute | solution.py:688
  56.6 16.0 %collective-permute-start.21 = (f32[32,768]{1,0:T(8,128)S(1)}, f32[32,768]{1,0:T(8,128)S(1)}, u32[]{:S(2)}, u32[]{:S(2)}) collective-permute-start(f32[32,768]{1,0:T(8,128)S(1)} %get-tuple-element.93), channel_id=1, source_target_pairs={{0,20},{4,16},{8,28},{12,24},{16,4},{20,0},{24,12},{28,8},{1,21},{... | collective-permute-start | bytes 294920 | tf_op jit(solution)/shard_map/ppermute | solution.py:688
  58.4 14.3 %collective-permute-start.22 = (f32[32,768]{1,0:T(8,128)S(1)}, f32[32,768]{1,0:T(8,128)S(1)}, u32[]{:S(2)}, u32[]{:S(2)}) collective-permute-start(f32[32,768]{1,0:T(8,128)S(1)} %get-tuple-element.94), channel_id=1, source_target_pairs={{0,8},{4,12},{8,0},{12,4},{16,24},{20,28},{24,16},{28,20},{1,9},{5... | collective-permute-start | bytes 294920 | tf_op jit(solution)/shard_map/ppermute | solution.py:688
  60.1 14.3 %collective-permute-start.23 = (f32[32,768]{1,0:T(8,128)S(1)}, f32[32,768]{1,0:T(8,128)S(1)}, u32[]{:S(2)}, u32[]{:S(2)}) collective-permute-start(f32[32,768]{1,0:T(8,128)S(1)} %get-tuple-element.95), channel_id=1, source_target_pairs={{0,24},{4,28},{8,16},{12,20},{16,8},{20,12},{24,0},{28,4},{1,25},{... | collective-permute-start | bytes 294920 | tf_op jit(solution)/shard_map/ppermute | solution.py:688
  68.8 7.6 %collective-permute-start.24 = (f32[32,768]{1,0:T(8,128)S(1)}, f32[32,768]{1,0:T(8,128)S(1)}, u32[]{:S(2)}, u32[]{:S(2)}) collective-permute-start(f32[32,768]{1,0:T(8,128)S(1)} %get-tuple-element.96), channel_id=1, source_target_pairs={{0,12},{4,8},{8,4},{12,0},{16,28},{20,24},{24,20},{28,16},{1,13},{... | collective-permute-start | bytes 294920 | tf_op jit(solution)/shard_map/ppermute | solution.py:688
  68.8 7.6 %collective-permute-start.25 = (f32[32,768]{1,0:T(8,128)S(1)}, f32[32,768]{1,0:T(8,128)S(1)}, u32[]{:S(2)}, u32[]{:S(2)}) collective-permute-start(f32[32,768]{1,0:T(8,128)S(1)} %get-tuple-element.97), channel_id=1, source_target_pairs={{0,28},{4,24},{8,20},{12,16},{16,12},{20,8},{24,4},{28,0},{1,29},{... | collective-permute-start | bytes 294920 | tf_op jit(solution)/shard_map/ppermute | solution.py:688
  72.6 5.1 %collective-permute-start.4 = (f32[48,256]{1,0:T(8,128)S(1)}, f32[48,256]{1,0:T(8,128)S(1)}, u32[]{:S(2)}, u32[]{:S(2)}) collective-permute-start(f32[48,256]{1,0:T(8,128)S(1)} %get-tuple-element.72), channel_id=1, source_target_pairs={{0,1},{1,2},{2,3},{3,0},{4,5},{5,6},{6,7},{7,4},{8,9},{9,10},{10,1... | collective-permute-start | bytes 147464 | tf_op jit(solution)/shard_map/ppermute | solution.py:746
  72.7 5.1 %collective-permute-start.5 = (f32[48,256]{1,0:T(8,128)S(1)}, f32[48,256]{1,0:T(8,128)S(1)}, u32[]{:S(2)}, u32[]{:S(2)}) collective-permute-start(f32[48,256]{1,0:T(8,128)S(1)} %get-tuple-element.73), channel_id=1, source_target_pairs={{0,3},{1,0},{2,1},{3,2},{4,7},{5,4},{6,5},{7,6},{8,11},{9,8},{10,9... | collective-permute-start | bytes 147464 | tf_op jit(solution)/shard_map/ppermute | solution.py:747
  81.5 11.8 %collective-permute-start.26 = (f32[32,768]{1,0:T(8,128)S(1)}, f32[32,768]{1,0:T(8,128)S(1)}, u32[]{:S(2)}, u32[]{:S(2)}) collective-permute-start(f32[32,768]{1,0:T(8,128)S(1)} %get-tuple-element.100), channel_id=1, source_target_pairs={{0,16},{4,20},{8,24},{12,28},{16,0},{20,4},{24,8},{28,12},{1,17},{... | collective-permute-start | bytes 294920 | tf_op jit(solution)/shard_map/ppermute | solution.py:688
  83.8 9.5 %collective-permute-start.27 = (f32[32,768]{1,0:T(8,128)S(1)}, f32[32,768]{1,0:T(8,128)S(1)}, u32[]{:S(2)}, u32[]{:S(2)}) collective-permute-start(f32[32,768]{1,0:T(8,128)S(1)} %get-tuple-element.101), channel_id=1, source_target_pairs={{0,4},{4,0},{8,12},{12,8},{16,20},{20,16},{24,28},{28,24},{1,5},{5... | collective-permute-start | bytes 294920 | tf_op jit(solution)/shard_map/ppermute | solution.py:688
  84.4 14.0 %collective-permute-start.28 = (f32[32,768]{1,0:T(8,128)S(1)}, f32[32,768]{1,0:T(8,128)S(1)}, u32[]{:S(2)}, u32[]{:S(2)}) collective-permute-start(f32[32,768]{1,0:T(8,128)S(1)} %get-tuple-element.102), channel_id=1, source_target_pairs={{0,20},{4,16},{8,28},{12,24},{16,4},{20,0},{24,12},{28,8},{1,21},{... | collective-permute-start | bytes 294920 | tf_op jit(solution)/shard_map/ppermute | solution.py:688
  85.9 13.2 %collective-permute-start.29 = (f32[32,768]{1,0:T(8,128)S(1)}, f32[32,768]{1,0:T(8,128)S(1)}, u32[]{:S(2)}, u32[]{:S(2)}) collective-permute-start(f32[32,768]{1,0:T(8,128)S(1)} %get-tuple-element.103), channel_id=1, source_target_pairs={{0,8},{4,12},{8,0},{12,4},{16,24},{20,28},{24,16},{28,20},{1,9},{5... | collective-permute-start | bytes 294920 | tf_op jit(solution)/shard_map/ppermute | solution.py:688
  87.4 13.1 %collective-permute-start.30 = (f32[32,768]{1,0:T(8,128)S(1)}, f32[32,768]{1,0:T(8,128)S(1)}, u32[]{:S(2)}, u32[]{:S(2)}) collective-permute-start(f32[32,768]{1,0:T(8,128)S(1)} %get-tuple-element.104), channel_id=1, source_target_pairs={{0,24},{4,28},{8,16},{12,20},{16,8},{20,12},{24,0},{28,4},{1,25},{... | collective-permute-start | bytes 294920 | tf_op jit(solution)/shard_map/ppermute | solution.py:688
  93.2 9.6 %collective-permute-start.31 = (f32[32,768]{1,0:T(8,128)S(1)}, f32[32,768]{1,0:T(8,128)S(1)}, u32[]{:S(2)}, u32[]{:S(2)}) collective-permute-start(f32[32,768]{1,0:T(8,128)S(1)} %get-tuple-element.105), channel_id=1, source_target_pairs={{0,12},{4,8},{8,4},{12,0},{16,28},{20,24},{24,20},{28,16},{1,13},{... | collective-permute-start | bytes 294920 | tf_op jit(solution)/shard_map/ppermute | solution.py:688
  93.2 10.0 %collective-permute-start.32 = (f32[32,768]{1,0:T(8,128)S(1)}, f32[32,768]{1,0:T(8,128)S(1)}, u32[]{:S(2)}, u32[]{:S(2)}) collective-permute-start(f32[32,768]{1,0:T(8,128)S(1)} %get-tuple-element.106), channel_id=1, source_target_pairs={{0,28},{4,24},{8,20},{12,16},{16,12},{20,8},{24,4},{28,0},{1,29},{... | collective-permute-start | bytes 294920 | tf_op jit(solution)/shard_map/ppermute | solution.py:688
  98.4 11.7 %collective-permute-start.36 = (f32[32,768]{1,0:T(8,128)S(1)}, f32[32,768]{1,0:T(8,128)S(1)}, u32[]{:S(2)}, u32[]{:S(2)}) collective-permute-start(f32[32,768]{1,0:T(8,128)S(1)} %get-tuple-element.116), channel_id=1, source_target_pairs={{0,16},{4,20},{8,24},{12,28},{16,0},{20,4},{24,8},{28,12},{1,17},{... | collective-permute-start | bytes 294920 | tf_op jit(solution)/shard_map/ppermute | solution.py:688
  99.1 11.0 %collective-permute-start.37 = (f32[32,768]{1,0:T(8,128)S(1)}, f32[32,768]{1,0:T(8,128)S(1)}, u32[]{:S(2)}, u32[]{:S(2)}) collective-permute-start(f32[32,768]{1,0:T(8,128)S(1)} %get-tuple-element.117), channel_id=1, source_target_pairs={{0,4},{4,0},{8,12},{12,8},{16,20},{20,16},{24,28},{28,24},{1,5},{5... | collective-permute-start | bytes 294920 | tf_op jit(solution)/shard_map/ppermute | solution.py:688
  100.5 14.6 %collective-permute-start.38 = (f32[32,768]{1,0:T(8,128)S(1)}, f32[32,768]{1,0:T(8,128)S(1)}, u32[]{:S(2)}, u32[]{:S(2)}) collective-permute-start(f32[32,768]{1,0:T(8,128)S(1)} %get-tuple-element.118), channel_id=1, source_target_pairs={{0,20},{4,16},{8,28},{12,24},{16,4},{20,0},{24,12},{28,8},{1,21},{... | collective-permute-start | bytes 294920 | tf_op jit(solution)/shard_map/ppermute | solution.py:688
  102.8 12.2 %collective-permute-start.39 = (f32[32,768]{1,0:T(8,128)S(1)}, f32[32,768]{1,0:T(8,128)S(1)}, u32[]{:S(2)}, u32[]{:S(2)}) collective-permute-start(f32[32,768]{1,0:T(8,128)S(1)} %get-tuple-element.119), channel_id=1, source_target_pairs={{0,8},{4,12},{8,0},{12,4},{16,24},{20,28},{24,16},{28,20},{1,9},{5... | collective-permute-start | bytes 294920 | tf_op jit(solution)/shard_map/ppermute | solution.py:688
  105.0 10.1 %collective-permute-start.40 = (f32[32,768]{1,0:T(8,128)S(1)}, f32[32,768]{1,0:T(8,128)S(1)}, u32[]{:S(2)}, u32[]{:S(2)}) collective-permute-start(f32[32,768]{1,0:T(8,128)S(1)} %get-tuple-element.123), channel_id=1, source_target_pairs={{0,24},{4,28},{8,16},{12,20},{16,8},{20,12},{24,0},{28,4},{1,25},{... | collective-permute-start | bytes 294920 | tf_op jit(solution)/shard_map/ppermute | solution.py:688
  110.1 7.1 %collective-permute-start.41 = (f32[32,768]{1,0:T(8,128)S(1)}, f32[32,768]{1,0:T(8,128)S(1)}, u32[]{:S(2)}, u32[]{:S(2)}) collective-permute-start(f32[32,768]{1,0:T(8,128)S(1)} %get-tuple-element.124), channel_id=1, source_target_pairs={{0,12},{4,8},{8,4},{12,0},{16,28},{20,24},{24,20},{28,16},{1,13},{... | collective-permute-start | bytes 294920 | tf_op jit(solution)/shard_map/ppermute | solution.py:688
  110.1 7.5 %collective-permute-start.42 = (f32[32,768]{1,0:T(8,128)S(1)}, f32[32,768]{1,0:T(8,128)S(1)}, u32[]{:S(2)}, u32[]{:S(2)}) collective-permute-start(f32[32,768]{1,0:T(8,128)S(1)} %get-tuple-element.125), channel_id=1, source_target_pairs={{0,28},{4,24},{8,20},{12,16},{16,12},{20,8},{24,4},{28,0},{1,29},{... | collective-permute-start | bytes 294920 | tf_op jit(solution)/shard_map/ppermute | solution.py:688
  115.0 8.3 %collective-permute-start.33 = (f32[72,768]{1,0:T(8,128)S(1)}, f32[72,768]{1,0:T(8,128)S(1)}, u32[]{:S(2)}, u32[]{:S(2)}) collective-permute-start(f32[72,768]{1,0:T(8,128)S(1)} %get-tuple-element.108), channel_id=1, source_target_pairs={{0,2},{1,3},{2,0},{3,1},{4,6},{5,7},{6,4},{7,5},{8,10},{9,11},{10,... | collective-permute-start | bytes 663560 | tf_op jit(solution)/shard_map/ppermute | solution.py:688
  115.0 8.3 %collective-permute-start.34 = (f32[72,768]{1,0:T(8,128)S(1)}, f32[72,768]{1,0:T(8,128)S(1)}, u32[]{:S(2)}, u32[]{:S(2)}) collective-permute-start(f32[72,768]{1,0:T(8,128)S(1)} %get-tuple-element.109), channel_id=1, source_target_pairs={{0,1},{1,0},{2,3},{3,2},{4,5},{5,4},{6,7},{7,6},{8,9},{9,8},{10,11... | collective-permute-start | bytes 663560 | tf_op jit(solution)/shard_map/ppermute | solution.py:688
  115.0 8.9 %collective-permute-start.35 = (f32[72,768]{1,0:T(8,128)S(1)}, f32[72,768]{1,0:T(8,128)S(1)}, u32[]{:S(2)}, u32[]{:S(2)}) collective-permute-start(f32[72,768]{1,0:T(8,128)S(1)} %get-tuple-element.110), channel_id=1, source_target_pairs={{0,3},{1,2},{2,1},{3,0},{4,7},{5,6},{6,5},{7,4},{8,11},{9,10},{10,... | collective-permute-start | bytes 663560 | tf_op jit(solution)/shard_map/ppermute | solution.py:688
  119.2 13.4 %collective-permute-start.43 = (f32[72,768]{1,0:T(8,128)S(1)}, f32[72,768]{1,0:T(8,128)S(1)}, u32[]{:S(2)}, u32[]{:S(2)}) collective-permute-start(f32[72,768]{1,0:T(8,128)S(1)} %get-tuple-element.127), channel_id=1, source_target_pairs={{0,2},{1,3},{2,0},{3,1},{4,6},{5,7},{6,4},{7,5},{8,10},{9,11},{10,... | collective-permute-start | bytes 663560 | tf_op jit(solution)/shard_map/ppermute | solution.py:688
  120.0 12.6 %collective-permute-start.44 = (f32[72,768]{1,0:T(8,128)S(1)}, f32[72,768]{1,0:T(8,128)S(1)}, u32[]{:S(2)}, u32[]{:S(2)}) collective-permute-start(f32[72,768]{1,0:T(8,128)S(1)} %get-tuple-element.128), channel_id=1, source_target_pairs={{0,1},{1,0},{2,3},{3,2},{4,5},{5,4},{6,7},{7,6},{8,9},{9,8},{10,11... | collective-permute-start | bytes 663560 | tf_op jit(solution)/shard_map/ppermute | solution.py:688
  123.3 9.4 %collective-permute-start.45 = (f32[72,768]{1,0:T(8,128)S(1)}, f32[72,768]{1,0:T(8,128)S(1)}, u32[]{:S(2)}, u32[]{:S(2)}) collective-permute-start(f32[72,768]{1,0:T(8,128)S(1)} %get-tuple-element.129), channel_id=1, source_target_pairs={{0,3},{1,2},{2,1},{3,0},{4,7},{5,6},{6,5},{7,4},{8,11},{9,10},{10,... | collective-permute-start | bytes 663560 | tf_op jit(solution)/shard_map/ppermute | solution.py:688
  125.4 10.2 %collective-permute-start.46 = (f32[3,64,256]{2,1,0:T(8,128)S(1)}, f32[3,64,256]{2,1,0:T(8,128)S(1)}, u32[]{:S(2)}, u32[]{:S(2)}) collective-permute-start(f32[3,64,256]{2,1,0:T(8,128)S(1)} %get-tuple-element.132), channel_id=1, source_target_pairs={{0,4},{4,8},{8,12},{12,16},{16,20},{20,24},{24,28},{28,0},{1,5},{5... | collective-permute-start | bytes 589832 | tf_op jit(solution)/shard_map/ppermute | solution.py:817
  126.2 9.5 %collective-permute-start.47 = (f32[3,64,256]{2,1,0:T(8,128)S(1)}, f32[3,64,256]{2,1,0:T(8,128)S(1)}, u32[]{:S(2)}, u32[]{:S(2)}) collective-permute-start(f32[3,64,256]{2,1,0:T(8,128)S(1)} %get-tuple-element.133), channel_id=1, source_target_pairs={{0,28},{4,0},{8,4},{12,8},{16,12},{20,16},{24,20},{28,24},{1,29},{... | collective-permute-start | bytes 589832 | tf_op jit(solution)/shard_map/ppermute | solution.py:816
  (9 other events, 108.2 us)

commit v9 on v8

--- a/solution.py
+++ b/solution.py
@@ -263,9 +263,9 @@
         out[...] = made[d]
 
 
-def x_ahead_kernel(sends, place, t_high, t_low, *refs):
+def x_ahead_kernel(sends, passed, place, t_high, t_low, *refs):
     held, made = refs[-2:]
-    outs, parts = refs[-2 - sends : -2], refs[: -2 - sends]
+    outs, parts = refs[-2 - sends : -2], refs[passed : -2 - sends]
     gather_blocks(parts, held, place[1])
     pencils, rows, width = held.shape
     cols = rows - RIM
@@ -747,16 +747,19 @@
     high_rim = lax.ppermute(rims[1], "gx", ring("gx", -1))
 
     tile = max(1, block // 4)
-    data = [None, None]
+    data, before = [None, None], []
     for n in (1, 0):
         chunk, part, width = chunks[n], parts[n], widths[n]
         shapes = sent_shapes("gz", block, width)
         part = call(
-            functools.partial(x_ahead_kernel, len(shapes)),
-            [here, (VM, x_ahead[0]), (VM, x_ahead[1])] + [(VM, p) for p in part],
+            functools.partial(x_ahead_kernel, len(shapes), len(before)),
+            [here, (VM, x_ahead[0]), (VM, x_ahead[1])]
+            + [(AN, b) for b in before]
+            + [(VM, p) for p in part],
             [(VM, shape) for shape in shapes],
             [((pencils, rows, width), F32), ((slabs, block, width), F32)],
         )
+        before = [part[0]]
         (entered,) = call(
             functools.partial(enter_kernel, chunk, nz),
             [here] + [(VM, p) for p in exchange(part, "gz")],

time: 139 us -> 142 us (1.022); the launches traced: 137 us -> 142 us
  starting transfers between devices: 65.5 us -> 74.8 us
  waiting for transfers between devices: 38.7 us -> 34.3 us
    ppermute x40, waiting for transfers between devices: 34.3 us -> 24.7 us  [exchange(): lax.ppermute(block, axis, [(i, i ^ k) for i in range(count)])]
    ppermute x40, starting transfers between devices: 50.9 us -> 59.8 us  [exchange(): lax.ppermute(block, axis, [(i, i ^ k) for i in range(count)])]
    ppermute x1, waiting for transfers between devices: 0.01 us -> 2.99 us  [on_device(): before = lax.ppermute(last, 'gz', ring('gz', 1))]
    ppermute x1, starting transfers between devices: 0.8 us -> 3.15 us  [on_device(): before = lax.ppermute(last, 'gz', ring('gz', 1))]
    ppermute x1, waiting for transfers between devices: 0.01 us -> 2.22 us  [on_device(): after = lax.ppermute(first, 'gz', ring('gz', -1))]
    ppermute x1, starting transfers between devices: 3.98 us -> 2.11 us  [on_device(): after = lax.ppermute(first, 'gz', ring('gz', -1))]
  transfers between devices with their start and end apart: 48 -> 48, of which waited for: 16 -> 15; matrix products, arithmetic and copies ran while one was open for 0% -> 0% of each run, Pallas kernels for 11% -> 14%
where the time goes in v9:
time: 142 us
  starting transfers between devices  74.8 us (53%)
  waiting for transfers between devices  34.3 us (24%)
  Pallas kernels  31.5 us (22%)
    ppermute x40, starting transfers between devices, exchange(): lax.ppermute(block, axis, [(i, i ^ k) for i in range(count)])  59.8 us
    pallas_call x16, Pallas kernels, call(): pl.pallas_call(kernel, out_shape=[jax.ShapeDtypeStruct(shape, F32) for _,...  31.5 us
    ppermute x40, waiting for transfers between devices, exchange(): lax.ppermute(block, axis, [(i, i ^ k) for i in range(count)])  24.7 us
    ppermute x1, starting transfers between devices, on_device(): up1 = lax.ppermute(packet, 'gz', ring('gz', -1))  6.03 us
    ppermute x1, starting transfers between devices, on_device(): before = lax.ppermute(last, 'gz', ring('gz', 1))  3.15 us
    ppermute x1, waiting for transfers between devices, on_device(): before = lax.ppermute(last, 'gz', ring('gz', 1))  2.99 us
    ppermute x1, waiting for transfers between devices, on_device(): down2 = lax.ppermute(movers, 'gz', ring('gz', 2))  2.89 us
  transfers between devices with their start and end apart: 48, of which 15 were waited for; matrix products, arithmetic and copies ran while one was open for 0% of the time, Pallas kernels for 14%

profile of v9, /device:TPU:0, one launch (start us, length us, event | category | flops | bytes accessed | tf_op | source)
XLA Modules:
  0.0 141.8 jit_solution(6655983421714725186)
XLA Ops:
  1.8 6.0 %collective-permute-start = (f32[8,512]{1,0:T(8,128)S(1)}, f32[8,512]{1,0:T(8,128)S(1)}, u32[]{:S(2)}, u32[]{:S(2)}) collective-permute-start(f32[8,512]{1,0:T(8,128)S(1)} %get-tuple-element.68.own), channel_id=1, source_target_pairs={{0,28},{4,0},{8,4},{12,8},{16,12},{20,16},{24,20},{28,24},{1,29},{... | collective-permute-start | bytes 49160 | tf_op jit(solution)/shard_map/ppermute | solution.py:722
  9.9 1.5 %collective-permute-done.2.up2 = f32[8,128]{1,0:T(8,128)S(1)} collective-permute-done((f32[8,128]{1,0:T(8,128)S(1)}, f32[8,128]{1,0:T(8,128)S(1)}, u32[]{:S(2)}, u32[]{:S(2)}) %collective-permute-start.2) | collective-permute-done | bytes 4128 | tf_op jit(solution)/shard_map/ppermute | solution.py:724
  11.4 2.9 %collective-permute-done.3.down2 = f32[8,128]{1,0:T(8,128)S(1)} collective-permute-done((f32[8,128]{1,0:T(8,128)S(1)}, f32[8,128]{1,0:T(8,128)S(1)}, u32[]{:S(2)}, u32[]{:S(2)}) %collective-permute-start.3) | collective-permute-done | bytes 4128 | tf_op jit(solution)/shard_map/ppermute | solution.py:725
  14.3 4.0 %shard_map.141 = (f32[3,4,64,256]{3,2,1,0:T(8,128)S(1)}, f32[24,256]{1,0:T(8,128)S(1)}, f32[24,256]{1,0:T(8,128)S(1)}, f32[72,768]{1,0:T(8,128)S(1)}, f32[72,768...) custom-call(s32[2]{0:T(128)S(1)} %pad_add_fusion.place, f32[8,512]{1,0:T(8,128)S(1)} %get-tuple-element.68.own, ...), custom_call_target="tpu_custom_call" | custom-call | flops 5000000000 | bytes 15000000 | tf_op jit(solution)/shard_map/pallas_call | solution.py:652
  18.3 1.6 %collective-permute-start.6 = (f32[72,768]{1,0:T(8,128)S(1)}, f32[72,768]{1,0:T(8,128)S(1)}, u32[]{:S(2)}, u32[]{:S(2)}) collective-permute-start(f32[72,768]{1,0:T(8,128)S(1)} %get-tuple-element.75), channel_id=1, source_target_pairs={{0,2},{1,3},{2,0},{3,1},{4,6},{5,7},{6,4},{7,5},{8,10},{9,11},{10,... | collective-permute-start | bytes 663560 | tf_op jit(solution)/shard_map/ppermute | solution.py:688
  20.5 6.6 %shard_map.142 = (f32[3,4,64,256]{3,2,1,0:T(8,128)S(1)}, f32[48,256]{1,0:T(8,128)S(1)}, f32[48,256]{1,0:T(8,128)S(1)}, f32[72,768]{1,0:T(8,128)S(1)}, f32[72,768...) custom-call(s32[2]{0:T(128)S(1)} %pad_add_fusion.place, f32[8,512]{1,0:T(8,128)S(1)} %get-tuple-element.68.own, ...), custom_call_target="tpu_custom_call" | custom-call | flops 5000000000 | bytes 15000000 | tf_op jit(solution)/shard_map/pallas_call | solution.py:652
  27.1 1.6 %collective-permute-start.9 = (f32[72,768]{1,0:T(8,128)S(1)}, f32[72,768]{1,0:T(8,128)S(1)}, u32[]{:S(2)}, u32[]{:S(2)}) collective-permute-start(f32[72,768]{1,0:T(8,128)S(1)} %get-tuple-element.80), channel_id=1, source_target_pairs={{0,2},{1,3},{2,0},{3,1},{4,6},{5,7},{6,4},{7,5},{8,10},{9,11},{10,... | collective-permute-start | bytes 663560 | tf_op jit(solution)/shard_map/ppermute | solution.py:688
  29.3 1.6 %shard_map.143 = (f32[32,768]{1,0:T(8,128)S(1)}, f32[32,768]{1,0:T(8,128)S(1)}, f32[32,768]{1,0:T(8,128)S(1)}, f32[32,768]{1,0:T(8,128)S(1)}, f32[32,768]{1,0:T(...) custom-call(s32[2]{0:T(128)S(1)} %pad_add_fusion.place, ...), custom_call_target="tpu_custom_call" | custom-call | flops 2000000000 | bytes 6000000 | tf_op jit(solution)/shard_map/pallas_call | solution.py:652
  30.9 4.5 %collective-permute-done.9.refs_2_ = f32[72,768]{1,0:T(8,128)S(1)} collective-permute-done((f32[72,768]{1,0:T(8,128)S(1)}, f32[72,768]{1,0:T(8,128)S(1)}, u32[]{:S(2)}, u32[]{:S(2)}) %collective-permute-start.9) | collective-permute-done | bytes 221216 | tf_op jit(solution)/shard_map/ppermute | solution.py:688
  35.5 2.8 %collective-permute-done.11.refs_4_ = f32[72,768]{1,0:T(8,128)S(1)} collective-permute-done((f32[72,768]{1,0:T(8,128)S(1)}, f32[72,768]{1,0:T(8,128)S(1)}, u32[]{:S(2)}, u32[]{:S(2)}) %collective-permute-start.11) | collective-permute-done | bytes 221216 | tf_op jit(solution)/shard_map/ppermute | solution.py:688
  38.3 1.6 %shard_map.144 = (f32[32,768]{1,0:T(8,128)S(1)}, f32[32,768]{1,0:T(8,128)S(1)}, f32[32,768]{1,0:T(8,128)S(1)}, f32[32,768]{1,0:T(8,128)S(1)}, f32[32,768]{1,0:T(...) custom-call(s32[2]{0:T(128)S(1)} %pad_add_fusion.place, ...), custom_call_target="tpu_custom_call" | custom-call | flops 2000000000 | bytes 6000000 | tf_op jit(solution)/shard_map/pallas_call | solution.py:652
  39.9 4.3 %collective-permute-start.13 = (f32[32,768]{1,0:T(8,128)S(1)}, f32[32,768]{1,0:T(8,128)S(1)}, u32[]{:S(2)}, u32[]{:S(2)}) collective-permute-start(f32[32,768]{1,0:T(8,128)S(1)} %get-tuple-element.85), channel_id=1, source_target_pairs={{0,4},{4,0},{8,12},{12,8},{16,20},{20,16},{24,28},{28,24},{1,5},{5... | collective-permute-start | bytes 294920 | tf_op jit(solution)/shard_map/ppermute | solution.py:688
  44.2 2.8 %collective-permute-start.19 = (f32[32,768]{1,0:T(8,128)S(1)}, f32[32,768]{1,0:T(8,128)S(1)}, u32[]{:S(2)}, u32[]{:S(2)}) collective-permute-start(f32[32,768]{1,0:T(8,128)S(1)} %get-tuple-element.91), channel_id=1, source_target_pairs={{0,16},{4,20},{8,24},{12,28},{16,0},{20,4},{24,8},{28,12},{1,17},{... | collective-permute-start | bytes 294920 | tf_op jit(solution)/shard_map/ppermute | solution.py:688
  47.0 1.5 %collective-permute-start.21 = (f32[32,768]{1,0:T(8,128)S(1)}, f32[32,768]{1,0:T(8,128)S(1)}, u32[]{:S(2)}, u32[]{:S(2)}) collective-permute-start(f32[32,768]{1,0:T(8,128)S(1)} %get-tuple-element.93), channel_id=1, source_target_pairs={{0,20},{4,16},{8,28},{12,24},{16,4},{20,0},{24,12},{28,8},{1,21},{... | collective-permute-start | bytes 294920 | tf_op jit(solution)/shard_map/ppermute | solution.py:688
  49.1 3.8 %collective-permute-start.23 = (f32[32,768]{1,0:T(8,128)S(1)}, f32[32,768]{1,0:T(8,128)S(1)}, u32[]{:S(2)}, u32[]{:S(2)}) collective-permute-start(f32[32,768]{1,0:T(8,128)S(1)} %get-tuple-element.95), channel_id=1, source_target_pairs={{0,24},{4,28},{8,16},{12,20},{16,8},{20,12},{24,0},{28,4},{1,25},{... | collective-permute-start | bytes 294920 | tf_op jit(solution)/shard_map/ppermute | solution.py:688
  52.9 2.3 %collective-permute-done.19.refs_1_ = f32[32,768]{1,0:T(8,128)S(1)} collective-permute-done((f32[32,768]{1,0:T(8,128)S(1)}, f32[32,768]{1,0:T(8,128)S(1)}, u32[]{:S(2)}, u32[]{:S(2)}) %collective-permute-start.19) | collective-permute-done | bytes 98336 | tf_op jit(solution)/shard_map/ppermute | solution.py:688
  55.3 2.3 %collective-permute-start.24 = (f32[32,768]{1,0:T(8,128)S(1)}, f32[32,768]{1,0:T(8,128)S(1)}, u32[]{:S(2)}, u32[]{:S(2)}) collective-permute-start(f32[32,768]{1,0:T(8,128)S(1)} %get-tuple-element.96), channel_id=1, source_target_pairs={{0,12},{4,8},{8,4},{12,0},{16,28},{20,24},{24,20},{28,16},{1,13},{... | collective-permute-start | bytes 294920 | tf_op jit(solution)/shard_map/ppermute | solution.py:688
  58.6 2.3 %collective-permute-start.14 = (f32[32,768]{1,0:T(8,128)S(1)}, f32[32,768]{1,0:T(8,128)S(1)}, u32[]{:S(2)}, u32[]{:S(2)}) collective-permute-start(f32[32,768]{1,0:T(8,128)S(1)} %get-tuple-element.86), channel_id=1, source_target_pairs={{0,20},{4,16},{8,28},{12,24},{16,4},{20,0},{24,12},{28,8},{1,21},{... | collective-permute-start | bytes 294920 | tf_op jit(solution)/shard_map/ppermute | solution.py:688
  60.9 2.0 %collective-permute-start.15 = (f32[32,768]{1,0:T(8,128)S(1)}, f32[32,768]{1,0:T(8,128)S(1)}, u32[]{:S(2)}, u32[]{:S(2)}) collective-permute-start(f32[32,768]{1,0:T(8,128)S(1)} %get-tuple-element.87), channel_id=1, source_target_pairs={{0,8},{4,12},{8,0},{12,4},{16,24},{20,28},{24,16},{28,20},{1,9},{5... | collective-permute-start | bytes 294920 | tf_op jit(solution)/shard_map/ppermute | solution.py:688
  64.2 2.4 %collective-permute-done.24.refs_6_ = f32[32,768]{1,0:T(8,128)S(1)} collective-permute-done((f32[32,768]{1,0:T(8,128)S(1)}, f32[32,768]{1,0:T(8,128)S(1)}, u32[]{:S(2)}, u32[]{:S(2)}) %collective-permute-start.24) | collective-permute-done | bytes 98336 | tf_op jit(solution)/shard_map/ppermute | solution.py:688
  66.7 1.5 %collective-permute-start.17 = (f32[32,768]{1,0:T(8,128)S(1)}, f32[32,768]{1,0:T(8,128)S(1)}, u32[]{:S(2)}, u32[]{:S(2)}) collective-permute-start(f32[32,768]{1,0:T(8,128)S(1)} %get-tuple-element.89), channel_id=1, source_target_pairs={{0,12},{4,8},{8,4},{12,0},{16,28},{20,24},{24,20},{28,16},{1,13},{... | collective-permute-start | bytes 294920 | tf_op jit(solution)/shard_map/ppermute | solution.py:688
  69.6 4.2 %collective-permute-done.14.refs_3_ = f32[32,768]{1,0:T(8,128)S(1)} collective-permute-done((f32[32,768]{1,0:T(8,128)S(1)}, f32[32,768]{1,0:T(8,128)S(1)}, u32[]{:S(2)}, u32[]{:S(2)}) %collective-permute-start.14) | collective-permute-done | bytes 98336 | tf_op jit(solution)/shard_map/ppermute | solution.py:688
  73.8 1.7 %collective-permute-start.5 = (f32[48,256]{1,0:T(8,128)S(1)}, f32[48,256]{1,0:T(8,128)S(1)}, u32[]{:S(2)}, u32[]{:S(2)}) collective-permute-start(f32[48,256]{1,0:T(8,128)S(1)} %get-tuple-element.73), channel_id=1, source_target_pairs={{0,3},{1,0},{2,1},{3,2},{4,7},{5,4},{6,5},{7,6},{8,11},{9,8},{10,9... | collective-permute-start | bytes 147464 | tf_op jit(solution)/shard_map/ppermute | solution.py:747
  75.6 1.6 %collective-permute-done.17.refs_6_ = f32[32,768]{1,0:T(8,128)S(1)} collective-permute-done((f32[32,768]{1,0:T(8,128)S(1)}, f32[32,768]{1,0:T(8,128)S(1)}, u32[]{:S(2)}, u32[]{:S(2)}) %collective-permute-start.17) | collective-permute-done | bytes 98336 | tf_op jit(solution)/shard_map/ppermute | solution.py:688
  78.5 2.3 %shard_map.147 = (f32[3,2,4,8,8,128]{5,4,3,2,1,0:T(8,128)S(1)}, f32[3,2,4,8,8,128]{5,4,3,2,1,0:T(8,128)S(1)}) custom-call(s32[2]{0:T(128)S(1)} %pad_add_fusion.place, f32[48,256]{1,0:T(8,128)S(1)} %collective-permute-done.4.low_rim.refs_1_, f32[48,256]{1,0:T(8,128)S(1)} %collective-permute-done.5.high_rim.refs_2_, ...), custom_call_target="tpu_custom_call" | custom-call | flops 5000000000 | bytes 15000000 | tf_op jit(solution)/shard_map/pallas_call | solution.py:652
  80.8 1.4 shard_map.148
  82.2 3.6 %collective-permute-start.26 = (f32[32,768]{1,0:T(8,128)S(1)}, f32[32,768]{1,0:T(8,128)S(1)}, u32[]{:S(2)}, u32[]{:S(2)}) collective-permute-start(f32[32,768]{1,0:T(8,128)S(1)} %get-tuple-element.100), channel_id=1, source_target_pairs={{0,16},{4,20},{8,24},{12,28},{16,0},{20,4},{24,8},{28,12},{1,17},{... | collective-permute-start | bytes 294920 | tf_op jit(solution)/shard_map/ppermute | solution.py:688
  85.8 1.5 %collective-permute-start.28 = (f32[32,768]{1,0:T(8,128)S(1)}, f32[32,768]{1,0:T(8,128)S(1)}, u32[]{:S(2)}, u32[]{:S(2)}) collective-permute-start(f32[32,768]{1,0:T(8,128)S(1)} %get-tuple-element.102), channel_id=1, source_target_pairs={{0,20},{4,16},{8,28},{12,24},{16,4},{20,0},{24,12},{28,8},{1,21},{... | collective-permute-start | bytes 294920 | tf_op jit(solution)/shard_map/ppermute | solution.py:688
  87.4 2.0 %collective-permute-start.29 = (f32[32,768]{1,0:T(8,128)S(1)}, f32[32,768]{1,0:T(8,128)S(1)}, u32[]{:S(2)}, u32[]{:S(2)}) collective-permute-start(f32[32,768]{1,0:T(8,128)S(1)} %get-tuple-element.103), channel_id=1, source_target_pairs={{0,8},{4,12},{8,0},{12,4},{16,24},{20,28},{24,16},{28,20},{1,9},{5... | collective-permute-start | bytes 294920 | tf_op jit(solution)/shard_map/ppermute | solution.py:688
  89.3 2.3 %collective-permute-start.30 = (f32[32,768]{1,0:T(8,128)S(1)}, f32[32,768]{1,0:T(8,128)S(1)}, u32[]{:S(2)}, u32[]{:S(2)}) collective-permute-start(f32[32,768]{1,0:T(8,128)S(1)} %get-tuple-element.104), channel_id=1, source_target_pairs={{0,24},{4,28},{8,16},{12,20},{16,8},{20,12},{24,0},{28,4},{1,25},{... | collective-permute-start | bytes 294920 | tf_op jit(solution)/shard_map/ppermute | solution.py:688
  91.7 2.9 %collective-permute-start.32 = (f32[32,768]{1,0:T(8,128)S(1)}, f32[32,768]{1,0:T(8,128)S(1)}, u32[]{:S(2)}, u32[]{:S(2)}) collective-permute-start(f32[32,768]{1,0:T(8,128)S(1)} %get-tuple-element.106), channel_id=1, source_target_pairs={{0,28},{4,24},{8,20},{12,16},{16,12},{20,8},{24,4},{28,0},{1,29},{... | collective-permute-start | bytes 294920 | tf_op jit(solution)/shard_map/ppermute | solution.py:688
  94.5 1.4 shard_map.151
  96.0 1.6 %collective-permute-start.36 = (f32[32,768]{1,0:T(8,128)S(1)}, f32[32,768]{1,0:T(8,128)S(1)}, u32[]{:S(2)}, u32[]{:S(2)}) collective-permute-start(f32[32,768]{1,0:T(8,128)S(1)} %get-tuple-element.116), channel_id=1, source_target_pairs={{0,16},{4,20},{8,24},{12,28},{16,0},{20,4},{24,8},{28,12},{1,17},{... | collective-permute-start | bytes 294920 | tf_op jit(solution)/shard_map/ppermute | solution.py:688
  97.6 2.7 %collective-permute-start.37 = (f32[32,768]{1,0:T(8,128)S(1)}, f32[32,768]{1,0:T(8,128)S(1)}, u32[]{:S(2)}, u32[]{:S(2)}) collective-permute-start(f32[32,768]{1,0:T(8,128)S(1)} %get-tuple-element.117), channel_id=1, source_target_pairs={{0,4},{4,0},{8,12},{12,8},{16,20},{20,16},{24,28},{28,24},{1,5},{5... | collective-permute-start | bytes 294920 | tf_op jit(solution)/shard_map/ppermute | solution.py:688
  100.2 1.8 %collective-permute-start.38 = (f32[32,768]{1,0:T(8,128)S(1)}, f32[32,768]{1,0:T(8,128)S(1)}, u32[]{:S(2)}, u32[]{:S(2)}) collective-permute-start(f32[32,768]{1,0:T(8,128)S(1)} %get-tuple-element.118), channel_id=1, source_target_pairs={{0,20},{4,16},{8,28},{12,24},{16,4},{20,0},{24,12},{28,8},{1,21},{... | collective-permute-start | bytes 294920 | tf_op jit(solution)/shard_map/ppermute | solution.py:688
  102.1 2.5 %collective-permute-start.39 = (f32[32,768]{1,0:T(8,128)S(1)}, f32[32,768]{1,0:T(8,128)S(1)}, u32[]{:S(2)}, u32[]{:S(2)}) collective-permute-start(f32[32,768]{1,0:T(8,128)S(1)} %get-tuple-element.119), channel_id=1, source_target_pairs={{0,8},{4,12},{8,0},{12,4},{16,24},{20,28},{24,16},{28,20},{1,9},{5... | collective-permute-start | bytes 294920 | tf_op jit(solution)/shard_map/ppermute | solution.py:688
  104.6 1.7 %shard_map.149 = (f32[72,768]{1,0:T(8,128)S(1)}, f32[72,768]{1,0:T(8,128)S(1)}, f32[72,768]{1,0:T(8,128)S(1)}, f32[72,768]{1,0:T(8,128)S(1)}) custom-call(s32[2]{0:T(128)S(1)} %pad_add_fusion.place, bf16[576,256]{1,0:T(8,128)(2,1)S(1)} %copy-done.5, bf16[576,256]{1,0:T(8,128)(2,1)S(1)} %copy-done.6, f32[32,768]{1,0:T(8,128)S(1)} %get-tuple-element.99.refs_0_, ...), custom_call_target="tpu_custom_call" | custom-call | flops 2000000000 | bytes 6000000 | tf_op jit(solution)/shard_map/pallas_call | solution.py:652
  106.3 3.2 %collective-permute-start.40 = (f32[32,768]{1,0:T(8,128)S(1)}, f32[32,768]{1,0:T(8,128)S(1)}, u32[]{:S(2)}, u32[]{:S(2)}) collective-permute-start(f32[32,768]{1,0:T(8,128)S(1)} %get-tuple-element.123), channel_id=1, source_target_pairs={{0,24},{4,28},{8,16},{12,20},{16,8},{20,12},{24,0},{28,4},{1,25},{... | collective-permute-start | bytes 294920 | tf_op jit(solution)/shard_map/ppermute | solution.py:688
  109.7 3.0 %collective-permute-start.41 = (f32[32,768]{1,0:T(8,128)S(1)}, f32[32,768]{1,0:T(8,128)S(1)}, u32[]{:S(2)}, u32[]{:S(2)}) collective-permute-start(f32[32,768]{1,0:T(8,128)S(1)} %get-tuple-element.124), channel_id=1, source_target_pairs={{0,12},{4,8},{8,4},{12,0},{16,28},{20,24},{24,20},{28,16},{1,13},{... | collective-permute-start | bytes 294920 | tf_op jit(solution)/shard_map/ppermute | solution.py:688
  115.3 2.2 %collective-permute-done.41.refs_6_ = f32[32,768]{1,0:T(8,128)S(1)} collective-permute-done((f32[32,768]{1,0:T(8,128)S(1)}, f32[32,768]{1,0:T(8,128)S(1)}, u32[]{:S(2)}, u32[]{:S(2)}) %collective-permute-start.41) | collective-permute-done | bytes 98336 | tf_op jit(solution)/shard_map/ppermute | solution.py:688
  117.5 2.5 %collective-permute-done.42.refs_7_ = f32[32,768]{1,0:T(8,128)S(1)} collective-permute-done((f32[32,768]{1,0:T(8,128)S(1)}, f32[32,768]{1,0:T(8,128)S(1)}, u32[]{:S(2)}, u32[]{:S(2)}) %collective-permute-start.42) | collective-permute-done | bytes 98336 | tf_op jit(solution)/shard_map/ppermute | solution.py:688
  120.0 1.7 %shard_map.153 = (f32[72,768]{1,0:T(8,128)S(1)}, f32[72,768]{1,0:T(8,128)S(1)}, f32[72,768]{1,0:T(8,128)S(1)}, f32[72,768]{1,0:T(8,128)S(1)}) custom-call(s32[2]{0:T(128)S(1)} %pad_add_fusion.place, bf16[576,256]{1,0:T(8,128)(2,1)S(1)} %copy-done.5, bf16[576,256]{1,0:T(8,128)(2,1)S(1)} %copy-done.6, f32[32,768]{1,0:T(8,128)S(1)} %get-tuple-element.115.refs_0_, ...), custom_call_target="tpu_custom_call" | custom-call | flops 2000000000 | bytes 6000000 | tf_op jit(solution)/shard_map/pallas_call | solution.py:652
  124.2 1.5 %shard_map.150 = (f32[3,4,80,256]{3,2,1,0:T(8,128)S(1)}, f32[3,64,256]{2,1,0:T(8,128)S(1)}, f32[3,64,256]{2,1,0:T(8,128)S(1)}) custom-call(s32[2]{0:T(128)S(1)} %pad_add_fusion.place, bf16[512,512]{1,0:T(8,128)(2,1)S(1)} %copy-done.1, bf16[512,512]{1,0:T(8,128)(2,1)S(1)} %copy-done.2, f32[72,768]{1,0:T(8,128)S(1)} %get-tuple-element.107.refs_0_.before, ...), custom_call_target="tpu_custom_call" | custom-call | flops 2000000000 | bytes 6000000 | tf_op jit(solution)/shard_map/pallas_call | solution.py:652
  125.7 3.2 %collective-permute-start.46 = (f32[3,64,256]{2,1,0:T(8,128)S(1)}, f32[3,64,256]{2,1,0:T(8,128)S(1)}, u32[]{:S(2)}, u32[]{:S(2)}) collective-permute-start(f32[3,64,256]{2,1,0:T(8,128)S(1)} %get-tuple-element.132), channel_id=1, source_target_pairs={{0,4},{4,8},{8,12},{12,16},{16,20},{20,24},{24,28},{28,0},{1,5},{5... | collective-permute-start | bytes 589832 | tf_op jit(solution)/shard_map/ppermute | solution.py:820
  128.9 2.1 %collective-permute-start.47 = (f32[3,64,256]{2,1,0:T(8,128)S(1)}, f32[3,64,256]{2,1,0:T(8,128)S(1)}, u32[]{:S(2)}, u32[]{:S(2)}) collective-permute-start(f32[3,64,256]{2,1,0:T(8,128)S(1)} %get-tuple-element.133), channel_id=1, source_target_pairs={{0,28},{4,0},{8,4},{12,8},{16,12},{20,16},{24,20},{28,24},{1,29},{... | collective-permute-start | bytes 589832 | tf_op jit(solution)/shard_map/ppermute | solution.py:819
  132.4 3.0 %shard_map.154 = (f32[3,8,64,256]{3,2,1,0:T(8,128)}, f32[3,8,64,256]{3,2,1,0:T(8,128)}) custom-call(s32[2]{0:T(128)S(1)} %pad_add_fusion.place, bf16[512,512]{1,0:T(8,128)(2,1)S(1)} %copy-done.1, bf16[512,512]{1,0:T(8,128)(2,1)S(1)} %copy-done.2, f32[3,4,80,256]{3,2,1,0:T(8,128)S(1)} %get-tuple-element.111.refs_0_.edges, ...), custom_call_target="tpu_custom_call" | custom-call | flops 4000000000 | bytes 12000000 | tf_op jit(solution)/shard_map/pallas_call | solution.py:652
  135.4 3.0 %collective-permute-done.46.before = f32[3,64,256]{2,1,0:T(8,128)S(1)} collective-permute-done((f32[3,64,256]{2,1,0:T(8,128)S(1)}, f32[3,64,256]{2,1,0:T(8,128)S(1)}, u32[]{:S(2)}, u32[]{:S(2)}) %collective-permute-start.46) | collective-permute-done | bytes 196640 | tf_op jit(solution)/shard_map/ppermute | solution.py:820
  138.4 2.2 %collective-permute-done.47.after = f32[3,64,256]{2,1,0:T(8,128)S(1)} collective-permute-done((f32[3,64,256]{2,1,0:T(8,128)S(1)}, f32[3,64,256]{2,1,0:T(8,128)S(1)}, u32[]{:S(2)}, u32[]{:S(2)}) %collective-permute-start.47) | collective-permute-done | bytes 196640 | tf_op jit(solution)/shard_map/ppermute | solution.py:819
  (83 shorter events, 17.8 us)
Async XLA Ops:
  1.8 12.5 %collective-permute-start = (f32[8,512]{1,0:T(8,128)S(1)}, f32[8,512]{1,0:T(8,128)S(1)}, u32[]{:S(2)}, u32[]{:S(2)}) collective-permute-start(f32[8,512]{1,0:T(8,128)S(1)} %get-tuple-element.68.own), channel_id=1, source_target_pairs={{0,28},{4,0},{8,4},{12,8},{16,12},{20,16},{24,20},{28,24},{1,29},{... | collective-permute-start | bytes 49160 | tf_op jit(solution)/shard_map/ppermute | solution.py:722
  7.8 6.5 %collective-permute-start.1 = (f32[8,512]{1,0:T(8,128)S(1)}, f32[8,512]{1,0:T(8,128)S(1)}, u32[]{:S(2)}, u32[]{:S(2)}) collective-permute-start(f32[8,512]{1,0:T(8,128)S(1)} %get-tuple-element.68.own), channel_id=1, source_target_pairs={{0,4},{4,8},{8,12},{12,16},{16,20},{20,24},{24,28},{28,0},{1,5},{5... | collective-permute-start | bytes 49160 | tf_op jit(solution)/shard_map/ppermute | solution.py:723
  7.8 3.6 %collective-permute-start.2 = (f32[8,128]{1,0:T(8,128)S(1)}, f32[8,128]{1,0:T(8,128)S(1)}, u32[]{:S(2)}, u32[]{:S(2)}) collective-permute-start(f32[8,128]{1,0:T(8,128)S(1)} %get-tuple-element.69), channel_id=1, source_target_pairs={{0,24},{4,28},{8,0},{12,4},{16,8},{20,12},{24,16},{28,20},{1,25},{... | collective-permute-start | bytes 12296 | tf_op jit(solution)/shard_map/ppermute | solution.py:724
  8.9 5.4 %collective-permute-start.3 = (f32[8,128]{1,0:T(8,128)S(1)}, f32[8,128]{1,0:T(8,128)S(1)}, u32[]{:S(2)}, u32[]{:S(2)}) collective-permute-start(f32[8,128]{1,0:T(8,128)S(1)} %get-tuple-element.69), channel_id=1, source_target_pairs={{0,8},{4,12},{8,16},{12,20},{16,24},{20,28},{24,0},{28,4},{1,9},{5... | collective-permute-start | bytes 12296 | tf_op jit(solution)/shard_map/ppermute | solution.py:725
  18.3 10.4 %collective-permute-start.6 = (f32[72,768]{1,0:T(8,128)S(1)}, f32[72,768]{1,0:T(8,128)S(1)}, u32[]{:S(2)}, u32[]{:S(2)}) collective-permute-start(f32[72,768]{1,0:T(8,128)S(1)} %get-tuple-element.75), channel_id=1, source_target_pairs={{0,2},{1,3},{2,0},{3,1},{4,6},{5,7},{6,4},{7,5},{8,10},{9,11},{10,... | collective-permute-start | bytes 663560 | tf_op jit(solution)/shard_map/ppermute | solution.py:688
  19.9 9.4 %collective-permute-start.7 = (f32[72,768]{1,0:T(8,128)S(1)}, f32[72,768]{1,0:T(8,128)S(1)}, u32[]{:S(2)}, u32[]{:S(2)}) collective-permute-start(f32[72,768]{1,0:T(8,128)S(1)} %get-tuple-element.76), channel_id=1, source_target_pairs={{0,1},{1,0},{2,3},{3,2},{4,5},{5,4},{6,7},{7,6},{8,9},{9,8},{10,11... | collective-permute-start | bytes 663560 | tf_op jit(solution)/shard_map/ppermute | solution.py:688
  19.9 9.4 %collective-permute-start.8 = (f32[72,768]{1,0:T(8,128)S(1)}, f32[72,768]{1,0:T(8,128)S(1)}, u32[]{:S(2)}, u32[]{:S(2)}) collective-permute-start(f32[72,768]{1,0:T(8,128)S(1)} %get-tuple-element.77), channel_id=1, source_target_pairs={{0,3},{1,2},{2,1},{3,0},{4,7},{5,6},{6,5},{7,4},{8,11},{9,10},{10,... | collective-permute-start | bytes 663560 | tf_op jit(solution)/shard_map/ppermute | solution.py:688
  27.1 8.4 %collective-permute-start.9 = (f32[72,768]{1,0:T(8,128)S(1)}, f32[72,768]{1,0:T(8,128)S(1)}, u32[]{:S(2)}, u32[]{:S(2)}) collective-permute-start(f32[72,768]{1,0:T(8,128)S(1)} %get-tuple-element.80), channel_id=1, source_target_pairs={{0,2},{1,3},{2,0},{3,1},{4,6},{5,7},{6,4},{7,5},{8,10},{9,11},{10,... | collective-permute-start | bytes 663560 | tf_op jit(solution)/shard_map/ppermute | solution.py:688
  28.7 6.8 %collective-permute-start.10 = (f32[72,768]{1,0:T(8,128)S(1)}, f32[72,768]{1,0:T(8,128)S(1)}, u32[]{:S(2)}, u32[]{:S(2)}) collective-permute-start(f32[72,768]{1,0:T(8,128)S(1)} %get-tuple-element.81), channel_id=1, source_target_pairs={{0,1},{1,0},{2,3},{3,2},{4,5},{5,4},{6,7},{7,6},{8,9},{9,8},{10,11... | collective-permute-start | bytes 663560 | tf_op jit(solution)/shard_map/ppermute | solution.py:688
  28.7 9.6 %collective-permute-start.11 = (f32[72,768]{1,0:T(8,128)S(1)}, f32[72,768]{1,0:T(8,128)S(1)}, u32[]{:S(2)}, u32[]{:S(2)}) collective-permute-start(f32[72,768]{1,0:T(8,128)S(1)} %get-tuple-element.82), channel_id=1, source_target_pairs={{0,3},{1,2},{2,1},{3,0},{4,7},{5,6},{6,5},{7,4},{8,11},{9,10},{10,... | collective-permute-start | bytes 663560 | tf_op jit(solution)/shard_map/ppermute | solution.py:688
  39.9 8.7 %collective-permute-start.12 = (f32[32,768]{1,0:T(8,128)S(1)}, f32[32,768]{1,0:T(8,128)S(1)}, u32[]{:S(2)}, u32[]{:S(2)}) collective-permute-start(f32[32,768]{1,0:T(8,128)S(1)} %get-tuple-element.84), channel_id=1, source_target_pairs={{0,16},{4,20},{8,24},{12,28},{16,0},{20,4},{24,8},{28,12},{1,17},{... | collective-permute-start | bytes 294920 | tf_op jit(solution)/shard_map/ppermute | solution.py:688
  39.9 9.1 %collective-permute-start.13 = (f32[32,768]{1,0:T(8,128)S(1)}, f32[32,768]{1,0:T(8,128)S(1)}, u32[]{:S(2)}, u32[]{:S(2)}) collective-permute-start(f32[32,768]{1,0:T(8,128)S(1)} %get-tuple-element.85), channel_id=1, source_target_pairs={{0,4},{4,0},{8,12},{12,8},{16,20},{20,16},{24,28},{28,24},{1,5},{5... | collective-permute-start | bytes 294920 | tf_op jit(solution)/shard_map/ppermute | solution.py:688
  44.2 11.1 %collective-permute-start.19 = (f32[32,768]{1,0:T(8,128)S(1)}, f32[32,768]{1,0:T(8,128)S(1)}, u32[]{:S(2)}, u32[]{:S(2)}) collective-permute-start(f32[32,768]{1,0:T(8,128)S(1)} %get-tuple-element.91), channel_id=1, source_target_pairs={{0,16},{4,20},{8,24},{12,28},{16,0},{20,4},{24,8},{28,12},{1,17},{... | collective-permute-start | bytes 294920 | tf_op jit(solution)/shard_map/ppermute | solution.py:688
  47.0 10.5 %collective-permute-start.20 = (f32[32,768]{1,0:T(8,128)S(1)}, f32[32,768]{1,0:T(8,128)S(1)}, u32[]{:S(2)}, u32[]{:S(2)}) collective-permute-start(f32[32,768]{1,0:T(8,128)S(1)} %get-tuple-element.92), channel_id=1, source_target_pairs={{0,4},{4,0},{8,12},{12,8},{16,20},{20,16},{24,28},{28,24},{1,5},{5... | collective-permute-start | bytes 294920 | tf_op jit(solution)/shard_map/ppermute | solution.py:688
  47.0 11.5 %collective-permute-start.21 = (f32[32,768]{1,0:T(8,128)S(1)}, f32[32,768]{1,0:T(8,128)S(1)}, u32[]{:S(2)}, u32[]{:S(2)}) collective-permute-start(f32[32,768]{1,0:T(8,128)S(1)} %get-tuple-element.93), channel_id=1, source_target_pairs={{0,20},{4,16},{8,28},{12,24},{16,4},{20,0},{24,12},{28,8},{1,21},{... | collective-permute-start | bytes 294920 | tf_op jit(solution)/shard_map/ppermute | solution.py:688
  48.6 12.3 %collective-permute-start.22 = (f32[32,768]{1,0:T(8,128)S(1)}, f32[32,768]{1,0:T(8,128)S(1)}, u32[]{:S(2)}, u32[]{:S(2)}) collective-permute-start(f32[32,768]{1,0:T(8,128)S(1)} %get-tuple-element.94), channel_id=1, source_target_pairs={{0,8},{4,12},{8,0},{12,4},{16,24},{20,28},{24,16},{28,20},{1,9},{5... | collective-permute-start | bytes 294920 | tf_op jit(solution)/shard_map/ppermute | solution.py:688
  49.1 13.8 %collective-permute-start.23 = (f32[32,768]{1,0:T(8,128)S(1)}, f32[32,768]{1,0:T(8,128)S(1)}, u32[]{:S(2)}, u32[]{:S(2)}) collective-permute-start(f32[32,768]{1,0:T(8,128)S(1)} %get-tuple-element.95), channel_id=1, source_target_pairs={{0,24},{4,28},{8,16},{12,20},{16,8},{20,12},{24,0},{28,4},{1,25},{... | collective-permute-start | bytes 294920 | tf_op jit(solution)/shard_map/ppermute | solution.py:688
  55.3 11.4 %collective-permute-start.24 = (f32[32,768]{1,0:T(8,128)S(1)}, f32[32,768]{1,0:T(8,128)S(1)}, u32[]{:S(2)}, u32[]{:S(2)}) collective-permute-start(f32[32,768]{1,0:T(8,128)S(1)} %get-tuple-element.96), channel_id=1, source_target_pairs={{0,12},{4,8},{8,4},{12,0},{16,28},{20,24},{24,20},{28,16},{1,13},{... | collective-permute-start | bytes 294920 | tf_op jit(solution)/shard_map/ppermute | solution.py:688
  57.6 10.6 %collective-permute-start.25 = (f32[32,768]{1,0:T(8,128)S(1)}, f32[32,768]{1,0:T(8,128)S(1)}, u32[]{:S(2)}, u32[]{:S(2)}) collective-permute-start(f32[32,768]{1,0:T(8,128)S(1)} %get-tuple-element.97), channel_id=1, source_target_pairs={{0,28},{4,24},{8,20},{12,16},{16,12},{20,8},{24,4},{28,0},{1,29},{... | collective-permute-start | bytes 294920 | tf_op jit(solution)/shard_map/ppermute | solution.py:688
  58.6 15.2 %collective-permute-start.14 = (f32[32,768]{1,0:T(8,128)S(1)}, f32[32,768]{1,0:T(8,128)S(1)}, u32[]{:S(2)}, u32[]{:S(2)}) collective-permute-start(f32[32,768]{1,0:T(8,128)S(1)} %get-tuple-element.86), channel_id=1, source_target_pairs={{0,20},{4,16},{8,28},{12,24},{16,4},{20,0},{24,12},{28,8},{1,21},{... | collective-permute-start | bytes 294920 | tf_op jit(solution)/shard_map/ppermute | solution.py:688
  60.9 12.9 %collective-permute-start.15 = (f32[32,768]{1,0:T(8,128)S(1)}, f32[32,768]{1,0:T(8,128)S(1)}, u32[]{:S(2)}, u32[]{:S(2)}) collective-permute-start(f32[32,768]{1,0:T(8,128)S(1)} %get-tuple-element.87), channel_id=1, source_target_pairs={{0,8},{4,12},{8,0},{12,4},{16,24},{20,28},{24,16},{28,20},{1,9},{5... | collective-permute-start | bytes 294920 | tf_op jit(solution)/shard_map/ppermute | solution.py:688
  62.9 12.7 %collective-permute-start.16 = (f32[32,768]{1,0:T(8,128)S(1)}, f32[32,768]{1,0:T(8,128)S(1)}, u32[]{:S(2)}, u32[]{:S(2)}) collective-permute-start(f32[32,768]{1,0:T(8,128)S(1)} %get-tuple-element.88), channel_id=1, source_target_pairs={{0,24},{4,28},{8,16},{12,20},{16,8},{20,12},{24,0},{28,4},{1,25},{... | collective-permute-start | bytes 294920 | tf_op jit(solution)/shard_map/ppermute | solution.py:688
  66.7 10.4 %collective-permute-start.17 = (f32[32,768]{1,0:T(8,128)S(1)}, f32[32,768]{1,0:T(8,128)S(1)}, u32[]{:S(2)}, u32[]{:S(2)}) collective-permute-start(f32[32,768]{1,0:T(8,128)S(1)} %get-tuple-element.89), channel_id=1, source_target_pairs={{0,12},{4,8},{8,4},{12,0},{16,28},{20,24},{24,20},{28,16},{1,13},{... | collective-permute-start | bytes 294920 | tf_op jit(solution)/shard_map/ppermute | solution.py:688
  68.2 8.9 %collective-permute-start.18 = (f32[32,768]{1,0:T(8,128)S(1)}, f32[32,768]{1,0:T(8,128)S(1)}, u32[]{:S(2)}, u32[]{:S(2)}) collective-permute-start(f32[32,768]{1,0:T(8,128)S(1)} %get-tuple-element.90), channel_id=1, source_target_pairs={{0,28},{4,24},{8,20},{12,16},{16,12},{20,8},{24,4},{28,0},{1,29},{... | collective-permute-start | bytes 294920 | tf_op jit(solution)/shard_map/ppermute | solution.py:688
  73.8 4.7 %collective-permute-start.4 = (f32[48,256]{1,0:T(8,128)S(1)}, f32[48,256]{1,0:T(8,128)S(1)}, u32[]{:S(2)}, u32[]{:S(2)}) collective-permute-start(f32[48,256]{1,0:T(8,128)S(1)} %get-tuple-element.72), channel_id=1, source_target_pairs={{0,1},{1,2},{2,3},{3,0},{4,5},{5,6},{6,7},{7,4},{8,9},{9,10},{10,1... | collective-permute-start | bytes 147464 | tf_op jit(solution)/shard_map/ppermute | solution.py:746
  73.8 4.7 %collective-permute-start.5 = (f32[48,256]{1,0:T(8,128)S(1)}, f32[48,256]{1,0:T(8,128)S(1)}, u32[]{:S(2)}, u32[]{:S(2)}) collective-permute-start(f32[48,256]{1,0:T(8,128)S(1)} %get-tuple-element.73), channel_id=1, source_target_pairs={{0,3},{1,0},{2,1},{3,2},{4,7},{5,4},{6,5},{7,6},{8,11},{9,8},{10,9... | collective-permute-start | bytes 147464 | tf_op jit(solution)/shard_map/ppermute | solution.py:747
  82.2 9.5 %collective-permute-start.26 = (f32[32,768]{1,0:T(8,128)S(1)}, f32[32,768]{1,0:T(8,128)S(1)}, u32[]{:S(2)}, u32[]{:S(2)}) collective-permute-start(f32[32,768]{1,0:T(8,128)S(1)} %get-tuple-element.100), channel_id=1, source_target_pairs={{0,16},{4,20},{8,24},{12,28},{16,0},{20,4},{24,8},{28,12},{1,17},{... | collective-permute-start | bytes 294920 | tf_op jit(solution)/shard_map/ppermute | solution.py:688
  85.8 5.9 %collective-permute-start.27 = (f32[32,768]{1,0:T(8,128)S(1)}, f32[32,768]{1,0:T(8,128)S(1)}, u32[]{:S(2)}, u32[]{:S(2)}) collective-permute-start(f32[32,768]{1,0:T(8,128)S(1)} %get-tuple-element.101), channel_id=1, source_target_pairs={{0,4},{4,0},{8,12},{12,8},{16,20},{20,16},{24,28},{28,24},{1,5},{5... | collective-permute-start | bytes 294920 | tf_op jit(solution)/shard_map/ppermute | solution.py:688
  85.8 10.1 %collective-permute-start.28 = (f32[32,768]{1,0:T(8,128)S(1)}, f32[32,768]{1,0:T(8,128)S(1)}, u32[]{:S(2)}, u32[]{:S(2)}) collective-permute-start(f32[32,768]{1,0:T(8,128)S(1)} %get-tuple-element.102), channel_id=1, source_target_pairs={{0,20},{4,16},{8,28},{12,24},{16,4},{20,0},{24,12},{28,8},{1,21},{... | collective-permute-start | bytes 294920 | tf_op jit(solution)/shard_map/ppermute | solution.py:688
  87.4 10.2 %collective-permute-start.29 = (f32[32,768]{1,0:T(8,128)S(1)}, f32[32,768]{1,0:T(8,128)S(1)}, u32[]{:S(2)}, u32[]{:S(2)}) collective-permute-start(f32[32,768]{1,0:T(8,128)S(1)} %get-tuple-element.103), channel_id=1, source_target_pairs={{0,8},{4,12},{8,0},{12,4},{16,24},{20,28},{24,16},{28,20},{1,9},{5... | collective-permute-start | bytes 294920 | tf_op jit(solution)/shard_map/ppermute | solution.py:688
  89.3 10.9 %collective-permute-start.30 = (f32[32,768]{1,0:T(8,128)S(1)}, f32[32,768]{1,0:T(8,128)S(1)}, u32[]{:S(2)}, u32[]{:S(2)}) collective-permute-start(f32[32,768]{1,0:T(8,128)S(1)} %get-tuple-element.104), channel_id=1, source_target_pairs={{0,24},{4,28},{8,16},{12,20},{16,8},{20,12},{24,0},{28,4},{1,25},{... | collective-permute-start | bytes 294920 | tf_op jit(solution)/shard_map/ppermute | solution.py:688
  91.7 10.4 %collective-permute-start.31 = (f32[32,768]{1,0:T(8,128)S(1)}, f32[32,768]{1,0:T(8,128)S(1)}, u32[]{:S(2)}, u32[]{:S(2)}) collective-permute-start(f32[32,768]{1,0:T(8,128)S(1)} %get-tuple-element.105), channel_id=1, source_target_pairs={{0,12},{4,8},{8,4},{12,0},{16,28},{20,24},{24,20},{28,16},{1,13},{... | collective-permute-start | bytes 294920 | tf_op jit(solution)/shard_map/ppermute | solution.py:688
  91.7 12.9 %collective-permute-start.32 = (f32[32,768]{1,0:T(8,128)S(1)}, f32[32,768]{1,0:T(8,128)S(1)}, u32[]{:S(2)}, u32[]{:S(2)}) collective-permute-start(f32[32,768]{1,0:T(8,128)S(1)} %get-tuple-element.106), channel_id=1, source_target_pairs={{0,28},{4,24},{8,20},{12,16},{16,12},{20,8},{24,4},{28,0},{1,29},{... | collective-permute-start | bytes 294920 | tf_op jit(solution)/shard_map/ppermute | solution.py:688
  96.0 13.8 %collective-permute-start.36 = (f32[32,768]{1,0:T(8,128)S(1)}, f32[32,768]{1,0:T(8,128)S(1)}, u32[]{:S(2)}, u32[]{:S(2)}) collective-permute-start(f32[32,768]{1,0:T(8,128)S(1)} %get-tuple-element.116), channel_id=1, source_target_pairs={{0,16},{4,20},{8,24},{12,28},{16,0},{20,4},{24,8},{28,12},{1,17},{... | collective-permute-start | bytes 294920 | tf_op jit(solution)/shard_map/ppermute | solution.py:688
  97.6 15.2 %collective-permute-start.37 = (f32[32,768]{1,0:T(8,128)S(1)}, f32[32,768]{1,0:T(8,128)S(1)}, u32[]{:S(2)}, u32[]{:S(2)}) collective-permute-start(f32[32,768]{1,0:T(8,128)S(1)} %get-tuple-element.117), channel_id=1, source_target_pairs={{0,4},{4,0},{8,12},{12,8},{16,20},{20,16},{24,28},{28,24},{1,5},{5... | collective-permute-start | bytes 294920 | tf_op jit(solution)/shard_map/ppermute | solution.py:688
  100.2 12.9 %collective-permute-start.38 = (f32[32,768]{1,0:T(8,128)S(1)}, f32[32,768]{1,0:T(8,128)S(1)}, u32[]{:S(2)}, u32[]{:S(2)}) collective-permute-start(f32[32,768]{1,0:T(8,128)S(1)} %get-tuple-element.118), channel_id=1, source_target_pairs={{0,20},{4,16},{8,28},{12,24},{16,4},{20,0},{24,12},{28,8},{1,21},{... | collective-permute-start | bytes 294920 | tf_op jit(solution)/shard_map/ppermute | solution.py:688
  102.1 12.2 %collective-permute-start.39 = (f32[32,768]{1,0:T(8,128)S(1)}, f32[32,768]{1,0:T(8,128)S(1)}, u32[]{:S(2)}, u32[]{:S(2)}) collective-permute-start(f32[32,768]{1,0:T(8,128)S(1)} %get-tuple-element.119), channel_id=1, source_target_pairs={{0,8},{4,12},{8,0},{12,4},{16,24},{20,28},{24,16},{28,20},{1,9},{5... | collective-permute-start | bytes 294920 | tf_op jit(solution)/shard_map/ppermute | solution.py:688
  106.3 8.0 %collective-permute-start.40 = (f32[32,768]{1,0:T(8,128)S(1)}, f32[32,768]{1,0:T(8,128)S(1)}, u32[]{:S(2)}, u32[]{:S(2)}) collective-permute-start(f32[32,768]{1,0:T(8,128)S(1)} %get-tuple-element.123), channel_id=1, source_target_pairs={{0,24},{4,28},{8,16},{12,20},{16,8},{20,12},{24,0},{28,4},{1,25},{... | collective-permute-start | bytes 294920 | tf_op jit(solution)/shard_map/ppermute | solution.py:688
  109.7 7.8 %collective-permute-start.41 = (f32[32,768]{1,0:T(8,128)S(1)}, f32[32,768]{1,0:T(8,128)S(1)}, u32[]{:S(2)}, u32[]{:S(2)}) collective-permute-start(f32[32,768]{1,0:T(8,128)S(1)} %get-tuple-element.124), channel_id=1, source_target_pairs={{0,12},{4,8},{8,4},{12,0},{16,28},{20,24},{24,20},{28,16},{1,13},{... | collective-permute-start | bytes 294920 | tf_op jit(solution)/shard_map/ppermute | solution.py:688
  112.7 7.3 %collective-permute-start.42 = (f32[32,768]{1,0:T(8,128)S(1)}, f32[32,768]{1,0:T(8,128)S(1)}, u32[]{:S(2)}, u32[]{:S(2)}) collective-permute-start(f32[32,768]{1,0:T(8,128)S(1)} %get-tuple-element.125), channel_id=1, source_target_pairs={{0,28},{4,24},{8,20},{12,16},{16,12},{20,8},{24,4},{28,0},{1,29},{... | collective-permute-start | bytes 294920 | tf_op jit(solution)/shard_map/ppermute | solution.py:688
  113.1 9.9 %collective-permute-start.33 = (f32[72,768]{1,0:T(8,128)S(1)}, f32[72,768]{1,0:T(8,128)S(1)}, u32[]{:S(2)}, u32[]{:S(2)}) collective-permute-start(f32[72,768]{1,0:T(8,128)S(1)} %get-tuple-element.108), channel_id=1, source_target_pairs={{0,2},{1,3},{2,0},{3,1},{4,6},{5,7},{6,4},{7,5},{8,10},{9,11},{10,... | collective-permute-start | bytes 663560 | tf_op jit(solution)/shard_map/ppermute | solution.py:688
  114.3 9.6 %collective-permute-start.34 = (f32[72,768]{1,0:T(8,128)S(1)}, f32[72,768]{1,0:T(8,128)S(1)}, u32[]{:S(2)}, u32[]{:S(2)}) collective-permute-start(f32[72,768]{1,0:T(8,128)S(1)} %get-tuple-element.109), channel_id=1, source_target_pairs={{0,1},{1,0},{2,3},{3,2},{4,5},{5,4},{6,7},{7,6},{8,9},{9,8},{10,11... | collective-permute-start | bytes 663560 | tf_op jit(solution)/shard_map/ppermute | solution.py:688
  114.3 9.9 %collective-permute-start.35 = (f32[72,768]{1,0:T(8,128)S(1)}, f32[72,768]{1,0:T(8,128)S(1)}, u32[]{:S(2)}, u32[]{:S(2)}) collective-permute-start(f32[72,768]{1,0:T(8,128)S(1)} %get-tuple-element.110), channel_id=1, source_target_pairs={{0,3},{1,2},{2,1},{3,0},{4,7},{5,6},{6,5},{7,4},{8,11},{9,10},{10,... | collective-permute-start | bytes 663560 | tf_op jit(solution)/shard_map/ppermute | solution.py:688
  121.7 9.3 %collective-permute-start.43 = (f32[72,768]{1,0:T(8,128)S(1)}, f32[72,768]{1,0:T(8,128)S(1)}, u32[]{:S(2)}, u32[]{:S(2)}) collective-permute-start(f32[72,768]{1,0:T(8,128)S(1)} %get-tuple-element.127), channel_id=1, source_target_pairs={{0,2},{1,3},{2,0},{3,1},{4,6},{5,7},{6,4},{7,5},{8,10},{9,11},{10,... | collective-permute-start | bytes 663560 | tf_op jit(solution)/shard_map/ppermute | solution.py:688
  123.0 7.9 %collective-permute-start.44 = (f32[72,768]{1,0:T(8,128)S(1)}, f32[72,768]{1,0:T(8,128)S(1)}, u32[]{:S(2)}, u32[]{:S(2)}) collective-permute-start(f32[72,768]{1,0:T(8,128)S(1)} %get-tuple-element.128), channel_id=1, source_target_pairs={{0,1},{1,0},{2,3},{3,2},{4,5},{5,4},{6,7},{7,6},{8,9},{9,8},{10,11... | collective-permute-start | bytes 663560 | tf_op jit(solution)/shard_map/ppermute | solution.py:688
  123.0 9.3 %collective-permute-start.45 = (f32[72,768]{1,0:T(8,128)S(1)}, f32[72,768]{1,0:T(8,128)S(1)}, u32[]{:S(2)}, u32[]{:S(2)}) collective-permute-start(f32[72,768]{1,0:T(8,128)S(1)} %get-tuple-element.129), channel_id=1, source_target_pairs={{0,3},{1,2},{2,1},{3,0},{4,7},{5,6},{6,5},{7,4},{8,11},{9,10},{10,... | collective-permute-start | bytes 663560 | tf_op jit(solution)/shard_map/ppermute | solution.py:688
  125.7 12.7 %collective-permute-start.46 = (f32[3,64,256]{2,1,0:T(8,128)S(1)}, f32[3,64,256]{2,1,0:T(8,128)S(1)}, u32[]{:S(2)}, u32[]{:S(2)}) collective-permute-start(f32[3,64,256]{2,1,0:T(8,128)S(1)} %get-tuple-element.132), channel_id=1, source_target_pairs={{0,4},{4,8},{8,12},{12,16},{16,20},{20,24},{24,28},{28,0},{1,5},{5... | collective-permute-start | bytes 589832 | tf_op jit(solution)/shard_map/ppermute | solution.py:820
  128.9 11.7 %collective-permute-start.47 = (f32[3,64,256]{2,1,0:T(8,128)S(1)}, f32[3,64,256]{2,1,0:T(8,128)S(1)}, u32[]{:S(2)}, u32[]{:S(2)}) collective-permute-start(f32[3,64,256]{2,1,0:T(8,128)S(1)} %get-tuple-element.133), channel_id=1, source_target_pairs={{0,28},{4,0},{8,4},{12,8},{16,12},{20,16},{24,20},{28,24},{1,29},{... | collective-permute-start | bytes 589832 | tf_op jit(solution)/shard_map/ppermute | solution.py:819
  (9 other events, 87.2 us)

commit v10 on v9

--- a/solution.py
+++ b/solution.py
@@ -356,9 +356,8 @@
     lax.fori_loop(0, 3, body, 0)
 
 
-def pass_kernel(before, *refs):
-    for source, target in zip(refs[: len(refs) // 2], refs[len(refs) // 2 :]):
-        target[...] = source[...]
+def pass_kernel(*_):
+    pass
 
 
 def leave_kernel(pairs, nz, place, source, *refs):
@@ -680,6 +679,18 @@
     return [(count, rows, width)] if whole or not spread(axis) else [(rows, width)] * count
 
 
+def held_back(blocks, before):
+    return list(
+        call(
+            pass_kernel,
+            [(AN, before)] + [(AN, b) for b in blocks],
+            [(AN, b.shape) for b in blocks],
+            micros=0.1,
+            aliases={n + 1: n for n in range(len(blocks))},
+        )
+    )
+
+
 def exchange(blocks, axis, start=0):
     if not spread(axis):
         return [lax.all_to_all(blocks[0], axis, split_axis=0, concat_axis=0, tiled=True)]
@@ -742,14 +753,14 @@
         )
         meshes[n] = mesh
         rims = [rim_high, rim_low]
-        parts[n] = exchange(part, "gx")
+        parts[n] = part
     low_rim = lax.ppermute(rims[0], "gx", ring("gx", 1))
     high_rim = lax.ppermute(rims[1], "gx", ring("gx", -1))
 
     tile = max(1, block // 4)
     data, before = [None, None], []
     for n in (1, 0):
-        chunk, part, width = chunks[n], parts[n], widths[n]
+        chunk, part, width = chunks[n], exchange(parts[n], "gx"), widths[n]
         shapes = sent_shapes("gz", block, width)
         part = call(
             functools.partial(x_ahead_kernel, len(shapes), len(before)),
@@ -759,10 +770,13 @@
             [(VM, shape) for shape in shapes],
             [((pencils, rows, width), F32), ((slabs, block, width), F32)],
         )
-        before = [part[0]]
+        if n:
+            parts[0] = held_back(parts[0], part[0])
+        part = exchange(part, "gz")
+        before = part[1:4]
         (entered,) = call(
             functools.partial(enter_kernel, chunk, nz),
-            [here] + [(VM, p) for p in exchange(part, "gz")],
+            [here] + [(VM, p) for p in part],
             [(VM, (3, 2, 2 * len(chunk), slabs, tile, LANES))],
         )
         data[n] = entered
@@ -808,12 +822,7 @@
         [((pencils, rows, widths[0]), F32)],
     )
     if early < len(left[1]):
-        late = call(
-            pass_kernel,
-            [(AN, parts[0][0])] + [(VM, p) for p in left[1][early:]],
-            [(VM, p.shape) for p in left[1][early:]],
-            micros=0.3,
-        )
+        late = held_back(left[1][early:], parts[0][0])
         second += exchange(late, "gz", early)
     parts.append(back(second, widths[1]))
     after = lax.ppermute(first, "gz", ring("gz", -1))

time: 142 us -> 141 us (level)
  waiting for transfers between devices: 34.3 us -> 30.2 us
  starting transfers between devices: 74.8 us -> 77.8 us
    ppermute x40, starting transfers between devices: 59.8 us -> 63.2 us  [exchange(): lax.ppermute(block, axis, [(i, i ^ k) for i in range(count)])]
    ppermute x40, waiting for transfers between devices: 24.7 us -> 21.7 us  [exchange(): lax.ppermute(block, axis, [(i, i ^ k) for i in range(count)])]
    ppermute x1, waiting for transfers between devices: 2.99 us -> 1.38 us  [on_device(): before = lax.ppermute(last, 'gz', ring('gz', 1))]
    ppermute x1, starting transfers between devices: 3.15 us -> 1.7 us  [on_device(): before = lax.ppermute(last, 'gz', ring('gz', 1))]
    pallas_call x16 -> x17, Pallas kernels: 31.5 us -> 31.4 us  [call(): pl.pallas_call(kernel, out_shape=[jax.ShapeDtypeStruct(shape, F32) for _,...]
  transfers between devices with their start and end apart: 48 -> 48, of which waited for: 15 -> 19; matrix products, arithmetic and copies ran while one was open for 0% -> 0% of each run, Pallas kernels for 14% -> 14%
where the time goes in v10:
time: 141 us
  starting transfers between devices  77.8 us (55%)
  Pallas kernels  31.4 us (22%)
  waiting for transfers between devices  30.2 us (21%)
    ppermute x40, starting transfers between devices, exchange(): lax.ppermute(block, axis, [(i, i ^ k) for i in range(count)])  63.2 us
    pallas_call x17, Pallas kernels, call(): pl.pallas_call(kernel, out_shape=[jax.ShapeDtypeStruct(shape, F32) for _,...  31.4 us
    ppermute x40, waiting for transfers between devices, exchange(): lax.ppermute(block, axis, [(i, i ^ k) for i in range(count)])  21.7 us
    ppermute x1, starting transfers between devices, on_device(): up1 = lax.ppermute(packet, 'gz', ring('gz', -1))  6.03 us
    ppermute x1, starting transfers between devices, on_device(): after = lax.ppermute(first, 'gz', ring('gz', -1))  3.08 us
    ppermute x1, waiting for transfers between devices, on_device(): down2 = lax.ppermute(movers, 'gz', ring('gz', 2))  2.89 us
  transfers between devices with their start and end apart: 48, of which 19 were waited for; matrix products, arithmetic and copies ran while one was open for 0% of the time, Pallas kernels for 14%

profile of v10, /device:TPU:0, one launch (start us, length us, event | category | flops | bytes accessed | tf_op | source)
XLA Modules:
  0.0 140.6 jit_solution(8841747692559891310)
XLA Ops:
  1.8 6.0 %collective-permute-start = (f32[8,512]{1,0:T(8,128)S(1)}, f32[8,512]{1,0:T(8,128)S(1)}, u32[]{:S(2)}, u32[]{:S(2)}) collective-permute-start(f32[8,512]{1,0:T(8,128)S(1)} %get-tuple-element.72.own), channel_id=1, source_target_pairs={{0,28},{4,0},{8,4},{12,8},{16,12},{20,16},{24,20},{28,24},{1,29},{... | collective-permute-start | bytes 49160 | tf_op jit(solution)/shard_map/ppermute | solution.py:733
  9.9 1.5 %collective-permute-done.2.up2 = f32[8,128]{1,0:T(8,128)S(1)} collective-permute-done((f32[8,128]{1,0:T(8,128)S(1)}, f32[8,128]{1,0:T(8,128)S(1)}, u32[]{:S(2)}, u32[]{:S(2)}) %collective-permute-start.2) | collective-permute-done | bytes 4128 | tf_op jit(solution)/shard_map/ppermute | solution.py:735
  11.4 2.9 %collective-permute-done.3.down2 = f32[8,128]{1,0:T(8,128)S(1)} collective-permute-done((f32[8,128]{1,0:T(8,128)S(1)}, f32[8,128]{1,0:T(8,128)S(1)}, u32[]{:S(2)}, u32[]{:S(2)}) %collective-permute-start.3) | collective-permute-done | bytes 4128 | tf_op jit(solution)/shard_map/ppermute | solution.py:736
  14.3 4.0 %shard_map.141 = (f32[3,4,64,256]{3,2,1,0:T(8,128)S(1)}, f32[24,256]{1,0:T(8,128)S(1)}, f32[24,256]{1,0:T(8,128)S(1)}, f32[72,768]{1,0:T(8,128)S(1)}, f32[72,768...) custom-call(s32[2]{0:T(128)S(1)} %pad_add_fusion.place, f32[8,512]{1,0:T(8,128)S(1)} %get-tuple-element.72.own, ...), custom_call_target="tpu_custom_call" | custom-call | flops 5000000000 | bytes 15000000 | tf_op jit(solution)/shard_map/pallas_call | solution.py:651
  18.3 1.6 %collective-permute-start.6 = (f32[72,768]{1,0:T(8,128)S(1)}, f32[72,768]{1,0:T(8,128)S(1)}, u32[]{:S(2)}, u32[]{:S(2)}) collective-permute-start(f32[72,768]{1,0:T(8,128)S(1)} %get-tuple-element.79), channel_id=1, source_target_pairs={{0,2},{1,3},{2,0},{3,1},{4,6},{5,7},{6,4},{7,5},{8,10},{9,11},{10,... | collective-permute-start | bytes 663560 | tf_op jit(solution)/shard_map/ppermute | solution.py:699
  20.5 6.6 %shard_map.142 = (f32[3,4,64,256]{3,2,1,0:T(8,128)S(1)}, f32[48,256]{1,0:T(8,128)S(1)}, f32[48,256]{1,0:T(8,128)S(1)}, f32[72,768]{1,0:T(8,128)S(1)}, f32[72,768...) custom-call(s32[2]{0:T(128)S(1)} %pad_add_fusion.place, f32[8,512]{1,0:T(8,128)S(1)} %get-tuple-element.72.own, ...), custom_call_target="tpu_custom_call" | custom-call | flops 5000000000 | bytes 15000000 | tf_op jit(solution)/shard_map/pallas_call | solution.py:651
  28.0 1.6 %shard_map.143 = (f32[32,768]{1,0:T(8,128)S(1)}, f32[32,768]{1,0:T(8,128)S(1)}, f32[32,768]{1,0:T(8,128)S(1)}, f32[32,768]{1,0:T(8,128)S(1)}, f32[32,768]{1,0:T(...) custom-call(s32[2]{0:T(128)S(1)} %pad_add_fusion.place, ...), custom_call_target="tpu_custom_call" | custom-call | flops 2000000000 | bytes 6000000 | tf_op jit(solution)/shard_map/pallas_call | solution.py:651
  30.3 1.4 collective-permute-start.13
  31.9 4.2 %collective-permute-start.10 = (f32[32,768]{1,0:T(8,128)S(1)}, f32[32,768]{1,0:T(8,128)S(1)}, u32[]{:S(2)}, u32[]{:S(2)}) collective-permute-start(f32[32,768]{1,0:T(8,128)S(1)} %get-tuple-element.83), channel_id=1, source_target_pairs={{0,4},{4,0},{8,12},{12,8},{16,20},{20,16},{24,28},{28,24},{1,5},{5... | collective-permute-start | bytes 294920 | tf_op jit(solution)/shard_map/ppermute | solution.py:699
  36.1 2.6 %collective-permute-done.9.refs_0_.refs_1_ = f32[32,768]{1,0:T(8,128)S(1)} collective-permute-done((f32[32,768]{1,0:T(8,128)S(1)}, f32[32,768]{1,0:T(8,128)S(1)}, u32[]{:S(2)}, u32[]{:S(2)}) %collective-permute-start.9) | collective-permute-done | bytes 98336 | tf_op jit(solution)/shard_map/ppermute | solution.py:699
  38.7 3.3 %collective-permute-start.11 = (f32[32,768]{1,0:T(8,128)S(1)}, f32[32,768]{1,0:T(8,128)S(1)}, u32[]{:S(2)}, u32[]{:S(2)}) collective-permute-start(f32[32,768]{1,0:T(8,128)S(1)} %get-tuple-element.84), channel_id=1, source_target_pairs={{0,20},{4,16},{8,28},{12,24},{16,4},{20,0},{24,12},{28,8},{1,21},{... | collective-permute-start | bytes 294920 | tf_op jit(solution)/shard_map/ppermute | solution.py:699
  42.0 2.3 %collective-permute-start.22 = (f32[32,768]{1,0:T(8,128)S(1)}, f32[32,768]{1,0:T(8,128)S(1)}, u32[]{:S(2)}, u32[]{:S(2)}) collective-permute-start(f32[32,768]{1,0:T(8,128)S(1)} %get-tuple-element.102), channel_id=1, source_target_pairs={{0,8},{4,12},{8,0},{12,4},{16,24},{20,28},{24,16},{28,20},{1,9},{5... | collective-permute-start | bytes 294920 | tf_op jit(solution)/shard_map/ppermute | solution.py:699
  44.3 3.0 %collective-permute-done.11.refs_2_.refs_3_ = f32[32,768]{1,0:T(8,128)S(1)} collective-permute-done((f32[32,768]{1,0:T(8,128)S(1)}, f32[32,768]{1,0:T(8,128)S(1)}, u32[]{:S(2)}, u32[]{:S(2)}) %collective-permute-start.11) | collective-permute-done | bytes 98336 | tf_op jit(solution)/shard_map/ppermute | solution.py:699
  49.3 3.6 %collective-permute-start.25 = (f32[32,768]{1,0:T(8,128)S(1)}, f32[32,768]{1,0:T(8,128)S(1)}, u32[]{:S(2)}, u32[]{:S(2)}) collective-permute-start(f32[32,768]{1,0:T(8,128)S(1)} %get-tuple-element.105), channel_id=1, source_target_pairs={{0,28},{4,24},{8,20},{12,16},{16,12},{20,8},{24,4},{28,0},{1,29},{... | collective-permute-start | bytes 294920 | tf_op jit(solution)/shard_map/ppermute | solution.py:699
  52.9 1.6 %shard_map.145 = (f32[32,768]{1,0:T(8,128)S(1)}, f32[32,768]{1,0:T(8,128)S(1)}, f32[32,768]{1,0:T(8,128)S(1)}, f32[32,768]{1,0:T(8,128)S(1)}, f32[32,768]{1,0:T(...) custom-call(s32[2]{0:T(128)S(1)} %pad_add_fusion.place, ...), custom_call_target="tpu_custom_call" | custom-call | flops 2000000000 | bytes 6000000 | tf_op jit(solution)/shard_map/pallas_call | solution.py:651
  55.1 4.1 %collective-permute-start.16 = (f32[32,768]{1,0:T(8,128)S(1)}, f32[32,768]{1,0:T(8,128)S(1)}, u32[]{:S(2)}, u32[]{:S(2)}) collective-permute-start(f32[32,768]{1,0:T(8,128)S(1)} %get-tuple-element.96), channel_id=1, source_target_pairs={{0,4},{4,0},{8,12},{12,8},{16,20},{20,16},{24,28},{28,24},{1,5},{5... | collective-permute-start | bytes 294920 | tf_op jit(solution)/shard_map/ppermute | solution.py:699
  59.2 1.5 %collective-permute-start.18 = (f32[32,768]{1,0:T(8,128)S(1)}, f32[32,768]{1,0:T(8,128)S(1)}, u32[]{:S(2)}, u32[]{:S(2)}) collective-permute-start(f32[32,768]{1,0:T(8,128)S(1)} %get-tuple-element.98), channel_id=1, source_target_pairs={{0,8},{4,12},{8,0},{12,4},{16,24},{20,28},{24,16},{28,20},{1,9},{5... | collective-permute-start | bytes 294920 | tf_op jit(solution)/shard_map/ppermute | solution.py:699
  60.7 3.4 %collective-permute-start.19 = (f32[32,768]{1,0:T(8,128)S(1)}, f32[32,768]{1,0:T(8,128)S(1)}, u32[]{:S(2)}, u32[]{:S(2)}) collective-permute-start(f32[32,768]{1,0:T(8,128)S(1)} %get-tuple-element.99), channel_id=1, source_target_pairs={{0,24},{4,28},{8,16},{12,20},{16,8},{20,12},{24,0},{28,4},{1,25},{... | collective-permute-start | bytes 294920 | tf_op jit(solution)/shard_map/ppermute | solution.py:699
  64.1 2.3 %collective-permute-done.15.refs_1_ = f32[32,768]{1,0:T(8,128)S(1)} collective-permute-done((f32[32,768]{1,0:T(8,128)S(1)}, f32[32,768]{1,0:T(8,128)S(1)}, u32[]{:S(2)}, u32[]{:S(2)}) %collective-permute-start.15) | collective-permute-done | bytes 98336 | tf_op jit(solution)/shard_map/ppermute | solution.py:699
  66.4 2.7 %collective-permute-start.20 = (f32[32,768]{1,0:T(8,128)S(1)}, f32[32,768]{1,0:T(8,128)S(1)}, u32[]{:S(2)}, u32[]{:S(2)}) collective-permute-start(f32[32,768]{1,0:T(8,128)S(1)} %get-tuple-element.100), channel_id=1, source_target_pairs={{0,12},{4,8},{8,4},{12,0},{16,28},{20,24},{24,20},{28,16},{1,13},{... | collective-permute-start | bytes 294920 | tf_op jit(solution)/shard_map/ppermute | solution.py:699
  69.1 3.0 %collective-permute-start.21 = (f32[32,768]{1,0:T(8,128)S(1)}, f32[32,768]{1,0:T(8,128)S(1)}, u32[]{:S(2)}, u32[]{:S(2)}) collective-permute-start(f32[32,768]{1,0:T(8,128)S(1)} %get-tuple-element.101), channel_id=1, source_target_pairs={{0,28},{4,24},{8,20},{12,16},{16,12},{20,8},{24,4},{28,0},{1,29},{... | collective-permute-start | bytes 294920 | tf_op jit(solution)/shard_map/ppermute | solution.py:699
  73.5 1.7 %collective-permute-start.5 = (f32[48,256]{1,0:T(8,128)S(1)}, f32[48,256]{1,0:T(8,128)S(1)}, u32[]{:S(2)}, u32[]{:S(2)}) collective-permute-start(f32[48,256]{1,0:T(8,128)S(1)} %get-tuple-element.77), channel_id=1, source_target_pairs={{0,3},{1,0},{2,1},{3,2},{4,7},{5,4},{6,5},{7,6},{8,11},{9,8},{10,9... | collective-permute-start | bytes 147464 | tf_op jit(solution)/shard_map/ppermute | solution.py:758
  76.5 1.3 shard_map.146.refs_0_
  77.9 2.3 %shard_map.148 = (f32[3,2,4,8,8,128]{5,4,3,2,1,0:T(8,128)S(1)}, f32[3,2,4,8,8,128]{5,4,3,2,1,0:T(8,128)S(1)}) custom-call(s32[2]{0:T(128)S(1)} %pad_add_fusion.place, f32[48,256]{1,0:T(8,128)S(1)} %collective-permute-done.4.low_rim.refs_1_, f32[48,256]{1,0:T(8,128)S(1)} %collective-permute-done.5.high_rim.refs_2_, ...), custom_call_target="tpu_custom_call" | custom-call | flops 5000000000 | bytes 15000000 | tf_op jit(solution)/shard_map/pallas_call | solution.py:651
  80.2 1.4 shard_map.149
  81.6 2.6 %collective-permute-start.26 = (f32[32,768]{1,0:T(8,128)S(1)}, f32[32,768]{1,0:T(8,128)S(1)}, u32[]{:S(2)}, u32[]{:S(2)}) collective-permute-start(f32[32,768]{1,0:T(8,128)S(1)} %get-tuple-element.108), channel_id=1, source_target_pairs={{0,16},{4,20},{8,24},{12,28},{16,0},{20,4},{24,8},{28,12},{1,17},{... | collective-permute-start | bytes 294920 | tf_op jit(solution)/shard_map/ppermute | solution.py:699
  84.2 1.9 %collective-permute-start.28 = (f32[32,768]{1,0:T(8,128)S(1)}, f32[32,768]{1,0:T(8,128)S(1)}, u32[]{:S(2)}, u32[]{:S(2)}) collective-permute-start(f32[32,768]{1,0:T(8,128)S(1)} %get-tuple-element.110), channel_id=1, source_target_pairs={{0,20},{4,16},{8,28},{12,24},{16,4},{20,0},{24,12},{28,8},{1,21},{... | collective-permute-start | bytes 294920 | tf_op jit(solution)/shard_map/ppermute | solution.py:699
  86.1 1.7 %collective-permute-start.29 = (f32[32,768]{1,0:T(8,128)S(1)}, f32[32,768]{1,0:T(8,128)S(1)}, u32[]{:S(2)}, u32[]{:S(2)}) collective-permute-start(f32[32,768]{1,0:T(8,128)S(1)} %get-tuple-element.111), channel_id=1, source_target_pairs={{0,8},{4,12},{8,0},{12,4},{16,24},{20,28},{24,16},{28,20},{1,9},{5... | collective-permute-start | bytes 294920 | tf_op jit(solution)/shard_map/ppermute | solution.py:699
  87.8 2.2 %collective-permute-start.30 = (f32[32,768]{1,0:T(8,128)S(1)}, f32[32,768]{1,0:T(8,128)S(1)}, u32[]{:S(2)}, u32[]{:S(2)}) collective-permute-start(f32[32,768]{1,0:T(8,128)S(1)} %get-tuple-element.112), channel_id=1, source_target_pairs={{0,24},{4,28},{8,16},{12,20},{16,8},{20,12},{24,0},{28,4},{1,25},{... | collective-permute-start | bytes 294920 | tf_op jit(solution)/shard_map/ppermute | solution.py:699
  90.9 2.1 %collective-permute-start.31 = (f32[32,768]{1,0:T(8,128)S(1)}, f32[32,768]{1,0:T(8,128)S(1)}, u32[]{:S(2)}, u32[]{:S(2)}) collective-permute-start(f32[32,768]{1,0:T(8,128)S(1)} %get-tuple-element.113), channel_id=1, source_target_pairs={{0,12},{4,8},{8,4},{12,0},{16,28},{20,24},{24,20},{28,16},{1,13},{... | collective-permute-start | bytes 294920 | tf_op jit(solution)/shard_map/ppermute | solution.py:699
  93.0 3.0 %collective-permute-start.32 = (f32[32,768]{1,0:T(8,128)S(1)}, f32[32,768]{1,0:T(8,128)S(1)}, u32[]{:S(2)}, u32[]{:S(2)}) collective-permute-start(f32[32,768]{1,0:T(8,128)S(1)} %get-tuple-element.114), channel_id=1, source_target_pairs={{0,28},{4,24},{8,20},{12,16},{16,12},{20,8},{24,4},{28,0},{1,29},{... | collective-permute-start | bytes 294920 | tf_op jit(solution)/shard_map/ppermute | solution.py:699
  96.0 1.4 %shard_map.152 = (f32[32,768]{1,0:T(8,128)S(1)}, f32[32,768]{1,0:T(8,128)S(1)}, f32[32,768]{1,0:T(8,128)S(1)}, f32[32,768]{1,0:T(8,128)S(1)}, f32[32,768]{1,0:T(...) custom-call(s32[2]{0:T(128)S(1)} %pad_add_fusion.place, ...), custom_call_target="tpu_custom_call" | custom-call | flops 2000000000 | bytes 6000000 | tf_op jit(solution)/shard_map/pallas_call | solution.py:651
  98.2 2.3 %collective-permute-start.37 = (f32[32,768]{1,0:T(8,128)S(1)}, f32[32,768]{1,0:T(8,128)S(1)}, u32[]{:S(2)}, u32[]{:S(2)}) collective-permute-start(f32[32,768]{1,0:T(8,128)S(1)} %get-tuple-element.125), channel_id=1, source_target_pairs={{0,4},{4,0},{8,12},{12,8},{16,20},{20,16},{24,28},{28,24},{1,5},{5... | collective-permute-start | bytes 294920 | tf_op jit(solution)/shard_map/ppermute | solution.py:699
  100.5 3.0 %collective-permute-start.38 = (f32[32,768]{1,0:T(8,128)S(1)}, f32[32,768]{1,0:T(8,128)S(1)}, u32[]{:S(2)}, u32[]{:S(2)}) collective-permute-start(f32[32,768]{1,0:T(8,128)S(1)} %get-tuple-element.126), channel_id=1, source_target_pairs={{0,20},{4,16},{8,28},{12,24},{16,4},{20,0},{24,12},{28,8},{1,21},{... | collective-permute-start | bytes 294920 | tf_op jit(solution)/shard_map/ppermute | solution.py:699
  103.5 1.7 %shard_map.150 = (f32[72,768]{1,0:T(8,128)S(1)}, f32[72,768]{1,0:T(8,128)S(1)}, f32[72,768]{1,0:T(8,128)S(1)}, f32[72,768]{1,0:T(8,128)S(1)}) custom-call(s32[2]{0:T(128)S(1)} %pad_add_fusion.place, bf16[576,256]{1,0:T(8,128)(2,1)S(1)} %copy-done.5, bf16[576,256]{1,0:T(8,128)(2,1)S(1)} %copy-done.6, f32[32,768]{1,0:T(8,128)S(1)} %get-tuple-element.107.refs_0_, ...), custom_call_target="tpu_custom_call" | custom-call | flops 2000000000 | bytes 6000000 | tf_op jit(solution)/shard_map/pallas_call | solution.py:651
  105.2 1.9 %collective-permute-start.40 = (f32[32,768]{1,0:T(8,128)S(1)}, f32[32,768]{1,0:T(8,128)S(1)}, u32[]{:S(2)}, u32[]{:S(2)}) collective-permute-start(f32[32,768]{1,0:T(8,128)S(1)} %get-tuple-element.131), channel_id=1, source_target_pairs={{0,24},{4,28},{8,16},{12,20},{16,8},{20,12},{24,0},{28,4},{1,25},{... | collective-permute-start | bytes 294920 | tf_op jit(solution)/shard_map/ppermute | solution.py:699
  107.1 2.3 %collective-permute-done.36.refs_1_ = f32[32,768]{1,0:T(8,128)S(1)} collective-permute-done((f32[32,768]{1,0:T(8,128)S(1)}, f32[32,768]{1,0:T(8,128)S(1)}, u32[]{:S(2)}, u32[]{:S(2)}) %collective-permute-start.36) | collective-permute-done | bytes 98336 | tf_op jit(solution)/shard_map/ppermute | solution.py:699
  109.7 4.1 %collective-permute-start.42 = (f32[32,768]{1,0:T(8,128)S(1)}, f32[32,768]{1,0:T(8,128)S(1)}, u32[]{:S(2)}, u32[]{:S(2)}) collective-permute-start(f32[32,768]{1,0:T(8,128)S(1)} %get-tuple-element.133), channel_id=1, source_target_pairs={{0,28},{4,24},{8,20},{12,16},{16,12},{20,8},{24,4},{28,0},{1,29},{... | collective-permute-start | bytes 294920 | tf_op jit(solution)/shard_map/ppermute | solution.py:699
  114.6 1.6 %collective-permute-start.35 = (f32[72,768]{1,0:T(8,128)S(1)}, f32[72,768]{1,0:T(8,128)S(1)}, u32[]{:S(2)}, u32[]{:S(2)}) collective-permute-start(f32[72,768]{1,0:T(8,128)S(1)} %get-tuple-element.118), channel_id=1, source_target_pairs={{0,3},{1,2},{2,1},{3,0},{4,7},{5,6},{6,5},{7,4},{8,11},{9,10},{10,... | collective-permute-start | bytes 663560 | tf_op jit(solution)/shard_map/ppermute | solution.py:699
  117.7 1.7 %shard_map.154 = (f32[72,768]{1,0:T(8,128)S(1)}, f32[72,768]{1,0:T(8,128)S(1)}, f32[72,768]{1,0:T(8,128)S(1)}, f32[72,768]{1,0:T(8,128)S(1)}) custom-call(s32[2]{0:T(128)S(1)} %pad_add_fusion.place, bf16[576,256]{1,0:T(8,128)(2,1)S(1)} %copy-done.5, bf16[576,256]{1,0:T(8,128)(2,1)S(1)} %copy-done.6, f32[32,768]{1,0:T(8,128)S(1)} %get-tuple-element.123.refs_0_, ...), custom_call_target="tpu_custom_call" | custom-call | flops 2000000000 | bytes 6000000 | tf_op jit(solution)/shard_map/pallas_call | solution.py:651
  120.1 2.1 %collective-permute-done.33.refs_1_ = f32[72,768]{1,0:T(8,128)S(1)} collective-permute-done((f32[72,768]{1,0:T(8,128)S(1)}, f32[72,768]{1,0:T(8,128)S(1)}, u32[]{:S(2)}, u32[]{:S(2)}) %collective-permute-start.33) | collective-permute-done | bytes 221216 | tf_op jit(solution)/shard_map/ppermute | solution.py:699
  122.3 2.0 %collective-permute-done.35.refs_3_ = f32[72,768]{1,0:T(8,128)S(1)} collective-permute-done((f32[72,768]{1,0:T(8,128)S(1)}, f32[72,768]{1,0:T(8,128)S(1)}, u32[]{:S(2)}, u32[]{:S(2)}) %collective-permute-start.35) | collective-permute-done | bytes 221216 | tf_op jit(solution)/shard_map/ppermute | solution.py:699
  124.3 1.5 %shard_map.151 = (f32[3,4,80,256]{3,2,1,0:T(8,128)S(1)}, f32[3,64,256]{2,1,0:T(8,128)S(1)}, f32[3,64,256]{2,1,0:T(8,128)S(1)}) custom-call(s32[2]{0:T(128)S(1)} %pad_add_fusion.place, bf16[512,512]{1,0:T(8,128)(2,1)S(1)} %copy-done.1, bf16[512,512]{1,0:T(8,128)(2,1)S(1)} %copy-done.2, f32[72,768]{1,0:T(8,128)S(1)} %get-tuple-element.115.refs_0_.__0_, ...), custom_call_target="tpu_custom_call" | custom-call | flops 2000000000 | bytes 6000000 | tf_op jit(solution)/shard_map/pallas_call | solution.py:651
  125.7 1.7 %collective-permute-start.46 = (f32[3,64,256]{2,1,0:T(8,128)S(1)}, f32[3,64,256]{2,1,0:T(8,128)S(1)}, u32[]{:S(2)}, u32[]{:S(2)}) collective-permute-start(f32[3,64,256]{2,1,0:T(8,128)S(1)} %get-tuple-element.140), channel_id=1, source_target_pairs={{0,4},{4,8},{8,12},{12,16},{16,20},{20,24},{24,28},{28,0},{1,5},{5... | collective-permute-start | bytes 589832 | tf_op jit(solution)/shard_map/ppermute | solution.py:829
  127.4 3.1 %collective-permute-start.47 = (f32[3,64,256]{2,1,0:T(8,128)S(1)}, f32[3,64,256]{2,1,0:T(8,128)S(1)}, u32[]{:S(2)}, u32[]{:S(2)}) collective-permute-start(f32[3,64,256]{2,1,0:T(8,128)S(1)} %get-tuple-element.141), channel_id=1, source_target_pairs={{0,28},{4,0},{8,4},{12,8},{16,12},{20,16},{24,20},{28,24},{1,29},{... | collective-permute-start | bytes 589832 | tf_op jit(solution)/shard_map/ppermute | solution.py:828
  132.3 3.0 %shard_map.155 = (f32[3,8,64,256]{3,2,1,0:T(8,128)}, f32[3,8,64,256]{3,2,1,0:T(8,128)}) custom-call(s32[2]{0:T(128)S(1)} %pad_add_fusion.place, bf16[512,512]{1,0:T(8,128)(2,1)S(1)} %copy-done.1, bf16[512,512]{1,0:T(8,128)(2,1)S(1)} %copy-done.2, f32[3,4,80,256]{3,2,1,0:T(8,128)S(1)} %get-tuple-element.119.refs_0_.edges, ...), custom_call_target="tpu_custom_call" | custom-call | flops 4000000000 | bytes 12000000 | tf_op jit(solution)/shard_map/pallas_call | solution.py:651
  135.3 1.4 collective-permute-done.46.before
  136.7 2.7 %collective-permute-done.47.after = f32[3,64,256]{2,1,0:T(8,128)S(1)} collective-permute-done((f32[3,64,256]{2,1,0:T(8,128)S(1)}, f32[3,64,256]{2,1,0:T(8,128)S(1)}, u32[]{:S(2)}, u32[]{:S(2)}) %collective-permute-start.47) | collective-permute-done | bytes 196640 | tf_op jit(solution)/shard_map/ppermute | solution.py:828
  (84 shorter events, 18.9 us)
Async XLA Ops:
  1.8 12.5 %collective-permute-start = (f32[8,512]{1,0:T(8,128)S(1)}, f32[8,512]{1,0:T(8,128)S(1)}, u32[]{:S(2)}, u32[]{:S(2)}) collective-permute-start(f32[8,512]{1,0:T(8,128)S(1)} %get-tuple-element.72.own), channel_id=1, source_target_pairs={{0,28},{4,0},{8,4},{12,8},{16,12},{20,16},{24,20},{28,24},{1,29},{... | collective-permute-start | bytes 49160 | tf_op jit(solution)/shard_map/ppermute | solution.py:733
  7.8 6.5 %collective-permute-start.1 = (f32[8,512]{1,0:T(8,128)S(1)}, f32[8,512]{1,0:T(8,128)S(1)}, u32[]{:S(2)}, u32[]{:S(2)}) collective-permute-start(f32[8,512]{1,0:T(8,128)S(1)} %get-tuple-element.72.own), channel_id=1, source_target_pairs={{0,4},{4,8},{8,12},{12,16},{16,20},{20,24},{24,28},{28,0},{1,5},{5... | collective-permute-start | bytes 49160 | tf_op jit(solution)/shard_map/ppermute | solution.py:734
  7.8 3.6 %collective-permute-start.2 = (f32[8,128]{1,0:T(8,128)S(1)}, f32[8,128]{1,0:T(8,128)S(1)}, u32[]{:S(2)}, u32[]{:S(2)}) collective-permute-start(f32[8,128]{1,0:T(8,128)S(1)} %get-tuple-element.73), channel_id=1, source_target_pairs={{0,24},{4,28},{8,0},{12,4},{16,8},{20,12},{24,16},{28,20},{1,25},{... | collective-permute-start | bytes 12296 | tf_op jit(solution)/shard_map/ppermute | solution.py:735
  8.9 5.4 %collective-permute-start.3 = (f32[8,128]{1,0:T(8,128)S(1)}, f32[8,128]{1,0:T(8,128)S(1)}, u32[]{:S(2)}, u32[]{:S(2)}) collective-permute-start(f32[8,128]{1,0:T(8,128)S(1)} %get-tuple-element.73), channel_id=1, source_target_pairs={{0,8},{4,12},{8,16},{12,20},{16,24},{20,28},{24,0},{28,4},{1,9},{5... | collective-permute-start | bytes 12296 | tf_op jit(solution)/shard_map/ppermute | solution.py:736
  18.3 8.8 %collective-permute-start.6 = (f32[72,768]{1,0:T(8,128)S(1)}, f32[72,768]{1,0:T(8,128)S(1)}, u32[]{:S(2)}, u32[]{:S(2)}) collective-permute-start(f32[72,768]{1,0:T(8,128)S(1)} %get-tuple-element.79), channel_id=1, source_target_pairs={{0,2},{1,3},{2,0},{3,1},{4,6},{5,7},{6,4},{7,5},{8,10},{9,11},{10,... | collective-permute-start | bytes 663560 | tf_op jit(solution)/shard_map/ppermute | solution.py:699
  19.9 7.2 %collective-permute-start.7 = (f32[72,768]{1,0:T(8,128)S(1)}, f32[72,768]{1,0:T(8,128)S(1)}, u32[]{:S(2)}, u32[]{:S(2)}) collective-permute-start(f32[72,768]{1,0:T(8,128)S(1)} %get-tuple-element.80), channel_id=1, source_target_pairs={{0,1},{1,0},{2,3},{3,2},{4,5},{5,4},{6,7},{7,6},{8,9},{9,8},{10,11... | collective-permute-start | bytes 663560 | tf_op jit(solution)/shard_map/ppermute | solution.py:699
  19.9 8.1 %collective-permute-start.8 = (f32[72,768]{1,0:T(8,128)S(1)}, f32[72,768]{1,0:T(8,128)S(1)}, u32[]{:S(2)}, u32[]{:S(2)}) collective-permute-start(f32[72,768]{1,0:T(8,128)S(1)} %get-tuple-element.81), channel_id=1, source_target_pairs={{0,3},{1,2},{2,1},{3,0},{4,7},{5,6},{6,5},{7,4},{8,11},{9,10},{10,... | collective-permute-start | bytes 663560 | tf_op jit(solution)/shard_map/ppermute | solution.py:699
  29.6 18.5 %collective-permute-start.12 = (f32[72,768]{1,0:T(8,128)S(1)}, f32[72,768]{1,0:T(8,128)S(1)}, u32[]{:S(2)}, u32[]{:S(2)}) collective-permute-start(f32[72,768]{1,0:T(8,128)S(1)} %get-tuple-element.91), channel_id=1, source_target_pairs={{0,2},{1,3},{2,0},{3,1},{4,6},{5,7},{6,4},{7,5},{8,10},{9,11},{10,... | collective-permute-start | bytes 663560 | tf_op jit(solution)/shard_map/ppermute | solution.py:699
  30.3 19.0 %collective-permute-start.13 = (f32[72,768]{1,0:T(8,128)S(1)}, f32[72,768]{1,0:T(8,128)S(1)}, u32[]{:S(2)}, u32[]{:S(2)}) collective-permute-start(f32[72,768]{1,0:T(8,128)S(1)} %get-tuple-element.92), channel_id=1, source_target_pairs={{0,1},{1,0},{2,3},{3,2},{4,5},{5,4},{6,7},{7,6},{8,9},{9,8},{10,11... | collective-permute-start | bytes 663560 | tf_op jit(solution)/shard_map/ppermute | solution.py:699
  31.7 21.2 %collective-permute-start.14 = (f32[72,768]{1,0:T(8,128)S(1)}, f32[72,768]{1,0:T(8,128)S(1)}, u32[]{:S(2)}, u32[]{:S(2)}) collective-permute-start(f32[72,768]{1,0:T(8,128)S(1)} %get-tuple-element.93), channel_id=1, source_target_pairs={{0,3},{1,2},{2,1},{3,0},{4,7},{5,6},{6,5},{7,4},{8,11},{9,10},{10,... | collective-permute-start | bytes 663560 | tf_op jit(solution)/shard_map/ppermute | solution.py:699
  31.9 6.8 %collective-permute-start.9 = (f32[32,768]{1,0:T(8,128)S(1)}, f32[32,768]{1,0:T(8,128)S(1)}, u32[]{:S(2)}, u32[]{:S(2)}) collective-permute-start(f32[32,768]{1,0:T(8,128)S(1)} %get-tuple-element.82), channel_id=1, source_target_pairs={{0,16},{4,20},{8,24},{12,28},{16,0},{20,4},{24,8},{28,12},{1,17},{... | collective-permute-start | bytes 294920 | tf_op jit(solution)/shard_map/ppermute | solution.py:699
  31.9 10.1 %collective-permute-start.10 = (f32[32,768]{1,0:T(8,128)S(1)}, f32[32,768]{1,0:T(8,128)S(1)}, u32[]{:S(2)}, u32[]{:S(2)}) collective-permute-start(f32[32,768]{1,0:T(8,128)S(1)} %get-tuple-element.83), channel_id=1, source_target_pairs={{0,4},{4,0},{8,12},{12,8},{16,20},{20,16},{24,28},{28,24},{1,5},{5... | collective-permute-start | bytes 294920 | tf_op jit(solution)/shard_map/ppermute | solution.py:699
  38.7 8.6 %collective-permute-start.11 = (f32[32,768]{1,0:T(8,128)S(1)}, f32[32,768]{1,0:T(8,128)S(1)}, u32[]{:S(2)}, u32[]{:S(2)}) collective-permute-start(f32[32,768]{1,0:T(8,128)S(1)} %get-tuple-element.84), channel_id=1, source_target_pairs={{0,20},{4,16},{8,28},{12,24},{16,4},{20,0},{24,12},{28,8},{1,21},{... | collective-permute-start | bytes 294920 | tf_op jit(solution)/shard_map/ppermute | solution.py:699
  42.0 13.1 %collective-permute-start.22 = (f32[32,768]{1,0:T(8,128)S(1)}, f32[32,768]{1,0:T(8,128)S(1)}, u32[]{:S(2)}, u32[]{:S(2)}) collective-permute-start(f32[32,768]{1,0:T(8,128)S(1)} %get-tuple-element.102), channel_id=1, source_target_pairs={{0,8},{4,12},{8,0},{12,4},{16,24},{20,28},{24,16},{28,20},{1,9},{5... | collective-permute-start | bytes 294920 | tf_op jit(solution)/shard_map/ppermute | solution.py:699
  47.3 11.9 %collective-permute-start.23 = (f32[32,768]{1,0:T(8,128)S(1)}, f32[32,768]{1,0:T(8,128)S(1)}, u32[]{:S(2)}, u32[]{:S(2)}) collective-permute-start(f32[32,768]{1,0:T(8,128)S(1)} %get-tuple-element.103), channel_id=1, source_target_pairs={{0,24},{4,28},{8,16},{12,20},{16,8},{20,12},{24,0},{28,4},{1,25},{... | collective-permute-start | bytes 294920 | tf_op jit(solution)/shard_map/ppermute | solution.py:699
  48.1 11.1 %collective-permute-start.24 = (f32[32,768]{1,0:T(8,128)S(1)}, f32[32,768]{1,0:T(8,128)S(1)}, u32[]{:S(2)}, u32[]{:S(2)}) collective-permute-start(f32[32,768]{1,0:T(8,128)S(1)} %get-tuple-element.104), channel_id=1, source_target_pairs={{0,12},{4,8},{8,4},{12,0},{16,28},{20,24},{24,20},{28,16},{1,13},{... | collective-permute-start | bytes 294920 | tf_op jit(solution)/shard_map/ppermute | solution.py:699
  49.3 11.4 %collective-permute-start.25 = (f32[32,768]{1,0:T(8,128)S(1)}, f32[32,768]{1,0:T(8,128)S(1)}, u32[]{:S(2)}, u32[]{:S(2)}) collective-permute-start(f32[32,768]{1,0:T(8,128)S(1)} %get-tuple-element.105), channel_id=1, source_target_pairs={{0,28},{4,24},{8,20},{12,16},{16,12},{20,8},{24,4},{28,0},{1,29},{... | collective-permute-start | bytes 294920 | tf_op jit(solution)/shard_map/ppermute | solution.py:699
  54.5 12.0 %collective-permute-start.15 = (f32[32,768]{1,0:T(8,128)S(1)}, f32[32,768]{1,0:T(8,128)S(1)}, u32[]{:S(2)}, u32[]{:S(2)}) collective-permute-start(f32[32,768]{1,0:T(8,128)S(1)} %get-tuple-element.95), channel_id=1, source_target_pairs={{0,16},{4,20},{8,24},{12,28},{16,0},{20,4},{24,8},{28,12},{1,17},{... | collective-permute-start | bytes 294920 | tf_op jit(solution)/shard_map/ppermute | solution.py:699
  55.1 14.1 %collective-permute-start.16 = (f32[32,768]{1,0:T(8,128)S(1)}, f32[32,768]{1,0:T(8,128)S(1)}, u32[]{:S(2)}, u32[]{:S(2)}) collective-permute-start(f32[32,768]{1,0:T(8,128)S(1)} %get-tuple-element.96), channel_id=1, source_target_pairs={{0,4},{4,0},{8,12},{12,8},{16,20},{20,16},{24,28},{28,24},{1,5},{5... | collective-permute-start | bytes 294920 | tf_op jit(solution)/shard_map/ppermute | solution.py:699
  59.2 14.3 %collective-permute-start.17 = (f32[32,768]{1,0:T(8,128)S(1)}, f32[32,768]{1,0:T(8,128)S(1)}, u32[]{:S(2)}, u32[]{:S(2)}) collective-permute-start(f32[32,768]{1,0:T(8,128)S(1)} %get-tuple-element.97), channel_id=1, source_target_pairs={{0,20},{4,16},{8,28},{12,24},{16,4},{20,0},{24,12},{28,8},{1,21},{... | collective-permute-start | bytes 294920 | tf_op jit(solution)/shard_map/ppermute | solution.py:699
  59.2 14.3 %collective-permute-start.18 = (f32[32,768]{1,0:T(8,128)S(1)}, f32[32,768]{1,0:T(8,128)S(1)}, u32[]{:S(2)}, u32[]{:S(2)}) collective-permute-start(f32[32,768]{1,0:T(8,128)S(1)} %get-tuple-element.98), channel_id=1, source_target_pairs={{0,8},{4,12},{8,0},{12,4},{16,24},{20,28},{24,16},{28,20},{1,9},{5... | collective-permute-start | bytes 294920 | tf_op jit(solution)/shard_map/ppermute | solution.py:699
  60.7 14.6 %collective-permute-start.19 = (f32[32,768]{1,0:T(8,128)S(1)}, f32[32,768]{1,0:T(8,128)S(1)}, u32[]{:S(2)}, u32[]{:S(2)}) collective-permute-start(f32[32,768]{1,0:T(8,128)S(1)} %get-tuple-element.99), channel_id=1, source_target_pairs={{0,24},{4,28},{8,16},{12,20},{16,8},{20,12},{24,0},{28,4},{1,25},{... | collective-permute-start | bytes 294920 | tf_op jit(solution)/shard_map/ppermute | solution.py:699
  66.4 8.8 %collective-permute-start.20 = (f32[32,768]{1,0:T(8,128)S(1)}, f32[32,768]{1,0:T(8,128)S(1)}, u32[]{:S(2)}, u32[]{:S(2)}) collective-permute-start(f32[32,768]{1,0:T(8,128)S(1)} %get-tuple-element.100), channel_id=1, source_target_pairs={{0,12},{4,8},{8,4},{12,0},{16,28},{20,24},{24,20},{28,16},{1,13},{... | collective-permute-start | bytes 294920 | tf_op jit(solution)/shard_map/ppermute | solution.py:699
  69.1 7.4 %collective-permute-start.21 = (f32[32,768]{1,0:T(8,128)S(1)}, f32[32,768]{1,0:T(8,128)S(1)}, u32[]{:S(2)}, u32[]{:S(2)}) collective-permute-start(f32[32,768]{1,0:T(8,128)S(1)} %get-tuple-element.101), channel_id=1, source_target_pairs={{0,28},{4,24},{8,20},{12,16},{16,12},{20,8},{24,4},{28,0},{1,29},{... | collective-permute-start | bytes 294920 | tf_op jit(solution)/shard_map/ppermute | solution.py:699
  73.5 4.4 %collective-permute-start.4 = (f32[48,256]{1,0:T(8,128)S(1)}, f32[48,256]{1,0:T(8,128)S(1)}, u32[]{:S(2)}, u32[]{:S(2)}) collective-permute-start(f32[48,256]{1,0:T(8,128)S(1)} %get-tuple-element.76), channel_id=1, source_target_pairs={{0,1},{1,2},{2,3},{3,0},{4,5},{5,6},{6,7},{7,4},{8,9},{9,10},{10,1... | collective-permute-start | bytes 147464 | tf_op jit(solution)/shard_map/ppermute | solution.py:757
  73.5 4.4 %collective-permute-start.5 = (f32[48,256]{1,0:T(8,128)S(1)}, f32[48,256]{1,0:T(8,128)S(1)}, u32[]{:S(2)}, u32[]{:S(2)}) collective-permute-start(f32[48,256]{1,0:T(8,128)S(1)} %get-tuple-element.77), channel_id=1, source_target_pairs={{0,3},{1,0},{2,1},{3,2},{4,7},{5,4},{6,5},{7,6},{8,11},{9,8},{10,9... | collective-permute-start | bytes 147464 | tf_op jit(solution)/shard_map/ppermute | solution.py:758
  81.6 9.3 %collective-permute-start.26 = (f32[32,768]{1,0:T(8,128)S(1)}, f32[32,768]{1,0:T(8,128)S(1)}, u32[]{:S(2)}, u32[]{:S(2)}) collective-permute-start(f32[32,768]{1,0:T(8,128)S(1)} %get-tuple-element.108), channel_id=1, source_target_pairs={{0,16},{4,20},{8,24},{12,28},{16,0},{20,4},{24,8},{28,12},{1,17},{... | collective-permute-start | bytes 294920 | tf_op jit(solution)/shard_map/ppermute | solution.py:699
  84.2 8.8 %collective-permute-start.27 = (f32[32,768]{1,0:T(8,128)S(1)}, f32[32,768]{1,0:T(8,128)S(1)}, u32[]{:S(2)}, u32[]{:S(2)}) collective-permute-start(f32[32,768]{1,0:T(8,128)S(1)} %get-tuple-element.109), channel_id=1, source_target_pairs={{0,4},{4,0},{8,12},{12,8},{16,20},{20,16},{24,28},{28,24},{1,5},{5... | collective-permute-start | bytes 294920 | tf_op jit(solution)/shard_map/ppermute | solution.py:699
  84.2 14.0 %collective-permute-start.28 = (f32[32,768]{1,0:T(8,128)S(1)}, f32[32,768]{1,0:T(8,128)S(1)}, u32[]{:S(2)}, u32[]{:S(2)}) collective-permute-start(f32[32,768]{1,0:T(8,128)S(1)} %get-tuple-element.110), channel_id=1, source_target_pairs={{0,20},{4,16},{8,28},{12,24},{16,4},{20,0},{24,12},{28,8},{1,21},{... | collective-permute-start | bytes 294920 | tf_op jit(solution)/shard_map/ppermute | solution.py:699
  86.1 12.2 %collective-permute-start.29 = (f32[32,768]{1,0:T(8,128)S(1)}, f32[32,768]{1,0:T(8,128)S(1)}, u32[]{:S(2)}, u32[]{:S(2)}) collective-permute-start(f32[32,768]{1,0:T(8,128)S(1)} %get-tuple-element.111), channel_id=1, source_target_pairs={{0,8},{4,12},{8,0},{12,4},{16,24},{20,28},{24,16},{28,20},{1,9},{5... | collective-permute-start | bytes 294920 | tf_op jit(solution)/shard_map/ppermute | solution.py:699
  87.8 12.7 %collective-permute-start.30 = (f32[32,768]{1,0:T(8,128)S(1)}, f32[32,768]{1,0:T(8,128)S(1)}, u32[]{:S(2)}, u32[]{:S(2)}) collective-permute-start(f32[32,768]{1,0:T(8,128)S(1)} %get-tuple-element.112), channel_id=1, source_target_pairs={{0,24},{4,28},{8,16},{12,20},{16,8},{20,12},{24,0},{28,4},{1,25},{... | collective-permute-start | bytes 294920 | tf_op jit(solution)/shard_map/ppermute | solution.py:699
  90.9 12.6 %collective-permute-start.31 = (f32[32,768]{1,0:T(8,128)S(1)}, f32[32,768]{1,0:T(8,128)S(1)}, u32[]{:S(2)}, u32[]{:S(2)}) collective-permute-start(f32[32,768]{1,0:T(8,128)S(1)} %get-tuple-element.113), channel_id=1, source_target_pairs={{0,12},{4,8},{8,4},{12,0},{16,28},{20,24},{24,20},{28,16},{1,13},{... | collective-permute-start | bytes 294920 | tf_op jit(solution)/shard_map/ppermute | solution.py:699
  93.0 10.5 %collective-permute-start.32 = (f32[32,768]{1,0:T(8,128)S(1)}, f32[32,768]{1,0:T(8,128)S(1)}, u32[]{:S(2)}, u32[]{:S(2)}) collective-permute-start(f32[32,768]{1,0:T(8,128)S(1)} %get-tuple-element.114), channel_id=1, source_target_pairs={{0,28},{4,24},{8,20},{12,16},{16,12},{20,8},{24,4},{28,0},{1,29},{... | collective-permute-start | bytes 294920 | tf_op jit(solution)/shard_map/ppermute | solution.py:699
  98.2 11.2 %collective-permute-start.36 = (f32[32,768]{1,0:T(8,128)S(1)}, f32[32,768]{1,0:T(8,128)S(1)}, u32[]{:S(2)}, u32[]{:S(2)}) collective-permute-start(f32[32,768]{1,0:T(8,128)S(1)} %get-tuple-element.124), channel_id=1, source_target_pairs={{0,16},{4,20},{8,24},{12,28},{16,0},{20,4},{24,8},{28,12},{1,17},{... | collective-permute-start | bytes 294920 | tf_op jit(solution)/shard_map/ppermute | solution.py:699
  98.2 11.5 %collective-permute-start.37 = (f32[32,768]{1,0:T(8,128)S(1)}, f32[32,768]{1,0:T(8,128)S(1)}, u32[]{:S(2)}, u32[]{:S(2)}) collective-permute-start(f32[32,768]{1,0:T(8,128)S(1)} %get-tuple-element.125), channel_id=1, source_target_pairs={{0,4},{4,0},{8,12},{12,8},{16,20},{20,16},{24,28},{28,24},{1,5},{5... | collective-permute-start | bytes 294920 | tf_op jit(solution)/shard_map/ppermute | solution.py:699
  100.5 13.5 %collective-permute-start.38 = (f32[32,768]{1,0:T(8,128)S(1)}, f32[32,768]{1,0:T(8,128)S(1)}, u32[]{:S(2)}, u32[]{:S(2)}) collective-permute-start(f32[32,768]{1,0:T(8,128)S(1)} %get-tuple-element.126), channel_id=1, source_target_pairs={{0,20},{4,16},{8,28},{12,24},{16,4},{20,0},{24,12},{28,8},{1,21},{... | collective-permute-start | bytes 294920 | tf_op jit(solution)/shard_map/ppermute | solution.py:699
  103.5 11.1 %collective-permute-start.39 = (f32[32,768]{1,0:T(8,128)S(1)}, f32[32,768]{1,0:T(8,128)S(1)}, u32[]{:S(2)}, u32[]{:S(2)}) collective-permute-start(f32[32,768]{1,0:T(8,128)S(1)} %get-tuple-element.127), channel_id=1, source_target_pairs={{0,8},{4,12},{8,0},{12,4},{16,24},{20,28},{24,16},{28,20},{1,9},{5... | collective-permute-start | bytes 294920 | tf_op jit(solution)/shard_map/ppermute | solution.py:699
  105.2 9.4 %collective-permute-start.40 = (f32[32,768]{1,0:T(8,128)S(1)}, f32[32,768]{1,0:T(8,128)S(1)}, u32[]{:S(2)}, u32[]{:S(2)}) collective-permute-start(f32[32,768]{1,0:T(8,128)S(1)} %get-tuple-element.131), channel_id=1, source_target_pairs={{0,24},{4,28},{8,16},{12,20},{16,8},{20,12},{24,0},{28,4},{1,25},{... | collective-permute-start | bytes 294920 | tf_op jit(solution)/shard_map/ppermute | solution.py:699
  109.4 7.1 %collective-permute-start.41 = (f32[32,768]{1,0:T(8,128)S(1)}, f32[32,768]{1,0:T(8,128)S(1)}, u32[]{:S(2)}, u32[]{:S(2)}) collective-permute-start(f32[32,768]{1,0:T(8,128)S(1)} %get-tuple-element.132), channel_id=1, source_target_pairs={{0,12},{4,8},{8,4},{12,0},{16,28},{20,24},{24,20},{28,16},{1,13},{... | collective-permute-start | bytes 294920 | tf_op jit(solution)/shard_map/ppermute | solution.py:699
  109.7 8.0 %collective-permute-start.42 = (f32[32,768]{1,0:T(8,128)S(1)}, f32[32,768]{1,0:T(8,128)S(1)}, u32[]{:S(2)}, u32[]{:S(2)}) collective-permute-start(f32[32,768]{1,0:T(8,128)S(1)} %get-tuple-element.133), channel_id=1, source_target_pairs={{0,28},{4,24},{8,20},{12,16},{16,12},{20,8},{24,4},{28,0},{1,29},{... | collective-permute-start | bytes 294920 | tf_op jit(solution)/shard_map/ppermute | solution.py:699
  114.0 8.2 %collective-permute-start.33 = (f32[72,768]{1,0:T(8,128)S(1)}, f32[72,768]{1,0:T(8,128)S(1)}, u32[]{:S(2)}, u32[]{:S(2)}) collective-permute-start(f32[72,768]{1,0:T(8,128)S(1)} %get-tuple-element.116), channel_id=1, source_target_pairs={{0,2},{1,3},{2,0},{3,1},{4,6},{5,7},{6,4},{7,5},{8,10},{9,11},{10,... | collective-permute-start | bytes 663560 | tf_op jit(solution)/shard_map/ppermute | solution.py:699
  114.6 7.6 %collective-permute-start.34 = (f32[72,768]{1,0:T(8,128)S(1)}, f32[72,768]{1,0:T(8,128)S(1)}, u32[]{:S(2)}, u32[]{:S(2)}) collective-permute-start(f32[72,768]{1,0:T(8,128)S(1)} %get-tuple-element.117), channel_id=1, source_target_pairs={{0,1},{1,0},{2,3},{3,2},{4,5},{5,4},{6,7},{7,6},{8,9},{9,8},{10,11... | collective-permute-start | bytes 663560 | tf_op jit(solution)/shard_map/ppermute | solution.py:699
  114.6 9.6 %collective-permute-start.35 = (f32[72,768]{1,0:T(8,128)S(1)}, f32[72,768]{1,0:T(8,128)S(1)}, u32[]{:S(2)}, u32[]{:S(2)}) collective-permute-start(f32[72,768]{1,0:T(8,128)S(1)} %get-tuple-element.118), channel_id=1, source_target_pairs={{0,3},{1,2},{2,1},{3,0},{4,7},{5,6},{6,5},{7,4},{8,11},{9,10},{10,... | collective-permute-start | bytes 663560 | tf_op jit(solution)/shard_map/ppermute | solution.py:699
  119.3 12.4 %collective-permute-start.43 = (f32[72,768]{1,0:T(8,128)S(1)}, f32[72,768]{1,0:T(8,128)S(1)}, u32[]{:S(2)}, u32[]{:S(2)}) collective-permute-start(f32[72,768]{1,0:T(8,128)S(1)} %get-tuple-element.135), channel_id=1, source_target_pairs={{0,2},{1,3},{2,0},{3,1},{4,6},{5,7},{6,4},{7,5},{8,10},{9,11},{10,... | collective-permute-start | bytes 663560 | tf_op jit(solution)/shard_map/ppermute | solution.py:699
  120.1 11.6 %collective-permute-start.44 = (f32[72,768]{1,0:T(8,128)S(1)}, f32[72,768]{1,0:T(8,128)S(1)}, u32[]{:S(2)}, u32[]{:S(2)}) collective-permute-start(f32[72,768]{1,0:T(8,128)S(1)} %get-tuple-element.136), channel_id=1, source_target_pairs={{0,1},{1,0},{2,3},{3,2},{4,5},{5,4},{6,7},{7,6},{8,9},{9,8},{10,11... | collective-permute-start | bytes 663560 | tf_op jit(solution)/shard_map/ppermute | solution.py:699
  122.3 10.0 %collective-permute-start.45 = (f32[72,768]{1,0:T(8,128)S(1)}, f32[72,768]{1,0:T(8,128)S(1)}, u32[]{:S(2)}, u32[]{:S(2)}) collective-permute-start(f32[72,768]{1,0:T(8,128)S(1)} %get-tuple-element.137), channel_id=1, source_target_pairs={{0,3},{1,2},{2,1},{3,0},{4,7},{5,6},{6,5},{7,4},{8,11},{9,10},{10,... | collective-permute-start | bytes 663560 | tf_op jit(solution)/shard_map/ppermute | solution.py:699
  125.7 11.0 %collective-permute-start.46 = (f32[3,64,256]{2,1,0:T(8,128)S(1)}, f32[3,64,256]{2,1,0:T(8,128)S(1)}, u32[]{:S(2)}, u32[]{:S(2)}) collective-permute-start(f32[3,64,256]{2,1,0:T(8,128)S(1)} %get-tuple-element.140), channel_id=1, source_target_pairs={{0,4},{4,8},{8,12},{12,16},{16,20},{20,24},{24,28},{28,0},{1,5},{5... | collective-permute-start | bytes 589832 | tf_op jit(solution)/shard_map/ppermute | solution.py:829
  127.4 12.0 %collective-permute-start.47 = (f32[3,64,256]{2,1,0:T(8,128)S(1)}, f32[3,64,256]{2,1,0:T(8,128)S(1)}, u32[]{:S(2)}, u32[]{:S(2)}) collective-permute-start(f32[3,64,256]{2,1,0:T(8,128)S(1)} %get-tuple-element.141), channel_id=1, source_target_pairs={{0,28},{4,0},{8,4},{12,8},{16,12},{20,16},{24,20},{28,24},{1,29},{... | collective-permute-start | bytes 589832 | tf_op jit(solution)/shard_map/ppermute | solution.py:828
  (9 other events, 84.3 us)

commit v11 on v8

--- a/solution.py
+++ b/solution.py
@@ -558,8 +558,8 @@
         out[c][...] = omega[c] + TIME_STEP * stretch
 
 
-def ends_kernel(_, edges, before, after, low_rim, high_rim, *refs):
-    meshes, vorticity, out, sems = refs[:-3], refs[-3], refs[-2], refs[-1]
+def ends_kernel(_, __, edges, before, after, low_rim, high_rim, *refs):
+    meshes, vorticity, out, sems = refs[:-4], refs[-3], refs[-2], refs[-1]
     cols = before.shape[1]
     size = edges.shape[1]
     copies = []
@@ -830,17 +830,18 @@
         sems=2 * planes,
         micros=4.0,
     )
-    (vorticity,) = call(
-        ends_kernel,
-        [(AN, vorticity)]
-        + [(VM, v) for v in (edges, before, after, low_rim, high_rim, *meshes)],
-        [(AN, ambient.shape)],
-        [((3, 2, cols, ny), F32)],
-        sems=2,
-        micros=1.0,
-        aliases={0: 0},
-    )
-    return velocity, vorticity
+    return tuple(
+        call(
+            ends_kernel,
+            [(AN, velocity), (AN, vorticity)]
+            + [(VM, v) for v in (edges, before, after, low_rim, high_rim, *meshes)],
+            [(AN, ambient.shape), (AN, ambient.shape)],
+            [((3, 2, cols, ny), F32)],
+            sems=2,
+            micros=1.0,
+            aliases={0: 0, 1: 1},
+        )
+    )
 
 
 def solution(mesh):

time: 139 us -> 131 us (0.942); the launches traced: 137 us -> 131 us
  waiting for transfers between devices: 38.7 us -> 29.1 us
  starting transfers between devices: 65.5 us -> 69.4 us
    ppermute x40, waiting for transfers between devices: 34.3 us -> 22.9 us  [exchange(): lax.ppermute(block, axis, [(i, i ^ k) for i in range(count)])]
    ppermute x1, starting transfers between devices: 3.98 us -> 0.8 us  [on_device(): after = lax.ppermute(first, 'gz', ring('gz', -1))]
    ppermute x1, starting transfers between devices: 0.8 us -> 3.98 us  [on_device(): before = lax.ppermute(last, 'gz', ring('gz', 1))]
    ppermute x1, waiting for transfers between devices: 0.01 us -> 3.09 us  [on_device(): before = lax.ppermute(last, 'gz', ring('gz', 1))]
    ppermute x1, starting transfers between devices: 6.03 us -> 3.08 us  [on_device(): up1 = lax.ppermute(packet, 'gz', ring('gz', -1))]
    ppermute x1, waiting for transfers between devices: 2.89 us -> 0.01 us  [on_device(): down2 = lax.ppermute(movers, 'gz', ring('gz', 2))]
    ppermute x40, starting transfers between devices: 50.9 us -> 53 us  [exchange(): lax.ppermute(block, axis, [(i, i ^ k) for i in range(count)])]
    ppermute x1, starting transfers between devices: 0.93 us -> 3.08 us  [on_device(): down2 = lax.ppermute(movers, 'gz', ring('gz', 2))]
  transfers between devices with their start and end apart: 48 -> 48, of which waited for: 16 -> 16; matrix products, arithmetic and copies ran while one was open for 0% -> 0% of each run, Pallas kernels for 11% -> 17%
where the time goes in v11:
time: 131 us
  starting transfers between devices  69.4 us (53%)
  Pallas kernels  31.5 us (24%)
  waiting for transfers between devices  29.1 us (22%)
    ppermute x40, starting transfers between devices, exchange(): lax.ppermute(block, axis, [(i, i ^ k) for i in range(count)])  53 us
    pallas_call x16, Pallas kernels, call(): pl.pallas_call(kernel, out_shape=[jax.ShapeDtypeStruct(shape, F32) for _,...  31.5 us
    ppermute x40, waiting for transfers between devices, exchange(): lax.ppermute(block, axis, [(i, i ^ k) for i in range(count)])  22.9 us
    ppermute x1, starting transfers between devices, on_device(): before = lax.ppermute(last, 'gz', ring('gz', 1))  3.98 us
    ppermute x1, waiting for transfers between devices, on_device(): before = lax.ppermute(last, 'gz', ring('gz', 1))  3.09 us
    ppermute x1, starting transfers between devices, on_device(): down2 = lax.ppermute(movers, 'gz', ring('gz', 2))  3.08 us
    ppermute x1, starting transfers between devices, on_device(): up1 = lax.ppermute(packet, 'gz', ring('gz', -1))  3.08 us
  transfers between devices with their start and end apart: 48, of which 16 were waited for; matrix products, arithmetic and copies ran while one was open for 0% of the time, Pallas kernels for 17%

profile of v11, /device:TPU:0, one launch (start us, length us, event | category | flops | bytes accessed | tf_op | source)
XLA Modules:
  0.0 131.2 jit_solution(17481004359385363812)
XLA Ops:
  1.8 3.1 %collective-permute-start.3 = (f32[8,128]{1,0:T(8,128)S(1)}, f32[8,128]{1,0:T(8,128)S(1)}, u32[]{:S(2)}, u32[]{:S(2)}) collective-permute-start(f32[8,128]{1,0:T(8,128)S(1)} %get-tuple-element.69), channel_id=1, source_target_pairs={{0,8},{4,12},{8,16},{12,20},{16,24},{20,28},{24,0},{28,4},{1,9},{5... | collective-permute-start | bytes 12296 | tf_op jit(solution)/shard_map/ppermute | solution.py:725
  4.8 2.1 %collective-permute-start.2 = (f32[8,128]{1,0:T(8,128)S(1)}, f32[8,128]{1,0:T(8,128)S(1)}, u32[]{:S(2)}, u32[]{:S(2)}) collective-permute-start(f32[8,128]{1,0:T(8,128)S(1)} %get-tuple-element.69), channel_id=1, source_target_pairs={{0,24},{4,28},{8,0},{12,4},{16,8},{20,12},{24,16},{28,20},{1,25},{... | collective-permute-start | bytes 12296 | tf_op jit(solution)/shard_map/ppermute | solution.py:724
  6.9 1.6 %collective-permute-start.1 = (f32[8,512]{1,0:T(8,128)S(1)}, f32[8,512]{1,0:T(8,128)S(1)}, u32[]{:S(2)}, u32[]{:S(2)}) collective-permute-start(f32[8,512]{1,0:T(8,128)S(1)} %get-tuple-element.68.own), channel_id=1, source_target_pairs={{0,4},{4,8},{8,12},{12,16},{16,20},{20,24},{24,28},{28,0},{1,5},{5... | collective-permute-start | bytes 49160 | tf_op jit(solution)/shard_map/ppermute | solution.py:723
  8.6 3.1 %collective-permute-start = (f32[8,512]{1,0:T(8,128)S(1)}, f32[8,512]{1,0:T(8,128)S(1)}, u32[]{:S(2)}, u32[]{:S(2)}) collective-permute-start(f32[8,512]{1,0:T(8,128)S(1)} %get-tuple-element.68.own), channel_id=1, source_target_pairs={{0,28},{4,0},{8,4},{12,8},{16,12},{20,16},{24,20},{28,24},{1,29},{... | collective-permute-start | bytes 49160 | tf_op jit(solution)/shard_map/ppermute | solution.py:722
  11.7 1.6 %collective-permute-done.1.down1 = f32[8,512]{1,0:T(8,128)S(1)} collective-permute-done((f32[8,512]{1,0:T(8,128)S(1)}, f32[8,512]{1,0:T(8,128)S(1)}, u32[]{:S(2)}, u32[]{:S(2)}) %collective-permute-start.1) | collective-permute-done | bytes 16416 | tf_op jit(solution)/shard_map/ppermute | solution.py:723
  13.4 3.9 %shard_map.141 = (f32[3,4,64,256]{3,2,1,0:T(8,128)S(1)}, f32[24,256]{1,0:T(8,128)S(1)}, f32[24,256]{1,0:T(8,128)S(1)}, f32[72,768]{1,0:T(8,128)S(1)}, f32[72,768...) custom-call(s32[2]{0:T(128)S(1)} %pad_add_fusion.place, f32[8,512]{1,0:T(8,128)S(1)} %get-tuple-element.68.own, ...), custom_call_target="tpu_custom_call" | custom-call | flops 5000000000 | bytes 15000000 | tf_op jit(solution)/shard_map/pallas_call | solution.py:652
  17.3 1.7 %collective-permute-start.16 = (f32[72,768]{1,0:T(8,128)S(1)}, f32[72,768]{1,0:T(8,128)S(1)}, u32[]{:S(2)}, u32[]{:S(2)}) collective-permute-start(f32[72,768]{1,0:T(8,128)S(1)} %get-tuple-element.87), channel_id=1, source_target_pairs={{0,2},{1,3},{2,0},{3,1},{4,6},{5,7},{6,4},{7,5},{8,10},{9,11},{10,... | collective-permute-start | bytes 663560 | tf_op jit(solution)/shard_map/ppermute | solution.py:688
  19.5 6.6 %shard_map.142 = (f32[3,4,64,256]{3,2,1,0:T(8,128)S(1)}, f32[48,256]{1,0:T(8,128)S(1)}, f32[48,256]{1,0:T(8,128)S(1)}, f32[72,768]{1,0:T(8,128)S(1)}, f32[72,768...) custom-call(s32[2]{0:T(128)S(1)} %pad_add_fusion.place, f32[8,512]{1,0:T(8,128)S(1)} %get-tuple-element.68.own, ...), custom_call_target="tpu_custom_call" | custom-call | flops 5000000000 | bytes 15000000 | tf_op jit(solution)/shard_map/pallas_call | solution.py:652
  26.1 1.7 %collective-permute-start.6 = (f32[72,768]{1,0:T(8,128)S(1)}, f32[72,768]{1,0:T(8,128)S(1)}, u32[]{:S(2)}, u32[]{:S(2)}) collective-permute-start(f32[72,768]{1,0:T(8,128)S(1)} %get-tuple-element.75), channel_id=1, source_target_pairs={{0,2},{1,3},{2,0},{3,1},{4,6},{5,7},{6,4},{7,5},{8,10},{9,11},{10,... | collective-permute-start | bytes 663560 | tf_op jit(solution)/shard_map/ppermute | solution.py:688
  28.4 1.6 %shard_map.145 = (f32[32,768]{1,0:T(8,128)S(1)}, f32[32,768]{1,0:T(8,128)S(1)}, f32[32,768]{1,0:T(8,128)S(1)}, f32[32,768]{1,0:T(8,128)S(1)}, f32[32,768]{1,0:T(...) custom-call(s32[2]{0:T(128)S(1)} %pad_add_fusion.place, ...), custom_call_target="tpu_custom_call" | custom-call | flops 2000000000 | bytes 6000000 | tf_op jit(solution)/shard_map/pallas_call | solution.py:652
  30.1 2.2 %collective-permute-start.20 = (f32[32,768]{1,0:T(8,128)S(1)}, f32[32,768]{1,0:T(8,128)S(1)}, u32[]{:S(2)}, u32[]{:S(2)}) collective-permute-start(f32[32,768]{1,0:T(8,128)S(1)} %get-tuple-element.92), channel_id=1, source_target_pairs={{0,4},{4,0},{8,12},{12,8},{16,20},{20,16},{24,28},{28,24},{1,5},{5... | collective-permute-start | bytes 294920 | tf_op jit(solution)/shard_map/ppermute | solution.py:688
  32.2 2.3 %collective-permute-done.6.refs_1_ = f32[72,768]{1,0:T(8,128)S(1)} collective-permute-done((f32[72,768]{1,0:T(8,128)S(1)}, f32[72,768]{1,0:T(8,128)S(1)}, u32[]{:S(2)}, u32[]{:S(2)}) %collective-permute-start.6) | collective-permute-done | bytes 221216 | tf_op jit(solution)/shard_map/ppermute | solution.py:688
  34.5 1.6 %collective-permute-start.21 = (f32[32,768]{1,0:T(8,128)S(1)}, f32[32,768]{1,0:T(8,128)S(1)}, u32[]{:S(2)}, u32[]{:S(2)}) collective-permute-start(f32[32,768]{1,0:T(8,128)S(1)} %get-tuple-element.93), channel_id=1, source_target_pairs={{0,20},{4,16},{8,28},{12,24},{16,4},{20,0},{24,12},{28,8},{1,21},{... | collective-permute-start | bytes 294920 | tf_op jit(solution)/shard_map/ppermute | solution.py:688
  36.1 3.7 %collective-permute-start.22 = (f32[32,768]{1,0:T(8,128)S(1)}, f32[32,768]{1,0:T(8,128)S(1)}, u32[]{:S(2)}, u32[]{:S(2)}) collective-permute-start(f32[32,768]{1,0:T(8,128)S(1)} %get-tuple-element.94), channel_id=1, source_target_pairs={{0,8},{4,12},{8,0},{12,4},{16,24},{20,28},{24,16},{28,20},{1,9},{5... | collective-permute-start | bytes 294920 | tf_op jit(solution)/shard_map/ppermute | solution.py:688
  39.8 1.6 %shard_map.143 = (f32[32,768]{1,0:T(8,128)S(1)}, f32[32,768]{1,0:T(8,128)S(1)}, f32[32,768]{1,0:T(8,128)S(1)}, f32[32,768]{1,0:T(8,128)S(1)}, f32[32,768]{1,0:T(...) custom-call(s32[2]{0:T(128)S(1)} %pad_add_fusion.place, ...), custom_call_target="tpu_custom_call" | custom-call | flops 2000000000 | bytes 6000000 | tf_op jit(solution)/shard_map/pallas_call | solution.py:652
  42.0 3.3 %collective-permute-start.25 = (f32[32,768]{1,0:T(8,128)S(1)}, f32[32,768]{1,0:T(8,128)S(1)}, u32[]{:S(2)}, u32[]{:S(2)}) collective-permute-start(f32[32,768]{1,0:T(8,128)S(1)} %get-tuple-element.97), channel_id=1, source_target_pairs={{0,28},{4,24},{8,20},{12,16},{16,12},{20,8},{24,4},{28,0},{1,29},{... | collective-permute-start | bytes 294920 | tf_op jit(solution)/shard_map/ppermute | solution.py:688
  45.9 3.0 %collective-permute-start.10 = (f32[32,768]{1,0:T(8,128)S(1)}, f32[32,768]{1,0:T(8,128)S(1)}, u32[]{:S(2)}, u32[]{:S(2)}) collective-permute-start(f32[32,768]{1,0:T(8,128)S(1)} %get-tuple-element.80), channel_id=1, source_target_pairs={{0,4},{4,0},{8,12},{12,8},{16,20},{20,16},{24,28},{28,24},{1,5},{5... | collective-permute-start | bytes 294920 | tf_op jit(solution)/shard_map/ppermute | solution.py:688
  49.8 2.0 %collective-permute-start.12 = (f32[32,768]{1,0:T(8,128)S(1)}, f32[32,768]{1,0:T(8,128)S(1)}, u32[]{:S(2)}, u32[]{:S(2)}) collective-permute-start(f32[32,768]{1,0:T(8,128)S(1)} %get-tuple-element.82), channel_id=1, source_target_pairs={{0,8},{4,12},{8,0},{12,4},{16,24},{20,28},{24,16},{28,20},{1,9},{5... | collective-permute-start | bytes 294920 | tf_op jit(solution)/shard_map/ppermute | solution.py:688
  51.7 2.2 %collective-permute-start.13 = (f32[32,768]{1,0:T(8,128)S(1)}, f32[32,768]{1,0:T(8,128)S(1)}, u32[]{:S(2)}, u32[]{:S(2)}) collective-permute-start(f32[32,768]{1,0:T(8,128)S(1)} %get-tuple-element.83), channel_id=1, source_target_pairs={{0,24},{4,28},{8,16},{12,20},{16,8},{20,12},{24,0},{28,4},{1,25},{... | collective-permute-start | bytes 294920 | tf_op jit(solution)/shard_map/ppermute | solution.py:688
  54.0 6.1 %collective-permute-done.9.refs_1_ = f32[32,768]{1,0:T(8,128)S(1)} collective-permute-done((f32[32,768]{1,0:T(8,128)S(1)}, f32[32,768]{1,0:T(8,128)S(1)}, u32[]{:S(2)}, u32[]{:S(2)}) %collective-permute-start.9) | collective-permute-done | bytes 98336 | tf_op jit(solution)/shard_map/ppermute | solution.py:688
  60.0 2.5 %collective-permute-start.15 = (f32[32,768]{1,0:T(8,128)S(1)}, f32[32,768]{1,0:T(8,128)S(1)}, u32[]{:S(2)}, u32[]{:S(2)}) collective-permute-start(f32[32,768]{1,0:T(8,128)S(1)} %get-tuple-element.85), channel_id=1, source_target_pairs={{0,28},{4,24},{8,20},{12,16},{16,12},{20,8},{24,4},{28,0},{1,29},{... | collective-permute-start | bytes 294920 | tf_op jit(solution)/shard_map/ppermute | solution.py:688
  64.0 1.7 %collective-permute-start.5 = (f32[48,256]{1,0:T(8,128)S(1)}, f32[48,256]{1,0:T(8,128)S(1)}, u32[]{:S(2)}, u32[]{:S(2)}) collective-permute-start(f32[48,256]{1,0:T(8,128)S(1)} %get-tuple-element.73), channel_id=1, source_target_pairs={{0,3},{1,0},{2,1},{3,2},{4,7},{5,4},{6,5},{7,6},{8,11},{9,8},{10,9... | collective-permute-start | bytes 147464 | tf_op jit(solution)/shard_map/ppermute | solution.py:747
  65.7 1.9 %collective-permute-done.14.refs_6_ = f32[32,768]{1,0:T(8,128)S(1)} collective-permute-done((f32[32,768]{1,0:T(8,128)S(1)}, f32[32,768]{1,0:T(8,128)S(1)}, u32[]{:S(2)}, u32[]{:S(2)}) %collective-permute-start.14) | collective-permute-done | bytes 98336 | tf_op jit(solution)/shard_map/ppermute | solution.py:688
  67.7 1.3 %shard_map.144.refs_0_ = f32[3,2,4,8,8,128]{5,4,3,2,1,0:T(8,128)S(1)} custom-call(s32[2]{0:T(128)S(1)} %pad_add_fusion.place, f32[32,768]{1,0:T(8,128)S(1)} %get-tuple-element.78.refs_0_, f32[32,768]{1,0:T(8,128)S(1)} %collective-permute-done.9.refs_1_, f32[32,768]{1,0:T(8,128)S(1)} %collective-permute-done.10.refs_2_, ...), custom_call_target="tpu_custom_call" | custom-call | flops 2000000000 | bytes 6000000 | tf_op jit(solution)/shard_map/pallas_call | solution.py:652
  69.0 2.3 %shard_map.147 = (f32[3,2,4,8,8,128]{5,4,3,2,1,0:T(8,128)S(1)}, f32[3,2,4,8,8,128]{5,4,3,2,1,0:T(8,128)S(1)}) custom-call(s32[2]{0:T(128)S(1)} %pad_add_fusion.place, f32[48,256]{1,0:T(8,128)S(1)} %collective-permute-done.4.low_rim.refs_1_, f32[48,256]{1,0:T(8,128)S(1)} %collective-permute-done.5.high_rim.refs_2_, ...), custom_call_target="tpu_custom_call" | custom-call | flops 5000000000 | bytes 15000000 | tf_op jit(solution)/shard_map/pallas_call | solution.py:652
  71.4 1.4 %shard_map.148 = (f32[32,768]{1,0:T(8,128)S(1)}, f32[32,768]{1,0:T(8,128)S(1)}, f32[32,768]{1,0:T(8,128)S(1)}, f32[32,768]{1,0:T(8,128)S(1)}, f32[32,768]{1,0:T(...) custom-call(s32[2]{0:T(128)S(1)} %pad_add_fusion.place, ...), custom_call_target="tpu_custom_call" | custom-call | flops 2000000000 | bytes 6000000 | tf_op jit(solution)/shard_map/pallas_call | solution.py:652
  72.8 2.2 %collective-permute-start.26 = (f32[32,768]{1,0:T(8,128)S(1)}, f32[32,768]{1,0:T(8,128)S(1)}, u32[]{:S(2)}, u32[]{:S(2)}) collective-permute-start(f32[32,768]{1,0:T(8,128)S(1)} %get-tuple-element.100), channel_id=1, source_target_pairs={{0,16},{4,20},{8,24},{12,28},{16,0},{20,4},{24,8},{28,12},{1,17},{... | collective-permute-start | bytes 294920 | tf_op jit(solution)/shard_map/ppermute | solution.py:688
  77.3 2.0 %collective-permute-start.29 = (f32[32,768]{1,0:T(8,128)S(1)}, f32[32,768]{1,0:T(8,128)S(1)}, u32[]{:S(2)}, u32[]{:S(2)}) collective-permute-start(f32[32,768]{1,0:T(8,128)S(1)} %get-tuple-element.103), channel_id=1, source_target_pairs={{0,8},{4,12},{8,0},{12,4},{16,24},{20,28},{24,16},{28,20},{1,9},{5... | collective-permute-start | bytes 294920 | tf_op jit(solution)/shard_map/ppermute | solution.py:688
  79.2 1.6 %collective-permute-start.30 = (f32[32,768]{1,0:T(8,128)S(1)}, f32[32,768]{1,0:T(8,128)S(1)}, u32[]{:S(2)}, u32[]{:S(2)}) collective-permute-start(f32[32,768]{1,0:T(8,128)S(1)} %get-tuple-element.104), channel_id=1, source_target_pairs={{0,24},{4,28},{8,16},{12,20},{16,8},{20,12},{24,0},{28,4},{1,25},{... | collective-permute-start | bytes 294920 | tf_op jit(solution)/shard_map/ppermute | solution.py:688
  80.8 1.6 %collective-permute-done.26.refs_1_ = f32[32,768]{1,0:T(8,128)S(1)} collective-permute-done((f32[32,768]{1,0:T(8,128)S(1)}, f32[32,768]{1,0:T(8,128)S(1)}, u32[]{:S(2)}, u32[]{:S(2)}) %collective-permute-start.26) | collective-permute-done | bytes 98336 | tf_op jit(solution)/shard_map/ppermute | solution.py:688
  82.4 3.5 %collective-permute-start.32 = (f32[32,768]{1,0:T(8,128)S(1)}, f32[32,768]{1,0:T(8,128)S(1)}, u32[]{:S(2)}, u32[]{:S(2)}) collective-permute-start(f32[32,768]{1,0:T(8,128)S(1)} %get-tuple-element.106), channel_id=1, source_target_pairs={{0,28},{4,24},{8,20},{12,16},{16,12},{20,8},{24,4},{28,0},{1,29},{... | collective-permute-start | bytes 294920 | tf_op jit(solution)/shard_map/ppermute | solution.py:688
  86.0 1.4 %shard_map.151 = (f32[32,768]{1,0:T(8,128)S(1)}, f32[32,768]{1,0:T(8,128)S(1)}, f32[32,768]{1,0:T(8,128)S(1)}, f32[32,768]{1,0:T(8,128)S(1)}, f32[32,768]{1,0:T(...) custom-call(s32[2]{0:T(128)S(1)} %pad_add_fusion.place, ...), custom_call_target="tpu_custom_call" | custom-call | flops 2000000000 | bytes 6000000 | tf_op jit(solution)/shard_map/pallas_call | solution.py:652
  87.4 1.7 %collective-permute-done.28.refs_3_ = f32[32,768]{1,0:T(8,128)S(1)} collective-permute-done((f32[32,768]{1,0:T(8,128)S(1)}, f32[32,768]{1,0:T(8,128)S(1)}, u32[]{:S(2)}, u32[]{:S(2)}) %collective-permute-start.28) | collective-permute-done | bytes 98336 | tf_op jit(solution)/shard_map/ppermute | solution.py:688
  89.1 2.2 %collective-permute-start.37 = (f32[32,768]{1,0:T(8,128)S(1)}, f32[32,768]{1,0:T(8,128)S(1)}, u32[]{:S(2)}, u32[]{:S(2)}) collective-permute-start(f32[32,768]{1,0:T(8,128)S(1)} %get-tuple-element.117), channel_id=1, source_target_pairs={{0,4},{4,0},{8,12},{12,8},{16,20},{20,16},{24,28},{28,24},{1,5},{5... | collective-permute-start | bytes 294920 | tf_op jit(solution)/shard_map/ppermute | solution.py:688
  91.3 2.5 %collective-permute-start.38 = (f32[32,768]{1,0:T(8,128)S(1)}, f32[32,768]{1,0:T(8,128)S(1)}, u32[]{:S(2)}, u32[]{:S(2)}) collective-permute-start(f32[32,768]{1,0:T(8,128)S(1)} %get-tuple-element.118), channel_id=1, source_target_pairs={{0,20},{4,16},{8,28},{12,24},{16,4},{20,0},{24,12},{28,8},{1,21},{... | collective-permute-start | bytes 294920 | tf_op jit(solution)/shard_map/ppermute | solution.py:688
  93.9 1.7 %shard_map.149 = (f32[72,768]{1,0:T(8,128)S(1)}, f32[72,768]{1,0:T(8,128)S(1)}, f32[72,768]{1,0:T(8,128)S(1)}, f32[72,768]{1,0:T(8,128)S(1)}) custom-call(s32[2]{0:T(128)S(1)} %pad_add_fusion.place, bf16[576,256]{1,0:T(8,128)(2,1)S(1)} %copy-done.6, bf16[576,256]{1,0:T(8,128)(2,1)S(1)} %copy-done.5, f32[32,768]{1,0:T(8,128)S(1)} %get-tuple-element.99.refs_0_, ...), custom_call_target="tpu_custom_call" | custom-call | flops 2000000000 | bytes 6000000 | tf_op jit(solution)/shard_map/pallas_call | solution.py:652
  95.6 2.4 %collective-permute-start.40 = (f32[32,768]{1,0:T(8,128)S(1)}, f32[32,768]{1,0:T(8,128)S(1)}, u32[]{:S(2)}, u32[]{:S(2)}) collective-permute-start(f32[32,768]{1,0:T(8,128)S(1)} %get-tuple-element.123), channel_id=1, source_target_pairs={{0,24},{4,28},{8,16},{12,20},{16,8},{20,12},{24,0},{28,4},{1,25},{... | collective-permute-start | bytes 294920 | tf_op jit(solution)/shard_map/ppermute | solution.py:688
  98.0 2.7 %collective-permute-done.36.refs_1_ = f32[32,768]{1,0:T(8,128)S(1)} collective-permute-done((f32[32,768]{1,0:T(8,128)S(1)}, f32[32,768]{1,0:T(8,128)S(1)}, u32[]{:S(2)}, u32[]{:S(2)}) %collective-permute-start.36) | collective-permute-done | bytes 98336 | tf_op jit(solution)/shard_map/ppermute | solution.py:688
  101.0 2.6 %collective-permute-start.42 = (f32[32,768]{1,0:T(8,128)S(1)}, f32[32,768]{1,0:T(8,128)S(1)}, u32[]{:S(2)}, u32[]{:S(2)}) collective-permute-start(f32[32,768]{1,0:T(8,128)S(1)} %get-tuple-element.125), channel_id=1, source_target_pairs={{0,28},{4,24},{8,20},{12,16},{16,12},{20,8},{24,4},{28,0},{1,29},{... | collective-permute-start | bytes 294920 | tf_op jit(solution)/shard_map/ppermute | solution.py:688
  104.9 2.1 %collective-permute-start.35 = (f32[72,768]{1,0:T(8,128)S(1)}, f32[72,768]{1,0:T(8,128)S(1)}, u32[]{:S(2)}, u32[]{:S(2)}) collective-permute-start(f32[72,768]{1,0:T(8,128)S(1)} %get-tuple-element.110), channel_id=1, source_target_pairs={{0,3},{1,2},{2,1},{3,0},{4,7},{5,6},{6,5},{7,4},{8,11},{9,10},{10,... | collective-permute-start | bytes 663560 | tf_op jit(solution)/shard_map/ppermute | solution.py:688
  108.4 1.7 %shard_map.153 = (f32[72,768]{1,0:T(8,128)S(1)}, f32[72,768]{1,0:T(8,128)S(1)}, f32[72,768]{1,0:T(8,128)S(1)}, f32[72,768]{1,0:T(8,128)S(1)}) custom-call(s32[2]{0:T(128)S(1)} %pad_add_fusion.place, bf16[576,256]{1,0:T(8,128)(2,1)S(1)} %copy-done.6, bf16[576,256]{1,0:T(8,128)(2,1)S(1)} %copy-done.5, f32[32,768]{1,0:T(8,128)S(1)} %get-tuple-element.115.refs_0_, ...), custom_call_target="tpu_custom_call" | custom-call | flops 2000000000 | bytes 6000000 | tf_op jit(solution)/shard_map/pallas_call | solution.py:652
  110.1 2.3 %collective-permute-start.43 = (f32[72,768]{1,0:T(8,128)S(1)}, f32[72,768]{1,0:T(8,128)S(1)}, u32[]{:S(2)}, u32[]{:S(2)}) collective-permute-start(f32[72,768]{1,0:T(8,128)S(1)} %get-tuple-element.127), channel_id=1, source_target_pairs={{0,2},{1,3},{2,0},{3,1},{4,6},{5,7},{6,4},{7,5},{8,10},{9,11},{10,... | collective-permute-start | bytes 663560 | tf_op jit(solution)/shard_map/ppermute | solution.py:688
  113.8 1.5 %shard_map.150 = (f32[3,4,80,256]{3,2,1,0:T(8,128)S(1)}, f32[3,64,256]{2,1,0:T(8,128)S(1)}, f32[3,64,256]{2,1,0:T(8,128)S(1)}) custom-call(s32[2]{0:T(128)S(1)} %pad_add_fusion.place, bf16[512,512]{1,0:T(8,128)(2,1)S(1)} %copy-done.2, bf16[512,512]{1,0:T(8,128)(2,1)S(1)} %copy-done.1, f32[72,768]{1,0:T(8,128)S(1)} %get-tuple-element.107.refs_0_.before, ...), custom_call_target="tpu_custom_call" | custom-call | flops 2000000000 | bytes 6000000 | tf_op jit(solution)/shard_map/pallas_call | solution.py:652
  115.3 4.0 %collective-permute-start.46 = (f32[3,64,256]{2,1,0:T(8,128)S(1)}, f32[3,64,256]{2,1,0:T(8,128)S(1)}, u32[]{:S(2)}, u32[]{:S(2)}) collective-permute-start(f32[3,64,256]{2,1,0:T(8,128)S(1)} %get-tuple-element.132), channel_id=1, source_target_pairs={{0,4},{4,8},{8,12},{12,16},{16,20},{20,24},{24,28},{28,0},{1,5},{5... | collective-permute-start | bytes 589832 | tf_op jit(solution)/shard_map/ppermute | solution.py:817
  120.1 2.4 %collective-permute-done.43.refs_6_ = f32[72,768]{1,0:T(8,128)S(1)} collective-permute-done((f32[72,768]{1,0:T(8,128)S(1)}, f32[72,768]{1,0:T(8,128)S(1)}, u32[]{:S(2)}, u32[]{:S(2)}) %collective-permute-start.43) | collective-permute-done | bytes 221216 | tf_op jit(solution)/shard_map/ppermute | solution.py:688
  122.5 3.0 %shard_map.154 = (f32[3,8,64,256]{3,2,1,0:T(8,128)}, f32[3,8,64,256]{3,2,1,0:T(8,128)}) custom-call(s32[2]{0:T(128)S(1)} %pad_add_fusion.place, bf16[512,512]{1,0:T(8,128)(2,1)S(1)} %copy-done.2, bf16[512,512]{1,0:T(8,128)(2,1)S(1)} %copy-done.1, f32[3,4,80,256]{3,2,1,0:T(8,128)S(1)} %get-tuple-element.111.refs_0_.edges, ...), custom_call_target="tpu_custom_call" | custom-call | flops 4000000000 | bytes 12000000 | tf_op jit(solution)/shard_map/pallas_call | solution.py:652
  125.5 3.1 %collective-permute-done.46.before = f32[3,64,256]{2,1,0:T(8,128)S(1)} collective-permute-done((f32[3,64,256]{2,1,0:T(8,128)S(1)}, f32[3,64,256]{2,1,0:T(8,128)S(1)}, u32[]{:S(2)}, u32[]{:S(2)}) %collective-permute-start.46) | collective-permute-done | bytes 196640 | tf_op jit(solution)/shard_map/ppermute | solution.py:817
  128.6 1.4 %collective-permute-done.47.after = f32[3,64,256]{2,1,0:T(8,128)S(1)} collective-permute-done((f32[3,64,256]{2,1,0:T(8,128)S(1)}, f32[3,64,256]{2,1,0:T(8,128)S(1)}, u32[]{:S(2)}, u32[]{:S(2)}) %collective-permute-start.47) | collective-permute-done | bytes 196640 | tf_op jit(solution)/shard_map/ppermute | solution.py:816
  (83 shorter events, 14.3 us)
Async XLA Ops:
  1.8 10.0 %collective-permute-start.3 = (f32[8,128]{1,0:T(8,128)S(1)}, f32[8,128]{1,0:T(8,128)S(1)}, u32[]{:S(2)}, u32[]{:S(2)}) collective-permute-start(f32[8,128]{1,0:T(8,128)S(1)} %get-tuple-element.69), channel_id=1, source_target_pairs={{0,8},{4,12},{8,16},{12,20},{16,24},{20,28},{24,0},{28,4},{1,9},{5... | collective-permute-start | bytes 12296 | tf_op jit(solution)/shard_map/ppermute | solution.py:725
  4.8 6.9 %collective-permute-start.2 = (f32[8,128]{1,0:T(8,128)S(1)}, f32[8,128]{1,0:T(8,128)S(1)}, u32[]{:S(2)}, u32[]{:S(2)}) collective-permute-start(f32[8,128]{1,0:T(8,128)S(1)} %get-tuple-element.69), channel_id=1, source_target_pairs={{0,24},{4,28},{8,0},{12,4},{16,8},{20,12},{24,16},{28,20},{1,25},{... | collective-permute-start | bytes 12296 | tf_op jit(solution)/shard_map/ppermute | solution.py:724
  6.9 6.4 %collective-permute-start.1 = (f32[8,512]{1,0:T(8,128)S(1)}, f32[8,512]{1,0:T(8,128)S(1)}, u32[]{:S(2)}, u32[]{:S(2)}) collective-permute-start(f32[8,512]{1,0:T(8,128)S(1)} %get-tuple-element.68.own), channel_id=1, source_target_pairs={{0,4},{4,8},{8,12},{12,16},{16,20},{20,24},{24,28},{28,0},{1,5},{5... | collective-permute-start | bytes 49160 | tf_op jit(solution)/shard_map/ppermute | solution.py:723
  8.6 4.8 %collective-permute-start = (f32[8,512]{1,0:T(8,128)S(1)}, f32[8,512]{1,0:T(8,128)S(1)}, u32[]{:S(2)}, u32[]{:S(2)}) collective-permute-start(f32[8,512]{1,0:T(8,128)S(1)} %get-tuple-element.68.own), channel_id=1, source_target_pairs={{0,28},{4,0},{8,4},{12,8},{16,12},{20,16},{24,20},{28,24},{1,29},{... | collective-permute-start | bytes 49160 | tf_op jit(solution)/shard_map/ppermute | solution.py:722
  17.3 10.6 %collective-permute-start.16 = (f32[72,768]{1,0:T(8,128)S(1)}, f32[72,768]{1,0:T(8,128)S(1)}, u32[]{:S(2)}, u32[]{:S(2)}) collective-permute-start(f32[72,768]{1,0:T(8,128)S(1)} %get-tuple-element.87), channel_id=1, source_target_pairs={{0,2},{1,3},{2,0},{3,1},{4,6},{5,7},{6,4},{7,5},{8,10},{9,11},{10,... | collective-permute-start | bytes 663560 | tf_op jit(solution)/shard_map/ppermute | solution.py:688
  19.1 9.3 %collective-permute-start.17 = (f32[72,768]{1,0:T(8,128)S(1)}, f32[72,768]{1,0:T(8,128)S(1)}, u32[]{:S(2)}, u32[]{:S(2)}) collective-permute-start(f32[72,768]{1,0:T(8,128)S(1)} %get-tuple-element.88), channel_id=1, source_target_pairs={{0,1},{1,0},{2,3},{3,2},{4,5},{5,4},{6,7},{7,6},{8,9},{9,8},{10,11... | collective-permute-start | bytes 663560 | tf_op jit(solution)/shard_map/ppermute | solution.py:688
  19.1 9.3 %collective-permute-start.18 = (f32[72,768]{1,0:T(8,128)S(1)}, f32[72,768]{1,0:T(8,128)S(1)}, u32[]{:S(2)}, u32[]{:S(2)}) collective-permute-start(f32[72,768]{1,0:T(8,128)S(1)} %get-tuple-element.89), channel_id=1, source_target_pairs={{0,3},{1,2},{2,1},{3,0},{4,7},{5,6},{6,5},{7,4},{8,11},{9,10},{10,... | collective-permute-start | bytes 663560 | tf_op jit(solution)/shard_map/ppermute | solution.py:688
  26.1 8.4 %collective-permute-start.6 = (f32[72,768]{1,0:T(8,128)S(1)}, f32[72,768]{1,0:T(8,128)S(1)}, u32[]{:S(2)}, u32[]{:S(2)}) collective-permute-start(f32[72,768]{1,0:T(8,128)S(1)} %get-tuple-element.75), channel_id=1, source_target_pairs={{0,2},{1,3},{2,0},{3,1},{4,6},{5,7},{6,4},{7,5},{8,10},{9,11},{10,... | collective-permute-start | bytes 663560 | tf_op jit(solution)/shard_map/ppermute | solution.py:688
  27.9 8.2 %collective-permute-start.7 = (f32[72,768]{1,0:T(8,128)S(1)}, f32[72,768]{1,0:T(8,128)S(1)}, u32[]{:S(2)}, u32[]{:S(2)}) collective-permute-start(f32[72,768]{1,0:T(8,128)S(1)} %get-tuple-element.76), channel_id=1, source_target_pairs={{0,1},{1,0},{2,3},{3,2},{4,5},{5,4},{6,7},{7,6},{8,9},{9,8},{10,11... | collective-permute-start | bytes 663560 | tf_op jit(solution)/shard_map/ppermute | solution.py:688
  27.9 11.9 %collective-permute-start.8 = (f32[72,768]{1,0:T(8,128)S(1)}, f32[72,768]{1,0:T(8,128)S(1)}, u32[]{:S(2)}, u32[]{:S(2)}) collective-permute-start(f32[72,768]{1,0:T(8,128)S(1)} %get-tuple-element.77), channel_id=1, source_target_pairs={{0,3},{1,2},{2,1},{3,0},{4,7},{5,6},{6,5},{7,4},{8,11},{9,10},{10,... | collective-permute-start | bytes 663560 | tf_op jit(solution)/shard_map/ppermute | solution.py:688
  30.0 11.4 %collective-permute-start.19 = (f32[32,768]{1,0:T(8,128)S(1)}, f32[32,768]{1,0:T(8,128)S(1)}, u32[]{:S(2)}, u32[]{:S(2)}) collective-permute-start(f32[32,768]{1,0:T(8,128)S(1)} %get-tuple-element.91), channel_id=1, source_target_pairs={{0,16},{4,20},{8,24},{12,28},{16,0},{20,4},{24,8},{28,12},{1,17},{... | collective-permute-start | bytes 294920 | tf_op jit(solution)/shard_map/ppermute | solution.py:688
  30.1 12.0 %collective-permute-start.20 = (f32[32,768]{1,0:T(8,128)S(1)}, f32[32,768]{1,0:T(8,128)S(1)}, u32[]{:S(2)}, u32[]{:S(2)}) collective-permute-start(f32[32,768]{1,0:T(8,128)S(1)} %get-tuple-element.92), channel_id=1, source_target_pairs={{0,4},{4,0},{8,12},{12,8},{16,20},{20,16},{24,28},{28,24},{1,5},{5... | collective-permute-start | bytes 294920 | tf_op jit(solution)/shard_map/ppermute | solution.py:688
  34.5 10.9 %collective-permute-start.21 = (f32[32,768]{1,0:T(8,128)S(1)}, f32[32,768]{1,0:T(8,128)S(1)}, u32[]{:S(2)}, u32[]{:S(2)}) collective-permute-start(f32[32,768]{1,0:T(8,128)S(1)} %get-tuple-element.93), channel_id=1, source_target_pairs={{0,20},{4,16},{8,28},{12,24},{16,4},{20,0},{24,12},{28,8},{1,21},{... | collective-permute-start | bytes 294920 | tf_op jit(solution)/shard_map/ppermute | solution.py:688
  36.1 9.7 %collective-permute-start.22 = (f32[32,768]{1,0:T(8,128)S(1)}, f32[32,768]{1,0:T(8,128)S(1)}, u32[]{:S(2)}, u32[]{:S(2)}) collective-permute-start(f32[32,768]{1,0:T(8,128)S(1)} %get-tuple-element.94), channel_id=1, source_target_pairs={{0,8},{4,12},{8,0},{12,4},{16,24},{20,28},{24,16},{28,20},{1,9},{5... | collective-permute-start | bytes 294920 | tf_op jit(solution)/shard_map/ppermute | solution.py:688
  39.8 9.1 %collective-permute-start.23 = (f32[32,768]{1,0:T(8,128)S(1)}, f32[32,768]{1,0:T(8,128)S(1)}, u32[]{:S(2)}, u32[]{:S(2)}) collective-permute-start(f32[32,768]{1,0:T(8,128)S(1)} %get-tuple-element.95), channel_id=1, source_target_pairs={{0,24},{4,28},{8,16},{12,20},{16,8},{20,12},{24,0},{28,4},{1,25},{... | collective-permute-start | bytes 294920 | tf_op jit(solution)/shard_map/ppermute | solution.py:688
  41.4 8.4 %collective-permute-start.24 = (f32[32,768]{1,0:T(8,128)S(1)}, f32[32,768]{1,0:T(8,128)S(1)}, u32[]{:S(2)}, u32[]{:S(2)}) collective-permute-start(f32[32,768]{1,0:T(8,128)S(1)} %get-tuple-element.96), channel_id=1, source_target_pairs={{0,12},{4,8},{8,4},{12,0},{16,28},{20,24},{24,20},{28,16},{1,13},{... | collective-permute-start | bytes 294920 | tf_op jit(solution)/shard_map/ppermute | solution.py:688
  42.0 9.7 %collective-permute-start.25 = (f32[32,768]{1,0:T(8,128)S(1)}, f32[32,768]{1,0:T(8,128)S(1)}, u32[]{:S(2)}, u32[]{:S(2)}) collective-permute-start(f32[32,768]{1,0:T(8,128)S(1)} %get-tuple-element.97), channel_id=1, source_target_pairs={{0,28},{4,24},{8,20},{12,16},{16,12},{20,8},{24,4},{28,0},{1,29},{... | collective-permute-start | bytes 294920 | tf_op jit(solution)/shard_map/ppermute | solution.py:688
  45.4 14.7 %collective-permute-start.9 = (f32[32,768]{1,0:T(8,128)S(1)}, f32[32,768]{1,0:T(8,128)S(1)}, u32[]{:S(2)}, u32[]{:S(2)}) collective-permute-start(f32[32,768]{1,0:T(8,128)S(1)} %get-tuple-element.79), channel_id=1, source_target_pairs={{0,16},{4,20},{8,24},{12,28},{16,0},{20,4},{24,8},{28,12},{1,17},{... | collective-permute-start | bytes 294920 | tf_op jit(solution)/shard_map/ppermute | solution.py:688
  45.9 14.2 %collective-permute-start.10 = (f32[32,768]{1,0:T(8,128)S(1)}, f32[32,768]{1,0:T(8,128)S(1)}, u32[]{:S(2)}, u32[]{:S(2)}) collective-permute-start(f32[32,768]{1,0:T(8,128)S(1)} %get-tuple-element.80), channel_id=1, source_target_pairs={{0,4},{4,0},{8,12},{12,8},{16,20},{20,16},{24,28},{28,24},{1,5},{5... | collective-permute-start | bytes 294920 | tf_op jit(solution)/shard_map/ppermute | solution.py:688
  48.9 15.1 %collective-permute-start.11 = (f32[32,768]{1,0:T(8,128)S(1)}, f32[32,768]{1,0:T(8,128)S(1)}, u32[]{:S(2)}, u32[]{:S(2)}) collective-permute-start(f32[32,768]{1,0:T(8,128)S(1)} %get-tuple-element.81), channel_id=1, source_target_pairs={{0,20},{4,16},{8,28},{12,24},{16,4},{20,0},{24,12},{28,8},{1,21},{... | collective-permute-start | bytes 294920 | tf_op jit(solution)/shard_map/ppermute | solution.py:688
  49.8 14.2 %collective-permute-start.12 = (f32[32,768]{1,0:T(8,128)S(1)}, f32[32,768]{1,0:T(8,128)S(1)}, u32[]{:S(2)}, u32[]{:S(2)}) collective-permute-start(f32[32,768]{1,0:T(8,128)S(1)} %get-tuple-element.82), channel_id=1, source_target_pairs={{0,8},{4,12},{8,0},{12,4},{16,24},{20,28},{24,16},{28,20},{1,9},{5... | collective-permute-start | bytes 294920 | tf_op jit(solution)/shard_map/ppermute | solution.py:688
  51.7 14.0 %collective-permute-start.13 = (f32[32,768]{1,0:T(8,128)S(1)}, f32[32,768]{1,0:T(8,128)S(1)}, u32[]{:S(2)}, u32[]{:S(2)}) collective-permute-start(f32[32,768]{1,0:T(8,128)S(1)} %get-tuple-element.83), channel_id=1, source_target_pairs={{0,24},{4,28},{8,16},{12,20},{16,8},{20,12},{24,0},{28,4},{1,25},{... | collective-permute-start | bytes 294920 | tf_op jit(solution)/shard_map/ppermute | solution.py:688
  60.0 7.6 %collective-permute-start.14 = (f32[32,768]{1,0:T(8,128)S(1)}, f32[32,768]{1,0:T(8,128)S(1)}, u32[]{:S(2)}, u32[]{:S(2)}) collective-permute-start(f32[32,768]{1,0:T(8,128)S(1)} %get-tuple-element.84), channel_id=1, source_target_pairs={{0,12},{4,8},{8,4},{12,0},{16,28},{20,24},{24,20},{28,16},{1,13},{... | collective-permute-start | bytes 294920 | tf_op jit(solution)/shard_map/ppermute | solution.py:688
  60.0 7.6 %collective-permute-start.15 = (f32[32,768]{1,0:T(8,128)S(1)}, f32[32,768]{1,0:T(8,128)S(1)}, u32[]{:S(2)}, u32[]{:S(2)}) collective-permute-start(f32[32,768]{1,0:T(8,128)S(1)} %get-tuple-element.85), channel_id=1, source_target_pairs={{0,28},{4,24},{8,20},{12,16},{16,12},{20,8},{24,4},{28,0},{1,29},{... | collective-permute-start | bytes 294920 | tf_op jit(solution)/shard_map/ppermute | solution.py:688
  64.0 5.1 %collective-permute-start.4 = (f32[48,256]{1,0:T(8,128)S(1)}, f32[48,256]{1,0:T(8,128)S(1)}, u32[]{:S(2)}, u32[]{:S(2)}) collective-permute-start(f32[48,256]{1,0:T(8,128)S(1)} %get-tuple-element.72), channel_id=1, source_target_pairs={{0,1},{1,2},{2,3},{3,0},{4,5},{5,6},{6,7},{7,4},{8,9},{9,10},{10,1... | collective-permute-start | bytes 147464 | tf_op jit(solution)/shard_map/ppermute | solution.py:746
  64.0 5.0 %collective-permute-start.5 = (f32[48,256]{1,0:T(8,128)S(1)}, f32[48,256]{1,0:T(8,128)S(1)}, u32[]{:S(2)}, u32[]{:S(2)}) collective-permute-start(f32[48,256]{1,0:T(8,128)S(1)} %get-tuple-element.73), channel_id=1, source_target_pairs={{0,3},{1,0},{2,1},{3,2},{4,7},{5,4},{6,5},{7,6},{8,11},{9,8},{10,9... | collective-permute-start | bytes 147464 | tf_op jit(solution)/shard_map/ppermute | solution.py:747
  72.8 9.6 %collective-permute-start.26 = (f32[32,768]{1,0:T(8,128)S(1)}, f32[32,768]{1,0:T(8,128)S(1)}, u32[]{:S(2)}, u32[]{:S(2)}) collective-permute-start(f32[32,768]{1,0:T(8,128)S(1)} %get-tuple-element.100), channel_id=1, source_target_pairs={{0,16},{4,20},{8,24},{12,28},{16,0},{20,4},{24,8},{28,12},{1,17},{... | collective-permute-start | bytes 294920 | tf_op jit(solution)/shard_map/ppermute | solution.py:688
  75.0 7.5 %collective-permute-start.27 = (f32[32,768]{1,0:T(8,128)S(1)}, f32[32,768]{1,0:T(8,128)S(1)}, u32[]{:S(2)}, u32[]{:S(2)}) collective-permute-start(f32[32,768]{1,0:T(8,128)S(1)} %get-tuple-element.101), channel_id=1, source_target_pairs={{0,4},{4,0},{8,12},{12,8},{16,20},{20,16},{24,28},{28,24},{1,5},{5... | collective-permute-start | bytes 294920 | tf_op jit(solution)/shard_map/ppermute | solution.py:688
  76.0 13.0 %collective-permute-start.28 = (f32[32,768]{1,0:T(8,128)S(1)}, f32[32,768]{1,0:T(8,128)S(1)}, u32[]{:S(2)}, u32[]{:S(2)}) collective-permute-start(f32[32,768]{1,0:T(8,128)S(1)} %get-tuple-element.102), channel_id=1, source_target_pairs={{0,20},{4,16},{8,28},{12,24},{16,4},{20,0},{24,12},{28,8},{1,21},{... | collective-permute-start | bytes 294920 | tf_op jit(solution)/shard_map/ppermute | solution.py:688
  77.3 11.8 %collective-permute-start.29 = (f32[32,768]{1,0:T(8,128)S(1)}, f32[32,768]{1,0:T(8,128)S(1)}, u32[]{:S(2)}, u32[]{:S(2)}) collective-permute-start(f32[32,768]{1,0:T(8,128)S(1)} %get-tuple-element.103), channel_id=1, source_target_pairs={{0,8},{4,12},{8,0},{12,4},{16,24},{20,28},{24,16},{28,20},{1,9},{5... | collective-permute-start | bytes 294920 | tf_op jit(solution)/shard_map/ppermute | solution.py:688
  79.2 12.1 %collective-permute-start.30 = (f32[32,768]{1,0:T(8,128)S(1)}, f32[32,768]{1,0:T(8,128)S(1)}, u32[]{:S(2)}, u32[]{:S(2)}) collective-permute-start(f32[32,768]{1,0:T(8,128)S(1)} %get-tuple-element.104), channel_id=1, source_target_pairs={{0,24},{4,28},{8,16},{12,20},{16,8},{20,12},{24,0},{28,4},{1,25},{... | collective-permute-start | bytes 294920 | tf_op jit(solution)/shard_map/ppermute | solution.py:688
  82.4 11.4 %collective-permute-start.31 = (f32[32,768]{1,0:T(8,128)S(1)}, f32[32,768]{1,0:T(8,128)S(1)}, u32[]{:S(2)}, u32[]{:S(2)}) collective-permute-start(f32[32,768]{1,0:T(8,128)S(1)} %get-tuple-element.105), channel_id=1, source_target_pairs={{0,12},{4,8},{8,4},{12,0},{16,28},{20,24},{24,20},{28,16},{1,13},{... | collective-permute-start | bytes 294920 | tf_op jit(solution)/shard_map/ppermute | solution.py:688
  82.4 11.4 %collective-permute-start.32 = (f32[32,768]{1,0:T(8,128)S(1)}, f32[32,768]{1,0:T(8,128)S(1)}, u32[]{:S(2)}, u32[]{:S(2)}) collective-permute-start(f32[32,768]{1,0:T(8,128)S(1)} %get-tuple-element.106), channel_id=1, source_target_pairs={{0,28},{4,24},{8,20},{12,16},{16,12},{20,8},{24,4},{28,0},{1,29},{... | collective-permute-start | bytes 294920 | tf_op jit(solution)/shard_map/ppermute | solution.py:688
  89.1 11.6 %collective-permute-start.36 = (f32[32,768]{1,0:T(8,128)S(1)}, f32[32,768]{1,0:T(8,128)S(1)}, u32[]{:S(2)}, u32[]{:S(2)}) collective-permute-start(f32[32,768]{1,0:T(8,128)S(1)} %get-tuple-element.116), channel_id=1, source_target_pairs={{0,16},{4,20},{8,24},{12,28},{16,0},{20,4},{24,8},{28,12},{1,17},{... | collective-permute-start | bytes 294920 | tf_op jit(solution)/shard_map/ppermute | solution.py:688
  89.1 11.9 %collective-permute-start.37 = (f32[32,768]{1,0:T(8,128)S(1)}, f32[32,768]{1,0:T(8,128)S(1)}, u32[]{:S(2)}, u32[]{:S(2)}) collective-permute-start(f32[32,768]{1,0:T(8,128)S(1)} %get-tuple-element.117), channel_id=1, source_target_pairs={{0,4},{4,0},{8,12},{12,8},{16,20},{20,16},{24,28},{28,24},{1,5},{5... | collective-permute-start | bytes 294920 | tf_op jit(solution)/shard_map/ppermute | solution.py:688
  91.3 13.5 %collective-permute-start.38 = (f32[32,768]{1,0:T(8,128)S(1)}, f32[32,768]{1,0:T(8,128)S(1)}, u32[]{:S(2)}, u32[]{:S(2)}) collective-permute-start(f32[32,768]{1,0:T(8,128)S(1)} %get-tuple-element.118), channel_id=1, source_target_pairs={{0,20},{4,16},{8,28},{12,24},{16,4},{20,0},{24,12},{28,8},{1,21},{... | collective-permute-start | bytes 294920 | tf_op jit(solution)/shard_map/ppermute | solution.py:688
  93.8 11.0 %collective-permute-start.39 = (f32[32,768]{1,0:T(8,128)S(1)}, f32[32,768]{1,0:T(8,128)S(1)}, u32[]{:S(2)}, u32[]{:S(2)}) collective-permute-start(f32[32,768]{1,0:T(8,128)S(1)} %get-tuple-element.119), channel_id=1, source_target_pairs={{0,8},{4,12},{8,0},{12,4},{16,24},{20,28},{24,16},{28,20},{1,9},{5... | collective-permute-start | bytes 294920 | tf_op jit(solution)/shard_map/ppermute | solution.py:688
  95.6 9.3 %collective-permute-start.40 = (f32[32,768]{1,0:T(8,128)S(1)}, f32[32,768]{1,0:T(8,128)S(1)}, u32[]{:S(2)}, u32[]{:S(2)}) collective-permute-start(f32[32,768]{1,0:T(8,128)S(1)} %get-tuple-element.123), channel_id=1, source_target_pairs={{0,24},{4,28},{8,16},{12,20},{16,8},{20,12},{24,0},{28,4},{1,25},{... | collective-permute-start | bytes 294920 | tf_op jit(solution)/shard_map/ppermute | solution.py:688
  100.7 6.6 %collective-permute-start.41 = (f32[32,768]{1,0:T(8,128)S(1)}, f32[32,768]{1,0:T(8,128)S(1)}, u32[]{:S(2)}, u32[]{:S(2)}) collective-permute-start(f32[32,768]{1,0:T(8,128)S(1)} %get-tuple-element.124), channel_id=1, source_target_pairs={{0,12},{4,8},{8,4},{12,0},{16,28},{20,24},{24,20},{28,16},{1,13},{... | collective-permute-start | bytes 294920 | tf_op jit(solution)/shard_map/ppermute | solution.py:688
  101.0 7.4 %collective-permute-start.42 = (f32[32,768]{1,0:T(8,128)S(1)}, f32[32,768]{1,0:T(8,128)S(1)}, u32[]{:S(2)}, u32[]{:S(2)}) collective-permute-start(f32[32,768]{1,0:T(8,128)S(1)} %get-tuple-element.125), channel_id=1, source_target_pairs={{0,28},{4,24},{8,20},{12,16},{16,12},{20,8},{24,4},{28,0},{1,29},{... | collective-permute-start | bytes 294920 | tf_op jit(solution)/shard_map/ppermute | solution.py:688
  104.8 8.3 %collective-permute-start.33 = (f32[72,768]{1,0:T(8,128)S(1)}, f32[72,768]{1,0:T(8,128)S(1)}, u32[]{:S(2)}, u32[]{:S(2)}) collective-permute-start(f32[72,768]{1,0:T(8,128)S(1)} %get-tuple-element.108), channel_id=1, source_target_pairs={{0,2},{1,3},{2,0},{3,1},{4,6},{5,7},{6,4},{7,5},{8,10},{9,11},{10,... | collective-permute-start | bytes 663560 | tf_op jit(solution)/shard_map/ppermute | solution.py:688
  104.8 8.3 %collective-permute-start.34 = (f32[72,768]{1,0:T(8,128)S(1)}, f32[72,768]{1,0:T(8,128)S(1)}, u32[]{:S(2)}, u32[]{:S(2)}) collective-permute-start(f32[72,768]{1,0:T(8,128)S(1)} %get-tuple-element.109), channel_id=1, source_target_pairs={{0,1},{1,0},{2,3},{3,2},{4,5},{5,4},{6,7},{7,6},{8,9},{9,8},{10,11... | collective-permute-start | bytes 663560 | tf_op jit(solution)/shard_map/ppermute | solution.py:688
  104.9 8.9 %collective-permute-start.35 = (f32[72,768]{1,0:T(8,128)S(1)}, f32[72,768]{1,0:T(8,128)S(1)}, u32[]{:S(2)}, u32[]{:S(2)}) collective-permute-start(f32[72,768]{1,0:T(8,128)S(1)} %get-tuple-element.110), channel_id=1, source_target_pairs={{0,3},{1,2},{2,1},{3,0},{4,7},{5,6},{6,5},{7,4},{8,11},{9,10},{10,... | collective-permute-start | bytes 663560 | tf_op jit(solution)/shard_map/ppermute | solution.py:688
  110.1 12.4 %collective-permute-start.43 = (f32[72,768]{1,0:T(8,128)S(1)}, f32[72,768]{1,0:T(8,128)S(1)}, u32[]{:S(2)}, u32[]{:S(2)}) collective-permute-start(f32[72,768]{1,0:T(8,128)S(1)} %get-tuple-element.127), channel_id=1, source_target_pairs={{0,2},{1,3},{2,0},{3,1},{4,6},{5,7},{6,4},{7,5},{8,10},{9,11},{10,... | collective-permute-start | bytes 663560 | tf_op jit(solution)/shard_map/ppermute | solution.py:688
  112.4 10.1 %collective-permute-start.44 = (f32[72,768]{1,0:T(8,128)S(1)}, f32[72,768]{1,0:T(8,128)S(1)}, u32[]{:S(2)}, u32[]{:S(2)}) collective-permute-start(f32[72,768]{1,0:T(8,128)S(1)} %get-tuple-element.128), channel_id=1, source_target_pairs={{0,1},{1,0},{2,3},{3,2},{4,5},{5,4},{6,7},{7,6},{8,9},{9,8},{10,11... | collective-permute-start | bytes 663560 | tf_op jit(solution)/shard_map/ppermute | solution.py:688
  113.1 9.4 %collective-permute-start.45 = (f32[72,768]{1,0:T(8,128)S(1)}, f32[72,768]{1,0:T(8,128)S(1)}, u32[]{:S(2)}, u32[]{:S(2)}) collective-permute-start(f32[72,768]{1,0:T(8,128)S(1)} %get-tuple-element.129), channel_id=1, source_target_pairs={{0,3},{1,2},{2,1},{3,0},{4,7},{5,6},{6,5},{7,4},{8,11},{9,10},{10,... | collective-permute-start | bytes 663560 | tf_op jit(solution)/shard_map/ppermute | solution.py:688
  115.3 13.3 %collective-permute-start.46 = (f32[3,64,256]{2,1,0:T(8,128)S(1)}, f32[3,64,256]{2,1,0:T(8,128)S(1)}, u32[]{:S(2)}, u32[]{:S(2)}) collective-permute-start(f32[3,64,256]{2,1,0:T(8,128)S(1)} %get-tuple-element.132), channel_id=1, source_target_pairs={{0,4},{4,8},{8,12},{12,16},{16,20},{20,24},{24,28},{28,0},{1,5},{5... | collective-permute-start | bytes 589832 | tf_op jit(solution)/shard_map/ppermute | solution.py:817
  119.3 10.8 %collective-permute-start.47 = (f32[3,64,256]{2,1,0:T(8,128)S(1)}, f32[3,64,256]{2,1,0:T(8,128)S(1)}, u32[]{:S(2)}, u32[]{:S(2)}) collective-permute-start(f32[3,64,256]{2,1,0:T(8,128)S(1)} %get-tuple-element.133), channel_id=1, source_target_pairs={{0,28},{4,0},{8,4},{12,8},{16,12},{20,16},{24,20},{28,24},{1,29},{... | collective-permute-start | bytes 589832 | tf_op jit(solution)/shard_map/ppermute | solution.py:816
  (9 other events, 82.4 us)

commit v12 on v11

--- a/solution.py
+++ b/solution.py
@@ -98,9 +98,21 @@
 
 def kernel_weight(distance):
     radius = jnp.abs(distance)
-    near = 1.0 - 2.5 * radius * radius + 1.5 * radius * radius * radius
-    far = 0.5 * (2.0 - radius) * (2.0 - radius) * (1.0 - radius)
-    return jnp.where(radius < 1.0, near, jnp.where(radius < 2.0, far, 0.0))
+    near = 1.0 + radius * radius * (1.5 * radius - 2.5)
+    rest = jnp.maximum(2.0 - radius, 0.0)
+    return jnp.where(radius < 1.0, near, 0.5 * rest * rest * (1.0 - radius))
+
+
+def quotient(values, size):
+    if size & (size - 1):
+        return lax.div(values, size)
+    return lax.shift_right_logical(values, size.bit_length() - 1)
+
+
+def remainder(values, size):
+    if size & (size - 1):
+        return lax.rem(values, size)
+    return values & (size - 1)
 
 
 def turned(value, wave, extent, sign):
@@ -130,10 +142,12 @@
     return plus + minus
 
 
-def offset_order(count):
-    if count < 4:
-        return list(range(count))
+def offset_order(count, near_first=False):
     far, near = list(range(count // 2, count)), list(range(1, count // 2))
+    if near_first:
+        return [0] + near + far
+    if count == 4:
+        return [0] + far + near
     order = [0]
     while far or near:
         order += far[:1] + near[:1]
@@ -141,14 +155,14 @@
     return order
 
 
-def blocks_of(refs, at):
+def blocks_of(refs, at, near_first=False):
     if len(refs) == 1:
         return [(d, refs[0].at[d]) for d in range(refs[0].shape[0])]
-    return [(at ^ k, ref) for k, ref in zip(offset_order(len(refs)), refs)]
-
-
-def gather_blocks(refs, held, at):
-    for d, ref in blocks_of(refs, at):
+    return [(at ^ k, ref) for k, ref in zip(offset_order(len(refs), near_first), refs)]
+
+
+def gather_blocks(refs, held, at, near_first=False):
+    for d, ref in blocks_of(refs, at, near_first):
         held[d] = ref[...]
 
 
@@ -174,7 +188,7 @@
 
 
 def deposit_kernel(
-    pairs, rims_before, place, own, up1, down1, up2, down2, ambient, t_high, t_low, *refs
+    pairs, rims_before, near_first, place, own, up1, down1, up2, down2, ambient, t_high, t_low, *refs
 ):
     rims, refs = refs[:rims_before], refs[rims_before:]
     mesh, rim_high, rim_low = refs[:3]
@@ -190,9 +204,9 @@
         packet = ref[:, start:stop]
         cell = packet[6:7].astype(jnp.int32)
         move = packet[7:8].astype(jnp.int32)
-        z_cell = lax.div(cell, cols * ny) + planes * (move + shift)
-        x_cell = lax.rem(lax.div(cell, ny), cols)
-        return packet[0:6], z_cell, x_cell, lax.rem(cell, ny)
+        z_cell = quotient(cell, cols * ny) + planes * (move + shift)
+        x_cell = remainder(quotient(cell, ny), cols)
+        return packet[0:6], z_cell, x_cell, remainder(cell, ny)
 
     def joined(pieces):
         return [jnp.concatenate(p, axis=1) if len(p) > 1 else p[0] for p in zip(*pieces)]
@@ -206,7 +220,7 @@
         x_at = jnp.where(row < cols + 2, row, jnp.where(row >= rows - 2, row - rows, 4 * rows))
         w_x = kernel_weight((x_at - x_cell).astype(F32) - values[4:5])
         y_at = lax.broadcasted_iota(jnp.int32, (ny, width), 0)
-        y_off = lax.rem(y_at - y_cell + (ny + ny // 2), ny) - ny // 2
+        y_off = remainder(y_at + (ny + ny // 2 - y_cell), ny) - ny // 2
         w_y = kernel_weight(y_off.astype(F32) - values[5:6])
         y_high, y_low = split(w_y)
         right = jnp.concatenate([y_high, y_high, y_low], axis=1)
@@ -259,14 +273,14 @@
             made[g, :, n * LANES : (n + 1) * LANES] = wide[
                 n * rows : (n + 1) * rows, g * LANES : (g + 1) * LANES
             ]
-    for d, out in blocks_of(outs, place[1]):
+    for d, out in blocks_of(outs, place[1], near_first):
         out[...] = made[d]
 
 
-def x_ahead_kernel(sends, place, t_high, t_low, *refs):
+def x_ahead_kernel(sends, near_first, place, t_high, t_low, *refs):
     held, made = refs[-2:]
     outs, parts = refs[-2 - sends : -2], refs[: -2 - sends]
-    gather_blocks(parts, held, place[1])
+    gather_blocks(parts, held, place[1], near_first)
     pencils, rows, width = held.shape
     cols = rows - RIM
     row = lax.broadcasted_iota(jnp.int32, (RIM, width), 0)
@@ -680,13 +694,13 @@
     return [(count, rows, width)] if whole or not spread(axis) else [(rows, width)] * count
 
 
-def exchange(blocks, axis, start=0):
+def exchange(blocks, axis, start=0, near_first=False):
     if not spread(axis):
         return [lax.all_to_all(blocks[0], axis, split_axis=0, concat_axis=0, tiled=True)]
     count = lax.axis_size(axis)
     return [
         lax.ppermute(block, axis, [(i, i ^ k) for i in range(count)]) if k else block
-        for k, block in zip(offset_order(count)[start:], blocks)
+        for k, block in zip(offset_order(count, near_first)[start:], blocks)
     ]
 
 
@@ -730,7 +744,7 @@
         size = 2 * len(chunk)
         rim = (6 * size + (rims[0].shape[0] if rims else 0), ny)
         mesh, rim_high, rim_low, *part = call(
-            functools.partial(deposit_kernel, chunk, len(rims)),
+            functools.partial(deposit_kernel, chunk, len(rims), n == 0),
             [here]
             + [(VM, value) for value in (packet, up1, down1, up2, down2)]
             + [(VM, ambient), (VM, y_ahead[0]), (VM, y_ahead[1])]
@@ -742,7 +756,7 @@
         )
         meshes[n] = mesh
         rims = [rim_high, rim_low]
-        parts[n] = exchange(part, "gx")
+        parts[n] = exchange(part, "gx", near_first=n == 0)
     low_rim = lax.ppermute(rims[0], "gx", ring("gx", 1))
     high_rim = lax.ppermute(rims[1], "gx", ring("gx", -1))
 
@@ -752,7 +766,7 @@
         chunk, part, width = chunks[n], parts[n], widths[n]
         shapes = sent_shapes("gz", block, width)
         part = call(
-            functools.partial(x_ahead_kernel, len(shapes)),
+            functools.partial(x_ahead_kernel, len(shapes), n == 0),
             [here, (VM, x_ahead[0]), (VM, x_ahead[1])] + [(VM, p) for p in part],
             [(VM, shape) for shape in shapes],
             [((pencils, rows, width), F32), ((slabs, block, width), F32)],

time: 131 us -> 132 us (level)
  starting transfers between devices: 69.4 us -> 72.8 us
  waiting for transfers between devices: 29.1 us -> 27.4 us
    ppermute x40, starting transfers between devices: 53 us -> 56.4 us  [exchange(): lax.ppermute(block, axis, [(i, i ^ k) for i in range(count)])]
    ppermute x40, waiting for transfers between devices: 22.9 us -> 21.2 us  [exchange(): lax.ppermute(block, axis, [(i, i ^ k) for i in range(count)])]
  transfers between devices with their start and end apart: 48 -> 48, of which waited for: 16 -> 16; matrix products, arithmetic and copies ran while one was open for 0% -> 0% of each run, Pallas kernels for 17% -> 16%
where the time goes in v12:
time: 132 us
  starting transfers between devices  72.8 us (55%)
  Pallas kernels  30.6 us (23%)
  waiting for transfers between devices  27.4 us (21%)
    ppermute x40, starting transfers between devices, exchange(): lax.ppermute(block, axis, [(i, i ^ k) for i in range(count)])  56.4 us
    pallas_call x16, Pallas kernels, call(): pl.pallas_call(kernel, out_shape=[jax.ShapeDtypeStruct(shape, F32) for _,...  30.6 us
    ppermute x40, waiting for transfers between devices, exchange(): lax.ppermute(block, axis, [(i, i ^ k) for i in range(count)])  21.2 us
    ppermute x1, starting transfers between devices, on_device(): before = lax.ppermute(last, 'gz', ring('gz', 1))  4.32 us
    ppermute x1, starting transfers between devices, on_device(): down2 = lax.ppermute(movers, 'gz', ring('gz', 2))  3.08 us
    ppermute x1, starting transfers between devices, on_device(): up1 = lax.ppermute(packet, 'gz', ring('gz', -1))  3.08 us
    ppermute x1, waiting for transfers between devices, on_device(): before = lax.ppermute(last, 'gz', ring('gz', 1))  2.76 us
  transfers between devices with their start and end apart: 48, of which 16 were waited for; matrix products, arithmetic and copies ran while one was open for 0% of the time, Pallas kernels for 16%

profile of v12, /device:TPU:0, one launch (start us, length us, event | category | flops | bytes accessed | tf_op | source)
XLA Modules:
  0.0 132.1 jit_solution(2703128885634061068)
XLA Ops:
  1.8 3.1 %collective-permute-start.3 = (f32[8,128]{1,0:T(8,128)S(1)}, f32[8,128]{1,0:T(8,128)S(1)}, u32[]{:S(2)}, u32[]{:S(2)}) collective-permute-start(f32[8,128]{1,0:T(8,128)S(1)} %get-tuple-element.69), channel_id=1, source_target_pairs={{0,8},{4,12},{8,16},{12,20},{16,24},{20,28},{24,0},{28,4},{1,9},{5... | collective-permute-start | bytes 12296 | tf_op jit(solution)/shard_map/ppermute | solution.py:739
  4.8 2.1 %collective-permute-start.2 = (f32[8,128]{1,0:T(8,128)S(1)}, f32[8,128]{1,0:T(8,128)S(1)}, u32[]{:S(2)}, u32[]{:S(2)}) collective-permute-start(f32[8,128]{1,0:T(8,128)S(1)} %get-tuple-element.69), channel_id=1, source_target_pairs={{0,24},{4,28},{8,0},{12,4},{16,8},{20,12},{24,16},{28,20},{1,25},{... | collective-permute-start | bytes 12296 | tf_op jit(solution)/shard_map/ppermute | solution.py:738
  6.9 1.6 %collective-permute-start.1 = (f32[8,512]{1,0:T(8,128)S(1)}, f32[8,512]{1,0:T(8,128)S(1)}, u32[]{:S(2)}, u32[]{:S(2)}) collective-permute-start(f32[8,512]{1,0:T(8,128)S(1)} %get-tuple-element.68.own), channel_id=1, source_target_pairs={{0,4},{4,8},{8,12},{12,16},{16,20},{20,24},{24,28},{28,0},{1,5},{5... | collective-permute-start | bytes 49160 | tf_op jit(solution)/shard_map/ppermute | solution.py:737
  8.6 3.1 %collective-permute-start = (f32[8,512]{1,0:T(8,128)S(1)}, f32[8,512]{1,0:T(8,128)S(1)}, u32[]{:S(2)}, u32[]{:S(2)}) collective-permute-start(f32[8,512]{1,0:T(8,128)S(1)} %get-tuple-element.68.own), channel_id=1, source_target_pairs={{0,28},{4,0},{8,4},{12,8},{16,12},{20,16},{24,20},{28,24},{1,29},{... | collective-permute-start | bytes 49160 | tf_op jit(solution)/shard_map/ppermute | solution.py:736
  11.7 1.6 %collective-permute-done.1.down1 = f32[8,512]{1,0:T(8,128)S(1)} collective-permute-done((f32[8,512]{1,0:T(8,128)S(1)}, f32[8,512]{1,0:T(8,128)S(1)}, u32[]{:S(2)}, u32[]{:S(2)}) %collective-permute-start.1) | collective-permute-done | bytes 16416 | tf_op jit(solution)/shard_map/ppermute | solution.py:737
  13.4 3.7 %shard_map.141 = (f32[3,4,64,256]{3,2,1,0:T(8,128)S(1)}, f32[24,256]{1,0:T(8,128)S(1)}, f32[24,256]{1,0:T(8,128)S(1)}, f32[72,768]{1,0:T(8,128)S(1)}, f32[72,768...) custom-call(s32[2]{0:T(128)S(1)} %pad_add_fusion.place, f32[8,512]{1,0:T(8,128)S(1)} %get-tuple-element.68.own, ...), custom_call_target="tpu_custom_call" | custom-call | flops 5000000000 | bytes 15000000 | tf_op jit(solution)/shard_map/pallas_call | solution.py:666
  17.1 1.7 %collective-permute-start.16 = (f32[72,768]{1,0:T(8,128)S(1)}, f32[72,768]{1,0:T(8,128)S(1)}, u32[]{:S(2)}, u32[]{:S(2)}) collective-permute-start(f32[72,768]{1,0:T(8,128)S(1)} %get-tuple-element.87), channel_id=1, source_target_pairs={{0,2},{1,3},{2,0},{3,1},{4,6},{5,7},{6,4},{7,5},{8,10},{9,11},{10,... | collective-permute-start | bytes 663560 | tf_op jit(solution)/shard_map/ppermute | solution.py:702
  19.3 6.0 %shard_map.142 = (f32[3,4,64,256]{3,2,1,0:T(8,128)S(1)}, f32[48,256]{1,0:T(8,128)S(1)}, f32[48,256]{1,0:T(8,128)S(1)}, f32[72,768]{1,0:T(8,128)S(1)}, f32[72,768...) custom-call(s32[2]{0:T(128)S(1)} %pad_add_fusion.place, f32[8,512]{1,0:T(8,128)S(1)} %get-tuple-element.68.own, ...), custom_call_target="tpu_custom_call" | custom-call | flops 5000000000 | bytes 15000000 | tf_op jit(solution)/shard_map/pallas_call | solution.py:666
  25.4 1.7 %collective-permute-start.7 = (f32[72,768]{1,0:T(8,128)S(1)}, f32[72,768]{1,0:T(8,128)S(1)}, u32[]{:S(2)}, u32[]{:S(2)}) collective-permute-start(f32[72,768]{1,0:T(8,128)S(1)} %get-tuple-element.76), channel_id=1, source_target_pairs={{0,2},{1,3},{2,0},{3,1},{4,6},{5,7},{6,4},{7,5},{8,10},{9,11},{10,... | collective-permute-start | bytes 663560 | tf_op jit(solution)/shard_map/ppermute | solution.py:702
  27.2 1.6 %shard_map.145 = (f32[32,768]{1,0:T(8,128)S(1)}, f32[32,768]{1,0:T(8,128)S(1)}, f32[32,768]{1,0:T(8,128)S(1)}, f32[32,768]{1,0:T(8,128)S(1)}, f32[32,768]{1,0:T(...) custom-call(s32[2]{0:T(128)S(1)} %pad_add_fusion.place, ...), custom_call_target="tpu_custom_call" | custom-call | flops 2000000000 | bytes 6000000 | tf_op jit(solution)/shard_map/pallas_call | solution.py:666
  28.9 2.2 %collective-permute-start.20 = (f32[32,768]{1,0:T(8,128)S(1)}, f32[32,768]{1,0:T(8,128)S(1)}, u32[]{:S(2)}, u32[]{:S(2)}) collective-permute-start(f32[32,768]{1,0:T(8,128)S(1)} %get-tuple-element.92), channel_id=1, source_target_pairs={{0,4},{4,0},{8,12},{12,8},{16,20},{20,16},{24,28},{28,24},{1,5},{5... | collective-permute-start | bytes 294920 | tf_op jit(solution)/shard_map/ppermute | solution.py:702
  31.1 2.2 %collective-permute-start.21 = (f32[32,768]{1,0:T(8,128)S(1)}, f32[32,768]{1,0:T(8,128)S(1)}, u32[]{:S(2)}, u32[]{:S(2)}) collective-permute-start(f32[32,768]{1,0:T(8,128)S(1)} %get-tuple-element.93), channel_id=1, source_target_pairs={{0,20},{4,16},{8,28},{12,24},{16,4},{20,0},{24,12},{28,8},{1,21},{... | collective-permute-start | bytes 294920 | tf_op jit(solution)/shard_map/ppermute | solution.py:702
  34.8 2.7 %collective-permute-done.8.refs_3_ = f32[72,768]{1,0:T(8,128)S(1)} collective-permute-done((f32[72,768]{1,0:T(8,128)S(1)}, f32[72,768]{1,0:T(8,128)S(1)}, u32[]{:S(2)}, u32[]{:S(2)}) %collective-permute-start.8) | collective-permute-done | bytes 221216 | tf_op jit(solution)/shard_map/ppermute | solution.py:702
  38.2 1.6 %shard_map.143 = (f32[32,768]{1,0:T(8,128)S(1)}, f32[32,768]{1,0:T(8,128)S(1)}, f32[32,768]{1,0:T(8,128)S(1)}, f32[32,768]{1,0:T(8,128)S(1)}, f32[32,768]{1,0:T(...) custom-call(s32[2]{0:T(128)S(1)} %pad_add_fusion.place, ...), custom_call_target="tpu_custom_call" | custom-call | flops 2000000000 | bytes 6000000 | tf_op jit(solution)/shard_map/pallas_call | solution.py:666
  39.8 1.5 %collective-permute-start.24 = (f32[32,768]{1,0:T(8,128)S(1)}, f32[32,768]{1,0:T(8,128)S(1)}, u32[]{:S(2)}, u32[]{:S(2)}) collective-permute-start(f32[32,768]{1,0:T(8,128)S(1)} %get-tuple-element.96), channel_id=1, source_target_pairs={{0,12},{4,8},{8,4},{12,0},{16,28},{20,24},{24,20},{28,16},{1,13},{... | collective-permute-start | bytes 294920 | tf_op jit(solution)/shard_map/ppermute | solution.py:702
  41.3 2.6 %collective-permute-start.25 = (f32[32,768]{1,0:T(8,128)S(1)}, f32[32,768]{1,0:T(8,128)S(1)}, u32[]{:S(2)}, u32[]{:S(2)}) collective-permute-start(f32[32,768]{1,0:T(8,128)S(1)} %get-tuple-element.97), channel_id=1, source_target_pairs={{0,28},{4,24},{8,20},{12,16},{16,12},{20,8},{24,4},{28,0},{1,29},{... | collective-permute-start | bytes 294920 | tf_op jit(solution)/shard_map/ppermute | solution.py:702
  44.5 4.3 %collective-permute-start.10 = (f32[32,768]{1,0:T(8,128)S(1)}, f32[32,768]{1,0:T(8,128)S(1)}, u32[]{:S(2)}, u32[]{:S(2)}) collective-permute-start(f32[32,768]{1,0:T(8,128)S(1)} %get-tuple-element.80), channel_id=1, source_target_pairs={{0,4},{4,0},{8,12},{12,8},{16,20},{20,16},{24,28},{28,24},{1,5},{5... | collective-permute-start | bytes 294920 | tf_op jit(solution)/shard_map/ppermute | solution.py:702
  48.8 3.2 %collective-permute-start.12 = (f32[32,768]{1,0:T(8,128)S(1)}, f32[32,768]{1,0:T(8,128)S(1)}, u32[]{:S(2)}, u32[]{:S(2)}) collective-permute-start(f32[32,768]{1,0:T(8,128)S(1)} %get-tuple-element.82), channel_id=1, source_target_pairs={{0,8},{4,12},{8,0},{12,4},{16,24},{20,28},{24,16},{28,20},{1,9},{5... | collective-permute-start | bytes 294920 | tf_op jit(solution)/shard_map/ppermute | solution.py:702
  52.1 1.8 %collective-permute-start.13 = (f32[32,768]{1,0:T(8,128)S(1)}, f32[32,768]{1,0:T(8,128)S(1)}, u32[]{:S(2)}, u32[]{:S(2)}) collective-permute-start(f32[32,768]{1,0:T(8,128)S(1)} %get-tuple-element.83), channel_id=1, source_target_pairs={{0,24},{4,28},{8,16},{12,20},{16,8},{20,12},{24,0},{28,4},{1,25},{... | collective-permute-start | bytes 294920 | tf_op jit(solution)/shard_map/ppermute | solution.py:702
  53.9 3.5 %collective-permute-done.9.refs_1_ = f32[32,768]{1,0:T(8,128)S(1)} collective-permute-done((f32[32,768]{1,0:T(8,128)S(1)}, f32[32,768]{1,0:T(8,128)S(1)}, u32[]{:S(2)}, u32[]{:S(2)}) %collective-permute-start.9) | collective-permute-done | bytes 98336 | tf_op jit(solution)/shard_map/ppermute | solution.py:702
  57.4 2.0 %collective-permute-start.14 = (f32[32,768]{1,0:T(8,128)S(1)}, f32[32,768]{1,0:T(8,128)S(1)}, u32[]{:S(2)}, u32[]{:S(2)}) collective-permute-start(f32[32,768]{1,0:T(8,128)S(1)} %get-tuple-element.84), channel_id=1, source_target_pairs={{0,12},{4,8},{8,4},{12,0},{16,28},{20,24},{24,20},{28,16},{1,13},{... | collective-permute-start | bytes 294920 | tf_op jit(solution)/shard_map/ppermute | solution.py:702
  59.4 3.0 %collective-permute-start.15 = (f32[32,768]{1,0:T(8,128)S(1)}, f32[32,768]{1,0:T(8,128)S(1)}, u32[]{:S(2)}, u32[]{:S(2)}) collective-permute-start(f32[32,768]{1,0:T(8,128)S(1)} %get-tuple-element.85), channel_id=1, source_target_pairs={{0,28},{4,24},{8,20},{12,16},{16,12},{20,8},{24,4},{28,0},{1,29},{... | collective-permute-start | bytes 294920 | tf_op jit(solution)/shard_map/ppermute | solution.py:702
  63.8 1.7 %collective-permute-start.5 = (f32[48,256]{1,0:T(8,128)S(1)}, f32[48,256]{1,0:T(8,128)S(1)}, u32[]{:S(2)}, u32[]{:S(2)}) collective-permute-start(f32[48,256]{1,0:T(8,128)S(1)} %get-tuple-element.73), channel_id=1, source_target_pairs={{0,3},{1,0},{2,1},{3,2},{4,7},{5,4},{6,5},{7,6},{8,11},{9,8},{10,9... | collective-permute-start | bytes 147464 | tf_op jit(solution)/shard_map/ppermute | solution.py:761
  65.6 2.3 %collective-permute-done.14.refs_6_ = f32[32,768]{1,0:T(8,128)S(1)} collective-permute-done((f32[32,768]{1,0:T(8,128)S(1)}, f32[32,768]{1,0:T(8,128)S(1)}, u32[]{:S(2)}, u32[]{:S(2)}) %collective-permute-start.14) | collective-permute-done | bytes 98336 | tf_op jit(solution)/shard_map/ppermute | solution.py:702
  69.3 2.3 %shard_map.147 = (f32[3,2,4,8,8,128]{5,4,3,2,1,0:T(8,128)S(1)}, f32[3,2,4,8,8,128]{5,4,3,2,1,0:T(8,128)S(1)}) custom-call(s32[2]{0:T(128)S(1)} %pad_add_fusion.place, f32[48,256]{1,0:T(8,128)S(1)} %collective-permute-done.4.low_rim.refs_1_, f32[48,256]{1,0:T(8,128)S(1)} %collective-permute-done.5.high_rim.refs_2_, ...), custom_call_target="tpu_custom_call" | custom-call | flops 5000000000 | bytes 15000000 | tf_op jit(solution)/shard_map/pallas_call | solution.py:666
  73.0 1.8 %collective-permute-start.26 = (f32[32,768]{1,0:T(8,128)S(1)}, f32[32,768]{1,0:T(8,128)S(1)}, u32[]{:S(2)}, u32[]{:S(2)}) collective-permute-start(f32[32,768]{1,0:T(8,128)S(1)} %get-tuple-element.100), channel_id=1, source_target_pairs={{0,16},{4,20},{8,24},{12,28},{16,0},{20,4},{24,8},{28,12},{1,17},{... | collective-permute-start | bytes 294920 | tf_op jit(solution)/shard_map/ppermute | solution.py:702
  75.8 1.7 %collective-permute-start.28 = (f32[32,768]{1,0:T(8,128)S(1)}, f32[32,768]{1,0:T(8,128)S(1)}, u32[]{:S(2)}, u32[]{:S(2)}) collective-permute-start(f32[32,768]{1,0:T(8,128)S(1)} %get-tuple-element.102), channel_id=1, source_target_pairs={{0,20},{4,16},{8,28},{12,24},{16,4},{20,0},{24,12},{28,8},{1,21},{... | collective-permute-start | bytes 294920 | tf_op jit(solution)/shard_map/ppermute | solution.py:702
  77.5 1.7 %collective-permute-start.29 = (f32[32,768]{1,0:T(8,128)S(1)}, f32[32,768]{1,0:T(8,128)S(1)}, u32[]{:S(2)}, u32[]{:S(2)}) collective-permute-start(f32[32,768]{1,0:T(8,128)S(1)} %get-tuple-element.103), channel_id=1, source_target_pairs={{0,8},{4,12},{8,0},{12,4},{16,24},{20,28},{24,16},{28,20},{1,9},{5... | collective-permute-start | bytes 294920 | tf_op jit(solution)/shard_map/ppermute | solution.py:702
  79.1 1.5 %collective-permute-start.30 = (f32[32,768]{1,0:T(8,128)S(1)}, f32[32,768]{1,0:T(8,128)S(1)}, u32[]{:S(2)}, u32[]{:S(2)}) collective-permute-start(f32[32,768]{1,0:T(8,128)S(1)} %get-tuple-element.104), channel_id=1, source_target_pairs={{0,24},{4,28},{8,16},{12,20},{16,8},{20,12},{24,0},{28,4},{1,25},{... | collective-permute-start | bytes 294920 | tf_op jit(solution)/shard_map/ppermute | solution.py:702
  80.7 2.8 %collective-permute-done.26.refs_1_ = f32[32,768]{1,0:T(8,128)S(1)} collective-permute-done((f32[32,768]{1,0:T(8,128)S(1)}, f32[32,768]{1,0:T(8,128)S(1)}, u32[]{:S(2)}, u32[]{:S(2)}) %collective-permute-start.26) | collective-permute-done | bytes 98336 | tf_op jit(solution)/shard_map/ppermute | solution.py:702
  83.6 3.0 %collective-permute-start.32 = (f32[32,768]{1,0:T(8,128)S(1)}, f32[32,768]{1,0:T(8,128)S(1)}, u32[]{:S(2)}, u32[]{:S(2)}) collective-permute-start(f32[32,768]{1,0:T(8,128)S(1)} %get-tuple-element.106), channel_id=1, source_target_pairs={{0,28},{4,24},{8,20},{12,16},{16,12},{20,8},{24,4},{28,0},{1,29},{... | collective-permute-start | bytes 294920 | tf_op jit(solution)/shard_map/ppermute | solution.py:702
  88.0 1.4 %collective-permute-done.28.refs_3_ = f32[32,768]{1,0:T(8,128)S(1)} collective-permute-done((f32[32,768]{1,0:T(8,128)S(1)}, f32[32,768]{1,0:T(8,128)S(1)}, u32[]{:S(2)}, u32[]{:S(2)}) %collective-permute-start.28) | collective-permute-done | bytes 98336 | tf_op jit(solution)/shard_map/ppermute | solution.py:702
  89.4 1.6 %collective-permute-start.37 = (f32[32,768]{1,0:T(8,128)S(1)}, f32[32,768]{1,0:T(8,128)S(1)}, u32[]{:S(2)}, u32[]{:S(2)}) collective-permute-start(f32[32,768]{1,0:T(8,128)S(1)} %get-tuple-element.117), channel_id=1, source_target_pairs={{0,4},{4,0},{8,12},{12,8},{16,20},{20,16},{24,28},{28,24},{1,5},{5... | collective-permute-start | bytes 294920 | tf_op jit(solution)/shard_map/ppermute | solution.py:702
  91.0 3.1 %collective-permute-start.38 = (f32[32,768]{1,0:T(8,128)S(1)}, f32[32,768]{1,0:T(8,128)S(1)}, u32[]{:S(2)}, u32[]{:S(2)}) collective-permute-start(f32[32,768]{1,0:T(8,128)S(1)} %get-tuple-element.118), channel_id=1, source_target_pairs={{0,20},{4,16},{8,28},{12,24},{16,4},{20,0},{24,12},{28,8},{1,21},{... | collective-permute-start | bytes 294920 | tf_op jit(solution)/shard_map/ppermute | solution.py:702
  94.1 1.7 %shard_map.149 = (f32[72,768]{1,0:T(8,128)S(1)}, f32[72,768]{1,0:T(8,128)S(1)}, f32[72,768]{1,0:T(8,128)S(1)}, f32[72,768]{1,0:T(8,128)S(1)}) custom-call(s32[2]{0:T(128)S(1)} %pad_add_fusion.place, bf16[576,256]{1,0:T(8,128)(2,1)S(1)} %copy-done.6, bf16[576,256]{1,0:T(8,128)(2,1)S(1)} %copy-done.5, f32[32,768]{1,0:T(8,128)S(1)} %get-tuple-element.99.refs_0_, ...), custom_call_target="tpu_custom_call" | custom-call | flops 2000000000 | bytes 6000000 | tf_op jit(solution)/shard_map/pallas_call | solution.py:666
  95.8 2.9 %collective-permute-start.40 = (f32[32,768]{1,0:T(8,128)S(1)}, f32[32,768]{1,0:T(8,128)S(1)}, u32[]{:S(2)}, u32[]{:S(2)}) collective-permute-start(f32[32,768]{1,0:T(8,128)S(1)} %get-tuple-element.123), channel_id=1, source_target_pairs={{0,24},{4,28},{8,16},{12,20},{16,8},{20,12},{24,0},{28,4},{1,25},{... | collective-permute-start | bytes 294920 | tf_op jit(solution)/shard_map/ppermute | solution.py:702
  98.7 2.4 %collective-permute-done.36.refs_1_ = f32[32,768]{1,0:T(8,128)S(1)} collective-permute-done((f32[32,768]{1,0:T(8,128)S(1)}, f32[32,768]{1,0:T(8,128)S(1)}, u32[]{:S(2)}, u32[]{:S(2)}) %collective-permute-start.36) | collective-permute-done | bytes 98336 | tf_op jit(solution)/shard_map/ppermute | solution.py:702
  101.2 4.3 %collective-permute-start.42 = (f32[32,768]{1,0:T(8,128)S(1)}, f32[32,768]{1,0:T(8,128)S(1)}, u32[]{:S(2)}, u32[]{:S(2)}) collective-permute-start(f32[32,768]{1,0:T(8,128)S(1)} %get-tuple-element.125), channel_id=1, source_target_pairs={{0,28},{4,24},{8,20},{12,16},{16,12},{20,8},{24,4},{28,0},{1,29},{... | collective-permute-start | bytes 294920 | tf_op jit(solution)/shard_map/ppermute | solution.py:702
  105.6 2.1 %collective-permute-start.35 = (f32[72,768]{1,0:T(8,128)S(1)}, f32[72,768]{1,0:T(8,128)S(1)}, u32[]{:S(2)}, u32[]{:S(2)}) collective-permute-start(f32[72,768]{1,0:T(8,128)S(1)} %get-tuple-element.110), channel_id=1, source_target_pairs={{0,1},{1,0},{2,3},{3,2},{4,5},{5,4},{6,7},{7,6},{8,9},{9,8},{10,11... | collective-permute-start | bytes 663560 | tf_op jit(solution)/shard_map/ppermute | solution.py:702
  107.8 1.4 %collective-permute-done.42.refs_7_ = f32[32,768]{1,0:T(8,128)S(1)} collective-permute-done((f32[32,768]{1,0:T(8,128)S(1)}, f32[32,768]{1,0:T(8,128)S(1)}, u32[]{:S(2)}, u32[]{:S(2)}) %collective-permute-start.42) | collective-permute-done | bytes 98336 | tf_op jit(solution)/shard_map/ppermute | solution.py:702
  109.2 1.7 %shard_map.153 = (f32[72,768]{1,0:T(8,128)S(1)}, f32[72,768]{1,0:T(8,128)S(1)}, f32[72,768]{1,0:T(8,128)S(1)}, f32[72,768]{1,0:T(8,128)S(1)}) custom-call(s32[2]{0:T(128)S(1)} %pad_add_fusion.place, bf16[576,256]{1,0:T(8,128)(2,1)S(1)} %copy-done.6, bf16[576,256]{1,0:T(8,128)(2,1)S(1)} %copy-done.5, f32[32,768]{1,0:T(8,128)S(1)} %get-tuple-element.115.refs_0_, ...), custom_call_target="tpu_custom_call" | custom-call | flops 2000000000 | bytes 6000000 | tf_op jit(solution)/shard_map/pallas_call | solution.py:666
  110.9 2.1 %collective-permute-start.43 = (f32[72,768]{1,0:T(8,128)S(1)}, f32[72,768]{1,0:T(8,128)S(1)}, u32[]{:S(2)}, u32[]{:S(2)}) collective-permute-start(f32[72,768]{1,0:T(8,128)S(1)} %get-tuple-element.127), channel_id=1, source_target_pairs={{0,2},{1,3},{2,0},{3,1},{4,6},{5,7},{6,4},{7,5},{8,10},{9,11},{10,... | collective-permute-start | bytes 663560 | tf_op jit(solution)/shard_map/ppermute | solution.py:702
  114.7 1.5 %shard_map.150 = (f32[3,4,80,256]{3,2,1,0:T(8,128)S(1)}, f32[3,64,256]{2,1,0:T(8,128)S(1)}, f32[3,64,256]{2,1,0:T(8,128)S(1)}) custom-call(s32[2]{0:T(128)S(1)} %pad_add_fusion.place, bf16[512,512]{1,0:T(8,128)(2,1)S(1)} %copy-done.2, bf16[512,512]{1,0:T(8,128)(2,1)S(1)} %copy-done.1, f32[72,768]{1,0:T(8,128)S(1)} %get-tuple-element.107.refs_0_.before, ...), custom_call_target="tpu_custom_call" | custom-call | flops 2000000000 | bytes 6000000 | tf_op jit(solution)/shard_map/pallas_call | solution.py:666
  116.1 4.3 %collective-permute-start.46 = (f32[3,64,256]{2,1,0:T(8,128)S(1)}, f32[3,64,256]{2,1,0:T(8,128)S(1)}, u32[]{:S(2)}, u32[]{:S(2)}) collective-permute-start(f32[3,64,256]{2,1,0:T(8,128)S(1)} %get-tuple-element.132), channel_id=1, source_target_pairs={{0,4},{4,8},{8,12},{12,16},{16,20},{20,24},{24,28},{28,0},{1,5},{5... | collective-permute-start | bytes 589832 | tf_op jit(solution)/shard_map/ppermute | solution.py:831
  120.9 1.9 %collective-permute-done.43.refs_6_ = f32[72,768]{1,0:T(8,128)S(1)} collective-permute-done((f32[72,768]{1,0:T(8,128)S(1)}, f32[72,768]{1,0:T(8,128)S(1)}, u32[]{:S(2)}, u32[]{:S(2)}) %collective-permute-start.43) | collective-permute-done | bytes 221216 | tf_op jit(solution)/shard_map/ppermute | solution.py:702
  123.3 3.0 %shard_map.154 = (f32[3,8,64,256]{3,2,1,0:T(8,128)}, f32[3,8,64,256]{3,2,1,0:T(8,128)}) custom-call(s32[2]{0:T(128)S(1)} %pad_add_fusion.place, bf16[512,512]{1,0:T(8,128)(2,1)S(1)} %copy-done.2, bf16[512,512]{1,0:T(8,128)(2,1)S(1)} %copy-done.1, f32[3,4,80,256]{3,2,1,0:T(8,128)S(1)} %get-tuple-element.111.refs_0_.edges, ...), custom_call_target="tpu_custom_call" | custom-call | flops 4000000000 | bytes 12000000 | tf_op jit(solution)/shard_map/pallas_call | solution.py:666
  126.3 2.8 %collective-permute-done.46.before = f32[3,64,256]{2,1,0:T(8,128)S(1)} collective-permute-done((f32[3,64,256]{2,1,0:T(8,128)S(1)}, f32[3,64,256]{2,1,0:T(8,128)S(1)}, u32[]{:S(2)}, u32[]{:S(2)}) %collective-permute-start.46) | collective-permute-done | bytes 196640 | tf_op jit(solution)/shard_map/ppermute | solution.py:831
  129.1 1.8 %collective-permute-done.47.after = f32[3,64,256]{2,1,0:T(8,128)S(1)} collective-permute-done((f32[3,64,256]{2,1,0:T(8,128)S(1)}, f32[3,64,256]{2,1,0:T(8,128)S(1)}, u32[]{:S(2)}, u32[]{:S(2)}) %collective-permute-start.47) | collective-permute-done | bytes 196640 | tf_op jit(solution)/shard_map/ppermute | solution.py:830
  (83 shorter events, 15.3 us)
Async XLA Ops:
  1.8 10.0 %collective-permute-start.3 = (f32[8,128]{1,0:T(8,128)S(1)}, f32[8,128]{1,0:T(8,128)S(1)}, u32[]{:S(2)}, u32[]{:S(2)}) collective-permute-start(f32[8,128]{1,0:T(8,128)S(1)} %get-tuple-element.69), channel_id=1, source_target_pairs={{0,8},{4,12},{8,16},{12,20},{16,24},{20,28},{24,0},{28,4},{1,9},{5... | collective-permute-start | bytes 12296 | tf_op jit(solution)/shard_map/ppermute | solution.py:739
  4.8 6.9 %collective-permute-start.2 = (f32[8,128]{1,0:T(8,128)S(1)}, f32[8,128]{1,0:T(8,128)S(1)}, u32[]{:S(2)}, u32[]{:S(2)}) collective-permute-start(f32[8,128]{1,0:T(8,128)S(1)} %get-tuple-element.69), channel_id=1, source_target_pairs={{0,24},{4,28},{8,0},{12,4},{16,8},{20,12},{24,16},{28,20},{1,25},{... | collective-permute-start | bytes 12296 | tf_op jit(solution)/shard_map/ppermute | solution.py:738
  6.9 6.4 %collective-permute-start.1 = (f32[8,512]{1,0:T(8,128)S(1)}, f32[8,512]{1,0:T(8,128)S(1)}, u32[]{:S(2)}, u32[]{:S(2)}) collective-permute-start(f32[8,512]{1,0:T(8,128)S(1)} %get-tuple-element.68.own), channel_id=1, source_target_pairs={{0,4},{4,8},{8,12},{12,16},{16,20},{20,24},{24,28},{28,0},{1,5},{5... | collective-permute-start | bytes 49160 | tf_op jit(solution)/shard_map/ppermute | solution.py:737
  8.6 4.8 %collective-permute-start = (f32[8,512]{1,0:T(8,128)S(1)}, f32[8,512]{1,0:T(8,128)S(1)}, u32[]{:S(2)}, u32[]{:S(2)}) collective-permute-start(f32[8,512]{1,0:T(8,128)S(1)} %get-tuple-element.68.own), channel_id=1, source_target_pairs={{0,28},{4,0},{8,4},{12,8},{16,12},{20,16},{24,20},{28,24},{1,29},{... | collective-permute-start | bytes 49160 | tf_op jit(solution)/shard_map/ppermute | solution.py:736
  17.1 10.0 %collective-permute-start.16 = (f32[72,768]{1,0:T(8,128)S(1)}, f32[72,768]{1,0:T(8,128)S(1)}, u32[]{:S(2)}, u32[]{:S(2)}) collective-permute-start(f32[72,768]{1,0:T(8,128)S(1)} %get-tuple-element.87), channel_id=1, source_target_pairs={{0,2},{1,3},{2,0},{3,1},{4,6},{5,7},{6,4},{7,5},{8,10},{9,11},{10,... | collective-permute-start | bytes 663560 | tf_op jit(solution)/shard_map/ppermute | solution.py:702
  18.8 8.4 %collective-permute-start.17 = (f32[72,768]{1,0:T(8,128)S(1)}, f32[72,768]{1,0:T(8,128)S(1)}, u32[]{:S(2)}, u32[]{:S(2)}) collective-permute-start(f32[72,768]{1,0:T(8,128)S(1)} %get-tuple-element.88), channel_id=1, source_target_pairs={{0,3},{1,2},{2,1},{3,0},{4,7},{5,6},{6,5},{7,4},{8,11},{9,10},{10,... | collective-permute-start | bytes 663560 | tf_op jit(solution)/shard_map/ppermute | solution.py:702
  18.8 8.4 %collective-permute-start.18 = (f32[72,768]{1,0:T(8,128)S(1)}, f32[72,768]{1,0:T(8,128)S(1)}, u32[]{:S(2)}, u32[]{:S(2)}) collective-permute-start(f32[72,768]{1,0:T(8,128)S(1)} %get-tuple-element.89), channel_id=1, source_target_pairs={{0,1},{1,0},{2,3},{3,2},{4,5},{5,4},{6,7},{7,6},{8,9},{9,8},{10,11... | collective-permute-start | bytes 663560 | tf_op jit(solution)/shard_map/ppermute | solution.py:702
  25.3 5.8 %collective-permute-start.6 = (f32[72,768]{1,0:T(8,128)S(1)}, f32[72,768]{1,0:T(8,128)S(1)}, u32[]{:S(2)}, u32[]{:S(2)}) collective-permute-start(f32[72,768]{1,0:T(8,128)S(1)} %get-tuple-element.75), channel_id=1, source_target_pairs={{0,1},{1,0},{2,3},{3,2},{4,5},{5,4},{6,7},{7,6},{8,9},{9,8},{10,11... | collective-permute-start | bytes 663560 | tf_op jit(solution)/shard_map/ppermute | solution.py:702
  25.4 8.3 %collective-permute-start.7 = (f32[72,768]{1,0:T(8,128)S(1)}, f32[72,768]{1,0:T(8,128)S(1)}, u32[]{:S(2)}, u32[]{:S(2)}) collective-permute-start(f32[72,768]{1,0:T(8,128)S(1)} %get-tuple-element.76), channel_id=1, source_target_pairs={{0,2},{1,3},{2,0},{3,1},{4,6},{5,7},{6,4},{7,5},{8,10},{9,11},{10,... | collective-permute-start | bytes 663560 | tf_op jit(solution)/shard_map/ppermute | solution.py:702
  27.1 10.4 %collective-permute-start.8 = (f32[72,768]{1,0:T(8,128)S(1)}, f32[72,768]{1,0:T(8,128)S(1)}, u32[]{:S(2)}, u32[]{:S(2)}) collective-permute-start(f32[72,768]{1,0:T(8,128)S(1)} %get-tuple-element.77), channel_id=1, source_target_pairs={{0,3},{1,2},{2,1},{3,0},{4,7},{5,6},{6,5},{7,4},{8,11},{9,10},{10,... | collective-permute-start | bytes 663560 | tf_op jit(solution)/shard_map/ppermute | solution.py:702
  28.8 11.0 %collective-permute-start.19 = (f32[32,768]{1,0:T(8,128)S(1)}, f32[32,768]{1,0:T(8,128)S(1)}, u32[]{:S(2)}, u32[]{:S(2)}) collective-permute-start(f32[32,768]{1,0:T(8,128)S(1)} %get-tuple-element.91), channel_id=1, source_target_pairs={{0,16},{4,20},{8,24},{12,28},{16,0},{20,4},{24,8},{28,12},{1,17},{... | collective-permute-start | bytes 294920 | tf_op jit(solution)/shard_map/ppermute | solution.py:702
  28.9 12.4 %collective-permute-start.20 = (f32[32,768]{1,0:T(8,128)S(1)}, f32[32,768]{1,0:T(8,128)S(1)}, u32[]{:S(2)}, u32[]{:S(2)}) collective-permute-start(f32[32,768]{1,0:T(8,128)S(1)} %get-tuple-element.92), channel_id=1, source_target_pairs={{0,4},{4,0},{8,12},{12,8},{16,20},{20,16},{24,28},{28,24},{1,5},{5... | collective-permute-start | bytes 294920 | tf_op jit(solution)/shard_map/ppermute | solution.py:702
  31.1 12.9 %collective-permute-start.21 = (f32[32,768]{1,0:T(8,128)S(1)}, f32[32,768]{1,0:T(8,128)S(1)}, u32[]{:S(2)}, u32[]{:S(2)}) collective-permute-start(f32[32,768]{1,0:T(8,128)S(1)} %get-tuple-element.93), channel_id=1, source_target_pairs={{0,20},{4,16},{8,28},{12,24},{16,4},{20,0},{24,12},{28,8},{1,21},{... | collective-permute-start | bytes 294920 | tf_op jit(solution)/shard_map/ppermute | solution.py:702
  33.6 10.9 %collective-permute-start.22 = (f32[32,768]{1,0:T(8,128)S(1)}, f32[32,768]{1,0:T(8,128)S(1)}, u32[]{:S(2)}, u32[]{:S(2)}) collective-permute-start(f32[32,768]{1,0:T(8,128)S(1)} %get-tuple-element.94), channel_id=1, source_target_pairs={{0,8},{4,12},{8,0},{12,4},{16,24},{20,28},{24,16},{28,20},{1,9},{5... | collective-permute-start | bytes 294920 | tf_op jit(solution)/shard_map/ppermute | solution.py:702
  37.5 11.4 %collective-permute-start.23 = (f32[32,768]{1,0:T(8,128)S(1)}, f32[32,768]{1,0:T(8,128)S(1)}, u32[]{:S(2)}, u32[]{:S(2)}) collective-permute-start(f32[32,768]{1,0:T(8,128)S(1)} %get-tuple-element.95), channel_id=1, source_target_pairs={{0,24},{4,28},{8,16},{12,20},{16,8},{20,12},{24,0},{28,4},{1,25},{... | collective-permute-start | bytes 294920 | tf_op jit(solution)/shard_map/ppermute | solution.py:702
  39.8 9.0 %collective-permute-start.24 = (f32[32,768]{1,0:T(8,128)S(1)}, f32[32,768]{1,0:T(8,128)S(1)}, u32[]{:S(2)}, u32[]{:S(2)}) collective-permute-start(f32[32,768]{1,0:T(8,128)S(1)} %get-tuple-element.96), channel_id=1, source_target_pairs={{0,12},{4,8},{8,4},{12,0},{16,28},{20,24},{24,20},{28,16},{1,13},{... | collective-permute-start | bytes 294920 | tf_op jit(solution)/shard_map/ppermute | solution.py:702
  41.3 10.8 %collective-permute-start.25 = (f32[32,768]{1,0:T(8,128)S(1)}, f32[32,768]{1,0:T(8,128)S(1)}, u32[]{:S(2)}, u32[]{:S(2)}) collective-permute-start(f32[32,768]{1,0:T(8,128)S(1)} %get-tuple-element.97), channel_id=1, source_target_pairs={{0,28},{4,24},{8,20},{12,16},{16,12},{20,8},{24,4},{28,0},{1,29},{... | collective-permute-start | bytes 294920 | tf_op jit(solution)/shard_map/ppermute | solution.py:702
  44.0 13.4 %collective-permute-start.9 = (f32[32,768]{1,0:T(8,128)S(1)}, f32[32,768]{1,0:T(8,128)S(1)}, u32[]{:S(2)}, u32[]{:S(2)}) collective-permute-start(f32[32,768]{1,0:T(8,128)S(1)} %get-tuple-element.79), channel_id=1, source_target_pairs={{0,16},{4,20},{8,24},{12,28},{16,0},{20,4},{24,8},{28,12},{1,17},{... | collective-permute-start | bytes 294920 | tf_op jit(solution)/shard_map/ppermute | solution.py:702
  44.5 14.9 %collective-permute-start.10 = (f32[32,768]{1,0:T(8,128)S(1)}, f32[32,768]{1,0:T(8,128)S(1)}, u32[]{:S(2)}, u32[]{:S(2)}) collective-permute-start(f32[32,768]{1,0:T(8,128)S(1)} %get-tuple-element.80), channel_id=1, source_target_pairs={{0,4},{4,0},{8,12},{12,8},{16,20},{20,16},{24,28},{28,24},{1,5},{5... | collective-permute-start | bytes 294920 | tf_op jit(solution)/shard_map/ppermute | solution.py:702
  48.8 14.9 %collective-permute-start.11 = (f32[32,768]{1,0:T(8,128)S(1)}, f32[32,768]{1,0:T(8,128)S(1)}, u32[]{:S(2)}, u32[]{:S(2)}) collective-permute-start(f32[32,768]{1,0:T(8,128)S(1)} %get-tuple-element.81), channel_id=1, source_target_pairs={{0,20},{4,16},{8,28},{12,24},{16,4},{20,0},{24,12},{28,8},{1,21},{... | collective-permute-start | bytes 294920 | tf_op jit(solution)/shard_map/ppermute | solution.py:702
  48.8 15.0 %collective-permute-start.12 = (f32[32,768]{1,0:T(8,128)S(1)}, f32[32,768]{1,0:T(8,128)S(1)}, u32[]{:S(2)}, u32[]{:S(2)}) collective-permute-start(f32[32,768]{1,0:T(8,128)S(1)} %get-tuple-element.82), channel_id=1, source_target_pairs={{0,8},{4,12},{8,0},{12,4},{16,24},{20,28},{24,16},{28,20},{1,9},{5... | collective-permute-start | bytes 294920 | tf_op jit(solution)/shard_map/ppermute | solution.py:702
  52.1 13.5 %collective-permute-start.13 = (f32[32,768]{1,0:T(8,128)S(1)}, f32[32,768]{1,0:T(8,128)S(1)}, u32[]{:S(2)}, u32[]{:S(2)}) collective-permute-start(f32[32,768]{1,0:T(8,128)S(1)} %get-tuple-element.83), channel_id=1, source_target_pairs={{0,24},{4,28},{8,16},{12,20},{16,8},{20,12},{24,0},{28,4},{1,25},{... | collective-permute-start | bytes 294920 | tf_op jit(solution)/shard_map/ppermute | solution.py:702
  57.4 10.5 %collective-permute-start.14 = (f32[32,768]{1,0:T(8,128)S(1)}, f32[32,768]{1,0:T(8,128)S(1)}, u32[]{:S(2)}, u32[]{:S(2)}) collective-permute-start(f32[32,768]{1,0:T(8,128)S(1)} %get-tuple-element.84), channel_id=1, source_target_pairs={{0,12},{4,8},{8,4},{12,0},{16,28},{20,24},{24,20},{28,16},{1,13},{... | collective-permute-start | bytes 294920 | tf_op jit(solution)/shard_map/ppermute | solution.py:702
  59.4 8.4 %collective-permute-start.15 = (f32[32,768]{1,0:T(8,128)S(1)}, f32[32,768]{1,0:T(8,128)S(1)}, u32[]{:S(2)}, u32[]{:S(2)}) collective-permute-start(f32[32,768]{1,0:T(8,128)S(1)} %get-tuple-element.85), channel_id=1, source_target_pairs={{0,28},{4,24},{8,20},{12,16},{16,12},{20,8},{24,4},{28,0},{1,29},{... | collective-permute-start | bytes 294920 | tf_op jit(solution)/shard_map/ppermute | solution.py:702
  63.8 5.5 %collective-permute-start.4 = (f32[48,256]{1,0:T(8,128)S(1)}, f32[48,256]{1,0:T(8,128)S(1)}, u32[]{:S(2)}, u32[]{:S(2)}) collective-permute-start(f32[48,256]{1,0:T(8,128)S(1)} %get-tuple-element.72), channel_id=1, source_target_pairs={{0,1},{1,2},{2,3},{3,0},{4,5},{5,6},{6,7},{7,4},{8,9},{9,10},{10,1... | collective-permute-start | bytes 147464 | tf_op jit(solution)/shard_map/ppermute | solution.py:760
  63.8 5.4 %collective-permute-start.5 = (f32[48,256]{1,0:T(8,128)S(1)}, f32[48,256]{1,0:T(8,128)S(1)}, u32[]{:S(2)}, u32[]{:S(2)}) collective-permute-start(f32[48,256]{1,0:T(8,128)S(1)} %get-tuple-element.73), channel_id=1, source_target_pairs={{0,3},{1,0},{2,1},{3,2},{4,7},{5,4},{6,5},{7,6},{8,11},{9,8},{10,9... | collective-permute-start | bytes 147464 | tf_op jit(solution)/shard_map/ppermute | solution.py:761
  73.0 10.5 %collective-permute-start.26 = (f32[32,768]{1,0:T(8,128)S(1)}, f32[32,768]{1,0:T(8,128)S(1)}, u32[]{:S(2)}, u32[]{:S(2)}) collective-permute-start(f32[32,768]{1,0:T(8,128)S(1)} %get-tuple-element.100), channel_id=1, source_target_pairs={{0,16},{4,20},{8,24},{12,28},{16,0},{20,4},{24,8},{28,12},{1,17},{... | collective-permute-start | bytes 294920 | tf_op jit(solution)/shard_map/ppermute | solution.py:702
  74.8 8.8 %collective-permute-start.27 = (f32[32,768]{1,0:T(8,128)S(1)}, f32[32,768]{1,0:T(8,128)S(1)}, u32[]{:S(2)}, u32[]{:S(2)}) collective-permute-start(f32[32,768]{1,0:T(8,128)S(1)} %get-tuple-element.101), channel_id=1, source_target_pairs={{0,4},{4,0},{8,12},{12,8},{16,20},{20,16},{24,28},{28,24},{1,5},{5... | collective-permute-start | bytes 294920 | tf_op jit(solution)/shard_map/ppermute | solution.py:702
  75.8 13.7 %collective-permute-start.28 = (f32[32,768]{1,0:T(8,128)S(1)}, f32[32,768]{1,0:T(8,128)S(1)}, u32[]{:S(2)}, u32[]{:S(2)}) collective-permute-start(f32[32,768]{1,0:T(8,128)S(1)} %get-tuple-element.102), channel_id=1, source_target_pairs={{0,20},{4,16},{8,28},{12,24},{16,4},{20,0},{24,12},{28,8},{1,21},{... | collective-permute-start | bytes 294920 | tf_op jit(solution)/shard_map/ppermute | solution.py:702
  77.5 12.0 %collective-permute-start.29 = (f32[32,768]{1,0:T(8,128)S(1)}, f32[32,768]{1,0:T(8,128)S(1)}, u32[]{:S(2)}, u32[]{:S(2)}) collective-permute-start(f32[32,768]{1,0:T(8,128)S(1)} %get-tuple-element.103), channel_id=1, source_target_pairs={{0,8},{4,12},{8,0},{12,4},{16,24},{20,28},{24,16},{28,20},{1,9},{5... | collective-permute-start | bytes 294920 | tf_op jit(solution)/shard_map/ppermute | solution.py:702
  79.1 11.9 %collective-permute-start.30 = (f32[32,768]{1,0:T(8,128)S(1)}, f32[32,768]{1,0:T(8,128)S(1)}, u32[]{:S(2)}, u32[]{:S(2)}) collective-permute-start(f32[32,768]{1,0:T(8,128)S(1)} %get-tuple-element.104), channel_id=1, source_target_pairs={{0,24},{4,28},{8,16},{12,20},{16,8},{20,12},{24,0},{28,4},{1,25},{... | collective-permute-start | bytes 294920 | tf_op jit(solution)/shard_map/ppermute | solution.py:702
  83.5 10.6 %collective-permute-start.31 = (f32[32,768]{1,0:T(8,128)S(1)}, f32[32,768]{1,0:T(8,128)S(1)}, u32[]{:S(2)}, u32[]{:S(2)}) collective-permute-start(f32[32,768]{1,0:T(8,128)S(1)} %get-tuple-element.105), channel_id=1, source_target_pairs={{0,12},{4,8},{8,4},{12,0},{16,28},{20,24},{24,20},{28,16},{1,13},{... | collective-permute-start | bytes 294920 | tf_op jit(solution)/shard_map/ppermute | solution.py:702
  83.6 10.5 %collective-permute-start.32 = (f32[32,768]{1,0:T(8,128)S(1)}, f32[32,768]{1,0:T(8,128)S(1)}, u32[]{:S(2)}, u32[]{:S(2)}) collective-permute-start(f32[32,768]{1,0:T(8,128)S(1)} %get-tuple-element.106), channel_id=1, source_target_pairs={{0,28},{4,24},{8,20},{12,16},{16,12},{20,8},{24,4},{28,0},{1,29},{... | collective-permute-start | bytes 294920 | tf_op jit(solution)/shard_map/ppermute | solution.py:702
  89.4 11.7 %collective-permute-start.36 = (f32[32,768]{1,0:T(8,128)S(1)}, f32[32,768]{1,0:T(8,128)S(1)}, u32[]{:S(2)}, u32[]{:S(2)}) collective-permute-start(f32[32,768]{1,0:T(8,128)S(1)} %get-tuple-element.116), channel_id=1, source_target_pairs={{0,16},{4,20},{8,24},{12,28},{16,0},{20,4},{24,8},{28,12},{1,17},{... | collective-permute-start | bytes 294920 | tf_op jit(solution)/shard_map/ppermute | solution.py:702
  89.4 11.7 %collective-permute-start.37 = (f32[32,768]{1,0:T(8,128)S(1)}, f32[32,768]{1,0:T(8,128)S(1)}, u32[]{:S(2)}, u32[]{:S(2)}) collective-permute-start(f32[32,768]{1,0:T(8,128)S(1)} %get-tuple-element.117), channel_id=1, source_target_pairs={{0,4},{4,0},{8,12},{12,8},{16,20},{20,16},{24,28},{28,24},{1,5},{5... | collective-permute-start | bytes 294920 | tf_op jit(solution)/shard_map/ppermute | solution.py:702
  91.0 14.6 %collective-permute-start.38 = (f32[32,768]{1,0:T(8,128)S(1)}, f32[32,768]{1,0:T(8,128)S(1)}, u32[]{:S(2)}, u32[]{:S(2)}) collective-permute-start(f32[32,768]{1,0:T(8,128)S(1)} %get-tuple-element.118), channel_id=1, source_target_pairs={{0,20},{4,16},{8,28},{12,24},{16,4},{20,0},{24,12},{28,8},{1,21},{... | collective-permute-start | bytes 294920 | tf_op jit(solution)/shard_map/ppermute | solution.py:702
  94.1 11.5 %collective-permute-start.39 = (f32[32,768]{1,0:T(8,128)S(1)}, f32[32,768]{1,0:T(8,128)S(1)}, u32[]{:S(2)}, u32[]{:S(2)}) collective-permute-start(f32[32,768]{1,0:T(8,128)S(1)} %get-tuple-element.119), channel_id=1, source_target_pairs={{0,8},{4,12},{8,0},{12,4},{16,24},{20,28},{24,16},{28,20},{1,9},{5... | collective-permute-start | bytes 294920 | tf_op jit(solution)/shard_map/ppermute | solution.py:702
  95.8 9.8 %collective-permute-start.40 = (f32[32,768]{1,0:T(8,128)S(1)}, f32[32,768]{1,0:T(8,128)S(1)}, u32[]{:S(2)}, u32[]{:S(2)}) collective-permute-start(f32[32,768]{1,0:T(8,128)S(1)} %get-tuple-element.123), channel_id=1, source_target_pairs={{0,24},{4,28},{8,16},{12,20},{16,8},{20,12},{24,0},{28,4},{1,25},{... | collective-permute-start | bytes 294920 | tf_op jit(solution)/shard_map/ppermute | solution.py:702
  101.2 6.6 %collective-permute-start.41 = (f32[32,768]{1,0:T(8,128)S(1)}, f32[32,768]{1,0:T(8,128)S(1)}, u32[]{:S(2)}, u32[]{:S(2)}) collective-permute-start(f32[32,768]{1,0:T(8,128)S(1)} %get-tuple-element.124), channel_id=1, source_target_pairs={{0,12},{4,8},{8,4},{12,0},{16,28},{20,24},{24,20},{28,16},{1,13},{... | collective-permute-start | bytes 294920 | tf_op jit(solution)/shard_map/ppermute | solution.py:702
  101.2 8.0 %collective-permute-start.42 = (f32[32,768]{1,0:T(8,128)S(1)}, f32[32,768]{1,0:T(8,128)S(1)}, u32[]{:S(2)}, u32[]{:S(2)}) collective-permute-start(f32[32,768]{1,0:T(8,128)S(1)} %get-tuple-element.125), channel_id=1, source_target_pairs={{0,28},{4,24},{8,20},{12,16},{16,12},{20,8},{24,4},{28,0},{1,29},{... | collective-permute-start | bytes 294920 | tf_op jit(solution)/shard_map/ppermute | solution.py:702
  105.6 8.2 %collective-permute-start.33 = (f32[72,768]{1,0:T(8,128)S(1)}, f32[72,768]{1,0:T(8,128)S(1)}, u32[]{:S(2)}, u32[]{:S(2)}) collective-permute-start(f32[72,768]{1,0:T(8,128)S(1)} %get-tuple-element.108), channel_id=1, source_target_pairs={{0,2},{1,3},{2,0},{3,1},{4,6},{5,7},{6,4},{7,5},{8,10},{9,11},{10,... | collective-permute-start | bytes 663560 | tf_op jit(solution)/shard_map/ppermute | solution.py:702
  105.6 9.0 %collective-permute-start.34 = (f32[72,768]{1,0:T(8,128)S(1)}, f32[72,768]{1,0:T(8,128)S(1)}, u32[]{:S(2)}, u32[]{:S(2)}) collective-permute-start(f32[72,768]{1,0:T(8,128)S(1)} %get-tuple-element.109), channel_id=1, source_target_pairs={{0,3},{1,2},{2,1},{3,0},{4,7},{5,6},{6,5},{7,4},{8,11},{9,10},{10,... | collective-permute-start | bytes 663560 | tf_op jit(solution)/shard_map/ppermute | solution.py:702
  105.6 9.0 %collective-permute-start.35 = (f32[72,768]{1,0:T(8,128)S(1)}, f32[72,768]{1,0:T(8,128)S(1)}, u32[]{:S(2)}, u32[]{:S(2)}) collective-permute-start(f32[72,768]{1,0:T(8,128)S(1)} %get-tuple-element.110), channel_id=1, source_target_pairs={{0,1},{1,0},{2,3},{3,2},{4,5},{5,4},{6,7},{7,6},{8,9},{9,8},{10,11... | collective-permute-start | bytes 663560 | tf_op jit(solution)/shard_map/ppermute | solution.py:702
  110.9 12.0 %collective-permute-start.43 = (f32[72,768]{1,0:T(8,128)S(1)}, f32[72,768]{1,0:T(8,128)S(1)}, u32[]{:S(2)}, u32[]{:S(2)}) collective-permute-start(f32[72,768]{1,0:T(8,128)S(1)} %get-tuple-element.127), channel_id=1, source_target_pairs={{0,2},{1,3},{2,0},{3,1},{4,6},{5,7},{6,4},{7,5},{8,10},{9,11},{10,... | collective-permute-start | bytes 663560 | tf_op jit(solution)/shard_map/ppermute | solution.py:702
  113.0 10.3 %collective-permute-start.44 = (f32[72,768]{1,0:T(8,128)S(1)}, f32[72,768]{1,0:T(8,128)S(1)}, u32[]{:S(2)}, u32[]{:S(2)}) collective-permute-start(f32[72,768]{1,0:T(8,128)S(1)} %get-tuple-element.128), channel_id=1, source_target_pairs={{0,3},{1,2},{2,1},{3,0},{4,7},{5,6},{6,5},{7,4},{8,11},{9,10},{10,... | collective-permute-start | bytes 663560 | tf_op jit(solution)/shard_map/ppermute | solution.py:702
  113.9 9.4 %collective-permute-start.45 = (f32[72,768]{1,0:T(8,128)S(1)}, f32[72,768]{1,0:T(8,128)S(1)}, u32[]{:S(2)}, u32[]{:S(2)}) collective-permute-start(f32[72,768]{1,0:T(8,128)S(1)} %get-tuple-element.129), channel_id=1, source_target_pairs={{0,1},{1,0},{2,3},{3,2},{4,5},{5,4},{6,7},{7,6},{8,9},{9,8},{10,11... | collective-permute-start | bytes 663560 | tf_op jit(solution)/shard_map/ppermute | solution.py:702
  116.1 12.9 %collective-permute-start.46 = (f32[3,64,256]{2,1,0:T(8,128)S(1)}, f32[3,64,256]{2,1,0:T(8,128)S(1)}, u32[]{:S(2)}, u32[]{:S(2)}) collective-permute-start(f32[3,64,256]{2,1,0:T(8,128)S(1)} %get-tuple-element.132), channel_id=1, source_target_pairs={{0,4},{4,8},{8,12},{12,16},{16,20},{20,24},{24,28},{28,0},{1,5},{5... | collective-permute-start | bytes 589832 | tf_op jit(solution)/shard_map/ppermute | solution.py:831
  120.5 10.4 %collective-permute-start.47 = (f32[3,64,256]{2,1,0:T(8,128)S(1)}, f32[3,64,256]{2,1,0:T(8,128)S(1)}, u32[]{:S(2)}, u32[]{:S(2)}) collective-permute-start(f32[3,64,256]{2,1,0:T(8,128)S(1)} %get-tuple-element.133), channel_id=1, source_target_pairs={{0,28},{4,0},{8,4},{12,8},{16,12},{20,16},{24,20},{28,24},{1,29},{... | collective-permute-start | bytes 589832 | tf_op jit(solution)/shard_map/ppermute | solution.py:830
  (9 other events, 80.1 us)

commit v13 on v12

--- a/solution.py
+++ b/solution.py
@@ -142,11 +142,11 @@
     return plus + minus
 
 
-def offset_order(count, near_first=False):
+def offset_order(count, first=None):
     far, near = list(range(count // 2, count)), list(range(1, count // 2))
-    if near_first:
+    if first == "near":
         return [0] + near + far
-    if count == 4:
+    if first == "far":
         return [0] + far + near
     order = [0]
     while far or near:
@@ -155,14 +155,14 @@
     return order
 
 
-def blocks_of(refs, at, near_first=False):
+def blocks_of(refs, at, first=None):
     if len(refs) == 1:
         return [(d, refs[0].at[d]) for d in range(refs[0].shape[0])]
-    return [(at ^ k, ref) for k, ref in zip(offset_order(len(refs), near_first), refs)]
-
-
-def gather_blocks(refs, held, at, near_first=False):
-    for d, ref in blocks_of(refs, at, near_first):
+    return [(at ^ k, ref) for k, ref in zip(offset_order(len(refs), first), refs)]
+
+
+def gather_blocks(refs, held, at, first=None):
+    for d, ref in blocks_of(refs, at, first):
         held[d] = ref[...]
 
 
@@ -188,7 +188,7 @@
 
 
 def deposit_kernel(
-    pairs, rims_before, near_first, place, own, up1, down1, up2, down2, ambient, t_high, t_low, *refs
+    pairs, rims_before, first, place, own, up1, down1, up2, down2, ambient, t_high, t_low, *refs
 ):
     rims, refs = refs[:rims_before], refs[rims_before:]
     mesh, rim_high, rim_low = refs[:3]
@@ -273,14 +273,14 @@
             made[g, :, n * LANES : (n + 1) * LANES] = wide[
                 n * rows : (n + 1) * rows, g * LANES : (g + 1) * LANES
             ]
-    for d, out in blocks_of(outs, place[1], near_first):
+    for d, out in blocks_of(outs, place[1], first):
         out[...] = made[d]
 
 
-def x_ahead_kernel(sends, near_first, place, t_high, t_low, *refs):
+def x_ahead_kernel(sends, first, place, t_high, t_low, *refs):
     held, made = refs[-2:]
     outs, parts = refs[-2 - sends : -2], refs[: -2 - sends]
-    gather_blocks(parts, held, place[1], near_first)
+    gather_blocks(parts, held, place[1], first)
     pencils, rows, width = held.shape
     cols = rows - RIM
     row = lax.broadcasted_iota(jnp.int32, (RIM, width), 0)
@@ -301,7 +301,7 @@
         out[...] = made[d]
 
 
-def x_back_kernel(sends, tables, place, *refs):
+def x_back_kernel(sends, first, tables, place, *refs):
     held, made = refs[-2:]
     outs, parts = refs[-2 - sends : -2], refs[: -2 - sends]
     gather_blocks(parts, held, place[0])
@@ -312,7 +312,7 @@
         lanes = slice(n * LANES, (n + 1) * LANES)
         value = both[:half, lanes] + times_i(both[half:, lanes])
         made[:, :, lanes] = value.reshape(pencils, rows, LANES)
-    for d, out in blocks_of(outs, place[1]):
+    for d, out in blocks_of(outs, place[1], first):
         out[...] = made[d]
 
 
@@ -624,7 +624,7 @@
                 send(talls[n].at[:, i, pl.ds(RIM, cols)], velocity.at[:, z])
 
     send_velocity(0)
-    gather_blocks(refs[:-6], held, place[1])
+    gather_blocks(refs[:-6], held, place[1], "far")
     for (c, z), value in planes_of(held, chunks[1], tables).items():
         hold(inner, c, spot[z][1], value)
     send_velocity(1)
@@ -694,13 +694,13 @@
     return [(count, rows, width)] if whole or not spread(axis) else [(rows, width)] * count
 
 
-def exchange(blocks, axis, start=0, near_first=False):
+def exchange(blocks, axis, start=0, first=None):
     if not spread(axis):
         return [lax.all_to_all(blocks[0], axis, split_axis=0, concat_axis=0, tiled=True)]
     count = lax.axis_size(axis)
     return [
         lax.ppermute(block, axis, [(i, i ^ k) for i in range(count)]) if k else block
-        for k, block in zip(offset_order(count, near_first)[start:], blocks)
+        for k, block in zip(offset_order(count, first)[start:], blocks)
     ]
 
 
@@ -744,7 +744,7 @@
         size = 2 * len(chunk)
         rim = (6 * size + (rims[0].shape[0] if rims else 0), ny)
         mesh, rim_high, rim_low, *part = call(
-            functools.partial(deposit_kernel, chunk, len(rims), n == 0),
+            functools.partial(deposit_kernel, chunk, len(rims), None if n else "near"),
             [here]
             + [(VM, value) for value in (packet, up1, down1, up2, down2)]
             + [(VM, ambient), (VM, y_ahead[0]), (VM, y_ahead[1])]
@@ -756,7 +756,7 @@
         )
         meshes[n] = mesh
         rims = [rim_high, rim_low]
-        parts[n] = exchange(part, "gx", near_first=n == 0)
+        parts[n] = exchange(part, "gx", first="near" if n == 0 else None)
     low_rim = lax.ppermute(rims[0], "gx", ring("gx", 1))
     high_rim = lax.ppermute(rims[1], "gx", ring("gx", -1))
 
@@ -766,7 +766,7 @@
         chunk, part, width = chunks[n], parts[n], widths[n]
         shapes = sent_shapes("gz", block, width)
         part = call(
-            functools.partial(x_ahead_kernel, len(shapes), n == 0),
+            functools.partial(x_ahead_kernel, len(shapes), None if n else "near"),
             [here, (VM, x_ahead[0]), (VM, x_ahead[1])] + [(VM, p) for p in part],
             [(VM, shape) for shape in shapes],
             [((pencils, rows, width), F32), ((slabs, block, width), F32)],
@@ -797,17 +797,17 @@
         for chunk, source, width in zip(chunks, data, widths)
     ]
 
-    def back(part, width):
+    def back(part, width, first=None):
         shapes = sent_shapes("gx", rows, width)
         part = call(
-            loaded(functools.partial(x_back_kernel, len(shapes))),
+            loaded(functools.partial(x_back_kernel, len(shapes), first)),
             [here]
             + [(VM, t) for t in x_back]
             + [(VM, p) for p in part],
             [(VM, shape) for shape in shapes],
             [((slabs, block, width), F32), ((pencils, rows, width), F32)],
         )
-        return exchange(part, "gx")
+        return exchange(part, "gx", first=first)
 
     early = max(1, len(left[1]) - LATE)
     second = exchange(left[1][:early], "gz")
@@ -826,7 +826,7 @@
             micros=0.3,
         )
         second += exchange(late, "gz", early)
-    parts.append(back(second, widths[1]))
+    parts.append(back(second, widths[1], "far"))
     after = lax.ppermute(first, "gz", ring("gz", -1))
     before = lax.ppermute(last, "gz", ring("gz", 1))
     velocity, vorticity = call(

time: 132 us -> 132 us (level)
  no operation moved by 1% of the time
where the time goes in v13:
time: 132 us
  starting transfers between devices  72.9 us (55%)
  Pallas kernels  30.6 us (23%)
  waiting for transfers between devices  27.3 us (21%)
    ppermute x40, starting transfers between devices, exchange(): lax.ppermute(block, axis, [(i, i ^ k) for i in range(count)])  56.4 us
    pallas_call x16, Pallas kernels, call(): pl.pallas_call(kernel, out_shape=[jax.ShapeDtypeStruct(shape, F32) for _,...  30.6 us
    ppermute x40, waiting for transfers between devices, exchange(): lax.ppermute(block, axis, [(i, i ^ k) for i in range(count)])  21.2 us
    ppermute x1, starting transfers between devices, on_device(): before = lax.ppermute(last, 'gz', ring('gz', 1))  4.4 us
    ppermute x1, starting transfers between devices, on_device(): down2 = lax.ppermute(movers, 'gz', ring('gz', 2))  3.08 us
    ppermute x1, starting transfers between devices, on_device(): up1 = lax.ppermute(packet, 'gz', ring('gz', -1))  3.08 us
    ppermute x1, waiting for transfers between devices, on_device(): before = lax.ppermute(last, 'gz', ring('gz', 1))  2.82 us
  transfers between devices with their start and end apart: 48, of which 16 were waited for; matrix products, arithmetic and copies ran while one was open for 0% of the time, Pallas kernels for 16%

profile of v13, /device:TPU:0, one launch (start us, length us, event | category | flops | bytes accessed | tf_op | source)
XLA Modules:
  0.0 132.0 jit_solution(5237047344027729662)
XLA Ops:
  1.8 3.1 %collective-permute-start.3 = (f32[8,128]{1,0:T(8,128)S(1)}, f32[8,128]{1,0:T(8,128)S(1)}, u32[]{:S(2)}, u32[]{:S(2)}) collective-permute-start(f32[8,128]{1,0:T(8,128)S(1)} %get-tuple-element.69), channel_id=1, source_target_pairs={{0,8},{4,12},{8,16},{12,20},{16,24},{20,28},{24,0},{28,4},{1,9},{5... | collective-permute-start | bytes 12296 | tf_op jit(solution)/shard_map/ppermute | solution.py:739
  4.8 2.1 %collective-permute-start.2 = (f32[8,128]{1,0:T(8,128)S(1)}, f32[8,128]{1,0:T(8,128)S(1)}, u32[]{:S(2)}, u32[]{:S(2)}) collective-permute-start(f32[8,128]{1,0:T(8,128)S(1)} %get-tuple-element.69), channel_id=1, source_target_pairs={{0,24},{4,28},{8,0},{12,4},{16,8},{20,12},{24,16},{28,20},{1,25},{... | collective-permute-start | bytes 12296 | tf_op jit(solution)/shard_map/ppermute | solution.py:738
  6.9 1.6 %collective-permute-start.1 = (f32[8,512]{1,0:T(8,128)S(1)}, f32[8,512]{1,0:T(8,128)S(1)}, u32[]{:S(2)}, u32[]{:S(2)}) collective-permute-start(f32[8,512]{1,0:T(8,128)S(1)} %get-tuple-element.68.own), channel_id=1, source_target_pairs={{0,4},{4,8},{8,12},{12,16},{16,20},{20,24},{24,28},{28,0},{1,5},{5... | collective-permute-start | bytes 49160 | tf_op jit(solution)/shard_map/ppermute | solution.py:737
  8.6 3.1 %collective-permute-start = (f32[8,512]{1,0:T(8,128)S(1)}, f32[8,512]{1,0:T(8,128)S(1)}, u32[]{:S(2)}, u32[]{:S(2)}) collective-permute-start(f32[8,512]{1,0:T(8,128)S(1)} %get-tuple-element.68.own), channel_id=1, source_target_pairs={{0,28},{4,0},{8,4},{12,8},{16,12},{20,16},{24,20},{28,24},{1,29},{... | collective-permute-start | bytes 49160 | tf_op jit(solution)/shard_map/ppermute | solution.py:736
  11.7 1.6 %collective-permute-done.1.down1 = f32[8,512]{1,0:T(8,128)S(1)} collective-permute-done((f32[8,512]{1,0:T(8,128)S(1)}, f32[8,512]{1,0:T(8,128)S(1)}, u32[]{:S(2)}, u32[]{:S(2)}) %collective-permute-start.1) | collective-permute-done | bytes 16416 | tf_op jit(solution)/shard_map/ppermute | solution.py:737
  13.4 3.7 %shard_map.141 = (f32[3,4,64,256]{3,2,1,0:T(8,128)S(1)}, f32[24,256]{1,0:T(8,128)S(1)}, f32[24,256]{1,0:T(8,128)S(1)}, f32[72,768]{1,0:T(8,128)S(1)}, f32[72,768...) custom-call(s32[2]{0:T(128)S(1)} %pad_add_fusion.place, f32[8,512]{1,0:T(8,128)S(1)} %get-tuple-element.68.own, ...), custom_call_target="tpu_custom_call" | custom-call | flops 5000000000 | bytes 15000000 | tf_op jit(solution)/shard_map/pallas_call | solution.py:666
  17.1 1.7 %collective-permute-start.16 = (f32[72,768]{1,0:T(8,128)S(1)}, f32[72,768]{1,0:T(8,128)S(1)}, u32[]{:S(2)}, u32[]{:S(2)}) collective-permute-start(f32[72,768]{1,0:T(8,128)S(1)} %get-tuple-element.87), channel_id=1, source_target_pairs={{0,2},{1,3},{2,0},{3,1},{4,6},{5,7},{6,4},{7,5},{8,10},{9,11},{10,... | collective-permute-start | bytes 663560 | tf_op jit(solution)/shard_map/ppermute | solution.py:702
  19.3 6.0 %shard_map.142 = (f32[3,4,64,256]{3,2,1,0:T(8,128)S(1)}, f32[48,256]{1,0:T(8,128)S(1)}, f32[48,256]{1,0:T(8,128)S(1)}, f32[72,768]{1,0:T(8,128)S(1)}, f32[72,768...) custom-call(s32[2]{0:T(128)S(1)} %pad_add_fusion.place, f32[8,512]{1,0:T(8,128)S(1)} %get-tuple-element.68.own, ...), custom_call_target="tpu_custom_call" | custom-call | flops 5000000000 | bytes 15000000 | tf_op jit(solution)/shard_map/pallas_call | solution.py:666
  25.4 1.7 %collective-permute-start.7 = (f32[72,768]{1,0:T(8,128)S(1)}, f32[72,768]{1,0:T(8,128)S(1)}, u32[]{:S(2)}, u32[]{:S(2)}) collective-permute-start(f32[72,768]{1,0:T(8,128)S(1)} %get-tuple-element.76), channel_id=1, source_target_pairs={{0,2},{1,3},{2,0},{3,1},{4,6},{5,7},{6,4},{7,5},{8,10},{9,11},{10,... | collective-permute-start | bytes 663560 | tf_op jit(solution)/shard_map/ppermute | solution.py:702
  27.2 1.6 %shard_map.145 = (f32[32,768]{1,0:T(8,128)S(1)}, f32[32,768]{1,0:T(8,128)S(1)}, f32[32,768]{1,0:T(8,128)S(1)}, f32[32,768]{1,0:T(8,128)S(1)}, f32[32,768]{1,0:T(...) custom-call(s32[2]{0:T(128)S(1)} %pad_add_fusion.place, ...), custom_call_target="tpu_custom_call" | custom-call | flops 2000000000 | bytes 6000000 | tf_op jit(solution)/shard_map/pallas_call | solution.py:666
  28.9 2.2 %collective-permute-start.20 = (f32[32,768]{1,0:T(8,128)S(1)}, f32[32,768]{1,0:T(8,128)S(1)}, u32[]{:S(2)}, u32[]{:S(2)}) collective-permute-start(f32[32,768]{1,0:T(8,128)S(1)} %get-tuple-element.92), channel_id=1, source_target_pairs={{0,4},{4,0},{8,12},{12,8},{16,20},{20,16},{24,28},{28,24},{1,5},{5... | collective-permute-start | bytes 294920 | tf_op jit(solution)/shard_map/ppermute | solution.py:702
  31.1 2.2 %collective-permute-start.21 = (f32[32,768]{1,0:T(8,128)S(1)}, f32[32,768]{1,0:T(8,128)S(1)}, u32[]{:S(2)}, u32[]{:S(2)}) collective-permute-start(f32[32,768]{1,0:T(8,128)S(1)} %get-tuple-element.93), channel_id=1, source_target_pairs={{0,20},{4,16},{8,28},{12,24},{16,4},{20,0},{24,12},{28,8},{1,21},{... | collective-permute-start | bytes 294920 | tf_op jit(solution)/shard_map/ppermute | solution.py:702
  34.8 2.6 %collective-permute-done.8.refs_3_ = f32[72,768]{1,0:T(8,128)S(1)} collective-permute-done((f32[72,768]{1,0:T(8,128)S(1)}, f32[72,768]{1,0:T(8,128)S(1)}, u32[]{:S(2)}, u32[]{:S(2)}) %collective-permute-start.8) | collective-permute-done | bytes 221216 | tf_op jit(solution)/shard_map/ppermute | solution.py:702
  38.2 1.6 %shard_map.143 = (f32[32,768]{1,0:T(8,128)S(1)}, f32[32,768]{1,0:T(8,128)S(1)}, f32[32,768]{1,0:T(8,128)S(1)}, f32[32,768]{1,0:T(8,128)S(1)}, f32[32,768]{1,0:T(...) custom-call(s32[2]{0:T(128)S(1)} %pad_add_fusion.place, ...), custom_call_target="tpu_custom_call" | custom-call | flops 2000000000 | bytes 6000000 | tf_op jit(solution)/shard_map/pallas_call | solution.py:666
  39.8 1.5 %collective-permute-start.24 = (f32[32,768]{1,0:T(8,128)S(1)}, f32[32,768]{1,0:T(8,128)S(1)}, u32[]{:S(2)}, u32[]{:S(2)}) collective-permute-start(f32[32,768]{1,0:T(8,128)S(1)} %get-tuple-element.96), channel_id=1, source_target_pairs={{0,12},{4,8},{8,4},{12,0},{16,28},{20,24},{24,20},{28,16},{1,13},{... | collective-permute-start | bytes 294920 | tf_op jit(solution)/shard_map/ppermute | solution.py:702
  41.3 2.6 %collective-permute-start.25 = (f32[32,768]{1,0:T(8,128)S(1)}, f32[32,768]{1,0:T(8,128)S(1)}, u32[]{:S(2)}, u32[]{:S(2)}) collective-permute-start(f32[32,768]{1,0:T(8,128)S(1)} %get-tuple-element.97), channel_id=1, source_target_pairs={{0,28},{4,24},{8,20},{12,16},{16,12},{20,8},{24,4},{28,0},{1,29},{... | collective-permute-start | bytes 294920 | tf_op jit(solution)/shard_map/ppermute | solution.py:702
  44.5 4.3 %collective-permute-start.10 = (f32[32,768]{1,0:T(8,128)S(1)}, f32[32,768]{1,0:T(8,128)S(1)}, u32[]{:S(2)}, u32[]{:S(2)}) collective-permute-start(f32[32,768]{1,0:T(8,128)S(1)} %get-tuple-element.80), channel_id=1, source_target_pairs={{0,4},{4,0},{8,12},{12,8},{16,20},{20,16},{24,28},{28,24},{1,5},{5... | collective-permute-start | bytes 294920 | tf_op jit(solution)/shard_map/ppermute | solution.py:702
  48.8 3.2 %collective-permute-start.12 = (f32[32,768]{1,0:T(8,128)S(1)}, f32[32,768]{1,0:T(8,128)S(1)}, u32[]{:S(2)}, u32[]{:S(2)}) collective-permute-start(f32[32,768]{1,0:T(8,128)S(1)} %get-tuple-element.82), channel_id=1, source_target_pairs={{0,8},{4,12},{8,0},{12,4},{16,24},{20,28},{24,16},{28,20},{1,9},{5... | collective-permute-start | bytes 294920 | tf_op jit(solution)/shard_map/ppermute | solution.py:702
  52.1 1.8 %collective-permute-start.13 = (f32[32,768]{1,0:T(8,128)S(1)}, f32[32,768]{1,0:T(8,128)S(1)}, u32[]{:S(2)}, u32[]{:S(2)}) collective-permute-start(f32[32,768]{1,0:T(8,128)S(1)} %get-tuple-element.83), channel_id=1, source_target_pairs={{0,24},{4,28},{8,16},{12,20},{16,8},{20,12},{24,0},{28,4},{1,25},{... | collective-permute-start | bytes 294920 | tf_op jit(solution)/shard_map/ppermute | solution.py:702
  53.9 3.5 %collective-permute-done.9.refs_1_ = f32[32,768]{1,0:T(8,128)S(1)} collective-permute-done((f32[32,768]{1,0:T(8,128)S(1)}, f32[32,768]{1,0:T(8,128)S(1)}, u32[]{:S(2)}, u32[]{:S(2)}) %collective-permute-start.9) | collective-permute-done | bytes 98336 | tf_op jit(solution)/shard_map/ppermute | solution.py:702
  57.4 2.0 %collective-permute-start.14 = (f32[32,768]{1,0:T(8,128)S(1)}, f32[32,768]{1,0:T(8,128)S(1)}, u32[]{:S(2)}, u32[]{:S(2)}) collective-permute-start(f32[32,768]{1,0:T(8,128)S(1)} %get-tuple-element.84), channel_id=1, source_target_pairs={{0,12},{4,8},{8,4},{12,0},{16,28},{20,24},{24,20},{28,16},{1,13},{... | collective-permute-start | bytes 294920 | tf_op jit(solution)/shard_map/ppermute | solution.py:702
  59.4 3.0 %collective-permute-start.15 = (f32[32,768]{1,0:T(8,128)S(1)}, f32[32,768]{1,0:T(8,128)S(1)}, u32[]{:S(2)}, u32[]{:S(2)}) collective-permute-start(f32[32,768]{1,0:T(8,128)S(1)} %get-tuple-element.85), channel_id=1, source_target_pairs={{0,28},{4,24},{8,20},{12,16},{16,12},{20,8},{24,4},{28,0},{1,29},{... | collective-permute-start | bytes 294920 | tf_op jit(solution)/shard_map/ppermute | solution.py:702
  63.8 1.7 %collective-permute-start.5 = (f32[48,256]{1,0:T(8,128)S(1)}, f32[48,256]{1,0:T(8,128)S(1)}, u32[]{:S(2)}, u32[]{:S(2)}) collective-permute-start(f32[48,256]{1,0:T(8,128)S(1)} %get-tuple-element.73), channel_id=1, source_target_pairs={{0,3},{1,0},{2,1},{3,2},{4,7},{5,4},{6,5},{7,6},{8,11},{9,8},{10,9... | collective-permute-start | bytes 147464 | tf_op jit(solution)/shard_map/ppermute | solution.py:761
  65.6 2.3 %collective-permute-done.14.refs_6_ = f32[32,768]{1,0:T(8,128)S(1)} collective-permute-done((f32[32,768]{1,0:T(8,128)S(1)}, f32[32,768]{1,0:T(8,128)S(1)}, u32[]{:S(2)}, u32[]{:S(2)}) %collective-permute-start.14) | collective-permute-done | bytes 98336 | tf_op jit(solution)/shard_map/ppermute | solution.py:702
  69.3 2.3 %shard_map.147 = (f32[3,2,4,8,8,128]{5,4,3,2,1,0:T(8,128)S(1)}, f32[3,2,4,8,8,128]{5,4,3,2,1,0:T(8,128)S(1)}) custom-call(s32[2]{0:T(128)S(1)} %pad_add_fusion.place, f32[48,256]{1,0:T(8,128)S(1)} %collective-permute-done.4.low_rim.refs_1_, f32[48,256]{1,0:T(8,128)S(1)} %collective-permute-done.5.high_rim.refs_2_, ...), custom_call_target="tpu_custom_call" | custom-call | flops 5000000000 | bytes 15000000 | tf_op jit(solution)/shard_map/pallas_call | solution.py:666
  73.0 1.8 %collective-permute-start.26 = (f32[32,768]{1,0:T(8,128)S(1)}, f32[32,768]{1,0:T(8,128)S(1)}, u32[]{:S(2)}, u32[]{:S(2)}) collective-permute-start(f32[32,768]{1,0:T(8,128)S(1)} %get-tuple-element.100), channel_id=1, source_target_pairs={{0,16},{4,20},{8,24},{12,28},{16,0},{20,4},{24,8},{28,12},{1,17},{... | collective-permute-start | bytes 294920 | tf_op jit(solution)/shard_map/ppermute | solution.py:702
  75.8 1.7 %collective-permute-start.28 = (f32[32,768]{1,0:T(8,128)S(1)}, f32[32,768]{1,0:T(8,128)S(1)}, u32[]{:S(2)}, u32[]{:S(2)}) collective-permute-start(f32[32,768]{1,0:T(8,128)S(1)} %get-tuple-element.102), channel_id=1, source_target_pairs={{0,20},{4,16},{8,28},{12,24},{16,4},{20,0},{24,12},{28,8},{1,21},{... | collective-permute-start | bytes 294920 | tf_op jit(solution)/shard_map/ppermute | solution.py:702
  77.5 1.7 %collective-permute-start.29 = (f32[32,768]{1,0:T(8,128)S(1)}, f32[32,768]{1,0:T(8,128)S(1)}, u32[]{:S(2)}, u32[]{:S(2)}) collective-permute-start(f32[32,768]{1,0:T(8,128)S(1)} %get-tuple-element.103), channel_id=1, source_target_pairs={{0,8},{4,12},{8,0},{12,4},{16,24},{20,28},{24,16},{28,20},{1,9},{5... | collective-permute-start | bytes 294920 | tf_op jit(solution)/shard_map/ppermute | solution.py:702
  79.1 1.5 %collective-permute-start.30 = (f32[32,768]{1,0:T(8,128)S(1)}, f32[32,768]{1,0:T(8,128)S(1)}, u32[]{:S(2)}, u32[]{:S(2)}) collective-permute-start(f32[32,768]{1,0:T(8,128)S(1)} %get-tuple-element.104), channel_id=1, source_target_pairs={{0,24},{4,28},{8,16},{12,20},{16,8},{20,12},{24,0},{28,4},{1,25},{... | collective-permute-start | bytes 294920 | tf_op jit(solution)/shard_map/ppermute | solution.py:702
  80.7 2.8 %collective-permute-done.26.refs_1_ = f32[32,768]{1,0:T(8,128)S(1)} collective-permute-done((f32[32,768]{1,0:T(8,128)S(1)}, f32[32,768]{1,0:T(8,128)S(1)}, u32[]{:S(2)}, u32[]{:S(2)}) %collective-permute-start.26) | collective-permute-done | bytes 98336 | tf_op jit(solution)/shard_map/ppermute | solution.py:702
  83.6 3.0 %collective-permute-start.32 = (f32[32,768]{1,0:T(8,128)S(1)}, f32[32,768]{1,0:T(8,128)S(1)}, u32[]{:S(2)}, u32[]{:S(2)}) collective-permute-start(f32[32,768]{1,0:T(8,128)S(1)} %get-tuple-element.106), channel_id=1, source_target_pairs={{0,28},{4,24},{8,20},{12,16},{16,12},{20,8},{24,4},{28,0},{1,29},{... | collective-permute-start | bytes 294920 | tf_op jit(solution)/shard_map/ppermute | solution.py:702
  88.0 1.4 %collective-permute-done.28.refs_3_ = f32[32,768]{1,0:T(8,128)S(1)} collective-permute-done((f32[32,768]{1,0:T(8,128)S(1)}, f32[32,768]{1,0:T(8,128)S(1)}, u32[]{:S(2)}, u32[]{:S(2)}) %collective-permute-start.28) | collective-permute-done | bytes 98336 | tf_op jit(solution)/shard_map/ppermute | solution.py:702
  89.4 1.6 %collective-permute-start.37 = (f32[32,768]{1,0:T(8,128)S(1)}, f32[32,768]{1,0:T(8,128)S(1)}, u32[]{:S(2)}, u32[]{:S(2)}) collective-permute-start(f32[32,768]{1,0:T(8,128)S(1)} %get-tuple-element.117), channel_id=1, source_target_pairs={{0,4},{4,0},{8,12},{12,8},{16,20},{20,16},{24,28},{28,24},{1,5},{5... | collective-permute-start | bytes 294920 | tf_op jit(solution)/shard_map/ppermute | solution.py:702
  91.0 3.1 %collective-permute-start.38 = (f32[32,768]{1,0:T(8,128)S(1)}, f32[32,768]{1,0:T(8,128)S(1)}, u32[]{:S(2)}, u32[]{:S(2)}) collective-permute-start(f32[32,768]{1,0:T(8,128)S(1)} %get-tuple-element.118), channel_id=1, source_target_pairs={{0,20},{4,16},{8,28},{12,24},{16,4},{20,0},{24,12},{28,8},{1,21},{... | collective-permute-start | bytes 294920 | tf_op jit(solution)/shard_map/ppermute | solution.py:702
  94.1 1.7 %shard_map.149 = (f32[72,768]{1,0:T(8,128)S(1)}, f32[72,768]{1,0:T(8,128)S(1)}, f32[72,768]{1,0:T(8,128)S(1)}, f32[72,768]{1,0:T(8,128)S(1)}) custom-call(s32[2]{0:T(128)S(1)} %pad_add_fusion.place, bf16[576,256]{1,0:T(8,128)(2,1)S(1)} %copy-done.6, bf16[576,256]{1,0:T(8,128)(2,1)S(1)} %copy-done.5, f32[32,768]{1,0:T(8,128)S(1)} %get-tuple-element.99.refs_0_, ...), custom_call_target="tpu_custom_call" | custom-call | flops 2000000000 | bytes 6000000 | tf_op jit(solution)/shard_map/pallas_call | solution.py:666
  95.8 2.9 %collective-permute-start.40 = (f32[32,768]{1,0:T(8,128)S(1)}, f32[32,768]{1,0:T(8,128)S(1)}, u32[]{:S(2)}, u32[]{:S(2)}) collective-permute-start(f32[32,768]{1,0:T(8,128)S(1)} %get-tuple-element.123), channel_id=1, source_target_pairs={{0,24},{4,28},{8,16},{12,20},{16,8},{20,12},{24,0},{28,4},{1,25},{... | collective-permute-start | bytes 294920 | tf_op jit(solution)/shard_map/ppermute | solution.py:702
  98.7 2.4 %collective-permute-done.36.refs_1_ = f32[32,768]{1,0:T(8,128)S(1)} collective-permute-done((f32[32,768]{1,0:T(8,128)S(1)}, f32[32,768]{1,0:T(8,128)S(1)}, u32[]{:S(2)}, u32[]{:S(2)}) %collective-permute-start.36) | collective-permute-done | bytes 98336 | tf_op jit(solution)/shard_map/ppermute | solution.py:702
  101.2 4.3 %collective-permute-start.42 = (f32[32,768]{1,0:T(8,128)S(1)}, f32[32,768]{1,0:T(8,128)S(1)}, u32[]{:S(2)}, u32[]{:S(2)}) collective-permute-start(f32[32,768]{1,0:T(8,128)S(1)} %get-tuple-element.125), channel_id=1, source_target_pairs={{0,28},{4,24},{8,20},{12,16},{16,12},{20,8},{24,4},{28,0},{1,29},{... | collective-permute-start | bytes 294920 | tf_op jit(solution)/shard_map/ppermute | solution.py:702
  105.6 2.1 %collective-permute-start.35 = (f32[72,768]{1,0:T(8,128)S(1)}, f32[72,768]{1,0:T(8,128)S(1)}, u32[]{:S(2)}, u32[]{:S(2)}) collective-permute-start(f32[72,768]{1,0:T(8,128)S(1)} %get-tuple-element.110), channel_id=1, source_target_pairs={{0,3},{1,2},{2,1},{3,0},{4,7},{5,6},{6,5},{7,4},{8,11},{9,10},{10,... | collective-permute-start | bytes 663560 | tf_op jit(solution)/shard_map/ppermute | solution.py:702
  107.8 1.4 %collective-permute-done.42.refs_7_ = f32[32,768]{1,0:T(8,128)S(1)} collective-permute-done((f32[32,768]{1,0:T(8,128)S(1)}, f32[32,768]{1,0:T(8,128)S(1)}, u32[]{:S(2)}, u32[]{:S(2)}) %collective-permute-start.42) | collective-permute-done | bytes 98336 | tf_op jit(solution)/shard_map/ppermute | solution.py:702
  109.2 1.7 %shard_map.153 = (f32[72,768]{1,0:T(8,128)S(1)}, f32[72,768]{1,0:T(8,128)S(1)}, f32[72,768]{1,0:T(8,128)S(1)}, f32[72,768]{1,0:T(8,128)S(1)}) custom-call(s32[2]{0:T(128)S(1)} %pad_add_fusion.place, bf16[576,256]{1,0:T(8,128)(2,1)S(1)} %copy-done.6, bf16[576,256]{1,0:T(8,128)(2,1)S(1)} %copy-done.5, f32[32,768]{1,0:T(8,128)S(1)} %get-tuple-element.115.refs_0_, ...), custom_call_target="tpu_custom_call" | custom-call | flops 2000000000 | bytes 6000000 | tf_op jit(solution)/shard_map/pallas_call | solution.py:666
  110.9 2.1 %collective-permute-start.43 = (f32[72,768]{1,0:T(8,128)S(1)}, f32[72,768]{1,0:T(8,128)S(1)}, u32[]{:S(2)}, u32[]{:S(2)}) collective-permute-start(f32[72,768]{1,0:T(8,128)S(1)} %get-tuple-element.127), channel_id=1, source_target_pairs={{0,2},{1,3},{2,0},{3,1},{4,6},{5,7},{6,4},{7,5},{8,10},{9,11},{10,... | collective-permute-start | bytes 663560 | tf_op jit(solution)/shard_map/ppermute | solution.py:702
  114.6 1.5 %shard_map.150 = (f32[3,4,80,256]{3,2,1,0:T(8,128)S(1)}, f32[3,64,256]{2,1,0:T(8,128)S(1)}, f32[3,64,256]{2,1,0:T(8,128)S(1)}) custom-call(s32[2]{0:T(128)S(1)} %pad_add_fusion.place, bf16[512,512]{1,0:T(8,128)(2,1)S(1)} %copy-done.2, bf16[512,512]{1,0:T(8,128)(2,1)S(1)} %copy-done.1, f32[72,768]{1,0:T(8,128)S(1)} %get-tuple-element.107.refs_0_.before, ...), custom_call_target="tpu_custom_call" | custom-call | flops 2000000000 | bytes 6000000 | tf_op jit(solution)/shard_map/pallas_call | solution.py:666
  116.1 4.4 %collective-permute-start.46 = (f32[3,64,256]{2,1,0:T(8,128)S(1)}, f32[3,64,256]{2,1,0:T(8,128)S(1)}, u32[]{:S(2)}, u32[]{:S(2)}) collective-permute-start(f32[3,64,256]{2,1,0:T(8,128)S(1)} %get-tuple-element.132), channel_id=1, source_target_pairs={{0,4},{4,8},{8,12},{12,16},{16,20},{20,24},{24,28},{28,0},{1,5},{5... | collective-permute-start | bytes 589832 | tf_op jit(solution)/shard_map/ppermute | solution.py:831
  120.8 2.4 %collective-permute-done.43.refs_6_ = f32[72,768]{1,0:T(8,128)S(1)} collective-permute-done((f32[72,768]{1,0:T(8,128)S(1)}, f32[72,768]{1,0:T(8,128)S(1)}, u32[]{:S(2)}, u32[]{:S(2)}) %collective-permute-start.43) | collective-permute-done | bytes 221216 | tf_op jit(solution)/shard_map/ppermute | solution.py:702
  123.3 3.0 %shard_map.154 = (f32[3,8,64,256]{3,2,1,0:T(8,128)}, f32[3,8,64,256]{3,2,1,0:T(8,128)}) custom-call(s32[2]{0:T(128)S(1)} %pad_add_fusion.place, bf16[512,512]{1,0:T(8,128)(2,1)S(1)} %copy-done.2, bf16[512,512]{1,0:T(8,128)(2,1)S(1)} %copy-done.1, f32[3,4,80,256]{3,2,1,0:T(8,128)S(1)} %get-tuple-element.111.refs_0_.edges, ...), custom_call_target="tpu_custom_call" | custom-call | flops 4000000000 | bytes 12000000 | tf_op jit(solution)/shard_map/pallas_call | solution.py:666
  126.3 2.8 %collective-permute-done.46.before = f32[3,64,256]{2,1,0:T(8,128)S(1)} collective-permute-done((f32[3,64,256]{2,1,0:T(8,128)S(1)}, f32[3,64,256]{2,1,0:T(8,128)S(1)}, u32[]{:S(2)}, u32[]{:S(2)}) %collective-permute-start.46) | collective-permute-done | bytes 196640 | tf_op jit(solution)/shard_map/ppermute | solution.py:831
  129.1 1.7 %collective-permute-done.47.after = f32[3,64,256]{2,1,0:T(8,128)S(1)} collective-permute-done((f32[3,64,256]{2,1,0:T(8,128)S(1)}, f32[3,64,256]{2,1,0:T(8,128)S(1)}, u32[]{:S(2)}, u32[]{:S(2)}) %collective-permute-start.47) | collective-permute-done | bytes 196640 | tf_op jit(solution)/shard_map/ppermute | solution.py:830
  (83 shorter events, 14.8 us)
Async XLA Ops:
  1.8 10.0 %collective-permute-start.3 = (f32[8,128]{1,0:T(8,128)S(1)}, f32[8,128]{1,0:T(8,128)S(1)}, u32[]{:S(2)}, u32[]{:S(2)}) collective-permute-start(f32[8,128]{1,0:T(8,128)S(1)} %get-tuple-element.69), channel_id=1, source_target_pairs={{0,8},{4,12},{8,16},{12,20},{16,24},{20,28},{24,0},{28,4},{1,9},{5... | collective-permute-start | bytes 12296 | tf_op jit(solution)/shard_map/ppermute | solution.py:739
  4.8 6.9 %collective-permute-start.2 = (f32[8,128]{1,0:T(8,128)S(1)}, f32[8,128]{1,0:T(8,128)S(1)}, u32[]{:S(2)}, u32[]{:S(2)}) collective-permute-start(f32[8,128]{1,0:T(8,128)S(1)} %get-tuple-element.69), channel_id=1, source_target_pairs={{0,24},{4,28},{8,0},{12,4},{16,8},{20,12},{24,16},{28,20},{1,25},{... | collective-permute-start | bytes 12296 | tf_op jit(solution)/shard_map/ppermute | solution.py:738
  6.9 6.4 %collective-permute-start.1 = (f32[8,512]{1,0:T(8,128)S(1)}, f32[8,512]{1,0:T(8,128)S(1)}, u32[]{:S(2)}, u32[]{:S(2)}) collective-permute-start(f32[8,512]{1,0:T(8,128)S(1)} %get-tuple-element.68.own), channel_id=1, source_target_pairs={{0,4},{4,8},{8,12},{12,16},{16,20},{20,24},{24,28},{28,0},{1,5},{5... | collective-permute-start | bytes 49160 | tf_op jit(solution)/shard_map/ppermute | solution.py:737
  8.6 4.8 %collective-permute-start = (f32[8,512]{1,0:T(8,128)S(1)}, f32[8,512]{1,0:T(8,128)S(1)}, u32[]{:S(2)}, u32[]{:S(2)}) collective-permute-start(f32[8,512]{1,0:T(8,128)S(1)} %get-tuple-element.68.own), channel_id=1, source_target_pairs={{0,28},{4,0},{8,4},{12,8},{16,12},{20,16},{24,20},{28,24},{1,29},{... | collective-permute-start | bytes 49160 | tf_op jit(solution)/shard_map/ppermute | solution.py:736
  17.1 10.0 %collective-permute-start.16 = (f32[72,768]{1,0:T(8,128)S(1)}, f32[72,768]{1,0:T(8,128)S(1)}, u32[]{:S(2)}, u32[]{:S(2)}) collective-permute-start(f32[72,768]{1,0:T(8,128)S(1)} %get-tuple-element.87), channel_id=1, source_target_pairs={{0,2},{1,3},{2,0},{3,1},{4,6},{5,7},{6,4},{7,5},{8,10},{9,11},{10,... | collective-permute-start | bytes 663560 | tf_op jit(solution)/shard_map/ppermute | solution.py:702
  18.8 8.4 %collective-permute-start.17 = (f32[72,768]{1,0:T(8,128)S(1)}, f32[72,768]{1,0:T(8,128)S(1)}, u32[]{:S(2)}, u32[]{:S(2)}) collective-permute-start(f32[72,768]{1,0:T(8,128)S(1)} %get-tuple-element.88), channel_id=1, source_target_pairs={{0,1},{1,0},{2,3},{3,2},{4,5},{5,4},{6,7},{7,6},{8,9},{9,8},{10,11... | collective-permute-start | bytes 663560 | tf_op jit(solution)/shard_map/ppermute | solution.py:702
  18.8 8.4 %collective-permute-start.18 = (f32[72,768]{1,0:T(8,128)S(1)}, f32[72,768]{1,0:T(8,128)S(1)}, u32[]{:S(2)}, u32[]{:S(2)}) collective-permute-start(f32[72,768]{1,0:T(8,128)S(1)} %get-tuple-element.89), channel_id=1, source_target_pairs={{0,3},{1,2},{2,1},{3,0},{4,7},{5,6},{6,5},{7,4},{8,11},{9,10},{10,... | collective-permute-start | bytes 663560 | tf_op jit(solution)/shard_map/ppermute | solution.py:702
  25.3 5.8 %collective-permute-start.6 = (f32[72,768]{1,0:T(8,128)S(1)}, f32[72,768]{1,0:T(8,128)S(1)}, u32[]{:S(2)}, u32[]{:S(2)}) collective-permute-start(f32[72,768]{1,0:T(8,128)S(1)} %get-tuple-element.75), channel_id=1, source_target_pairs={{0,1},{1,0},{2,3},{3,2},{4,5},{5,4},{6,7},{7,6},{8,9},{9,8},{10,11... | collective-permute-start | bytes 663560 | tf_op jit(solution)/shard_map/ppermute | solution.py:702
  25.4 8.3 %collective-permute-start.7 = (f32[72,768]{1,0:T(8,128)S(1)}, f32[72,768]{1,0:T(8,128)S(1)}, u32[]{:S(2)}, u32[]{:S(2)}) collective-permute-start(f32[72,768]{1,0:T(8,128)S(1)} %get-tuple-element.76), channel_id=1, source_target_pairs={{0,2},{1,3},{2,0},{3,1},{4,6},{5,7},{6,4},{7,5},{8,10},{9,11},{10,... | collective-permute-start | bytes 663560 | tf_op jit(solution)/shard_map/ppermute | solution.py:702
  27.1 10.4 %collective-permute-start.8 = (f32[72,768]{1,0:T(8,128)S(1)}, f32[72,768]{1,0:T(8,128)S(1)}, u32[]{:S(2)}, u32[]{:S(2)}) collective-permute-start(f32[72,768]{1,0:T(8,128)S(1)} %get-tuple-element.77), channel_id=1, source_target_pairs={{0,3},{1,2},{2,1},{3,0},{4,7},{5,6},{6,5},{7,4},{8,11},{9,10},{10,... | collective-permute-start | bytes 663560 | tf_op jit(solution)/shard_map/ppermute | solution.py:702
  28.8 11.0 %collective-permute-start.19 = (f32[32,768]{1,0:T(8,128)S(1)}, f32[32,768]{1,0:T(8,128)S(1)}, u32[]{:S(2)}, u32[]{:S(2)}) collective-permute-start(f32[32,768]{1,0:T(8,128)S(1)} %get-tuple-element.91), channel_id=1, source_target_pairs={{0,16},{4,20},{8,24},{12,28},{16,0},{20,4},{24,8},{28,12},{1,17},{... | collective-permute-start | bytes 294920 | tf_op jit(solution)/shard_map/ppermute | solution.py:702
  28.9 12.4 %collective-permute-start.20 = (f32[32,768]{1,0:T(8,128)S(1)}, f32[32,768]{1,0:T(8,128)S(1)}, u32[]{:S(2)}, u32[]{:S(2)}) collective-permute-start(f32[32,768]{1,0:T(8,128)S(1)} %get-tuple-element.92), channel_id=1, source_target_pairs={{0,4},{4,0},{8,12},{12,8},{16,20},{20,16},{24,28},{28,24},{1,5},{5... | collective-permute-start | bytes 294920 | tf_op jit(solution)/shard_map/ppermute | solution.py:702
  31.1 12.9 %collective-permute-start.21 = (f32[32,768]{1,0:T(8,128)S(1)}, f32[32,768]{1,0:T(8,128)S(1)}, u32[]{:S(2)}, u32[]{:S(2)}) collective-permute-start(f32[32,768]{1,0:T(8,128)S(1)} %get-tuple-element.93), channel_id=1, source_target_pairs={{0,20},{4,16},{8,28},{12,24},{16,4},{20,0},{24,12},{28,8},{1,21},{... | collective-permute-start | bytes 294920 | tf_op jit(solution)/shard_map/ppermute | solution.py:702
  33.6 10.9 %collective-permute-start.22 = (f32[32,768]{1,0:T(8,128)S(1)}, f32[32,768]{1,0:T(8,128)S(1)}, u32[]{:S(2)}, u32[]{:S(2)}) collective-permute-start(f32[32,768]{1,0:T(8,128)S(1)} %get-tuple-element.94), channel_id=1, source_target_pairs={{0,8},{4,12},{8,0},{12,4},{16,24},{20,28},{24,16},{28,20},{1,9},{5... | collective-permute-start | bytes 294920 | tf_op jit(solution)/shard_map/ppermute | solution.py:702
  37.5 11.4 %collective-permute-start.23 = (f32[32,768]{1,0:T(8,128)S(1)}, f32[32,768]{1,0:T(8,128)S(1)}, u32[]{:S(2)}, u32[]{:S(2)}) collective-permute-start(f32[32,768]{1,0:T(8,128)S(1)} %get-tuple-element.95), channel_id=1, source_target_pairs={{0,24},{4,28},{8,16},{12,20},{16,8},{20,12},{24,0},{28,4},{1,25},{... | collective-permute-start | bytes 294920 | tf_op jit(solution)/shard_map/ppermute | solution.py:702
  39.8 9.0 %collective-permute-start.24 = (f32[32,768]{1,0:T(8,128)S(1)}, f32[32,768]{1,0:T(8,128)S(1)}, u32[]{:S(2)}, u32[]{:S(2)}) collective-permute-start(f32[32,768]{1,0:T(8,128)S(1)} %get-tuple-element.96), channel_id=1, source_target_pairs={{0,12},{4,8},{8,4},{12,0},{16,28},{20,24},{24,20},{28,16},{1,13},{... | collective-permute-start | bytes 294920 | tf_op jit(solution)/shard_map/ppermute | solution.py:702
  41.3 10.7 %collective-permute-start.25 = (f32[32,768]{1,0:T(8,128)S(1)}, f32[32,768]{1,0:T(8,128)S(1)}, u32[]{:S(2)}, u32[]{:S(2)}) collective-permute-start(f32[32,768]{1,0:T(8,128)S(1)} %get-tuple-element.97), channel_id=1, source_target_pairs={{0,28},{4,24},{8,20},{12,16},{16,12},{20,8},{24,4},{28,0},{1,29},{... | collective-permute-start | bytes 294920 | tf_op jit(solution)/shard_map/ppermute | solution.py:702
  44.0 13.4 %collective-permute-start.9 = (f32[32,768]{1,0:T(8,128)S(1)}, f32[32,768]{1,0:T(8,128)S(1)}, u32[]{:S(2)}, u32[]{:S(2)}) collective-permute-start(f32[32,768]{1,0:T(8,128)S(1)} %get-tuple-element.79), channel_id=1, source_target_pairs={{0,16},{4,20},{8,24},{12,28},{16,0},{20,4},{24,8},{28,12},{1,17},{... | collective-permute-start | bytes 294920 | tf_op jit(solution)/shard_map/ppermute | solution.py:702
  44.5 14.9 %collective-permute-start.10 = (f32[32,768]{1,0:T(8,128)S(1)}, f32[32,768]{1,0:T(8,128)S(1)}, u32[]{:S(2)}, u32[]{:S(2)}) collective-permute-start(f32[32,768]{1,0:T(8,128)S(1)} %get-tuple-element.80), channel_id=1, source_target_pairs={{0,4},{4,0},{8,12},{12,8},{16,20},{20,16},{24,28},{28,24},{1,5},{5... | collective-permute-start | bytes 294920 | tf_op jit(solution)/shard_map/ppermute | solution.py:702
  48.8 14.9 %collective-permute-start.11 = (f32[32,768]{1,0:T(8,128)S(1)}, f32[32,768]{1,0:T(8,128)S(1)}, u32[]{:S(2)}, u32[]{:S(2)}) collective-permute-start(f32[32,768]{1,0:T(8,128)S(1)} %get-tuple-element.81), channel_id=1, source_target_pairs={{0,20},{4,16},{8,28},{12,24},{16,4},{20,0},{24,12},{28,8},{1,21},{... | collective-permute-start | bytes 294920 | tf_op jit(solution)/shard_map/ppermute | solution.py:702
  48.8 15.0 %collective-permute-start.12 = (f32[32,768]{1,0:T(8,128)S(1)}, f32[32,768]{1,0:T(8,128)S(1)}, u32[]{:S(2)}, u32[]{:S(2)}) collective-permute-start(f32[32,768]{1,0:T(8,128)S(1)} %get-tuple-element.82), channel_id=1, source_target_pairs={{0,8},{4,12},{8,0},{12,4},{16,24},{20,28},{24,16},{28,20},{1,9},{5... | collective-permute-start | bytes 294920 | tf_op jit(solution)/shard_map/ppermute | solution.py:702
  52.1 13.5 %collective-permute-start.13 = (f32[32,768]{1,0:T(8,128)S(1)}, f32[32,768]{1,0:T(8,128)S(1)}, u32[]{:S(2)}, u32[]{:S(2)}) collective-permute-start(f32[32,768]{1,0:T(8,128)S(1)} %get-tuple-element.83), channel_id=1, source_target_pairs={{0,24},{4,28},{8,16},{12,20},{16,8},{20,12},{24,0},{28,4},{1,25},{... | collective-permute-start | bytes 294920 | tf_op jit(solution)/shard_map/ppermute | solution.py:702
  57.4 10.5 %collective-permute-start.14 = (f32[32,768]{1,0:T(8,128)S(1)}, f32[32,768]{1,0:T(8,128)S(1)}, u32[]{:S(2)}, u32[]{:S(2)}) collective-permute-start(f32[32,768]{1,0:T(8,128)S(1)} %get-tuple-element.84), channel_id=1, source_target_pairs={{0,12},{4,8},{8,4},{12,0},{16,28},{20,24},{24,20},{28,16},{1,13},{... | collective-permute-start | bytes 294920 | tf_op jit(solution)/shard_map/ppermute | solution.py:702
  59.4 8.4 %collective-permute-start.15 = (f32[32,768]{1,0:T(8,128)S(1)}, f32[32,768]{1,0:T(8,128)S(1)}, u32[]{:S(2)}, u32[]{:S(2)}) collective-permute-start(f32[32,768]{1,0:T(8,128)S(1)} %get-tuple-element.85), channel_id=1, source_target_pairs={{0,28},{4,24},{8,20},{12,16},{16,12},{20,8},{24,4},{28,0},{1,29},{... | collective-permute-start | bytes 294920 | tf_op jit(solution)/shard_map/ppermute | solution.py:702
  63.8 5.5 %collective-permute-start.4 = (f32[48,256]{1,0:T(8,128)S(1)}, f32[48,256]{1,0:T(8,128)S(1)}, u32[]{:S(2)}, u32[]{:S(2)}) collective-permute-start(f32[48,256]{1,0:T(8,128)S(1)} %get-tuple-element.72), channel_id=1, source_target_pairs={{0,1},{1,2},{2,3},{3,0},{4,5},{5,6},{6,7},{7,4},{8,9},{9,10},{10,1... | collective-permute-start | bytes 147464 | tf_op jit(solution)/shard_map/ppermute | solution.py:760
  63.8 5.4 %collective-permute-start.5 = (f32[48,256]{1,0:T(8,128)S(1)}, f32[48,256]{1,0:T(8,128)S(1)}, u32[]{:S(2)}, u32[]{:S(2)}) collective-permute-start(f32[48,256]{1,0:T(8,128)S(1)} %get-tuple-element.73), channel_id=1, source_target_pairs={{0,3},{1,0},{2,1},{3,2},{4,7},{5,4},{6,5},{7,6},{8,11},{9,8},{10,9... | collective-permute-start | bytes 147464 | tf_op jit(solution)/shard_map/ppermute | solution.py:761
  73.0 10.5 %collective-permute-start.26 = (f32[32,768]{1,0:T(8,128)S(1)}, f32[32,768]{1,0:T(8,128)S(1)}, u32[]{:S(2)}, u32[]{:S(2)}) collective-permute-start(f32[32,768]{1,0:T(8,128)S(1)} %get-tuple-element.100), channel_id=1, source_target_pairs={{0,16},{4,20},{8,24},{12,28},{16,0},{20,4},{24,8},{28,12},{1,17},{... | collective-permute-start | bytes 294920 | tf_op jit(solution)/shard_map/ppermute | solution.py:702
  74.8 8.8 %collective-permute-start.27 = (f32[32,768]{1,0:T(8,128)S(1)}, f32[32,768]{1,0:T(8,128)S(1)}, u32[]{:S(2)}, u32[]{:S(2)}) collective-permute-start(f32[32,768]{1,0:T(8,128)S(1)} %get-tuple-element.101), channel_id=1, source_target_pairs={{0,4},{4,0},{8,12},{12,8},{16,20},{20,16},{24,28},{28,24},{1,5},{5... | collective-permute-start | bytes 294920 | tf_op jit(solution)/shard_map/ppermute | solution.py:702
  75.8 13.7 %collective-permute-start.28 = (f32[32,768]{1,0:T(8,128)S(1)}, f32[32,768]{1,0:T(8,128)S(1)}, u32[]{:S(2)}, u32[]{:S(2)}) collective-permute-start(f32[32,768]{1,0:T(8,128)S(1)} %get-tuple-element.102), channel_id=1, source_target_pairs={{0,20},{4,16},{8,28},{12,24},{16,4},{20,0},{24,12},{28,8},{1,21},{... | collective-permute-start | bytes 294920 | tf_op jit(solution)/shard_map/ppermute | solution.py:702
  77.5 12.0 %collective-permute-start.29 = (f32[32,768]{1,0:T(8,128)S(1)}, f32[32,768]{1,0:T(8,128)S(1)}, u32[]{:S(2)}, u32[]{:S(2)}) collective-permute-start(f32[32,768]{1,0:T(8,128)S(1)} %get-tuple-element.103), channel_id=1, source_target_pairs={{0,8},{4,12},{8,0},{12,4},{16,24},{20,28},{24,16},{28,20},{1,9},{5... | collective-permute-start | bytes 294920 | tf_op jit(solution)/shard_map/ppermute | solution.py:702
  79.1 11.9 %collective-permute-start.30 = (f32[32,768]{1,0:T(8,128)S(1)}, f32[32,768]{1,0:T(8,128)S(1)}, u32[]{:S(2)}, u32[]{:S(2)}) collective-permute-start(f32[32,768]{1,0:T(8,128)S(1)} %get-tuple-element.104), channel_id=1, source_target_pairs={{0,24},{4,28},{8,16},{12,20},{16,8},{20,12},{24,0},{28,4},{1,25},{... | collective-permute-start | bytes 294920 | tf_op jit(solution)/shard_map/ppermute | solution.py:702
  83.5 10.6 %collective-permute-start.31 = (f32[32,768]{1,0:T(8,128)S(1)}, f32[32,768]{1,0:T(8,128)S(1)}, u32[]{:S(2)}, u32[]{:S(2)}) collective-permute-start(f32[32,768]{1,0:T(8,128)S(1)} %get-tuple-element.105), channel_id=1, source_target_pairs={{0,12},{4,8},{8,4},{12,0},{16,28},{20,24},{24,20},{28,16},{1,13},{... | collective-permute-start | bytes 294920 | tf_op jit(solution)/shard_map/ppermute | solution.py:702
  83.6 10.5 %collective-permute-start.32 = (f32[32,768]{1,0:T(8,128)S(1)}, f32[32,768]{1,0:T(8,128)S(1)}, u32[]{:S(2)}, u32[]{:S(2)}) collective-permute-start(f32[32,768]{1,0:T(8,128)S(1)} %get-tuple-element.106), channel_id=1, source_target_pairs={{0,28},{4,24},{8,20},{12,16},{16,12},{20,8},{24,4},{28,0},{1,29},{... | collective-permute-start | bytes 294920 | tf_op jit(solution)/shard_map/ppermute | solution.py:702
  89.4 11.7 %collective-permute-start.36 = (f32[32,768]{1,0:T(8,128)S(1)}, f32[32,768]{1,0:T(8,128)S(1)}, u32[]{:S(2)}, u32[]{:S(2)}) collective-permute-start(f32[32,768]{1,0:T(8,128)S(1)} %get-tuple-element.116), channel_id=1, source_target_pairs={{0,16},{4,20},{8,24},{12,28},{16,0},{20,4},{24,8},{28,12},{1,17},{... | collective-permute-start | bytes 294920 | tf_op jit(solution)/shard_map/ppermute | solution.py:702
  89.4 11.7 %collective-permute-start.37 = (f32[32,768]{1,0:T(8,128)S(1)}, f32[32,768]{1,0:T(8,128)S(1)}, u32[]{:S(2)}, u32[]{:S(2)}) collective-permute-start(f32[32,768]{1,0:T(8,128)S(1)} %get-tuple-element.117), channel_id=1, source_target_pairs={{0,4},{4,0},{8,12},{12,8},{16,20},{20,16},{24,28},{28,24},{1,5},{5... | collective-permute-start | bytes 294920 | tf_op jit(solution)/shard_map/ppermute | solution.py:702
  91.0 14.6 %collective-permute-start.38 = (f32[32,768]{1,0:T(8,128)S(1)}, f32[32,768]{1,0:T(8,128)S(1)}, u32[]{:S(2)}, u32[]{:S(2)}) collective-permute-start(f32[32,768]{1,0:T(8,128)S(1)} %get-tuple-element.118), channel_id=1, source_target_pairs={{0,20},{4,16},{8,28},{12,24},{16,4},{20,0},{24,12},{28,8},{1,21},{... | collective-permute-start | bytes 294920 | tf_op jit(solution)/shard_map/ppermute | solution.py:702
  94.1 11.5 %collective-permute-start.39 = (f32[32,768]{1,0:T(8,128)S(1)}, f32[32,768]{1,0:T(8,128)S(1)}, u32[]{:S(2)}, u32[]{:S(2)}) collective-permute-start(f32[32,768]{1,0:T(8,128)S(1)} %get-tuple-element.119), channel_id=1, source_target_pairs={{0,8},{4,12},{8,0},{12,4},{16,24},{20,28},{24,16},{28,20},{1,9},{5... | collective-permute-start | bytes 294920 | tf_op jit(solution)/shard_map/ppermute | solution.py:702
  95.8 9.8 %collective-permute-start.40 = (f32[32,768]{1,0:T(8,128)S(1)}, f32[32,768]{1,0:T(8,128)S(1)}, u32[]{:S(2)}, u32[]{:S(2)}) collective-permute-start(f32[32,768]{1,0:T(8,128)S(1)} %get-tuple-element.123), channel_id=1, source_target_pairs={{0,24},{4,28},{8,16},{12,20},{16,8},{20,12},{24,0},{28,4},{1,25},{... | collective-permute-start | bytes 294920 | tf_op jit(solution)/shard_map/ppermute | solution.py:702
  101.2 6.6 %collective-permute-start.41 = (f32[32,768]{1,0:T(8,128)S(1)}, f32[32,768]{1,0:T(8,128)S(1)}, u32[]{:S(2)}, u32[]{:S(2)}) collective-permute-start(f32[32,768]{1,0:T(8,128)S(1)} %get-tuple-element.124), channel_id=1, source_target_pairs={{0,12},{4,8},{8,4},{12,0},{16,28},{20,24},{24,20},{28,16},{1,13},{... | collective-permute-start | bytes 294920 | tf_op jit(solution)/shard_map/ppermute | solution.py:702
  101.2 8.0 %collective-permute-start.42 = (f32[32,768]{1,0:T(8,128)S(1)}, f32[32,768]{1,0:T(8,128)S(1)}, u32[]{:S(2)}, u32[]{:S(2)}) collective-permute-start(f32[32,768]{1,0:T(8,128)S(1)} %get-tuple-element.125), channel_id=1, source_target_pairs={{0,28},{4,24},{8,20},{12,16},{16,12},{20,8},{24,4},{28,0},{1,29},{... | collective-permute-start | bytes 294920 | tf_op jit(solution)/shard_map/ppermute | solution.py:702
  105.6 8.3 %collective-permute-start.33 = (f32[72,768]{1,0:T(8,128)S(1)}, f32[72,768]{1,0:T(8,128)S(1)}, u32[]{:S(2)}, u32[]{:S(2)}) collective-permute-start(f32[72,768]{1,0:T(8,128)S(1)} %get-tuple-element.108), channel_id=1, source_target_pairs={{0,2},{1,3},{2,0},{3,1},{4,6},{5,7},{6,4},{7,5},{8,10},{9,11},{10,... | collective-permute-start | bytes 663560 | tf_op jit(solution)/shard_map/ppermute | solution.py:702
  105.6 8.3 %collective-permute-start.34 = (f32[72,768]{1,0:T(8,128)S(1)}, f32[72,768]{1,0:T(8,128)S(1)}, u32[]{:S(2)}, u32[]{:S(2)}) collective-permute-start(f32[72,768]{1,0:T(8,128)S(1)} %get-tuple-element.109), channel_id=1, source_target_pairs={{0,1},{1,0},{2,3},{3,2},{4,5},{5,4},{6,7},{7,6},{8,9},{9,8},{10,11... | collective-permute-start | bytes 663560 | tf_op jit(solution)/shard_map/ppermute | solution.py:702
  105.6 8.9 %collective-permute-start.35 = (f32[72,768]{1,0:T(8,128)S(1)}, f32[72,768]{1,0:T(8,128)S(1)}, u32[]{:S(2)}, u32[]{:S(2)}) collective-permute-start(f32[72,768]{1,0:T(8,128)S(1)} %get-tuple-element.110), channel_id=1, source_target_pairs={{0,3},{1,2},{2,1},{3,0},{4,7},{5,6},{6,5},{7,4},{8,11},{9,10},{10,... | collective-permute-start | bytes 663560 | tf_op jit(solution)/shard_map/ppermute | solution.py:702
  110.9 12.4 %collective-permute-start.43 = (f32[72,768]{1,0:T(8,128)S(1)}, f32[72,768]{1,0:T(8,128)S(1)}, u32[]{:S(2)}, u32[]{:S(2)}) collective-permute-start(f32[72,768]{1,0:T(8,128)S(1)} %get-tuple-element.127), channel_id=1, source_target_pairs={{0,2},{1,3},{2,0},{3,1},{4,6},{5,7},{6,4},{7,5},{8,10},{9,11},{10,... | collective-permute-start | bytes 663560 | tf_op jit(solution)/shard_map/ppermute | solution.py:702
  113.0 10.3 %collective-permute-start.44 = (f32[72,768]{1,0:T(8,128)S(1)}, f32[72,768]{1,0:T(8,128)S(1)}, u32[]{:S(2)}, u32[]{:S(2)}) collective-permute-start(f32[72,768]{1,0:T(8,128)S(1)} %get-tuple-element.128), channel_id=1, source_target_pairs={{0,3},{1,2},{2,1},{3,0},{4,7},{5,6},{6,5},{7,4},{8,11},{9,10},{10,... | collective-permute-start | bytes 663560 | tf_op jit(solution)/shard_map/ppermute | solution.py:702
  113.9 9.4 %collective-permute-start.45 = (f32[72,768]{1,0:T(8,128)S(1)}, f32[72,768]{1,0:T(8,128)S(1)}, u32[]{:S(2)}, u32[]{:S(2)}) collective-permute-start(f32[72,768]{1,0:T(8,128)S(1)} %get-tuple-element.129), channel_id=1, source_target_pairs={{0,1},{1,0},{2,3},{3,2},{4,5},{5,4},{6,7},{7,6},{8,9},{9,8},{10,11... | collective-permute-start | bytes 663560 | tf_op jit(solution)/shard_map/ppermute | solution.py:702
  116.1 13.1 %collective-permute-start.46 = (f32[3,64,256]{2,1,0:T(8,128)S(1)}, f32[3,64,256]{2,1,0:T(8,128)S(1)}, u32[]{:S(2)}, u32[]{:S(2)}) collective-permute-start(f32[3,64,256]{2,1,0:T(8,128)S(1)} %get-tuple-element.132), channel_id=1, source_target_pairs={{0,4},{4,8},{8,12},{12,16},{16,20},{20,24},{24,28},{28,0},{1,5},{5... | collective-permute-start | bytes 589832 | tf_op jit(solution)/shard_map/ppermute | solution.py:831
  120.5 10.3 %collective-permute-start.47 = (f32[3,64,256]{2,1,0:T(8,128)S(1)}, f32[3,64,256]{2,1,0:T(8,128)S(1)}, u32[]{:S(2)}, u32[]{:S(2)}) collective-permute-start(f32[3,64,256]{2,1,0:T(8,128)S(1)} %get-tuple-element.133), channel_id=1, source_target_pairs={{0,28},{4,0},{8,4},{12,8},{16,12},{20,16},{24,20},{28,24},{1,29},{... | collective-permute-start | bytes 589832 | tf_op jit(solution)/shard_map/ppermute | solution.py:830
  (9 other events, 80.0 us)

commit v14 on v13

--- a/solution.py
+++ b/solution.py
@@ -13,7 +13,7 @@
 MIG = 64
 LANES = 128
 RIM = 8
-LATE = 3
+LATE = 1
 TIME_STEP = 0.25
 VMEM = 24 * 1024 * 1024
 F32 = jnp.float32
@@ -148,11 +148,12 @@
         return [0] + near + far
     if first == "far":
         return [0] + far + near
-    order = [0]
+    order, last = [0], near[-1:]
+    near = near[:-1]
     while far or near:
         order += far[:1] + near[:1]
         far, near = far[1:], near[1:]
-    return order
+    return order + last
 
 
 def blocks_of(refs, at, first=None):
@@ -301,9 +302,9 @@
         out[...] = made[d]
 
 
-def x_back_kernel(sends, first, tables, place, *refs):
+def x_back_kernel(sends, first, passed, tables, place, *refs):
     held, made = refs[-2:]
-    outs, parts = refs[-2 - sends : -2], refs[: -2 - sends]
+    outs, parts = refs[-2 - sends : -2], refs[passed : -2 - sends]
     gather_blocks(parts, held, place[0])
     pencils, rows, width = made.shape
     both = table_left(tables[0][...], tables[1][...], held[...].reshape(-1, width))
@@ -371,7 +372,8 @@
 
 
 def pass_kernel(before, *refs):
-    for source, target in zip(refs[: len(refs) // 2], refs[len(refs) // 2 :]):
+    half = LATE
+    for source, target in zip(refs[-2 * half : -half], refs[-half:]):
         target[...] = source[...]
 
 
@@ -797,12 +799,13 @@
         for chunk, source, width in zip(chunks, data, widths)
     ]
 
-    def back(part, width, first=None):
+    def back(part, width, first=None, before=()):
         shapes = sent_shapes("gx", rows, width)
         part = call(
-            loaded(functools.partial(x_back_kernel, len(shapes), first)),
+            loaded(functools.partial(x_back_kernel, len(shapes), first, len(before))),
             [here]
             + [(VM, t) for t in x_back]
+            + [(AN, b) for b in before]
             + [(VM, p) for p in part],
             [(VM, shape) for shape in shapes],
             [((slabs, block, width), F32), ((pencils, rows, width), F32)],
@@ -821,12 +824,12 @@
     if early < len(left[1]):
         late = call(
             pass_kernel,
-            [(AN, parts[0][0])] + [(VM, p) for p in left[1][early:]],
+            [(AN, parts[0][0])] + [(AN, p) for p in second[1:]] + [(VM, p) for p in left[1][early:]],
             [(VM, p.shape) for p in left[1][early:]],
             micros=0.3,
         )
         second += exchange(late, "gz", early)
-    parts.append(back(second, widths[1], "far"))
+    parts.append(back(second, widths[1], "far", [first]))
     after = lax.ppermute(first, "gz", ring("gz", -1))
     before = lax.ppermute(last, "gz", ring("gz", 1))
     velocity, vorticity = call(

time: 132 us -> 132 us (level)
    ppermute x1, starting transfers between devices: 4.4 us -> 0.01 us  [on_device(): before = lax.ppermute(last, 'gz', ring('gz', 1))]
    ppermute x40, waiting for transfers between devices: 21.2 us -> 24 us  [exchange(): lax.ppermute(block, axis, [(i, i ^ k) for i in range(count)])]
    ppermute x40, starting transfers between devices: 56.4 us -> 59 us  [exchange(): lax.ppermute(block, axis, [(i, i ^ k) for i in range(count)])]
    ppermute x1, waiting for transfers between devices: 1.68 us -> 0.01 us  [on_device(): after = lax.ppermute(first, 'gz', ring('gz', -1))]
    ppermute x1, starting transfers between devices: 0.37 us -> 2.02 us  [on_device(): after = lax.ppermute(first, 'gz', ring('gz', -1))]
  transfers between devices with their start and end apart: 48 -> 48, of which waited for: 16 -> 13; matrix products, arithmetic and copies ran while one was open for 0% -> 0% of each run, Pallas kernels for 16% -> 15%
where the time goes in v14:
time: 132 us
  starting transfers between devices  72.7 us (55%)
  Pallas kernels  30.6 us (23%)
  waiting for transfers between devices  27.2 us (21%)
    ppermute x40, starting transfers between devices, exchange(): lax.ppermute(block, axis, [(i, i ^ k) for i in range(count)])  59 us
    pallas_call x16, Pallas kernels, call(): pl.pallas_call(kernel, out_shape=[jax.ShapeDtypeStruct(shape, F32) for _,...  30.6 us
    ppermute x40, waiting for transfers between devices, exchange(): lax.ppermute(block, axis, [(i, i ^ k) for i in range(count)])  24 us
    ppermute x1, starting transfers between devices, on_device(): down2 = lax.ppermute(movers, 'gz', ring('gz', 2))  3.08 us
    ppermute x1, starting transfers between devices, on_device(): up1 = lax.ppermute(packet, 'gz', ring('gz', -1))  3.08 us
  transfers between devices with their start and end apart: 48, of which 13 were waited for; matrix products, arithmetic and copies ran while one was open for 0% of the time, Pallas kernels for 15%

profile of v14, /device:TPU:0, one launch (start us, length us, event | category | flops | bytes accessed | tf_op | source)
XLA Modules:
  0.0 131.7 jit_solution(3065617432559624375)
XLA Ops:
  1.8 3.1 %collective-permute-start.3 = (f32[8,128]{1,0:T(8,128)S(1)}, f32[8,128]{1,0:T(8,128)S(1)}, u32[]{:S(2)}, u32[]{:S(2)}) collective-permute-start(f32[8,128]{1,0:T(8,128)S(1)} %get-tuple-element.66), channel_id=1, source_target_pairs={{0,8},{4,12},{8,16},{12,20},{16,24},{20,28},{24,0},{28,4},{1,9},{5... | collective-permute-start | bytes 12296 | tf_op jit(solution)/shard_map/ppermute | solution.py:741
  4.8 2.1 %collective-permute-start.2 = (f32[8,128]{1,0:T(8,128)S(1)}, f32[8,128]{1,0:T(8,128)S(1)}, u32[]{:S(2)}, u32[]{:S(2)}) collective-permute-start(f32[8,128]{1,0:T(8,128)S(1)} %get-tuple-element.66), channel_id=1, source_target_pairs={{0,24},{4,28},{8,0},{12,4},{16,8},{20,12},{24,16},{28,20},{1,25},{... | collective-permute-start | bytes 12296 | tf_op jit(solution)/shard_map/ppermute | solution.py:740
  6.9 1.6 %collective-permute-start.1 = (f32[8,512]{1,0:T(8,128)S(1)}, f32[8,512]{1,0:T(8,128)S(1)}, u32[]{:S(2)}, u32[]{:S(2)}) collective-permute-start(f32[8,512]{1,0:T(8,128)S(1)} %get-tuple-element.65.own), channel_id=1, source_target_pairs={{0,4},{4,8},{8,12},{12,16},{16,20},{20,24},{24,28},{28,0},{1,5},{5... | collective-permute-start | bytes 49160 | tf_op jit(solution)/shard_map/ppermute | solution.py:739
  8.6 3.1 %collective-permute-start = (f32[8,512]{1,0:T(8,128)S(1)}, f32[8,512]{1,0:T(8,128)S(1)}, u32[]{:S(2)}, u32[]{:S(2)}) collective-permute-start(f32[8,512]{1,0:T(8,128)S(1)} %get-tuple-element.65.own), channel_id=1, source_target_pairs={{0,28},{4,0},{8,4},{12,8},{16,12},{20,16},{24,20},{28,24},{1,29},{... | collective-permute-start | bytes 49160 | tf_op jit(solution)/shard_map/ppermute | solution.py:738
  11.7 1.6 %collective-permute-done.1.down1 = f32[8,512]{1,0:T(8,128)S(1)} collective-permute-done((f32[8,512]{1,0:T(8,128)S(1)}, f32[8,512]{1,0:T(8,128)S(1)}, u32[]{:S(2)}, u32[]{:S(2)}) %collective-permute-start.1) | collective-permute-done | bytes 16416 | tf_op jit(solution)/shard_map/ppermute | solution.py:739
  13.4 3.7 %shard_map.141 = (f32[3,4,64,256]{3,2,1,0:T(8,128)S(1)}, f32[24,256]{1,0:T(8,128)S(1)}, f32[24,256]{1,0:T(8,128)S(1)}, f32[72,768]{1,0:T(8,128)S(1)}, f32[72,768...) custom-call(s32[2]{0:T(128)S(1)} %pad_add_fusion.place, f32[8,512]{1,0:T(8,128)S(1)} %get-tuple-element.65.own, ...), custom_call_target="tpu_custom_call" | custom-call | flops 5000000000 | bytes 15000000 | tf_op jit(solution)/shard_map/pallas_call | solution.py:668
  17.1 1.7 %collective-permute-start.16 = (f32[72,768]{1,0:T(8,128)S(1)}, f32[72,768]{1,0:T(8,128)S(1)}, u32[]{:S(2)}, u32[]{:S(2)}) collective-permute-start(f32[72,768]{1,0:T(8,128)S(1)} %get-tuple-element.84), channel_id=1, source_target_pairs={{0,2},{1,3},{2,0},{3,1},{4,6},{5,7},{6,4},{7,5},{8,10},{9,11},{10,... | collective-permute-start | bytes 663560 | tf_op jit(solution)/shard_map/ppermute | solution.py:704
  19.3 6.0 %shard_map.142 = (f32[3,4,64,256]{3,2,1,0:T(8,128)S(1)}, f32[48,256]{1,0:T(8,128)S(1)}, f32[48,256]{1,0:T(8,128)S(1)}, f32[72,768]{1,0:T(8,128)S(1)}, f32[72,768...) custom-call(s32[2]{0:T(128)S(1)} %pad_add_fusion.place, f32[8,512]{1,0:T(8,128)S(1)} %get-tuple-element.65.own, ...), custom_call_target="tpu_custom_call" | custom-call | flops 5000000000 | bytes 15000000 | tf_op jit(solution)/shard_map/pallas_call | solution.py:668
  25.4 1.7 %collective-permute-start.7 = (f32[72,768]{1,0:T(8,128)S(1)}, f32[72,768]{1,0:T(8,128)S(1)}, u32[]{:S(2)}, u32[]{:S(2)}) collective-permute-start(f32[72,768]{1,0:T(8,128)S(1)} %get-tuple-element.73), channel_id=1, source_target_pairs={{0,2},{1,3},{2,0},{3,1},{4,6},{5,7},{6,4},{7,5},{8,10},{9,11},{10,... | collective-permute-start | bytes 663560 | tf_op jit(solution)/shard_map/ppermute | solution.py:704
  27.2 1.6 %shard_map.145 = (f32[32,768]{1,0:T(8,128)S(1)}, f32[32,768]{1,0:T(8,128)S(1)}, f32[32,768]{1,0:T(8,128)S(1)}, f32[32,768]{1,0:T(8,128)S(1)}, f32[32,768]{1,0:T(...) custom-call(s32[2]{0:T(128)S(1)} %pad_add_fusion.place, ...), custom_call_target="tpu_custom_call" | custom-call | flops 2000000000 | bytes 6000000 | tf_op jit(solution)/shard_map/pallas_call | solution.py:668
  28.9 2.2 %collective-permute-start.20 = (f32[32,768]{1,0:T(8,128)S(1)}, f32[32,768]{1,0:T(8,128)S(1)}, u32[]{:S(2)}, u32[]{:S(2)}) collective-permute-start(f32[32,768]{1,0:T(8,128)S(1)} %get-tuple-element.89), channel_id=1, source_target_pairs={{0,4},{4,0},{8,12},{12,8},{16,20},{20,16},{24,28},{28,24},{1,5},{5... | collective-permute-start | bytes 294920 | tf_op jit(solution)/shard_map/ppermute | solution.py:704
  31.1 2.2 %collective-permute-start.21 = (f32[32,768]{1,0:T(8,128)S(1)}, f32[32,768]{1,0:T(8,128)S(1)}, u32[]{:S(2)}, u32[]{:S(2)}) collective-permute-start(f32[32,768]{1,0:T(8,128)S(1)} %get-tuple-element.90), channel_id=1, source_target_pairs={{0,20},{4,16},{8,28},{12,24},{16,4},{20,0},{24,12},{28,8},{1,21},{... | collective-permute-start | bytes 294920 | tf_op jit(solution)/shard_map/ppermute | solution.py:704
  33.6 1.2 collective-permute-start.22
  34.8 2.7 %collective-permute-done.8.refs_3_ = f32[72,768]{1,0:T(8,128)S(1)} collective-permute-done((f32[72,768]{1,0:T(8,128)S(1)}, f32[72,768]{1,0:T(8,128)S(1)}, u32[]{:S(2)}, u32[]{:S(2)}) %collective-permute-start.8) | collective-permute-done | bytes 221216 | tf_op jit(solution)/shard_map/ppermute | solution.py:704
  38.2 1.6 %shard_map.143 = (f32[32,768]{1,0:T(8,128)S(1)}, f32[32,768]{1,0:T(8,128)S(1)}, f32[32,768]{1,0:T(8,128)S(1)}, f32[32,768]{1,0:T(8,128)S(1)}, f32[32,768]{1,0:T(...) custom-call(s32[2]{0:T(128)S(1)} %pad_add_fusion.place, ...), custom_call_target="tpu_custom_call" | custom-call | flops 2000000000 | bytes 6000000 | tf_op jit(solution)/shard_map/pallas_call | solution.py:668
  39.8 4.0 %collective-permute-start.24 = (f32[32,768]{1,0:T(8,128)S(1)}, f32[32,768]{1,0:T(8,128)S(1)}, u32[]{:S(2)}, u32[]{:S(2)}) collective-permute-start(f32[32,768]{1,0:T(8,128)S(1)} %get-tuple-element.93), channel_id=1, source_target_pairs={{0,28},{4,24},{8,20},{12,16},{16,12},{20,8},{24,4},{28,0},{1,29},{... | collective-permute-start | bytes 294920 | tf_op jit(solution)/shard_map/ppermute | solution.py:704
  43.9 1.3 collective-permute-start.9
  45.2 4.5 %collective-permute-start.10 = (f32[32,768]{1,0:T(8,128)S(1)}, f32[32,768]{1,0:T(8,128)S(1)}, u32[]{:S(2)}, u32[]{:S(2)}) collective-permute-start(f32[32,768]{1,0:T(8,128)S(1)} %get-tuple-element.77), channel_id=1, source_target_pairs={{0,4},{4,0},{8,12},{12,8},{16,20},{20,16},{24,28},{28,24},{1,5},{5... | collective-permute-start | bytes 294920 | tf_op jit(solution)/shard_map/ppermute | solution.py:704
  50.8 5.4 %collective-permute-start.13 = (f32[32,768]{1,0:T(8,128)S(1)}, f32[32,768]{1,0:T(8,128)S(1)}, u32[]{:S(2)}, u32[]{:S(2)}) collective-permute-start(f32[32,768]{1,0:T(8,128)S(1)} %get-tuple-element.80), channel_id=1, source_target_pairs={{0,24},{4,28},{8,16},{12,20},{16,8},{20,12},{24,0},{28,4},{1,25},{... | collective-permute-start | bytes 294920 | tf_op jit(solution)/shard_map/ppermute | solution.py:704
  56.2 3.1 %collective-permute-start.14 = (f32[32,768]{1,0:T(8,128)S(1)}, f32[32,768]{1,0:T(8,128)S(1)}, u32[]{:S(2)}, u32[]{:S(2)}) collective-permute-start(f32[32,768]{1,0:T(8,128)S(1)} %get-tuple-element.81), channel_id=1, source_target_pairs={{0,28},{4,24},{8,20},{12,16},{16,12},{20,8},{24,4},{28,0},{1,29},{... | collective-permute-start | bytes 294920 | tf_op jit(solution)/shard_map/ppermute | solution.py:704
  59.3 1.3 %shard_map.146.refs_1_ = f32[3,2,4,8,8,128]{5,4,3,2,1,0:T(8,128)S(1)} custom-call(s32[2]{0:T(128)S(1)} %pad_add_fusion.place, f32[32,768]{1,0:T(8,128)S(1)} %get-tuple-element.87.refs_0_, f32[32,768]{1,0:T(8,128)S(1)} %collective-permute-done.19.refs_1_, f32[32,768]{1,0:T(8,128)S(1)} %collective-permute-done.20.refs_2_, ...), custom_call_target="tpu_custom_call" | custom-call | flops 2000000000 | bytes 6000000 | tf_op jit(solution)/shard_map/pallas_call | solution.py:668
  60.7 1.7 %collective-permute-start.5 = (f32[48,256]{1,0:T(8,128)S(1)}, f32[48,256]{1,0:T(8,128)S(1)}, u32[]{:S(2)}, u32[]{:S(2)}) collective-permute-start(f32[48,256]{1,0:T(8,128)S(1)} %get-tuple-element.70), channel_id=1, source_target_pairs={{0,3},{1,0},{2,1},{3,2},{4,7},{5,4},{6,5},{7,6},{8,11},{9,8},{10,9... | collective-permute-start | bytes 147464 | tf_op jit(solution)/shard_map/ppermute | solution.py:763
  62.5 1.7 %collective-permute-done.14.refs_6_ = f32[32,768]{1,0:T(8,128)S(1)} collective-permute-done((f32[32,768]{1,0:T(8,128)S(1)}, f32[32,768]{1,0:T(8,128)S(1)}, u32[]{:S(2)}, u32[]{:S(2)}) %collective-permute-start.14) | collective-permute-done | bytes 98336 | tf_op jit(solution)/shard_map/ppermute | solution.py:704
  64.2 1.8 %collective-permute-done.15.refs_7_ = f32[32,768]{1,0:T(8,128)S(1)} collective-permute-done((f32[32,768]{1,0:T(8,128)S(1)}, f32[32,768]{1,0:T(8,128)S(1)}, u32[]{:S(2)}, u32[]{:S(2)}) %collective-permute-start.15) | collective-permute-done | bytes 98336 | tf_op jit(solution)/shard_map/ppermute | solution.py:704
  66.0 1.3 %shard_map.144.refs_0_ = f32[3,2,4,8,8,128]{5,4,3,2,1,0:T(8,128)S(1)} custom-call(s32[2]{0:T(128)S(1)} %pad_add_fusion.place, f32[32,768]{1,0:T(8,128)S(1)} %get-tuple-element.75.refs_0_, f32[32,768]{1,0:T(8,128)S(1)} %collective-permute-done.9.refs_1_, f32[32,768]{1,0:T(8,128)S(1)} %collective-permute-done.10.refs_2_, ...), custom_call_target="tpu_custom_call" | custom-call | flops 2000000000 | bytes 6000000 | tf_op jit(solution)/shard_map/pallas_call | solution.py:668
  67.4 2.3 %shard_map.147 = (f32[3,2,4,8,8,128]{5,4,3,2,1,0:T(8,128)S(1)}, f32[3,2,4,8,8,128]{5,4,3,2,1,0:T(8,128)S(1)}) custom-call(s32[2]{0:T(128)S(1)} %pad_add_fusion.place, f32[48,256]{1,0:T(8,128)S(1)} %collective-permute-done.4.low_rim.refs_1_, f32[48,256]{1,0:T(8,128)S(1)} %collective-permute-done.5.high_rim.refs_2_, ...), custom_call_target="tpu_custom_call" | custom-call | flops 5000000000 | bytes 15000000 | tf_op jit(solution)/shard_map/pallas_call | solution.py:668
  69.7 1.4 %shard_map.148 = (f32[32,768]{1,0:T(8,128)S(1)}, f32[32,768]{1,0:T(8,128)S(1)}, f32[32,768]{1,0:T(8,128)S(1)}, f32[32,768]{1,0:T(8,128)S(1)}, f32[32,768]{1,0:T(...) custom-call(s32[2]{0:T(128)S(1)} %pad_add_fusion.place, ...), custom_call_target="tpu_custom_call" | custom-call | flops 2000000000 | bytes 6000000 | tf_op jit(solution)/shard_map/pallas_call | solution.py:668
  71.1 2.3 %collective-permute-start.26 = (f32[32,768]{1,0:T(8,128)S(1)}, f32[32,768]{1,0:T(8,128)S(1)}, u32[]{:S(2)}, u32[]{:S(2)}) collective-permute-start(f32[32,768]{1,0:T(8,128)S(1)} %get-tuple-element.97), channel_id=1, source_target_pairs={{0,16},{4,20},{8,24},{12,28},{16,0},{20,4},{24,8},{28,12},{1,17},{... | collective-permute-start | bytes 294920 | tf_op jit(solution)/shard_map/ppermute | solution.py:704
  73.4 1.2 collective-permute-start.27
  75.6 1.2 collective-permute-start.29
  76.8 2.5 %collective-permute-start.30 = (f32[32,768]{1,0:T(8,128)S(1)}, f32[32,768]{1,0:T(8,128)S(1)}, u32[]{:S(2)}, u32[]{:S(2)}) collective-permute-start(f32[32,768]{1,0:T(8,128)S(1)} %get-tuple-element.101), channel_id=1, source_target_pairs={{0,24},{4,28},{8,16},{12,20},{16,8},{20,12},{24,0},{28,4},{1,25},{... | collective-permute-start | bytes 294920 | tf_op jit(solution)/shard_map/ppermute | solution.py:704
  79.3 1.2 collective-permute-done.26.refs_1_
  80.4 1.4 %collective-permute-start.31 = (f32[32,768]{1,0:T(8,128)S(1)}, f32[32,768]{1,0:T(8,128)S(1)}, u32[]{:S(2)}, u32[]{:S(2)}) collective-permute-start(f32[32,768]{1,0:T(8,128)S(1)} %get-tuple-element.102), channel_id=1, source_target_pairs={{0,28},{4,24},{8,20},{12,16},{16,12},{20,8},{24,4},{28,0},{1,29},{... | collective-permute-start | bytes 294920 | tf_op jit(solution)/shard_map/ppermute | solution.py:704
  81.8 1.4 %shard_map.151 = (f32[32,768]{1,0:T(8,128)S(1)}, f32[32,768]{1,0:T(8,128)S(1)}, f32[32,768]{1,0:T(8,128)S(1)}, f32[32,768]{1,0:T(8,128)S(1)}, f32[32,768]{1,0:T(...) custom-call(s32[2]{0:T(128)S(1)} %pad_add_fusion.place, ...), custom_call_target="tpu_custom_call" | custom-call | flops 2000000000 | bytes 6000000 | tf_op jit(solution)/shard_map/pallas_call | solution.py:668
  83.2 5.6 %collective-permute-done.28.refs_3_ = f32[32,768]{1,0:T(8,128)S(1)} collective-permute-done((f32[32,768]{1,0:T(8,128)S(1)}, f32[32,768]{1,0:T(8,128)S(1)}, u32[]{:S(2)}, u32[]{:S(2)}) %collective-permute-start.28) | collective-permute-done | bytes 98336 | tf_op jit(solution)/shard_map/ppermute | solution.py:704
  89.9 3.3 %collective-permute-start.38 = (f32[32,768]{1,0:T(8,128)S(1)}, f32[32,768]{1,0:T(8,128)S(1)}, u32[]{:S(2)}, u32[]{:S(2)}) collective-permute-start(f32[32,768]{1,0:T(8,128)S(1)} %get-tuple-element.116), channel_id=1, source_target_pairs={{0,20},{4,16},{8,28},{12,24},{16,4},{20,0},{24,12},{28,8},{1,21},{... | collective-permute-start | bytes 294920 | tf_op jit(solution)/shard_map/ppermute | solution.py:704
  93.2 3.6 %collective-permute-start.39 = (f32[32,768]{1,0:T(8,128)S(1)}, f32[32,768]{1,0:T(8,128)S(1)}, u32[]{:S(2)}, u32[]{:S(2)}) collective-permute-start(f32[32,768]{1,0:T(8,128)S(1)} %get-tuple-element.117), channel_id=1, source_target_pairs={{0,8},{4,12},{8,0},{12,4},{16,24},{20,28},{24,16},{28,20},{1,9},{5... | collective-permute-start | bytes 294920 | tf_op jit(solution)/shard_map/ppermute | solution.py:704
  96.8 1.7 %shard_map.149 = (f32[72,768]{1,0:T(8,128)S(1)}, f32[72,768]{1,0:T(8,128)S(1)}, f32[72,768]{1,0:T(8,128)S(1)}, f32[72,768]{1,0:T(8,128)S(1)}) custom-call(s32[2]{0:T(128)S(1)} %pad_add_fusion.place, bf16[576,256]{1,0:T(8,128)(2,1)S(1)} %copy-done.6, bf16[576,256]{1,0:T(8,128)(2,1)S(1)} %copy-done.5, f32[32,768]{1,0:T(8,128)S(1)} %get-tuple-element.96.refs_0_, ...), custom_call_target="tpu_custom_call" | custom-call | flops 2000000000 | bytes 6000000 | tf_op jit(solution)/shard_map/pallas_call | solution.py:668
  101.6 2.9 %collective-permute-start.41 = (f32[32,768]{1,0:T(8,128)S(1)}, f32[32,768]{1,0:T(8,128)S(1)}, u32[]{:S(2)}, u32[]{:S(2)}) collective-permute-start(f32[32,768]{1,0:T(8,128)S(1)} %get-tuple-element.119), channel_id=1, source_target_pairs={{0,28},{4,24},{8,20},{12,16},{16,12},{20,8},{24,4},{28,0},{1,29},{... | collective-permute-start | bytes 294920 | tf_op jit(solution)/shard_map/ppermute | solution.py:704
  104.5 3.8 %collective-permute-done.40.refs_4_.refs_6_ = f32[32,768]{1,0:T(8,128)S(1)} collective-permute-done((f32[32,768]{1,0:T(8,128)S(1)}, f32[32,768]{1,0:T(8,128)S(1)}, u32[]{:S(2)}, u32[]{:S(2)}) %collective-permute-start.40) | collective-permute-done | bytes 98336 | tf_op jit(solution)/shard_map/ppermute | solution.py:704
  109.4 3.4 %collective-permute-start.42 = (f32[32,768]{1,0:T(8,128)S(1)}, f32[32,768]{1,0:T(8,128)S(1)}, u32[]{:S(2)}, u32[]{:S(2)}) collective-permute-start(f32[32,768]{1,0:T(8,128)S(1)} %shard_map.152), channel_id=1, source_target_pairs={{0,12},{4,8},{8,4},{12,0},{16,28},{20,24},{24,20},{28,16},{1,13},{... | collective-permute-start | bytes 294920 | tf_op jit(solution)/shard_map/ppermute | solution.py:704
  112.8 1.5 %shard_map.150 = (f32[3,4,80,256]{3,2,1,0:T(8,128)S(1)}, f32[3,64,256]{2,1,0:T(8,128)S(1)}, f32[3,64,256]{2,1,0:T(8,128)S(1)}) custom-call(s32[2]{0:T(128)S(1)} %pad_add_fusion.place, bf16[512,512]{1,0:T(8,128)(2,1)S(1)} %copy-done.2, bf16[512,512]{1,0:T(8,128)(2,1)S(1)} %copy-done.1, f32[72,768]{1,0:T(8,128)S(1)} %get-tuple-element.104.refs_0_.before, ...), custom_call_target="tpu_custom_call" | custom-call | flops 2000000000 | bytes 6000000 | tf_op jit(solution)/shard_map/pallas_call | solution.py:668
  115.4 1.7 %shard_map.153 = (f32[72,768]{1,0:T(8,128)S(1)}, f32[72,768]{1,0:T(8,128)S(1)}, f32[72,768]{1,0:T(8,128)S(1)}, f32[72,768]{1,0:T(8,128)S(1)}) custom-call(s32[2]{0:T(128)S(1)} %pad_add_fusion.place, bf16[576,256]{1,0:T(8,128)(2,1)S(1)} %copy-done.6, bf16[576,256]{1,0:T(8,128)(2,1)S(1)} %copy-done.5, f32[3,64,256]{2,1,0:T(8,128)S(1)} %get-tuple-element.111.refs_0_, ...), custom_call_target="tpu_custom_call" | custom-call | flops 2000000000 | bytes 6000000 | tf_op jit(solution)/shard_map/pallas_call | solution.py:668
  117.8 1.5 %collective-permute-start.45 = (f32[72,768]{1,0:T(8,128)S(1)}, f32[72,768]{1,0:T(8,128)S(1)}, u32[]{:S(2)}, u32[]{:S(2)}) collective-permute-start(f32[72,768]{1,0:T(8,128)S(1)} %get-tuple-element.124), channel_id=1, source_target_pairs={{0,1},{1,0},{2,3},{3,2},{4,5},{5,4},{6,7},{7,6},{8,9},{9,8},{10,11... | collective-permute-start | bytes 663560 | tf_op jit(solution)/shard_map/ppermute | solution.py:704
  119.3 2.0 %collective-permute-start.47 = (f32[3,64,256]{2,1,0:T(8,128)S(1)}, f32[3,64,256]{2,1,0:T(8,128)S(1)}, u32[]{:S(2)}, u32[]{:S(2)}) collective-permute-start(f32[3,64,256]{2,1,0:T(8,128)S(1)} %get-tuple-element.111.refs_0_), channel_id=1, source_target_pairs={{0,28},{4,0},{8,4},{12,8},{16,12},{20,16},{24,20},{28,24},{1,29},{... | collective-permute-start | bytes 589832 | tf_op jit(solution)/shard_map/ppermute | solution.py:833
  121.3 4.0 %collective-permute-done.43.refs_6_ = f32[72,768]{1,0:T(8,128)S(1)} collective-permute-done((f32[72,768]{1,0:T(8,128)S(1)}, f32[72,768]{1,0:T(8,128)S(1)}, u32[]{:S(2)}, u32[]{:S(2)}) %collective-permute-start.43) | collective-permute-done | bytes 221216 | tf_op jit(solution)/shard_map/ppermute | solution.py:704
  126.0 3.0 %shard_map.154 = (f32[3,8,64,256]{3,2,1,0:T(8,128)}, f32[3,8,64,256]{3,2,1,0:T(8,128)}) custom-call(s32[2]{0:T(128)S(1)} %pad_add_fusion.place, bf16[512,512]{1,0:T(8,128)(2,1)S(1)} %copy-done.2, bf16[512,512]{1,0:T(8,128)(2,1)S(1)} %copy-done.1, f32[3,4,80,256]{3,2,1,0:T(8,128)S(1)} %get-tuple-element.108.refs_0_.edges, ...), custom_call_target="tpu_custom_call" | custom-call | flops 4000000000 | bytes 12000000 | tf_op jit(solution)/shard_map/pallas_call | solution.py:668
  129.0 1.5 %collective-permute-done.46.before = f32[3,64,256]{2,1,0:T(8,128)S(1)} collective-permute-done((f32[3,64,256]{2,1,0:T(8,128)S(1)}, f32[3,64,256]{2,1,0:T(8,128)S(1)}, u32[]{:S(2)}, u32[]{:S(2)}) %collective-permute-start.46) | collective-permute-done | bytes 196640 | tf_op jit(solution)/shard_map/ppermute | solution.py:834
  (83 shorter events, 14.2 us)
Async XLA Ops:
  1.8 10.0 %collective-permute-start.3 = (f32[8,128]{1,0:T(8,128)S(1)}, f32[8,128]{1,0:T(8,128)S(1)}, u32[]{:S(2)}, u32[]{:S(2)}) collective-permute-start(f32[8,128]{1,0:T(8,128)S(1)} %get-tuple-element.66), channel_id=1, source_target_pairs={{0,8},{4,12},{8,16},{12,20},{16,24},{20,28},{24,0},{28,4},{1,9},{5... | collective-permute-start | bytes 12296 | tf_op jit(solution)/shard_map/ppermute | solution.py:741
  4.8 6.9 %collective-permute-start.2 = (f32[8,128]{1,0:T(8,128)S(1)}, f32[8,128]{1,0:T(8,128)S(1)}, u32[]{:S(2)}, u32[]{:S(2)}) collective-permute-start(f32[8,128]{1,0:T(8,128)S(1)} %get-tuple-element.66), channel_id=1, source_target_pairs={{0,24},{4,28},{8,0},{12,4},{16,8},{20,12},{24,16},{28,20},{1,25},{... | collective-permute-start | bytes 12296 | tf_op jit(solution)/shard_map/ppermute | solution.py:740
  6.9 6.4 %collective-permute-start.1 = (f32[8,512]{1,0:T(8,128)S(1)}, f32[8,512]{1,0:T(8,128)S(1)}, u32[]{:S(2)}, u32[]{:S(2)}) collective-permute-start(f32[8,512]{1,0:T(8,128)S(1)} %get-tuple-element.65.own), channel_id=1, source_target_pairs={{0,4},{4,8},{8,12},{12,16},{16,20},{20,24},{24,28},{28,0},{1,5},{5... | collective-permute-start | bytes 49160 | tf_op jit(solution)/shard_map/ppermute | solution.py:739
  8.6 4.8 %collective-permute-start = (f32[8,512]{1,0:T(8,128)S(1)}, f32[8,512]{1,0:T(8,128)S(1)}, u32[]{:S(2)}, u32[]{:S(2)}) collective-permute-start(f32[8,512]{1,0:T(8,128)S(1)} %get-tuple-element.65.own), channel_id=1, source_target_pairs={{0,28},{4,0},{8,4},{12,8},{16,12},{20,16},{24,20},{28,24},{1,29},{... | collective-permute-start | bytes 49160 | tf_op jit(solution)/shard_map/ppermute | solution.py:738
  17.1 10.0 %collective-permute-start.16 = (f32[72,768]{1,0:T(8,128)S(1)}, f32[72,768]{1,0:T(8,128)S(1)}, u32[]{:S(2)}, u32[]{:S(2)}) collective-permute-start(f32[72,768]{1,0:T(8,128)S(1)} %get-tuple-element.84), channel_id=1, source_target_pairs={{0,2},{1,3},{2,0},{3,1},{4,6},{5,7},{6,4},{7,5},{8,10},{9,11},{10,... | collective-permute-start | bytes 663560 | tf_op jit(solution)/shard_map/ppermute | solution.py:704
  18.8 8.4 %collective-permute-start.17 = (f32[72,768]{1,0:T(8,128)S(1)}, f32[72,768]{1,0:T(8,128)S(1)}, u32[]{:S(2)}, u32[]{:S(2)}) collective-permute-start(f32[72,768]{1,0:T(8,128)S(1)} %get-tuple-element.85), channel_id=1, source_target_pairs={{0,3},{1,2},{2,1},{3,0},{4,7},{5,6},{6,5},{7,4},{8,11},{9,10},{10,... | collective-permute-start | bytes 663560 | tf_op jit(solution)/shard_map/ppermute | solution.py:704
  18.8 8.4 %collective-permute-start.18 = (f32[72,768]{1,0:T(8,128)S(1)}, f32[72,768]{1,0:T(8,128)S(1)}, u32[]{:S(2)}, u32[]{:S(2)}) collective-permute-start(f32[72,768]{1,0:T(8,128)S(1)} %get-tuple-element.86), channel_id=1, source_target_pairs={{0,1},{1,0},{2,3},{3,2},{4,5},{5,4},{6,7},{7,6},{8,9},{9,8},{10,11... | collective-permute-start | bytes 663560 | tf_op jit(solution)/shard_map/ppermute | solution.py:704
  25.3 5.8 %collective-permute-start.6 = (f32[72,768]{1,0:T(8,128)S(1)}, f32[72,768]{1,0:T(8,128)S(1)}, u32[]{:S(2)}, u32[]{:S(2)}) collective-permute-start(f32[72,768]{1,0:T(8,128)S(1)} %get-tuple-element.72), channel_id=1, source_target_pairs={{0,1},{1,0},{2,3},{3,2},{4,5},{5,4},{6,7},{7,6},{8,9},{9,8},{10,11... | collective-permute-start | bytes 663560 | tf_op jit(solution)/shard_map/ppermute | solution.py:704
  25.4 8.3 %collective-permute-start.7 = (f32[72,768]{1,0:T(8,128)S(1)}, f32[72,768]{1,0:T(8,128)S(1)}, u32[]{:S(2)}, u32[]{:S(2)}) collective-permute-start(f32[72,768]{1,0:T(8,128)S(1)} %get-tuple-element.73), channel_id=1, source_target_pairs={{0,2},{1,3},{2,0},{3,1},{4,6},{5,7},{6,4},{7,5},{8,10},{9,11},{10,... | collective-permute-start | bytes 663560 | tf_op jit(solution)/shard_map/ppermute | solution.py:704
  27.1 10.4 %collective-permute-start.8 = (f32[72,768]{1,0:T(8,128)S(1)}, f32[72,768]{1,0:T(8,128)S(1)}, u32[]{:S(2)}, u32[]{:S(2)}) collective-permute-start(f32[72,768]{1,0:T(8,128)S(1)} %get-tuple-element.74), channel_id=1, source_target_pairs={{0,3},{1,2},{2,1},{3,0},{4,7},{5,6},{6,5},{7,4},{8,11},{9,10},{10,... | collective-permute-start | bytes 663560 | tf_op jit(solution)/shard_map/ppermute | solution.py:704
  28.8 11.0 %collective-permute-start.19 = (f32[32,768]{1,0:T(8,128)S(1)}, f32[32,768]{1,0:T(8,128)S(1)}, u32[]{:S(2)}, u32[]{:S(2)}) collective-permute-start(f32[32,768]{1,0:T(8,128)S(1)} %get-tuple-element.88), channel_id=1, source_target_pairs={{0,16},{4,20},{8,24},{12,28},{16,0},{20,4},{24,8},{28,12},{1,17},{... | collective-permute-start | bytes 294920 | tf_op jit(solution)/shard_map/ppermute | solution.py:704
  28.9 15.0 %collective-permute-start.20 = (f32[32,768]{1,0:T(8,128)S(1)}, f32[32,768]{1,0:T(8,128)S(1)}, u32[]{:S(2)}, u32[]{:S(2)}) collective-permute-start(f32[32,768]{1,0:T(8,128)S(1)} %get-tuple-element.89), channel_id=1, source_target_pairs={{0,4},{4,0},{8,12},{12,8},{16,20},{20,16},{24,28},{28,24},{1,5},{5... | collective-permute-start | bytes 294920 | tf_op jit(solution)/shard_map/ppermute | solution.py:704
  31.1 12.8 %collective-permute-start.21 = (f32[32,768]{1,0:T(8,128)S(1)}, f32[32,768]{1,0:T(8,128)S(1)}, u32[]{:S(2)}, u32[]{:S(2)}) collective-permute-start(f32[32,768]{1,0:T(8,128)S(1)} %get-tuple-element.90), channel_id=1, source_target_pairs={{0,20},{4,16},{8,28},{12,24},{16,4},{20,0},{24,12},{28,8},{1,21},{... | collective-permute-start | bytes 294920 | tf_op jit(solution)/shard_map/ppermute | solution.py:704
  33.6 11.6 %collective-permute-start.22 = (f32[32,768]{1,0:T(8,128)S(1)}, f32[32,768]{1,0:T(8,128)S(1)}, u32[]{:S(2)}, u32[]{:S(2)}) collective-permute-start(f32[32,768]{1,0:T(8,128)S(1)} %get-tuple-element.91), channel_id=1, source_target_pairs={{0,8},{4,12},{8,0},{12,4},{16,24},{20,28},{24,16},{28,20},{1,9},{5... | collective-permute-start | bytes 294920 | tf_op jit(solution)/shard_map/ppermute | solution.py:704
  37.5 12.3 %collective-permute-start.23 = (f32[32,768]{1,0:T(8,128)S(1)}, f32[32,768]{1,0:T(8,128)S(1)}, u32[]{:S(2)}, u32[]{:S(2)}) collective-permute-start(f32[32,768]{1,0:T(8,128)S(1)} %get-tuple-element.92), channel_id=1, source_target_pairs={{0,24},{4,28},{8,16},{12,20},{16,8},{20,12},{24,0},{28,4},{1,25},{... | collective-permute-start | bytes 294920 | tf_op jit(solution)/shard_map/ppermute | solution.py:704
  39.8 9.9 %collective-permute-start.24 = (f32[32,768]{1,0:T(8,128)S(1)}, f32[32,768]{1,0:T(8,128)S(1)}, u32[]{:S(2)}, u32[]{:S(2)}) collective-permute-start(f32[32,768]{1,0:T(8,128)S(1)} %get-tuple-element.93), channel_id=1, source_target_pairs={{0,28},{4,24},{8,20},{12,16},{16,12},{20,8},{24,4},{28,0},{1,29},{... | collective-permute-start | bytes 294920 | tf_op jit(solution)/shard_map/ppermute | solution.py:704
  43.9 7.0 %collective-permute-start.25 = (f32[32,768]{1,0:T(8,128)S(1)}, f32[32,768]{1,0:T(8,128)S(1)}, u32[]{:S(2)}, u32[]{:S(2)}) collective-permute-start(f32[32,768]{1,0:T(8,128)S(1)} %get-tuple-element.94), channel_id=1, source_target_pairs={{0,12},{4,8},{8,4},{12,0},{16,28},{20,24},{24,20},{28,16},{1,13},{... | collective-permute-start | bytes 294920 | tf_op jit(solution)/shard_map/ppermute | solution.py:704
  43.9 12.3 %collective-permute-start.9 = (f32[32,768]{1,0:T(8,128)S(1)}, f32[32,768]{1,0:T(8,128)S(1)}, u32[]{:S(2)}, u32[]{:S(2)}) collective-permute-start(f32[32,768]{1,0:T(8,128)S(1)} %get-tuple-element.76), channel_id=1, source_target_pairs={{0,16},{4,20},{8,24},{12,28},{16,0},{20,4},{24,8},{28,12},{1,17},{... | collective-permute-start | bytes 294920 | tf_op jit(solution)/shard_map/ppermute | solution.py:704
  45.2 14.1 %collective-permute-start.10 = (f32[32,768]{1,0:T(8,128)S(1)}, f32[32,768]{1,0:T(8,128)S(1)}, u32[]{:S(2)}, u32[]{:S(2)}) collective-permute-start(f32[32,768]{1,0:T(8,128)S(1)} %get-tuple-element.77), channel_id=1, source_target_pairs={{0,4},{4,0},{8,12},{12,8},{16,20},{20,16},{24,28},{28,24},{1,5},{5... | collective-permute-start | bytes 294920 | tf_op jit(solution)/shard_map/ppermute | solution.py:704
  49.7 10.9 %collective-permute-start.11 = (f32[32,768]{1,0:T(8,128)S(1)}, f32[32,768]{1,0:T(8,128)S(1)}, u32[]{:S(2)}, u32[]{:S(2)}) collective-permute-start(f32[32,768]{1,0:T(8,128)S(1)} %get-tuple-element.78), channel_id=1, source_target_pairs={{0,20},{4,16},{8,28},{12,24},{16,4},{20,0},{24,12},{28,8},{1,21},{... | collective-permute-start | bytes 294920 | tf_op jit(solution)/shard_map/ppermute | solution.py:704
  49.7 11.0 %collective-permute-start.12 = (f32[32,768]{1,0:T(8,128)S(1)}, f32[32,768]{1,0:T(8,128)S(1)}, u32[]{:S(2)}, u32[]{:S(2)}) collective-permute-start(f32[32,768]{1,0:T(8,128)S(1)} %get-tuple-element.79), channel_id=1, source_target_pairs={{0,8},{4,12},{8,0},{12,4},{16,24},{20,28},{24,16},{28,20},{1,9},{5... | collective-permute-start | bytes 294920 | tf_op jit(solution)/shard_map/ppermute | solution.py:704
  50.8 11.6 %collective-permute-start.13 = (f32[32,768]{1,0:T(8,128)S(1)}, f32[32,768]{1,0:T(8,128)S(1)}, u32[]{:S(2)}, u32[]{:S(2)}) collective-permute-start(f32[32,768]{1,0:T(8,128)S(1)} %get-tuple-element.80), channel_id=1, source_target_pairs={{0,24},{4,28},{8,16},{12,20},{16,8},{20,12},{24,0},{28,4},{1,25},{... | collective-permute-start | bytes 294920 | tf_op jit(solution)/shard_map/ppermute | solution.py:704
  56.2 8.0 %collective-permute-start.14 = (f32[32,768]{1,0:T(8,128)S(1)}, f32[32,768]{1,0:T(8,128)S(1)}, u32[]{:S(2)}, u32[]{:S(2)}) collective-permute-start(f32[32,768]{1,0:T(8,128)S(1)} %get-tuple-element.81), channel_id=1, source_target_pairs={{0,28},{4,24},{8,20},{12,16},{16,12},{20,8},{24,4},{28,0},{1,29},{... | collective-permute-start | bytes 294920 | tf_op jit(solution)/shard_map/ppermute | solution.py:704
  59.3 6.7 %collective-permute-start.15 = (f32[32,768]{1,0:T(8,128)S(1)}, f32[32,768]{1,0:T(8,128)S(1)}, u32[]{:S(2)}, u32[]{:S(2)}) collective-permute-start(f32[32,768]{1,0:T(8,128)S(1)} %get-tuple-element.82), channel_id=1, source_target_pairs={{0,12},{4,8},{8,4},{12,0},{16,28},{20,24},{24,20},{28,16},{1,13},{... | collective-permute-start | bytes 294920 | tf_op jit(solution)/shard_map/ppermute | solution.py:704
  60.7 6.7 %collective-permute-start.4 = (f32[48,256]{1,0:T(8,128)S(1)}, f32[48,256]{1,0:T(8,128)S(1)}, u32[]{:S(2)}, u32[]{:S(2)}) collective-permute-start(f32[48,256]{1,0:T(8,128)S(1)} %get-tuple-element.69), channel_id=1, source_target_pairs={{0,1},{1,2},{2,3},{3,0},{4,5},{5,6},{6,7},{7,4},{8,9},{9,10},{10,1... | collective-permute-start | bytes 147464 | tf_op jit(solution)/shard_map/ppermute | solution.py:762
  60.7 6.6 %collective-permute-start.5 = (f32[48,256]{1,0:T(8,128)S(1)}, f32[48,256]{1,0:T(8,128)S(1)}, u32[]{:S(2)}, u32[]{:S(2)}) collective-permute-start(f32[48,256]{1,0:T(8,128)S(1)} %get-tuple-element.70), channel_id=1, source_target_pairs={{0,3},{1,0},{2,1},{3,2},{4,7},{5,4},{6,5},{7,6},{8,11},{9,8},{10,9... | collective-permute-start | bytes 147464 | tf_op jit(solution)/shard_map/ppermute | solution.py:763
  71.1 9.3 %collective-permute-start.26 = (f32[32,768]{1,0:T(8,128)S(1)}, f32[32,768]{1,0:T(8,128)S(1)}, u32[]{:S(2)}, u32[]{:S(2)}) collective-permute-start(f32[32,768]{1,0:T(8,128)S(1)} %get-tuple-element.97), channel_id=1, source_target_pairs={{0,16},{4,20},{8,24},{12,28},{16,0},{20,4},{24,8},{28,12},{1,17},{... | collective-permute-start | bytes 294920 | tf_op jit(solution)/shard_map/ppermute | solution.py:704
  73.4 8.4 %collective-permute-start.27 = (f32[32,768]{1,0:T(8,128)S(1)}, f32[32,768]{1,0:T(8,128)S(1)}, u32[]{:S(2)}, u32[]{:S(2)}) collective-permute-start(f32[32,768]{1,0:T(8,128)S(1)} %get-tuple-element.98), channel_id=1, source_target_pairs={{0,4},{4,0},{8,12},{12,8},{16,20},{20,16},{24,28},{28,24},{1,5},{5... | collective-permute-start | bytes 294920 | tf_op jit(solution)/shard_map/ppermute | solution.py:704
  74.6 14.2 %collective-permute-start.28 = (f32[32,768]{1,0:T(8,128)S(1)}, f32[32,768]{1,0:T(8,128)S(1)}, u32[]{:S(2)}, u32[]{:S(2)}) collective-permute-start(f32[32,768]{1,0:T(8,128)S(1)} %get-tuple-element.99), channel_id=1, source_target_pairs={{0,20},{4,16},{8,28},{12,24},{16,4},{20,0},{24,12},{28,8},{1,21},{... | collective-permute-start | bytes 294920 | tf_op jit(solution)/shard_map/ppermute | solution.py:704
  75.6 13.2 %collective-permute-start.29 = (f32[32,768]{1,0:T(8,128)S(1)}, f32[32,768]{1,0:T(8,128)S(1)}, u32[]{:S(2)}, u32[]{:S(2)}) collective-permute-start(f32[32,768]{1,0:T(8,128)S(1)} %get-tuple-element.100), channel_id=1, source_target_pairs={{0,8},{4,12},{8,0},{12,4},{16,24},{20,28},{24,16},{28,20},{1,9},{5... | collective-permute-start | bytes 294920 | tf_op jit(solution)/shard_map/ppermute | solution.py:704
  76.8 13.1 %collective-permute-start.30 = (f32[32,768]{1,0:T(8,128)S(1)}, f32[32,768]{1,0:T(8,128)S(1)}, u32[]{:S(2)}, u32[]{:S(2)}) collective-permute-start(f32[32,768]{1,0:T(8,128)S(1)} %get-tuple-element.101), channel_id=1, source_target_pairs={{0,24},{4,28},{8,16},{12,20},{16,8},{20,12},{24,0},{28,4},{1,25},{... | collective-permute-start | bytes 294920 | tf_op jit(solution)/shard_map/ppermute | solution.py:704
  80.4 12.8 %collective-permute-start.31 = (f32[32,768]{1,0:T(8,128)S(1)}, f32[32,768]{1,0:T(8,128)S(1)}, u32[]{:S(2)}, u32[]{:S(2)}) collective-permute-start(f32[32,768]{1,0:T(8,128)S(1)} %get-tuple-element.102), channel_id=1, source_target_pairs={{0,28},{4,24},{8,20},{12,16},{16,12},{20,8},{24,4},{28,0},{1,29},{... | collective-permute-start | bytes 294920 | tf_op jit(solution)/shard_map/ppermute | solution.py:704
  81.8 15.0 %collective-permute-start.32 = (f32[32,768]{1,0:T(8,128)S(1)}, f32[32,768]{1,0:T(8,128)S(1)}, u32[]{:S(2)}, u32[]{:S(2)}) collective-permute-start(f32[32,768]{1,0:T(8,128)S(1)} %get-tuple-element.103), channel_id=1, source_target_pairs={{0,12},{4,8},{8,4},{12,0},{16,28},{20,24},{24,20},{28,16},{1,13},{... | collective-permute-start | bytes 294920 | tf_op jit(solution)/shard_map/ppermute | solution.py:704
  88.8 10.4 %collective-permute-start.36 = (f32[32,768]{1,0:T(8,128)S(1)}, f32[32,768]{1,0:T(8,128)S(1)}, u32[]{:S(2)}, u32[]{:S(2)}) collective-permute-start(f32[32,768]{1,0:T(8,128)S(1)} %get-tuple-element.114), channel_id=1, source_target_pairs={{0,16},{4,20},{8,24},{12,28},{16,0},{20,4},{24,8},{28,12},{1,17},{... | collective-permute-start | bytes 294920 | tf_op jit(solution)/shard_map/ppermute | solution.py:704
  88.8 10.9 %collective-permute-start.37 = (f32[32,768]{1,0:T(8,128)S(1)}, f32[32,768]{1,0:T(8,128)S(1)}, u32[]{:S(2)}, u32[]{:S(2)}) collective-permute-start(f32[32,768]{1,0:T(8,128)S(1)} %get-tuple-element.115), channel_id=1, source_target_pairs={{0,4},{4,0},{8,12},{12,8},{16,20},{20,16},{24,28},{28,24},{1,5},{5... | collective-permute-start | bytes 294920 | tf_op jit(solution)/shard_map/ppermute | solution.py:704
  89.9 10.8 %collective-permute-start.38 = (f32[32,768]{1,0:T(8,128)S(1)}, f32[32,768]{1,0:T(8,128)S(1)}, u32[]{:S(2)}, u32[]{:S(2)}) collective-permute-start(f32[32,768]{1,0:T(8,128)S(1)} %get-tuple-element.116), channel_id=1, source_target_pairs={{0,20},{4,16},{8,28},{12,24},{16,4},{20,0},{24,12},{28,8},{1,21},{... | collective-permute-start | bytes 294920 | tf_op jit(solution)/shard_map/ppermute | solution.py:704
  93.2 8.4 %collective-permute-start.39 = (f32[32,768]{1,0:T(8,128)S(1)}, f32[32,768]{1,0:T(8,128)S(1)}, u32[]{:S(2)}, u32[]{:S(2)}) collective-permute-start(f32[32,768]{1,0:T(8,128)S(1)} %get-tuple-element.117), channel_id=1, source_target_pairs={{0,8},{4,12},{8,0},{12,4},{16,24},{20,28},{24,16},{28,20},{1,9},{5... | collective-permute-start | bytes 294920 | tf_op jit(solution)/shard_map/ppermute | solution.py:704
  98.5 14.3 %collective-permute-start.33 = (f32[72,768]{1,0:T(8,128)S(1)}, f32[72,768]{1,0:T(8,128)S(1)}, u32[]{:S(2)}, u32[]{:S(2)}) collective-permute-start(f32[72,768]{1,0:T(8,128)S(1)} %get-tuple-element.105), channel_id=1, source_target_pairs={{0,2},{1,3},{2,0},{3,1},{4,6},{5,7},{6,4},{7,5},{8,10},{9,11},{10,... | collective-permute-start | bytes 663560 | tf_op jit(solution)/shard_map/ppermute | solution.py:704
  99.2 13.6 %collective-permute-start.34 = (f32[72,768]{1,0:T(8,128)S(1)}, f32[72,768]{1,0:T(8,128)S(1)}, u32[]{:S(2)}, u32[]{:S(2)}) collective-permute-start(f32[72,768]{1,0:T(8,128)S(1)} %get-tuple-element.106), channel_id=1, source_target_pairs={{0,3},{1,2},{2,1},{3,0},{4,7},{5,6},{6,5},{7,4},{8,11},{9,10},{10,... | collective-permute-start | bytes 663560 | tf_op jit(solution)/shard_map/ppermute | solution.py:704
  99.7 13.1 %collective-permute-start.35 = (f32[72,768]{1,0:T(8,128)S(1)}, f32[72,768]{1,0:T(8,128)S(1)}, u32[]{:S(2)}, u32[]{:S(2)}) collective-permute-start(f32[72,768]{1,0:T(8,128)S(1)} %get-tuple-element.107), channel_id=1, source_target_pairs={{0,1},{1,0},{2,3},{3,2},{4,5},{5,4},{6,7},{7,6},{8,9},{9,8},{10,11... | collective-permute-start | bytes 663560 | tf_op jit(solution)/shard_map/ppermute | solution.py:704
  100.7 7.6 %collective-permute-start.40 = (f32[32,768]{1,0:T(8,128)S(1)}, f32[32,768]{1,0:T(8,128)S(1)}, u32[]{:S(2)}, u32[]{:S(2)}) collective-permute-start(f32[32,768]{1,0:T(8,128)S(1)} %get-tuple-element.118), channel_id=1, source_target_pairs={{0,24},{4,28},{8,16},{12,20},{16,8},{20,12},{24,0},{28,4},{1,25},{... | collective-permute-start | bytes 294920 | tf_op jit(solution)/shard_map/ppermute | solution.py:704
  101.6 7.8 %collective-permute-start.41 = (f32[32,768]{1,0:T(8,128)S(1)}, f32[32,768]{1,0:T(8,128)S(1)}, u32[]{:S(2)}, u32[]{:S(2)}) collective-permute-start(f32[32,768]{1,0:T(8,128)S(1)} %get-tuple-element.119), channel_id=1, source_target_pairs={{0,28},{4,24},{8,20},{12,16},{16,12},{20,8},{24,4},{28,0},{1,29},{... | collective-permute-start | bytes 294920 | tf_op jit(solution)/shard_map/ppermute | solution.py:704
  109.4 6.0 %collective-permute-start.42 = (f32[32,768]{1,0:T(8,128)S(1)}, f32[32,768]{1,0:T(8,128)S(1)}, u32[]{:S(2)}, u32[]{:S(2)}) collective-permute-start(f32[32,768]{1,0:T(8,128)S(1)} %shard_map.152), channel_id=1, source_target_pairs={{0,12},{4,8},{8,4},{12,0},{16,28},{20,24},{24,20},{28,16},{1,13},{... | collective-permute-start | bytes 294920 | tf_op jit(solution)/shard_map/ppermute | solution.py:704
  117.1 8.3 %collective-permute-start.43 = (f32[72,768]{1,0:T(8,128)S(1)}, f32[72,768]{1,0:T(8,128)S(1)}, u32[]{:S(2)}, u32[]{:S(2)}) collective-permute-start(f32[72,768]{1,0:T(8,128)S(1)} %get-tuple-element.122), channel_id=1, source_target_pairs={{0,2},{1,3},{2,0},{3,1},{4,6},{5,7},{6,4},{7,5},{8,10},{9,11},{10,... | collective-permute-start | bytes 663560 | tf_op jit(solution)/shard_map/ppermute | solution.py:704
  117.8 8.2 %collective-permute-start.44 = (f32[72,768]{1,0:T(8,128)S(1)}, f32[72,768]{1,0:T(8,128)S(1)}, u32[]{:S(2)}, u32[]{:S(2)}) collective-permute-start(f32[72,768]{1,0:T(8,128)S(1)} %get-tuple-element.123), channel_id=1, source_target_pairs={{0,3},{1,2},{2,1},{3,0},{4,7},{5,6},{6,5},{7,4},{8,11},{9,10},{10,... | collective-permute-start | bytes 663560 | tf_op jit(solution)/shard_map/ppermute | solution.py:704
  117.8 8.2 %collective-permute-start.45 = (f32[72,768]{1,0:T(8,128)S(1)}, f32[72,768]{1,0:T(8,128)S(1)}, u32[]{:S(2)}, u32[]{:S(2)}) collective-permute-start(f32[72,768]{1,0:T(8,128)S(1)} %get-tuple-element.124), channel_id=1, source_target_pairs={{0,1},{1,0},{2,3},{3,2},{4,5},{5,4},{6,7},{7,6},{8,9},{9,8},{10,11... | collective-permute-start | bytes 663560 | tf_op jit(solution)/shard_map/ppermute | solution.py:704
  119.3 11.3 %collective-permute-start.47 = (f32[3,64,256]{2,1,0:T(8,128)S(1)}, f32[3,64,256]{2,1,0:T(8,128)S(1)}, u32[]{:S(2)}, u32[]{:S(2)}) collective-permute-start(f32[3,64,256]{2,1,0:T(8,128)S(1)} %get-tuple-element.111.refs_0_), channel_id=1, source_target_pairs={{0,28},{4,0},{8,4},{12,8},{16,12},{20,16},{24,20},{28,24},{1,29},{... | collective-permute-start | bytes 589832 | tf_op jit(solution)/shard_map/ppermute | solution.py:833
  121.3 9.2 %collective-permute-start.46 = (f32[3,64,256]{2,1,0:T(8,128)S(1)}, f32[3,64,256]{2,1,0:T(8,128)S(1)}, u32[]{:S(2)}, u32[]{:S(2)}) collective-permute-start(f32[3,64,256]{2,1,0:T(8,128)S(1)} %get-tuple-element.127), channel_id=1, source_target_pairs={{0,4},{4,8},{8,12},{12,16},{16,20},{20,24},{24,28},{28,0},{1,5},{5... | collective-permute-start | bytes 589832 | tf_op jit(solution)/shard_map/ppermute | solution.py:834
  (9 other events, 116.1 us)

commit v15 on v13

--- a/solution.py
+++ b/solution.py
@@ -148,11 +148,12 @@
         return [0] + near + far
     if first == "far":
         return [0] + far + near
-    order = [0]
+    order, last = [0], near[2:]
+    near = near[:2]
     while far or near:
         order += far[:1] + near[:1]
         far, near = far[1:], near[1:]
-    return order
+    return order + last
 
 
 def blocks_of(refs, at, first=None):

time: 132 us -> 129 us (0.977)
  starting transfers between devices: 72.9 us -> 68.7 us
  waiting for transfers between devices: 27.3 us -> 28.7 us
    ppermute x40, waiting for transfers between devices: 21.2 us -> 25.4 us  [exchange(): lax.ppermute(block, axis, [(i, i ^ k) for i in range(count)])]
    ppermute x40, starting transfers between devices: 56.4 us -> 52.2 us  [exchange(): lax.ppermute(block, axis, [(i, i ^ k) for i in range(count)])]
    ppermute x1, starting transfers between devices: 0.37 us -> 4.35 us  [on_device(): after = lax.ppermute(first, 'gz', ring('gz', -1))]
    ppermute x1, starting transfers between devices: 4.4 us -> 0.42 us  [on_device(): before = lax.ppermute(last, 'gz', ring('gz', 1))]
    ppermute x1, waiting for transfers between devices: 2.82 us -> 0.01 us  [on_device(): before = lax.ppermute(last, 'gz', ring('gz', 1))]
where the time goes in v15:
time: 129 us
  starting transfers between devices  68.7 us (53%)
  Pallas kernels  30.6 us (24%)
  waiting for transfers between devices  28.7 us (22%)
    ppermute x40, starting transfers between devices, exchange(): lax.ppermute(block, axis, [(i, i ^ k) for i in range(count)])  52.2 us
    pallas_call x16, Pallas kernels, call(): pl.pallas_call(kernel, out_shape=[jax.ShapeDtypeStruct(shape, F32) for _,...  30.6 us
    ppermute x40, waiting for transfers between devices, exchange(): lax.ppermute(block, axis, [(i, i ^ k) for i in range(count)])  25.4 us
    ppermute x1, starting transfers between devices, on_device(): after = lax.ppermute(first, 'gz', ring('gz', -1))  4.35 us
    ppermute x1, starting transfers between devices, on_device(): down2 = lax.ppermute(movers, 'gz', ring('gz', 2))  3.08 us
    ppermute x1, starting transfers between devices, on_device(): up1 = lax.ppermute(packet, 'gz', ring('gz', -1))  3.08 us
  transfers between devices with their start and end apart: 48, of which 16 were waited for; matrix products, arithmetic and copies ran while one was open for 0% of the time, Pallas kernels for 16%

profile of v15, /device:TPU:0, one launch (start us, length us, event | category | flops | bytes accessed | tf_op | source)
XLA Modules:
  0.0 129.3 jit_solution(6825684214951352916)
XLA Ops:
  1.8 3.1 %collective-permute-start.3 = (f32[8,128]{1,0:T(8,128)S(1)}, f32[8,128]{1,0:T(8,128)S(1)}, u32[]{:S(2)}, u32[]{:S(2)}) collective-permute-start(f32[8,128]{1,0:T(8,128)S(1)} %get-tuple-element.69), channel_id=1, source_target_pairs={{0,8},{4,12},{8,16},{12,20},{16,24},{20,28},{24,0},{28,4},{1,9},{5... | collective-permute-start | bytes 12296 | tf_op jit(solution)/shard_map/ppermute | solution.py:740
  4.8 2.1 %collective-permute-start.2 = (f32[8,128]{1,0:T(8,128)S(1)}, f32[8,128]{1,0:T(8,128)S(1)}, u32[]{:S(2)}, u32[]{:S(2)}) collective-permute-start(f32[8,128]{1,0:T(8,128)S(1)} %get-tuple-element.69), channel_id=1, source_target_pairs={{0,24},{4,28},{8,0},{12,4},{16,8},{20,12},{24,16},{28,20},{1,25},{... | collective-permute-start | bytes 12296 | tf_op jit(solution)/shard_map/ppermute | solution.py:739
  6.9 1.6 %collective-permute-start.1 = (f32[8,512]{1,0:T(8,128)S(1)}, f32[8,512]{1,0:T(8,128)S(1)}, u32[]{:S(2)}, u32[]{:S(2)}) collective-permute-start(f32[8,512]{1,0:T(8,128)S(1)} %get-tuple-element.68.own), channel_id=1, source_target_pairs={{0,4},{4,8},{8,12},{12,16},{16,20},{20,24},{24,28},{28,0},{1,5},{5... | collective-permute-start | bytes 49160 | tf_op jit(solution)/shard_map/ppermute | solution.py:738
  8.6 3.1 %collective-permute-start = (f32[8,512]{1,0:T(8,128)S(1)}, f32[8,512]{1,0:T(8,128)S(1)}, u32[]{:S(2)}, u32[]{:S(2)}) collective-permute-start(f32[8,512]{1,0:T(8,128)S(1)} %get-tuple-element.68.own), channel_id=1, source_target_pairs={{0,28},{4,0},{8,4},{12,8},{16,12},{20,16},{24,20},{28,24},{1,29},{... | collective-permute-start | bytes 49160 | tf_op jit(solution)/shard_map/ppermute | solution.py:737
  11.7 1.6 %collective-permute-done.1.down1 = f32[8,512]{1,0:T(8,128)S(1)} collective-permute-done((f32[8,512]{1,0:T(8,128)S(1)}, f32[8,512]{1,0:T(8,128)S(1)}, u32[]{:S(2)}, u32[]{:S(2)}) %collective-permute-start.1) | collective-permute-done | bytes 16416 | tf_op jit(solution)/shard_map/ppermute | solution.py:738
  13.4 3.7 %shard_map.141 = (f32[3,4,64,256]{3,2,1,0:T(8,128)S(1)}, f32[24,256]{1,0:T(8,128)S(1)}, f32[24,256]{1,0:T(8,128)S(1)}, f32[72,768]{1,0:T(8,128)S(1)}, f32[72,768...) custom-call(s32[2]{0:T(128)S(1)} %pad_add_fusion.place, f32[8,512]{1,0:T(8,128)S(1)} %get-tuple-element.68.own, ...), custom_call_target="tpu_custom_call" | custom-call | flops 5000000000 | bytes 15000000 | tf_op jit(solution)/shard_map/pallas_call | solution.py:667
  17.1 1.7 %collective-permute-start.16 = (f32[72,768]{1,0:T(8,128)S(1)}, f32[72,768]{1,0:T(8,128)S(1)}, u32[]{:S(2)}, u32[]{:S(2)}) collective-permute-start(f32[72,768]{1,0:T(8,128)S(1)} %get-tuple-element.87), channel_id=1, source_target_pairs={{0,2},{1,3},{2,0},{3,1},{4,6},{5,7},{6,4},{7,5},{8,10},{9,11},{10,... | collective-permute-start | bytes 663560 | tf_op jit(solution)/shard_map/ppermute | solution.py:703
  19.3 6.0 %shard_map.142 = (f32[3,4,64,256]{3,2,1,0:T(8,128)S(1)}, f32[48,256]{1,0:T(8,128)S(1)}, f32[48,256]{1,0:T(8,128)S(1)}, f32[72,768]{1,0:T(8,128)S(1)}, f32[72,768...) custom-call(s32[2]{0:T(128)S(1)} %pad_add_fusion.place, f32[8,512]{1,0:T(8,128)S(1)} %get-tuple-element.68.own, ...), custom_call_target="tpu_custom_call" | custom-call | flops 5000000000 | bytes 15000000 | tf_op jit(solution)/shard_map/pallas_call | solution.py:667
  25.4 1.7 %collective-permute-start.7 = (f32[72,768]{1,0:T(8,128)S(1)}, f32[72,768]{1,0:T(8,128)S(1)}, u32[]{:S(2)}, u32[]{:S(2)}) collective-permute-start(f32[72,768]{1,0:T(8,128)S(1)} %get-tuple-element.76), channel_id=1, source_target_pairs={{0,2},{1,3},{2,0},{3,1},{4,6},{5,7},{6,4},{7,5},{8,10},{9,11},{10,... | collective-permute-start | bytes 663560 | tf_op jit(solution)/shard_map/ppermute | solution.py:703
  27.2 1.6 %shard_map.145 = (f32[32,768]{1,0:T(8,128)S(1)}, f32[32,768]{1,0:T(8,128)S(1)}, f32[32,768]{1,0:T(8,128)S(1)}, f32[32,768]{1,0:T(8,128)S(1)}, f32[32,768]{1,0:T(...) custom-call(s32[2]{0:T(128)S(1)} %pad_add_fusion.place, ...), custom_call_target="tpu_custom_call" | custom-call | flops 2000000000 | bytes 6000000 | tf_op jit(solution)/shard_map/pallas_call | solution.py:667
  28.9 2.2 %collective-permute-start.20 = (f32[32,768]{1,0:T(8,128)S(1)}, f32[32,768]{1,0:T(8,128)S(1)}, u32[]{:S(2)}, u32[]{:S(2)}) collective-permute-start(f32[32,768]{1,0:T(8,128)S(1)} %get-tuple-element.92), channel_id=1, source_target_pairs={{0,4},{4,0},{8,12},{12,8},{16,20},{20,16},{24,28},{28,24},{1,5},{5... | collective-permute-start | bytes 294920 | tf_op jit(solution)/shard_map/ppermute | solution.py:703
  31.1 2.2 %collective-permute-start.21 = (f32[32,768]{1,0:T(8,128)S(1)}, f32[32,768]{1,0:T(8,128)S(1)}, u32[]{:S(2)}, u32[]{:S(2)}) collective-permute-start(f32[32,768]{1,0:T(8,128)S(1)} %get-tuple-element.93), channel_id=1, source_target_pairs={{0,20},{4,16},{8,28},{12,24},{16,4},{20,0},{24,12},{28,8},{1,21},{... | collective-permute-start | bytes 294920 | tf_op jit(solution)/shard_map/ppermute | solution.py:703
  34.8 2.6 %collective-permute-done.8.refs_3_ = f32[72,768]{1,0:T(8,128)S(1)} collective-permute-done((f32[72,768]{1,0:T(8,128)S(1)}, f32[72,768]{1,0:T(8,128)S(1)}, u32[]{:S(2)}, u32[]{:S(2)}) %collective-permute-start.8) | collective-permute-done | bytes 221216 | tf_op jit(solution)/shard_map/ppermute | solution.py:703
  38.2 1.6 %shard_map.143 = (f32[32,768]{1,0:T(8,128)S(1)}, f32[32,768]{1,0:T(8,128)S(1)}, f32[32,768]{1,0:T(8,128)S(1)}, f32[32,768]{1,0:T(8,128)S(1)}, f32[32,768]{1,0:T(...) custom-call(s32[2]{0:T(128)S(1)} %pad_add_fusion.place, ...), custom_call_target="tpu_custom_call" | custom-call | flops 2000000000 | bytes 6000000 | tf_op jit(solution)/shard_map/pallas_call | solution.py:667
  39.8 4.0 %collective-permute-start.24 = (f32[32,768]{1,0:T(8,128)S(1)}, f32[32,768]{1,0:T(8,128)S(1)}, u32[]{:S(2)}, u32[]{:S(2)}) collective-permute-start(f32[32,768]{1,0:T(8,128)S(1)} %get-tuple-element.96), channel_id=1, source_target_pairs={{0,28},{4,24},{8,20},{12,16},{16,12},{20,8},{24,4},{28,0},{1,29},{... | collective-permute-start | bytes 294920 | tf_op jit(solution)/shard_map/ppermute | solution.py:703
  43.9 1.3 %collective-permute-start.9 = (f32[32,768]{1,0:T(8,128)S(1)}, f32[32,768]{1,0:T(8,128)S(1)}, u32[]{:S(2)}, u32[]{:S(2)}) collective-permute-start(f32[32,768]{1,0:T(8,128)S(1)} %get-tuple-element.79), channel_id=1, source_target_pairs={{0,16},{4,20},{8,24},{12,28},{16,0},{20,4},{24,8},{28,12},{1,17},{... | collective-permute-start | bytes 294920 | tf_op jit(solution)/shard_map/ppermute | solution.py:703
  45.2 4.5 %collective-permute-start.10 = (f32[32,768]{1,0:T(8,128)S(1)}, f32[32,768]{1,0:T(8,128)S(1)}, u32[]{:S(2)}, u32[]{:S(2)}) collective-permute-start(f32[32,768]{1,0:T(8,128)S(1)} %get-tuple-element.80), channel_id=1, source_target_pairs={{0,4},{4,0},{8,12},{12,8},{16,20},{20,16},{24,28},{28,24},{1,5},{5... | collective-permute-start | bytes 294920 | tf_op jit(solution)/shard_map/ppermute | solution.py:703
  50.8 5.4 %collective-permute-start.13 = (f32[32,768]{1,0:T(8,128)S(1)}, f32[32,768]{1,0:T(8,128)S(1)}, u32[]{:S(2)}, u32[]{:S(2)}) collective-permute-start(f32[32,768]{1,0:T(8,128)S(1)} %get-tuple-element.83), channel_id=1, source_target_pairs={{0,24},{4,28},{8,16},{12,20},{16,8},{20,12},{24,0},{28,4},{1,25},{... | collective-permute-start | bytes 294920 | tf_op jit(solution)/shard_map/ppermute | solution.py:703
  56.3 3.0 %collective-permute-start.14 = (f32[32,768]{1,0:T(8,128)S(1)}, f32[32,768]{1,0:T(8,128)S(1)}, u32[]{:S(2)}, u32[]{:S(2)}) collective-permute-start(f32[32,768]{1,0:T(8,128)S(1)} %get-tuple-element.84), channel_id=1, source_target_pairs={{0,28},{4,24},{8,20},{12,16},{16,12},{20,8},{24,4},{28,0},{1,29},{... | collective-permute-start | bytes 294920 | tf_op jit(solution)/shard_map/ppermute | solution.py:703
  59.3 1.3 %shard_map.146.refs_1_ = f32[3,2,4,8,8,128]{5,4,3,2,1,0:T(8,128)S(1)} custom-call(s32[2]{0:T(128)S(1)} %pad_add_fusion.place, f32[32,768]{1,0:T(8,128)S(1)} %get-tuple-element.90.refs_0_, f32[32,768]{1,0:T(8,128)S(1)} %collective-permute-done.19.refs_1_, f32[32,768]{1,0:T(8,128)S(1)} %collective-permute-done.20.refs_2_, ...), custom_call_target="tpu_custom_call" | custom-call | flops 2000000000 | bytes 6000000 | tf_op jit(solution)/shard_map/pallas_call | solution.py:667
  60.7 1.7 %collective-permute-start.5 = (f32[48,256]{1,0:T(8,128)S(1)}, f32[48,256]{1,0:T(8,128)S(1)}, u32[]{:S(2)}, u32[]{:S(2)}) collective-permute-start(f32[48,256]{1,0:T(8,128)S(1)} %get-tuple-element.73), channel_id=1, source_target_pairs={{0,3},{1,0},{2,1},{3,2},{4,7},{5,4},{6,5},{7,6},{8,11},{9,8},{10,9... | collective-permute-start | bytes 147464 | tf_op jit(solution)/shard_map/ppermute | solution.py:762
  62.5 1.8 %collective-permute-done.14.refs_6_ = f32[32,768]{1,0:T(8,128)S(1)} collective-permute-done((f32[32,768]{1,0:T(8,128)S(1)}, f32[32,768]{1,0:T(8,128)S(1)}, u32[]{:S(2)}, u32[]{:S(2)}) %collective-permute-start.14) | collective-permute-done | bytes 98336 | tf_op jit(solution)/shard_map/ppermute | solution.py:703
  64.3 1.7 %collective-permute-done.15.refs_7_ = f32[32,768]{1,0:T(8,128)S(1)} collective-permute-done((f32[32,768]{1,0:T(8,128)S(1)}, f32[32,768]{1,0:T(8,128)S(1)}, u32[]{:S(2)}, u32[]{:S(2)}) %collective-permute-start.15) | collective-permute-done | bytes 98336 | tf_op jit(solution)/shard_map/ppermute | solution.py:703
  66.0 1.3 %shard_map.144.refs_0_ = f32[3,2,4,8,8,128]{5,4,3,2,1,0:T(8,128)S(1)} custom-call(s32[2]{0:T(128)S(1)} %pad_add_fusion.place, f32[32,768]{1,0:T(8,128)S(1)} %get-tuple-element.78.refs_0_, f32[32,768]{1,0:T(8,128)S(1)} %collective-permute-done.9.refs_1_, f32[32,768]{1,0:T(8,128)S(1)} %collective-permute-done.10.refs_2_, ...), custom_call_target="tpu_custom_call" | custom-call | flops 2000000000 | bytes 6000000 | tf_op jit(solution)/shard_map/pallas_call | solution.py:667
  67.4 2.3 %shard_map.147 = (f32[3,2,4,8,8,128]{5,4,3,2,1,0:T(8,128)S(1)}, f32[3,2,4,8,8,128]{5,4,3,2,1,0:T(8,128)S(1)}) custom-call(s32[2]{0:T(128)S(1)} %pad_add_fusion.place, f32[48,256]{1,0:T(8,128)S(1)} %collective-permute-done.4.low_rim.refs_1_, f32[48,256]{1,0:T(8,128)S(1)} %collective-permute-done.5.high_rim.refs_2_, ...), custom_call_target="tpu_custom_call" | custom-call | flops 5000000000 | bytes 15000000 | tf_op jit(solution)/shard_map/pallas_call | solution.py:667
  69.7 1.4 %shard_map.148 = (f32[32,768]{1,0:T(8,128)S(1)}, f32[32,768]{1,0:T(8,128)S(1)}, f32[32,768]{1,0:T(8,128)S(1)}, f32[32,768]{1,0:T(8,128)S(1)}, f32[32,768]{1,0:T(...) custom-call(s32[2]{0:T(128)S(1)} %pad_add_fusion.place, ...), custom_call_target="tpu_custom_call" | custom-call | flops 2000000000 | bytes 6000000 | tf_op jit(solution)/shard_map/pallas_call | solution.py:667
  71.1 2.2 %collective-permute-start.26 = (f32[32,768]{1,0:T(8,128)S(1)}, f32[32,768]{1,0:T(8,128)S(1)}, u32[]{:S(2)}, u32[]{:S(2)}) collective-permute-start(f32[32,768]{1,0:T(8,128)S(1)} %get-tuple-element.100), channel_id=1, source_target_pairs={{0,16},{4,20},{8,24},{12,28},{16,0},{20,4},{24,8},{28,12},{1,17},{... | collective-permute-start | bytes 294920 | tf_op jit(solution)/shard_map/ppermute | solution.py:703
  73.3 1.2 collective-permute-start.27
  76.8 2.4 %collective-permute-start.30 = (f32[32,768]{1,0:T(8,128)S(1)}, f32[32,768]{1,0:T(8,128)S(1)}, u32[]{:S(2)}, u32[]{:S(2)}) collective-permute-start(f32[32,768]{1,0:T(8,128)S(1)} %get-tuple-element.104), channel_id=1, source_target_pairs={{0,24},{4,28},{8,16},{12,20},{16,8},{20,12},{24,0},{28,4},{1,25},{... | collective-permute-start | bytes 294920 | tf_op jit(solution)/shard_map/ppermute | solution.py:703
  79.2 1.2 collective-permute-done.26.refs_1_
  80.4 1.4 %collective-permute-start.31 = (f32[32,768]{1,0:T(8,128)S(1)}, f32[32,768]{1,0:T(8,128)S(1)}, u32[]{:S(2)}, u32[]{:S(2)}) collective-permute-start(f32[32,768]{1,0:T(8,128)S(1)} %get-tuple-element.105), channel_id=1, source_target_pairs={{0,28},{4,24},{8,20},{12,16},{16,12},{20,8},{24,4},{28,0},{1,29},{... | collective-permute-start | bytes 294920 | tf_op jit(solution)/shard_map/ppermute | solution.py:703
  81.8 1.4 %shard_map.151 = (f32[32,768]{1,0:T(8,128)S(1)}, f32[32,768]{1,0:T(8,128)S(1)}, f32[32,768]{1,0:T(8,128)S(1)}, f32[32,768]{1,0:T(8,128)S(1)}, f32[32,768]{1,0:T(...) custom-call(s32[2]{0:T(128)S(1)} %pad_add_fusion.place, ...), custom_call_target="tpu_custom_call" | custom-call | flops 2000000000 | bytes 6000000 | tf_op jit(solution)/shard_map/pallas_call | solution.py:667
  83.2 5.6 %collective-permute-done.28.refs_3_ = f32[32,768]{1,0:T(8,128)S(1)} collective-permute-done((f32[32,768]{1,0:T(8,128)S(1)}, f32[32,768]{1,0:T(8,128)S(1)}, u32[]{:S(2)}, u32[]{:S(2)}) %collective-permute-start.28) | collective-permute-done | bytes 98336 | tf_op jit(solution)/shard_map/ppermute | solution.py:703
  89.9 3.3 %collective-permute-start.38 = (f32[32,768]{1,0:T(8,128)S(1)}, f32[32,768]{1,0:T(8,128)S(1)}, u32[]{:S(2)}, u32[]{:S(2)}) collective-permute-start(f32[32,768]{1,0:T(8,128)S(1)} %get-tuple-element.118), channel_id=1, source_target_pairs={{0,20},{4,16},{8,28},{12,24},{16,4},{20,0},{24,12},{28,8},{1,21},{... | collective-permute-start | bytes 294920 | tf_op jit(solution)/shard_map/ppermute | solution.py:703
  93.2 2.5 %collective-permute-start.39 = (f32[32,768]{1,0:T(8,128)S(1)}, f32[32,768]{1,0:T(8,128)S(1)}, u32[]{:S(2)}, u32[]{:S(2)}) collective-permute-start(f32[32,768]{1,0:T(8,128)S(1)} %get-tuple-element.119), channel_id=1, source_target_pairs={{0,8},{4,12},{8,0},{12,4},{16,24},{20,28},{24,16},{28,20},{1,9},{5... | collective-permute-start | bytes 294920 | tf_op jit(solution)/shard_map/ppermute | solution.py:703
  95.8 1.7 %shard_map.149 = (f32[72,768]{1,0:T(8,128)S(1)}, f32[72,768]{1,0:T(8,128)S(1)}, f32[72,768]{1,0:T(8,128)S(1)}, f32[72,768]{1,0:T(8,128)S(1)}) custom-call(s32[2]{0:T(128)S(1)} %pad_add_fusion.place, bf16[576,256]{1,0:T(8,128)(2,1)S(1)} %copy-done.6, bf16[576,256]{1,0:T(8,128)(2,1)S(1)} %copy-done.5, f32[32,768]{1,0:T(8,128)S(1)} %get-tuple-element.99.refs_0_, ...), custom_call_target="tpu_custom_call" | custom-call | flops 2000000000 | bytes 6000000 | tf_op jit(solution)/shard_map/pallas_call | solution.py:667
  97.7 1.8 %collective-permute-start.41 = (f32[32,768]{1,0:T(8,128)S(1)}, f32[32,768]{1,0:T(8,128)S(1)}, u32[]{:S(2)}, u32[]{:S(2)}) collective-permute-start(f32[32,768]{1,0:T(8,128)S(1)} %get-tuple-element.124), channel_id=1, source_target_pairs={{0,28},{4,24},{8,20},{12,16},{16,12},{20,8},{24,4},{28,0},{1,29},{... | collective-permute-start | bytes 294920 | tf_op jit(solution)/shard_map/ppermute | solution.py:703
  100.5 2.1 %collective-permute-done.38.refs_3_ = f32[32,768]{1,0:T(8,128)S(1)} collective-permute-done((f32[32,768]{1,0:T(8,128)S(1)}, f32[32,768]{1,0:T(8,128)S(1)}, u32[]{:S(2)}, u32[]{:S(2)}) %collective-permute-start.38) | collective-permute-done | bytes 98336 | tf_op jit(solution)/shard_map/ppermute | solution.py:703
  103.5 1.6 %collective-permute-done.40.refs_5_ = f32[32,768]{1,0:T(8,128)S(1)} collective-permute-done((f32[32,768]{1,0:T(8,128)S(1)}, f32[32,768]{1,0:T(8,128)S(1)}, u32[]{:S(2)}, u32[]{:S(2)}) %collective-permute-start.40) | collective-permute-done | bytes 98336 | tf_op jit(solution)/shard_map/ppermute | solution.py:703
  105.9 1.8 %collective-permute-done.42.refs_7_ = f32[32,768]{1,0:T(8,128)S(1)} collective-permute-done((f32[32,768]{1,0:T(8,128)S(1)}, f32[32,768]{1,0:T(8,128)S(1)}, u32[]{:S(2)}, u32[]{:S(2)}) %collective-permute-start.42) | collective-permute-done | bytes 98336 | tf_op jit(solution)/shard_map/ppermute | solution.py:703
  107.7 1.7 %shard_map.153 = (f32[72,768]{1,0:T(8,128)S(1)}, f32[72,768]{1,0:T(8,128)S(1)}, f32[72,768]{1,0:T(8,128)S(1)}, f32[72,768]{1,0:T(8,128)S(1)}) custom-call(s32[2]{0:T(128)S(1)} %pad_add_fusion.place, bf16[576,256]{1,0:T(8,128)(2,1)S(1)} %copy-done.6, bf16[576,256]{1,0:T(8,128)(2,1)S(1)} %copy-done.5, f32[32,768]{1,0:T(8,128)S(1)} %get-tuple-element.115.refs_0_, ...), custom_call_target="tpu_custom_call" | custom-call | flops 2000000000 | bytes 6000000 | tf_op jit(solution)/shard_map/pallas_call | solution.py:667
  109.4 1.2 collective-permute-start.43
  111.6 2.2 %collective-permute-done.35.refs_3_ = f32[72,768]{1,0:T(8,128)S(1)} collective-permute-done((f32[72,768]{1,0:T(8,128)S(1)}, f32[72,768]{1,0:T(8,128)S(1)}, u32[]{:S(2)}, u32[]{:S(2)}) %collective-permute-start.35) | collective-permute-done | bytes 221216 | tf_op jit(solution)/shard_map/ppermute | solution.py:703
  113.8 1.5 %shard_map.150 = (f32[3,4,80,256]{3,2,1,0:T(8,128)S(1)}, f32[3,64,256]{2,1,0:T(8,128)S(1)}, f32[3,64,256]{2,1,0:T(8,128)S(1)}) custom-call(s32[2]{0:T(128)S(1)} %pad_add_fusion.place, bf16[512,512]{1,0:T(8,128)(2,1)S(1)} %copy-done.2, bf16[512,512]{1,0:T(8,128)(2,1)S(1)} %copy-done.1, f32[72,768]{1,0:T(8,128)S(1)} %get-tuple-element.107.refs_0_.before, ...), custom_call_target="tpu_custom_call" | custom-call | flops 2000000000 | bytes 6000000 | tf_op jit(solution)/shard_map/pallas_call | solution.py:667
  115.7 4.4 %collective-permute-start.47 = (f32[3,64,256]{2,1,0:T(8,128)S(1)}, f32[3,64,256]{2,1,0:T(8,128)S(1)}, u32[]{:S(2)}, u32[]{:S(2)}) collective-permute-start(f32[3,64,256]{2,1,0:T(8,128)S(1)} %get-tuple-element.133), channel_id=1, source_target_pairs={{0,28},{4,0},{8,4},{12,8},{16,12},{20,16},{24,20},{28,24},{1,29},{... | collective-permute-start | bytes 589832 | tf_op jit(solution)/shard_map/ppermute | solution.py:831
  120.4 3.0 %collective-permute-done.44.refs_7_ = f32[72,768]{1,0:T(8,128)S(1)} collective-permute-done((f32[72,768]{1,0:T(8,128)S(1)}, f32[72,768]{1,0:T(8,128)S(1)}, u32[]{:S(2)}, u32[]{:S(2)}) %collective-permute-start.44) | collective-permute-done | bytes 221216 | tf_op jit(solution)/shard_map/ppermute | solution.py:703
  123.3 3.0 %shard_map.154 = (f32[3,8,64,256]{3,2,1,0:T(8,128)}, f32[3,8,64,256]{3,2,1,0:T(8,128)}) custom-call(s32[2]{0:T(128)S(1)} %pad_add_fusion.place, bf16[512,512]{1,0:T(8,128)(2,1)S(1)} %copy-done.2, bf16[512,512]{1,0:T(8,128)(2,1)S(1)} %copy-done.1, f32[3,4,80,256]{3,2,1,0:T(8,128)S(1)} %get-tuple-element.111.refs_0_.edges, ...), custom_call_target="tpu_custom_call" | custom-call | flops 4000000000 | bytes 12000000 | tf_op jit(solution)/shard_map/pallas_call | solution.py:667
  126.3 1.7 %collective-permute-done.47.after = f32[3,64,256]{2,1,0:T(8,128)S(1)} collective-permute-done((f32[3,64,256]{2,1,0:T(8,128)S(1)}, f32[3,64,256]{2,1,0:T(8,128)S(1)}, u32[]{:S(2)}, u32[]{:S(2)}) %collective-permute-start.47) | collective-permute-done | bytes 196640 | tf_op jit(solution)/shard_map/ppermute | solution.py:831
  (83 shorter events, 14.5 us)
Async XLA Ops:
  1.8 10.0 %collective-permute-start.3 = (f32[8,128]{1,0:T(8,128)S(1)}, f32[8,128]{1,0:T(8,128)S(1)}, u32[]{:S(2)}, u32[]{:S(2)}) collective-permute-start(f32[8,128]{1,0:T(8,128)S(1)} %get-tuple-element.69), channel_id=1, source_target_pairs={{0,8},{4,12},{8,16},{12,20},{16,24},{20,28},{24,0},{28,4},{1,9},{5... | collective-permute-start | bytes 12296 | tf_op jit(solution)/shard_map/ppermute | solution.py:740
  4.8 6.9 %collective-permute-start.2 = (f32[8,128]{1,0:T(8,128)S(1)}, f32[8,128]{1,0:T(8,128)S(1)}, u32[]{:S(2)}, u32[]{:S(2)}) collective-permute-start(f32[8,128]{1,0:T(8,128)S(1)} %get-tuple-element.69), channel_id=1, source_target_pairs={{0,24},{4,28},{8,0},{12,4},{16,8},{20,12},{24,16},{28,20},{1,25},{... | collective-permute-start | bytes 12296 | tf_op jit(solution)/shard_map/ppermute | solution.py:739
  6.9 6.4 %collective-permute-start.1 = (f32[8,512]{1,0:T(8,128)S(1)}, f32[8,512]{1,0:T(8,128)S(1)}, u32[]{:S(2)}, u32[]{:S(2)}) collective-permute-start(f32[8,512]{1,0:T(8,128)S(1)} %get-tuple-element.68.own), channel_id=1, source_target_pairs={{0,4},{4,8},{8,12},{12,16},{16,20},{20,24},{24,28},{28,0},{1,5},{5... | collective-permute-start | bytes 49160 | tf_op jit(solution)/shard_map/ppermute | solution.py:738
  8.6 4.8 %collective-permute-start = (f32[8,512]{1,0:T(8,128)S(1)}, f32[8,512]{1,0:T(8,128)S(1)}, u32[]{:S(2)}, u32[]{:S(2)}) collective-permute-start(f32[8,512]{1,0:T(8,128)S(1)} %get-tuple-element.68.own), channel_id=1, source_target_pairs={{0,28},{4,0},{8,4},{12,8},{16,12},{20,16},{24,20},{28,24},{1,29},{... | collective-permute-start | bytes 49160 | tf_op jit(solution)/shard_map/ppermute | solution.py:737
  17.1 10.0 %collective-permute-start.16 = (f32[72,768]{1,0:T(8,128)S(1)}, f32[72,768]{1,0:T(8,128)S(1)}, u32[]{:S(2)}, u32[]{:S(2)}) collective-permute-start(f32[72,768]{1,0:T(8,128)S(1)} %get-tuple-element.87), channel_id=1, source_target_pairs={{0,2},{1,3},{2,0},{3,1},{4,6},{5,7},{6,4},{7,5},{8,10},{9,11},{10,... | collective-permute-start | bytes 663560 | tf_op jit(solution)/shard_map/ppermute | solution.py:703
  18.8 8.4 %collective-permute-start.17 = (f32[72,768]{1,0:T(8,128)S(1)}, f32[72,768]{1,0:T(8,128)S(1)}, u32[]{:S(2)}, u32[]{:S(2)}) collective-permute-start(f32[72,768]{1,0:T(8,128)S(1)} %get-tuple-element.88), channel_id=1, source_target_pairs={{0,1},{1,0},{2,3},{3,2},{4,5},{5,4},{6,7},{7,6},{8,9},{9,8},{10,11... | collective-permute-start | bytes 663560 | tf_op jit(solution)/shard_map/ppermute | solution.py:703
  18.8 8.4 %collective-permute-start.18 = (f32[72,768]{1,0:T(8,128)S(1)}, f32[72,768]{1,0:T(8,128)S(1)}, u32[]{:S(2)}, u32[]{:S(2)}) collective-permute-start(f32[72,768]{1,0:T(8,128)S(1)} %get-tuple-element.89), channel_id=1, source_target_pairs={{0,3},{1,2},{2,1},{3,0},{4,7},{5,6},{6,5},{7,4},{8,11},{9,10},{10,... | collective-permute-start | bytes 663560 | tf_op jit(solution)/shard_map/ppermute | solution.py:703
  25.3 5.8 %collective-permute-start.6 = (f32[72,768]{1,0:T(8,128)S(1)}, f32[72,768]{1,0:T(8,128)S(1)}, u32[]{:S(2)}, u32[]{:S(2)}) collective-permute-start(f32[72,768]{1,0:T(8,128)S(1)} %get-tuple-element.75), channel_id=1, source_target_pairs={{0,1},{1,0},{2,3},{3,2},{4,5},{5,4},{6,7},{7,6},{8,9},{9,8},{10,11... | collective-permute-start | bytes 663560 | tf_op jit(solution)/shard_map/ppermute | solution.py:703
  25.4 8.3 %collective-permute-start.7 = (f32[72,768]{1,0:T(8,128)S(1)}, f32[72,768]{1,0:T(8,128)S(1)}, u32[]{:S(2)}, u32[]{:S(2)}) collective-permute-start(f32[72,768]{1,0:T(8,128)S(1)} %get-tuple-element.76), channel_id=1, source_target_pairs={{0,2},{1,3},{2,0},{3,1},{4,6},{5,7},{6,4},{7,5},{8,10},{9,11},{10,... | collective-permute-start | bytes 663560 | tf_op jit(solution)/shard_map/ppermute | solution.py:703
  27.1 10.4 %collective-permute-start.8 = (f32[72,768]{1,0:T(8,128)S(1)}, f32[72,768]{1,0:T(8,128)S(1)}, u32[]{:S(2)}, u32[]{:S(2)}) collective-permute-start(f32[72,768]{1,0:T(8,128)S(1)} %get-tuple-element.77), channel_id=1, source_target_pairs={{0,3},{1,2},{2,1},{3,0},{4,7},{5,6},{6,5},{7,4},{8,11},{9,10},{10,... | collective-permute-start | bytes 663560 | tf_op jit(solution)/shard_map/ppermute | solution.py:703
  28.8 11.0 %collective-permute-start.19 = (f32[32,768]{1,0:T(8,128)S(1)}, f32[32,768]{1,0:T(8,128)S(1)}, u32[]{:S(2)}, u32[]{:S(2)}) collective-permute-start(f32[32,768]{1,0:T(8,128)S(1)} %get-tuple-element.91), channel_id=1, source_target_pairs={{0,16},{4,20},{8,24},{12,28},{16,0},{20,4},{24,8},{28,12},{1,17},{... | collective-permute-start | bytes 294920 | tf_op jit(solution)/shard_map/ppermute | solution.py:703
  28.9 15.0 %collective-permute-start.20 = (f32[32,768]{1,0:T(8,128)S(1)}, f32[32,768]{1,0:T(8,128)S(1)}, u32[]{:S(2)}, u32[]{:S(2)}) collective-permute-start(f32[32,768]{1,0:T(8,128)S(1)} %get-tuple-element.92), channel_id=1, source_target_pairs={{0,4},{4,0},{8,12},{12,8},{16,20},{20,16},{24,28},{28,24},{1,5},{5... | collective-permute-start | bytes 294920 | tf_op jit(solution)/shard_map/ppermute | solution.py:703
  31.1 12.8 %collective-permute-start.21 = (f32[32,768]{1,0:T(8,128)S(1)}, f32[32,768]{1,0:T(8,128)S(1)}, u32[]{:S(2)}, u32[]{:S(2)}) collective-permute-start(f32[32,768]{1,0:T(8,128)S(1)} %get-tuple-element.93), channel_id=1, source_target_pairs={{0,20},{4,16},{8,28},{12,24},{16,4},{20,0},{24,12},{28,8},{1,21},{... | collective-permute-start | bytes 294920 | tf_op jit(solution)/shard_map/ppermute | solution.py:703
  33.6 11.5 %collective-permute-start.22 = (f32[32,768]{1,0:T(8,128)S(1)}, f32[32,768]{1,0:T(8,128)S(1)}, u32[]{:S(2)}, u32[]{:S(2)}) collective-permute-start(f32[32,768]{1,0:T(8,128)S(1)} %get-tuple-element.94), channel_id=1, source_target_pairs={{0,8},{4,12},{8,0},{12,4},{16,24},{20,28},{24,16},{28,20},{1,9},{5... | collective-permute-start | bytes 294920 | tf_op jit(solution)/shard_map/ppermute | solution.py:703
  37.5 12.3 %collective-permute-start.23 = (f32[32,768]{1,0:T(8,128)S(1)}, f32[32,768]{1,0:T(8,128)S(1)}, u32[]{:S(2)}, u32[]{:S(2)}) collective-permute-start(f32[32,768]{1,0:T(8,128)S(1)} %get-tuple-element.95), channel_id=1, source_target_pairs={{0,24},{4,28},{8,16},{12,20},{16,8},{20,12},{24,0},{28,4},{1,25},{... | collective-permute-start | bytes 294920 | tf_op jit(solution)/shard_map/ppermute | solution.py:703
  39.8 9.9 %collective-permute-start.24 = (f32[32,768]{1,0:T(8,128)S(1)}, f32[32,768]{1,0:T(8,128)S(1)}, u32[]{:S(2)}, u32[]{:S(2)}) collective-permute-start(f32[32,768]{1,0:T(8,128)S(1)} %get-tuple-element.96), channel_id=1, source_target_pairs={{0,28},{4,24},{8,20},{12,16},{16,12},{20,8},{24,4},{28,0},{1,29},{... | collective-permute-start | bytes 294920 | tf_op jit(solution)/shard_map/ppermute | solution.py:703
  43.9 7.0 %collective-permute-start.25 = (f32[32,768]{1,0:T(8,128)S(1)}, f32[32,768]{1,0:T(8,128)S(1)}, u32[]{:S(2)}, u32[]{:S(2)}) collective-permute-start(f32[32,768]{1,0:T(8,128)S(1)} %get-tuple-element.97), channel_id=1, source_target_pairs={{0,12},{4,8},{8,4},{12,0},{16,28},{20,24},{24,20},{28,16},{1,13},{... | collective-permute-start | bytes 294920 | tf_op jit(solution)/shard_map/ppermute | solution.py:703
  43.9 12.4 %collective-permute-start.9 = (f32[32,768]{1,0:T(8,128)S(1)}, f32[32,768]{1,0:T(8,128)S(1)}, u32[]{:S(2)}, u32[]{:S(2)}) collective-permute-start(f32[32,768]{1,0:T(8,128)S(1)} %get-tuple-element.79), channel_id=1, source_target_pairs={{0,16},{4,20},{8,24},{12,28},{16,0},{20,4},{24,8},{28,12},{1,17},{... | collective-permute-start | bytes 294920 | tf_op jit(solution)/shard_map/ppermute | solution.py:703
  45.2 14.1 %collective-permute-start.10 = (f32[32,768]{1,0:T(8,128)S(1)}, f32[32,768]{1,0:T(8,128)S(1)}, u32[]{:S(2)}, u32[]{:S(2)}) collective-permute-start(f32[32,768]{1,0:T(8,128)S(1)} %get-tuple-element.80), channel_id=1, source_target_pairs={{0,4},{4,0},{8,12},{12,8},{16,20},{20,16},{24,28},{28,24},{1,5},{5... | collective-permute-start | bytes 294920 | tf_op jit(solution)/shard_map/ppermute | solution.py:703
  49.7 10.9 %collective-permute-start.11 = (f32[32,768]{1,0:T(8,128)S(1)}, f32[32,768]{1,0:T(8,128)S(1)}, u32[]{:S(2)}, u32[]{:S(2)}) collective-permute-start(f32[32,768]{1,0:T(8,128)S(1)} %get-tuple-element.81), channel_id=1, source_target_pairs={{0,20},{4,16},{8,28},{12,24},{16,4},{20,0},{24,12},{28,8},{1,21},{... | collective-permute-start | bytes 294920 | tf_op jit(solution)/shard_map/ppermute | solution.py:703
  49.7 11.0 %collective-permute-start.12 = (f32[32,768]{1,0:T(8,128)S(1)}, f32[32,768]{1,0:T(8,128)S(1)}, u32[]{:S(2)}, u32[]{:S(2)}) collective-permute-start(f32[32,768]{1,0:T(8,128)S(1)} %get-tuple-element.82), channel_id=1, source_target_pairs={{0,8},{4,12},{8,0},{12,4},{16,24},{20,28},{24,16},{28,20},{1,9},{5... | collective-permute-start | bytes 294920 | tf_op jit(solution)/shard_map/ppermute | solution.py:703
  50.8 11.6 %collective-permute-start.13 = (f32[32,768]{1,0:T(8,128)S(1)}, f32[32,768]{1,0:T(8,128)S(1)}, u32[]{:S(2)}, u32[]{:S(2)}) collective-permute-start(f32[32,768]{1,0:T(8,128)S(1)} %get-tuple-element.83), channel_id=1, source_target_pairs={{0,24},{4,28},{8,16},{12,20},{16,8},{20,12},{24,0},{28,4},{1,25},{... | collective-permute-start | bytes 294920 | tf_op jit(solution)/shard_map/ppermute | solution.py:703
  56.3 8.0 %collective-permute-start.14 = (f32[32,768]{1,0:T(8,128)S(1)}, f32[32,768]{1,0:T(8,128)S(1)}, u32[]{:S(2)}, u32[]{:S(2)}) collective-permute-start(f32[32,768]{1,0:T(8,128)S(1)} %get-tuple-element.84), channel_id=1, source_target_pairs={{0,28},{4,24},{8,20},{12,16},{16,12},{20,8},{24,4},{28,0},{1,29},{... | collective-permute-start | bytes 294920 | tf_op jit(solution)/shard_map/ppermute | solution.py:703
  59.3 6.7 %collective-permute-start.15 = (f32[32,768]{1,0:T(8,128)S(1)}, f32[32,768]{1,0:T(8,128)S(1)}, u32[]{:S(2)}, u32[]{:S(2)}) collective-permute-start(f32[32,768]{1,0:T(8,128)S(1)} %get-tuple-element.85), channel_id=1, source_target_pairs={{0,12},{4,8},{8,4},{12,0},{16,28},{20,24},{24,20},{28,16},{1,13},{... | collective-permute-start | bytes 294920 | tf_op jit(solution)/shard_map/ppermute | solution.py:703
  60.7 6.7 %collective-permute-start.4 = (f32[48,256]{1,0:T(8,128)S(1)}, f32[48,256]{1,0:T(8,128)S(1)}, u32[]{:S(2)}, u32[]{:S(2)}) collective-permute-start(f32[48,256]{1,0:T(8,128)S(1)} %get-tuple-element.72), channel_id=1, source_target_pairs={{0,1},{1,2},{2,3},{3,0},{4,5},{5,6},{6,7},{7,4},{8,9},{9,10},{10,1... | collective-permute-start | bytes 147464 | tf_op jit(solution)/shard_map/ppermute | solution.py:761
  60.7 6.6 %collective-permute-start.5 = (f32[48,256]{1,0:T(8,128)S(1)}, f32[48,256]{1,0:T(8,128)S(1)}, u32[]{:S(2)}, u32[]{:S(2)}) collective-permute-start(f32[48,256]{1,0:T(8,128)S(1)} %get-tuple-element.73), channel_id=1, source_target_pairs={{0,3},{1,0},{2,1},{3,2},{4,7},{5,4},{6,5},{7,6},{8,11},{9,8},{10,9... | collective-permute-start | bytes 147464 | tf_op jit(solution)/shard_map/ppermute | solution.py:762
  71.1 9.3 %collective-permute-start.26 = (f32[32,768]{1,0:T(8,128)S(1)}, f32[32,768]{1,0:T(8,128)S(1)}, u32[]{:S(2)}, u32[]{:S(2)}) collective-permute-start(f32[32,768]{1,0:T(8,128)S(1)} %get-tuple-element.100), channel_id=1, source_target_pairs={{0,16},{4,20},{8,24},{12,28},{16,0},{20,4},{24,8},{28,12},{1,17},{... | collective-permute-start | bytes 294920 | tf_op jit(solution)/shard_map/ppermute | solution.py:703
  73.3 8.5 %collective-permute-start.27 = (f32[32,768]{1,0:T(8,128)S(1)}, f32[32,768]{1,0:T(8,128)S(1)}, u32[]{:S(2)}, u32[]{:S(2)}) collective-permute-start(f32[32,768]{1,0:T(8,128)S(1)} %get-tuple-element.101), channel_id=1, source_target_pairs={{0,4},{4,0},{8,12},{12,8},{16,20},{20,16},{24,28},{28,24},{1,5},{5... | collective-permute-start | bytes 294920 | tf_op jit(solution)/shard_map/ppermute | solution.py:703
  74.6 14.2 %collective-permute-start.28 = (f32[32,768]{1,0:T(8,128)S(1)}, f32[32,768]{1,0:T(8,128)S(1)}, u32[]{:S(2)}, u32[]{:S(2)}) collective-permute-start(f32[32,768]{1,0:T(8,128)S(1)} %get-tuple-element.102), channel_id=1, source_target_pairs={{0,20},{4,16},{8,28},{12,24},{16,4},{20,0},{24,12},{28,8},{1,21},{... | collective-permute-start | bytes 294920 | tf_op jit(solution)/shard_map/ppermute | solution.py:703
  75.6 13.2 %collective-permute-start.29 = (f32[32,768]{1,0:T(8,128)S(1)}, f32[32,768]{1,0:T(8,128)S(1)}, u32[]{:S(2)}, u32[]{:S(2)}) collective-permute-start(f32[32,768]{1,0:T(8,128)S(1)} %get-tuple-element.103), channel_id=1, source_target_pairs={{0,8},{4,12},{8,0},{12,4},{16,24},{20,28},{24,16},{28,20},{1,9},{5... | collective-permute-start | bytes 294920 | tf_op jit(solution)/shard_map/ppermute | solution.py:703
  76.8 13.1 %collective-permute-start.30 = (f32[32,768]{1,0:T(8,128)S(1)}, f32[32,768]{1,0:T(8,128)S(1)}, u32[]{:S(2)}, u32[]{:S(2)}) collective-permute-start(f32[32,768]{1,0:T(8,128)S(1)} %get-tuple-element.104), channel_id=1, source_target_pairs={{0,24},{4,28},{8,16},{12,20},{16,8},{20,12},{24,0},{28,4},{1,25},{... | collective-permute-start | bytes 294920 | tf_op jit(solution)/shard_map/ppermute | solution.py:703
  80.4 12.8 %collective-permute-start.31 = (f32[32,768]{1,0:T(8,128)S(1)}, f32[32,768]{1,0:T(8,128)S(1)}, u32[]{:S(2)}, u32[]{:S(2)}) collective-permute-start(f32[32,768]{1,0:T(8,128)S(1)} %get-tuple-element.105), channel_id=1, source_target_pairs={{0,28},{4,24},{8,20},{12,16},{16,12},{20,8},{24,4},{28,0},{1,29},{... | collective-permute-start | bytes 294920 | tf_op jit(solution)/shard_map/ppermute | solution.py:703
  81.8 13.9 %collective-permute-start.32 = (f32[32,768]{1,0:T(8,128)S(1)}, f32[32,768]{1,0:T(8,128)S(1)}, u32[]{:S(2)}, u32[]{:S(2)}) collective-permute-start(f32[32,768]{1,0:T(8,128)S(1)} %get-tuple-element.106), channel_id=1, source_target_pairs={{0,12},{4,8},{8,4},{12,0},{16,28},{20,24},{24,20},{28,16},{1,13},{... | collective-permute-start | bytes 294920 | tf_op jit(solution)/shard_map/ppermute | solution.py:703
  88.8 8.9 %collective-permute-start.36 = (f32[32,768]{1,0:T(8,128)S(1)}, f32[32,768]{1,0:T(8,128)S(1)}, u32[]{:S(2)}, u32[]{:S(2)}) collective-permute-start(f32[32,768]{1,0:T(8,128)S(1)} %get-tuple-element.116), channel_id=1, source_target_pairs={{0,16},{4,20},{8,24},{12,28},{16,0},{20,4},{24,8},{28,12},{1,17},{... | collective-permute-start | bytes 294920 | tf_op jit(solution)/shard_map/ppermute | solution.py:703
  88.8 10.7 %collective-permute-start.37 = (f32[32,768]{1,0:T(8,128)S(1)}, f32[32,768]{1,0:T(8,128)S(1)}, u32[]{:S(2)}, u32[]{:S(2)}) collective-permute-start(f32[32,768]{1,0:T(8,128)S(1)} %get-tuple-element.117), channel_id=1, source_target_pairs={{0,4},{4,0},{8,12},{12,8},{16,20},{20,16},{24,28},{28,24},{1,5},{5... | collective-permute-start | bytes 294920 | tf_op jit(solution)/shard_map/ppermute | solution.py:703
  89.9 12.7 %collective-permute-start.38 = (f32[32,768]{1,0:T(8,128)S(1)}, f32[32,768]{1,0:T(8,128)S(1)}, u32[]{:S(2)}, u32[]{:S(2)}) collective-permute-start(f32[32,768]{1,0:T(8,128)S(1)} %get-tuple-element.118), channel_id=1, source_target_pairs={{0,20},{4,16},{8,28},{12,24},{16,4},{20,0},{24,12},{28,8},{1,21},{... | collective-permute-start | bytes 294920 | tf_op jit(solution)/shard_map/ppermute | solution.py:703
  93.2 10.3 %collective-permute-start.39 = (f32[32,768]{1,0:T(8,128)S(1)}, f32[32,768]{1,0:T(8,128)S(1)}, u32[]{:S(2)}, u32[]{:S(2)}) collective-permute-start(f32[32,768]{1,0:T(8,128)S(1)} %get-tuple-element.119), channel_id=1, source_target_pairs={{0,8},{4,12},{8,0},{12,4},{16,24},{20,28},{24,16},{28,20},{1,9},{5... | collective-permute-start | bytes 294920 | tf_op jit(solution)/shard_map/ppermute | solution.py:703
  97.5 7.6 %collective-permute-start.40 = (f32[32,768]{1,0:T(8,128)S(1)}, f32[32,768]{1,0:T(8,128)S(1)}, u32[]{:S(2)}, u32[]{:S(2)}) collective-permute-start(f32[32,768]{1,0:T(8,128)S(1)} %get-tuple-element.123), channel_id=1, source_target_pairs={{0,24},{4,28},{8,16},{12,20},{16,8},{20,12},{24,0},{28,4},{1,25},{... | collective-permute-start | bytes 294920 | tf_op jit(solution)/shard_map/ppermute | solution.py:703
  97.7 8.2 %collective-permute-start.41 = (f32[32,768]{1,0:T(8,128)S(1)}, f32[32,768]{1,0:T(8,128)S(1)}, u32[]{:S(2)}, u32[]{:S(2)}) collective-permute-start(f32[32,768]{1,0:T(8,128)S(1)} %get-tuple-element.124), channel_id=1, source_target_pairs={{0,28},{4,24},{8,20},{12,16},{16,12},{20,8},{24,4},{28,0},{1,29},{... | collective-permute-start | bytes 294920 | tf_op jit(solution)/shard_map/ppermute | solution.py:703
  99.5 8.3 %collective-permute-start.42 = (f32[32,768]{1,0:T(8,128)S(1)}, f32[32,768]{1,0:T(8,128)S(1)}, u32[]{:S(2)}, u32[]{:S(2)}) collective-permute-start(f32[32,768]{1,0:T(8,128)S(1)} %get-tuple-element.125), channel_id=1, source_target_pairs={{0,12},{4,8},{8,4},{12,0},{16,28},{20,24},{24,20},{28,16},{1,13},{... | collective-permute-start | bytes 294920 | tf_op jit(solution)/shard_map/ppermute | solution.py:703
  102.6 8.3 %collective-permute-start.33 = (f32[72,768]{1,0:T(8,128)S(1)}, f32[72,768]{1,0:T(8,128)S(1)}, u32[]{:S(2)}, u32[]{:S(2)}) collective-permute-start(f32[72,768]{1,0:T(8,128)S(1)} %get-tuple-element.108), channel_id=1, source_target_pairs={{0,2},{1,3},{2,0},{3,1},{4,6},{5,7},{6,4},{7,5},{8,10},{9,11},{10,... | collective-permute-start | bytes 663560 | tf_op jit(solution)/shard_map/ppermute | solution.py:703
  103.5 8.2 %collective-permute-start.34 = (f32[72,768]{1,0:T(8,128)S(1)}, f32[72,768]{1,0:T(8,128)S(1)}, u32[]{:S(2)}, u32[]{:S(2)}) collective-permute-start(f32[72,768]{1,0:T(8,128)S(1)} %get-tuple-element.109), channel_id=1, source_target_pairs={{0,1},{1,0},{2,3},{3,2},{4,5},{5,4},{6,7},{7,6},{8,9},{9,8},{10,11... | collective-permute-start | bytes 663560 | tf_op jit(solution)/shard_map/ppermute | solution.py:703
  105.1 8.8 %collective-permute-start.35 = (f32[72,768]{1,0:T(8,128)S(1)}, f32[72,768]{1,0:T(8,128)S(1)}, u32[]{:S(2)}, u32[]{:S(2)}) collective-permute-start(f32[72,768]{1,0:T(8,128)S(1)} %get-tuple-element.110), channel_id=1, source_target_pairs={{0,3},{1,2},{2,1},{3,0},{4,7},{5,6},{6,5},{7,4},{8,11},{9,10},{10,... | collective-permute-start | bytes 663560 | tf_op jit(solution)/shard_map/ppermute | solution.py:703
  109.4 10.9 %collective-permute-start.43 = (f32[72,768]{1,0:T(8,128)S(1)}, f32[72,768]{1,0:T(8,128)S(1)}, u32[]{:S(2)}, u32[]{:S(2)}) collective-permute-start(f32[72,768]{1,0:T(8,128)S(1)} %get-tuple-element.127), channel_id=1, source_target_pairs={{0,2},{1,3},{2,0},{3,1},{4,6},{5,7},{6,4},{7,5},{8,10},{9,11},{10,... | collective-permute-start | bytes 663560 | tf_op jit(solution)/shard_map/ppermute | solution.py:703
  110.7 12.7 %collective-permute-start.44 = (f32[72,768]{1,0:T(8,128)S(1)}, f32[72,768]{1,0:T(8,128)S(1)}, u32[]{:S(2)}, u32[]{:S(2)}) collective-permute-start(f32[72,768]{1,0:T(8,128)S(1)} %get-tuple-element.128), channel_id=1, source_target_pairs={{0,3},{1,2},{2,1},{3,0},{4,7},{5,6},{6,5},{7,4},{8,11},{9,10},{10,... | collective-permute-start | bytes 663560 | tf_op jit(solution)/shard_map/ppermute | solution.py:703
  110.9 12.4 %collective-permute-start.45 = (f32[72,768]{1,0:T(8,128)S(1)}, f32[72,768]{1,0:T(8,128)S(1)}, u32[]{:S(2)}, u32[]{:S(2)}) collective-permute-start(f32[72,768]{1,0:T(8,128)S(1)} %get-tuple-element.129), channel_id=1, source_target_pairs={{0,1},{1,0},{2,3},{3,2},{4,5},{5,4},{6,7},{7,6},{8,9},{9,8},{10,11... | collective-permute-start | bytes 663560 | tf_op jit(solution)/shard_map/ppermute | solution.py:703
  115.3 11.0 %collective-permute-start.46 = (f32[3,64,256]{2,1,0:T(8,128)S(1)}, f32[3,64,256]{2,1,0:T(8,128)S(1)}, u32[]{:S(2)}, u32[]{:S(2)}) collective-permute-start(f32[3,64,256]{2,1,0:T(8,128)S(1)} %get-tuple-element.132), channel_id=1, source_target_pairs={{0,4},{4,8},{8,12},{12,16},{16,20},{20,24},{24,28},{28,0},{1,5},{5... | collective-permute-start | bytes 589832 | tf_op jit(solution)/shard_map/ppermute | solution.py:832
  115.7 12.3 %collective-permute-start.47 = (f32[3,64,256]{2,1,0:T(8,128)S(1)}, f32[3,64,256]{2,1,0:T(8,128)S(1)}, u32[]{:S(2)}, u32[]{:S(2)}) collective-permute-start(f32[3,64,256]{2,1,0:T(8,128)S(1)} %get-tuple-element.133), channel_id=1, source_target_pairs={{0,28},{4,0},{8,4},{12,8},{16,12},{20,16},{24,20},{28,24},{1,29},{... | collective-permute-start | bytes 589832 | tf_op jit(solution)/shard_map/ppermute | solution.py:831
  (9 other events, 94.1 us)

commit v16 on v15

--- a/solution.py
+++ b/solution.py
@@ -146,13 +146,15 @@
     far, near = list(range(count // 2, count)), list(range(1, count // 2))
     if first == "near":
         return [0] + near + far
+    if count == 4 and first is None:
+        return [0, 2, 1, 3]
     if first == "far":
         return [0] + far + near
-    order, last = [0], near[2:]
-    near = near[:2]
+    order, last = [0], near[1:]
+    near = near[:1]
     while far or near:
-        order += far[:1] + near[:1]
-        far, near = far[1:], near[1:]
+        order += far[:2] + near[:1]
+        far, near = far[2:], near[1:]
     return order + last
 
 

time: 129 us -> 136 us (1.054)
  waiting for transfers between devices: 28.7 us -> 33.5 us
  starting transfers between devices: 68.7 us -> 70.7 us
    ppermute x40, waiting for transfers between devices: 25.4 us -> 28.6 us  [exchange(): lax.ppermute(block, axis, [(i, i ^ k) for i in range(count)])]
    ppermute x40, starting transfers between devices: 52.2 us -> 54.3 us  [exchange(): lax.ppermute(block, axis, [(i, i ^ k) for i in range(count)])]
  transfers between devices with their start and end apart: 48 -> 48, of which waited for: 16 -> 16; matrix products, arithmetic and copies ran while one was open for 0% -> 0% of each run, Pallas kernels for 16% -> 15%
where the time goes in v16:
time: 136 us
  starting transfers between devices  70.7 us (52%)
  waiting for transfers between devices  33.5 us (25%)
  Pallas kernels  30.6 us (22%)
    ppermute x40, starting transfers between devices, exchange(): lax.ppermute(block, axis, [(i, i ^ k) for i in range(count)])  54.3 us
    pallas_call x16, Pallas kernels, call(): pl.pallas_call(kernel, out_shape=[jax.ShapeDtypeStruct(shape, F32) for _,...  30.6 us
    ppermute x40, waiting for transfers between devices, exchange(): lax.ppermute(block, axis, [(i, i ^ k) for i in range(count)])  28.6 us
    ppermute x1, starting transfers between devices, on_device(): after = lax.ppermute(first, 'gz', ring('gz', -1))  4.13 us
    ppermute x1, starting transfers between devices, on_device(): down2 = lax.ppermute(movers, 'gz', ring('gz', 2))  3.08 us
    ppermute x1, starting transfers between devices, on_device(): up1 = lax.ppermute(packet, 'gz', ring('gz', -1))  3.08 us
    ppermute x1, waiting for transfers between devices, on_device(): after = lax.ppermute(first, 'gz', ring('gz', -1))  3.06 us
  transfers between devices with their start and end apart: 48, of which 16 were waited for; matrix products, arithmetic and copies ran while one was open for 0% of the time, Pallas kernels for 15%

profile of v16, /device:TPU:0, one launch (start us, length us, event | category | flops | bytes accessed | tf_op | source)
XLA Modules:
  0.0 136.1 jit_solution(5180065772465270720)
XLA Ops:
  1.8 3.1 %collective-permute-start.3 = (f32[8,128]{1,0:T(8,128)S(1)}, f32[8,128]{1,0:T(8,128)S(1)}, u32[]{:S(2)}, u32[]{:S(2)}) collective-permute-start(f32[8,128]{1,0:T(8,128)S(1)} %get-tuple-element.69), channel_id=1, source_target_pairs={{0,8},{4,12},{8,16},{12,20},{16,24},{20,28},{24,0},{28,4},{1,9},{5... | collective-permute-start | bytes 12296 | tf_op jit(solution)/shard_map/ppermute | solution.py:742
  4.8 2.1 %collective-permute-start.2 = (f32[8,128]{1,0:T(8,128)S(1)}, f32[8,128]{1,0:T(8,128)S(1)}, u32[]{:S(2)}, u32[]{:S(2)}) collective-permute-start(f32[8,128]{1,0:T(8,128)S(1)} %get-tuple-element.69), channel_id=1, source_target_pairs={{0,24},{4,28},{8,0},{12,4},{16,8},{20,12},{24,16},{28,20},{1,25},{... | collective-permute-start | bytes 12296 | tf_op jit(solution)/shard_map/ppermute | solution.py:741
  6.9 1.6 %collective-permute-start.1 = (f32[8,512]{1,0:T(8,128)S(1)}, f32[8,512]{1,0:T(8,128)S(1)}, u32[]{:S(2)}, u32[]{:S(2)}) collective-permute-start(f32[8,512]{1,0:T(8,128)S(1)} %get-tuple-element.68.own), channel_id=1, source_target_pairs={{0,4},{4,8},{8,12},{12,16},{16,20},{20,24},{24,28},{28,0},{1,5},{5... | collective-permute-start | bytes 49160 | tf_op jit(solution)/shard_map/ppermute | solution.py:740
  8.6 3.1 %collective-permute-start = (f32[8,512]{1,0:T(8,128)S(1)}, f32[8,512]{1,0:T(8,128)S(1)}, u32[]{:S(2)}, u32[]{:S(2)}) collective-permute-start(f32[8,512]{1,0:T(8,128)S(1)} %get-tuple-element.68.own), channel_id=1, source_target_pairs={{0,28},{4,0},{8,4},{12,8},{16,12},{20,16},{24,20},{28,24},{1,29},{... | collective-permute-start | bytes 49160 | tf_op jit(solution)/shard_map/ppermute | solution.py:739
  11.7 1.6 %collective-permute-done.1.down1 = f32[8,512]{1,0:T(8,128)S(1)} collective-permute-done((f32[8,512]{1,0:T(8,128)S(1)}, f32[8,512]{1,0:T(8,128)S(1)}, u32[]{:S(2)}, u32[]{:S(2)}) %collective-permute-start.1) | collective-permute-done | bytes 16416 | tf_op jit(solution)/shard_map/ppermute | solution.py:740
  13.4 3.7 %shard_map.141 = (f32[3,4,64,256]{3,2,1,0:T(8,128)S(1)}, f32[24,256]{1,0:T(8,128)S(1)}, f32[24,256]{1,0:T(8,128)S(1)}, f32[72,768]{1,0:T(8,128)S(1)}, f32[72,768...) custom-call(s32[2]{0:T(128)S(1)} %pad_add_fusion.place, f32[8,512]{1,0:T(8,128)S(1)} %get-tuple-element.68.own, ...), custom_call_target="tpu_custom_call" | custom-call | flops 5000000000 | bytes 15000000 | tf_op jit(solution)/shard_map/pallas_call | solution.py:669
  17.1 1.7 %collective-permute-start.16 = (f32[72,768]{1,0:T(8,128)S(1)}, f32[72,768]{1,0:T(8,128)S(1)}, u32[]{:S(2)}, u32[]{:S(2)}) collective-permute-start(f32[72,768]{1,0:T(8,128)S(1)} %get-tuple-element.87), channel_id=1, source_target_pairs={{0,2},{1,3},{2,0},{3,1},{4,6},{5,7},{6,4},{7,5},{8,10},{9,11},{10,... | collective-permute-start | bytes 663560 | tf_op jit(solution)/shard_map/ppermute | solution.py:705
  19.3 6.0 %shard_map.142 = (f32[3,4,64,256]{3,2,1,0:T(8,128)S(1)}, f32[48,256]{1,0:T(8,128)S(1)}, f32[48,256]{1,0:T(8,128)S(1)}, f32[72,768]{1,0:T(8,128)S(1)}, f32[72,768...) custom-call(s32[2]{0:T(128)S(1)} %pad_add_fusion.place, f32[8,512]{1,0:T(8,128)S(1)} %get-tuple-element.68.own, ...), custom_call_target="tpu_custom_call" | custom-call | flops 5000000000 | bytes 15000000 | tf_op jit(solution)/shard_map/pallas_call | solution.py:669
  25.4 1.7 %collective-permute-start.7 = (f32[72,768]{1,0:T(8,128)S(1)}, f32[72,768]{1,0:T(8,128)S(1)}, u32[]{:S(2)}, u32[]{:S(2)}) collective-permute-start(f32[72,768]{1,0:T(8,128)S(1)} %get-tuple-element.76), channel_id=1, source_target_pairs={{0,2},{1,3},{2,0},{3,1},{4,6},{5,7},{6,4},{7,5},{8,10},{9,11},{10,... | collective-permute-start | bytes 663560 | tf_op jit(solution)/shard_map/ppermute | solution.py:705
  27.2 1.6 %shard_map.145 = (f32[32,768]{1,0:T(8,128)S(1)}, f32[32,768]{1,0:T(8,128)S(1)}, f32[32,768]{1,0:T(8,128)S(1)}, f32[32,768]{1,0:T(8,128)S(1)}, f32[32,768]{1,0:T(...) custom-call(s32[2]{0:T(128)S(1)} %pad_add_fusion.place, ...), custom_call_target="tpu_custom_call" | custom-call | flops 2000000000 | bytes 6000000 | tf_op jit(solution)/shard_map/pallas_call | solution.py:669
  28.9 2.2 %collective-permute-start.20 = (f32[32,768]{1,0:T(8,128)S(1)}, f32[32,768]{1,0:T(8,128)S(1)}, u32[]{:S(2)}, u32[]{:S(2)}) collective-permute-start(f32[32,768]{1,0:T(8,128)S(1)} %get-tuple-element.92), channel_id=1, source_target_pairs={{0,20},{4,16},{8,28},{12,24},{16,4},{20,0},{24,12},{28,8},{1,21},{... | collective-permute-start | bytes 294920 | tf_op jit(solution)/shard_map/ppermute | solution.py:705
  31.1 2.2 %collective-permute-start.21 = (f32[32,768]{1,0:T(8,128)S(1)}, f32[32,768]{1,0:T(8,128)S(1)}, u32[]{:S(2)}, u32[]{:S(2)}) collective-permute-start(f32[32,768]{1,0:T(8,128)S(1)} %get-tuple-element.93), channel_id=1, source_target_pairs={{0,4},{4,0},{8,12},{12,8},{16,20},{20,16},{24,28},{28,24},{1,5},{5... | collective-permute-start | bytes 294920 | tf_op jit(solution)/shard_map/ppermute | solution.py:705
  33.6 3.0 %collective-permute-start.22 = (f32[32,768]{1,0:T(8,128)S(1)}, f32[32,768]{1,0:T(8,128)S(1)}, u32[]{:S(2)}, u32[]{:S(2)}) collective-permute-start(f32[32,768]{1,0:T(8,128)S(1)} %get-tuple-element.94), channel_id=1, source_target_pairs={{0,24},{4,28},{8,16},{12,20},{16,8},{20,12},{24,0},{28,4},{1,25},{... | collective-permute-start | bytes 294920 | tf_op jit(solution)/shard_map/ppermute | solution.py:705
  37.5 4.7 %collective-permute-start.23 = (f32[32,768]{1,0:T(8,128)S(1)}, f32[32,768]{1,0:T(8,128)S(1)}, u32[]{:S(2)}, u32[]{:S(2)}) collective-permute-start(f32[32,768]{1,0:T(8,128)S(1)} %get-tuple-element.95), channel_id=1, source_target_pairs={{0,28},{4,24},{8,20},{12,16},{16,12},{20,8},{24,4},{28,0},{1,29},{... | collective-permute-start | bytes 294920 | tf_op jit(solution)/shard_map/ppermute | solution.py:705
  42.2 1.6 %shard_map.143 = (f32[32,768]{1,0:T(8,128)S(1)}, f32[32,768]{1,0:T(8,128)S(1)}, f32[32,768]{1,0:T(8,128)S(1)}, f32[32,768]{1,0:T(8,128)S(1)}, f32[32,768]{1,0:T(...) custom-call(s32[2]{0:T(128)S(1)} %pad_add_fusion.place, ...), custom_call_target="tpu_custom_call" | custom-call | flops 2000000000 | bytes 6000000 | tf_op jit(solution)/shard_map/pallas_call | solution.py:669
  43.9 1.3 collective-permute-start.25
  46.0 3.7 %collective-permute-start.10 = (f32[32,768]{1,0:T(8,128)S(1)}, f32[32,768]{1,0:T(8,128)S(1)}, u32[]{:S(2)}, u32[]{:S(2)}) collective-permute-start(f32[32,768]{1,0:T(8,128)S(1)} %get-tuple-element.80), channel_id=1, source_target_pairs={{0,20},{4,16},{8,28},{12,24},{16,4},{20,0},{24,12},{28,8},{1,21},{... | collective-permute-start | bytes 294920 | tf_op jit(solution)/shard_map/ppermute | solution.py:705
  50.1 1.4 %collective-permute-done.24.refs_6_ = f32[32,768]{1,0:T(8,128)S(1)} collective-permute-done((f32[32,768]{1,0:T(8,128)S(1)}, f32[32,768]{1,0:T(8,128)S(1)}, u32[]{:S(2)}, u32[]{:S(2)}) %collective-permute-start.24) | collective-permute-done | bytes 98336 | tf_op jit(solution)/shard_map/ppermute | solution.py:705
  52.4 3.0 %collective-permute-start.13 = (f32[32,768]{1,0:T(8,128)S(1)}, f32[32,768]{1,0:T(8,128)S(1)}, u32[]{:S(2)}, u32[]{:S(2)}) collective-permute-start(f32[32,768]{1,0:T(8,128)S(1)} %get-tuple-element.83), channel_id=1, source_target_pairs={{0,28},{4,24},{8,20},{12,16},{16,12},{20,8},{24,4},{28,0},{1,29},{... | collective-permute-start | bytes 294920 | tf_op jit(solution)/shard_map/ppermute | solution.py:705
  55.5 4.3 %collective-permute-start.14 = (f32[32,768]{1,0:T(8,128)S(1)}, f32[32,768]{1,0:T(8,128)S(1)}, u32[]{:S(2)}, u32[]{:S(2)}) collective-permute-start(f32[32,768]{1,0:T(8,128)S(1)} %get-tuple-element.84), channel_id=1, source_target_pairs={{0,8},{4,12},{8,0},{12,4},{16,24},{20,28},{24,16},{28,20},{1,9},{5... | collective-permute-start | bytes 294920 | tf_op jit(solution)/shard_map/ppermute | solution.py:705
  59.8 3.1 %collective-permute-done.10.refs_2_ = f32[32,768]{1,0:T(8,128)S(1)} collective-permute-done((f32[32,768]{1,0:T(8,128)S(1)}, f32[32,768]{1,0:T(8,128)S(1)}, u32[]{:S(2)}, u32[]{:S(2)}) %collective-permute-start.10) | collective-permute-done | bytes 98336 | tf_op jit(solution)/shard_map/ppermute | solution.py:705
  63.1 1.3 shard_map.146.refs_1_
  64.5 1.7 %collective-permute-start.5 = (f32[48,256]{1,0:T(8,128)S(1)}, f32[48,256]{1,0:T(8,128)S(1)}, u32[]{:S(2)}, u32[]{:S(2)}) collective-permute-start(f32[48,256]{1,0:T(8,128)S(1)} %get-tuple-element.73), channel_id=1, source_target_pairs={{0,3},{1,0},{2,1},{3,2},{4,7},{5,4},{6,5},{7,6},{8,11},{9,8},{10,9... | collective-permute-start | bytes 147464 | tf_op jit(solution)/shard_map/ppermute | solution.py:764
  66.2 2.2 %collective-permute-done.15.refs_7_ = f32[32,768]{1,0:T(8,128)S(1)} collective-permute-done((f32[32,768]{1,0:T(8,128)S(1)}, f32[32,768]{1,0:T(8,128)S(1)}, u32[]{:S(2)}, u32[]{:S(2)}) %collective-permute-start.15) | collective-permute-done | bytes 98336 | tf_op jit(solution)/shard_map/ppermute | solution.py:705
  68.5 1.3 shard_map.144.refs_0_
  69.8 2.3 %shard_map.147 = (f32[3,2,4,8,8,128]{5,4,3,2,1,0:T(8,128)S(1)}, f32[3,2,4,8,8,128]{5,4,3,2,1,0:T(8,128)S(1)}) custom-call(s32[2]{0:T(128)S(1)} %pad_add_fusion.place, f32[48,256]{1,0:T(8,128)S(1)} %collective-permute-done.4.low_rim.refs_1_, f32[48,256]{1,0:T(8,128)S(1)} %collective-permute-done.5.high_rim.refs_2_, ...), custom_call_target="tpu_custom_call" | custom-call | flops 5000000000 | bytes 15000000 | tf_op jit(solution)/shard_map/pallas_call | solution.py:669
  72.2 1.4 %shard_map.148 = (f32[32,768]{1,0:T(8,128)S(1)}, f32[32,768]{1,0:T(8,128)S(1)}, f32[32,768]{1,0:T(8,128)S(1)}, f32[32,768]{1,0:T(8,128)S(1)}, f32[32,768]{1,0:T(...) custom-call(s32[2]{0:T(128)S(1)} %pad_add_fusion.place, ...), custom_call_target="tpu_custom_call" | custom-call | flops 2000000000 | bytes 6000000 | tf_op jit(solution)/shard_map/pallas_call | solution.py:669
  73.6 2.6 %collective-permute-start.26 = (f32[32,768]{1,0:T(8,128)S(1)}, f32[32,768]{1,0:T(8,128)S(1)}, u32[]{:S(2)}, u32[]{:S(2)}) collective-permute-start(f32[32,768]{1,0:T(8,128)S(1)} %get-tuple-element.100), channel_id=1, source_target_pairs={{0,16},{4,20},{8,24},{12,28},{16,0},{20,4},{24,8},{28,12},{1,17},{... | collective-permute-start | bytes 294920 | tf_op jit(solution)/shard_map/ppermute | solution.py:705
  76.2 1.8 %collective-permute-start.28 = (f32[32,768]{1,0:T(8,128)S(1)}, f32[32,768]{1,0:T(8,128)S(1)}, u32[]{:S(2)}, u32[]{:S(2)}) collective-permute-start(f32[32,768]{1,0:T(8,128)S(1)} %get-tuple-element.102), channel_id=1, source_target_pairs={{0,4},{4,0},{8,12},{12,8},{16,20},{20,16},{24,28},{28,24},{1,5},{5... | collective-permute-start | bytes 294920 | tf_op jit(solution)/shard_map/ppermute | solution.py:705
  78.0 3.0 %collective-permute-start.29 = (f32[32,768]{1,0:T(8,128)S(1)}, f32[32,768]{1,0:T(8,128)S(1)}, u32[]{:S(2)}, u32[]{:S(2)}) collective-permute-start(f32[32,768]{1,0:T(8,128)S(1)} %get-tuple-element.103), channel_id=1, source_target_pairs={{0,24},{4,28},{8,16},{12,20},{16,8},{20,12},{24,0},{28,4},{1,25},{... | collective-permute-start | bytes 294920 | tf_op jit(solution)/shard_map/ppermute | solution.py:705
  81.5 6.3 %collective-permute-done.26.refs_1_ = f32[32,768]{1,0:T(8,128)S(1)} collective-permute-done((f32[32,768]{1,0:T(8,128)S(1)}, f32[32,768]{1,0:T(8,128)S(1)}, u32[]{:S(2)}, u32[]{:S(2)}) %collective-permute-start.26) | collective-permute-done | bytes 98336 | tf_op jit(solution)/shard_map/ppermute | solution.py:705
  88.3 2.0 %collective-permute-done.27.refs_2_ = f32[32,768]{1,0:T(8,128)S(1)} collective-permute-done((f32[32,768]{1,0:T(8,128)S(1)}, f32[32,768]{1,0:T(8,128)S(1)}, u32[]{:S(2)}, u32[]{:S(2)}) %collective-permute-start.27) | collective-permute-done | bytes 98336 | tf_op jit(solution)/shard_map/ppermute | solution.py:705
  91.0 1.4 %shard_map.151 = (f32[32,768]{1,0:T(8,128)S(1)}, f32[32,768]{1,0:T(8,128)S(1)}, f32[32,768]{1,0:T(8,128)S(1)}, f32[32,768]{1,0:T(8,128)S(1)}, f32[32,768]{1,0:T(...) custom-call(s32[2]{0:T(128)S(1)} %pad_add_fusion.place, ...), custom_call_target="tpu_custom_call" | custom-call | flops 2000000000 | bytes 6000000 | tf_op jit(solution)/shard_map/pallas_call | solution.py:669
  92.4 3.7 %collective-permute-start.36 = (f32[32,768]{1,0:T(8,128)S(1)}, f32[32,768]{1,0:T(8,128)S(1)}, u32[]{:S(2)}, u32[]{:S(2)}) collective-permute-start(f32[32,768]{1,0:T(8,128)S(1)} %get-tuple-element.116), channel_id=1, source_target_pairs={{0,16},{4,20},{8,24},{12,28},{16,0},{20,4},{24,8},{28,12},{1,17},{... | collective-permute-start | bytes 294920 | tf_op jit(solution)/shard_map/ppermute | solution.py:705
  97.7 2.0 %collective-permute-start.39 = (f32[32,768]{1,0:T(8,128)S(1)}, f32[32,768]{1,0:T(8,128)S(1)}, u32[]{:S(2)}, u32[]{:S(2)}) collective-permute-start(f32[32,768]{1,0:T(8,128)S(1)} %get-tuple-element.119), channel_id=1, source_target_pairs={{0,24},{4,28},{8,16},{12,20},{16,8},{20,12},{24,0},{28,4},{1,25},{... | collective-permute-start | bytes 294920 | tf_op jit(solution)/shard_map/ppermute | solution.py:705
  99.7 1.7 %shard_map.149 = (f32[72,768]{1,0:T(8,128)S(1)}, f32[72,768]{1,0:T(8,128)S(1)}, f32[72,768]{1,0:T(8,128)S(1)}, f32[72,768]{1,0:T(8,128)S(1)}) custom-call(s32[2]{0:T(128)S(1)} %pad_add_fusion.place, bf16[576,256]{1,0:T(8,128)(2,1)S(1)} %copy-done.6, bf16[576,256]{1,0:T(8,128)(2,1)S(1)} %copy-done.5, f32[32,768]{1,0:T(8,128)S(1)} %get-tuple-element.99.refs_0_, ...), custom_call_target="tpu_custom_call" | custom-call | flops 2000000000 | bytes 6000000 | tf_op jit(solution)/shard_map/pallas_call | solution.py:669
  101.5 2.5 %collective-permute-start.40 = (f32[32,768]{1,0:T(8,128)S(1)}, f32[32,768]{1,0:T(8,128)S(1)}, u32[]{:S(2)}, u32[]{:S(2)}) collective-permute-start(f32[32,768]{1,0:T(8,128)S(1)} %get-tuple-element.123), channel_id=1, source_target_pairs={{0,28},{4,24},{8,20},{12,16},{16,12},{20,8},{24,4},{28,0},{1,29},{... | collective-permute-start | bytes 294920 | tf_op jit(solution)/shard_map/ppermute | solution.py:705
  104.0 2.2 %collective-permute-done.36.refs_1_ = f32[32,768]{1,0:T(8,128)S(1)} collective-permute-done((f32[32,768]{1,0:T(8,128)S(1)}, f32[32,768]{1,0:T(8,128)S(1)}, u32[]{:S(2)}, u32[]{:S(2)}) %collective-permute-start.36) | collective-permute-done | bytes 98336 | tf_op jit(solution)/shard_map/ppermute | solution.py:705
  106.2 3.9 %collective-permute-done.37.refs_2_ = f32[32,768]{1,0:T(8,128)S(1)} collective-permute-done((f32[32,768]{1,0:T(8,128)S(1)}, f32[32,768]{1,0:T(8,128)S(1)}, u32[]{:S(2)}, u32[]{:S(2)}) %collective-permute-start.37) | collective-permute-done | bytes 98336 | tf_op jit(solution)/shard_map/ppermute | solution.py:705
  110.9 1.4 %collective-permute-start.35 = (f32[72,768]{1,0:T(8,128)S(1)}, f32[72,768]{1,0:T(8,128)S(1)}, u32[]{:S(2)}, u32[]{:S(2)}) collective-permute-start(f32[72,768]{1,0:T(8,128)S(1)} %get-tuple-element.110), channel_id=1, source_target_pairs={{0,3},{1,2},{2,1},{3,0},{4,7},{5,6},{6,5},{7,4},{8,11},{9,10},{10,... | collective-permute-start | bytes 663560 | tf_op jit(solution)/shard_map/ppermute | solution.py:705
  112.3 3.4 %collective-permute-done.42.refs_7_ = f32[32,768]{1,0:T(8,128)S(1)} collective-permute-done((f32[32,768]{1,0:T(8,128)S(1)}, f32[32,768]{1,0:T(8,128)S(1)}, u32[]{:S(2)}, u32[]{:S(2)}) %collective-permute-start.42) | collective-permute-done | bytes 98336 | tf_op jit(solution)/shard_map/ppermute | solution.py:705
  115.6 1.7 %shard_map.153 = (f32[72,768]{1,0:T(8,128)S(1)}, f32[72,768]{1,0:T(8,128)S(1)}, f32[72,768]{1,0:T(8,128)S(1)}, f32[72,768]{1,0:T(8,128)S(1)}) custom-call(s32[2]{0:T(128)S(1)} %pad_add_fusion.place, bf16[576,256]{1,0:T(8,128)(2,1)S(1)} %copy-done.6, bf16[576,256]{1,0:T(8,128)(2,1)S(1)} %copy-done.5, f32[32,768]{1,0:T(8,128)S(1)} %get-tuple-element.115.refs_0_, ...), custom_call_target="tpu_custom_call" | custom-call | flops 2000000000 | bytes 6000000 | tf_op jit(solution)/shard_map/pallas_call | solution.py:669
  118.1 1.4 %collective-permute-start.45 = (f32[72,768]{1,0:T(8,128)S(1)}, f32[72,768]{1,0:T(8,128)S(1)}, u32[]{:S(2)}, u32[]{:S(2)}) collective-permute-start(f32[72,768]{1,0:T(8,128)S(1)} %get-tuple-element.129), channel_id=1, source_target_pairs={{0,1},{1,0},{2,3},{3,2},{4,5},{5,4},{6,7},{7,6},{8,9},{9,8},{10,11... | collective-permute-start | bytes 663560 | tf_op jit(solution)/shard_map/ppermute | solution.py:705
  119.5 1.2 collective-permute-done.35.refs_3_
  120.7 1.5 %shard_map.150 = (f32[3,4,80,256]{3,2,1,0:T(8,128)S(1)}, f32[3,64,256]{2,1,0:T(8,128)S(1)}, f32[3,64,256]{2,1,0:T(8,128)S(1)}) custom-call(s32[2]{0:T(128)S(1)} %pad_add_fusion.place, bf16[512,512]{1,0:T(8,128)(2,1)S(1)} %copy-done.2, bf16[512,512]{1,0:T(8,128)(2,1)S(1)} %copy-done.1, f32[72,768]{1,0:T(8,128)S(1)} %get-tuple-element.107.refs_0_.before, ...), custom_call_target="tpu_custom_call" | custom-call | flops 2000000000 | bytes 6000000 | tf_op jit(solution)/shard_map/pallas_call | solution.py:669
  122.8 4.1 %collective-permute-start.47 = (f32[3,64,256]{2,1,0:T(8,128)S(1)}, f32[3,64,256]{2,1,0:T(8,128)S(1)}, u32[]{:S(2)}, u32[]{:S(2)}) collective-permute-start(f32[3,64,256]{2,1,0:T(8,128)S(1)} %get-tuple-element.133), channel_id=1, source_target_pairs={{0,28},{4,0},{8,4},{12,8},{16,12},{20,16},{24,20},{28,24},{1,29},{... | collective-permute-start | bytes 589832 | tf_op jit(solution)/shard_map/ppermute | solution.py:833
  128.6 3.0 %shard_map.154 = (f32[3,8,64,256]{3,2,1,0:T(8,128)}, f32[3,8,64,256]{3,2,1,0:T(8,128)}) custom-call(s32[2]{0:T(128)S(1)} %pad_add_fusion.place, bf16[512,512]{1,0:T(8,128)(2,1)S(1)} %copy-done.2, bf16[512,512]{1,0:T(8,128)(2,1)S(1)} %copy-done.1, f32[3,4,80,256]{3,2,1,0:T(8,128)S(1)} %get-tuple-element.111.refs_0_.edges, ...), custom_call_target="tpu_custom_call" | custom-call | flops 4000000000 | bytes 12000000 | tf_op jit(solution)/shard_map/pallas_call | solution.py:669
  131.8 3.1 %collective-permute-done.47.after = f32[3,64,256]{2,1,0:T(8,128)S(1)} collective-permute-done((f32[3,64,256]{2,1,0:T(8,128)S(1)}, f32[3,64,256]{2,1,0:T(8,128)S(1)}, u32[]{:S(2)}, u32[]{:S(2)}) %collective-permute-start.47) | collective-permute-done | bytes 196640 | tf_op jit(solution)/shard_map/ppermute | solution.py:833
  (83 shorter events, 14.0 us)
Async XLA Ops:
  1.8 10.0 %collective-permute-start.3 = (f32[8,128]{1,0:T(8,128)S(1)}, f32[8,128]{1,0:T(8,128)S(1)}, u32[]{:S(2)}, u32[]{:S(2)}) collective-permute-start(f32[8,128]{1,0:T(8,128)S(1)} %get-tuple-element.69), channel_id=1, source_target_pairs={{0,8},{4,12},{8,16},{12,20},{16,24},{20,28},{24,0},{28,4},{1,9},{5... | collective-permute-start | bytes 12296 | tf_op jit(solution)/shard_map/ppermute | solution.py:742
  4.8 6.9 %collective-permute-start.2 = (f32[8,128]{1,0:T(8,128)S(1)}, f32[8,128]{1,0:T(8,128)S(1)}, u32[]{:S(2)}, u32[]{:S(2)}) collective-permute-start(f32[8,128]{1,0:T(8,128)S(1)} %get-tuple-element.69), channel_id=1, source_target_pairs={{0,24},{4,28},{8,0},{12,4},{16,8},{20,12},{24,16},{28,20},{1,25},{... | collective-permute-start | bytes 12296 | tf_op jit(solution)/shard_map/ppermute | solution.py:741
  6.9 6.4 %collective-permute-start.1 = (f32[8,512]{1,0:T(8,128)S(1)}, f32[8,512]{1,0:T(8,128)S(1)}, u32[]{:S(2)}, u32[]{:S(2)}) collective-permute-start(f32[8,512]{1,0:T(8,128)S(1)} %get-tuple-element.68.own), channel_id=1, source_target_pairs={{0,4},{4,8},{8,12},{12,16},{16,20},{20,24},{24,28},{28,0},{1,5},{5... | collective-permute-start | bytes 49160 | tf_op jit(solution)/shard_map/ppermute | solution.py:740
  8.6 4.8 %collective-permute-start = (f32[8,512]{1,0:T(8,128)S(1)}, f32[8,512]{1,0:T(8,128)S(1)}, u32[]{:S(2)}, u32[]{:S(2)}) collective-permute-start(f32[8,512]{1,0:T(8,128)S(1)} %get-tuple-element.68.own), channel_id=1, source_target_pairs={{0,28},{4,0},{8,4},{12,8},{16,12},{20,16},{24,20},{28,24},{1,29},{... | collective-permute-start | bytes 49160 | tf_op jit(solution)/shard_map/ppermute | solution.py:739
  17.1 10.0 %collective-permute-start.16 = (f32[72,768]{1,0:T(8,128)S(1)}, f32[72,768]{1,0:T(8,128)S(1)}, u32[]{:S(2)}, u32[]{:S(2)}) collective-permute-start(f32[72,768]{1,0:T(8,128)S(1)} %get-tuple-element.87), channel_id=1, source_target_pairs={{0,2},{1,3},{2,0},{3,1},{4,6},{5,7},{6,4},{7,5},{8,10},{9,11},{10,... | collective-permute-start | bytes 663560 | tf_op jit(solution)/shard_map/ppermute | solution.py:705
  18.8 8.4 %collective-permute-start.17 = (f32[72,768]{1,0:T(8,128)S(1)}, f32[72,768]{1,0:T(8,128)S(1)}, u32[]{:S(2)}, u32[]{:S(2)}) collective-permute-start(f32[72,768]{1,0:T(8,128)S(1)} %get-tuple-element.88), channel_id=1, source_target_pairs={{0,1},{1,0},{2,3},{3,2},{4,5},{5,4},{6,7},{7,6},{8,9},{9,8},{10,11... | collective-permute-start | bytes 663560 | tf_op jit(solution)/shard_map/ppermute | solution.py:705
  18.8 8.4 %collective-permute-start.18 = (f32[72,768]{1,0:T(8,128)S(1)}, f32[72,768]{1,0:T(8,128)S(1)}, u32[]{:S(2)}, u32[]{:S(2)}) collective-permute-start(f32[72,768]{1,0:T(8,128)S(1)} %get-tuple-element.89), channel_id=1, source_target_pairs={{0,3},{1,2},{2,1},{3,0},{4,7},{5,6},{6,5},{7,4},{8,11},{9,10},{10,... | collective-permute-start | bytes 663560 | tf_op jit(solution)/shard_map/ppermute | solution.py:705
  25.3 5.9 %collective-permute-start.6 = (f32[72,768]{1,0:T(8,128)S(1)}, f32[72,768]{1,0:T(8,128)S(1)}, u32[]{:S(2)}, u32[]{:S(2)}) collective-permute-start(f32[72,768]{1,0:T(8,128)S(1)} %get-tuple-element.75), channel_id=1, source_target_pairs={{0,1},{1,0},{2,3},{3,2},{4,5},{5,4},{6,7},{7,6},{8,9},{9,8},{10,11... | collective-permute-start | bytes 663560 | tf_op jit(solution)/shard_map/ppermute | solution.py:705
  25.4 8.3 %collective-permute-start.7 = (f32[72,768]{1,0:T(8,128)S(1)}, f32[72,768]{1,0:T(8,128)S(1)}, u32[]{:S(2)}, u32[]{:S(2)}) collective-permute-start(f32[72,768]{1,0:T(8,128)S(1)} %get-tuple-element.76), channel_id=1, source_target_pairs={{0,2},{1,3},{2,0},{3,1},{4,6},{5,7},{6,4},{7,5},{8,10},{9,11},{10,... | collective-permute-start | bytes 663560 | tf_op jit(solution)/shard_map/ppermute | solution.py:705
  27.1 10.4 %collective-permute-start.8 = (f32[72,768]{1,0:T(8,128)S(1)}, f32[72,768]{1,0:T(8,128)S(1)}, u32[]{:S(2)}, u32[]{:S(2)}) collective-permute-start(f32[72,768]{1,0:T(8,128)S(1)} %get-tuple-element.77), channel_id=1, source_target_pairs={{0,3},{1,2},{2,1},{3,0},{4,7},{5,6},{6,5},{7,4},{8,11},{9,10},{10,... | collective-permute-start | bytes 663560 | tf_op jit(solution)/shard_map/ppermute | solution.py:705
  28.8 14.9 %collective-permute-start.19 = (f32[32,768]{1,0:T(8,128)S(1)}, f32[32,768]{1,0:T(8,128)S(1)}, u32[]{:S(2)}, u32[]{:S(2)}) collective-permute-start(f32[32,768]{1,0:T(8,128)S(1)} %get-tuple-element.91), channel_id=1, source_target_pairs={{0,16},{4,20},{8,24},{12,28},{16,0},{20,4},{24,8},{28,12},{1,17},{... | collective-permute-start | bytes 294920 | tf_op jit(solution)/shard_map/ppermute | solution.py:705
  28.9 15.0 %collective-permute-start.20 = (f32[32,768]{1,0:T(8,128)S(1)}, f32[32,768]{1,0:T(8,128)S(1)}, u32[]{:S(2)}, u32[]{:S(2)}) collective-permute-start(f32[32,768]{1,0:T(8,128)S(1)} %get-tuple-element.92), channel_id=1, source_target_pairs={{0,20},{4,16},{8,28},{12,24},{16,4},{20,0},{24,12},{28,8},{1,21},{... | collective-permute-start | bytes 294920 | tf_op jit(solution)/shard_map/ppermute | solution.py:705
  31.1 14.0 %collective-permute-start.21 = (f32[32,768]{1,0:T(8,128)S(1)}, f32[32,768]{1,0:T(8,128)S(1)}, u32[]{:S(2)}, u32[]{:S(2)}) collective-permute-start(f32[32,768]{1,0:T(8,128)S(1)} %get-tuple-element.93), channel_id=1, source_target_pairs={{0,4},{4,0},{8,12},{12,8},{16,20},{20,16},{24,28},{28,24},{1,5},{5... | collective-permute-start | bytes 294920 | tf_op jit(solution)/shard_map/ppermute | solution.py:705
  33.6 12.4 %collective-permute-start.22 = (f32[32,768]{1,0:T(8,128)S(1)}, f32[32,768]{1,0:T(8,128)S(1)}, u32[]{:S(2)}, u32[]{:S(2)}) collective-permute-start(f32[32,768]{1,0:T(8,128)S(1)} %get-tuple-element.94), channel_id=1, source_target_pairs={{0,24},{4,28},{8,16},{12,20},{16,8},{20,12},{24,0},{28,4},{1,25},{... | collective-permute-start | bytes 294920 | tf_op jit(solution)/shard_map/ppermute | solution.py:705
  37.5 12.2 %collective-permute-start.23 = (f32[32,768]{1,0:T(8,128)S(1)}, f32[32,768]{1,0:T(8,128)S(1)}, u32[]{:S(2)}, u32[]{:S(2)}) collective-permute-start(f32[32,768]{1,0:T(8,128)S(1)} %get-tuple-element.95), channel_id=1, source_target_pairs={{0,28},{4,24},{8,20},{12,16},{16,12},{20,8},{24,4},{28,0},{1,29},{... | collective-permute-start | bytes 294920 | tf_op jit(solution)/shard_map/ppermute | solution.py:705
  43.8 7.8 %collective-permute-start.24 = (f32[32,768]{1,0:T(8,128)S(1)}, f32[32,768]{1,0:T(8,128)S(1)}, u32[]{:S(2)}, u32[]{:S(2)}) collective-permute-start(f32[32,768]{1,0:T(8,128)S(1)} %get-tuple-element.96), channel_id=1, source_target_pairs={{0,8},{4,12},{8,0},{12,4},{16,24},{20,28},{24,16},{28,20},{1,9},{5... | collective-permute-start | bytes 294920 | tf_op jit(solution)/shard_map/ppermute | solution.py:705
  43.9 8.6 %collective-permute-start.25 = (f32[32,768]{1,0:T(8,128)S(1)}, f32[32,768]{1,0:T(8,128)S(1)}, u32[]{:S(2)}, u32[]{:S(2)}) collective-permute-start(f32[32,768]{1,0:T(8,128)S(1)} %get-tuple-element.97), channel_id=1, source_target_pairs={{0,12},{4,8},{8,4},{12,0},{16,28},{20,24},{24,20},{28,16},{1,13},{... | collective-permute-start | bytes 294920 | tf_op jit(solution)/shard_map/ppermute | solution.py:705
  45.1 10.3 %collective-permute-start.9 = (f32[32,768]{1,0:T(8,128)S(1)}, f32[32,768]{1,0:T(8,128)S(1)}, u32[]{:S(2)}, u32[]{:S(2)}) collective-permute-start(f32[32,768]{1,0:T(8,128)S(1)} %get-tuple-element.79), channel_id=1, source_target_pairs={{0,16},{4,20},{8,24},{12,28},{16,0},{20,4},{24,8},{28,12},{1,17},{... | collective-permute-start | bytes 294920 | tf_op jit(solution)/shard_map/ppermute | solution.py:705
  46.0 16.9 %collective-permute-start.10 = (f32[32,768]{1,0:T(8,128)S(1)}, f32[32,768]{1,0:T(8,128)S(1)}, u32[]{:S(2)}, u32[]{:S(2)}) collective-permute-start(f32[32,768]{1,0:T(8,128)S(1)} %get-tuple-element.80), channel_id=1, source_target_pairs={{0,20},{4,16},{8,28},{12,24},{16,4},{20,0},{24,12},{28,8},{1,21},{... | collective-permute-start | bytes 294920 | tf_op jit(solution)/shard_map/ppermute | solution.py:705
  49.7 14.7 %collective-permute-start.11 = (f32[32,768]{1,0:T(8,128)S(1)}, f32[32,768]{1,0:T(8,128)S(1)}, u32[]{:S(2)}, u32[]{:S(2)}) collective-permute-start(f32[32,768]{1,0:T(8,128)S(1)} %get-tuple-element.81), channel_id=1, source_target_pairs={{0,4},{4,0},{8,12},{12,8},{16,20},{20,16},{24,28},{28,24},{1,5},{5... | collective-permute-start | bytes 294920 | tf_op jit(solution)/shard_map/ppermute | solution.py:705
  51.6 12.9 %collective-permute-start.12 = (f32[32,768]{1,0:T(8,128)S(1)}, f32[32,768]{1,0:T(8,128)S(1)}, u32[]{:S(2)}, u32[]{:S(2)}) collective-permute-start(f32[32,768]{1,0:T(8,128)S(1)} %get-tuple-element.82), channel_id=1, source_target_pairs={{0,24},{4,28},{8,16},{12,20},{16,8},{20,12},{24,0},{28,4},{1,25},{... | collective-permute-start | bytes 294920 | tf_op jit(solution)/shard_map/ppermute | solution.py:705
  52.4 13.8 %collective-permute-start.13 = (f32[32,768]{1,0:T(8,128)S(1)}, f32[32,768]{1,0:T(8,128)S(1)}, u32[]{:S(2)}, u32[]{:S(2)}) collective-permute-start(f32[32,768]{1,0:T(8,128)S(1)} %get-tuple-element.83), channel_id=1, source_target_pairs={{0,28},{4,24},{8,20},{12,16},{16,12},{20,8},{24,4},{28,0},{1,29},{... | collective-permute-start | bytes 294920 | tf_op jit(solution)/shard_map/ppermute | solution.py:705
  55.5 10.7 %collective-permute-start.14 = (f32[32,768]{1,0:T(8,128)S(1)}, f32[32,768]{1,0:T(8,128)S(1)}, u32[]{:S(2)}, u32[]{:S(2)}) collective-permute-start(f32[32,768]{1,0:T(8,128)S(1)} %get-tuple-element.84), channel_id=1, source_target_pairs={{0,8},{4,12},{8,0},{12,4},{16,24},{20,28},{24,16},{28,20},{1,9},{5... | collective-permute-start | bytes 294920 | tf_op jit(solution)/shard_map/ppermute | solution.py:705
  62.9 5.5 %collective-permute-start.15 = (f32[32,768]{1,0:T(8,128)S(1)}, f32[32,768]{1,0:T(8,128)S(1)}, u32[]{:S(2)}, u32[]{:S(2)}) collective-permute-start(f32[32,768]{1,0:T(8,128)S(1)} %get-tuple-element.85), channel_id=1, source_target_pairs={{0,12},{4,8},{8,4},{12,0},{16,28},{20,24},{24,20},{28,16},{1,13},{... | collective-permute-start | bytes 294920 | tf_op jit(solution)/shard_map/ppermute | solution.py:705
  64.4 5.4 %collective-permute-start.4 = (f32[48,256]{1,0:T(8,128)S(1)}, f32[48,256]{1,0:T(8,128)S(1)}, u32[]{:S(2)}, u32[]{:S(2)}) collective-permute-start(f32[48,256]{1,0:T(8,128)S(1)} %get-tuple-element.72), channel_id=1, source_target_pairs={{0,1},{1,2},{2,3},{3,0},{4,5},{5,6},{6,7},{7,4},{8,9},{9,10},{10,1... | collective-permute-start | bytes 147464 | tf_op jit(solution)/shard_map/ppermute | solution.py:763
  64.5 5.3 %collective-permute-start.5 = (f32[48,256]{1,0:T(8,128)S(1)}, f32[48,256]{1,0:T(8,128)S(1)}, u32[]{:S(2)}, u32[]{:S(2)}) collective-permute-start(f32[48,256]{1,0:T(8,128)S(1)} %get-tuple-element.73), channel_id=1, source_target_pairs={{0,3},{1,0},{2,1},{3,2},{4,7},{5,4},{6,5},{7,6},{8,11},{9,8},{10,9... | collective-permute-start | bytes 147464 | tf_op jit(solution)/shard_map/ppermute | solution.py:764
  73.6 14.2 %collective-permute-start.26 = (f32[32,768]{1,0:T(8,128)S(1)}, f32[32,768]{1,0:T(8,128)S(1)}, u32[]{:S(2)}, u32[]{:S(2)}) collective-permute-start(f32[32,768]{1,0:T(8,128)S(1)} %get-tuple-element.100), channel_id=1, source_target_pairs={{0,16},{4,20},{8,24},{12,28},{16,0},{20,4},{24,8},{28,12},{1,17},{... | collective-permute-start | bytes 294920 | tf_op jit(solution)/shard_map/ppermute | solution.py:705
  76.2 14.0 %collective-permute-start.27 = (f32[32,768]{1,0:T(8,128)S(1)}, f32[32,768]{1,0:T(8,128)S(1)}, u32[]{:S(2)}, u32[]{:S(2)}) collective-permute-start(f32[32,768]{1,0:T(8,128)S(1)} %get-tuple-element.101), channel_id=1, source_target_pairs={{0,20},{4,16},{8,28},{12,24},{16,4},{20,0},{24,12},{28,8},{1,21},{... | collective-permute-start | bytes 294920 | tf_op jit(solution)/shard_map/ppermute | solution.py:705
  76.2 16.2 %collective-permute-start.28 = (f32[32,768]{1,0:T(8,128)S(1)}, f32[32,768]{1,0:T(8,128)S(1)}, u32[]{:S(2)}, u32[]{:S(2)}) collective-permute-start(f32[32,768]{1,0:T(8,128)S(1)} %get-tuple-element.102), channel_id=1, source_target_pairs={{0,4},{4,0},{8,12},{12,8},{16,20},{20,16},{24,28},{28,24},{1,5},{5... | collective-permute-start | bytes 294920 | tf_op jit(solution)/shard_map/ppermute | solution.py:705
  78.0 18.1 %collective-permute-start.29 = (f32[32,768]{1,0:T(8,128)S(1)}, f32[32,768]{1,0:T(8,128)S(1)}, u32[]{:S(2)}, u32[]{:S(2)}) collective-permute-start(f32[32,768]{1,0:T(8,128)S(1)} %get-tuple-element.103), channel_id=1, source_target_pairs={{0,24},{4,28},{8,16},{12,20},{16,8},{20,12},{24,0},{28,4},{1,25},{... | collective-permute-start | bytes 294920 | tf_op jit(solution)/shard_map/ppermute | solution.py:705
  81.1 15.8 %collective-permute-start.30 = (f32[32,768]{1,0:T(8,128)S(1)}, f32[32,768]{1,0:T(8,128)S(1)}, u32[]{:S(2)}, u32[]{:S(2)}) collective-permute-start(f32[32,768]{1,0:T(8,128)S(1)} %get-tuple-element.104), channel_id=1, source_target_pairs={{0,28},{4,24},{8,20},{12,16},{16,12},{20,8},{24,4},{28,0},{1,29},{... | collective-permute-start | bytes 294920 | tf_op jit(solution)/shard_map/ppermute | solution.py:705
  87.8 9.9 %collective-permute-start.31 = (f32[32,768]{1,0:T(8,128)S(1)}, f32[32,768]{1,0:T(8,128)S(1)}, u32[]{:S(2)}, u32[]{:S(2)}) collective-permute-start(f32[32,768]{1,0:T(8,128)S(1)} %get-tuple-element.105), channel_id=1, source_target_pairs={{0,8},{4,12},{8,0},{12,4},{16,24},{20,28},{24,16},{28,20},{1,9},{5... | collective-permute-start | bytes 294920 | tf_op jit(solution)/shard_map/ppermute | solution.py:705
  90.3 9.5 %collective-permute-start.32 = (f32[32,768]{1,0:T(8,128)S(1)}, f32[32,768]{1,0:T(8,128)S(1)}, u32[]{:S(2)}, u32[]{:S(2)}) collective-permute-start(f32[32,768]{1,0:T(8,128)S(1)} %get-tuple-element.106), channel_id=1, source_target_pairs={{0,12},{4,8},{8,4},{12,0},{16,28},{20,24},{24,20},{28,16},{1,13},{... | collective-permute-start | bytes 294920 | tf_op jit(solution)/shard_map/ppermute | solution.py:705
  92.4 13.7 %collective-permute-start.36 = (f32[32,768]{1,0:T(8,128)S(1)}, f32[32,768]{1,0:T(8,128)S(1)}, u32[]{:S(2)}, u32[]{:S(2)}) collective-permute-start(f32[32,768]{1,0:T(8,128)S(1)} %get-tuple-element.116), channel_id=1, source_target_pairs={{0,16},{4,20},{8,24},{12,28},{16,0},{20,4},{24,8},{28,12},{1,17},{... | collective-permute-start | bytes 294920 | tf_op jit(solution)/shard_map/ppermute | solution.py:705
  96.1 14.0 %collective-permute-start.37 = (f32[32,768]{1,0:T(8,128)S(1)}, f32[32,768]{1,0:T(8,128)S(1)}, u32[]{:S(2)}, u32[]{:S(2)}) collective-permute-start(f32[32,768]{1,0:T(8,128)S(1)} %get-tuple-element.117), channel_id=1, source_target_pairs={{0,20},{4,16},{8,28},{12,24},{16,4},{20,0},{24,12},{28,8},{1,21},{... | collective-permute-start | bytes 294920 | tf_op jit(solution)/shard_map/ppermute | solution.py:705
  96.9 13.2 %collective-permute-start.38 = (f32[32,768]{1,0:T(8,128)S(1)}, f32[32,768]{1,0:T(8,128)S(1)}, u32[]{:S(2)}, u32[]{:S(2)}) collective-permute-start(f32[32,768]{1,0:T(8,128)S(1)} %get-tuple-element.118), channel_id=1, source_target_pairs={{0,4},{4,0},{8,12},{12,8},{16,20},{20,16},{24,28},{28,24},{1,5},{5... | collective-permute-start | bytes 294920 | tf_op jit(solution)/shard_map/ppermute | solution.py:705
  97.7 13.2 %collective-permute-start.39 = (f32[32,768]{1,0:T(8,128)S(1)}, f32[32,768]{1,0:T(8,128)S(1)}, u32[]{:S(2)}, u32[]{:S(2)}) collective-permute-start(f32[32,768]{1,0:T(8,128)S(1)} %get-tuple-element.119), channel_id=1, source_target_pairs={{0,24},{4,28},{8,16},{12,20},{16,8},{20,12},{24,0},{28,4},{1,25},{... | collective-permute-start | bytes 294920 | tf_op jit(solution)/shard_map/ppermute | solution.py:705
  101.5 9.4 %collective-permute-start.40 = (f32[32,768]{1,0:T(8,128)S(1)}, f32[32,768]{1,0:T(8,128)S(1)}, u32[]{:S(2)}, u32[]{:S(2)}) collective-permute-start(f32[32,768]{1,0:T(8,128)S(1)} %get-tuple-element.123), channel_id=1, source_target_pairs={{0,28},{4,24},{8,20},{12,16},{16,12},{20,8},{24,4},{28,0},{1,29},{... | collective-permute-start | bytes 294920 | tf_op jit(solution)/shard_map/ppermute | solution.py:705
  106.2 6.1 %collective-permute-start.41 = (f32[32,768]{1,0:T(8,128)S(1)}, f32[32,768]{1,0:T(8,128)S(1)}, u32[]{:S(2)}, u32[]{:S(2)}) collective-permute-start(f32[32,768]{1,0:T(8,128)S(1)} %get-tuple-element.124), channel_id=1, source_target_pairs={{0,8},{4,12},{8,0},{12,4},{16,24},{20,28},{24,16},{28,20},{1,9},{5... | collective-permute-start | bytes 294920 | tf_op jit(solution)/shard_map/ppermute | solution.py:705
  110.1 5.5 %collective-permute-start.42 = (f32[32,768]{1,0:T(8,128)S(1)}, f32[32,768]{1,0:T(8,128)S(1)}, u32[]{:S(2)}, u32[]{:S(2)}) collective-permute-start(f32[32,768]{1,0:T(8,128)S(1)} %get-tuple-element.125), channel_id=1, source_target_pairs={{0,12},{4,8},{8,4},{12,0},{16,28},{20,24},{24,20},{28,16},{1,13},{... | collective-permute-start | bytes 294920 | tf_op jit(solution)/shard_map/ppermute | solution.py:705
  110.1 8.0 %collective-permute-start.33 = (f32[72,768]{1,0:T(8,128)S(1)}, f32[72,768]{1,0:T(8,128)S(1)}, u32[]{:S(2)}, u32[]{:S(2)}) collective-permute-start(f32[72,768]{1,0:T(8,128)S(1)} %get-tuple-element.108), channel_id=1, source_target_pairs={{0,2},{1,3},{2,0},{3,1},{4,6},{5,7},{6,4},{7,5},{8,10},{9,11},{10,... | collective-permute-start | bytes 663560 | tf_op jit(solution)/shard_map/ppermute | solution.py:705
  110.9 8.6 %collective-permute-start.34 = (f32[72,768]{1,0:T(8,128)S(1)}, f32[72,768]{1,0:T(8,128)S(1)}, u32[]{:S(2)}, u32[]{:S(2)}) collective-permute-start(f32[72,768]{1,0:T(8,128)S(1)} %get-tuple-element.109), channel_id=1, source_target_pairs={{0,1},{1,0},{2,3},{3,2},{4,5},{5,4},{6,7},{7,6},{8,9},{9,8},{10,11... | collective-permute-start | bytes 663560 | tf_op jit(solution)/shard_map/ppermute | solution.py:705
  110.9 9.8 %collective-permute-start.35 = (f32[72,768]{1,0:T(8,128)S(1)}, f32[72,768]{1,0:T(8,128)S(1)}, u32[]{:S(2)}, u32[]{:S(2)}) collective-permute-start(f32[72,768]{1,0:T(8,128)S(1)} %get-tuple-element.110), channel_id=1, source_target_pairs={{0,3},{1,2},{2,1},{3,0},{4,7},{5,6},{6,5},{7,4},{8,11},{9,10},{10,... | collective-permute-start | bytes 663560 | tf_op jit(solution)/shard_map/ppermute | solution.py:705
  117.3 10.3 %collective-permute-start.43 = (f32[72,768]{1,0:T(8,128)S(1)}, f32[72,768]{1,0:T(8,128)S(1)}, u32[]{:S(2)}, u32[]{:S(2)}) collective-permute-start(f32[72,768]{1,0:T(8,128)S(1)} %get-tuple-element.127), channel_id=1, source_target_pairs={{0,2},{1,3},{2,0},{3,1},{4,6},{5,7},{6,4},{7,5},{8,10},{9,11},{10,... | collective-permute-start | bytes 663560 | tf_op jit(solution)/shard_map/ppermute | solution.py:705
  118.1 10.4 %collective-permute-start.44 = (f32[72,768]{1,0:T(8,128)S(1)}, f32[72,768]{1,0:T(8,128)S(1)}, u32[]{:S(2)}, u32[]{:S(2)}) collective-permute-start(f32[72,768]{1,0:T(8,128)S(1)} %get-tuple-element.128), channel_id=1, source_target_pairs={{0,3},{1,2},{2,1},{3,0},{4,7},{5,6},{6,5},{7,4},{8,11},{9,10},{10,... | collective-permute-start | bytes 663560 | tf_op jit(solution)/shard_map/ppermute | solution.py:705
  118.1 10.4 %collective-permute-start.45 = (f32[72,768]{1,0:T(8,128)S(1)}, f32[72,768]{1,0:T(8,128)S(1)}, u32[]{:S(2)}, u32[]{:S(2)}) collective-permute-start(f32[72,768]{1,0:T(8,128)S(1)} %get-tuple-element.129), channel_id=1, source_target_pairs={{0,1},{1,0},{2,3},{3,2},{4,5},{5,4},{6,7},{7,6},{8,9},{9,8},{10,11... | collective-permute-start | bytes 663560 | tf_op jit(solution)/shard_map/ppermute | solution.py:705
  122.2 9.6 %collective-permute-start.46 = (f32[3,64,256]{2,1,0:T(8,128)S(1)}, f32[3,64,256]{2,1,0:T(8,128)S(1)}, u32[]{:S(2)}, u32[]{:S(2)}) collective-permute-start(f32[3,64,256]{2,1,0:T(8,128)S(1)} %get-tuple-element.132), channel_id=1, source_target_pairs={{0,4},{4,8},{8,12},{12,16},{16,20},{20,24},{24,28},{28,0},{1,5},{5... | collective-permute-start | bytes 589832 | tf_op jit(solution)/shard_map/ppermute | solution.py:834
  122.8 12.0 %collective-permute-start.47 = (f32[3,64,256]{2,1,0:T(8,128)S(1)}, f32[3,64,256]{2,1,0:T(8,128)S(1)}, u32[]{:S(2)}, u32[]{:S(2)}) collective-permute-start(f32[3,64,256]{2,1,0:T(8,128)S(1)} %get-tuple-element.133), channel_id=1, source_target_pairs={{0,28},{4,0},{8,4},{12,8},{16,12},{20,16},{24,20},{28,24},{1,29},{... | collective-permute-start | bytes 589832 | tf_op jit(solution)/shard_map/ppermute | solution.py:833
  (9 other events, 81.7 us)

commit v17 on v15

--- a/solution.py
+++ b/solution.py
@@ -13,7 +13,7 @@
 MIG = 64
 LANES = 128
 RIM = 8
-LATE = 3
+LATE = 2
 TIME_STEP = 0.25
 VMEM = 24 * 1024 * 1024
 F32 = jnp.float32

time: 129 us -> 129 us (level)
  waiting for transfers between devices: 28.7 us -> 27.3 us
  starting transfers between devices: 68.7 us -> 70.1 us
    ppermute x40, starting transfers between devices: 52.2 us -> 53.6 us  [exchange(): lax.ppermute(block, axis, [(i, i ^ k) for i in range(count)])]
    ppermute x40, waiting for transfers between devices: 25.4 us -> 24 us  [exchange(): lax.ppermute(block, axis, [(i, i ^ k) for i in range(count)])]
    ppermute x1, starting transfers between devices: 4.35 us -> 2.99 us  [on_device(): after = lax.ppermute(first, 'gz', ring('gz', -1))]
    ppermute x1, starting transfers between devices: 0.42 us -> 1.78 us  [on_device(): before = lax.ppermute(last, 'gz', ring('gz', 1))]
  transfers between devices with their start and end apart: 48 -> 48, of which waited for: 16 -> 14; matrix products, arithmetic and copies ran while one was open for 0% -> 0% of each run, Pallas kernels for 16% -> 16%
where the time goes in v17:
time: 129 us
  starting transfers between devices  70.1 us (54%)
  Pallas kernels  30.6 us (24%)
  waiting for transfers between devices  27.3 us (21%)
    ppermute x40, starting transfers between devices, exchange(): lax.ppermute(block, axis, [(i, i ^ k) for i in range(count)])  53.6 us
    pallas_call x16, Pallas kernels, call(): pl.pallas_call(kernel, out_shape=[jax.ShapeDtypeStruct(shape, F32) for _,...  30.6 us
    ppermute x40, waiting for transfers between devices, exchange(): lax.ppermute(block, axis, [(i, i ^ k) for i in range(count)])  24 us
    ppermute x1, starting transfers between devices, on_device(): down2 = lax.ppermute(movers, 'gz', ring('gz', 2))  3.08 us
    ppermute x1, starting transfers between devices, on_device(): up1 = lax.ppermute(packet, 'gz', ring('gz', -1))  3.08 us
    ppermute x1, starting transfers between devices, on_device(): after = lax.ppermute(first, 'gz', ring('gz', -1))  2.99 us
  transfers between devices with their start and end apart: 48, of which 14 were waited for; matrix products, arithmetic and copies ran while one was open for 0% of the time, Pallas kernels for 16%

profile of v17, /device:TPU:0, one launch (start us, length us, event | category | flops | bytes accessed | tf_op | source)
XLA Modules:
  0.0 129.3 jit_solution(2393420858367237764)
XLA Ops:
  1.8 3.1 %collective-permute-start.3 = (f32[8,128]{1,0:T(8,128)S(1)}, f32[8,128]{1,0:T(8,128)S(1)}, u32[]{:S(2)}, u32[]{:S(2)}) collective-permute-start(f32[8,128]{1,0:T(8,128)S(1)} %get-tuple-element.68), channel_id=1, source_target_pairs={{0,8},{4,12},{8,16},{12,20},{16,24},{20,28},{24,0},{28,4},{1,9},{5... | collective-permute-start | bytes 12296 | tf_op jit(solution)/shard_map/ppermute | solution.py:740
  4.8 2.1 %collective-permute-start.2 = (f32[8,128]{1,0:T(8,128)S(1)}, f32[8,128]{1,0:T(8,128)S(1)}, u32[]{:S(2)}, u32[]{:S(2)}) collective-permute-start(f32[8,128]{1,0:T(8,128)S(1)} %get-tuple-element.68), channel_id=1, source_target_pairs={{0,24},{4,28},{8,0},{12,4},{16,8},{20,12},{24,16},{28,20},{1,25},{... | collective-permute-start | bytes 12296 | tf_op jit(solution)/shard_map/ppermute | solution.py:739
  6.9 1.6 %collective-permute-start.1 = (f32[8,512]{1,0:T(8,128)S(1)}, f32[8,512]{1,0:T(8,128)S(1)}, u32[]{:S(2)}, u32[]{:S(2)}) collective-permute-start(f32[8,512]{1,0:T(8,128)S(1)} %get-tuple-element.67.own), channel_id=1, source_target_pairs={{0,4},{4,8},{8,12},{12,16},{16,20},{20,24},{24,28},{28,0},{1,5},{5... | collective-permute-start | bytes 49160 | tf_op jit(solution)/shard_map/ppermute | solution.py:738
  8.6 3.1 %collective-permute-start = (f32[8,512]{1,0:T(8,128)S(1)}, f32[8,512]{1,0:T(8,128)S(1)}, u32[]{:S(2)}, u32[]{:S(2)}) collective-permute-start(f32[8,512]{1,0:T(8,128)S(1)} %get-tuple-element.67.own), channel_id=1, source_target_pairs={{0,28},{4,0},{8,4},{12,8},{16,12},{20,16},{24,20},{28,24},{1,29},{... | collective-permute-start | bytes 49160 | tf_op jit(solution)/shard_map/ppermute | solution.py:737
  11.7 1.6 %collective-permute-done.1.down1 = f32[8,512]{1,0:T(8,128)S(1)} collective-permute-done((f32[8,512]{1,0:T(8,128)S(1)}, f32[8,512]{1,0:T(8,128)S(1)}, u32[]{:S(2)}, u32[]{:S(2)}) %collective-permute-start.1) | collective-permute-done | bytes 16416 | tf_op jit(solution)/shard_map/ppermute | solution.py:738
  13.4 3.7 %shard_map.141 = (f32[3,4,64,256]{3,2,1,0:T(8,128)S(1)}, f32[24,256]{1,0:T(8,128)S(1)}, f32[24,256]{1,0:T(8,128)S(1)}, f32[72,768]{1,0:T(8,128)S(1)}, f32[72,768...) custom-call(s32[2]{0:T(128)S(1)} %pad_add_fusion.place, f32[8,512]{1,0:T(8,128)S(1)} %get-tuple-element.67.own, ...), custom_call_target="tpu_custom_call" | custom-call | flops 5000000000 | bytes 15000000 | tf_op jit(solution)/shard_map/pallas_call | solution.py:667
  17.1 1.7 %collective-permute-start.16 = (f32[72,768]{1,0:T(8,128)S(1)}, f32[72,768]{1,0:T(8,128)S(1)}, u32[]{:S(2)}, u32[]{:S(2)}) collective-permute-start(f32[72,768]{1,0:T(8,128)S(1)} %get-tuple-element.86), channel_id=1, source_target_pairs={{0,2},{1,3},{2,0},{3,1},{4,6},{5,7},{6,4},{7,5},{8,10},{9,11},{10,... | collective-permute-start | bytes 663560 | tf_op jit(solution)/shard_map/ppermute | solution.py:703
  19.3 6.0 %shard_map.142 = (f32[3,4,64,256]{3,2,1,0:T(8,128)S(1)}, f32[48,256]{1,0:T(8,128)S(1)}, f32[48,256]{1,0:T(8,128)S(1)}, f32[72,768]{1,0:T(8,128)S(1)}, f32[72,768...) custom-call(s32[2]{0:T(128)S(1)} %pad_add_fusion.place, f32[8,512]{1,0:T(8,128)S(1)} %get-tuple-element.67.own, ...), custom_call_target="tpu_custom_call" | custom-call | flops 5000000000 | bytes 15000000 | tf_op jit(solution)/shard_map/pallas_call | solution.py:667
  25.4 1.7 %collective-permute-start.7 = (f32[72,768]{1,0:T(8,128)S(1)}, f32[72,768]{1,0:T(8,128)S(1)}, u32[]{:S(2)}, u32[]{:S(2)}) collective-permute-start(f32[72,768]{1,0:T(8,128)S(1)} %get-tuple-element.75), channel_id=1, source_target_pairs={{0,2},{1,3},{2,0},{3,1},{4,6},{5,7},{6,4},{7,5},{8,10},{9,11},{10,... | collective-permute-start | bytes 663560 | tf_op jit(solution)/shard_map/ppermute | solution.py:703
  27.2 1.6 %shard_map.145 = (f32[32,768]{1,0:T(8,128)S(1)}, f32[32,768]{1,0:T(8,128)S(1)}, f32[32,768]{1,0:T(8,128)S(1)}, f32[32,768]{1,0:T(8,128)S(1)}, f32[32,768]{1,0:T(...) custom-call(s32[2]{0:T(128)S(1)} %pad_add_fusion.place, ...), custom_call_target="tpu_custom_call" | custom-call | flops 2000000000 | bytes 6000000 | tf_op jit(solution)/shard_map/pallas_call | solution.py:667
  28.9 2.2 %collective-permute-start.20 = (f32[32,768]{1,0:T(8,128)S(1)}, f32[32,768]{1,0:T(8,128)S(1)}, u32[]{:S(2)}, u32[]{:S(2)}) collective-permute-start(f32[32,768]{1,0:T(8,128)S(1)} %get-tuple-element.91), channel_id=1, source_target_pairs={{0,4},{4,0},{8,12},{12,8},{16,20},{20,16},{24,28},{28,24},{1,5},{5... | collective-permute-start | bytes 294920 | tf_op jit(solution)/shard_map/ppermute | solution.py:703
  31.1 2.2 %collective-permute-start.21 = (f32[32,768]{1,0:T(8,128)S(1)}, f32[32,768]{1,0:T(8,128)S(1)}, u32[]{:S(2)}, u32[]{:S(2)}) collective-permute-start(f32[32,768]{1,0:T(8,128)S(1)} %get-tuple-element.92), channel_id=1, source_target_pairs={{0,20},{4,16},{8,28},{12,24},{16,4},{20,0},{24,12},{28,8},{1,21},{... | collective-permute-start | bytes 294920 | tf_op jit(solution)/shard_map/ppermute | solution.py:703
  34.8 2.6 %collective-permute-done.8.refs_3_ = f32[72,768]{1,0:T(8,128)S(1)} collective-permute-done((f32[72,768]{1,0:T(8,128)S(1)}, f32[72,768]{1,0:T(8,128)S(1)}, u32[]{:S(2)}, u32[]{:S(2)}) %collective-permute-start.8) | collective-permute-done | bytes 221216 | tf_op jit(solution)/shard_map/ppermute | solution.py:703
  38.2 1.6 %shard_map.143 = (f32[32,768]{1,0:T(8,128)S(1)}, f32[32,768]{1,0:T(8,128)S(1)}, f32[32,768]{1,0:T(8,128)S(1)}, f32[32,768]{1,0:T(8,128)S(1)}, f32[32,768]{1,0:T(...) custom-call(s32[2]{0:T(128)S(1)} %pad_add_fusion.place, ...), custom_call_target="tpu_custom_call" | custom-call | flops 2000000000 | bytes 6000000 | tf_op jit(solution)/shard_map/pallas_call | solution.py:667
  39.8 4.0 %collective-permute-start.24 = (f32[32,768]{1,0:T(8,128)S(1)}, f32[32,768]{1,0:T(8,128)S(1)}, u32[]{:S(2)}, u32[]{:S(2)}) collective-permute-start(f32[32,768]{1,0:T(8,128)S(1)} %get-tuple-element.95), channel_id=1, source_target_pairs={{0,28},{4,24},{8,20},{12,16},{16,12},{20,8},{24,4},{28,0},{1,29},{... | collective-permute-start | bytes 294920 | tf_op jit(solution)/shard_map/ppermute | solution.py:703
  43.9 1.3 %collective-permute-start.9 = (f32[32,768]{1,0:T(8,128)S(1)}, f32[32,768]{1,0:T(8,128)S(1)}, u32[]{:S(2)}, u32[]{:S(2)}) collective-permute-start(f32[32,768]{1,0:T(8,128)S(1)} %get-tuple-element.78), channel_id=1, source_target_pairs={{0,16},{4,20},{8,24},{12,28},{16,0},{20,4},{24,8},{28,12},{1,17},{... | collective-permute-start | bytes 294920 | tf_op jit(solution)/shard_map/ppermute | solution.py:703
  45.2 4.5 %collective-permute-start.10 = (f32[32,768]{1,0:T(8,128)S(1)}, f32[32,768]{1,0:T(8,128)S(1)}, u32[]{:S(2)}, u32[]{:S(2)}) collective-permute-start(f32[32,768]{1,0:T(8,128)S(1)} %get-tuple-element.79), channel_id=1, source_target_pairs={{0,4},{4,0},{8,12},{12,8},{16,20},{20,16},{24,28},{28,24},{1,5},{5... | collective-permute-start | bytes 294920 | tf_op jit(solution)/shard_map/ppermute | solution.py:703
  50.8 5.4 %collective-permute-start.13 = (f32[32,768]{1,0:T(8,128)S(1)}, f32[32,768]{1,0:T(8,128)S(1)}, u32[]{:S(2)}, u32[]{:S(2)}) collective-permute-start(f32[32,768]{1,0:T(8,128)S(1)} %get-tuple-element.82), channel_id=1, source_target_pairs={{0,24},{4,28},{8,16},{12,20},{16,8},{20,12},{24,0},{28,4},{1,25},{... | collective-permute-start | bytes 294920 | tf_op jit(solution)/shard_map/ppermute | solution.py:703
  56.3 3.0 %collective-permute-start.14 = (f32[32,768]{1,0:T(8,128)S(1)}, f32[32,768]{1,0:T(8,128)S(1)}, u32[]{:S(2)}, u32[]{:S(2)}) collective-permute-start(f32[32,768]{1,0:T(8,128)S(1)} %get-tuple-element.83), channel_id=1, source_target_pairs={{0,28},{4,24},{8,20},{12,16},{16,12},{20,8},{24,4},{28,0},{1,29},{... | collective-permute-start | bytes 294920 | tf_op jit(solution)/shard_map/ppermute | solution.py:703
  59.3 1.3 %shard_map.146.refs_1_ = f32[3,2,4,8,8,128]{5,4,3,2,1,0:T(8,128)S(1)} custom-call(s32[2]{0:T(128)S(1)} %pad_add_fusion.place, f32[32,768]{1,0:T(8,128)S(1)} %get-tuple-element.89.refs_0_, f32[32,768]{1,0:T(8,128)S(1)} %collective-permute-done.19.refs_1_, f32[32,768]{1,0:T(8,128)S(1)} %collective-permute-done.20.refs_2_, ...), custom_call_target="tpu_custom_call" | custom-call | flops 2000000000 | bytes 6000000 | tf_op jit(solution)/shard_map/pallas_call | solution.py:667
  60.7 1.7 %collective-permute-start.5 = (f32[48,256]{1,0:T(8,128)S(1)}, f32[48,256]{1,0:T(8,128)S(1)}, u32[]{:S(2)}, u32[]{:S(2)}) collective-permute-start(f32[48,256]{1,0:T(8,128)S(1)} %get-tuple-element.72), channel_id=1, source_target_pairs={{0,3},{1,0},{2,1},{3,2},{4,7},{5,4},{6,5},{7,6},{8,11},{9,8},{10,9... | collective-permute-start | bytes 147464 | tf_op jit(solution)/shard_map/ppermute | solution.py:762
  62.5 1.8 %collective-permute-done.14.refs_6_ = f32[32,768]{1,0:T(8,128)S(1)} collective-permute-done((f32[32,768]{1,0:T(8,128)S(1)}, f32[32,768]{1,0:T(8,128)S(1)}, u32[]{:S(2)}, u32[]{:S(2)}) %collective-permute-start.14) | collective-permute-done | bytes 98336 | tf_op jit(solution)/shard_map/ppermute | solution.py:703
  64.3 1.7 %collective-permute-done.15.refs_7_ = f32[32,768]{1,0:T(8,128)S(1)} collective-permute-done((f32[32,768]{1,0:T(8,128)S(1)}, f32[32,768]{1,0:T(8,128)S(1)}, u32[]{:S(2)}, u32[]{:S(2)}) %collective-permute-start.15) | collective-permute-done | bytes 98336 | tf_op jit(solution)/shard_map/ppermute | solution.py:703
  66.0 1.3 %shard_map.144.refs_0_ = f32[3,2,4,8,8,128]{5,4,3,2,1,0:T(8,128)S(1)} custom-call(s32[2]{0:T(128)S(1)} %pad_add_fusion.place, f32[32,768]{1,0:T(8,128)S(1)} %get-tuple-element.77.refs_0_, f32[32,768]{1,0:T(8,128)S(1)} %collective-permute-done.9.refs_1_, f32[32,768]{1,0:T(8,128)S(1)} %collective-permute-done.10.refs_2_, ...), custom_call_target="tpu_custom_call" | custom-call | flops 2000000000 | bytes 6000000 | tf_op jit(solution)/shard_map/pallas_call | solution.py:667
  67.4 2.3 %shard_map.147 = (f32[3,2,4,8,8,128]{5,4,3,2,1,0:T(8,128)S(1)}, f32[3,2,4,8,8,128]{5,4,3,2,1,0:T(8,128)S(1)}) custom-call(s32[2]{0:T(128)S(1)} %pad_add_fusion.place, f32[48,256]{1,0:T(8,128)S(1)} %collective-permute-done.4.low_rim.refs_1_, f32[48,256]{1,0:T(8,128)S(1)} %collective-permute-done.5.high_rim.refs_2_, ...), custom_call_target="tpu_custom_call" | custom-call | flops 5000000000 | bytes 15000000 | tf_op jit(solution)/shard_map/pallas_call | solution.py:667
  69.7 1.4 %shard_map.148 = (f32[32,768]{1,0:T(8,128)S(1)}, f32[32,768]{1,0:T(8,128)S(1)}, f32[32,768]{1,0:T(8,128)S(1)}, f32[32,768]{1,0:T(8,128)S(1)}, f32[32,768]{1,0:T(...) custom-call(s32[2]{0:T(128)S(1)} %pad_add_fusion.place, ...), custom_call_target="tpu_custom_call" | custom-call | flops 2000000000 | bytes 6000000 | tf_op jit(solution)/shard_map/pallas_call | solution.py:667
  71.1 2.2 %collective-permute-start.26 = (f32[32,768]{1,0:T(8,128)S(1)}, f32[32,768]{1,0:T(8,128)S(1)}, u32[]{:S(2)}, u32[]{:S(2)}) collective-permute-start(f32[32,768]{1,0:T(8,128)S(1)} %get-tuple-element.99), channel_id=1, source_target_pairs={{0,16},{4,20},{8,24},{12,28},{16,0},{20,4},{24,8},{28,12},{1,17},{... | collective-permute-start | bytes 294920 | tf_op jit(solution)/shard_map/ppermute | solution.py:703
  73.3 1.2 collective-permute-start.27
  76.8 2.4 %collective-permute-start.30 = (f32[32,768]{1,0:T(8,128)S(1)}, f32[32,768]{1,0:T(8,128)S(1)}, u32[]{:S(2)}, u32[]{:S(2)}) collective-permute-start(f32[32,768]{1,0:T(8,128)S(1)} %get-tuple-element.103), channel_id=1, source_target_pairs={{0,24},{4,28},{8,16},{12,20},{16,8},{20,12},{24,0},{28,4},{1,25},{... | collective-permute-start | bytes 294920 | tf_op jit(solution)/shard_map/ppermute | solution.py:703
  80.4 1.4 %collective-permute-start.31 = (f32[32,768]{1,0:T(8,128)S(1)}, f32[32,768]{1,0:T(8,128)S(1)}, u32[]{:S(2)}, u32[]{:S(2)}) collective-permute-start(f32[32,768]{1,0:T(8,128)S(1)} %get-tuple-element.104), channel_id=1, source_target_pairs={{0,28},{4,24},{8,20},{12,16},{16,12},{20,8},{24,4},{28,0},{1,29},{... | collective-permute-start | bytes 294920 | tf_op jit(solution)/shard_map/ppermute | solution.py:703
  81.8 1.4 %shard_map.151 = (f32[32,768]{1,0:T(8,128)S(1)}, f32[32,768]{1,0:T(8,128)S(1)}, f32[32,768]{1,0:T(8,128)S(1)}, f32[32,768]{1,0:T(8,128)S(1)}, f32[32,768]{1,0:T(...) custom-call(s32[2]{0:T(128)S(1)} %pad_add_fusion.place, ...), custom_call_target="tpu_custom_call" | custom-call | flops 2000000000 | bytes 6000000 | tf_op jit(solution)/shard_map/pallas_call | solution.py:667
  83.2 5.6 %collective-permute-done.28.refs_3_ = f32[32,768]{1,0:T(8,128)S(1)} collective-permute-done((f32[32,768]{1,0:T(8,128)S(1)}, f32[32,768]{1,0:T(8,128)S(1)}, u32[]{:S(2)}, u32[]{:S(2)}) %collective-permute-start.28) | collective-permute-done | bytes 98336 | tf_op jit(solution)/shard_map/ppermute | solution.py:703
  89.9 3.3 %collective-permute-start.38 = (f32[32,768]{1,0:T(8,128)S(1)}, f32[32,768]{1,0:T(8,128)S(1)}, u32[]{:S(2)}, u32[]{:S(2)}) collective-permute-start(f32[32,768]{1,0:T(8,128)S(1)} %get-tuple-element.117), channel_id=1, source_target_pairs={{0,20},{4,16},{8,28},{12,24},{16,4},{20,0},{24,12},{28,8},{1,21},{... | collective-permute-start | bytes 294920 | tf_op jit(solution)/shard_map/ppermute | solution.py:703
  93.2 2.5 %collective-permute-start.39 = (f32[32,768]{1,0:T(8,128)S(1)}, f32[32,768]{1,0:T(8,128)S(1)}, u32[]{:S(2)}, u32[]{:S(2)}) collective-permute-start(f32[32,768]{1,0:T(8,128)S(1)} %get-tuple-element.118), channel_id=1, source_target_pairs={{0,8},{4,12},{8,0},{12,4},{16,24},{20,28},{24,16},{28,20},{1,9},{5... | collective-permute-start | bytes 294920 | tf_op jit(solution)/shard_map/ppermute | solution.py:703
  95.9 1.7 %shard_map.149 = (f32[72,768]{1,0:T(8,128)S(1)}, f32[72,768]{1,0:T(8,128)S(1)}, f32[72,768]{1,0:T(8,128)S(1)}, f32[72,768]{1,0:T(8,128)S(1)}) custom-call(s32[2]{0:T(128)S(1)} %pad_add_fusion.place, bf16[576,256]{1,0:T(8,128)(2,1)S(1)} %copy-done.6, bf16[576,256]{1,0:T(8,128)(2,1)S(1)} %copy-done.5, f32[32,768]{1,0:T(8,128)S(1)} %get-tuple-element.98.refs_0_, ...), custom_call_target="tpu_custom_call" | custom-call | flops 2000000000 | bytes 6000000 | tf_op jit(solution)/shard_map/pallas_call | solution.py:667
  97.7 1.8 %collective-permute-start.41 = (f32[32,768]{1,0:T(8,128)S(1)}, f32[32,768]{1,0:T(8,128)S(1)}, u32[]{:S(2)}, u32[]{:S(2)}) collective-permute-start(f32[32,768]{1,0:T(8,128)S(1)} %get-tuple-element.122), channel_id=1, source_target_pairs={{0,28},{4,24},{8,20},{12,16},{16,12},{20,8},{24,4},{28,0},{1,29},{... | collective-permute-start | bytes 294920 | tf_op jit(solution)/shard_map/ppermute | solution.py:703
  100.5 2.1 %collective-permute-done.38.refs_3_ = f32[32,768]{1,0:T(8,128)S(1)} collective-permute-done((f32[32,768]{1,0:T(8,128)S(1)}, f32[32,768]{1,0:T(8,128)S(1)}, u32[]{:S(2)}, u32[]{:S(2)}) %collective-permute-start.38) | collective-permute-done | bytes 98336 | tf_op jit(solution)/shard_map/ppermute | solution.py:703
  103.5 1.5 %collective-permute-start.35 = (f32[72,768]{1,0:T(8,128)S(1)}, f32[72,768]{1,0:T(8,128)S(1)}, u32[]{:S(2)}, u32[]{:S(2)}) collective-permute-start(f32[72,768]{1,0:T(8,128)S(1)} %get-tuple-element.109), channel_id=1, source_target_pairs={{0,3},{1,2},{2,1},{3,0},{4,7},{5,6},{6,5},{7,4},{8,11},{9,10},{10,... | collective-permute-start | bytes 663560 | tf_op jit(solution)/shard_map/ppermute | solution.py:703
  105.9 1.9 %collective-permute-done.42.refs_7_ = f32[32,768]{1,0:T(8,128)S(1)} collective-permute-done((f32[32,768]{1,0:T(8,128)S(1)}, f32[32,768]{1,0:T(8,128)S(1)}, u32[]{:S(2)}, u32[]{:S(2)}) %collective-permute-start.42) | collective-permute-done | bytes 98336 | tf_op jit(solution)/shard_map/ppermute | solution.py:703
  107.7 1.7 %shard_map.153 = (f32[72,768]{1,0:T(8,128)S(1)}, f32[72,768]{1,0:T(8,128)S(1)}, f32[72,768]{1,0:T(8,128)S(1)}, f32[72,768]{1,0:T(8,128)S(1)}) custom-call(s32[2]{0:T(128)S(1)} %pad_add_fusion.place, bf16[576,256]{1,0:T(8,128)(2,1)S(1)} %copy-done.6, bf16[576,256]{1,0:T(8,128)(2,1)S(1)} %copy-done.5, f32[32,768]{1,0:T(8,128)S(1)} %get-tuple-element.114.refs_0_, ...), custom_call_target="tpu_custom_call" | custom-call | flops 2000000000 | bytes 6000000 | tf_op jit(solution)/shard_map/pallas_call | solution.py:667
  109.4 1.2 collective-permute-start.43
  111.6 2.5 %collective-permute-done.35.refs_3_ = f32[72,768]{1,0:T(8,128)S(1)} collective-permute-done((f32[72,768]{1,0:T(8,128)S(1)}, f32[72,768]{1,0:T(8,128)S(1)}, u32[]{:S(2)}, u32[]{:S(2)}) %collective-permute-start.35) | collective-permute-done | bytes 221216 | tf_op jit(solution)/shard_map/ppermute | solution.py:703
  114.1 1.5 %shard_map.150 = (f32[3,4,80,256]{3,2,1,0:T(8,128)S(1)}, f32[3,64,256]{2,1,0:T(8,128)S(1)}, f32[3,64,256]{2,1,0:T(8,128)S(1)}) custom-call(s32[2]{0:T(128)S(1)} %pad_add_fusion.place, bf16[512,512]{1,0:T(8,128)(2,1)S(1)} %copy-done.2, bf16[512,512]{1,0:T(8,128)(2,1)S(1)} %copy-done.1, f32[72,768]{1,0:T(8,128)S(1)} %get-tuple-element.106.refs_0_.before, ...), custom_call_target="tpu_custom_call" | custom-call | flops 2000000000 | bytes 6000000 | tf_op jit(solution)/shard_map/pallas_call | solution.py:667
  115.6 1.8 %collective-permute-start.46 = (f32[3,64,256]{2,1,0:T(8,128)S(1)}, f32[3,64,256]{2,1,0:T(8,128)S(1)}, u32[]{:S(2)}, u32[]{:S(2)}) collective-permute-start(f32[3,64,256]{2,1,0:T(8,128)S(1)} %get-tuple-element.130), channel_id=1, source_target_pairs={{0,4},{4,8},{8,12},{12,16},{16,20},{20,24},{24,28},{28,0},{1,5},{5... | collective-permute-start | bytes 589832 | tf_op jit(solution)/shard_map/ppermute | solution.py:832
  117.3 3.0 %collective-permute-start.47 = (f32[3,64,256]{2,1,0:T(8,128)S(1)}, f32[3,64,256]{2,1,0:T(8,128)S(1)}, u32[]{:S(2)}, u32[]{:S(2)}) collective-permute-start(f32[3,64,256]{2,1,0:T(8,128)S(1)} %get-tuple-element.131), channel_id=1, source_target_pairs={{0,28},{4,0},{8,4},{12,8},{16,12},{20,16},{24,20},{28,24},{1,29},{... | collective-permute-start | bytes 589832 | tf_op jit(solution)/shard_map/ppermute | solution.py:831
  120.4 3.0 %collective-permute-done.44.refs_7_ = f32[72,768]{1,0:T(8,128)S(1)} collective-permute-done((f32[72,768]{1,0:T(8,128)S(1)}, f32[72,768]{1,0:T(8,128)S(1)}, u32[]{:S(2)}, u32[]{:S(2)}) %collective-permute-start.44) | collective-permute-done | bytes 221216 | tf_op jit(solution)/shard_map/ppermute | solution.py:703
  123.3 3.0 %shard_map.154 = (f32[3,8,64,256]{3,2,1,0:T(8,128)}, f32[3,8,64,256]{3,2,1,0:T(8,128)}) custom-call(s32[2]{0:T(128)S(1)} %pad_add_fusion.place, bf16[512,512]{1,0:T(8,128)(2,1)S(1)} %copy-done.2, bf16[512,512]{1,0:T(8,128)(2,1)S(1)} %copy-done.1, f32[3,4,80,256]{3,2,1,0:T(8,128)S(1)} %get-tuple-element.110.refs_0_.edges, ...), custom_call_target="tpu_custom_call" | custom-call | flops 4000000000 | bytes 12000000 | tf_op jit(solution)/shard_map/pallas_call | solution.py:667
  126.3 1.7 %collective-permute-done.47.after = f32[3,64,256]{2,1,0:T(8,128)S(1)} collective-permute-done((f32[3,64,256]{2,1,0:T(8,128)S(1)}, f32[3,64,256]{2,1,0:T(8,128)S(1)}, u32[]{:S(2)}, u32[]{:S(2)}) %collective-permute-start.47) | collective-permute-done | bytes 196640 | tf_op jit(solution)/shard_map/ppermute | solution.py:831
  (83 shorter events, 15.1 us)
Async XLA Ops:
  1.8 10.0 %collective-permute-start.3 = (f32[8,128]{1,0:T(8,128)S(1)}, f32[8,128]{1,0:T(8,128)S(1)}, u32[]{:S(2)}, u32[]{:S(2)}) collective-permute-start(f32[8,128]{1,0:T(8,128)S(1)} %get-tuple-element.68), channel_id=1, source_target_pairs={{0,8},{4,12},{8,16},{12,20},{16,24},{20,28},{24,0},{28,4},{1,9},{5... | collective-permute-start | bytes 12296 | tf_op jit(solution)/shard_map/ppermute | solution.py:740
  4.8 6.9 %collective-permute-start.2 = (f32[8,128]{1,0:T(8,128)S(1)}, f32[8,128]{1,0:T(8,128)S(1)}, u32[]{:S(2)}, u32[]{:S(2)}) collective-permute-start(f32[8,128]{1,0:T(8,128)S(1)} %get-tuple-element.68), channel_id=1, source_target_pairs={{0,24},{4,28},{8,0},{12,4},{16,8},{20,12},{24,16},{28,20},{1,25},{... | collective-permute-start | bytes 12296 | tf_op jit(solution)/shard_map/ppermute | solution.py:739
  6.9 6.4 %collective-permute-start.1 = (f32[8,512]{1,0:T(8,128)S(1)}, f32[8,512]{1,0:T(8,128)S(1)}, u32[]{:S(2)}, u32[]{:S(2)}) collective-permute-start(f32[8,512]{1,0:T(8,128)S(1)} %get-tuple-element.67.own), channel_id=1, source_target_pairs={{0,4},{4,8},{8,12},{12,16},{16,20},{20,24},{24,28},{28,0},{1,5},{5... | collective-permute-start | bytes 49160 | tf_op jit(solution)/shard_map/ppermute | solution.py:738
  8.6 4.8 %collective-permute-start = (f32[8,512]{1,0:T(8,128)S(1)}, f32[8,512]{1,0:T(8,128)S(1)}, u32[]{:S(2)}, u32[]{:S(2)}) collective-permute-start(f32[8,512]{1,0:T(8,128)S(1)} %get-tuple-element.67.own), channel_id=1, source_target_pairs={{0,28},{4,0},{8,4},{12,8},{16,12},{20,16},{24,20},{28,24},{1,29},{... | collective-permute-start | bytes 49160 | tf_op jit(solution)/shard_map/ppermute | solution.py:737
  17.1 10.0 %collective-permute-start.16 = (f32[72,768]{1,0:T(8,128)S(1)}, f32[72,768]{1,0:T(8,128)S(1)}, u32[]{:S(2)}, u32[]{:S(2)}) collective-permute-start(f32[72,768]{1,0:T(8,128)S(1)} %get-tuple-element.86), channel_id=1, source_target_pairs={{0,2},{1,3},{2,0},{3,1},{4,6},{5,7},{6,4},{7,5},{8,10},{9,11},{10,... | collective-permute-start | bytes 663560 | tf_op jit(solution)/shard_map/ppermute | solution.py:703
  18.8 8.4 %collective-permute-start.17 = (f32[72,768]{1,0:T(8,128)S(1)}, f32[72,768]{1,0:T(8,128)S(1)}, u32[]{:S(2)}, u32[]{:S(2)}) collective-permute-start(f32[72,768]{1,0:T(8,128)S(1)} %get-tuple-element.87), channel_id=1, source_target_pairs={{0,1},{1,0},{2,3},{3,2},{4,5},{5,4},{6,7},{7,6},{8,9},{9,8},{10,11... | collective-permute-start | bytes 663560 | tf_op jit(solution)/shard_map/ppermute | solution.py:703
  18.8 8.4 %collective-permute-start.18 = (f32[72,768]{1,0:T(8,128)S(1)}, f32[72,768]{1,0:T(8,128)S(1)}, u32[]{:S(2)}, u32[]{:S(2)}) collective-permute-start(f32[72,768]{1,0:T(8,128)S(1)} %get-tuple-element.88), channel_id=1, source_target_pairs={{0,3},{1,2},{2,1},{3,0},{4,7},{5,6},{6,5},{7,4},{8,11},{9,10},{10,... | collective-permute-start | bytes 663560 | tf_op jit(solution)/shard_map/ppermute | solution.py:703
  25.3 5.8 %collective-permute-start.6 = (f32[72,768]{1,0:T(8,128)S(1)}, f32[72,768]{1,0:T(8,128)S(1)}, u32[]{:S(2)}, u32[]{:S(2)}) collective-permute-start(f32[72,768]{1,0:T(8,128)S(1)} %get-tuple-element.74), channel_id=1, source_target_pairs={{0,1},{1,0},{2,3},{3,2},{4,5},{5,4},{6,7},{7,6},{8,9},{9,8},{10,11... | collective-permute-start | bytes 663560 | tf_op jit(solution)/shard_map/ppermute | solution.py:703
  25.4 8.3 %collective-permute-start.7 = (f32[72,768]{1,0:T(8,128)S(1)}, f32[72,768]{1,0:T(8,128)S(1)}, u32[]{:S(2)}, u32[]{:S(2)}) collective-permute-start(f32[72,768]{1,0:T(8,128)S(1)} %get-tuple-element.75), channel_id=1, source_target_pairs={{0,2},{1,3},{2,0},{3,1},{4,6},{5,7},{6,4},{7,5},{8,10},{9,11},{10,... | collective-permute-start | bytes 663560 | tf_op jit(solution)/shard_map/ppermute | solution.py:703
  27.1 10.4 %collective-permute-start.8 = (f32[72,768]{1,0:T(8,128)S(1)}, f32[72,768]{1,0:T(8,128)S(1)}, u32[]{:S(2)}, u32[]{:S(2)}) collective-permute-start(f32[72,768]{1,0:T(8,128)S(1)} %get-tuple-element.76), channel_id=1, source_target_pairs={{0,3},{1,2},{2,1},{3,0},{4,7},{5,6},{6,5},{7,4},{8,11},{9,10},{10,... | collective-permute-start | bytes 663560 | tf_op jit(solution)/shard_map/ppermute | solution.py:703
  28.8 11.0 %collective-permute-start.19 = (f32[32,768]{1,0:T(8,128)S(1)}, f32[32,768]{1,0:T(8,128)S(1)}, u32[]{:S(2)}, u32[]{:S(2)}) collective-permute-start(f32[32,768]{1,0:T(8,128)S(1)} %get-tuple-element.90), channel_id=1, source_target_pairs={{0,16},{4,20},{8,24},{12,28},{16,0},{20,4},{24,8},{28,12},{1,17},{... | collective-permute-start | bytes 294920 | tf_op jit(solution)/shard_map/ppermute | solution.py:703
  28.9 15.0 %collective-permute-start.20 = (f32[32,768]{1,0:T(8,128)S(1)}, f32[32,768]{1,0:T(8,128)S(1)}, u32[]{:S(2)}, u32[]{:S(2)}) collective-permute-start(f32[32,768]{1,0:T(8,128)S(1)} %get-tuple-element.91), channel_id=1, source_target_pairs={{0,4},{4,0},{8,12},{12,8},{16,20},{20,16},{24,28},{28,24},{1,5},{5... | collective-permute-start | bytes 294920 | tf_op jit(solution)/shard_map/ppermute | solution.py:703
  31.1 12.8 %collective-permute-start.21 = (f32[32,768]{1,0:T(8,128)S(1)}, f32[32,768]{1,0:T(8,128)S(1)}, u32[]{:S(2)}, u32[]{:S(2)}) collective-permute-start(f32[32,768]{1,0:T(8,128)S(1)} %get-tuple-element.92), channel_id=1, source_target_pairs={{0,20},{4,16},{8,28},{12,24},{16,4},{20,0},{24,12},{28,8},{1,21},{... | collective-permute-start | bytes 294920 | tf_op jit(solution)/shard_map/ppermute | solution.py:703
  33.6 11.5 %collective-permute-start.22 = (f32[32,768]{1,0:T(8,128)S(1)}, f32[32,768]{1,0:T(8,128)S(1)}, u32[]{:S(2)}, u32[]{:S(2)}) collective-permute-start(f32[32,768]{1,0:T(8,128)S(1)} %get-tuple-element.93), channel_id=1, source_target_pairs={{0,8},{4,12},{8,0},{12,4},{16,24},{20,28},{24,16},{28,20},{1,9},{5... | collective-permute-start | bytes 294920 | tf_op jit(solution)/shard_map/ppermute | solution.py:703
  37.5 12.3 %collective-permute-start.23 = (f32[32,768]{1,0:T(8,128)S(1)}, f32[32,768]{1,0:T(8,128)S(1)}, u32[]{:S(2)}, u32[]{:S(2)}) collective-permute-start(f32[32,768]{1,0:T(8,128)S(1)} %get-tuple-element.94), channel_id=1, source_target_pairs={{0,24},{4,28},{8,16},{12,20},{16,8},{20,12},{24,0},{28,4},{1,25},{... | collective-permute-start | bytes 294920 | tf_op jit(solution)/shard_map/ppermute | solution.py:703
  39.8 9.9 %collective-permute-start.24 = (f32[32,768]{1,0:T(8,128)S(1)}, f32[32,768]{1,0:T(8,128)S(1)}, u32[]{:S(2)}, u32[]{:S(2)}) collective-permute-start(f32[32,768]{1,0:T(8,128)S(1)} %get-tuple-element.95), channel_id=1, source_target_pairs={{0,28},{4,24},{8,20},{12,16},{16,12},{20,8},{24,4},{28,0},{1,29},{... | collective-permute-start | bytes 294920 | tf_op jit(solution)/shard_map/ppermute | solution.py:703
  43.9 7.0 %collective-permute-start.25 = (f32[32,768]{1,0:T(8,128)S(1)}, f32[32,768]{1,0:T(8,128)S(1)}, u32[]{:S(2)}, u32[]{:S(2)}) collective-permute-start(f32[32,768]{1,0:T(8,128)S(1)} %get-tuple-element.96), channel_id=1, source_target_pairs={{0,12},{4,8},{8,4},{12,0},{16,28},{20,24},{24,20},{28,16},{1,13},{... | collective-permute-start | bytes 294920 | tf_op jit(solution)/shard_map/ppermute | solution.py:703
  43.9 12.4 %collective-permute-start.9 = (f32[32,768]{1,0:T(8,128)S(1)}, f32[32,768]{1,0:T(8,128)S(1)}, u32[]{:S(2)}, u32[]{:S(2)}) collective-permute-start(f32[32,768]{1,0:T(8,128)S(1)} %get-tuple-element.78), channel_id=1, source_target_pairs={{0,16},{4,20},{8,24},{12,28},{16,0},{20,4},{24,8},{28,12},{1,17},{... | collective-permute-start | bytes 294920 | tf_op jit(solution)/shard_map/ppermute | solution.py:703
  45.2 14.1 %collective-permute-start.10 = (f32[32,768]{1,0:T(8,128)S(1)}, f32[32,768]{1,0:T(8,128)S(1)}, u32[]{:S(2)}, u32[]{:S(2)}) collective-permute-start(f32[32,768]{1,0:T(8,128)S(1)} %get-tuple-element.79), channel_id=1, source_target_pairs={{0,4},{4,0},{8,12},{12,8},{16,20},{20,16},{24,28},{28,24},{1,5},{5... | collective-permute-start | bytes 294920 | tf_op jit(solution)/shard_map/ppermute | solution.py:703
  49.7 10.9 %collective-permute-start.11 = (f32[32,768]{1,0:T(8,128)S(1)}, f32[32,768]{1,0:T(8,128)S(1)}, u32[]{:S(2)}, u32[]{:S(2)}) collective-permute-start(f32[32,768]{1,0:T(8,128)S(1)} %get-tuple-element.80), channel_id=1, source_target_pairs={{0,20},{4,16},{8,28},{12,24},{16,4},{20,0},{24,12},{28,8},{1,21},{... | collective-permute-start | bytes 294920 | tf_op jit(solution)/shard_map/ppermute | solution.py:703
  49.7 11.0 %collective-permute-start.12 = (f32[32,768]{1,0:T(8,128)S(1)}, f32[32,768]{1,0:T(8,128)S(1)}, u32[]{:S(2)}, u32[]{:S(2)}) collective-permute-start(f32[32,768]{1,0:T(8,128)S(1)} %get-tuple-element.81), channel_id=1, source_target_pairs={{0,8},{4,12},{8,0},{12,4},{16,24},{20,28},{24,16},{28,20},{1,9},{5... | collective-permute-start | bytes 294920 | tf_op jit(solution)/shard_map/ppermute | solution.py:703
  50.8 11.6 %collective-permute-start.13 = (f32[32,768]{1,0:T(8,128)S(1)}, f32[32,768]{1,0:T(8,128)S(1)}, u32[]{:S(2)}, u32[]{:S(2)}) collective-permute-start(f32[32,768]{1,0:T(8,128)S(1)} %get-tuple-element.82), channel_id=1, source_target_pairs={{0,24},{4,28},{8,16},{12,20},{16,8},{20,12},{24,0},{28,4},{1,25},{... | collective-permute-start | bytes 294920 | tf_op jit(solution)/shard_map/ppermute | solution.py:703
  56.3 8.0 %collective-permute-start.14 = (f32[32,768]{1,0:T(8,128)S(1)}, f32[32,768]{1,0:T(8,128)S(1)}, u32[]{:S(2)}, u32[]{:S(2)}) collective-permute-start(f32[32,768]{1,0:T(8,128)S(1)} %get-tuple-element.83), channel_id=1, source_target_pairs={{0,28},{4,24},{8,20},{12,16},{16,12},{20,8},{24,4},{28,0},{1,29},{... | collective-permute-start | bytes 294920 | tf_op jit(solution)/shard_map/ppermute | solution.py:703
  59.3 6.7 %collective-permute-start.15 = (f32[32,768]{1,0:T(8,128)S(1)}, f32[32,768]{1,0:T(8,128)S(1)}, u32[]{:S(2)}, u32[]{:S(2)}) collective-permute-start(f32[32,768]{1,0:T(8,128)S(1)} %get-tuple-element.84), channel_id=1, source_target_pairs={{0,12},{4,8},{8,4},{12,0},{16,28},{20,24},{24,20},{28,16},{1,13},{... | collective-permute-start | bytes 294920 | tf_op jit(solution)/shard_map/ppermute | solution.py:703
  60.7 6.7 %collective-permute-start.4 = (f32[48,256]{1,0:T(8,128)S(1)}, f32[48,256]{1,0:T(8,128)S(1)}, u32[]{:S(2)}, u32[]{:S(2)}) collective-permute-start(f32[48,256]{1,0:T(8,128)S(1)} %get-tuple-element.71), channel_id=1, source_target_pairs={{0,1},{1,2},{2,3},{3,0},{4,5},{5,6},{6,7},{7,4},{8,9},{9,10},{10,1... | collective-permute-start | bytes 147464 | tf_op jit(solution)/shard_map/ppermute | solution.py:761
  60.7 6.6 %collective-permute-start.5 = (f32[48,256]{1,0:T(8,128)S(1)}, f32[48,256]{1,0:T(8,128)S(1)}, u32[]{:S(2)}, u32[]{:S(2)}) collective-permute-start(f32[48,256]{1,0:T(8,128)S(1)} %get-tuple-element.72), channel_id=1, source_target_pairs={{0,3},{1,0},{2,1},{3,2},{4,7},{5,4},{6,5},{7,6},{8,11},{9,8},{10,9... | collective-permute-start | bytes 147464 | tf_op jit(solution)/shard_map/ppermute | solution.py:762
  71.1 9.3 %collective-permute-start.26 = (f32[32,768]{1,0:T(8,128)S(1)}, f32[32,768]{1,0:T(8,128)S(1)}, u32[]{:S(2)}, u32[]{:S(2)}) collective-permute-start(f32[32,768]{1,0:T(8,128)S(1)} %get-tuple-element.99), channel_id=1, source_target_pairs={{0,16},{4,20},{8,24},{12,28},{16,0},{20,4},{24,8},{28,12},{1,17},{... | collective-permute-start | bytes 294920 | tf_op jit(solution)/shard_map/ppermute | solution.py:703
  73.3 8.5 %collective-permute-start.27 = (f32[32,768]{1,0:T(8,128)S(1)}, f32[32,768]{1,0:T(8,128)S(1)}, u32[]{:S(2)}, u32[]{:S(2)}) collective-permute-start(f32[32,768]{1,0:T(8,128)S(1)} %get-tuple-element.100), channel_id=1, source_target_pairs={{0,4},{4,0},{8,12},{12,8},{16,20},{20,16},{24,28},{28,24},{1,5},{5... | collective-permute-start | bytes 294920 | tf_op jit(solution)/shard_map/ppermute | solution.py:703
  74.6 14.2 %collective-permute-start.28 = (f32[32,768]{1,0:T(8,128)S(1)}, f32[32,768]{1,0:T(8,128)S(1)}, u32[]{:S(2)}, u32[]{:S(2)}) collective-permute-start(f32[32,768]{1,0:T(8,128)S(1)} %get-tuple-element.101), channel_id=1, source_target_pairs={{0,20},{4,16},{8,28},{12,24},{16,4},{20,0},{24,12},{28,8},{1,21},{... | collective-permute-start | bytes 294920 | tf_op jit(solution)/shard_map/ppermute | solution.py:703
  75.6 13.2 %collective-permute-start.29 = (f32[32,768]{1,0:T(8,128)S(1)}, f32[32,768]{1,0:T(8,128)S(1)}, u32[]{:S(2)}, u32[]{:S(2)}) collective-permute-start(f32[32,768]{1,0:T(8,128)S(1)} %get-tuple-element.102), channel_id=1, source_target_pairs={{0,8},{4,12},{8,0},{12,4},{16,24},{20,28},{24,16},{28,20},{1,9},{5... | collective-permute-start | bytes 294920 | tf_op jit(solution)/shard_map/ppermute | solution.py:703
  76.8 13.1 %collective-permute-start.30 = (f32[32,768]{1,0:T(8,128)S(1)}, f32[32,768]{1,0:T(8,128)S(1)}, u32[]{:S(2)}, u32[]{:S(2)}) collective-permute-start(f32[32,768]{1,0:T(8,128)S(1)} %get-tuple-element.103), channel_id=1, source_target_pairs={{0,24},{4,28},{8,16},{12,20},{16,8},{20,12},{24,0},{28,4},{1,25},{... | collective-permute-start | bytes 294920 | tf_op jit(solution)/shard_map/ppermute | solution.py:703
  80.4 12.8 %collective-permute-start.31 = (f32[32,768]{1,0:T(8,128)S(1)}, f32[32,768]{1,0:T(8,128)S(1)}, u32[]{:S(2)}, u32[]{:S(2)}) collective-permute-start(f32[32,768]{1,0:T(8,128)S(1)} %get-tuple-element.104), channel_id=1, source_target_pairs={{0,28},{4,24},{8,20},{12,16},{16,12},{20,8},{24,4},{28,0},{1,29},{... | collective-permute-start | bytes 294920 | tf_op jit(solution)/shard_map/ppermute | solution.py:703
  81.8 13.9 %collective-permute-start.32 = (f32[32,768]{1,0:T(8,128)S(1)}, f32[32,768]{1,0:T(8,128)S(1)}, u32[]{:S(2)}, u32[]{:S(2)}) collective-permute-start(f32[32,768]{1,0:T(8,128)S(1)} %get-tuple-element.105), channel_id=1, source_target_pairs={{0,12},{4,8},{8,4},{12,0},{16,28},{20,24},{24,20},{28,16},{1,13},{... | collective-permute-start | bytes 294920 | tf_op jit(solution)/shard_map/ppermute | solution.py:703
  88.8 8.8 %collective-permute-start.36 = (f32[32,768]{1,0:T(8,128)S(1)}, f32[32,768]{1,0:T(8,128)S(1)}, u32[]{:S(2)}, u32[]{:S(2)}) collective-permute-start(f32[32,768]{1,0:T(8,128)S(1)} %get-tuple-element.115), channel_id=1, source_target_pairs={{0,16},{4,20},{8,24},{12,28},{16,0},{20,4},{24,8},{28,12},{1,17},{... | collective-permute-start | bytes 294920 | tf_op jit(solution)/shard_map/ppermute | solution.py:703
  88.8 10.7 %collective-permute-start.37 = (f32[32,768]{1,0:T(8,128)S(1)}, f32[32,768]{1,0:T(8,128)S(1)}, u32[]{:S(2)}, u32[]{:S(2)}) collective-permute-start(f32[32,768]{1,0:T(8,128)S(1)} %get-tuple-element.116), channel_id=1, source_target_pairs={{0,4},{4,0},{8,12},{12,8},{16,20},{20,16},{24,28},{28,24},{1,5},{5... | collective-permute-start | bytes 294920 | tf_op jit(solution)/shard_map/ppermute | solution.py:703
  89.9 12.7 %collective-permute-start.38 = (f32[32,768]{1,0:T(8,128)S(1)}, f32[32,768]{1,0:T(8,128)S(1)}, u32[]{:S(2)}, u32[]{:S(2)}) collective-permute-start(f32[32,768]{1,0:T(8,128)S(1)} %get-tuple-element.117), channel_id=1, source_target_pairs={{0,20},{4,16},{8,28},{12,24},{16,4},{20,0},{24,12},{28,8},{1,21},{... | collective-permute-start | bytes 294920 | tf_op jit(solution)/shard_map/ppermute | solution.py:703
  93.2 10.3 %collective-permute-start.39 = (f32[32,768]{1,0:T(8,128)S(1)}, f32[32,768]{1,0:T(8,128)S(1)}, u32[]{:S(2)}, u32[]{:S(2)}) collective-permute-start(f32[32,768]{1,0:T(8,128)S(1)} %get-tuple-element.118), channel_id=1, source_target_pairs={{0,8},{4,12},{8,0},{12,4},{16,24},{20,28},{24,16},{28,20},{1,9},{5... | collective-permute-start | bytes 294920 | tf_op jit(solution)/shard_map/ppermute | solution.py:703
  95.7 7.7 %collective-permute-start.40 = (f32[32,768]{1,0:T(8,128)S(1)}, f32[32,768]{1,0:T(8,128)S(1)}, u32[]{:S(2)}, u32[]{:S(2)}) collective-permute-start(f32[32,768]{1,0:T(8,128)S(1)} %get-tuple-element.119), channel_id=1, source_target_pairs={{0,24},{4,28},{8,16},{12,20},{16,8},{20,12},{24,0},{28,4},{1,25},{... | collective-permute-start | bytes 294920 | tf_op jit(solution)/shard_map/ppermute | solution.py:703
  97.7 8.2 %collective-permute-start.41 = (f32[32,768]{1,0:T(8,128)S(1)}, f32[32,768]{1,0:T(8,128)S(1)}, u32[]{:S(2)}, u32[]{:S(2)}) collective-permute-start(f32[32,768]{1,0:T(8,128)S(1)} %get-tuple-element.122), channel_id=1, source_target_pairs={{0,28},{4,24},{8,20},{12,16},{16,12},{20,8},{24,4},{28,0},{1,29},{... | collective-permute-start | bytes 294920 | tf_op jit(solution)/shard_map/ppermute | solution.py:703
  99.5 8.3 %collective-permute-start.42 = (f32[32,768]{1,0:T(8,128)S(1)}, f32[32,768]{1,0:T(8,128)S(1)}, u32[]{:S(2)}, u32[]{:S(2)}) collective-permute-start(f32[32,768]{1,0:T(8,128)S(1)} %get-tuple-element.123), channel_id=1, source_target_pairs={{0,12},{4,8},{8,4},{12,0},{16,28},{20,24},{24,20},{28,16},{1,13},{... | collective-permute-start | bytes 294920 | tf_op jit(solution)/shard_map/ppermute | solution.py:703
  102.6 8.3 %collective-permute-start.33 = (f32[72,768]{1,0:T(8,128)S(1)}, f32[72,768]{1,0:T(8,128)S(1)}, u32[]{:S(2)}, u32[]{:S(2)}) collective-permute-start(f32[72,768]{1,0:T(8,128)S(1)} %get-tuple-element.107), channel_id=1, source_target_pairs={{0,2},{1,3},{2,0},{3,1},{4,6},{5,7},{6,4},{7,5},{8,10},{9,11},{10,... | collective-permute-start | bytes 663560 | tf_op jit(solution)/shard_map/ppermute | solution.py:703
  103.5 8.2 %collective-permute-start.34 = (f32[72,768]{1,0:T(8,128)S(1)}, f32[72,768]{1,0:T(8,128)S(1)}, u32[]{:S(2)}, u32[]{:S(2)}) collective-permute-start(f32[72,768]{1,0:T(8,128)S(1)} %get-tuple-element.108), channel_id=1, source_target_pairs={{0,1},{1,0},{2,3},{3,2},{4,5},{5,4},{6,7},{7,6},{8,9},{9,8},{10,11... | collective-permute-start | bytes 663560 | tf_op jit(solution)/shard_map/ppermute | solution.py:703
  103.5 10.6 %collective-permute-start.35 = (f32[72,768]{1,0:T(8,128)S(1)}, f32[72,768]{1,0:T(8,128)S(1)}, u32[]{:S(2)}, u32[]{:S(2)}) collective-permute-start(f32[72,768]{1,0:T(8,128)S(1)} %get-tuple-element.109), channel_id=1, source_target_pairs={{0,3},{1,2},{2,1},{3,0},{4,7},{5,6},{6,5},{7,4},{8,11},{9,10},{10,... | collective-permute-start | bytes 663560 | tf_op jit(solution)/shard_map/ppermute | solution.py:703
  109.4 11.0 %collective-permute-start.43 = (f32[72,768]{1,0:T(8,128)S(1)}, f32[72,768]{1,0:T(8,128)S(1)}, u32[]{:S(2)}, u32[]{:S(2)}) collective-permute-start(f32[72,768]{1,0:T(8,128)S(1)} %get-tuple-element.125), channel_id=1, source_target_pairs={{0,2},{1,3},{2,0},{3,1},{4,6},{5,7},{6,4},{7,5},{8,10},{9,11},{10,... | collective-permute-start | bytes 663560 | tf_op jit(solution)/shard_map/ppermute | solution.py:703
  110.7 12.7 %collective-permute-start.44 = (f32[72,768]{1,0:T(8,128)S(1)}, f32[72,768]{1,0:T(8,128)S(1)}, u32[]{:S(2)}, u32[]{:S(2)}) collective-permute-start(f32[72,768]{1,0:T(8,128)S(1)} %get-tuple-element.126), channel_id=1, source_target_pairs={{0,3},{1,2},{2,1},{3,0},{4,7},{5,6},{6,5},{7,4},{8,11},{9,10},{10,... | collective-permute-start | bytes 663560 | tf_op jit(solution)/shard_map/ppermute | solution.py:703
  110.9 12.4 %collective-permute-start.45 = (f32[72,768]{1,0:T(8,128)S(1)}, f32[72,768]{1,0:T(8,128)S(1)}, u32[]{:S(2)}, u32[]{:S(2)}) collective-permute-start(f32[72,768]{1,0:T(8,128)S(1)} %get-tuple-element.127), channel_id=1, source_target_pairs={{0,1},{1,0},{2,3},{3,2},{4,5},{5,4},{6,7},{7,6},{8,9},{9,8},{10,11... | collective-permute-start | bytes 663560 | tf_op jit(solution)/shard_map/ppermute | solution.py:703
  115.6 10.8 %collective-permute-start.46 = (f32[3,64,256]{2,1,0:T(8,128)S(1)}, f32[3,64,256]{2,1,0:T(8,128)S(1)}, u32[]{:S(2)}, u32[]{:S(2)}) collective-permute-start(f32[3,64,256]{2,1,0:T(8,128)S(1)} %get-tuple-element.130), channel_id=1, source_target_pairs={{0,4},{4,8},{8,12},{12,16},{16,20},{20,24},{24,28},{28,0},{1,5},{5... | collective-permute-start | bytes 589832 | tf_op jit(solution)/shard_map/ppermute | solution.py:832
  117.3 10.7 %collective-permute-start.47 = (f32[3,64,256]{2,1,0:T(8,128)S(1)}, f32[3,64,256]{2,1,0:T(8,128)S(1)}, u32[]{:S(2)}, u32[]{:S(2)}) collective-permute-start(f32[3,64,256]{2,1,0:T(8,128)S(1)} %get-tuple-element.131), channel_id=1, source_target_pairs={{0,28},{4,0},{8,4},{12,8},{16,12},{20,16},{24,20},{28,24},{1,29},{... | collective-permute-start | bytes 589832 | tf_op jit(solution)/shard_map/ppermute | solution.py:831
  (9 other events, 95.0 us)

commit v18 on v15

--- a/solution.py
+++ b/solution.py
@@ -226,15 +226,18 @@
         y_high, y_low = split(w_y)
         right = jnp.concatenate([y_high, y_high, y_low], axis=1)
         at = [listed.index(z) for z in wanted]
+        left = []
         for c in range(3):
             s_z = values[c : c + 1] * w_z
-            left = jnp.concatenate([s_z[z : z + 1] * w_x for z in wanted], axis=0)
-            l_high, l_low = split(left)
-            left = jnp.concatenate([l_high, l_low, l_high], axis=1)
-            added = lax.dot_general(
-                left, right, (((1,), (1,)), ((), ())), preferred_element_type=F32
-            )
-            total[c, at[0] : at[-1] + 1] += added.reshape(len(wanted), rows, ny)
+            left += [s_z[z : z + 1] * w_x for z in wanted]
+        l_high, l_low = split(jnp.concatenate(left, axis=0))
+        added = lax.dot_general(
+            jnp.concatenate([l_high, l_low, l_high], axis=1),
+            right,
+            (((1,), (1,)), ((), ())),
+            preferred_element_type=F32,
+        )
+        total[:, at[0] : at[-1] + 1] += added.reshape(3, len(wanted), rows, ny)
 
     for n, z in enumerate(listed):
         total[:, n, 0:cols] = ambient[:, z]

time: 129 us -> 130 us (level)
  starting transfers between devices: 68.7 us -> 72.8 us
  waiting for transfers between devices: 28.7 us -> 25.6 us
    ppermute x40, starting transfers between devices: 52.2 us -> 56.4 us  [exchange(): lax.ppermute(block, axis, [(i, i ^ k) for i in range(count)])]
    ppermute x40, waiting for transfers between devices: 25.4 us -> 21.7 us  [exchange(): lax.ppermute(block, axis, [(i, i ^ k) for i in range(count)])]
  transfers between devices with their start and end apart: 48 -> 48, of which waited for: 16 -> 13; matrix products, arithmetic and copies ran while one was open for 0% -> 0% of each run, Pallas kernels for 16% -> 16%
where the time goes in v18:
time: 130 us
  starting transfers between devices  72.8 us (56%)
  Pallas kernels  30.1 us (23%)
  waiting for transfers between devices  25.6 us (20%)
    ppermute x40, starting transfers between devices, exchange(): lax.ppermute(block, axis, [(i, i ^ k) for i in range(count)])  56.4 us
    pallas_call x16, Pallas kernels, call(): pl.pallas_call(kernel, out_shape=[jax.ShapeDtypeStruct(shape, F32) for _,...  30.1 us
    ppermute x40, waiting for transfers between devices, exchange(): lax.ppermute(block, axis, [(i, i ^ k) for i in range(count)])  21.7 us
    ppermute x1, starting transfers between devices, on_device(): after = lax.ppermute(first, 'gz', ring('gz', -1))  4.14 us
    ppermute x1, starting transfers between devices, on_device(): down2 = lax.ppermute(movers, 'gz', ring('gz', 2))  3.08 us
    ppermute x1, starting transfers between devices, on_device(): up1 = lax.ppermute(packet, 'gz', ring('gz', -1))  3.08 us
  transfers between devices with their start and end apart: 48, of which 13 were waited for; matrix products, arithmetic and copies ran while one was open for 0% of the time, Pallas kernels for 16%

profile of v18, /device:TPU:0, one launch (start us, length us, event | category | flops | bytes accessed | tf_op | source)
XLA Modules:
  0.0 129.8 jit_solution(8284488670357598222)
XLA Ops:
  1.8 3.1 %collective-permute-start.3 = (f32[8,128]{1,0:T(8,128)S(1)}, f32[8,128]{1,0:T(8,128)S(1)}, u32[]{:S(2)}, u32[]{:S(2)}) collective-permute-start(f32[8,128]{1,0:T(8,128)S(1)} %get-tuple-element.69), channel_id=1, source_target_pairs={{0,8},{4,12},{8,16},{12,20},{16,24},{20,28},{24,0},{28,4},{1,9},{5... | collective-permute-start | bytes 12296 | tf_op jit(solution)/shard_map/ppermute | solution.py:743
  4.8 2.1 %collective-permute-start.2 = (f32[8,128]{1,0:T(8,128)S(1)}, f32[8,128]{1,0:T(8,128)S(1)}, u32[]{:S(2)}, u32[]{:S(2)}) collective-permute-start(f32[8,128]{1,0:T(8,128)S(1)} %get-tuple-element.69), channel_id=1, source_target_pairs={{0,24},{4,28},{8,0},{12,4},{16,8},{20,12},{24,16},{28,20},{1,25},{... | collective-permute-start | bytes 12296 | tf_op jit(solution)/shard_map/ppermute | solution.py:742
  6.9 1.6 %collective-permute-start.1 = (f32[8,512]{1,0:T(8,128)S(1)}, f32[8,512]{1,0:T(8,128)S(1)}, u32[]{:S(2)}, u32[]{:S(2)}) collective-permute-start(f32[8,512]{1,0:T(8,128)S(1)} %get-tuple-element.68.own), channel_id=1, source_target_pairs={{0,4},{4,8},{8,12},{12,16},{16,20},{20,24},{24,28},{28,0},{1,5},{5... | collective-permute-start | bytes 49160 | tf_op jit(solution)/shard_map/ppermute | solution.py:741
  8.6 3.1 %collective-permute-start = (f32[8,512]{1,0:T(8,128)S(1)}, f32[8,512]{1,0:T(8,128)S(1)}, u32[]{:S(2)}, u32[]{:S(2)}) collective-permute-start(f32[8,512]{1,0:T(8,128)S(1)} %get-tuple-element.68.own), channel_id=1, source_target_pairs={{0,28},{4,0},{8,4},{12,8},{16,12},{20,16},{24,20},{28,24},{1,29},{... | collective-permute-start | bytes 49160 | tf_op jit(solution)/shard_map/ppermute | solution.py:740
  11.7 1.6 %collective-permute-done.1.down1 = f32[8,512]{1,0:T(8,128)S(1)} collective-permute-done((f32[8,512]{1,0:T(8,128)S(1)}, f32[8,512]{1,0:T(8,128)S(1)}, u32[]{:S(2)}, u32[]{:S(2)}) %collective-permute-start.1) | collective-permute-done | bytes 16416 | tf_op jit(solution)/shard_map/ppermute | solution.py:741
  13.4 4.1 %shard_map.141 = (f32[3,4,64,256]{3,2,1,0:T(8,128)S(1)}, f32[24,256]{1,0:T(8,128)S(1)}, f32[24,256]{1,0:T(8,128)S(1)}, f32[72,768]{1,0:T(8,128)S(1)}, f32[72,768...) custom-call(s32[2]{0:T(128)S(1)} %pad_add_fusion.place, f32[8,512]{1,0:T(8,128)S(1)} %get-tuple-element.68.own, ...), custom_call_target="tpu_custom_call" | custom-call | flops 5000000000 | bytes 15000000 | tf_op jit(solution)/shard_map/pallas_call | solution.py:670
  17.5 1.7 %collective-permute-start.16 = (f32[72,768]{1,0:T(8,128)S(1)}, f32[72,768]{1,0:T(8,128)S(1)}, u32[]{:S(2)}, u32[]{:S(2)}) collective-permute-start(f32[72,768]{1,0:T(8,128)S(1)} %get-tuple-element.87), channel_id=1, source_target_pairs={{0,2},{1,3},{2,0},{3,1},{4,6},{5,7},{6,4},{7,5},{8,10},{9,11},{10,... | collective-permute-start | bytes 663560 | tf_op jit(solution)/shard_map/ppermute | solution.py:706
  19.7 5.0 %shard_map.142 = (f32[3,4,64,256]{3,2,1,0:T(8,128)S(1)}, f32[48,256]{1,0:T(8,128)S(1)}, f32[48,256]{1,0:T(8,128)S(1)}, f32[72,768]{1,0:T(8,128)S(1)}, f32[72,768...) custom-call(s32[2]{0:T(128)S(1)} %pad_add_fusion.place, f32[8,512]{1,0:T(8,128)S(1)} %get-tuple-element.68.own, ...), custom_call_target="tpu_custom_call" | custom-call | flops 5000000000 | bytes 15000000 | tf_op jit(solution)/shard_map/pallas_call | solution.py:670
  24.9 1.7 %collective-permute-start.7 = (f32[72,768]{1,0:T(8,128)S(1)}, f32[72,768]{1,0:T(8,128)S(1)}, u32[]{:S(2)}, u32[]{:S(2)}) collective-permute-start(f32[72,768]{1,0:T(8,128)S(1)} %get-tuple-element.76), channel_id=1, source_target_pairs={{0,2},{1,3},{2,0},{3,1},{4,6},{5,7},{6,4},{7,5},{8,10},{9,11},{10,... | collective-permute-start | bytes 663560 | tf_op jit(solution)/shard_map/ppermute | solution.py:706
  27.2 1.6 %shard_map.145 = (f32[32,768]{1,0:T(8,128)S(1)}, f32[32,768]{1,0:T(8,128)S(1)}, f32[32,768]{1,0:T(8,128)S(1)}, f32[32,768]{1,0:T(8,128)S(1)}, f32[32,768]{1,0:T(...) custom-call(s32[2]{0:T(128)S(1)} %pad_add_fusion.place, ...), custom_call_target="tpu_custom_call" | custom-call | flops 2000000000 | bytes 6000000 | tf_op jit(solution)/shard_map/pallas_call | solution.py:670
  28.9 2.3 %collective-permute-start.20 = (f32[32,768]{1,0:T(8,128)S(1)}, f32[32,768]{1,0:T(8,128)S(1)}, u32[]{:S(2)}, u32[]{:S(2)}) collective-permute-start(f32[32,768]{1,0:T(8,128)S(1)} %get-tuple-element.92), channel_id=1, source_target_pairs={{0,4},{4,0},{8,12},{12,8},{16,20},{20,16},{24,28},{28,24},{1,5},{5... | collective-permute-start | bytes 294920 | tf_op jit(solution)/shard_map/ppermute | solution.py:706
  31.2 2.1 %collective-permute-start.21 = (f32[32,768]{1,0:T(8,128)S(1)}, f32[32,768]{1,0:T(8,128)S(1)}, u32[]{:S(2)}, u32[]{:S(2)}) collective-permute-start(f32[32,768]{1,0:T(8,128)S(1)} %get-tuple-element.93), channel_id=1, source_target_pairs={{0,20},{4,16},{8,28},{12,24},{16,4},{20,0},{24,12},{28,8},{1,21},{... | collective-permute-start | bytes 294920 | tf_op jit(solution)/shard_map/ppermute | solution.py:706
  33.3 1.5 %collective-permute-start.22 = (f32[32,768]{1,0:T(8,128)S(1)}, f32[32,768]{1,0:T(8,128)S(1)}, u32[]{:S(2)}, u32[]{:S(2)}) collective-permute-start(f32[32,768]{1,0:T(8,128)S(1)} %get-tuple-element.94), channel_id=1, source_target_pairs={{0,8},{4,12},{8,0},{12,4},{16,24},{20,28},{24,16},{28,20},{1,9},{5... | collective-permute-start | bytes 294920 | tf_op jit(solution)/shard_map/ppermute | solution.py:706
  34.8 2.6 %collective-permute-done.8.refs_3_ = f32[72,768]{1,0:T(8,128)S(1)} collective-permute-done((f32[72,768]{1,0:T(8,128)S(1)}, f32[72,768]{1,0:T(8,128)S(1)}, u32[]{:S(2)}, u32[]{:S(2)}) %collective-permute-start.8) | collective-permute-done | bytes 221216 | tf_op jit(solution)/shard_map/ppermute | solution.py:706
  38.2 1.6 %shard_map.143 = (f32[32,768]{1,0:T(8,128)S(1)}, f32[32,768]{1,0:T(8,128)S(1)}, f32[32,768]{1,0:T(8,128)S(1)}, f32[32,768]{1,0:T(8,128)S(1)}, f32[32,768]{1,0:T(...) custom-call(s32[2]{0:T(128)S(1)} %pad_add_fusion.place, ...), custom_call_target="tpu_custom_call" | custom-call | flops 2000000000 | bytes 6000000 | tf_op jit(solution)/shard_map/pallas_call | solution.py:670
  39.8 4.0 %collective-permute-start.24 = (f32[32,768]{1,0:T(8,128)S(1)}, f32[32,768]{1,0:T(8,128)S(1)}, u32[]{:S(2)}, u32[]{:S(2)}) collective-permute-start(f32[32,768]{1,0:T(8,128)S(1)} %get-tuple-element.96), channel_id=1, source_target_pairs={{0,28},{4,24},{8,20},{12,16},{16,12},{20,8},{24,4},{28,0},{1,29},{... | collective-permute-start | bytes 294920 | tf_op jit(solution)/shard_map/ppermute | solution.py:706
  43.9 1.3 %collective-permute-start.9 = (f32[32,768]{1,0:T(8,128)S(1)}, f32[32,768]{1,0:T(8,128)S(1)}, u32[]{:S(2)}, u32[]{:S(2)}) collective-permute-start(f32[32,768]{1,0:T(8,128)S(1)} %get-tuple-element.79), channel_id=1, source_target_pairs={{0,16},{4,20},{8,24},{12,28},{16,0},{20,4},{24,8},{28,12},{1,17},{... | collective-permute-start | bytes 294920 | tf_op jit(solution)/shard_map/ppermute | solution.py:706
  45.2 4.5 %collective-permute-start.10 = (f32[32,768]{1,0:T(8,128)S(1)}, f32[32,768]{1,0:T(8,128)S(1)}, u32[]{:S(2)}, u32[]{:S(2)}) collective-permute-start(f32[32,768]{1,0:T(8,128)S(1)} %get-tuple-element.80), channel_id=1, source_target_pairs={{0,4},{4,0},{8,12},{12,8},{16,20},{20,16},{24,28},{28,24},{1,5},{5... | collective-permute-start | bytes 294920 | tf_op jit(solution)/shard_map/ppermute | solution.py:706
  49.7 5.2 %collective-permute-start.12 = (f32[32,768]{1,0:T(8,128)S(1)}, f32[32,768]{1,0:T(8,128)S(1)}, u32[]{:S(2)}, u32[]{:S(2)}) collective-permute-start(f32[32,768]{1,0:T(8,128)S(1)} %get-tuple-element.82), channel_id=1, source_target_pairs={{0,8},{4,12},{8,0},{12,4},{16,24},{20,28},{24,16},{28,20},{1,9},{5... | collective-permute-start | bytes 294920 | tf_op jit(solution)/shard_map/ppermute | solution.py:706
  54.9 4.3 %collective-permute-start.14 = (f32[32,768]{1,0:T(8,128)S(1)}, f32[32,768]{1,0:T(8,128)S(1)}, u32[]{:S(2)}, u32[]{:S(2)}) collective-permute-start(f32[32,768]{1,0:T(8,128)S(1)} %get-tuple-element.84), channel_id=1, source_target_pairs={{0,28},{4,24},{8,20},{12,16},{16,12},{20,8},{24,4},{28,0},{1,29},{... | collective-permute-start | bytes 294920 | tf_op jit(solution)/shard_map/ppermute | solution.py:706
  59.2 1.3 %shard_map.146.refs_1_ = f32[3,2,4,8,8,128]{5,4,3,2,1,0:T(8,128)S(1)} custom-call(s32[2]{0:T(128)S(1)} %pad_add_fusion.place, f32[32,768]{1,0:T(8,128)S(1)} %get-tuple-element.90.refs_0_, f32[32,768]{1,0:T(8,128)S(1)} %collective-permute-done.19.refs_1_, f32[32,768]{1,0:T(8,128)S(1)} %collective-permute-done.20.refs_2_, ...), custom_call_target="tpu_custom_call" | custom-call | flops 2000000000 | bytes 6000000 | tf_op jit(solution)/shard_map/pallas_call | solution.py:670
  60.6 1.7 %collective-permute-start.5 = (f32[48,256]{1,0:T(8,128)S(1)}, f32[48,256]{1,0:T(8,128)S(1)}, u32[]{:S(2)}, u32[]{:S(2)}) collective-permute-start(f32[48,256]{1,0:T(8,128)S(1)} %get-tuple-element.73), channel_id=1, source_target_pairs={{0,3},{1,0},{2,1},{3,2},{4,7},{5,4},{6,5},{7,6},{8,11},{9,8},{10,9... | collective-permute-start | bytes 147464 | tf_op jit(solution)/shard_map/ppermute | solution.py:765
  62.3 1.9 %collective-permute-done.14.refs_6_ = f32[32,768]{1,0:T(8,128)S(1)} collective-permute-done((f32[32,768]{1,0:T(8,128)S(1)}, f32[32,768]{1,0:T(8,128)S(1)}, u32[]{:S(2)}, u32[]{:S(2)}) %collective-permute-start.14) | collective-permute-done | bytes 98336 | tf_op jit(solution)/shard_map/ppermute | solution.py:706
  64.3 1.6 %collective-permute-done.15.refs_7_ = f32[32,768]{1,0:T(8,128)S(1)} collective-permute-done((f32[32,768]{1,0:T(8,128)S(1)}, f32[32,768]{1,0:T(8,128)S(1)}, u32[]{:S(2)}, u32[]{:S(2)}) %collective-permute-start.15) | collective-permute-done | bytes 98336 | tf_op jit(solution)/shard_map/ppermute | solution.py:706
  65.8 1.3 %shard_map.144.refs_0_ = f32[3,2,4,8,8,128]{5,4,3,2,1,0:T(8,128)S(1)} custom-call(s32[2]{0:T(128)S(1)} %pad_add_fusion.place, f32[32,768]{1,0:T(8,128)S(1)} %get-tuple-element.78.refs_0_, f32[32,768]{1,0:T(8,128)S(1)} %collective-permute-done.9.refs_1_, f32[32,768]{1,0:T(8,128)S(1)} %collective-permute-done.10.refs_2_, ...), custom_call_target="tpu_custom_call" | custom-call | flops 2000000000 | bytes 6000000 | tf_op jit(solution)/shard_map/pallas_call | solution.py:670
  67.2 2.3 %shard_map.147 = (f32[3,2,4,8,8,128]{5,4,3,2,1,0:T(8,128)S(1)}, f32[3,2,4,8,8,128]{5,4,3,2,1,0:T(8,128)S(1)}) custom-call(s32[2]{0:T(128)S(1)} %pad_add_fusion.place, f32[48,256]{1,0:T(8,128)S(1)} %collective-permute-done.4.low_rim.refs_1_, f32[48,256]{1,0:T(8,128)S(1)} %collective-permute-done.5.high_rim.refs_2_, ...), custom_call_target="tpu_custom_call" | custom-call | flops 5000000000 | bytes 15000000 | tf_op jit(solution)/shard_map/pallas_call | solution.py:670
  69.6 1.4 %shard_map.148 = (f32[32,768]{1,0:T(8,128)S(1)}, f32[32,768]{1,0:T(8,128)S(1)}, f32[32,768]{1,0:T(8,128)S(1)}, f32[32,768]{1,0:T(8,128)S(1)}, f32[32,768]{1,0:T(...) custom-call(s32[2]{0:T(128)S(1)} %pad_add_fusion.place, ...), custom_call_target="tpu_custom_call" | custom-call | flops 2000000000 | bytes 6000000 | tf_op jit(solution)/shard_map/pallas_call | solution.py:670
  71.0 3.0 %collective-permute-start.26 = (f32[32,768]{1,0:T(8,128)S(1)}, f32[32,768]{1,0:T(8,128)S(1)}, u32[]{:S(2)}, u32[]{:S(2)}) collective-permute-start(f32[32,768]{1,0:T(8,128)S(1)} %get-tuple-element.100), channel_id=1, source_target_pairs={{0,16},{4,20},{8,24},{12,28},{16,0},{20,4},{24,8},{28,12},{1,17},{... | collective-permute-start | bytes 294920 | tf_op jit(solution)/shard_map/ppermute | solution.py:706
  74.4 1.2 collective-permute-start.28
  75.5 1.5 %collective-permute-start.29 = (f32[32,768]{1,0:T(8,128)S(1)}, f32[32,768]{1,0:T(8,128)S(1)}, u32[]{:S(2)}, u32[]{:S(2)}) collective-permute-start(f32[32,768]{1,0:T(8,128)S(1)} %get-tuple-element.103), channel_id=1, source_target_pairs={{0,8},{4,12},{8,0},{12,4},{16,24},{20,28},{24,16},{28,20},{1,9},{5... | collective-permute-start | bytes 294920 | tf_op jit(solution)/shard_map/ppermute | solution.py:706
  77.1 2.8 %collective-permute-start.30 = (f32[32,768]{1,0:T(8,128)S(1)}, f32[32,768]{1,0:T(8,128)S(1)}, u32[]{:S(2)}, u32[]{:S(2)}) collective-permute-start(f32[32,768]{1,0:T(8,128)S(1)} %get-tuple-element.104), channel_id=1, source_target_pairs={{0,24},{4,28},{8,16},{12,20},{16,8},{20,12},{24,0},{28,4},{1,25},{... | collective-permute-start | bytes 294920 | tf_op jit(solution)/shard_map/ppermute | solution.py:706
  79.8 2.7 %collective-permute-done.26.refs_1_ = f32[32,768]{1,0:T(8,128)S(1)} collective-permute-done((f32[32,768]{1,0:T(8,128)S(1)}, f32[32,768]{1,0:T(8,128)S(1)}, u32[]{:S(2)}, u32[]{:S(2)}) %collective-permute-start.26) | collective-permute-done | bytes 98336 | tf_op jit(solution)/shard_map/ppermute | solution.py:706
  83.3 1.4 %shard_map.151 = (f32[32,768]{1,0:T(8,128)S(1)}, f32[32,768]{1,0:T(8,128)S(1)}, f32[32,768]{1,0:T(8,128)S(1)}, f32[32,768]{1,0:T(8,128)S(1)}, f32[32,768]{1,0:T(...) custom-call(s32[2]{0:T(128)S(1)} %pad_add_fusion.place, ...), custom_call_target="tpu_custom_call" | custom-call | flops 2000000000 | bytes 6000000 | tf_op jit(solution)/shard_map/pallas_call | solution.py:670
  84.7 2.2 %collective-permute-done.28.refs_3_ = f32[32,768]{1,0:T(8,128)S(1)} collective-permute-done((f32[32,768]{1,0:T(8,128)S(1)}, f32[32,768]{1,0:T(8,128)S(1)}, u32[]{:S(2)}, u32[]{:S(2)}) %collective-permute-start.28) | collective-permute-done | bytes 98336 | tf_op jit(solution)/shard_map/ppermute | solution.py:706
  86.9 2.5 %collective-permute-start.36 = (f32[32,768]{1,0:T(8,128)S(1)}, f32[32,768]{1,0:T(8,128)S(1)}, u32[]{:S(2)}, u32[]{:S(2)}) collective-permute-start(f32[32,768]{1,0:T(8,128)S(1)} %get-tuple-element.116), channel_id=1, source_target_pairs={{0,16},{4,20},{8,24},{12,28},{16,0},{20,4},{24,8},{28,12},{1,17},{... | collective-permute-start | bytes 294920 | tf_op jit(solution)/shard_map/ppermute | solution.py:706
  90.1 1.2 collective-permute-start.38
  91.3 5.7 %collective-permute-start.39 = (f32[32,768]{1,0:T(8,128)S(1)}, f32[32,768]{1,0:T(8,128)S(1)}, u32[]{:S(2)}, u32[]{:S(2)}) collective-permute-start(f32[32,768]{1,0:T(8,128)S(1)} %get-tuple-element.119), channel_id=1, source_target_pairs={{0,8},{4,12},{8,0},{12,4},{16,24},{20,28},{24,16},{28,20},{1,9},{5... | collective-permute-start | bytes 294920 | tf_op jit(solution)/shard_map/ppermute | solution.py:706
  97.0 1.7 %shard_map.149 = (f32[72,768]{1,0:T(8,128)S(1)}, f32[72,768]{1,0:T(8,128)S(1)}, f32[72,768]{1,0:T(8,128)S(1)}, f32[72,768]{1,0:T(8,128)S(1)}) custom-call(s32[2]{0:T(128)S(1)} %pad_add_fusion.place, bf16[576,256]{1,0:T(8,128)(2,1)S(1)} %copy-done.6, bf16[576,256]{1,0:T(8,128)(2,1)S(1)} %copy-done.5, f32[32,768]{1,0:T(8,128)S(1)} %get-tuple-element.99.refs_0_, ...), custom_call_target="tpu_custom_call" | custom-call | flops 2000000000 | bytes 6000000 | tf_op jit(solution)/shard_map/pallas_call | solution.py:670
  98.8 2.4 %collective-permute-start.41 = (f32[32,768]{1,0:T(8,128)S(1)}, f32[32,768]{1,0:T(8,128)S(1)}, u32[]{:S(2)}, u32[]{:S(2)}) collective-permute-start(f32[32,768]{1,0:T(8,128)S(1)} %get-tuple-element.124), channel_id=1, source_target_pairs={{0,28},{4,24},{8,20},{12,16},{16,12},{20,8},{24,4},{28,0},{1,29},{... | collective-permute-start | bytes 294920 | tf_op jit(solution)/shard_map/ppermute | solution.py:706
  101.7 1.4 %collective-permute-start.33 = (f32[72,768]{1,0:T(8,128)S(1)}, f32[72,768]{1,0:T(8,128)S(1)}, u32[]{:S(2)}, u32[]{:S(2)}) collective-permute-start(f32[72,768]{1,0:T(8,128)S(1)} %get-tuple-element.108), channel_id=1, source_target_pairs={{0,2},{1,3},{2,0},{3,1},{4,6},{5,7},{6,4},{7,5},{8,10},{9,11},{10,... | collective-permute-start | bytes 663560 | tf_op jit(solution)/shard_map/ppermute | solution.py:706
  103.2 3.1 %collective-permute-done.40.refs_5_ = f32[32,768]{1,0:T(8,128)S(1)} collective-permute-done((f32[32,768]{1,0:T(8,128)S(1)}, f32[32,768]{1,0:T(8,128)S(1)}, u32[]{:S(2)}, u32[]{:S(2)}) %collective-permute-start.40) | collective-permute-done | bytes 98336 | tf_op jit(solution)/shard_map/ppermute | solution.py:706
  107.9 1.7 %shard_map.153 = (f32[72,768]{1,0:T(8,128)S(1)}, f32[72,768]{1,0:T(8,128)S(1)}, f32[72,768]{1,0:T(8,128)S(1)}, f32[72,768]{1,0:T(8,128)S(1)}) custom-call(s32[2]{0:T(128)S(1)} %pad_add_fusion.place, bf16[576,256]{1,0:T(8,128)(2,1)S(1)} %copy-done.6, bf16[576,256]{1,0:T(8,128)(2,1)S(1)} %copy-done.5, f32[32,768]{1,0:T(8,128)S(1)} %get-tuple-element.115.refs_0_, ...), custom_call_target="tpu_custom_call" | custom-call | flops 2000000000 | bytes 6000000 | tf_op jit(solution)/shard_map/pallas_call | solution.py:670
  111.8 2.2 %collective-permute-done.35.refs_3_ = f32[72,768]{1,0:T(8,128)S(1)} collective-permute-done((f32[72,768]{1,0:T(8,128)S(1)}, f32[72,768]{1,0:T(8,128)S(1)}, u32[]{:S(2)}, u32[]{:S(2)}) %collective-permute-start.35) | collective-permute-done | bytes 221216 | tf_op jit(solution)/shard_map/ppermute | solution.py:706
  114.1 1.5 %shard_map.150 = (f32[3,4,80,256]{3,2,1,0:T(8,128)S(1)}, f32[3,64,256]{2,1,0:T(8,128)S(1)}, f32[3,64,256]{2,1,0:T(8,128)S(1)}) custom-call(s32[2]{0:T(128)S(1)} %pad_add_fusion.place, bf16[512,512]{1,0:T(8,128)(2,1)S(1)} %copy-done.2, bf16[512,512]{1,0:T(8,128)(2,1)S(1)} %copy-done.1, f32[72,768]{1,0:T(8,128)S(1)} %get-tuple-element.107.refs_0_.before, ...), custom_call_target="tpu_custom_call" | custom-call | flops 2000000000 | bytes 6000000 | tf_op jit(solution)/shard_map/pallas_call | solution.py:670
  116.2 4.1 %collective-permute-start.47 = (f32[3,64,256]{2,1,0:T(8,128)S(1)}, f32[3,64,256]{2,1,0:T(8,128)S(1)}, u32[]{:S(2)}, u32[]{:S(2)}) collective-permute-start(f32[3,64,256]{2,1,0:T(8,128)S(1)} %get-tuple-element.133), channel_id=1, source_target_pairs={{0,28},{4,0},{8,4},{12,8},{16,12},{20,16},{24,20},{28,24},{1,29},{... | collective-permute-start | bytes 589832 | tf_op jit(solution)/shard_map/ppermute | solution.py:834
  120.3 2.9 %collective-permute-done.44.refs_7_ = f32[72,768]{1,0:T(8,128)S(1)} collective-permute-done((f32[72,768]{1,0:T(8,128)S(1)}, f32[72,768]{1,0:T(8,128)S(1)}, u32[]{:S(2)}, u32[]{:S(2)}) %collective-permute-start.44) | collective-permute-done | bytes 221216 | tf_op jit(solution)/shard_map/ppermute | solution.py:706
  123.3 3.0 %shard_map.154 = (f32[3,8,64,256]{3,2,1,0:T(8,128)}, f32[3,8,64,256]{3,2,1,0:T(8,128)}) custom-call(s32[2]{0:T(128)S(1)} %pad_add_fusion.place, bf16[512,512]{1,0:T(8,128)(2,1)S(1)} %copy-done.2, bf16[512,512]{1,0:T(8,128)(2,1)S(1)} %copy-done.1, f32[3,4,80,256]{3,2,1,0:T(8,128)S(1)} %get-tuple-element.111.refs_0_.edges, ...), custom_call_target="tpu_custom_call" | custom-call | flops 4000000000 | bytes 12000000 | tf_op jit(solution)/shard_map/pallas_call | solution.py:670
  126.3 2.3 %collective-permute-done.47.after = f32[3,64,256]{2,1,0:T(8,128)S(1)} collective-permute-done((f32[3,64,256]{2,1,0:T(8,128)S(1)}, f32[3,64,256]{2,1,0:T(8,128)S(1)}, u32[]{:S(2)}, u32[]{:S(2)}) %collective-permute-start.47) | collective-permute-done | bytes 196640 | tf_op jit(solution)/shard_map/ppermute | solution.py:834
  (83 shorter events, 11.3 us)
Async XLA Ops:
  1.8 10.0 %collective-permute-start.3 = (f32[8,128]{1,0:T(8,128)S(1)}, f32[8,128]{1,0:T(8,128)S(1)}, u32[]{:S(2)}, u32[]{:S(2)}) collective-permute-start(f32[8,128]{1,0:T(8,128)S(1)} %get-tuple-element.69), channel_id=1, source_target_pairs={{0,8},{4,12},{8,16},{12,20},{16,24},{20,28},{24,0},{28,4},{1,9},{5... | collective-permute-start | bytes 12296 | tf_op jit(solution)/shard_map/ppermute | solution.py:743
  4.8 6.9 %collective-permute-start.2 = (f32[8,128]{1,0:T(8,128)S(1)}, f32[8,128]{1,0:T(8,128)S(1)}, u32[]{:S(2)}, u32[]{:S(2)}) collective-permute-start(f32[8,128]{1,0:T(8,128)S(1)} %get-tuple-element.69), channel_id=1, source_target_pairs={{0,24},{4,28},{8,0},{12,4},{16,8},{20,12},{24,16},{28,20},{1,25},{... | collective-permute-start | bytes 12296 | tf_op jit(solution)/shard_map/ppermute | solution.py:742
  6.9 6.4 %collective-permute-start.1 = (f32[8,512]{1,0:T(8,128)S(1)}, f32[8,512]{1,0:T(8,128)S(1)}, u32[]{:S(2)}, u32[]{:S(2)}) collective-permute-start(f32[8,512]{1,0:T(8,128)S(1)} %get-tuple-element.68.own), channel_id=1, source_target_pairs={{0,4},{4,8},{8,12},{12,16},{16,20},{20,24},{24,28},{28,0},{1,5},{5... | collective-permute-start | bytes 49160 | tf_op jit(solution)/shard_map/ppermute | solution.py:741
  8.6 4.8 %collective-permute-start = (f32[8,512]{1,0:T(8,128)S(1)}, f32[8,512]{1,0:T(8,128)S(1)}, u32[]{:S(2)}, u32[]{:S(2)}) collective-permute-start(f32[8,512]{1,0:T(8,128)S(1)} %get-tuple-element.68.own), channel_id=1, source_target_pairs={{0,28},{4,0},{8,4},{12,8},{16,12},{20,16},{24,20},{28,24},{1,29},{... | collective-permute-start | bytes 49160 | tf_op jit(solution)/shard_map/ppermute | solution.py:740
  17.5 9.1 %collective-permute-start.16 = (f32[72,768]{1,0:T(8,128)S(1)}, f32[72,768]{1,0:T(8,128)S(1)}, u32[]{:S(2)}, u32[]{:S(2)}) collective-permute-start(f32[72,768]{1,0:T(8,128)S(1)} %get-tuple-element.87), channel_id=1, source_target_pairs={{0,2},{1,3},{2,0},{3,1},{4,6},{5,7},{6,4},{7,5},{8,10},{9,11},{10,... | collective-permute-start | bytes 663560 | tf_op jit(solution)/shard_map/ppermute | solution.py:706
  19.2 7.5 %collective-permute-start.17 = (f32[72,768]{1,0:T(8,128)S(1)}, f32[72,768]{1,0:T(8,128)S(1)}, u32[]{:S(2)}, u32[]{:S(2)}) collective-permute-start(f32[72,768]{1,0:T(8,128)S(1)} %get-tuple-element.88), channel_id=1, source_target_pairs={{0,1},{1,0},{2,3},{3,2},{4,5},{5,4},{6,7},{7,6},{8,9},{9,8},{10,11... | collective-permute-start | bytes 663560 | tf_op jit(solution)/shard_map/ppermute | solution.py:706
  19.2 8.0 %collective-permute-start.18 = (f32[72,768]{1,0:T(8,128)S(1)}, f32[72,768]{1,0:T(8,128)S(1)}, u32[]{:S(2)}, u32[]{:S(2)}) collective-permute-start(f32[72,768]{1,0:T(8,128)S(1)} %get-tuple-element.89), channel_id=1, source_target_pairs={{0,3},{1,2},{2,1},{3,0},{4,7},{5,6},{6,5},{7,4},{8,11},{9,10},{10,... | collective-permute-start | bytes 663560 | tf_op jit(solution)/shard_map/ppermute | solution.py:706
  24.7 6.5 %collective-permute-start.6 = (f32[72,768]{1,0:T(8,128)S(1)}, f32[72,768]{1,0:T(8,128)S(1)}, u32[]{:S(2)}, u32[]{:S(2)}) collective-permute-start(f32[72,768]{1,0:T(8,128)S(1)} %get-tuple-element.75), channel_id=1, source_target_pairs={{0,1},{1,0},{2,3},{3,2},{4,5},{5,4},{6,7},{7,6},{8,9},{9,8},{10,11... | collective-permute-start | bytes 663560 | tf_op jit(solution)/shard_map/ppermute | solution.py:706
  24.9 8.5 %collective-permute-start.7 = (f32[72,768]{1,0:T(8,128)S(1)}, f32[72,768]{1,0:T(8,128)S(1)}, u32[]{:S(2)}, u32[]{:S(2)}) collective-permute-start(f32[72,768]{1,0:T(8,128)S(1)} %get-tuple-element.76), channel_id=1, source_target_pairs={{0,2},{1,3},{2,0},{3,1},{4,6},{5,7},{6,4},{7,5},{8,10},{9,11},{10,... | collective-permute-start | bytes 663560 | tf_op jit(solution)/shard_map/ppermute | solution.py:706
  26.6 10.9 %collective-permute-start.8 = (f32[72,768]{1,0:T(8,128)S(1)}, f32[72,768]{1,0:T(8,128)S(1)}, u32[]{:S(2)}, u32[]{:S(2)}) collective-permute-start(f32[72,768]{1,0:T(8,128)S(1)} %get-tuple-element.77), channel_id=1, source_target_pairs={{0,3},{1,2},{2,1},{3,0},{4,7},{5,6},{6,5},{7,4},{8,11},{9,10},{10,... | collective-permute-start | bytes 663560 | tf_op jit(solution)/shard_map/ppermute | solution.py:706
  28.9 11.0 %collective-permute-start.19 = (f32[32,768]{1,0:T(8,128)S(1)}, f32[32,768]{1,0:T(8,128)S(1)}, u32[]{:S(2)}, u32[]{:S(2)}) collective-permute-start(f32[32,768]{1,0:T(8,128)S(1)} %get-tuple-element.91), channel_id=1, source_target_pairs={{0,16},{4,20},{8,24},{12,28},{16,0},{20,4},{24,8},{28,12},{1,17},{... | collective-permute-start | bytes 294920 | tf_op jit(solution)/shard_map/ppermute | solution.py:706
  28.9 14.9 %collective-permute-start.20 = (f32[32,768]{1,0:T(8,128)S(1)}, f32[32,768]{1,0:T(8,128)S(1)}, u32[]{:S(2)}, u32[]{:S(2)}) collective-permute-start(f32[32,768]{1,0:T(8,128)S(1)} %get-tuple-element.92), channel_id=1, source_target_pairs={{0,4},{4,0},{8,12},{12,8},{16,20},{20,16},{24,28},{28,24},{1,5},{5... | collective-permute-start | bytes 294920 | tf_op jit(solution)/shard_map/ppermute | solution.py:706
  31.2 12.7 %collective-permute-start.21 = (f32[32,768]{1,0:T(8,128)S(1)}, f32[32,768]{1,0:T(8,128)S(1)}, u32[]{:S(2)}, u32[]{:S(2)}) collective-permute-start(f32[32,768]{1,0:T(8,128)S(1)} %get-tuple-element.93), channel_id=1, source_target_pairs={{0,20},{4,16},{8,28},{12,24},{16,4},{20,0},{24,12},{28,8},{1,21},{... | collective-permute-start | bytes 294920 | tf_op jit(solution)/shard_map/ppermute | solution.py:706
  33.3 11.9 %collective-permute-start.22 = (f32[32,768]{1,0:T(8,128)S(1)}, f32[32,768]{1,0:T(8,128)S(1)}, u32[]{:S(2)}, u32[]{:S(2)}) collective-permute-start(f32[32,768]{1,0:T(8,128)S(1)} %get-tuple-element.94), channel_id=1, source_target_pairs={{0,8},{4,12},{8,0},{12,4},{16,24},{20,28},{24,16},{28,20},{1,9},{5... | collective-permute-start | bytes 294920 | tf_op jit(solution)/shard_map/ppermute | solution.py:706
  37.5 12.3 %collective-permute-start.23 = (f32[32,768]{1,0:T(8,128)S(1)}, f32[32,768]{1,0:T(8,128)S(1)}, u32[]{:S(2)}, u32[]{:S(2)}) collective-permute-start(f32[32,768]{1,0:T(8,128)S(1)} %get-tuple-element.95), channel_id=1, source_target_pairs={{0,24},{4,28},{8,16},{12,20},{16,8},{20,12},{24,0},{28,4},{1,25},{... | collective-permute-start | bytes 294920 | tf_op jit(solution)/shard_map/ppermute | solution.py:706
  39.8 9.9 %collective-permute-start.24 = (f32[32,768]{1,0:T(8,128)S(1)}, f32[32,768]{1,0:T(8,128)S(1)}, u32[]{:S(2)}, u32[]{:S(2)}) collective-permute-start(f32[32,768]{1,0:T(8,128)S(1)} %get-tuple-element.96), channel_id=1, source_target_pairs={{0,28},{4,24},{8,20},{12,16},{16,12},{20,8},{24,4},{28,0},{1,29},{... | collective-permute-start | bytes 294920 | tf_op jit(solution)/shard_map/ppermute | solution.py:706
  43.9 11.0 %collective-permute-start.25 = (f32[32,768]{1,0:T(8,128)S(1)}, f32[32,768]{1,0:T(8,128)S(1)}, u32[]{:S(2)}, u32[]{:S(2)}) collective-permute-start(f32[32,768]{1,0:T(8,128)S(1)} %get-tuple-element.97), channel_id=1, source_target_pairs={{0,12},{4,8},{8,4},{12,0},{16,28},{20,24},{24,20},{28,16},{1,13},{... | collective-permute-start | bytes 294920 | tf_op jit(solution)/shard_map/ppermute | solution.py:706
  43.9 11.0 %collective-permute-start.9 = (f32[32,768]{1,0:T(8,128)S(1)}, f32[32,768]{1,0:T(8,128)S(1)}, u32[]{:S(2)}, u32[]{:S(2)}) collective-permute-start(f32[32,768]{1,0:T(8,128)S(1)} %get-tuple-element.79), channel_id=1, source_target_pairs={{0,16},{4,20},{8,24},{12,28},{16,0},{20,4},{24,8},{28,12},{1,17},{... | collective-permute-start | bytes 294920 | tf_op jit(solution)/shard_map/ppermute | solution.py:706
  45.2 14.0 %collective-permute-start.10 = (f32[32,768]{1,0:T(8,128)S(1)}, f32[32,768]{1,0:T(8,128)S(1)}, u32[]{:S(2)}, u32[]{:S(2)}) collective-permute-start(f32[32,768]{1,0:T(8,128)S(1)} %get-tuple-element.80), channel_id=1, source_target_pairs={{0,4},{4,0},{8,12},{12,8},{16,20},{20,16},{24,28},{28,24},{1,5},{5... | collective-permute-start | bytes 294920 | tf_op jit(solution)/shard_map/ppermute | solution.py:706
  49.7 10.8 %collective-permute-start.11 = (f32[32,768]{1,0:T(8,128)S(1)}, f32[32,768]{1,0:T(8,128)S(1)}, u32[]{:S(2)}, u32[]{:S(2)}) collective-permute-start(f32[32,768]{1,0:T(8,128)S(1)} %get-tuple-element.81), channel_id=1, source_target_pairs={{0,20},{4,16},{8,28},{12,24},{16,4},{20,0},{24,12},{28,8},{1,21},{... | collective-permute-start | bytes 294920 | tf_op jit(solution)/shard_map/ppermute | solution.py:706
  49.7 10.9 %collective-permute-start.12 = (f32[32,768]{1,0:T(8,128)S(1)}, f32[32,768]{1,0:T(8,128)S(1)}, u32[]{:S(2)}, u32[]{:S(2)}) collective-permute-start(f32[32,768]{1,0:T(8,128)S(1)} %get-tuple-element.82), channel_id=1, source_target_pairs={{0,8},{4,12},{8,0},{12,4},{16,24},{20,28},{24,16},{28,20},{1,9},{5... | collective-permute-start | bytes 294920 | tf_op jit(solution)/shard_map/ppermute | solution.py:706
  54.9 7.5 %collective-permute-start.13 = (f32[32,768]{1,0:T(8,128)S(1)}, f32[32,768]{1,0:T(8,128)S(1)}, u32[]{:S(2)}, u32[]{:S(2)}) collective-permute-start(f32[32,768]{1,0:T(8,128)S(1)} %get-tuple-element.83), channel_id=1, source_target_pairs={{0,24},{4,28},{8,16},{12,20},{16,8},{20,12},{24,0},{28,4},{1,25},{... | collective-permute-start | bytes 294920 | tf_op jit(solution)/shard_map/ppermute | solution.py:706
  54.9 9.4 %collective-permute-start.14 = (f32[32,768]{1,0:T(8,128)S(1)}, f32[32,768]{1,0:T(8,128)S(1)}, u32[]{:S(2)}, u32[]{:S(2)}) collective-permute-start(f32[32,768]{1,0:T(8,128)S(1)} %get-tuple-element.84), channel_id=1, source_target_pairs={{0,28},{4,24},{8,20},{12,16},{16,12},{20,8},{24,4},{28,0},{1,29},{... | collective-permute-start | bytes 294920 | tf_op jit(solution)/shard_map/ppermute | solution.py:706
  59.2 6.7 %collective-permute-start.15 = (f32[32,768]{1,0:T(8,128)S(1)}, f32[32,768]{1,0:T(8,128)S(1)}, u32[]{:S(2)}, u32[]{:S(2)}) collective-permute-start(f32[32,768]{1,0:T(8,128)S(1)} %get-tuple-element.85), channel_id=1, source_target_pairs={{0,12},{4,8},{8,4},{12,0},{16,28},{20,24},{24,20},{28,16},{1,13},{... | collective-permute-start | bytes 294920 | tf_op jit(solution)/shard_map/ppermute | solution.py:706
  60.5 6.7 %collective-permute-start.4 = (f32[48,256]{1,0:T(8,128)S(1)}, f32[48,256]{1,0:T(8,128)S(1)}, u32[]{:S(2)}, u32[]{:S(2)}) collective-permute-start(f32[48,256]{1,0:T(8,128)S(1)} %get-tuple-element.72), channel_id=1, source_target_pairs={{0,1},{1,2},{2,3},{3,0},{4,5},{5,6},{6,7},{7,4},{8,9},{9,10},{10,1... | collective-permute-start | bytes 147464 | tf_op jit(solution)/shard_map/ppermute | solution.py:764
  60.6 6.6 %collective-permute-start.5 = (f32[48,256]{1,0:T(8,128)S(1)}, f32[48,256]{1,0:T(8,128)S(1)}, u32[]{:S(2)}, u32[]{:S(2)}) collective-permute-start(f32[48,256]{1,0:T(8,128)S(1)} %get-tuple-element.73), channel_id=1, source_target_pairs={{0,3},{1,0},{2,1},{3,2},{4,7},{5,4},{6,5},{7,6},{8,11},{9,8},{10,9... | collective-permute-start | bytes 147464 | tf_op jit(solution)/shard_map/ppermute | solution.py:765
  71.0 11.6 %collective-permute-start.26 = (f32[32,768]{1,0:T(8,128)S(1)}, f32[32,768]{1,0:T(8,128)S(1)}, u32[]{:S(2)}, u32[]{:S(2)}) collective-permute-start(f32[32,768]{1,0:T(8,128)S(1)} %get-tuple-element.100), channel_id=1, source_target_pairs={{0,16},{4,20},{8,24},{12,28},{16,0},{20,4},{24,8},{28,12},{1,17},{... | collective-permute-start | bytes 294920 | tf_op jit(solution)/shard_map/ppermute | solution.py:706
  74.0 8.6 %collective-permute-start.27 = (f32[32,768]{1,0:T(8,128)S(1)}, f32[32,768]{1,0:T(8,128)S(1)}, u32[]{:S(2)}, u32[]{:S(2)}) collective-permute-start(f32[32,768]{1,0:T(8,128)S(1)} %get-tuple-element.101), channel_id=1, source_target_pairs={{0,4},{4,0},{8,12},{12,8},{16,20},{20,16},{24,28},{28,24},{1,5},{5... | collective-permute-start | bytes 294920 | tf_op jit(solution)/shard_map/ppermute | solution.py:706
  74.4 12.6 %collective-permute-start.28 = (f32[32,768]{1,0:T(8,128)S(1)}, f32[32,768]{1,0:T(8,128)S(1)}, u32[]{:S(2)}, u32[]{:S(2)}) collective-permute-start(f32[32,768]{1,0:T(8,128)S(1)} %get-tuple-element.102), channel_id=1, source_target_pairs={{0,20},{4,16},{8,28},{12,24},{16,4},{20,0},{24,12},{28,8},{1,21},{... | collective-permute-start | bytes 294920 | tf_op jit(solution)/shard_map/ppermute | solution.py:706
  75.5 13.8 %collective-permute-start.29 = (f32[32,768]{1,0:T(8,128)S(1)}, f32[32,768]{1,0:T(8,128)S(1)}, u32[]{:S(2)}, u32[]{:S(2)}) collective-permute-start(f32[32,768]{1,0:T(8,128)S(1)} %get-tuple-element.103), channel_id=1, source_target_pairs={{0,8},{4,12},{8,0},{12,4},{16,24},{20,28},{24,16},{28,20},{1,9},{5... | collective-permute-start | bytes 294920 | tf_op jit(solution)/shard_map/ppermute | solution.py:706
  77.1 13.0 %collective-permute-start.30 = (f32[32,768]{1,0:T(8,128)S(1)}, f32[32,768]{1,0:T(8,128)S(1)}, u32[]{:S(2)}, u32[]{:S(2)}) collective-permute-start(f32[32,768]{1,0:T(8,128)S(1)} %get-tuple-element.104), channel_id=1, source_target_pairs={{0,24},{4,28},{8,16},{12,20},{16,8},{20,12},{24,0},{28,4},{1,25},{... | collective-permute-start | bytes 294920 | tf_op jit(solution)/shard_map/ppermute | solution.py:706
  82.6 8.7 %collective-permute-start.31 = (f32[32,768]{1,0:T(8,128)S(1)}, f32[32,768]{1,0:T(8,128)S(1)}, u32[]{:S(2)}, u32[]{:S(2)}) collective-permute-start(f32[32,768]{1,0:T(8,128)S(1)} %get-tuple-element.105), channel_id=1, source_target_pairs={{0,28},{4,24},{8,20},{12,16},{16,12},{20,8},{24,4},{28,0},{1,29},{... | collective-permute-start | bytes 294920 | tf_op jit(solution)/shard_map/ppermute | solution.py:706
  82.6 14.4 %collective-permute-start.32 = (f32[32,768]{1,0:T(8,128)S(1)}, f32[32,768]{1,0:T(8,128)S(1)}, u32[]{:S(2)}, u32[]{:S(2)}) collective-permute-start(f32[32,768]{1,0:T(8,128)S(1)} %get-tuple-element.106), channel_id=1, source_target_pairs={{0,12},{4,8},{8,4},{12,0},{16,28},{20,24},{24,20},{28,16},{1,13},{... | collective-permute-start | bytes 294920 | tf_op jit(solution)/shard_map/ppermute | solution.py:706
  86.9 11.9 %collective-permute-start.36 = (f32[32,768]{1,0:T(8,128)S(1)}, f32[32,768]{1,0:T(8,128)S(1)}, u32[]{:S(2)}, u32[]{:S(2)}) collective-permute-start(f32[32,768]{1,0:T(8,128)S(1)} %get-tuple-element.116), channel_id=1, source_target_pairs={{0,16},{4,20},{8,24},{12,28},{16,0},{20,4},{24,8},{28,12},{1,17},{... | collective-permute-start | bytes 294920 | tf_op jit(solution)/shard_map/ppermute | solution.py:706
  89.4 11.8 %collective-permute-start.37 = (f32[32,768]{1,0:T(8,128)S(1)}, f32[32,768]{1,0:T(8,128)S(1)}, u32[]{:S(2)}, u32[]{:S(2)}) collective-permute-start(f32[32,768]{1,0:T(8,128)S(1)} %get-tuple-element.117), channel_id=1, source_target_pairs={{0,4},{4,0},{8,12},{12,8},{16,20},{20,16},{24,28},{28,24},{1,5},{5... | collective-permute-start | bytes 294920 | tf_op jit(solution)/shard_map/ppermute | solution.py:706
  90.1 11.7 %collective-permute-start.38 = (f32[32,768]{1,0:T(8,128)S(1)}, f32[32,768]{1,0:T(8,128)S(1)}, u32[]{:S(2)}, u32[]{:S(2)}) collective-permute-start(f32[32,768]{1,0:T(8,128)S(1)} %get-tuple-element.118), channel_id=1, source_target_pairs={{0,20},{4,16},{8,28},{12,24},{16,4},{20,0},{24,12},{28,8},{1,21},{... | collective-permute-start | bytes 294920 | tf_op jit(solution)/shard_map/ppermute | solution.py:706
  91.3 11.8 %collective-permute-start.39 = (f32[32,768]{1,0:T(8,128)S(1)}, f32[32,768]{1,0:T(8,128)S(1)}, u32[]{:S(2)}, u32[]{:S(2)}) collective-permute-start(f32[32,768]{1,0:T(8,128)S(1)} %get-tuple-element.119), channel_id=1, source_target_pairs={{0,8},{4,12},{8,0},{12,4},{16,24},{20,28},{24,16},{28,20},{1,9},{5... | collective-permute-start | bytes 294920 | tf_op jit(solution)/shard_map/ppermute | solution.py:706
  98.7 7.6 %collective-permute-start.40 = (f32[32,768]{1,0:T(8,128)S(1)}, f32[32,768]{1,0:T(8,128)S(1)}, u32[]{:S(2)}, u32[]{:S(2)}) collective-permute-start(f32[32,768]{1,0:T(8,128)S(1)} %get-tuple-element.123), channel_id=1, source_target_pairs={{0,24},{4,28},{8,16},{12,20},{16,8},{20,12},{24,0},{28,4},{1,25},{... | collective-permute-start | bytes 294920 | tf_op jit(solution)/shard_map/ppermute | solution.py:706
  98.8 8.2 %collective-permute-start.41 = (f32[32,768]{1,0:T(8,128)S(1)}, f32[32,768]{1,0:T(8,128)S(1)}, u32[]{:S(2)}, u32[]{:S(2)}) collective-permute-start(f32[32,768]{1,0:T(8,128)S(1)} %get-tuple-element.124), channel_id=1, source_target_pairs={{0,28},{4,24},{8,20},{12,16},{16,12},{20,8},{24,4},{28,0},{1,29},{... | collective-permute-start | bytes 294920 | tf_op jit(solution)/shard_map/ppermute | solution.py:706
  101.2 6.7 %collective-permute-start.42 = (f32[32,768]{1,0:T(8,128)S(1)}, f32[32,768]{1,0:T(8,128)S(1)}, u32[]{:S(2)}, u32[]{:S(2)}) collective-permute-start(f32[32,768]{1,0:T(8,128)S(1)} %get-tuple-element.125), channel_id=1, source_target_pairs={{0,12},{4,8},{8,4},{12,0},{16,28},{20,24},{24,20},{28,16},{1,13},{... | collective-permute-start | bytes 294920 | tf_op jit(solution)/shard_map/ppermute | solution.py:706
  101.7 9.0 %collective-permute-start.33 = (f32[72,768]{1,0:T(8,128)S(1)}, f32[72,768]{1,0:T(8,128)S(1)}, u32[]{:S(2)}, u32[]{:S(2)}) collective-permute-start(f32[72,768]{1,0:T(8,128)S(1)} %get-tuple-element.108), channel_id=1, source_target_pairs={{0,2},{1,3},{2,0},{3,1},{4,6},{5,7},{6,4},{7,5},{8,10},{9,11},{10,... | collective-permute-start | bytes 663560 | tf_op jit(solution)/shard_map/ppermute | solution.py:706
  103.2 8.7 %collective-permute-start.34 = (f32[72,768]{1,0:T(8,128)S(1)}, f32[72,768]{1,0:T(8,128)S(1)}, u32[]{:S(2)}, u32[]{:S(2)}) collective-permute-start(f32[72,768]{1,0:T(8,128)S(1)} %get-tuple-element.109), channel_id=1, source_target_pairs={{0,1},{1,0},{2,3},{3,2},{4,5},{5,4},{6,7},{7,6},{8,9},{9,8},{10,11... | collective-permute-start | bytes 663560 | tf_op jit(solution)/shard_map/ppermute | solution.py:706
  106.3 7.8 %collective-permute-start.35 = (f32[72,768]{1,0:T(8,128)S(1)}, f32[72,768]{1,0:T(8,128)S(1)}, u32[]{:S(2)}, u32[]{:S(2)}) collective-permute-start(f32[72,768]{1,0:T(8,128)S(1)} %get-tuple-element.110), channel_id=1, source_target_pairs={{0,3},{1,2},{2,1},{3,0},{4,7},{5,6},{6,5},{7,4},{8,11},{9,10},{10,... | collective-permute-start | bytes 663560 | tf_op jit(solution)/shard_map/ppermute | solution.py:706
  109.6 10.7 %collective-permute-start.43 = (f32[72,768]{1,0:T(8,128)S(1)}, f32[72,768]{1,0:T(8,128)S(1)}, u32[]{:S(2)}, u32[]{:S(2)}) collective-permute-start(f32[72,768]{1,0:T(8,128)S(1)} %get-tuple-element.127), channel_id=1, source_target_pairs={{0,2},{1,3},{2,0},{3,1},{4,6},{5,7},{6,4},{7,5},{8,10},{9,11},{10,... | collective-permute-start | bytes 663560 | tf_op jit(solution)/shard_map/ppermute | solution.py:706
  110.7 12.6 %collective-permute-start.44 = (f32[72,768]{1,0:T(8,128)S(1)}, f32[72,768]{1,0:T(8,128)S(1)}, u32[]{:S(2)}, u32[]{:S(2)}) collective-permute-start(f32[72,768]{1,0:T(8,128)S(1)} %get-tuple-element.128), channel_id=1, source_target_pairs={{0,3},{1,2},{2,1},{3,0},{4,7},{5,6},{6,5},{7,4},{8,11},{9,10},{10,... | collective-permute-start | bytes 663560 | tf_op jit(solution)/shard_map/ppermute | solution.py:706
  110.7 12.6 %collective-permute-start.45 = (f32[72,768]{1,0:T(8,128)S(1)}, f32[72,768]{1,0:T(8,128)S(1)}, u32[]{:S(2)}, u32[]{:S(2)}) collective-permute-start(f32[72,768]{1,0:T(8,128)S(1)} %get-tuple-element.129), channel_id=1, source_target_pairs={{0,1},{1,0},{2,3},{3,2},{4,5},{5,4},{6,7},{7,6},{8,9},{9,8},{10,11... | collective-permute-start | bytes 663560 | tf_op jit(solution)/shard_map/ppermute | solution.py:706
  115.5 10.7 %collective-permute-start.46 = (f32[3,64,256]{2,1,0:T(8,128)S(1)}, f32[3,64,256]{2,1,0:T(8,128)S(1)}, u32[]{:S(2)}, u32[]{:S(2)}) collective-permute-start(f32[3,64,256]{2,1,0:T(8,128)S(1)} %get-tuple-element.132), channel_id=1, source_target_pairs={{0,4},{4,8},{8,12},{12,16},{16,20},{20,24},{24,28},{28,0},{1,5},{5... | collective-permute-start | bytes 589832 | tf_op jit(solution)/shard_map/ppermute | solution.py:835
  116.2 12.4 %collective-permute-start.47 = (f32[3,64,256]{2,1,0:T(8,128)S(1)}, f32[3,64,256]{2,1,0:T(8,128)S(1)}, u32[]{:S(2)}, u32[]{:S(2)}) collective-permute-start(f32[3,64,256]{2,1,0:T(8,128)S(1)} %get-tuple-element.133), channel_id=1, source_target_pairs={{0,28},{4,0},{8,4},{12,8},{16,12},{20,16},{24,20},{28,24},{1,29},{... | collective-permute-start | bytes 589832 | tf_op jit(solution)/shard_map/ppermute | solution.py:834
  (9 other events, 93.0 us)

commit v19 on v15

--- a/solution.py
+++ b/solution.py
@@ -149,7 +149,7 @@
     if first == "far":
         return [0] + far + near
     order, last = [0], near[2:]
-    near = near[:2]
+    near, far = near[:2], far[::2] + far[1::2]
     while far or near:
         order += far[:1] + near[:1]
         far, near = far[1:], near[1:]

time: 129 us -> 131 us (1.016)
  starting transfers between devices: 68.7 us -> 71.9 us
  waiting for transfers between devices: 28.7 us -> 26.9 us
    ppermute x40, starting transfers between devices: 52.2 us -> 55.4 us  [exchange(): lax.ppermute(block, axis, [(i, i ^ k) for i in range(count)])]
    ppermute x40, waiting for transfers between devices: 25.4 us -> 22.7 us  [exchange(): lax.ppermute(block, axis, [(i, i ^ k) for i in range(count)])]
  transfers between devices with their start and end apart: 48 -> 48, of which waited for: 16 -> 15; matrix products, arithmetic and copies ran while one was open for 0% -> 0% of each run, Pallas kernels for 16% -> 16%
where the time goes in v19:
time: 131 us
  starting transfers between devices  71.9 us (55%)
  Pallas kernels  30.6 us (23%)
  waiting for transfers between devices  26.9 us (21%)
    ppermute x40, starting transfers between devices, exchange(): lax.ppermute(block, axis, [(i, i ^ k) for i in range(count)])  55.4 us
    pallas_call x16, Pallas kernels, call(): pl.pallas_call(kernel, out_shape=[jax.ShapeDtypeStruct(shape, F32) for _,...  30.6 us
    ppermute x40, waiting for transfers between devices, exchange(): lax.ppermute(block, axis, [(i, i ^ k) for i in range(count)])  22.7 us
    ppermute x1, starting transfers between devices, on_device(): after = lax.ppermute(first, 'gz', ring('gz', -1))  4.28 us
    ppermute x1, starting transfers between devices, on_device(): down2 = lax.ppermute(movers, 'gz', ring('gz', 2))  3.08 us
    ppermute x1, starting transfers between devices, on_device(): up1 = lax.ppermute(packet, 'gz', ring('gz', -1))  3.08 us
  transfers between devices with their start and end apart: 48, of which 15 were waited for; matrix products, arithmetic and copies ran while one was open for 0% of the time, Pallas kernels for 16%

profile of v19, /device:TPU:0, one launch (start us, length us, event | category | flops | bytes accessed | tf_op | source)
XLA Modules:
  0.0 130.6 jit_solution(6715622637529819015)
XLA Ops:
  1.8 3.1 %collective-permute-start.3 = (f32[8,128]{1,0:T(8,128)S(1)}, f32[8,128]{1,0:T(8,128)S(1)}, u32[]{:S(2)}, u32[]{:S(2)}) collective-permute-start(f32[8,128]{1,0:T(8,128)S(1)} %get-tuple-element.69), channel_id=1, source_target_pairs={{0,8},{4,12},{8,16},{12,20},{16,24},{20,28},{24,0},{28,4},{1,9},{5... | collective-permute-start | bytes 12296 | tf_op jit(solution)/shard_map/ppermute | solution.py:740
  4.8 2.1 %collective-permute-start.2 = (f32[8,128]{1,0:T(8,128)S(1)}, f32[8,128]{1,0:T(8,128)S(1)}, u32[]{:S(2)}, u32[]{:S(2)}) collective-permute-start(f32[8,128]{1,0:T(8,128)S(1)} %get-tuple-element.69), channel_id=1, source_target_pairs={{0,24},{4,28},{8,0},{12,4},{16,8},{20,12},{24,16},{28,20},{1,25},{... | collective-permute-start | bytes 12296 | tf_op jit(solution)/shard_map/ppermute | solution.py:739
  6.9 1.6 %collective-permute-start.1 = (f32[8,512]{1,0:T(8,128)S(1)}, f32[8,512]{1,0:T(8,128)S(1)}, u32[]{:S(2)}, u32[]{:S(2)}) collective-permute-start(f32[8,512]{1,0:T(8,128)S(1)} %get-tuple-element.68.own), channel_id=1, source_target_pairs={{0,4},{4,8},{8,12},{12,16},{16,20},{20,24},{24,28},{28,0},{1,5},{5... | collective-permute-start | bytes 49160 | tf_op jit(solution)/shard_map/ppermute | solution.py:738
  8.6 3.1 %collective-permute-start = (f32[8,512]{1,0:T(8,128)S(1)}, f32[8,512]{1,0:T(8,128)S(1)}, u32[]{:S(2)}, u32[]{:S(2)}) collective-permute-start(f32[8,512]{1,0:T(8,128)S(1)} %get-tuple-element.68.own), channel_id=1, source_target_pairs={{0,28},{4,0},{8,4},{12,8},{16,12},{20,16},{24,20},{28,24},{1,29},{... | collective-permute-start | bytes 49160 | tf_op jit(solution)/shard_map/ppermute | solution.py:737
  11.7 1.6 %collective-permute-done.1.down1 = f32[8,512]{1,0:T(8,128)S(1)} collective-permute-done((f32[8,512]{1,0:T(8,128)S(1)}, f32[8,512]{1,0:T(8,128)S(1)}, u32[]{:S(2)}, u32[]{:S(2)}) %collective-permute-start.1) | collective-permute-done | bytes 16416 | tf_op jit(solution)/shard_map/ppermute | solution.py:738
  13.4 3.7 %shard_map.141 = (f32[3,4,64,256]{3,2,1,0:T(8,128)S(1)}, f32[24,256]{1,0:T(8,128)S(1)}, f32[24,256]{1,0:T(8,128)S(1)}, f32[72,768]{1,0:T(8,128)S(1)}, f32[72,768...) custom-call(s32[2]{0:T(128)S(1)} %pad_add_fusion.place, f32[8,512]{1,0:T(8,128)S(1)} %get-tuple-element.68.own, ...), custom_call_target="tpu_custom_call" | custom-call | flops 5000000000 | bytes 15000000 | tf_op jit(solution)/shard_map/pallas_call | solution.py:667
  17.1 1.7 %collective-permute-start.16 = (f32[72,768]{1,0:T(8,128)S(1)}, f32[72,768]{1,0:T(8,128)S(1)}, u32[]{:S(2)}, u32[]{:S(2)}) collective-permute-start(f32[72,768]{1,0:T(8,128)S(1)} %get-tuple-element.87), channel_id=1, source_target_pairs={{0,2},{1,3},{2,0},{3,1},{4,6},{5,7},{6,4},{7,5},{8,10},{9,11},{10,... | collective-permute-start | bytes 663560 | tf_op jit(solution)/shard_map/ppermute | solution.py:703
  19.3 6.0 %shard_map.142 = (f32[3,4,64,256]{3,2,1,0:T(8,128)S(1)}, f32[48,256]{1,0:T(8,128)S(1)}, f32[48,256]{1,0:T(8,128)S(1)}, f32[72,768]{1,0:T(8,128)S(1)}, f32[72,768...) custom-call(s32[2]{0:T(128)S(1)} %pad_add_fusion.place, f32[8,512]{1,0:T(8,128)S(1)} %get-tuple-element.68.own, ...), custom_call_target="tpu_custom_call" | custom-call | flops 5000000000 | bytes 15000000 | tf_op jit(solution)/shard_map/pallas_call | solution.py:667
  25.4 1.7 %collective-permute-start.7 = (f32[72,768]{1,0:T(8,128)S(1)}, f32[72,768]{1,0:T(8,128)S(1)}, u32[]{:S(2)}, u32[]{:S(2)}) collective-permute-start(f32[72,768]{1,0:T(8,128)S(1)} %get-tuple-element.76), channel_id=1, source_target_pairs={{0,2},{1,3},{2,0},{3,1},{4,6},{5,7},{6,4},{7,5},{8,10},{9,11},{10,... | collective-permute-start | bytes 663560 | tf_op jit(solution)/shard_map/ppermute | solution.py:703
  27.2 1.6 %shard_map.145 = (f32[32,768]{1,0:T(8,128)S(1)}, f32[32,768]{1,0:T(8,128)S(1)}, f32[32,768]{1,0:T(8,128)S(1)}, f32[32,768]{1,0:T(8,128)S(1)}, f32[32,768]{1,0:T(...) custom-call(s32[2]{0:T(128)S(1)} %pad_add_fusion.place, ...), custom_call_target="tpu_custom_call" | custom-call | flops 2000000000 | bytes 6000000 | tf_op jit(solution)/shard_map/pallas_call | solution.py:667
  28.9 2.2 %collective-permute-start.20 = (f32[32,768]{1,0:T(8,128)S(1)}, f32[32,768]{1,0:T(8,128)S(1)}, u32[]{:S(2)}, u32[]{:S(2)}) collective-permute-start(f32[32,768]{1,0:T(8,128)S(1)} %get-tuple-element.92), channel_id=1, source_target_pairs={{0,4},{4,0},{8,12},{12,8},{16,20},{20,16},{24,28},{28,24},{1,5},{5... | collective-permute-start | bytes 294920 | tf_op jit(solution)/shard_map/ppermute | solution.py:703
  31.1 3.2 %collective-permute-start.21 = (f32[32,768]{1,0:T(8,128)S(1)}, f32[32,768]{1,0:T(8,128)S(1)}, u32[]{:S(2)}, u32[]{:S(2)}) collective-permute-start(f32[32,768]{1,0:T(8,128)S(1)} %get-tuple-element.93), channel_id=1, source_target_pairs={{0,24},{4,28},{8,16},{12,20},{16,8},{20,12},{24,0},{28,4},{1,25},{... | collective-permute-start | bytes 294920 | tf_op jit(solution)/shard_map/ppermute | solution.py:703
  34.8 2.6 %collective-permute-done.8.refs_3_ = f32[72,768]{1,0:T(8,128)S(1)} collective-permute-done((f32[72,768]{1,0:T(8,128)S(1)}, f32[72,768]{1,0:T(8,128)S(1)}, u32[]{:S(2)}, u32[]{:S(2)}) %collective-permute-start.8) | collective-permute-done | bytes 221216 | tf_op jit(solution)/shard_map/ppermute | solution.py:703
  37.5 1.6 %collective-permute-start.23 = (f32[32,768]{1,0:T(8,128)S(1)}, f32[32,768]{1,0:T(8,128)S(1)}, u32[]{:S(2)}, u32[]{:S(2)}) collective-permute-start(f32[32,768]{1,0:T(8,128)S(1)} %get-tuple-element.95), channel_id=1, source_target_pairs={{0,20},{4,16},{8,28},{12,24},{16,4},{20,0},{24,12},{28,8},{1,21},{... | collective-permute-start | bytes 294920 | tf_op jit(solution)/shard_map/ppermute | solution.py:703
  39.1 1.6 %shard_map.143 = (f32[32,768]{1,0:T(8,128)S(1)}, f32[32,768]{1,0:T(8,128)S(1)}, f32[32,768]{1,0:T(8,128)S(1)}, f32[32,768]{1,0:T(8,128)S(1)}, f32[32,768]{1,0:T(...) custom-call(s32[2]{0:T(128)S(1)} %pad_add_fusion.place, ...), custom_call_target="tpu_custom_call" | custom-call | flops 2000000000 | bytes 6000000 | tf_op jit(solution)/shard_map/pallas_call | solution.py:667
  40.7 3.2 %collective-permute-start.24 = (f32[32,768]{1,0:T(8,128)S(1)}, f32[32,768]{1,0:T(8,128)S(1)}, u32[]{:S(2)}, u32[]{:S(2)}) collective-permute-start(f32[32,768]{1,0:T(8,128)S(1)} %get-tuple-element.96), channel_id=1, source_target_pairs={{0,28},{4,24},{8,20},{12,16},{16,12},{20,8},{24,4},{28,0},{1,29},{... | collective-permute-start | bytes 294920 | tf_op jit(solution)/shard_map/ppermute | solution.py:703
  43.9 2.2 %collective-permute-start.9 = (f32[32,768]{1,0:T(8,128)S(1)}, f32[32,768]{1,0:T(8,128)S(1)}, u32[]{:S(2)}, u32[]{:S(2)}) collective-permute-start(f32[32,768]{1,0:T(8,128)S(1)} %get-tuple-element.79), channel_id=1, source_target_pairs={{0,16},{4,20},{8,24},{12,28},{16,0},{20,4},{24,8},{28,12},{1,17},{... | collective-permute-start | bytes 294920 | tf_op jit(solution)/shard_map/ppermute | solution.py:703
  46.1 1.4 %collective-permute-start.10 = (f32[32,768]{1,0:T(8,128)S(1)}, f32[32,768]{1,0:T(8,128)S(1)}, u32[]{:S(2)}, u32[]{:S(2)}) collective-permute-start(f32[32,768]{1,0:T(8,128)S(1)} %get-tuple-element.80), channel_id=1, source_target_pairs={{0,4},{4,0},{8,12},{12,8},{16,20},{20,16},{24,28},{28,24},{1,5},{5... | collective-permute-start | bytes 294920 | tf_op jit(solution)/shard_map/ppermute | solution.py:703
  47.4 1.7 %collective-permute-done.23.refs_5_ = f32[32,768]{1,0:T(8,128)S(1)} collective-permute-done((f32[32,768]{1,0:T(8,128)S(1)}, f32[32,768]{1,0:T(8,128)S(1)}, u32[]{:S(2)}, u32[]{:S(2)}) %collective-permute-start.23) | collective-permute-done | bytes 98336 | tf_op jit(solution)/shard_map/ppermute | solution.py:703
  49.1 1.6 %collective-permute-start.11 = (f32[32,768]{1,0:T(8,128)S(1)}, f32[32,768]{1,0:T(8,128)S(1)}, u32[]{:S(2)}, u32[]{:S(2)}) collective-permute-start(f32[32,768]{1,0:T(8,128)S(1)} %get-tuple-element.81), channel_id=1, source_target_pairs={{0,24},{4,28},{8,16},{12,20},{16,8},{20,12},{24,0},{28,4},{1,25},{... | collective-permute-start | bytes 294920 | tf_op jit(solution)/shard_map/ppermute | solution.py:703
  50.7 5.3 %collective-permute-start.12 = (f32[32,768]{1,0:T(8,128)S(1)}, f32[32,768]{1,0:T(8,128)S(1)}, u32[]{:S(2)}, u32[]{:S(2)}) collective-permute-start(f32[32,768]{1,0:T(8,128)S(1)} %get-tuple-element.82), channel_id=1, source_target_pairs={{0,8},{4,12},{8,0},{12,4},{16,24},{20,28},{24,16},{28,20},{1,9},{5... | collective-permute-start | bytes 294920 | tf_op jit(solution)/shard_map/ppermute | solution.py:703
  56.0 4.2 %collective-permute-start.14 = (f32[32,768]{1,0:T(8,128)S(1)}, f32[32,768]{1,0:T(8,128)S(1)}, u32[]{:S(2)}, u32[]{:S(2)}) collective-permute-start(f32[32,768]{1,0:T(8,128)S(1)} %get-tuple-element.84), channel_id=1, source_target_pairs={{0,28},{4,24},{8,20},{12,16},{16,12},{20,8},{24,4},{28,0},{1,29},{... | collective-permute-start | bytes 294920 | tf_op jit(solution)/shard_map/ppermute | solution.py:703
  60.2 1.3 %shard_map.146.refs_1_ = f32[3,2,4,8,8,128]{5,4,3,2,1,0:T(8,128)S(1)} custom-call(s32[2]{0:T(128)S(1)} %pad_add_fusion.place, f32[32,768]{1,0:T(8,128)S(1)} %get-tuple-element.90.refs_0_, f32[32,768]{1,0:T(8,128)S(1)} %collective-permute-done.19.refs_1_, f32[32,768]{1,0:T(8,128)S(1)} %collective-permute-done.20.refs_2_, ...), custom_call_target="tpu_custom_call" | custom-call | flops 2000000000 | bytes 6000000 | tf_op jit(solution)/shard_map/pallas_call | solution.py:667
  61.6 1.7 %collective-permute-start.5 = (f32[48,256]{1,0:T(8,128)S(1)}, f32[48,256]{1,0:T(8,128)S(1)}, u32[]{:S(2)}, u32[]{:S(2)}) collective-permute-start(f32[48,256]{1,0:T(8,128)S(1)} %get-tuple-element.73), channel_id=1, source_target_pairs={{0,3},{1,0},{2,1},{3,2},{4,7},{5,4},{6,5},{7,6},{8,11},{9,8},{10,9... | collective-permute-start | bytes 147464 | tf_op jit(solution)/shard_map/ppermute | solution.py:762
  63.4 2.6 %collective-permute-done.13.refs_5_ = f32[32,768]{1,0:T(8,128)S(1)} collective-permute-done((f32[32,768]{1,0:T(8,128)S(1)}, f32[32,768]{1,0:T(8,128)S(1)}, u32[]{:S(2)}, u32[]{:S(2)}) %collective-permute-start.13) | collective-permute-done | bytes 98336 | tf_op jit(solution)/shard_map/ppermute | solution.py:703
  66.0 1.5 %collective-permute-done.15.refs_7_ = f32[32,768]{1,0:T(8,128)S(1)} collective-permute-done((f32[32,768]{1,0:T(8,128)S(1)}, f32[32,768]{1,0:T(8,128)S(1)}, u32[]{:S(2)}, u32[]{:S(2)}) %collective-permute-start.15) | collective-permute-done | bytes 98336 | tf_op jit(solution)/shard_map/ppermute | solution.py:703
  68.8 2.3 %shard_map.147 = (f32[3,2,4,8,8,128]{5,4,3,2,1,0:T(8,128)S(1)}, f32[3,2,4,8,8,128]{5,4,3,2,1,0:T(8,128)S(1)}) custom-call(s32[2]{0:T(128)S(1)} %pad_add_fusion.place, f32[48,256]{1,0:T(8,128)S(1)} %collective-permute-done.4.low_rim.refs_1_, f32[48,256]{1,0:T(8,128)S(1)} %collective-permute-done.5.high_rim.refs_2_, ...), custom_call_target="tpu_custom_call" | custom-call | flops 5000000000 | bytes 15000000 | tf_op jit(solution)/shard_map/pallas_call | solution.py:667
  71.2 1.4 %shard_map.148 = (f32[32,768]{1,0:T(8,128)S(1)}, f32[32,768]{1,0:T(8,128)S(1)}, f32[32,768]{1,0:T(8,128)S(1)}, f32[32,768]{1,0:T(8,128)S(1)}, f32[32,768]{1,0:T(...) custom-call(s32[2]{0:T(128)S(1)} %pad_add_fusion.place, ...), custom_call_target="tpu_custom_call" | custom-call | flops 2000000000 | bytes 6000000 | tf_op jit(solution)/shard_map/pallas_call | solution.py:667
  73.4 2.1 %collective-permute-start.27 = (f32[32,768]{1,0:T(8,128)S(1)}, f32[32,768]{1,0:T(8,128)S(1)}, u32[]{:S(2)}, u32[]{:S(2)}) collective-permute-start(f32[32,768]{1,0:T(8,128)S(1)} %get-tuple-element.101), channel_id=1, source_target_pairs={{0,4},{4,0},{8,12},{12,8},{16,20},{20,16},{24,28},{28,24},{1,5},{5... | collective-permute-start | bytes 294920 | tf_op jit(solution)/shard_map/ppermute | solution.py:703
  76.4 2.9 %collective-permute-start.30 = (f32[32,768]{1,0:T(8,128)S(1)}, f32[32,768]{1,0:T(8,128)S(1)}, u32[]{:S(2)}, u32[]{:S(2)}) collective-permute-start(f32[32,768]{1,0:T(8,128)S(1)} %get-tuple-element.104), channel_id=1, source_target_pairs={{0,20},{4,16},{8,28},{12,24},{16,4},{20,0},{24,12},{28,8},{1,21},{... | collective-permute-start | bytes 294920 | tf_op jit(solution)/shard_map/ppermute | solution.py:703
  79.3 4.3 %collective-permute-done.26.refs_1_ = f32[32,768]{1,0:T(8,128)S(1)} collective-permute-done((f32[32,768]{1,0:T(8,128)S(1)}, f32[32,768]{1,0:T(8,128)S(1)}, u32[]{:S(2)}, u32[]{:S(2)}) %collective-permute-start.26) | collective-permute-done | bytes 98336 | tf_op jit(solution)/shard_map/ppermute | solution.py:703
  83.6 2.2 %collective-permute-start.31 = (f32[32,768]{1,0:T(8,128)S(1)}, f32[32,768]{1,0:T(8,128)S(1)}, u32[]{:S(2)}, u32[]{:S(2)}) collective-permute-start(f32[32,768]{1,0:T(8,128)S(1)} %get-tuple-element.105), channel_id=1, source_target_pairs={{0,28},{4,24},{8,20},{12,16},{16,12},{20,8},{24,4},{28,0},{1,29},{... | collective-permute-start | bytes 294920 | tf_op jit(solution)/shard_map/ppermute | solution.py:703
  85.9 1.4 %shard_map.151 = (f32[32,768]{1,0:T(8,128)S(1)}, f32[32,768]{1,0:T(8,128)S(1)}, f32[32,768]{1,0:T(8,128)S(1)}, f32[32,768]{1,0:T(8,128)S(1)}, f32[32,768]{1,0:T(...) custom-call(s32[2]{0:T(128)S(1)} %pad_add_fusion.place, ...), custom_call_target="tpu_custom_call" | custom-call | flops 2000000000 | bytes 6000000 | tf_op jit(solution)/shard_map/pallas_call | solution.py:667
  87.3 3.1 %collective-permute-start.36 = (f32[32,768]{1,0:T(8,128)S(1)}, f32[32,768]{1,0:T(8,128)S(1)}, u32[]{:S(2)}, u32[]{:S(2)}) collective-permute-start(f32[32,768]{1,0:T(8,128)S(1)} %get-tuple-element.116), channel_id=1, source_target_pairs={{0,16},{4,20},{8,24},{12,28},{16,0},{20,4},{24,8},{28,12},{1,17},{... | collective-permute-start | bytes 294920 | tf_op jit(solution)/shard_map/ppermute | solution.py:703
  91.7 2.5 %collective-permute-start.38 = (f32[32,768]{1,0:T(8,128)S(1)}, f32[32,768]{1,0:T(8,128)S(1)}, u32[]{:S(2)}, u32[]{:S(2)}) collective-permute-start(f32[32,768]{1,0:T(8,128)S(1)} %get-tuple-element.118), channel_id=1, source_target_pairs={{0,24},{4,28},{8,16},{12,20},{16,8},{20,12},{24,0},{28,4},{1,25},{... | collective-permute-start | bytes 294920 | tf_op jit(solution)/shard_map/ppermute | solution.py:703
  94.7 1.7 %shard_map.149 = (f32[72,768]{1,0:T(8,128)S(1)}, f32[72,768]{1,0:T(8,128)S(1)}, f32[72,768]{1,0:T(8,128)S(1)}, f32[72,768]{1,0:T(8,128)S(1)}) custom-call(s32[2]{0:T(128)S(1)} %pad_add_fusion.place, bf16[576,256]{1,0:T(8,128)(2,1)S(1)} %copy-done.6, bf16[576,256]{1,0:T(8,128)(2,1)S(1)} %copy-done.5, f32[32,768]{1,0:T(8,128)S(1)} %get-tuple-element.99.refs_0_, ...), custom_call_target="tpu_custom_call" | custom-call | flops 2000000000 | bytes 6000000 | tf_op jit(solution)/shard_map/pallas_call | solution.py:667
  96.4 3.1 %collective-permute-start.40 = (f32[32,768]{1,0:T(8,128)S(1)}, f32[32,768]{1,0:T(8,128)S(1)}, u32[]{:S(2)}, u32[]{:S(2)}) collective-permute-start(f32[32,768]{1,0:T(8,128)S(1)} %get-tuple-element.123), channel_id=1, source_target_pairs={{0,20},{4,16},{8,28},{12,24},{16,4},{20,0},{24,12},{28,8},{1,21},{... | collective-permute-start | bytes 294920 | tf_op jit(solution)/shard_map/ppermute | solution.py:703
  99.5 2.0 %collective-permute-done.36.refs_1_ = f32[32,768]{1,0:T(8,128)S(1)} collective-permute-done((f32[32,768]{1,0:T(8,128)S(1)}, f32[32,768]{1,0:T(8,128)S(1)}, u32[]{:S(2)}, u32[]{:S(2)}) %collective-permute-start.36) | collective-permute-done | bytes 98336 | tf_op jit(solution)/shard_map/ppermute | solution.py:703
  103.9 2.3 %collective-permute-start.33 = (f32[72,768]{1,0:T(8,128)S(1)}, f32[72,768]{1,0:T(8,128)S(1)}, u32[]{:S(2)}, u32[]{:S(2)}) collective-permute-start(f32[72,768]{1,0:T(8,128)S(1)} %get-tuple-element.108), channel_id=1, source_target_pairs={{0,2},{1,3},{2,0},{3,1},{4,6},{5,7},{6,4},{7,5},{8,10},{9,11},{10,... | collective-permute-start | bytes 663560 | tf_op jit(solution)/shard_map/ppermute | solution.py:703
  106.3 2.6 %collective-permute-done.41.refs_6_ = f32[32,768]{1,0:T(8,128)S(1)} collective-permute-done((f32[32,768]{1,0:T(8,128)S(1)}, f32[32,768]{1,0:T(8,128)S(1)}, u32[]{:S(2)}, u32[]{:S(2)}) %collective-permute-start.41) | collective-permute-done | bytes 98336 | tf_op jit(solution)/shard_map/ppermute | solution.py:703
  109.4 1.7 %shard_map.153 = (f32[72,768]{1,0:T(8,128)S(1)}, f32[72,768]{1,0:T(8,128)S(1)}, f32[72,768]{1,0:T(8,128)S(1)}, f32[72,768]{1,0:T(8,128)S(1)}) custom-call(s32[2]{0:T(128)S(1)} %pad_add_fusion.place, bf16[576,256]{1,0:T(8,128)(2,1)S(1)} %copy-done.6, bf16[576,256]{1,0:T(8,128)(2,1)S(1)} %copy-done.5, f32[32,768]{1,0:T(8,128)S(1)} %get-tuple-element.115.refs_0_, ...), custom_call_target="tpu_custom_call" | custom-call | flops 2000000000 | bytes 6000000 | tf_op jit(solution)/shard_map/pallas_call | solution.py:667
  111.1 1.4 %collective-permute-start.43 = (f32[72,768]{1,0:T(8,128)S(1)}, f32[72,768]{1,0:T(8,128)S(1)}, u32[]{:S(2)}, u32[]{:S(2)}) collective-permute-start(f32[72,768]{1,0:T(8,128)S(1)} %get-tuple-element.127), channel_id=1, source_target_pairs={{0,2},{1,3},{2,0},{3,1},{4,6},{5,7},{6,4},{7,5},{8,10},{9,11},{10,... | collective-permute-start | bytes 663560 | tf_op jit(solution)/shard_map/ppermute | solution.py:703
  113.3 2.9 %collective-permute-done.35.refs_3_ = f32[72,768]{1,0:T(8,128)S(1)} collective-permute-done((f32[72,768]{1,0:T(8,128)S(1)}, f32[72,768]{1,0:T(8,128)S(1)}, u32[]{:S(2)}, u32[]{:S(2)}) %collective-permute-start.35) | collective-permute-done | bytes 221216 | tf_op jit(solution)/shard_map/ppermute | solution.py:703
  116.2 1.5 %shard_map.150 = (f32[3,4,80,256]{3,2,1,0:T(8,128)S(1)}, f32[3,64,256]{2,1,0:T(8,128)S(1)}, f32[3,64,256]{2,1,0:T(8,128)S(1)}) custom-call(s32[2]{0:T(128)S(1)} %pad_add_fusion.place, bf16[512,512]{1,0:T(8,128)(2,1)S(1)} %copy-done.2, bf16[512,512]{1,0:T(8,128)(2,1)S(1)} %copy-done.1, f32[72,768]{1,0:T(8,128)S(1)} %get-tuple-element.107.refs_0_.before, ...), custom_call_target="tpu_custom_call" | custom-call | flops 2000000000 | bytes 6000000 | tf_op jit(solution)/shard_map/pallas_call | solution.py:667
  118.1 4.3 %collective-permute-start.47 = (f32[3,64,256]{2,1,0:T(8,128)S(1)}, f32[3,64,256]{2,1,0:T(8,128)S(1)}, u32[]{:S(2)}, u32[]{:S(2)}) collective-permute-start(f32[3,64,256]{2,1,0:T(8,128)S(1)} %get-tuple-element.133), channel_id=1, source_target_pairs={{0,28},{4,0},{8,4},{12,8},{16,12},{20,16},{24,20},{28,24},{1,29},{... | collective-permute-start | bytes 589832 | tf_op jit(solution)/shard_map/ppermute | solution.py:831
  122.4 1.4 %collective-permute-done.44.refs_7_ = f32[72,768]{1,0:T(8,128)S(1)} collective-permute-done((f32[72,768]{1,0:T(8,128)S(1)}, f32[72,768]{1,0:T(8,128)S(1)}, u32[]{:S(2)}, u32[]{:S(2)}) %collective-permute-start.44) | collective-permute-done | bytes 221216 | tf_op jit(solution)/shard_map/ppermute | solution.py:703
  123.8 3.0 %shard_map.154 = (f32[3,8,64,256]{3,2,1,0:T(8,128)}, f32[3,8,64,256]{3,2,1,0:T(8,128)}) custom-call(s32[2]{0:T(128)S(1)} %pad_add_fusion.place, bf16[512,512]{1,0:T(8,128)(2,1)S(1)} %copy-done.2, bf16[512,512]{1,0:T(8,128)(2,1)S(1)} %copy-done.1, f32[3,4,80,256]{3,2,1,0:T(8,128)S(1)} %get-tuple-element.111.refs_0_.edges, ...), custom_call_target="tpu_custom_call" | custom-call | flops 4000000000 | bytes 12000000 | tf_op jit(solution)/shard_map/pallas_call | solution.py:667
  127.2 2.2 %collective-permute-done.47.after = f32[3,64,256]{2,1,0:T(8,128)S(1)} collective-permute-done((f32[3,64,256]{2,1,0:T(8,128)S(1)}, f32[3,64,256]{2,1,0:T(8,128)S(1)}, u32[]{:S(2)}, u32[]{:S(2)}) %collective-permute-start.47) | collective-permute-done | bytes 196640 | tf_op jit(solution)/shard_map/ppermute | solution.py:831
  (83 shorter events, 13.3 us)
Async XLA Ops:
  1.8 10.0 %collective-permute-start.3 = (f32[8,128]{1,0:T(8,128)S(1)}, f32[8,128]{1,0:T(8,128)S(1)}, u32[]{:S(2)}, u32[]{:S(2)}) collective-permute-start(f32[8,128]{1,0:T(8,128)S(1)} %get-tuple-element.69), channel_id=1, source_target_pairs={{0,8},{4,12},{8,16},{12,20},{16,24},{20,28},{24,0},{28,4},{1,9},{5... | collective-permute-start | bytes 12296 | tf_op jit(solution)/shard_map/ppermute | solution.py:740
  4.8 6.9 %collective-permute-start.2 = (f32[8,128]{1,0:T(8,128)S(1)}, f32[8,128]{1,0:T(8,128)S(1)}, u32[]{:S(2)}, u32[]{:S(2)}) collective-permute-start(f32[8,128]{1,0:T(8,128)S(1)} %get-tuple-element.69), channel_id=1, source_target_pairs={{0,24},{4,28},{8,0},{12,4},{16,8},{20,12},{24,16},{28,20},{1,25},{... | collective-permute-start | bytes 12296 | tf_op jit(solution)/shard_map/ppermute | solution.py:739
  6.9 6.4 %collective-permute-start.1 = (f32[8,512]{1,0:T(8,128)S(1)}, f32[8,512]{1,0:T(8,128)S(1)}, u32[]{:S(2)}, u32[]{:S(2)}) collective-permute-start(f32[8,512]{1,0:T(8,128)S(1)} %get-tuple-element.68.own), channel_id=1, source_target_pairs={{0,4},{4,8},{8,12},{12,16},{16,20},{20,24},{24,28},{28,0},{1,5},{5... | collective-permute-start | bytes 49160 | tf_op jit(solution)/shard_map/ppermute | solution.py:738
  8.6 4.8 %collective-permute-start = (f32[8,512]{1,0:T(8,128)S(1)}, f32[8,512]{1,0:T(8,128)S(1)}, u32[]{:S(2)}, u32[]{:S(2)}) collective-permute-start(f32[8,512]{1,0:T(8,128)S(1)} %get-tuple-element.68.own), channel_id=1, source_target_pairs={{0,28},{4,0},{8,4},{12,8},{16,12},{20,16},{24,20},{28,24},{1,29},{... | collective-permute-start | bytes 49160 | tf_op jit(solution)/shard_map/ppermute | solution.py:737
  17.1 10.0 %collective-permute-start.16 = (f32[72,768]{1,0:T(8,128)S(1)}, f32[72,768]{1,0:T(8,128)S(1)}, u32[]{:S(2)}, u32[]{:S(2)}) collective-permute-start(f32[72,768]{1,0:T(8,128)S(1)} %get-tuple-element.87), channel_id=1, source_target_pairs={{0,2},{1,3},{2,0},{3,1},{4,6},{5,7},{6,4},{7,5},{8,10},{9,11},{10,... | collective-permute-start | bytes 663560 | tf_op jit(solution)/shard_map/ppermute | solution.py:703
  18.8 8.4 %collective-permute-start.17 = (f32[72,768]{1,0:T(8,128)S(1)}, f32[72,768]{1,0:T(8,128)S(1)}, u32[]{:S(2)}, u32[]{:S(2)}) collective-permute-start(f32[72,768]{1,0:T(8,128)S(1)} %get-tuple-element.88), channel_id=1, source_target_pairs={{0,1},{1,0},{2,3},{3,2},{4,5},{5,4},{6,7},{7,6},{8,9},{9,8},{10,11... | collective-permute-start | bytes 663560 | tf_op jit(solution)/shard_map/ppermute | solution.py:703
  18.8 8.4 %collective-permute-start.18 = (f32[72,768]{1,0:T(8,128)S(1)}, f32[72,768]{1,0:T(8,128)S(1)}, u32[]{:S(2)}, u32[]{:S(2)}) collective-permute-start(f32[72,768]{1,0:T(8,128)S(1)} %get-tuple-element.89), channel_id=1, source_target_pairs={{0,3},{1,2},{2,1},{3,0},{4,7},{5,6},{6,5},{7,4},{8,11},{9,10},{10,... | collective-permute-start | bytes 663560 | tf_op jit(solution)/shard_map/ppermute | solution.py:703
  25.3 5.8 %collective-permute-start.6 = (f32[72,768]{1,0:T(8,128)S(1)}, f32[72,768]{1,0:T(8,128)S(1)}, u32[]{:S(2)}, u32[]{:S(2)}) collective-permute-start(f32[72,768]{1,0:T(8,128)S(1)} %get-tuple-element.75), channel_id=1, source_target_pairs={{0,1},{1,0},{2,3},{3,2},{4,5},{5,4},{6,7},{7,6},{8,9},{9,8},{10,11... | collective-permute-start | bytes 663560 | tf_op jit(solution)/shard_map/ppermute | solution.py:703
  25.4 8.9 %collective-permute-start.7 = (f32[72,768]{1,0:T(8,128)S(1)}, f32[72,768]{1,0:T(8,128)S(1)}, u32[]{:S(2)}, u32[]{:S(2)}) collective-permute-start(f32[72,768]{1,0:T(8,128)S(1)} %get-tuple-element.76), channel_id=1, source_target_pairs={{0,2},{1,3},{2,0},{3,1},{4,6},{5,7},{6,4},{7,5},{8,10},{9,11},{10,... | collective-permute-start | bytes 663560 | tf_op jit(solution)/shard_map/ppermute | solution.py:703
  27.1 10.4 %collective-permute-start.8 = (f32[72,768]{1,0:T(8,128)S(1)}, f32[72,768]{1,0:T(8,128)S(1)}, u32[]{:S(2)}, u32[]{:S(2)}) collective-permute-start(f32[72,768]{1,0:T(8,128)S(1)} %get-tuple-element.77), channel_id=1, source_target_pairs={{0,3},{1,2},{2,1},{3,0},{4,7},{5,6},{6,5},{7,4},{8,11},{9,10},{10,... | collective-permute-start | bytes 663560 | tf_op jit(solution)/shard_map/ppermute | solution.py:703
  28.8 11.9 %collective-permute-start.19 = (f32[32,768]{1,0:T(8,128)S(1)}, f32[32,768]{1,0:T(8,128)S(1)}, u32[]{:S(2)}, u32[]{:S(2)}) collective-permute-start(f32[32,768]{1,0:T(8,128)S(1)} %get-tuple-element.91), channel_id=1, source_target_pairs={{0,16},{4,20},{8,24},{12,28},{16,0},{20,4},{24,8},{28,12},{1,17},{... | collective-permute-start | bytes 294920 | tf_op jit(solution)/shard_map/ppermute | solution.py:703
  28.9 15.0 %collective-permute-start.20 = (f32[32,768]{1,0:T(8,128)S(1)}, f32[32,768]{1,0:T(8,128)S(1)}, u32[]{:S(2)}, u32[]{:S(2)}) collective-permute-start(f32[32,768]{1,0:T(8,128)S(1)} %get-tuple-element.92), channel_id=1, source_target_pairs={{0,4},{4,0},{8,12},{12,8},{16,20},{20,16},{24,28},{28,24},{1,5},{5... | collective-permute-start | bytes 294920 | tf_op jit(solution)/shard_map/ppermute | solution.py:703
  31.1 12.8 %collective-permute-start.21 = (f32[32,768]{1,0:T(8,128)S(1)}, f32[32,768]{1,0:T(8,128)S(1)}, u32[]{:S(2)}, u32[]{:S(2)}) collective-permute-start(f32[32,768]{1,0:T(8,128)S(1)} %get-tuple-element.93), channel_id=1, source_target_pairs={{0,24},{4,28},{8,16},{12,20},{16,8},{20,12},{24,0},{28,4},{1,25},{... | collective-permute-start | bytes 294920 | tf_op jit(solution)/shard_map/ppermute | solution.py:703
  34.3 11.8 %collective-permute-start.22 = (f32[32,768]{1,0:T(8,128)S(1)}, f32[32,768]{1,0:T(8,128)S(1)}, u32[]{:S(2)}, u32[]{:S(2)}) collective-permute-start(f32[32,768]{1,0:T(8,128)S(1)} %get-tuple-element.94), channel_id=1, source_target_pairs={{0,8},{4,12},{8,0},{12,4},{16,24},{20,28},{24,16},{28,20},{1,9},{5... | collective-permute-start | bytes 294920 | tf_op jit(solution)/shard_map/ppermute | solution.py:703
  37.5 11.6 %collective-permute-start.23 = (f32[32,768]{1,0:T(8,128)S(1)}, f32[32,768]{1,0:T(8,128)S(1)}, u32[]{:S(2)}, u32[]{:S(2)}) collective-permute-start(f32[32,768]{1,0:T(8,128)S(1)} %get-tuple-element.95), channel_id=1, source_target_pairs={{0,20},{4,16},{8,28},{12,24},{16,4},{20,0},{24,12},{28,8},{1,21},{... | collective-permute-start | bytes 294920 | tf_op jit(solution)/shard_map/ppermute | solution.py:703
  40.7 10.0 %collective-permute-start.24 = (f32[32,768]{1,0:T(8,128)S(1)}, f32[32,768]{1,0:T(8,128)S(1)}, u32[]{:S(2)}, u32[]{:S(2)}) collective-permute-start(f32[32,768]{1,0:T(8,128)S(1)} %get-tuple-element.96), channel_id=1, source_target_pairs={{0,28},{4,24},{8,20},{12,16},{16,12},{20,8},{24,4},{28,0},{1,29},{... | collective-permute-start | bytes 294920 | tf_op jit(solution)/shard_map/ppermute | solution.py:703
  43.9 12.1 %collective-permute-start.25 = (f32[32,768]{1,0:T(8,128)S(1)}, f32[32,768]{1,0:T(8,128)S(1)}, u32[]{:S(2)}, u32[]{:S(2)}) collective-permute-start(f32[32,768]{1,0:T(8,128)S(1)} %get-tuple-element.97), channel_id=1, source_target_pairs={{0,12},{4,8},{8,4},{12,0},{16,28},{20,24},{24,20},{28,16},{1,13},{... | collective-permute-start | bytes 294920 | tf_op jit(solution)/shard_map/ppermute | solution.py:703
  43.9 12.1 %collective-permute-start.9 = (f32[32,768]{1,0:T(8,128)S(1)}, f32[32,768]{1,0:T(8,128)S(1)}, u32[]{:S(2)}, u32[]{:S(2)}) collective-permute-start(f32[32,768]{1,0:T(8,128)S(1)} %get-tuple-element.79), channel_id=1, source_target_pairs={{0,16},{4,20},{8,24},{12,28},{16,0},{20,4},{24,8},{28,12},{1,17},{... | collective-permute-start | bytes 294920 | tf_op jit(solution)/shard_map/ppermute | solution.py:703
  46.1 14.1 %collective-permute-start.10 = (f32[32,768]{1,0:T(8,128)S(1)}, f32[32,768]{1,0:T(8,128)S(1)}, u32[]{:S(2)}, u32[]{:S(2)}) collective-permute-start(f32[32,768]{1,0:T(8,128)S(1)} %get-tuple-element.80), channel_id=1, source_target_pairs={{0,4},{4,0},{8,12},{12,8},{16,20},{20,16},{24,28},{28,24},{1,5},{5... | collective-permute-start | bytes 294920 | tf_op jit(solution)/shard_map/ppermute | solution.py:703
  49.1 12.5 %collective-permute-start.11 = (f32[32,768]{1,0:T(8,128)S(1)}, f32[32,768]{1,0:T(8,128)S(1)}, u32[]{:S(2)}, u32[]{:S(2)}) collective-permute-start(f32[32,768]{1,0:T(8,128)S(1)} %get-tuple-element.81), channel_id=1, source_target_pairs={{0,24},{4,28},{8,16},{12,20},{16,8},{20,12},{24,0},{28,4},{1,25},{... | collective-permute-start | bytes 294920 | tf_op jit(solution)/shard_map/ppermute | solution.py:703
  50.7 10.9 %collective-permute-start.12 = (f32[32,768]{1,0:T(8,128)S(1)}, f32[32,768]{1,0:T(8,128)S(1)}, u32[]{:S(2)}, u32[]{:S(2)}) collective-permute-start(f32[32,768]{1,0:T(8,128)S(1)} %get-tuple-element.82), channel_id=1, source_target_pairs={{0,8},{4,12},{8,0},{12,4},{16,24},{20,28},{24,16},{28,20},{1,9},{5... | collective-permute-start | bytes 294920 | tf_op jit(solution)/shard_map/ppermute | solution.py:703
  56.0 10.0 %collective-permute-start.13 = (f32[32,768]{1,0:T(8,128)S(1)}, f32[32,768]{1,0:T(8,128)S(1)}, u32[]{:S(2)}, u32[]{:S(2)}) collective-permute-start(f32[32,768]{1,0:T(8,128)S(1)} %get-tuple-element.83), channel_id=1, source_target_pairs={{0,20},{4,16},{8,28},{12,24},{16,4},{20,0},{24,12},{28,8},{1,21},{... | collective-permute-start | bytes 294920 | tf_op jit(solution)/shard_map/ppermute | solution.py:703
  56.0 10.0 %collective-permute-start.14 = (f32[32,768]{1,0:T(8,128)S(1)}, f32[32,768]{1,0:T(8,128)S(1)}, u32[]{:S(2)}, u32[]{:S(2)}) collective-permute-start(f32[32,768]{1,0:T(8,128)S(1)} %get-tuple-element.84), channel_id=1, source_target_pairs={{0,28},{4,24},{8,20},{12,16},{16,12},{20,8},{24,4},{28,0},{1,29},{... | collective-permute-start | bytes 294920 | tf_op jit(solution)/shard_map/ppermute | solution.py:703
  60.2 7.3 %collective-permute-start.15 = (f32[32,768]{1,0:T(8,128)S(1)}, f32[32,768]{1,0:T(8,128)S(1)}, u32[]{:S(2)}, u32[]{:S(2)}) collective-permute-start(f32[32,768]{1,0:T(8,128)S(1)} %get-tuple-element.85), channel_id=1, source_target_pairs={{0,12},{4,8},{8,4},{12,0},{16,28},{20,24},{24,20},{28,16},{1,13},{... | collective-permute-start | bytes 294920 | tf_op jit(solution)/shard_map/ppermute | solution.py:703
  61.5 7.2 %collective-permute-start.4 = (f32[48,256]{1,0:T(8,128)S(1)}, f32[48,256]{1,0:T(8,128)S(1)}, u32[]{:S(2)}, u32[]{:S(2)}) collective-permute-start(f32[48,256]{1,0:T(8,128)S(1)} %get-tuple-element.72), channel_id=1, source_target_pairs={{0,1},{1,2},{2,3},{3,0},{4,5},{5,6},{6,7},{7,4},{8,9},{9,10},{10,1... | collective-permute-start | bytes 147464 | tf_op jit(solution)/shard_map/ppermute | solution.py:761
  61.6 7.2 %collective-permute-start.5 = (f32[48,256]{1,0:T(8,128)S(1)}, f32[48,256]{1,0:T(8,128)S(1)}, u32[]{:S(2)}, u32[]{:S(2)}) collective-permute-start(f32[48,256]{1,0:T(8,128)S(1)} %get-tuple-element.73), channel_id=1, source_target_pairs={{0,3},{1,0},{2,1},{3,2},{4,7},{5,4},{6,5},{7,6},{8,11},{9,8},{10,9... | collective-permute-start | bytes 147464 | tf_op jit(solution)/shard_map/ppermute | solution.py:762
  72.6 11.1 %collective-permute-start.26 = (f32[32,768]{1,0:T(8,128)S(1)}, f32[32,768]{1,0:T(8,128)S(1)}, u32[]{:S(2)}, u32[]{:S(2)}) collective-permute-start(f32[32,768]{1,0:T(8,128)S(1)} %get-tuple-element.100), channel_id=1, source_target_pairs={{0,16},{4,20},{8,24},{12,28},{16,0},{20,4},{24,8},{28,12},{1,17},{... | collective-permute-start | bytes 294920 | tf_op jit(solution)/shard_map/ppermute | solution.py:703
  73.4 12.4 %collective-permute-start.27 = (f32[32,768]{1,0:T(8,128)S(1)}, f32[32,768]{1,0:T(8,128)S(1)}, u32[]{:S(2)}, u32[]{:S(2)}) collective-permute-start(f32[32,768]{1,0:T(8,128)S(1)} %get-tuple-element.101), channel_id=1, source_target_pairs={{0,4},{4,0},{8,12},{12,8},{16,20},{20,16},{24,28},{28,24},{1,5},{5... | collective-permute-start | bytes 294920 | tf_op jit(solution)/shard_map/ppermute | solution.py:703
  75.5 11.8 %collective-permute-start.28 = (f32[32,768]{1,0:T(8,128)S(1)}, f32[32,768]{1,0:T(8,128)S(1)}, u32[]{:S(2)}, u32[]{:S(2)}) collective-permute-start(f32[32,768]{1,0:T(8,128)S(1)} %get-tuple-element.102), channel_id=1, source_target_pairs={{0,24},{4,28},{8,16},{12,20},{16,8},{20,12},{24,0},{28,4},{1,25},{... | collective-permute-start | bytes 294920 | tf_op jit(solution)/shard_map/ppermute | solution.py:703
  76.4 14.0 %collective-permute-start.29 = (f32[32,768]{1,0:T(8,128)S(1)}, f32[32,768]{1,0:T(8,128)S(1)}, u32[]{:S(2)}, u32[]{:S(2)}) collective-permute-start(f32[32,768]{1,0:T(8,128)S(1)} %get-tuple-element.103), channel_id=1, source_target_pairs={{0,8},{4,12},{8,0},{12,4},{16,24},{20,28},{24,16},{28,20},{1,9},{5... | collective-permute-start | bytes 294920 | tf_op jit(solution)/shard_map/ppermute | solution.py:703
  76.4 15.3 %collective-permute-start.30 = (f32[32,768]{1,0:T(8,128)S(1)}, f32[32,768]{1,0:T(8,128)S(1)}, u32[]{:S(2)}, u32[]{:S(2)}) collective-permute-start(f32[32,768]{1,0:T(8,128)S(1)} %get-tuple-element.104), channel_id=1, source_target_pairs={{0,20},{4,16},{8,28},{12,24},{16,4},{20,0},{24,12},{28,8},{1,21},{... | collective-permute-start | bytes 294920 | tf_op jit(solution)/shard_map/ppermute | solution.py:703
  83.6 10.6 %collective-permute-start.31 = (f32[32,768]{1,0:T(8,128)S(1)}, f32[32,768]{1,0:T(8,128)S(1)}, u32[]{:S(2)}, u32[]{:S(2)}) collective-permute-start(f32[32,768]{1,0:T(8,128)S(1)} %get-tuple-element.105), channel_id=1, source_target_pairs={{0,28},{4,24},{8,20},{12,16},{16,12},{20,8},{24,4},{28,0},{1,29},{... | collective-permute-start | bytes 294920 | tf_op jit(solution)/shard_map/ppermute | solution.py:703
  85.8 8.8 %collective-permute-start.32 = (f32[32,768]{1,0:T(8,128)S(1)}, f32[32,768]{1,0:T(8,128)S(1)}, u32[]{:S(2)}, u32[]{:S(2)}) collective-permute-start(f32[32,768]{1,0:T(8,128)S(1)} %get-tuple-element.106), channel_id=1, source_target_pairs={{0,12},{4,8},{8,4},{12,0},{16,28},{20,24},{24,20},{28,16},{1,13},{... | collective-permute-start | bytes 294920 | tf_op jit(solution)/shard_map/ppermute | solution.py:703
  87.3 14.2 %collective-permute-start.36 = (f32[32,768]{1,0:T(8,128)S(1)}, f32[32,768]{1,0:T(8,128)S(1)}, u32[]{:S(2)}, u32[]{:S(2)}) collective-permute-start(f32[32,768]{1,0:T(8,128)S(1)} %get-tuple-element.116), channel_id=1, source_target_pairs={{0,16},{4,20},{8,24},{12,28},{16,0},{20,4},{24,8},{28,12},{1,17},{... | collective-permute-start | bytes 294920 | tf_op jit(solution)/shard_map/ppermute | solution.py:703
  90.4 12.4 %collective-permute-start.37 = (f32[32,768]{1,0:T(8,128)S(1)}, f32[32,768]{1,0:T(8,128)S(1)}, u32[]{:S(2)}, u32[]{:S(2)}) collective-permute-start(f32[32,768]{1,0:T(8,128)S(1)} %get-tuple-element.117), channel_id=1, source_target_pairs={{0,4},{4,0},{8,12},{12,8},{16,20},{20,16},{24,28},{28,24},{1,5},{5... | collective-permute-start | bytes 294920 | tf_op jit(solution)/shard_map/ppermute | solution.py:703
  91.7 12.2 %collective-permute-start.38 = (f32[32,768]{1,0:T(8,128)S(1)}, f32[32,768]{1,0:T(8,128)S(1)}, u32[]{:S(2)}, u32[]{:S(2)}) collective-permute-start(f32[32,768]{1,0:T(8,128)S(1)} %get-tuple-element.118), channel_id=1, source_target_pairs={{0,24},{4,28},{8,16},{12,20},{16,8},{20,12},{24,0},{28,4},{1,25},{... | collective-permute-start | bytes 294920 | tf_op jit(solution)/shard_map/ppermute | solution.py:703
  94.3 11.9 %collective-permute-start.39 = (f32[32,768]{1,0:T(8,128)S(1)}, f32[32,768]{1,0:T(8,128)S(1)}, u32[]{:S(2)}, u32[]{:S(2)}) collective-permute-start(f32[32,768]{1,0:T(8,128)S(1)} %get-tuple-element.119), channel_id=1, source_target_pairs={{0,8},{4,12},{8,0},{12,4},{16,24},{20,28},{24,16},{28,20},{1,9},{5... | collective-permute-start | bytes 294920 | tf_op jit(solution)/shard_map/ppermute | solution.py:703
  96.4 9.8 %collective-permute-start.40 = (f32[32,768]{1,0:T(8,128)S(1)}, f32[32,768]{1,0:T(8,128)S(1)}, u32[]{:S(2)}, u32[]{:S(2)}) collective-permute-start(f32[32,768]{1,0:T(8,128)S(1)} %get-tuple-element.123), channel_id=1, source_target_pairs={{0,20},{4,16},{8,28},{12,24},{16,4},{20,0},{24,12},{28,8},{1,21},{... | collective-permute-start | bytes 294920 | tf_op jit(solution)/shard_map/ppermute | solution.py:703
  101.5 7.4 %collective-permute-start.41 = (f32[32,768]{1,0:T(8,128)S(1)}, f32[32,768]{1,0:T(8,128)S(1)}, u32[]{:S(2)}, u32[]{:S(2)}) collective-permute-start(f32[32,768]{1,0:T(8,128)S(1)} %get-tuple-element.124), channel_id=1, source_target_pairs={{0,28},{4,24},{8,20},{12,16},{16,12},{20,8},{24,4},{28,0},{1,29},{... | collective-permute-start | bytes 294920 | tf_op jit(solution)/shard_map/ppermute | solution.py:703
  102.8 6.6 %collective-permute-start.42 = (f32[32,768]{1,0:T(8,128)S(1)}, f32[32,768]{1,0:T(8,128)S(1)}, u32[]{:S(2)}, u32[]{:S(2)}) collective-permute-start(f32[32,768]{1,0:T(8,128)S(1)} %get-tuple-element.125), channel_id=1, source_target_pairs={{0,12},{4,8},{8,4},{12,0},{16,28},{20,24},{24,20},{28,16},{1,13},{... | collective-permute-start | bytes 294920 | tf_op jit(solution)/shard_map/ppermute | solution.py:703
  103.9 8.6 %collective-permute-start.33 = (f32[72,768]{1,0:T(8,128)S(1)}, f32[72,768]{1,0:T(8,128)S(1)}, u32[]{:S(2)}, u32[]{:S(2)}) collective-permute-start(f32[72,768]{1,0:T(8,128)S(1)} %get-tuple-element.108), channel_id=1, source_target_pairs={{0,2},{1,3},{2,0},{3,1},{4,6},{5,7},{6,4},{7,5},{8,10},{9,11},{10,... | collective-permute-start | bytes 663560 | tf_op jit(solution)/shard_map/ppermute | solution.py:703
  106.1 7.1 %collective-permute-start.34 = (f32[72,768]{1,0:T(8,128)S(1)}, f32[72,768]{1,0:T(8,128)S(1)}, u32[]{:S(2)}, u32[]{:S(2)}) collective-permute-start(f32[72,768]{1,0:T(8,128)S(1)} %get-tuple-element.109), channel_id=1, source_target_pairs={{0,1},{1,0},{2,3},{3,2},{4,5},{5,4},{6,7},{7,6},{8,9},{9,8},{10,11... | collective-permute-start | bytes 663560 | tf_op jit(solution)/shard_map/ppermute | solution.py:703
  106.2 9.9 %collective-permute-start.35 = (f32[72,768]{1,0:T(8,128)S(1)}, f32[72,768]{1,0:T(8,128)S(1)}, u32[]{:S(2)}, u32[]{:S(2)}) collective-permute-start(f32[72,768]{1,0:T(8,128)S(1)} %get-tuple-element.110), channel_id=1, source_target_pairs={{0,3},{1,2},{2,1},{3,0},{4,7},{5,6},{6,5},{7,4},{8,11},{9,10},{10,... | collective-permute-start | bytes 663560 | tf_op jit(solution)/shard_map/ppermute | solution.py:703
  111.1 11.4 %collective-permute-start.43 = (f32[72,768]{1,0:T(8,128)S(1)}, f32[72,768]{1,0:T(8,128)S(1)}, u32[]{:S(2)}, u32[]{:S(2)}) collective-permute-start(f32[72,768]{1,0:T(8,128)S(1)} %get-tuple-element.127), channel_id=1, source_target_pairs={{0,2},{1,3},{2,0},{3,1},{4,6},{5,7},{6,4},{7,5},{8,10},{9,11},{10,... | collective-permute-start | bytes 663560 | tf_op jit(solution)/shard_map/ppermute | solution.py:703
  112.5 11.3 %collective-permute-start.44 = (f32[72,768]{1,0:T(8,128)S(1)}, f32[72,768]{1,0:T(8,128)S(1)}, u32[]{:S(2)}, u32[]{:S(2)}) collective-permute-start(f32[72,768]{1,0:T(8,128)S(1)} %get-tuple-element.128), channel_id=1, source_target_pairs={{0,3},{1,2},{2,1},{3,0},{4,7},{5,6},{6,5},{7,4},{8,11},{9,10},{10,... | collective-permute-start | bytes 663560 | tf_op jit(solution)/shard_map/ppermute | solution.py:703
  112.5 11.3 %collective-permute-start.45 = (f32[72,768]{1,0:T(8,128)S(1)}, f32[72,768]{1,0:T(8,128)S(1)}, u32[]{:S(2)}, u32[]{:S(2)}) collective-permute-start(f32[72,768]{1,0:T(8,128)S(1)} %get-tuple-element.129), channel_id=1, source_target_pairs={{0,1},{1,0},{2,3},{3,2},{4,5},{5,4},{6,7},{7,6},{8,9},{9,8},{10,11... | collective-permute-start | bytes 663560 | tf_op jit(solution)/shard_map/ppermute | solution.py:703
  117.6 9.6 %collective-permute-start.46 = (f32[3,64,256]{2,1,0:T(8,128)S(1)}, f32[3,64,256]{2,1,0:T(8,128)S(1)}, u32[]{:S(2)}, u32[]{:S(2)}) collective-permute-start(f32[3,64,256]{2,1,0:T(8,128)S(1)} %get-tuple-element.132), channel_id=1, source_target_pairs={{0,4},{4,8},{8,12},{12,16},{16,20},{20,24},{24,28},{28,0},{1,5},{5... | collective-permute-start | bytes 589832 | tf_op jit(solution)/shard_map/ppermute | solution.py:832
  118.1 11.3 %collective-permute-start.47 = (f32[3,64,256]{2,1,0:T(8,128)S(1)}, f32[3,64,256]{2,1,0:T(8,128)S(1)}, u32[]{:S(2)}, u32[]{:S(2)}) collective-permute-start(f32[3,64,256]{2,1,0:T(8,128)S(1)} %get-tuple-element.133), channel_id=1, source_target_pairs={{0,28},{4,0},{8,4},{12,8},{16,12},{20,16},{24,20},{28,24},{1,29},{... | collective-permute-start | bytes 589832 | tf_op jit(solution)/shard_map/ppermute | solution.py:831
  (9 other events, 85.3 us)
